TPU v7x, 256 devices: a whole 4x4x8 slice. The times are simulated.
256 devices in a mesh: dp: 16 (over x, z_lo), tensor: 16 (over y, z_hi, core).
Axes of the slice: x: 4, y: 4, z: 8 (z_hi: 2, z_lo: 4; z = z_hi * 4 + z_lo), core: 2. Of those that a mesh axis runs over, the one named last changes fastest.
Arguments:
- gate_hidden_input: bfloat16 [32768, 4608], P(('dp', 'tensor')), may hold values from -6 to 6
- output_gradient: bfloat16 [32768, 4608], P(('dp', 'tensor')), may hold values from -6 to 6
- attention_mixture: bfloat16 [32768, 4096], P('dp', 'tensor'), may hold values from -6 to 6
- output_matrix: bfloat16 [4096, 4608], P('tensor'), may hold values from -0.09375 to 0.09375
- adapter_down_weight: bfloat16 [4096, 128], P('tensor'), may hold values from -0.09375 to 0.09375
- adapter_up_weight: bfloat16 [128, 4608], replicated, may hold values from -1.5 to 1.5
- gate_matrix: bfloat16 [8, 4608], replicated, may hold values from -0.09375 to 0.09375
Outputs:
- gate_grad: float32 [8, 4608], replicated
- attention_gradient: bfloat16 [32768, 4096], P('dp', 'tensor')
All inputs are finite; a program needn't handle non-finite values.
Results may differ from a plain program's by a relative error of at most 0.0047.
Values may be sent and summed in bfloat16 or wider, within the bound.
No kernel may reach another device: no remote copies, remote signals or barrier semaphores. Data moves between devices by JAX's collectives and lax.ppermute only.
A program may use at most 128 MiB of HBM per device.

v0:
```python
import jax
import jax.numpy as jnp
from jax import lax
from jax.sharding import PartitionSpec as P


def on_device(
    gate_hidden_input,
    output_gradient,
    attention_mixture,
    output_matrix,
    adapter_down_weight,
    adapter_up_weight,
    gate_matrix,
):
    token_rows = gate_hidden_input.shape[0]
    adapter_list = gate_matrix.shape[0]
    feature_width = adapter_up_weight.shape[0] // adapter_list
    logits = jnp.einsum(
        "td,kd->tk", gate_hidden_input, gate_matrix, preferred_element_type=jnp.float32
    )
    gates = jax.nn.sigmoid(logits)
    all_gates = lax.all_gather(gates, "tensor", axis=0, tiled=True)
    complete_gradient = lax.all_gather(output_gradient, "tensor", axis=0, tiled=True)
    backward_every = jnp.einsum(
        "kw,vw->kv", complete_gradient, adapter_up_weight, preferred_element_type=jnp.float32
    )
    backward_local = lax.dynamic_slice_in_dim(
        backward_every, lax.axis_index("tensor") * token_rows, token_rows, 0
    )
    incomplete_activation = jnp.dot(
        attention_mixture, adapter_down_weight, preferred_element_type=jnp.float32
    )
    total_act = lax.psum(incomplete_activation, "tensor")
    rank_local = lax.dynamic_slice_in_dim(
        total_act, lax.axis_index("tensor") * token_rows, token_rows, 0
    )
    gate_delta = 2.0 * jnp.sum(
        (rank_local * backward_local).reshape(token_rows, adapter_list, feature_width), axis=2
    )
    dlogit = gate_delta * gates * (1.0 - gates)
    local_grad = jnp.dot(
        dlogit.T, gate_hidden_input.astype(jnp.float32), precision=lax.Precision.HIGHEST
    )
    gate_grad = lax.psum(local_grad, ("dp", "tensor"))
    expanded = 2.0 * jnp.repeat(all_gates, feature_width, axis=1)
    blended_output = (expanded * backward_every).astype(jnp.bfloat16)
    base_offset = jnp.einsum(
        "td,qd->tq", complete_gradient, output_matrix, preferred_element_type=jnp.float32
    )
    adapter_index = jnp.einsum(
        "ux,ix->ui", blended_output, adapter_down_weight, preferred_element_type=jnp.float32
    )
    attention_gradient = (base_offset + adapter_index).astype(jnp.bfloat16)
    return (gate_grad, attention_gradient)


def solution(mesh):
    in_specs = (
        P(("dp", "tensor"), None),
        P(("dp", "tensor"), None),
        P("dp", "tensor"),
        P("tensor", None),
        P("tensor", None),
        P(),
        P(),
    )
    out_specs = (P(), P("dp", "tensor"))
    return jax.shard_map(
        on_device, mesh=mesh, in_specs=in_specs, out_specs=out_specs, check_vma=False
    )
```

profile of v0, /device:TPU:1, one launch (start us, length us, event | category | flops | bytes accessed | tf_op | source)
XLA Modules:
  0.0 643.7 jit_solution(5847809562991289360)
XLA Ops:
  7.2 0.0 copy-start
  7.2 0.0 copy-start.1
  7.2 0.0 all-gather.2.cloned.1.call-start
  7.2 0.7 all-gather.2.cloned.1.call-update
  7.9 0.0 all-reduce.3.cloned.1.call-start
  8.0 2.6 fusion.14
  10.6 0.0 all-reduce.3.cloned.1.call-update
  10.6 0.0 all-reduce.5.cloned.1.call-start
  10.7 0.0 copy-done.1
  10.7 1.3 fusion.3
  12.0 36.6 %all_gather.7 = f32[2048,8]{0,1:T(8,128)S(1)} all-gather(f32[128,8]{0,1:T(8,128)S(1)} %fusion.3), channel_id=1, replica_groups=mesh['dp'=16,'tensor'=16] {'tensor'}, dimensions={0}, use_global_device_ids=true | all-gather | bytes 69632 | tf_op jit(solution)/shard_map/all_gather | solution.py:23
  48.6 0.6 broadcast_multiply_fusion
  49.2 157.8 %all-gather.2.cloned.1.call-done = bf16[2048,4608]{1,0:T(8,128)(2,1)} async-done(((bf16[128,4608]{1,0:T(8,128)(2,1)}), bf16[2048,4608]{1,0:T(8,128)(2,1)}) %all-gather.2.cloned.1.call-update) | async-done | bytes 18874384 | tf_op jit(solution)/shard_map/all_gather | solution.py:24
  207.0 13.6 %fusion.4 = (bf16[2048,128]{0,1:T(8,128)(2,1)}, f32[2048,128]{0,1:T(8,128)S(1)}) fusion(f32[2048,8]{0,1:T(8,128)} %broadcast_multiply_fusion, bf16[2048,4608]{1,0:T(8,128)(2,1)} %all-gather.2.cloned.1.call-done, bf16[128,4608]{1,0:T(8,128)(2,1)} %param.12), kind=kOutput, calls=%fused_computation.7 | convolution fusion | flops 2416443392 | bytes 21692416 | tf_op jit(solution)/shard_map/kw,vw->kv/dot_general | solution.py:25
  220.6 0.6 constant_dynamic-slice_fusion
  221.2 1.6 copy.12
  222.8 162.0 %all-reduce.3.cloned.1.call-done = f32[2048,128]{1,0:T(8,128)} async-done(((f32[2048,128]{1,0:T(8,128)}), f32[2048,128]{1,0:T(8,128)}) %all-reduce.3.cloned.1.call-update) | async-done | bytes 1048592 | tf_op jit(solution)/shard_map/psum | solution.py:34
  384.8 1.5 dynamic-slice_multiply_fusion
  386.3 1.6 copy.11
  387.8 0.9 bitcast_reduce_fusion
  388.7 1.2 fusion.5
  389.9 0.0 all-reduce.5.cloned.1.call-update
  390.0 0.0 copy-done
  390.0 0.0 copy-start.2
  390.0 0.0 copy-start.3
  390.0 9.1 %fusion.15 = f32[2048,256]{1,0:T(8,128)S(1)} fusion(bf16[2048,4608]{1,0:T(8,128)(2,1)} %all-gather.2.cloned.1.call-done, bf16[256,4608]{1,0:T(8,128)(2,1)S(1)} %copy-done), kind=kOutput, calls=%fused_computation.22 | convolution fusion | flops 4831838208 | bytes 23330816 | tf_op jit(solution)/shard_map/td,qd->tq/dot_general | solution.py:48
  399.1 0.0 copy-done.2
  399.1 0.0 copy-done.3
  399.1 1.4 fusion
  400.5 235.0 %all-reduce.5.cloned.1.call-done = f32[8,4608]{1,0:T(8,128)} async-done(((f32[8,4608]{1,0:T(8,128)}), f32[8,4608]{1,0:T(8,128)}) %all-reduce.5.cloned.1.call-update) | async-done | bytes 147472 | tf_op jit(solution)/shard_map/psum | solution.py:45
  635.6 1.6 copy.15
Async XLA Ops:
  7.2 382.8 %copy-start = (bf16[256,4608]{1,0:T(8,128)(2,1)S(1)}, bf16[256,4608]{1,0:T(8,128)(2,1)}, u32[]{:S(2)}) copy-start(bf16[256,4608]{1,0:T(8,128)(2,1)} %param.10) | copy-start | bytes 7077892
  7.2 3.5 copy-start.1
  7.2 199.8 %all-gather.2.cloned.1.call-start = ((), (), s32[]{:S(2)}) async-start(), calls=%async_computation.1 | async-start | bytes 20054016 | tf_op jit(solution)/shard_map/all_gather | solution.py:24
  7.9 376.8 %all-reduce.3.cloned.1.call-start = ((), (), s32[]{:S(2)}) async-start(), calls=%async_computation | async-start | bytes 2097152 | tf_op jit(solution)/shard_map/psum | solution.py:34
  10.6 624.9 %all-reduce.5.cloned.1.call-start = ((), (), s32[]{:S(2)}) async-start(), calls=%async_computation.2 | async-start | bytes 294912 | tf_op jit(solution)/shard_map/psum | solution.py:45
  390.0 9.1 %copy-start.2 = (bf16[2048,128]{0,1:T(8,128)(2,1)S(1)}, bf16[2048,128]{0,1:T(8,128)(2,1)}, u32[]{:S(2)}) copy-start(bf16[2048,128]{0,1:T(8,128)(2,1)} %get-tuple-element.2) | copy-start | bytes 1572868
  390.0 9.1 %copy-start.3 = (bf16[256,128]{1,0:T(8,128)(2,1)S(1)}, bf16[256,128]{1,0:T(8,128)(2,1)}, u32[]{:S(2)}) copy-start(bf16[256,128]{1,0:T(8,128)(2,1)} %param.11) | copy-start | bytes 196612
Sparse Core Ops, SparseCore 0:
  10.7 196.2 all-gather.1
  210.2 174.5 all-reduce.2
  391.8 243.7 all-reduce.4
where the time goes:
time: 644 us
  waiting for transfers between devices  556 us (86%)
  blocking collectives  36.6 us (6%)
  matrix products  29.2 us (5%)
  between operations  13.8 us (2%)
    psum x1, waiting for transfers between devices, on_device(): gate_grad = lax.psum(local_grad, ('dp', 'tensor'))  235 us
    psum x1, waiting for transfers between devices, on_device(): total_act = lax.psum(incomplete_activation, 'tensor')  162 us
    all_gather x1, waiting for transfers between devices, on_device(): lax.all_gather(output_gradient, 'tensor', axis=0, tiled=True)  158 us
    all_gather x1, blocking collectives, on_device(): all_gates = lax.all_gather(gates, 'tensor', axis=0, tiled=True)  36.6 us
    dot_general x1, matrix products, on_device(): jnp.einsum('kw,vw->kv', complete_gradient, adapter_up_weight, preferred_e...  13.6 us
  transfers between devices with their start and end apart: 3, of which 3 were waited for; matrix products, arithmetic and copies ran while one was open for 5% of the time, Pallas kernels for 0%

commit v1 on v0

v1 whole, which is shorter than its diff:
```python
import jax
import jax.numpy as jnp
from jax import lax
from jax.sharding import Mesh
from jax.sharding import PartitionSpec as P

F32 = jnp.float32
BF16 = jnp.bfloat16
AXES = ("x", "zl", "y", "zh", "c")


def shift(value, axis, by):
    size = lax.axis_size(axis)
    return lax.ppermute(value, axis, [(i, (i + by) % size) for i in range(size)])


def swap(value, axis, mask):
    size = lax.axis_size(axis)
    return lax.ppermute(value, axis, [(i, i ^ mask) for i in range(size)])


def dot_t(left, right):
    return lax.dot_general(left, right, (((1,), (1,)), ((), ())), preferred_element_type=F32)


def ring_gather(piece, axis):
    half = piece.shape[0] // 2
    low = shift(piece, axis, 1)
    high = shift(piece, axis, -1)
    far_top = shift(low[:half], axis, 1)
    far_bottom = shift(high[half:], axis, -1)
    return low, high, far_top, far_bottom


def on_device(hidden, grad, mixture, weight, down, up, gate_matrix):
    tokens, width = grad.shape
    adapters = gate_matrix.shape[0]
    stacked = up.shape[0]
    rank = stacked // adapters
    features = weight.shape[0]
    x, y, zh, c = (lax.axis_index(a) for a in ("x", "y", "zh", "c"))

    quarter = features // 4
    mine = jnp.concatenate(
        [
            lax.dynamic_slice_in_dim(weight, x * quarter, quarter, 0),
            lax.dynamic_slice_in_dim(down, x * quarter, quarter, 0),
        ],
        axis=1,
    )
    far_piece = swap(mine, "zh", 1)

    partial = jnp.dot(mixture, down, preferred_element_type=F32).reshape(4, 2, 2, tokens, stacked)
    keep = lax.dynamic_index_in_dim(partial, c, 2, keepdims=False)
    give = lax.dynamic_index_in_dim(partial, 1 - c, 2, keepdims=False)
    act = keep + swap(give.astype(BF16), "c", 1).astype(F32)
    pick = lambda m: lax.dynamic_index_in_dim(act, y ^ m, 0, keepdims=False).astype(BF16)
    act = (lax.dynamic_index_in_dim(act, y, 0, keepdims=False) + swap(pick(1), "y", 1).astype(F32)) + (
        swap(pick(2), "y", 2).astype(F32) + swap(pick(3), "y", 3).astype(F32)
    )
    keep = lax.dynamic_index_in_dim(act, zh, 0, keepdims=False)
    give = lax.dynamic_index_in_dim(act, 1 - zh, 0, keepdims=False)
    rank_act = keep + swap(give.astype(BF16), "zh", 1).astype(F32)

    gates = jax.nn.sigmoid(dot_t(hidden, gate_matrix))
    back = dot_t(grad, up)
    mixed = (2.0 * jnp.repeat(gates, rank, axis=1) * back).astype(BF16)
    mixed_all = lax.all_gather(mixed, ("y", "c"), axis=0, tiled=True)

    gate_delta = 2.0 * jnp.sum((rank_act * back).reshape(tokens, adapters, rank), axis=2)
    dlogit = gate_delta * gates * (1.0 - gates)
    total = jnp.dot(dlogit.T, hidden.astype(F32), precision=lax.Precision.HIGHEST)
    half = width // 2
    total = lax.dynamic_slice_in_dim(total, c * half, half, 1) + swap(
        lax.dynamic_slice_in_dim(total, (1 - c) * half, half, 1), "c", 1
    )
    for axis, mask in (("x", 1), ("x", 2), ("y", 1), ("y", 2), ("zl", 1), ("zl", 2), ("zh", 1)):
        total = total + swap(total, axis, mask)
    other = swap(total, "c", 1)
    gate_grad = jnp.where(
        c == 0, jnp.concatenate([total, other], axis=1), jnp.concatenate([other, total], axis=1)
    )

    low, high, far_top, far_bottom = ring_gather(grad, "y")
    every = jnp.zeros((4, 2, tokens, width), BF16)
    for step, at, block in (
        (0, 0, grad),
        (3, 0, low),
        (1, 0, high),
        (2, 0, far_top),
        (2, tokens // 2, far_bottom),
    ):
        where = (y + step) % 4
        every = lax.dynamic_update_slice(every, block[None, None], (where, c, at, 0))
        every = lax.dynamic_update_slice(every, swap(block, "c", 1)[None, None], (where, 1 - c, at, 0))
    every = every.reshape(8 * tokens, width)

    low, high, far_top, far_bottom = ring_gather(far_piece, "x")
    far_weight = jnp.zeros((4, quarter, width + stacked), BF16)
    for step, at, block in (
        (0, 0, far_piece),
        (3, 0, low),
        (1, 0, high),
        (2, 0, far_top),
        (2, quarter // 2, far_bottom),
    ):
        far_weight = lax.dynamic_update_slice(far_weight, block[None], ((x + step) % 4, at, 0))
    far_weight = far_weight.reshape(features, width + stacked)

    far_out = (
        dot_t(every, far_weight[:, :width]) + dot_t(mixed_all, far_weight[:, width:])
    ).astype(BF16)
    own_out = (dot_t(every, weight) + dot_t(mixed_all, down)).astype(BF16)
    got = swap(far_out, "zh", 1)
    own_out, got = (v.reshape(4, 1, 2 * tokens, features) for v in (own_out, got))
    out = jnp.where(
        zh == 0, jnp.concatenate([own_out, got], axis=1), jnp.concatenate([got, own_out], axis=1)
    )
    return gate_grad, out.reshape(16 * tokens, features)


def solution(mesh):
    grid = Mesh(mesh.devices.reshape(4, 4, 4, 2, 2), AXES)
    dp, tensor = ("x", "zl"), ("y", "zh", "c")
    return jax.shard_map(
        on_device,
        mesh=grid,
        in_specs=(
            P(AXES, None),
            P(AXES, None),
            P(dp, tensor),
            P(tensor, None),
            P(tensor, None),
            P(),
            P(),
        ),
        out_specs=(P(), P(dp, tensor)),
        check_vma=False,
    )
```

time: 644 us -> 217 us (0.34)
  the two profiles are of different devices: /device:TPU:1 before, /device:TPU:6 now
where the time goes in v1:
time: 217 us; the launch traced here: 216 us
  waiting for transfers between devices  106 us (49%)
  starting transfers between devices  34.4 us (16%)
  local copies, waits for them, and re-layouts  32.6 us (15%)
  matrix products  20.8 us (10%)
  blocking collectives  11.7 us (5%)
  other arithmetic  10.4 us (5%)
    ppermute x21, waiting for transfers between devices, swap(): return lax.ppermute(value, axis, [(i, i ^ mask) for i in range(size)])  82 us
    ppermute x21, starting transfers between devices, swap(): return lax.ppermute(value, axis, [(i, i ^ mask) for i in range(size)])  25.4 us
    ppermute x8, waiting for transfers between devices, shift(): lax.ppermute(value, axis, [(i, (i + by) % size) for i in range(size)])  23.5 us
    dot_general x6, matrix products, dot_t(): lax.dot_general(left, right, (((1,), (1,)), ((), ())), preferred_element_...  18.4 us
    all_gather x1, blocking collectives, on_device(): mixed_all = lax.all_gather(mixed, ('y', 'c'), axis=0, tiled=True)  11.7 us
    ppermute x8, starting transfers between devices, shift(): lax.ppermute(value, axis, [(i, (i + by) % size) for i in range(size)])  9.04 us
    dynamic_update_slice x5, local copies, waits for them, and re-layouts, on_device(): lax.dynamic_update_slice(every, block[None, None], (where, c, at, 0))  6.46 us
    dynamic_update_slice x5, local copies, waits for them, and re-layouts, on_device(): lax.dynamic_update_slice(every, swap(block, 'c', 1)[None, None], (where,...  6.26 us
  transfers between devices with their start and end apart: 29, of which 13 were waited for; matrix products, arithmetic and copies ran while one was open for 19% of the time, Pallas kernels for 0%

profile of v1, /device:TPU:6, one launch (start us, length us, event | category | flops | bytes accessed | tf_op | source)
XLA Modules:
  0.0 216.3 jit_solution(15013261254273476595)
XLA Ops:
  0.7 1.8 fusion.30
  2.5 1.0 copy-done.3
  4.2 1.9 copy.12
  6.1 1.9 constant_dynamic-slice_fusion.4
  7.9 2.0 copy.9
  10.0 1.2 bitcast_add_fusion
  12.6 1.6 collective-permute-start.1
  14.2 2.9 %collective-permute-start.2 = (bf16[2,128,128]{1,2,0:T(8,128)(2,1)}, bf16[2,128,128]{1,2,0:T(8,128)(2,1)}, u32[]{:S(2)}, u32[]{:S(2)}) collective-permute-start(bf16[2,128,128]{1,2,0:T(8,128)(2,1)} %get-tuple-element.4), channel_id=1, source_target_pairs={{0,8},{4,12},{8,0},{12,4},{1,9},{5,13},{9,1},{13,5},{2,10},{6,14},... | collective-permute-start | bytes 196616 | tf_op jit(solution)/shard_map/ppermute | solution.py:19
  17.4 3.9 %collective-permute-done.2 = bf16[2,128,128]{1,2,0:T(8,128)(2,1)} collective-permute-done((bf16[2,128,128]{1,2,0:T(8,128)(2,1)}, bf16[2,128,128]{1,2,0:T(8,128)(2,1)}, u32[]{:S(2)}, u32[]{:S(2)}) %collective-permute-start.2) | collective-permute-done | bytes 65568 | tf_op jit(solution)/shard_map/ppermute | solution.py:19
  21.3 1.6 collective-permute-done.3
  22.9 1.0 fusion.12
  25.2 7.2 %collective-permute-start.4 = (bf16[128,128]{0,1:T(8,128)(2,1)}, bf16[128,128]{0,1:T(8,128)(2,1)}, u32[]{:S(2)}, u32[]{:S(2)}) collective-permute-start(bf16[128,128]{0,1:T(8,128)(2,1)} %fusion.20), channel_id=1, source_target_pairs={{0,2},{2,0},{1,3},{3,1},{4,6},{6,4},{5,7},{7,5},{8,10},{10,8},{9,1... | collective-permute-start | bytes 98312 | tf_op jit(solution)/shard_map/ppermute | solution.py:19
  32.4 1.3 broadcast_multiply_fusion
  33.7 2.8 %fusion.18 = (bf16[128,128]{0,1:T(8,128)(2,1)}, f32[128,128]{0,1:T(8,128)S(1)}) fusion(f32[128,8]{0,1:T(8,128)S(1)} %get-tuple-element.5, bf16[128,4608]{1,0:T(8,128)(2,1)} %param.8, bf16[128,4608]{1,0:T(8,128)(2,1)} %param.12), kind=kOutput, calls=%fused_computation.42 | convolution fusion | flops 151027712 | bytes 2461696 | tf_op jit(solution)/shard_map/dot_general | solution.py:23
  38.5 1.3 collective-permute-done.5
  39.7 1.5 dynamic-slice_add_fusion
  42.1 3.2 %collective-permute-start.17 = (bf16[128,4608]{1,0:T(8,128)(2,1)}, bf16[128,4608]{1,0:T(8,128)(2,1)S(1)}, u32[]{:S(2)}, u32[]{:S(2)}) collective-permute-start(bf16[128,4608]{1,0:T(8,128)(2,1)} %param.8), channel_id=1, source_target_pairs={{0,12},{4,0},{8,4},{12,8},{1,13},{5,1},{9,5},{13,9},{2,14},{6,2},{... | collective-permute-start | bytes 3538952 | tf_op jit(solution)/shard_map/ppermute | solution.py:14
  46.9 1.5 collective-permute-start.7
  48.4 4.4 %collective-permute-done.7 = f32[8,2304]{1,0:T(8,128)S(1)} collective-permute-done((f32[8,2304]{1,0:T(8,128)S(1)}, f32[8,2304]{1,0:T(8,128)S(1)}, u32[]{:S(2)}, u32[]{:S(2)}) %collective-permute-start.7) | collective-permute-done | bytes 73760 | tf_op jit(solution)/shard_map/ppermute | solution.py:19
  53.6 18.6 %collective-permute-done.8 = f32[8,2304]{1,0:T(8,128)S(1)} collective-permute-done((f32[8,2304]{1,0:T(8,128)S(1)}, f32[8,2304]{1,0:T(8,128)S(1)}, u32[]{:S(2)}, u32[]{:S(2)}) %collective-permute-start.8) | collective-permute-done | bytes 73760 | tf_op jit(solution)/shard_map/ppermute | solution.py:19
  72.9 2.7 %collective-permute-start.9 = (f32[8,2304]{1,0:T(8,128)}, f32[8,2304]{1,0:T(8,128)}, u32[]{:S(2)}, u32[]{:S(2)}) collective-permute-start(f32[8,2304]{1,0:T(8,128)} %add.194), channel_id=1, source_target_pairs={{0,8},{4,12},{8,0},{12,4},{1,9},{5,13},{9,1},{13,5},{2,10},{6,14},... | collective-permute-start | bytes 221192 | tf_op jit(solution)/shard_map/ppermute | solution.py:19
  76.5 4.1 %collective-permute-start.23 = (bf16[64,4736]{1,0:T(8,128)(2,1)}, bf16[64,4736]{1,0:T(8,128)(2,1)}, u32[]{:S(2)}, u32[]{:S(2)}) collective-permute-start(bf16[64,4736]{1,0:T(8,128)(2,1)} %pad_maximum_fusion), channel_id=1, source_target_pairs={{0,2},{2,0},{1,3},{3,1},{4,6},{6,4},{5,7},{7,5},{8,10},{10,8},{9,1... | collective-permute-start | bytes 1818632 | tf_op jit(solution)/shard_map/ppermute | solution.py:19
  80.6 0.9 add.195
  81.5 1.1 collective-permute-start.10
  82.6 4.4 %broadcast_in_dim.54 = bf16[4,2,128,4608]{3,2,1,0:T(8,128)(2,1)} broadcast(bf16[]{:T(256)} %constant.105.clone.1), dimensions={} | broadcast | bytes 9437186 | tf_op jit(solution)/shard_map/broadcast_in_dim | solution.py:85
  87.1 1.1 bitcast_dynamic-update-slice_fusion.5
  88.2 21.2 %collective-permute-done.10 = f32[8,2304]{1,0:T(8,128)S(1)} collective-permute-done((f32[8,2304]{1,0:T(8,128)S(1)}, f32[8,2304]{1,0:T(8,128)S(1)}, u32[]{:S(2)}, u32[]{:S(2)}) %collective-permute-start.10) | collective-permute-done | bytes 73760 | tf_op jit(solution)/shard_map/ppermute | solution.py:19
  109.4 1.6 collective-permute-start.11
  111.0 11.7 %all_gather.3 = bf16[1024,128]{0,1:T(8,128)(2,1)S(1)} all-gather(bf16[128,128]{0,1:T(8,128)(2,1)S(1)} %copy-done.12), channel_id=1, replica_groups=mesh['x'=4,'zl'=4,'y'=4,'zh'=2,'c'=2] {'y','c'}, dimensions={0}, use_global_device_ids=true | all-gather | bytes 294912 | tf_op jit(solution)/shard_map/all_gather | solution.py:68
  123.8 1.3 fusion.31
  125.1 1.1 collective-permute-start.24
  126.2 7.4 %collective-permute-done.12 = f32[8,2304]{1,0:T(8,128)} collective-permute-done((f32[8,2304]{1,0:T(8,128)}, f32[8,2304]{1,0:T(8,128)}, u32[]{:S(2)}, u32[]{:S(2)}) %collective-permute-start.12) | collective-permute-done | bytes 73760 | tf_op jit(solution)/shard_map/ppermute | solution.py:19
  134.9 1.1 bitcast_dynamic-update-slice_fusion.8
  136.0 1.3 collective-permute-start.25
  138.0 1.1 slice.24
  139.2 3.3 %collective-permute-start.21 = (bf16[64,4608]{1,0:T(8,128)(2,1)S(1)}, bf16[64,4608]{1,0:T(8,128)(2,1)S(1)}, u32[]{:S(2)}, u32[]{:S(2)}) collective-permute-start(bf16[64,4608]{1,0:T(8,128)(2,1)S(1)} %slice.25), channel_id=1, source_target_pairs={{0,12},{4,0},{8,4},{12,8},{1,13},{5,1},{9,5},{13,9},{2,14},{6,2},{... | collective-permute-start | bytes 1769480 | tf_op jit(solution)/shard_map/ppermute | solution.py:14
  142.5 2.4 %bitcast_dynamic-update-slice_fusion.4 = bf16[4,2,128,4608]{3,2,1,0:T(8,128)(2,1)} fusion(bf16[4,2,128,4608]{3,2,1,0:T(8,128)(2,1)} %bitcast_dynamic-update-slice_fusion.5, s32[]{:T(128)S(6)} %select_n.151, s32[]{:T(128)S(6)} %select_n.139, bf16[128,4608]{1,0:T(8,128)(2,1)} %collective-permute-done.14), kind=kLoop, calls=%fused_computation.10 | loop fusion | bytes 2359304 | tf_op jit(solution)/shard_map/dynamic_update_slice | solution.py:95
  144.9 2.5 %bitcast_dynamic-update-slice_fusion.3 = bf16[4,2,128,4608]{3,2,1,0:T(8,128)(2,1)} fusion(bf16[4,2,128,4608]{3,2,1,0:T(8,128)(2,1)} %bitcast_dynamic-update-slice_fusion.4, s32[]{:T(128)S(6)} %select_n.153, s32[]{:T(128)S(6)} %select_n.138, bf16[128,4608]{1,0:T(8,128)(2,1)} %collective-permute-done.15), kind=kLoop, calls=%fused_computation.9 | loop fusion | bytes 2359304 | tf_op jit(solution)/shard_map/dynamic_update_slice | solution.py:94
  147.9 5.7 %collective-permute-done.25 = bf16[64,4736]{1,0:T(8,128)(2,1)S(1)} collective-permute-done((bf16[64,4736]{1,0:T(8,128)(2,1)}, bf16[64,4736]{1,0:T(8,128)(2,1)S(1)}, u32[]{:S(2)}, u32[]{:S(2)}) %collective-permute-start.25) | collective-permute-done | bytes 606240 | tf_op jit(solution)/shard_map/ppermute | solution.py:14
  153.7 8.7 %collective-permute-done.26 = bf16[32,4736]{1,0:T(8,128)(2,1)S(1)} collective-permute-done((bf16[32,4736]{1,0:T(8,128)(2,1)S(1)}, bf16[32,4736]{1,0:T(8,128)(2,1)S(1)}, u32[]{:S(2)}, u32[]{:S(2)}) %collective-permute-start.26) | collective-permute-done | bytes 303136 | tf_op jit(solution)/shard_map/ppermute | solution.py:14
  162.4 9.1 %collective-permute-done.27 = bf16[32,4736]{1,0:T(8,128)(2,1)S(1)} collective-permute-done((bf16[32,4736]{1,0:T(8,128)(2,1)S(1)}, bf16[32,4736]{1,0:T(8,128)(2,1)S(1)}, u32[]{:S(2)}, u32[]{:S(2)}) %collective-permute-start.27) | collective-permute-done | bytes 303136 | tf_op jit(solution)/shard_map/ppermute | solution.py:14
  172.5 1.1 bitcast_dynamic-update-slice_fusion.2
  173.6 1.1 bitcast_dynamic-update-slice_fusion.1
  174.7 1.1 bitcast_dynamic-update-slice_fusion
  179.3 6.4 %fusion.6 = bf16[1024,256]{1,0:T(8,128)(2,1)S(1)} fusion(f32[1024,256]{1,0:T(8,128)S(1)} %fusion.16, bf16[1024,4608]{1,0:T(8,128)(2,1)} %bitcast.20, bf16[256,4736]{1,0:T(8,128)(2,1)S(1)} %bitcast.81), kind=kOutput, calls=%fused_computation.5 | convolution fusion | flops 2416443392 | bytes 13369344 | tf_op jit(solution)/shard_map/dot_general | solution.py:23
  185.8 6.3 %fusion.5 = bf16[1024,256]{1,0:T(8,128)(2,1)S(1)} fusion(f32[1024,256]{1,0:T(8,128)S(1)} %copy-done.7, bf16[1024,4608]{1,0:T(8,128)(2,1)} %bitcast.20, bf16[256,4608]{1,0:T(8,128)(2,1)S(1)} %copy-done), kind=kOutput, calls=%fused_computation.4 | convolution fusion | flops 2416443392 | bytes 13369344 | tf_op jit(solution)/shard_map/dot_general | solution.py:23
  192.2 22.9 %collective-permute-done.28 = bf16[1024,256]{1,0:T(8,128)(2,1)S(1)} collective-permute-done((bf16[1024,256]{1,0:T(8,128)(2,1)S(1)}, bf16[1024,256]{1,0:T(8,128)(2,1)S(1)}, u32[]{:S(2)}, u32[]{:S(2)}) %collective-permute-start.28) | collective-permute-done | bytes 524320 | tf_op jit(solution)/shard_map/ppermute | solution.py:19
  215.2 1.0 copy.11
  (90 shorter events, 19.2 us)
Async XLA Ops:
  0.6 47.7 %copy-start = (bf16[256,4608]{1,0:T(8,128)(2,1)S(1)}, bf16[256,4608]{1,0:T(8,128)(2,1)}, u32[]{:S(2)}) copy-start(bf16[256,4608]{1,0:T(8,128)(2,1)} %param.10) | copy-start | bytes 7077892
  2.5 1.0 copy-start.3
  4.2 28.2 %copy-start.1 = (bf16[128,4608]{1,0:T(8,128)(2,1)S(1)}, bf16[128,4608]{1,0:T(8,128)(2,1)}, u32[]{:S(2)}) copy-start(bf16[128,4608]{1,0:T(8,128)(2,1)} %param.7) | copy-start | bytes 3538948
  6.1 3.9 %collective-permute-start = (bf16[4,2,128,128]{2,3,1,0:T(8,128)(2,1)}, bf16[4,2,128,128]{2,3,1,0:T(8,128)(2,1)}, u32[]{:S(2)}, u32[]{:S(2)}) collective-permute-start(bf16[4,2,128,128]{2,3,1,0:T(8,128)(2,1)} %bitcast.85), channel_id=1, source_target_pairs={{0,1},{1,0},{2,3},{3,2},{4,5},{5,4},{6,7},{7,6},{8,9},{9,8},{10,11... | collective-permute-start | bytes 786440 | tf_op jit(solution)/shard_map/ppermute | solution.py:19
  11.1 0.8 copy-start.6
  12.6 4.8 %collective-permute-start.1 = (bf16[2,128,128]{1,2,0:T(8,128)(2,1)}, bf16[2,128,128]{1,2,0:T(8,128)(2,1)}, u32[]{:S(2)}, u32[]{:S(2)}) collective-permute-start(bf16[2,128,128]{1,2,0:T(8,128)(2,1)} %get-tuple-element.2), channel_id=1, source_target_pairs={{0,4},{4,0},{8,12},{12,8},{1,5},{5,1},{9,13},{13,9},{2,6},{6,2},{1... | collective-permute-start | bytes 196616 | tf_op jit(solution)/shard_map/ppermute | solution.py:19
  14.2 7.1 %collective-permute-start.2 = (bf16[2,128,128]{1,2,0:T(8,128)(2,1)}, bf16[2,128,128]{1,2,0:T(8,128)(2,1)}, u32[]{:S(2)}, u32[]{:S(2)}) collective-permute-start(bf16[2,128,128]{1,2,0:T(8,128)(2,1)} %get-tuple-element.4), channel_id=1, source_target_pairs={{0,8},{4,12},{8,0},{12,4},{1,9},{5,13},{9,1},{13,5},{2,10},{6,14},... | collective-permute-start | bytes 196616 | tf_op jit(solution)/shard_map/ppermute | solution.py:19
  17.1 5.8 %collective-permute-start.3 = (bf16[2,128,128]{1,2,0:T(8,128)(2,1)}, bf16[2,128,128]{1,2,0:T(8,128)(2,1)}, u32[]{:S(2)}, u32[]{:S(2)}) collective-permute-start(bf16[2,128,128]{1,2,0:T(8,128)(2,1)} %get-tuple-element.3), channel_id=1, source_target_pairs={{0,12},{4,8},{8,4},{12,0},{1,13},{5,9},{9,5},{13,1},{2,14},{6,10},... | collective-permute-start | bytes 196616 | tf_op jit(solution)/shard_map/ppermute | solution.py:19
  23.9 0.7 copy-start.9
  25.2 11.3 %collective-permute-start.4 = (bf16[128,128]{0,1:T(8,128)(2,1)}, bf16[128,128]{0,1:T(8,128)(2,1)}, u32[]{:S(2)}, u32[]{:S(2)}) collective-permute-start(bf16[128,128]{0,1:T(8,128)(2,1)} %fusion.20), channel_id=1, source_target_pairs={{0,2},{2,0},{1,3},{3,1},{4,6},{6,4},{5,7},{7,5},{8,10},{10,8},{9,1... | collective-permute-start | bytes 98312 | tf_op jit(solution)/shard_map/ppermute | solution.py:19
  33.7 2.8 %copy-start.10 = (f32[2,128,128]{1,2,0:T(8,128)S(1)}, f32[2,128,128]{1,2,0:T(8,128)}, u32[]{:S(2)}) copy-start(f32[2,128,128]{1,2,0:T(8,128)} %copy-done.9) | copy-start | bytes 393220
  37.8 0.7 copy-start.8
  38.5 1.3 collective-permute-start.5
  41.3 4.7 %collective-permute-start.6 = (f32[8,2304]{1,0:T(8,128)}, f32[8,2304]{1,0:T(8,128)}, u32[]{:S(2)}, u32[]{:S(2)}) collective-permute-start(f32[8,2304]{1,0:T(8,128)} %dynamic-slice_add_fusion), channel_id=1, source_target_pairs={{0,64},{64,0},{128,192},{192,128},{1,65},{65,1},{129,193},{193,129... | collective-permute-start | bytes 221192 | tf_op jit(solution)/shard_map/ppermute | solution.py:19
  42.1 100.4 %collective-permute-start.14 = (bf16[128,4608]{1,0:T(8,128)(2,1)}, bf16[128,4608]{1,0:T(8,128)(2,1)}, u32[]{:S(2)}, u32[]{:S(2)}) collective-permute-start(bf16[128,4608]{1,0:T(8,128)(2,1)} %param.8), channel_id=1, source_target_pairs={{0,1},{1,0},{2,3},{3,2},{4,5},{5,4},{6,7},{7,6},{8,9},{9,8},{10,11... | collective-permute-start | bytes 3538952 | tf_op jit(solution)/shard_map/ppermute | solution.py:19
  42.1 95.9 %collective-permute-start.15 = (bf16[128,4608]{1,0:T(8,128)(2,1)}, bf16[128,4608]{1,0:T(8,128)(2,1)}, u32[]{:S(2)}, u32[]{:S(2)}) collective-permute-start(bf16[128,4608]{1,0:T(8,128)(2,1)} %param.8), channel_id=1, source_target_pairs={{0,4},{4,8},{8,12},{12,0},{1,5},{5,9},{9,13},{13,1},{2,6},{6,10},{... | collective-permute-start | bytes 3538952 | tf_op jit(solution)/shard_map/ppermute | solution.py:14
  42.1 97.1 %collective-permute-start.17 = (bf16[128,4608]{1,0:T(8,128)(2,1)}, bf16[128,4608]{1,0:T(8,128)(2,1)S(1)}, u32[]{:S(2)}, u32[]{:S(2)}) collective-permute-start(bf16[128,4608]{1,0:T(8,128)(2,1)} %param.8), channel_id=1, source_target_pairs={{0,12},{4,0},{8,4},{12,8},{1,13},{5,1},{9,5},{13,9},{2,14},{6,2},{... | collective-permute-start | bytes 3538952 | tf_op jit(solution)/shard_map/ppermute | solution.py:14
  46.9 5.9 %collective-permute-start.7 = (f32[8,2304]{1,0:T(8,128)S(1)}, f32[8,2304]{1,0:T(8,128)S(1)}, u32[]{:S(2)}, u32[]{:S(2)}) collective-permute-start(f32[8,2304]{1,0:T(8,128)S(1)} %add.192), channel_id=1, source_target_pairs={{0,128},{64,192},{128,0},{192,64},{1,129},{65,193},{129,1},{193,65... | collective-permute-start | bytes 221192 | tf_op jit(solution)/shard_map/ppermute | solution.py:19
  52.8 19.4 %collective-permute-start.8 = (f32[8,2304]{1,0:T(8,128)S(1)}, f32[8,2304]{1,0:T(8,128)S(1)}, u32[]{:S(2)}, u32[]{:S(2)}) collective-permute-start(f32[8,2304]{1,0:T(8,128)S(1)} %add.193), channel_id=1, source_target_pairs={{0,4},{4,0},{8,12},{12,8},{1,5},{5,1},{9,13},{13,9},{2,6},{6,2},{1... | collective-permute-start | bytes 221192 | tf_op jit(solution)/shard_map/ppermute | solution.py:19
  72.9 7.7 %collective-permute-start.9 = (f32[8,2304]{1,0:T(8,128)}, f32[8,2304]{1,0:T(8,128)}, u32[]{:S(2)}, u32[]{:S(2)}) collective-permute-start(f32[8,2304]{1,0:T(8,128)} %add.194), channel_id=1, source_target_pairs={{0,8},{4,12},{8,0},{12,4},{1,9},{5,13},{9,1},{13,5},{2,10},{6,14},... | collective-permute-start | bytes 221192 | tf_op jit(solution)/shard_map/ppermute | solution.py:19
  76.5 48.6 %collective-permute-start.23 = (bf16[64,4736]{1,0:T(8,128)(2,1)}, bf16[64,4736]{1,0:T(8,128)(2,1)}, u32[]{:S(2)}, u32[]{:S(2)}) collective-permute-start(bf16[64,4736]{1,0:T(8,128)(2,1)} %pad_maximum_fusion), channel_id=1, source_target_pairs={{0,2},{2,0},{1,3},{3,1},{4,6},{6,4},{5,7},{7,5},{8,10},{10,8},{9,1... | collective-permute-start | bytes 1818632 | tf_op jit(solution)/shard_map/ppermute | solution.py:19
  81.5 5.6 %copy-start.2 = (bf16[128,4608]{1,0:T(8,128)(2,1)S(1)}, bf16[128,4608]{1,0:T(8,128)(2,1)}, u32[]{:S(2)}) copy-start(bf16[128,4608]{1,0:T(8,128)(2,1)} %param.8) | copy-start | bytes 3538948
  81.5 27.9 %collective-permute-start.10 = (f32[8,2304]{1,0:T(8,128)S(1)}, f32[8,2304]{1,0:T(8,128)S(1)}, u32[]{:S(2)}, u32[]{:S(2)}) collective-permute-start(f32[8,2304]{1,0:T(8,128)S(1)} %add.195), channel_id=1, source_target_pairs={{0,16},{16,0},{32,48},{48,32},{1,17},{17,1},{33,49},{49,33},{2,18}... | collective-permute-start | bytes 221192 | tf_op jit(solution)/shard_map/ppermute | solution.py:19
  87.1 23.9 %copy-start.12 = (bf16[128,128]{0,1:T(8,128)(2,1)S(1)}, bf16[128,128]{0,1:T(8,128)(2,1)}, u32[]{:S(2)}) copy-start(bf16[128,128]{0,1:T(8,128)(2,1)} %get-tuple-element.7) | copy-start | bytes 98308
  87.1 36.7 %copy-start.11 = (bf16[256,128]{1,0:T(8,128)(2,1)S(1)}, bf16[256,128]{1,0:T(8,128)(2,1)}, u32[]{:S(2)}) copy-start(bf16[256,128]{1,0:T(8,128)(2,1)} %param.11) | copy-start | bytes 196612
  109.4 13.2 %collective-permute-start.11 = (f32[8,2304]{1,0:T(8,128)S(1)}, f32[8,2304]{1,0:T(8,128)S(1)}, u32[]{:S(2)}, u32[]{:S(2)}) collective-permute-start(f32[8,2304]{1,0:T(8,128)S(1)} %add.196), channel_id=1, source_target_pairs={{0,32},{16,48},{32,0},{48,16},{1,33},{17,49},{33,1},{49,17},{2,34}... | collective-permute-start | bytes 221192 | tf_op jit(solution)/shard_map/ppermute | solution.py:19
  122.7 1.1 copy-start.4
  123.4 10.3 %collective-permute-start.12 = (f32[8,2304]{1,0:T(8,128)}, f32[8,2304]{1,0:T(8,128)}, u32[]{:S(2)}, u32[]{:S(2)}) collective-permute-start(f32[8,2304]{1,0:T(8,128)} %add.197), channel_id=1, source_target_pairs={{0,2},{2,0},{1,3},{3,1},{4,6},{6,4},{5,7},{7,5},{8,10},{10,8},{9,1... | collective-permute-start | bytes 221192 | tf_op jit(solution)/shard_map/ppermute | solution.py:19
  125.1 22.3 %collective-permute-start.24 = (bf16[64,4736]{1,0:T(8,128)(2,1)}, bf16[64,4736]{1,0:T(8,128)(2,1)S(1)}, u32[]{:S(2)}, u32[]{:S(2)}) collective-permute-start(bf16[64,4736]{1,0:T(8,128)(2,1)} %collective-permute-done.23), channel_id=1, source_target_pairs={{0,64},{64,128},{128,192},{192,0},{1,65},{65,129},{129,193},{193,1... | collective-permute-start | bytes 1818632 | tf_op jit(solution)/shard_map/ppermute | solution.py:14
  134.6 1.4 collective-permute-start.13
  136.0 17.6 %collective-permute-start.25 = (bf16[64,4736]{1,0:T(8,128)(2,1)}, bf16[64,4736]{1,0:T(8,128)(2,1)S(1)}, u32[]{:S(2)}, u32[]{:S(2)}) collective-permute-start(bf16[64,4736]{1,0:T(8,128)(2,1)} %collective-permute-done.23), channel_id=1, source_target_pairs={{0,192},{64,0},{128,64},{192,128},{1,193},{65,1},{129,65},{193,129... | collective-permute-start | bytes 1818632 | tf_op jit(solution)/shard_map/ppermute | solution.py:14
  139.1 32.8 %collective-permute-start.19 = (bf16[64,4608]{1,0:T(8,128)(2,1)S(1)}, bf16[64,4608]{1,0:T(8,128)(2,1)S(1)}, u32[]{:S(2)}, u32[]{:S(2)}) collective-permute-start(bf16[64,4608]{1,0:T(8,128)(2,1)S(1)} %slice.24), channel_id=1, source_target_pairs={{0,4},{4,8},{8,12},{12,0},{1,5},{5,9},{9,13},{13,1},{2,6},{6,10},{... | collective-permute-start | bytes 1769480 | tf_op jit(solution)/shard_map/ppermute | solution.py:14
  139.2 32.8 %collective-permute-start.21 = (bf16[64,4608]{1,0:T(8,128)(2,1)S(1)}, bf16[64,4608]{1,0:T(8,128)(2,1)S(1)}, u32[]{:S(2)}, u32[]{:S(2)}) collective-permute-start(bf16[64,4608]{1,0:T(8,128)(2,1)S(1)} %slice.25), channel_id=1, source_target_pairs={{0,12},{4,0},{8,4},{12,8},{1,13},{5,1},{9,5},{13,9},{2,14},{6,2},{... | collective-permute-start | bytes 1769480 | tf_op jit(solution)/shard_map/ppermute | solution.py:14
  142.5 30.0 %collective-permute-start.16 = (bf16[128,4608]{1,0:T(8,128)(2,1)}, bf16[128,4608]{1,0:T(8,128)(2,1)S(1)}, u32[]{:S(2)}, u32[]{:S(2)}) collective-permute-start(bf16[128,4608]{1,0:T(8,128)(2,1)} %collective-permute-done.15), channel_id=1, source_target_pairs={{0,1},{1,0},{2,3},{3,2},{4,5},{5,4},{6,7},{7,6},{8,9},{9,8},{10,11... | collective-permute-start | bytes 3538952 | tf_op jit(solution)/shard_map/ppermute | solution.py:19
  147.4 24.2 %copy-start.5 = (bf16[1024,128]{0,1:T(8,128)(2,1)S(1)}, bf16[1024,128]{0,1:T(8,128)(2,1)}, u32[]{:S(2)}) copy-start(bf16[1024,128]{0,1:T(8,128)(2,1)} %copy-done.4) | copy-start | bytes 786436
  147.4 27.4 %collective-permute-start.18 = (bf16[128,4608]{1,0:T(8,128)(2,1)S(1)}, bf16[128,4608]{1,0:T(8,128)(2,1)S(1)}, u32[]{:S(2)}, u32[]{:S(2)}) collective-permute-start(bf16[128,4608]{1,0:T(8,128)(2,1)S(1)} %collective-permute-done.17), channel_id=1, source_target_pairs={{0,1},{1,0},{2,3},{3,2},{4,5},{5,4},{6,7},{7,6},{8,9},{9,8},{10,11... | collective-permute-start | bytes 3538952 | tf_op jit(solution)/shard_map/ppermute | solution.py:19
  153.6 8.8 %collective-permute-start.26 = (bf16[32,4736]{1,0:T(8,128)(2,1)S(1)}, bf16[32,4736]{1,0:T(8,128)(2,1)S(1)}, u32[]{:S(2)}, u32[]{:S(2)}) collective-permute-start(bf16[32,4736]{1,0:T(8,128)(2,1)S(1)} %slice.26), channel_id=1, source_target_pairs={{0,64},{64,128},{128,192},{192,0},{1,65},{65,129},{129,193},{193,1... | collective-permute-start | bytes 909320 | tf_op jit(solution)/shard_map/ppermute | solution.py:14
  162.4 9.1 %collective-permute-start.27 = (bf16[32,4736]{1,0:T(8,128)(2,1)S(1)}, bf16[32,4736]{1,0:T(8,128)(2,1)S(1)}, u32[]{:S(2)}, u32[]{:S(2)}) collective-permute-start(bf16[32,4736]{1,0:T(8,128)(2,1)S(1)} %slice.27), channel_id=1, source_target_pairs={{0,192},{64,0},{128,64},{192,128},{1,193},{65,1},{129,65},{193,129... | collective-permute-start | bytes 909320 | tf_op jit(solution)/shard_map/ppermute | solution.py:14
  171.9 4.8 %collective-permute-start.20 = (bf16[64,4608]{1,0:T(8,128)(2,1)S(1)}, bf16[64,4608]{1,0:T(8,128)(2,1)S(1)}, u32[]{:S(2)}, u32[]{:S(2)}) collective-permute-start(bf16[64,4608]{1,0:T(8,128)(2,1)S(1)} %collective-permute-done.19), channel_id=1, source_target_pairs={{0,1},{1,0},{2,3},{3,2},{4,5},{5,4},{6,7},{7,6},{8,9},{9,8},{10,11... | collective-permute-start | bytes 1769480 | tf_op jit(solution)/shard_map/ppermute | solution.py:19
  172.0 6.4 %collective-permute-start.22 = (bf16[64,4608]{1,0:T(8,128)(2,1)S(1)}, bf16[64,4608]{1,0:T(8,128)(2,1)S(1)}, u32[]{:S(2)}, u32[]{:S(2)}) collective-permute-start(bf16[64,4608]{1,0:T(8,128)(2,1)S(1)} %collective-permute-done.21), channel_id=1, source_target_pairs={{0,1},{1,0},{2,3},{3,2},{4,5},{5,4},{6,7},{7,6},{8,9},{9,8},{10,11... | collective-permute-start | bytes 1769480 | tf_op jit(solution)/shard_map/ppermute | solution.py:19
  179.3 6.5 %copy-start.7 = (f32[1024,256]{1,0:T(8,128)S(1)}, f32[1024,256]{1,0:T(8,128)}, u32[]{:S(2)}) copy-start(f32[1024,256]{1,0:T(8,128)} %fusion.31) | copy-start | bytes 3145732
  185.7 29.3 %collective-permute-start.28 = (bf16[1024,256]{1,0:T(8,128)(2,1)S(1)}, bf16[1024,256]{1,0:T(8,128)(2,1)S(1)}, u32[]{:S(2)}, u32[]{:S(2)}) collective-permute-start(bf16[1024,256]{1,0:T(8,128)(2,1)S(1)} %fusion.6), channel_id=1, source_target_pairs={{0,2},{2,0},{1,3},{3,1},{4,6},{6,4},{5,7},{7,5},{8,10},{10,8},{9,1... | collective-permute-start | bytes 1572872 | tf_op jit(solution)/shard_map/ppermute | solution.py:19

commit v2 on v1

v2 whole, which is shorter than its diff:
```python
import functools

import jax
import jax.numpy as jnp
from jax import lax
from jax.experimental import pallas as pl
from jax.experimental.pallas import tpu as pltpu
from jax.sharding import Mesh
from jax.sharding import PartitionSpec as P

F32 = jnp.float32
BF16 = jnp.bfloat16
AXES = ("x", "zl", "y", "zh", "c")
VMEM = pl.BlockSpec(memory_space=pltpu.VMEM)
SMEM = pl.BlockSpec(memory_space=pltpu.SMEM)
ANY = pl.BlockSpec(memory_space=pl.ANY)
PARAMS = pltpu.CompilerParams(vmem_limit_bytes=48 * 1024 * 1024)


def shift(value, axis, by):
    size = lax.axis_size(axis)
    return lax.ppermute(value, axis, [(i, (i + by) % size) for i in range(size)])


def swap(value, axis, mask):
    size = lax.axis_size(axis)
    return lax.ppermute(value, axis, [(i, i ^ mask) for i in range(size)])


def dot_t(left, right, precision=None):
    return lax.dot_general(
        left, right, (((1,), (1,)), ((), ())), precision=precision, preferred_element_type=F32
    )


def shaped(shape, dtype):
    return jax.ShapeDtypeStruct(shape, dtype)


def cost(flops, moved):
    return pl.CostEstimate(flops=flops, bytes_accessed=moved, transcendentals=0)


def membership(adapters, stacked):
    row = lax.broadcasted_iota(jnp.int32, (adapters, stacked), 0)
    column = lax.broadcasted_iota(jnp.int32, (adapters, stacked), 1)
    low = row * (stacked // adapters)
    return jnp.where((column >= low) & (column < low + stacked // adapters), 1.0, 0.0)


def token_kernel(at, hidden, grad, up, gate, weight, down, tokens_out, piece, gates, back, sems):
    width = grad.shape[1]
    stacked = up.shape[0]
    quarter = piece.shape[0]
    rows = pl.ds(pl.multiple_of(at[0] * quarter, quarter), quarter)
    copies = [
        pltpu.make_async_copy(weight.at[rows], piece.at[:, pl.ds(0, width)], sems.at[0]),
        pltpu.make_async_copy(down.at[rows], piece.at[:, pl.ds(width, stacked)], sems.at[1]),
    ]
    for copy in copies:
        copy.start()
    ones = membership(gate.shape[0], stacked)
    gates[...] = jax.nn.sigmoid(dot_t(gate[...], hidden[...]))
    wide = lax.dot_general(
        ones.astype(BF16), gate[...], (((0,), (0,)), ((), ())), preferred_element_type=F32
    ).astype(BF16)
    pulled = dot_t(grad[...], up[...])
    back[...] = pulled
    mixed = 2.0 * jax.nn.sigmoid(dot_t(hidden[...], wide)) * pulled
    tokens_out[:, pl.ds(0, width)] = grad[...]
    tokens_out[:, pl.ds(width, stacked)] = mixed.astype(BF16)
    for copy in copies:
        copy.wait()


def act_kernel(at, mixture, down, tie, keep, give):
    c = at[3]
    blocks, _, tokens, depth = mixture.shape
    for out, side in ((give, 1 - c), (keep, c)):
        rows = mixture[:, side].reshape(blocks * tokens, depth)
        value = jnp.dot(rows, down[...], preferred_element_type=F32)
        out[...] = value.reshape(out.shape).astype(out.dtype)


def act_y_kernel(at, keep, got, first, second, third, rest):
    y = at[1]
    for out, mask in ((first, 1), (second, 2), (third, 3), (rest, 0)):
        row = jnp.bitwise_xor(y, mask)
        out[...] = (keep[row] + got[row].astype(F32)).astype(out.dtype)


def act_z_kernel(at, rest, first, second, third, keep, give):
    zh = at[2]
    for out, side in ((give, 1 - zh), (keep, zh)):
        total = (rest[side] + first[side].astype(F32)) + (
            second[side].astype(F32) + third[side].astype(F32)
        )
        out[...] = total.astype(out.dtype)


def gate_kernel(at, keep, got, back, gates, hidden, result, give):
    stacked = keep.shape[1]
    adapters = gates.shape[0]
    half = result.shape[1]
    product = (keep[...] + got[...].astype(F32)) * back[...]
    ones = membership(adapters, stacked)
    delta = 2.0 * dot_t(ones, product, lax.Precision.HIGHEST)
    dlogit = delta * gates[...] * (1.0 - gates[...])
    top = dlogit.astype(BF16).astype(F32)
    middle = (dlogit - top).astype(BF16).astype(F32)
    parts = jnp.concatenate([top, middle, dlogit - top - middle], axis=0).astype(BF16)
    c = at[3]
    for out, side in ((result, c), (give, 1 - c)):
        columns = pl.ds(pl.multiple_of(side * half, 128), half)
        total = jnp.dot(parts, hidden[:, columns], preferred_element_type=F32)
        out[...] = total[:adapters] + (
            total[adapters : 2 * adapters] + total[2 * adapters :]
        )


def gather_tokens(at, refs, held, sems):
    own, own_s, low, low_s, high, high_s, top, top_s, bottom, bottom_s = refs
    y, c = at[1], at[3]
    half = top.shape[0]
    full = pl.ds(0, own.shape[0])
    plan = (
        (0, ((own, c, full), (own_s, 1 - c, full))),
        (3, ((low, c, full), (low_s, 1 - c, full))),
        (1, ((high, c, full), (high_s, 1 - c, full))),
        (
            2,
            (
                (top, c, pl.ds(0, half)),
                (top_s, 1 - c, pl.ds(0, half)),
                (bottom, c, pl.ds(half, half)),
                (bottom_s, 1 - c, pl.ds(half, half)),
            ),
        ),
    )
    out, number = [], 0
    for step, parts in plan:
        row = lax.rem(y + step, 4)
        copies = []
        for ref, core, rows in parts:
            copies.append(pltpu.make_async_copy(ref, held.at[row, core, rows], sems.at[number]))
            copies[-1].start()
            number += 1
        out.append((row, copies))
    return out


def products(steps, held, weights, out):
    depth = held.shape[3]
    rows = held.shape[1] * held.shape[2]
    for row, copies in steps:
        for copy in copies:
            copy.wait()
        value = dot_t(held[row].reshape(rows, depth), weights())
        out[row] = value.astype(out.dtype)


def far_kernel(at, *refs):
    blocks, (piece, low, high, top, bottom), (out, held, weight, sems, weight_sems) = (
        refs[:10],
        refs[10:15],
        refs[15:],
    )
    x = at[0]
    half = top.shape[0]
    full = pl.ds(0, piece.shape[0])
    copies = []
    for number, (step, ref, rows) in enumerate(
        (
            (0, piece, full),
            (3, low, full),
            (1, high, full),
            (2, top, pl.ds(0, half)),
            (2, bottom, pl.ds(half, half)),
        )
    ):
        copies.append(
            pltpu.make_async_copy(
                ref, weight.at[lax.rem(x + step, 4), rows], weight_sems.at[number]
            )
        )
        copies[-1].start()
    steps = gather_tokens(at, blocks, held, sems)
    for copy in copies:
        copy.wait()
    depth = weight.shape[2]
    products(steps, held, lambda: weight[...].reshape(-1, depth), out)


def own_kernel(at, *refs):
    blocks, (first, second), (out, held, weight, result, sems, weight_sems) = (
        refs[:10],
        refs[10:12],
        refs[13:],
    )
    width = first.shape[1]
    copies = [
        pltpu.make_async_copy(first, weight.at[:, pl.ds(0, width)], weight_sems.at[0]),
        pltpu.make_async_copy(
            second, weight.at[:, pl.ds(width, second.shape[1])], weight_sems.at[1]
        ),
    ]
    for copy in copies:
        copy.start()
    steps = gather_tokens(at, blocks, held, sems)
    for copy in copies:
        copy.wait()
    products(steps, held, lambda: weight[...], result)
    copy = pltpu.make_async_copy(result, out.at[:, at[2]], weight_sems.at[2])
    copy.start()
    copy.wait()


def ring_gather(piece, axis):
    half = piece.shape[0] // 2
    low = shift(piece, axis, 1)
    high = shift(piece, axis, -1)
    return low, high, shift(low[:half], axis, 1), shift(high[half:], axis, -1)


def on_device(hidden, grad, mixture, weight, down, up, gate_matrix):
    tokens, width = grad.shape
    adapters = gate_matrix.shape[0]
    stacked = up.shape[0]
    features = weight.shape[0]
    depth = width + stacked
    quarter = features // 4
    at = jnp.stack([lax.axis_index(a) for a in ("x", "y", "zh", "c")]).astype(jnp.int32)
    c, zh = at[3], at[2]

    own, piece, gates, back = pl.pallas_call(
        token_kernel,
        in_specs=[SMEM, VMEM, VMEM, VMEM, VMEM, ANY, ANY],
        out_specs=[VMEM, ANY, VMEM, VMEM],
        out_shape=[
            shaped((tokens, depth), BF16),
            shaped((quarter, depth), BF16),
            shaped((adapters, tokens), F32),
            shaped((tokens, stacked), F32),
        ],
        scratch_shapes=[pltpu.SemaphoreType.DMA((2,))],
        compiler_params=PARAMS,
        cost_estimate=cost(6 * tokens * width * stacked, 12 * tokens * width),
        name="token_values",
    )(at, hidden, grad, up, gate_matrix, weight, down)

    far_piece = swap(piece, "zh", 1)
    low, high, top, bottom = ring_gather(own, "y")
    blocks = []
    for block in (own, low, high, top, bottom):
        blocks += [block, swap(block, "c", 1)]

    keep, give = pl.pallas_call(
        act_kernel,
        in_specs=[SMEM, VMEM, VMEM, ANY],
        out_specs=[VMEM, VMEM],
        out_shape=[
            shaped((4, 2, tokens, stacked), F32),
            shaped((4, 2, tokens, stacked), BF16),
        ],
        compiler_params=PARAMS,
        cost_estimate=cost(2 * mixture.size * stacked, 4 * mixture.size),
        name="rank_products",
    )(at, mixture.reshape(8, 2, tokens, -1), down, own)
    first, second, third, rest = pl.pallas_call(
        act_y_kernel,
        in_specs=[SMEM, VMEM, VMEM],
        out_specs=[VMEM] * 4,
        out_shape=[shaped((2, tokens, stacked), BF16)] * 3 + [shaped((2, tokens, stacked), F32)],
        compiler_params=PARAMS,
        name="rank_sum_core",
    )(at, keep, swap(give, "c", 1))
    keep, give = pl.pallas_call(
        act_z_kernel,
        in_specs=[SMEM] + [VMEM] * 4,
        out_specs=[VMEM, VMEM],
        out_shape=[shaped((tokens, stacked), F32), shaped((tokens, stacked), BF16)],
        compiler_params=PARAMS,
        name="rank_sum_y",
    )(at, rest, swap(first, "y", 1), swap(second, "y", 2), swap(third, "y", 3))

    total, give = pl.pallas_call(
        gate_kernel,
        in_specs=[SMEM] + [VMEM] * 5,
        out_specs=[VMEM, VMEM],
        out_shape=[shaped((adapters, width // 2), F32)] * 2,
        compiler_params=PARAMS,
        name="gate_products",
    )(at, keep, swap(give, "zh", 1), back, gates, hidden)
    total = total + swap(give, "c", 1)
    for axis, mask in (("x", 1), ("x", 2), ("y", 1), ("y", 2), ("zl", 1), ("zl", 2), ("zh", 1)):
        total = total + swap(total, axis, mask)
    other = swap(total, "c", 1)
    gate_grad = jnp.where(
        c == 0, jnp.concatenate([total, other], axis=1), jnp.concatenate([other, total], axis=1)
    )

    held = pltpu.VMEM((4, 2, tokens, depth), BF16)
    matmul_cost = cost(16 * tokens * depth * features, 24 * tokens * depth)
    far = pl.pallas_call(
        far_kernel,
        in_specs=[SMEM] + [ANY] * 15,
        out_specs=VMEM,
        out_shape=shaped((4, 2 * tokens, features), BF16),
        scratch_shapes=[
            held,
            pltpu.VMEM((4, quarter, depth), BF16),
            pltpu.SemaphoreType.DMA((10,)),
            pltpu.SemaphoreType.DMA((5,)),
        ],
        compiler_params=PARAMS,
        cost_estimate=matmul_cost,
        name="far_products",
    )(at, *blocks, far_piece, *ring_gather(far_piece, "x"))
    got = swap(far, "zh", 1)
    out = pl.pallas_call(
        own_kernel,
        in_specs=[SMEM] + [ANY] * 13,
        out_specs=ANY,
        out_shape=shaped((4, 2, 2 * tokens, features), BF16),
        scratch_shapes=[
            held,
            pltpu.VMEM((features, depth), BF16),
            pltpu.VMEM((4, 2 * tokens, features), BF16),
            pltpu.SemaphoreType.DMA((10,)),
            pltpu.SemaphoreType.DMA((3,)),
        ],
        compiler_params=PARAMS,
        cost_estimate=matmul_cost,
        name="own_products",
    )(at, *blocks, weight, down, far)
    out = lax.dynamic_update_slice(out, got[:, None], (0, 1 - zh, 0, 0))
    return gate_grad, out.reshape(16 * tokens, features)


def solution(mesh):
    grid = Mesh(mesh.devices.reshape(4, 4, 4, 2, 2), AXES)
    dp, tensor = ("x", "zl"), ("y", "zh", "c")
    return jax.shard_map(
        on_device,
        mesh=grid,
        in_specs=(
            P(AXES, None),
            P(AXES, None),
            P(dp, tensor),
            P(tensor, None),
            P(tensor, None),
            P(),
            P(),
        ),
        out_specs=(P(), P(dp, tensor)),
        check_vma=False,
    )
```

time: 217 us -> 175 us (0.81)
  the two profiles are of different devices: /device:TPU:6 before, /device:TPU:1 now
where the time goes in v2:
time: 175 us; the launch traced here: 174 us
  starting transfers between devices  75.1 us (43%)
  waiting for transfers between devices  58.4 us (33%)
  Pallas kernels  23.2 us (13%)
  local copies, waits for them, and re-layouts  15.6 us (9%)
    ppermute x21, starting transfers between devices, swap(): return lax.ppermute(value, axis, [(i, i ^ mask) for i in range(size)])  60.8 us
    ppermute x21, waiting for transfers between devices, swap(): return lax.ppermute(value, axis, [(i, i ^ mask) for i in range(size)])  52.3 us
    ppermute x8, starting transfers between devices, shift(): lax.ppermute(value, axis, [(i, (i + by) % size) for i in range(size)])  14.3 us
    unnamed x36, local copies, waits for them, and re-layouts  11.8 us
    pallas_call x1, Pallas kernels, on_device(): pl.pallas_call(own_kernel, in_specs=[SMEM] + [ANY] * 13, out_specs=ANY, o...  8.98 us
    pallas_call x1, Pallas kernels, on_device(): pl.pallas_call(far_kernel, in_specs=[SMEM] + [ANY] * 15, out_specs=VMEM,...  8.8 us
    ppermute x8, waiting for transfers between devices, shift(): lax.ppermute(value, axis, [(i, (i + by) % size) for i in range(size)])  6.14 us
  transfers between devices with their start and end apart: 29, of which 14 were waited for; matrix products, arithmetic and copies ran while one was open for 2% of the time, Pallas kernels for 12%

profile of v2, /device:TPU:1, one launch (start us, length us, event | category | flops | bytes accessed | tf_op | source)
XLA Modules:
  0.0 173.9 jit_solution(7672100446549641011)
XLA Ops:
  0.7 1.3 copy-done.4
  2.0 1.3 copy-done.10
  3.3 1.3 copy-done.11
  6.3 2.0 %token_values.1 = (bf16[128,4736]{1,0:T(8,128)(2,1)S(1)}, bf16[64,4736]{1,0:T(8,128)(2,1)S(1)}, f32[8,128]{1,0:T(8,128)S(1)}, f32[128,128]{1,0:T(8,128)S(1)}) custom-call(s32[4]{0:T(128)S(1)} %pad_add_fusion.at, bf16[128,4608]{1,0:T(8,128)(2,1)S(1)} %copy-done.4, bf16[128,4608]{1,0:T(8,128)(2,1)S(1)} %copy-done.10, bf16[128,4608]{1,0:T(8,128)(2,1)S(1)} %copy-done.11, ...), custom_call_target="tpu_custom_call" | custom-call | flops 452984832 | bytes 7077888 | tf_op jit(solution)/shard_map/token_values/pallas_call | solution.py:235
  8.3 2.2 %collective-permute-start.15 = (bf16[128,4736]{1,0:T(8,128)(2,1)S(1)}, bf16[128,4736]{1,0:T(8,128)(2,1)}, u32[]{:S(2)}, u32[]{:S(2)}) collective-permute-start(bf16[128,4736]{1,0:T(8,128)(2,1)S(1)} %get-tuple-element.16.tie.refs_0_), channel_id=1, source_target_pairs={{0,4},{4,8},{8,12},{12,0},{1,5},{5,9},{9,13},{13,1},{2,6},{6,10},{... | collective-permute-start | bytes 3637256 | tf_op jit(solution)/shard_map/ppermute | solution.py:22
  10.5 1.5 collective-permute-start.17
  12.0 2.8 %collective-permute-start.14 = (bf16[128,4736]{1,0:T(8,128)(2,1)S(1)}, bf16[128,4736]{1,0:T(8,128)(2,1)S(1)}, u32[]{:S(2)}, u32[]{:S(2)}) collective-permute-start(bf16[128,4736]{1,0:T(8,128)(2,1)S(1)} %get-tuple-element.16.tie.refs_0_), channel_id=1, source_target_pairs={{0,1},{1,0},{2,3},{3,2},{4,5},{5,4},{6,7},{7,6},{8,9},{9,8},{10,11... | collective-permute-start | bytes 3637256 | tf_op jit(solution)/shard_map/ppermute | solution.py:27
  14.9 5.2 %collective-permute-start.23 = (bf16[64,4736]{1,0:T(8,128)(2,1)S(1)}, bf16[64,4736]{1,0:T(8,128)(2,1)S(1)}, u32[]{:S(2)}, u32[]{:S(2)}) collective-permute-start(bf16[64,4736]{1,0:T(8,128)(2,1)S(1)} %get-tuple-element.29), channel_id=1, source_target_pairs={{0,2},{2,0},{1,3},{3,1},{4,6},{6,4},{5,7},{7,5},{8,10},{10,8},{9,1... | collective-permute-start | bytes 1818632 | tf_op jit(solution)/shard_map/ppermute | solution.py:27
  20.0 1.0 rank_products.1
  21.4 1.3 collective-permute-done.got
  23.4 15.6 %collective-permute-done.1.first = bf16[2,128,128]{2,1,0:T(8,128)(2,1)S(1)} collective-permute-done((bf16[2,128,128]{2,1,0:T(8,128)(2,1)S(1)}, bf16[2,128,128]{2,1,0:T(8,128)(2,1)S(1)}, u32[]{:S(2)}, u32[]{:S(2)}) %collective-permute-start.1) | collective-permute-done | bytes 65568 | tf_op jit(solution)/shard_map/ppermute | solution.py:27
  39.0 2.9 %collective-permute-start.2 = (bf16[2,128,128]{2,1,0:T(8,128)(2,1)S(1)}, bf16[2,128,128]{2,1,0:T(8,128)(2,1)S(1)}, u32[]{:S(2)}, u32[]{:S(2)}) collective-permute-start(bf16[2,128,128]{2,1,0:T(8,128)(2,1)S(1)} %get-tuple-element.21), channel_id=1, source_target_pairs={{0,8},{4,12},{8,0},{12,4},{1,9},{5,13},{9,1},{13,5},{2,10},{6,14},... | collective-permute-start | bytes 196616 | tf_op jit(solution)/shard_map/ppermute | solution.py:27
  41.9 1.7 collective-permute-done.2.second
  43.6 2.0 %collective-permute-start.3 = (bf16[2,128,128]{2,1,0:T(8,128)(2,1)S(1)}, bf16[2,128,128]{2,1,0:T(8,128)(2,1)S(1)}, u32[]{:S(2)}, u32[]{:S(2)}) collective-permute-start(bf16[2,128,128]{2,1,0:T(8,128)(2,1)S(1)} %get-tuple-element.22), channel_id=1, source_target_pairs={{0,12},{4,8},{8,4},{12,0},{1,13},{5,9},{9,5},{13,1},{2,14},{6,10},... | collective-permute-start | bytes 196616 | tf_op jit(solution)/shard_map/ppermute | solution.py:27
  45.6 2.3 %collective-permute-done.3.third = bf16[2,128,128]{2,1,0:T(8,128)(2,1)S(1)} collective-permute-done((bf16[2,128,128]{2,1,0:T(8,128)(2,1)S(1)}, bf16[2,128,128]{2,1,0:T(8,128)(2,1)S(1)}, u32[]{:S(2)}, u32[]{:S(2)}) %collective-permute-start.3) | collective-permute-done | bytes 65568 | tf_op jit(solution)/shard_map/ppermute | solution.py:27
  48.5 7.3 %collective-permute-start.4 = (bf16[128,128]{1,0:T(8,128)(2,1)S(1)}, bf16[128,128]{1,0:T(8,128)(2,1)S(1)}, u32[]{:S(2)}, u32[]{:S(2)}) collective-permute-start(bf16[128,128]{1,0:T(8,128)(2,1)S(1)} %get-tuple-element.24), channel_id=1, source_target_pairs={{0,2},{2,0},{1,3},{3,1},{4,6},{6,4},{5,7},{7,5},{8,10},{10,8},{9,1... | collective-permute-start | bytes 98312 | tf_op jit(solution)/shard_map/ppermute | solution.py:27
  55.8 1.5 collective-permute-start.24
  57.3 1.2 gate_products.1
  58.5 4.8 %collective-permute-start.5 = (f32[8,2304]{1,0:T(8,128)S(1)}, f32[8,2304]{1,0:T(8,128)S(1)}, u32[]{:S(2)}, u32[]{:S(2)}) collective-permute-start(f32[8,2304]{1,0:T(8,128)S(1)} %get-tuple-element.28), channel_id=1, source_target_pairs={{0,1},{1,0},{2,3},{3,2},{4,5},{5,4},{6,7},{7,6},{8,9},{9,8},{10,11... | collective-permute-start | bytes 221192 | tf_op jit(solution)/shard_map/ppermute | solution.py:27
  64.3 1.3 collective-permute-start.6
  65.6 2.3 %collective-permute-done.6 = f32[8,2304]{1,0:T(8,128)S(1)} collective-permute-done((f32[8,2304]{1,0:T(8,128)S(1)}, f32[8,2304]{1,0:T(8,128)S(1)}, u32[]{:S(2)}, u32[]{:S(2)}) %collective-permute-start.6) | collective-permute-done | bytes 73760 | tf_op jit(solution)/shard_map/ppermute | solution.py:27
  67.9 2.8 %collective-permute-start.7 = (f32[8,2304]{1,0:T(8,128)S(1)}, f32[8,2304]{1,0:T(8,128)S(1)}, u32[]{:S(2)}, u32[]{:S(2)}) collective-permute-start(f32[8,2304]{1,0:T(8,128)S(1)} %add.29), channel_id=1, source_target_pairs={{0,128},{64,192},{128,0},{192,64},{1,129},{65,193},{129,1},{193,65... | collective-permute-start | bytes 221192 | tf_op jit(solution)/shard_map/ppermute | solution.py:27
  70.7 2.8 %collective-permute-done.7 = f32[8,2304]{1,0:T(8,128)S(1)} collective-permute-done((f32[8,2304]{1,0:T(8,128)S(1)}, f32[8,2304]{1,0:T(8,128)S(1)}, u32[]{:S(2)}, u32[]{:S(2)}) %collective-permute-start.7) | collective-permute-done | bytes 73760 | tf_op jit(solution)/shard_map/ppermute | solution.py:27
  73.6 3.2 %collective-permute-done.8 = f32[8,2304]{1,0:T(8,128)S(1)} collective-permute-done((f32[8,2304]{1,0:T(8,128)S(1)}, f32[8,2304]{1,0:T(8,128)S(1)}, u32[]{:S(2)}, u32[]{:S(2)}) %collective-permute-start.8) | collective-permute-done | bytes 73760 | tf_op jit(solution)/shard_map/ppermute | solution.py:27
  76.8 1.8 %collective-permute-start.9 = (f32[8,2304]{1,0:T(8,128)S(1)}, f32[8,2304]{1,0:T(8,128)S(1)}, u32[]{:S(2)}, u32[]{:S(2)}) collective-permute-start(f32[8,2304]{1,0:T(8,128)S(1)} %add.31), channel_id=1, source_target_pairs={{0,8},{4,12},{8,0},{12,4},{1,9},{5,13},{9,1},{13,5},{2,10},{6,14},... | collective-permute-start | bytes 221192 | tf_op jit(solution)/shard_map/ppermute | solution.py:27
  78.7 3.0 %collective-permute-done.9 = f32[8,2304]{1,0:T(8,128)S(1)} collective-permute-done((f32[8,2304]{1,0:T(8,128)S(1)}, f32[8,2304]{1,0:T(8,128)S(1)}, u32[]{:S(2)}, u32[]{:S(2)}) %collective-permute-start.9) | collective-permute-done | bytes 73760 | tf_op jit(solution)/shard_map/ppermute | solution.py:27
  82.5 2.5 %collective-permute-done.10 = f32[8,2304]{1,0:T(8,128)S(1)} collective-permute-done((f32[8,2304]{1,0:T(8,128)S(1)}, f32[8,2304]{1,0:T(8,128)S(1)}, u32[]{:S(2)}, u32[]{:S(2)}) %collective-permute-start.10) | collective-permute-done | bytes 73760 | tf_op jit(solution)/shard_map/ppermute | solution.py:27
  84.9 2.2 %collective-permute-start.11 = (f32[8,2304]{1,0:T(8,128)S(1)}, f32[8,2304]{1,0:T(8,128)S(1)}, u32[]{:S(2)}, u32[]{:S(2)}) collective-permute-start(f32[8,2304]{1,0:T(8,128)S(1)} %add.33), channel_id=1, source_target_pairs={{0,32},{16,48},{32,0},{48,16},{1,33},{17,49},{33,1},{49,17},{2,34}... | collective-permute-start | bytes 221192 | tf_op jit(solution)/shard_map/ppermute | solution.py:27
  87.2 2.3 %collective-permute-done.11 = f32[8,2304]{1,0:T(8,128)S(1)} collective-permute-done((f32[8,2304]{1,0:T(8,128)S(1)}, f32[8,2304]{1,0:T(8,128)S(1)}, u32[]{:S(2)}, u32[]{:S(2)}) %collective-permute-start.11) | collective-permute-done | bytes 73760 | tf_op jit(solution)/shard_map/ppermute | solution.py:27
  89.4 5.9 %collective-permute-start.12 = (f32[8,2304]{1,0:T(8,128)S(1)}, f32[8,2304]{1,0:T(8,128)S(1)}, u32[]{:S(2)}, u32[]{:S(2)}) collective-permute-start(f32[8,2304]{1,0:T(8,128)S(1)} %add.34), channel_id=1, source_target_pairs={{0,2},{2,0},{1,3},{3,1},{4,6},{6,4},{5,7},{7,5},{8,10},{10,8},{9,1... | collective-permute-start | bytes 221192 | tf_op jit(solution)/shard_map/ppermute | solution.py:27
  95.4 2.5 %collective-permute-start.25 = (bf16[64,4736]{1,0:T(8,128)(2,1)S(1)}, bf16[64,4736]{1,0:T(8,128)(2,1)S(1)}, u32[]{:S(2)}, u32[]{:S(2)}) collective-permute-start(bf16[64,4736]{1,0:T(8,128)(2,1)S(1)} %collective-permute-done.23.refs_10_), channel_id=1, source_target_pairs={{0,192},{64,0},{128,64},{192,128},{1,193},{65,1},{129,65},{193,129... | collective-permute-start | bytes 1818632 | tf_op jit(solution)/shard_map/ppermute | solution.py:22
  97.8 1.1 slice.16
  99.1 1.1 slice.17
  100.2 2.7 %collective-permute-start.21 = (bf16[64,4736]{1,0:T(8,128)(2,1)S(1)}, bf16[64,4736]{1,0:T(8,128)(2,1)}, u32[]{:S(2)}, u32[]{:S(2)}) collective-permute-start(bf16[64,4736]{1,0:T(8,128)(2,1)S(1)} %slice.17), channel_id=1, source_target_pairs={{0,12},{4,0},{8,4},{12,8},{1,13},{5,1},{9,5},{13,9},{2,14},{6,2},{... | collective-permute-start | bytes 1818632 | tf_op jit(solution)/shard_map/ppermute | solution.py:22
  102.9 9.2 %collective-permute-start.16 = (bf16[128,4736]{1,0:T(8,128)(2,1)}, bf16[128,4736]{1,0:T(8,128)(2,1)}, u32[]{:S(2)}, u32[]{:S(2)}) collective-permute-start(bf16[128,4736]{1,0:T(8,128)(2,1)} %collective-permute-done.15.refs_2_), channel_id=1, source_target_pairs={{0,1},{1,0},{2,3},{3,2},{4,5},{5,4},{6,7},{7,6},{8,9},{9,8},{10,11... | collective-permute-start | bytes 3637256 | tf_op jit(solution)/shard_map/ppermute | solution.py:27
  113.2 1.2 collective-permute-start.26
  114.3 4.6 %collective-permute-start.20 = (bf16[64,4736]{1,0:T(8,128)(2,1)S(1)}, bf16[64,4736]{1,0:T(8,128)(2,1)S(1)}, u32[]{:S(2)}, u32[]{:S(2)}) collective-permute-start(bf16[64,4736]{1,0:T(8,128)(2,1)S(1)} %collective-permute-done.19.refs_6_), channel_id=1, source_target_pairs={{0,1},{1,0},{2,3},{3,2},{4,5},{5,4},{6,7},{7,6},{8,9},{9,8},{10,11... | collective-permute-start | bytes 1818632 | tf_op jit(solution)/shard_map/ppermute | solution.py:27
  121.7 2.6 %collective-permute-start.27 = (bf16[32,4736]{1,0:T(8,128)(2,1)}, bf16[32,4736]{1,0:T(8,128)(2,1)}, u32[]{:S(2)}, u32[]{:S(2)}) collective-permute-start(bf16[32,4736]{1,0:T(8,128)(2,1)} %slice.19), channel_id=1, source_target_pairs={{0,192},{64,0},{128,64},{192,128},{1,193},{65,1},{129,65},{193,129... | collective-permute-start | bytes 909320 | tf_op jit(solution)/shard_map/ppermute | solution.py:22
  124.3 5.8 %collective-permute-done.27.refs_14_ = bf16[32,4736]{1,0:T(8,128)(2,1)} collective-permute-done((bf16[32,4736]{1,0:T(8,128)(2,1)}, bf16[32,4736]{1,0:T(8,128)(2,1)}, u32[]{:S(2)}, u32[]{:S(2)}) %collective-permute-start.27) | collective-permute-done | bytes 303136 | tf_op jit(solution)/shard_map/ppermute | solution.py:22
  130.1 1.9 %collective-permute-start.13 = (f32[8,2304]{1,0:T(8,128)S(1)}, f32[8,2304]{1,0:T(8,128)S(1)}, u32[]{:S(2)}, u32[]{:S(2)}) collective-permute-start(f32[8,2304]{1,0:T(8,128)S(1)} %add.35), channel_id=1, source_target_pairs={{0,1},{1,0},{2,3},{3,2},{4,5},{5,4},{6,7},{7,6},{8,9},{9,8},{10,11... | collective-permute-start | bytes 221192 | tf_op jit(solution)/shard_map/ppermute | solution.py:27
  132.0 1.1 copy-done.7
  133.1 1.1 copy-done.9
  134.1 1.1 copy-done.14
  135.2 8.8 %far_products.1.refs_12_ = bf16[4,256,256]{2,1,0:T(8,128)(2,1)S(1)} custom-call(s32[4]{0:T(128)S(1)} %pad_add_fusion.at, bf16[128,4736]{1,0:T(8,128)(2,1)} %copy-done, bf16[128,4736]{1,0:T(8,128)(2,1)} %copy-done.2, bf16[128,4736]{1,0:T(8,128)(2,1)} %collective-permute-done.15.refs_2_, bf16[128,4736]{1,0:T(8,128)(2,1)} %collective-permute-done.16.refs_3_, ...), custom_call_target="tpu_custom_call" | custom-call | flops 2483027968 | bytes 14548992 | tf_op jit(solution)/shard_map/far_products/pallas_call | solution.py:304
  144.0 3.7 %collective-permute-start.28 = (bf16[4,256,256]{2,1,0:T(8,128)(2,1)S(1)}, bf16[4,256,256]{2,1,0:T(8,128)(2,1)S(1)}, u32[]{:S(2)}, u32[]{:S(2)}) collective-permute-start(bf16[4,256,256]{2,1,0:T(8,128)(2,1)S(1)} %far_products.1.refs_12_), channel_id=1, source_target_pairs={{0,2},{2,0},{1,3},{3,1},{4,6},{6,4},{5,7},{7,5},{8,10},{10,8},{9,1... | collective-permute-start | bytes 1572872 | tf_op jit(solution)/shard_map/ppermute | solution.py:27
  148.4 1.3 copy-done.3
  149.6 9.0 %own_products.1 = bf16[4,2,256,256]{3,2,1,0:T(8,128)(2,1)} custom-call(s32[4]{0:T(128)S(1)} %pad_add_fusion.at, bf16[128,4736]{1,0:T(8,128)(2,1)S(1)} %copy-done.1, bf16[128,4736]{1,0:T(8,128)(2,1)S(1)} %copy-done.3, bf16[128,4736]{1,0:T(8,128)(2,1)} %collective-permute-done.15.refs_2_, bf16[128,4736]{1,0:T(8,128)(2,1)} %collective-permute-done.16.refs_3_, ...), custom_call_target="tpu_custom_call" | custom-call | flops 2483027968 | bytes 14548992 | tf_op jit(solution)/shard_map/own_products/pallas_call | solution.py:320
  158.6 14.5 %collective-permute-done.28 = bf16[4,256,256]{2,1,0:T(8,128)(2,1)S(1)} collective-permute-done((bf16[4,256,256]{2,1,0:T(8,128)(2,1)S(1)}, bf16[4,256,256]{2,1,0:T(8,128)(2,1)S(1)}, u32[]{:S(2)}, u32[]{:S(2)}) %collective-permute-start.28) | collective-permute-done | bytes 524320 | tf_op jit(solution)/shard_map/ppermute | solution.py:27
  (68 shorter events, 10.8 us)
Async XLA Ops:
  0.7 1.3 copy-start.4
  2.0 1.3 copy-start.10
  3.3 1.3 copy-start.11
  4.5 0.8 copy-start.15
  5.4 0.9 copy-start.17
  6.3 13.8 %copy-start.12 = (bf16[2048,256]{1,0:T(8,128)(2,1)S(1)}, bf16[2048,256]{1,0:T(8,128)(2,1)}, u32[]{:S(2)}) copy-start(bf16[2048,256]{1,0:T(8,128)(2,1)} %param.9) | copy-start | bytes 3145732
  6.3 13.8 %copy-start.16 = (bf16[256,128]{1,0:T(8,128)(2,1)S(1)}, bf16[256,128]{1,0:T(8,128)(2,1)}, u32[]{:S(2)}) copy-start(bf16[256,128]{1,0:T(8,128)(2,1)} %refs_11_.1) | copy-start | bytes 196612
  8.3 14.9 %copy-start = (bf16[128,4736]{1,0:T(8,128)(2,1)}, bf16[128,4736]{1,0:T(8,128)(2,1)S(1)}, u32[]{:S(2)}) copy-start(bf16[128,4736]{1,0:T(8,128)(2,1)S(1)} %get-tuple-element.16.tie.refs_0_) | copy-start | bytes 3637252
  8.3 87.0 %collective-permute-start.15 = (bf16[128,4736]{1,0:T(8,128)(2,1)S(1)}, bf16[128,4736]{1,0:T(8,128)(2,1)}, u32[]{:S(2)}, u32[]{:S(2)}) collective-permute-start(bf16[128,4736]{1,0:T(8,128)(2,1)S(1)} %get-tuple-element.16.tie.refs_0_), channel_id=1, source_target_pairs={{0,4},{4,8},{8,12},{12,0},{1,5},{5,9},{9,13},{13,1},{2,6},{6,10},{... | collective-permute-start | bytes 3637256 | tf_op jit(solution)/shard_map/ppermute | solution.py:22
  10.5 88.4 %collective-permute-start.17 = (bf16[128,4736]{1,0:T(8,128)(2,1)S(1)}, bf16[128,4736]{1,0:T(8,128)(2,1)}, u32[]{:S(2)}, u32[]{:S(2)}) collective-permute-start(bf16[128,4736]{1,0:T(8,128)(2,1)S(1)} %get-tuple-element.16.tie.refs_0_), channel_id=1, source_target_pairs={{0,12},{4,0},{8,4},{12,8},{1,13},{5,1},{9,5},{13,9},{2,14},{6,2},{... | collective-permute-start | bytes 3637256 | tf_op jit(solution)/shard_map/ppermute | solution.py:22
  12.0 90.9 %collective-permute-start.14 = (bf16[128,4736]{1,0:T(8,128)(2,1)S(1)}, bf16[128,4736]{1,0:T(8,128)(2,1)S(1)}, u32[]{:S(2)}, u32[]{:S(2)}) collective-permute-start(bf16[128,4736]{1,0:T(8,128)(2,1)S(1)} %get-tuple-element.16.tie.refs_0_), channel_id=1, source_target_pairs={{0,1},{1,0},{2,3},{3,2},{4,5},{5,4},{6,7},{7,6},{8,9},{9,8},{10,11... | collective-permute-start | bytes 3637256 | tf_op jit(solution)/shard_map/ppermute | solution.py:27
  14.9 40.9 %collective-permute-start.23 = (bf16[64,4736]{1,0:T(8,128)(2,1)S(1)}, bf16[64,4736]{1,0:T(8,128)(2,1)S(1)}, u32[]{:S(2)}, u32[]{:S(2)}) collective-permute-start(bf16[64,4736]{1,0:T(8,128)(2,1)S(1)} %get-tuple-element.29), channel_id=1, source_target_pairs={{0,2},{2,0},{1,3},{3,1},{4,6},{6,4},{5,7},{7,5},{8,10},{10,8},{9,1... | collective-permute-start | bytes 1818632 | tf_op jit(solution)/shard_map/ppermute | solution.py:27
  20.0 37.2 %copy-start.5 = (bf16[128,4608]{1,0:T(8,128)(2,1)S(1)}, bf16[128,4608]{1,0:T(8,128)(2,1)}, u32[]{:S(2)}) copy-start(bf16[128,4608]{1,0:T(8,128)(2,1)} %hidden.3) | copy-start | bytes 3538948
  21.0 1.6 collective-permute-start
  23.2 15.7 %collective-permute-start.1 = (bf16[2,128,128]{2,1,0:T(8,128)(2,1)S(1)}, bf16[2,128,128]{2,1,0:T(8,128)(2,1)S(1)}, u32[]{:S(2)}, u32[]{:S(2)}) collective-permute-start(bf16[2,128,128]{2,1,0:T(8,128)(2,1)S(1)} %get-tuple-element.20), channel_id=1, source_target_pairs={{0,4},{4,0},{8,12},{12,8},{1,5},{5,1},{9,13},{13,9},{2,6},{6,2},{1... | collective-permute-start | bytes 196616 | tf_op jit(solution)/shard_map/ppermute | solution.py:27
  39.0 4.6 %collective-permute-start.2 = (bf16[2,128,128]{2,1,0:T(8,128)(2,1)S(1)}, bf16[2,128,128]{2,1,0:T(8,128)(2,1)S(1)}, u32[]{:S(2)}, u32[]{:S(2)}) collective-permute-start(bf16[2,128,128]{2,1,0:T(8,128)(2,1)S(1)} %get-tuple-element.21), channel_id=1, source_target_pairs={{0,8},{4,12},{8,0},{12,4},{1,9},{5,13},{9,1},{13,5},{2,10},{6,14},... | collective-permute-start | bytes 196616 | tf_op jit(solution)/shard_map/ppermute | solution.py:27
  43.6 4.3 %collective-permute-start.3 = (bf16[2,128,128]{2,1,0:T(8,128)(2,1)S(1)}, bf16[2,128,128]{2,1,0:T(8,128)(2,1)S(1)}, u32[]{:S(2)}, u32[]{:S(2)}) collective-permute-start(bf16[2,128,128]{2,1,0:T(8,128)(2,1)S(1)} %get-tuple-element.22), channel_id=1, source_target_pairs={{0,12},{4,8},{8,4},{12,0},{1,13},{5,9},{9,5},{13,1},{2,14},{6,10},... | collective-permute-start | bytes 196616 | tf_op jit(solution)/shard_map/ppermute | solution.py:27
  48.5 8.8 %collective-permute-start.4 = (bf16[128,128]{1,0:T(8,128)(2,1)S(1)}, bf16[128,128]{1,0:T(8,128)(2,1)S(1)}, u32[]{:S(2)}, u32[]{:S(2)}) collective-permute-start(bf16[128,128]{1,0:T(8,128)(2,1)S(1)} %get-tuple-element.24), channel_id=1, source_target_pairs={{0,2},{2,0},{1,3},{3,1},{4,6},{6,4},{5,7},{7,5},{8,10},{10,8},{9,1... | collective-permute-start | bytes 98312 | tf_op jit(solution)/shard_map/ppermute | solution.py:27
  55.8 39.6 %copy-start.13 = (bf16[64,4736]{1,0:T(8,128)(2,1)}, bf16[64,4736]{1,0:T(8,128)(2,1)S(1)}, u32[]{:S(2)}) copy-start(bf16[64,4736]{1,0:T(8,128)(2,1)S(1)} %collective-permute-done.23.refs_10_) | copy-start | bytes 1818628
  55.8 56.4 %collective-permute-start.24 = (bf16[64,4736]{1,0:T(8,128)(2,1)S(1)}, bf16[64,4736]{1,0:T(8,128)(2,1)S(1)}, u32[]{:S(2)}, u32[]{:S(2)}) collective-permute-start(bf16[64,4736]{1,0:T(8,128)(2,1)S(1)} %collective-permute-done.23.refs_10_), channel_id=1, source_target_pairs={{0,64},{64,128},{128,192},{192,0},{1,65},{65,129},{129,193},{193,1... | collective-permute-start | bytes 1818632 | tf_op jit(solution)/shard_map/ppermute | solution.py:22
  58.5 5.7 %collective-permute-start.5 = (f32[8,2304]{1,0:T(8,128)S(1)}, f32[8,2304]{1,0:T(8,128)S(1)}, u32[]{:S(2)}, u32[]{:S(2)}) collective-permute-start(f32[8,2304]{1,0:T(8,128)S(1)} %get-tuple-element.28), channel_id=1, source_target_pairs={{0,1},{1,0},{2,3},{3,2},{4,5},{5,4},{6,7},{7,6},{8,9},{9,8},{10,11... | collective-permute-start | bytes 221192 | tf_op jit(solution)/shard_map/ppermute | solution.py:27
  64.3 3.6 %collective-permute-start.6 = (f32[8,2304]{1,0:T(8,128)S(1)}, f32[8,2304]{1,0:T(8,128)S(1)}, u32[]{:S(2)}, u32[]{:S(2)}) collective-permute-start(f32[8,2304]{1,0:T(8,128)S(1)} %add.28), channel_id=1, source_target_pairs={{0,64},{64,0},{128,192},{192,128},{1,65},{65,1},{129,193},{193,129... | collective-permute-start | bytes 221192 | tf_op jit(solution)/shard_map/ppermute | solution.py:27
  67.9 5.7 %collective-permute-start.7 = (f32[8,2304]{1,0:T(8,128)S(1)}, f32[8,2304]{1,0:T(8,128)S(1)}, u32[]{:S(2)}, u32[]{:S(2)}) collective-permute-start(f32[8,2304]{1,0:T(8,128)S(1)} %add.29), channel_id=1, source_target_pairs={{0,128},{64,192},{128,0},{192,64},{1,129},{65,193},{129,1},{193,65... | collective-permute-start | bytes 221192 | tf_op jit(solution)/shard_map/ppermute | solution.py:27
  73.5 3.3 %collective-permute-start.8 = (f32[8,2304]{1,0:T(8,128)S(1)}, f32[8,2304]{1,0:T(8,128)S(1)}, u32[]{:S(2)}, u32[]{:S(2)}) collective-permute-start(f32[8,2304]{1,0:T(8,128)S(1)} %add.30), channel_id=1, source_target_pairs={{0,4},{4,0},{8,12},{12,8},{1,5},{5,1},{9,13},{13,9},{2,6},{6,2},{1... | collective-permute-start | bytes 221192 | tf_op jit(solution)/shard_map/ppermute | solution.py:27
  76.8 4.8 %collective-permute-start.9 = (f32[8,2304]{1,0:T(8,128)S(1)}, f32[8,2304]{1,0:T(8,128)S(1)}, u32[]{:S(2)}, u32[]{:S(2)}) collective-permute-start(f32[8,2304]{1,0:T(8,128)S(1)} %add.31), channel_id=1, source_target_pairs={{0,8},{4,12},{8,0},{12,4},{1,9},{5,13},{9,1},{13,5},{2,10},{6,14},... | collective-permute-start | bytes 221192 | tf_op jit(solution)/shard_map/ppermute | solution.py:27
  81.6 3.3 %collective-permute-start.10 = (f32[8,2304]{1,0:T(8,128)S(1)}, f32[8,2304]{1,0:T(8,128)S(1)}, u32[]{:S(2)}, u32[]{:S(2)}) collective-permute-start(f32[8,2304]{1,0:T(8,128)S(1)} %add.32), channel_id=1, source_target_pairs={{0,16},{16,0},{32,48},{48,32},{1,17},{17,1},{33,49},{49,33},{2,18}... | collective-permute-start | bytes 221192 | tf_op jit(solution)/shard_map/ppermute | solution.py:27
  84.9 4.5 %collective-permute-start.11 = (f32[8,2304]{1,0:T(8,128)S(1)}, f32[8,2304]{1,0:T(8,128)S(1)}, u32[]{:S(2)}, u32[]{:S(2)}) collective-permute-start(f32[8,2304]{1,0:T(8,128)S(1)} %add.33), channel_id=1, source_target_pairs={{0,32},{16,48},{32,0},{48,16},{1,33},{17,49},{33,1},{49,17},{2,34}... | collective-permute-start | bytes 221192 | tf_op jit(solution)/shard_map/ppermute | solution.py:27
  89.4 10.7 %collective-permute-start.12 = (f32[8,2304]{1,0:T(8,128)S(1)}, f32[8,2304]{1,0:T(8,128)S(1)}, u32[]{:S(2)}, u32[]{:S(2)}) collective-permute-start(f32[8,2304]{1,0:T(8,128)S(1)} %add.34), channel_id=1, source_target_pairs={{0,2},{2,0},{1,3},{3,1},{4,6},{6,4},{5,7},{7,5},{8,10},{10,8},{9,1... | collective-permute-start | bytes 221192 | tf_op jit(solution)/shard_map/ppermute | solution.py:27
  95.4 17.8 %collective-permute-start.25 = (bf16[64,4736]{1,0:T(8,128)(2,1)S(1)}, bf16[64,4736]{1,0:T(8,128)(2,1)S(1)}, u32[]{:S(2)}, u32[]{:S(2)}) collective-permute-start(bf16[64,4736]{1,0:T(8,128)(2,1)S(1)} %collective-permute-done.23.refs_10_), channel_id=1, source_target_pairs={{0,192},{64,0},{128,64},{192,128},{1,193},{65,1},{129,65},{193,129... | collective-permute-start | bytes 1818632 | tf_op jit(solution)/shard_map/ppermute | solution.py:22
  99.0 15.4 %collective-permute-start.19 = (bf16[64,4736]{1,0:T(8,128)(2,1)S(1)}, bf16[64,4736]{1,0:T(8,128)(2,1)S(1)}, u32[]{:S(2)}, u32[]{:S(2)}) collective-permute-start(bf16[64,4736]{1,0:T(8,128)(2,1)S(1)} %slice.16), channel_id=1, source_target_pairs={{0,4},{4,8},{8,12},{12,0},{1,5},{5,9},{9,13},{13,1},{2,6},{6,10},{... | collective-permute-start | bytes 1818632 | tf_op jit(solution)/shard_map/ppermute | solution.py:22
  100.2 18.8 %collective-permute-start.21 = (bf16[64,4736]{1,0:T(8,128)(2,1)S(1)}, bf16[64,4736]{1,0:T(8,128)(2,1)}, u32[]{:S(2)}, u32[]{:S(2)}) collective-permute-start(bf16[64,4736]{1,0:T(8,128)(2,1)S(1)} %slice.17), channel_id=1, source_target_pairs={{0,12},{4,0},{8,4},{12,8},{1,13},{5,1},{9,5},{13,9},{2,14},{6,2},{... | collective-permute-start | bytes 1818632 | tf_op jit(solution)/shard_map/ppermute | solution.py:22
  102.9 29.1 %copy-start.2 = (bf16[128,4736]{1,0:T(8,128)(2,1)}, bf16[128,4736]{1,0:T(8,128)(2,1)S(1)}, u32[]{:S(2)}) copy-start(bf16[128,4736]{1,0:T(8,128)(2,1)S(1)} %collective-permute-done.14.refs_1_) | copy-start | bytes 3637252
  102.9 29.0 %collective-permute-start.16 = (bf16[128,4736]{1,0:T(8,128)(2,1)}, bf16[128,4736]{1,0:T(8,128)(2,1)}, u32[]{:S(2)}, u32[]{:S(2)}) collective-permute-start(bf16[128,4736]{1,0:T(8,128)(2,1)} %collective-permute-done.15.refs_2_), channel_id=1, source_target_pairs={{0,1},{1,0},{2,3},{3,2},{4,5},{5,4},{6,7},{7,6},{8,9},{9,8},{10,11... | collective-permute-start | bytes 3637256 | tf_op jit(solution)/shard_map/ppermute | solution.py:27
  112.1 19.8 %collective-permute-start.18 = (bf16[128,4736]{1,0:T(8,128)(2,1)}, bf16[128,4736]{1,0:T(8,128)(2,1)}, u32[]{:S(2)}, u32[]{:S(2)}) collective-permute-start(bf16[128,4736]{1,0:T(8,128)(2,1)} %collective-permute-done.17.refs_4_), channel_id=1, source_target_pairs={{0,1},{1,0},{2,3},{3,2},{4,5},{5,4},{6,7},{7,6},{8,9},{9,8},{10,11... | collective-permute-start | bytes 3637256 | tf_op jit(solution)/shard_map/ppermute | solution.py:27
  112.3 0.9 copy-start.6
  113.2 8.5 %collective-permute-start.26 = (bf16[32,4736]{1,0:T(8,128)(2,1)S(1)}, bf16[32,4736]{1,0:T(8,128)(2,1)S(1)}, u32[]{:S(2)}, u32[]{:S(2)}) collective-permute-start(bf16[32,4736]{1,0:T(8,128)(2,1)S(1)} %slice.18), channel_id=1, source_target_pairs={{0,64},{64,128},{128,192},{192,0},{1,65},{65,129},{129,193},{193,1... | collective-permute-start | bytes 909320 | tf_op jit(solution)/shard_map/ppermute | solution.py:22
  114.3 17.6 %collective-permute-start.20 = (bf16[64,4736]{1,0:T(8,128)(2,1)S(1)}, bf16[64,4736]{1,0:T(8,128)(2,1)S(1)}, u32[]{:S(2)}, u32[]{:S(2)}) collective-permute-start(bf16[64,4736]{1,0:T(8,128)(2,1)S(1)} %collective-permute-done.19.refs_6_), channel_id=1, source_target_pairs={{0,1},{1,0},{2,3},{3,2},{4,5},{5,4},{6,7},{7,6},{8,9},{9,8},{10,11... | collective-permute-start | bytes 1818632 | tf_op jit(solution)/shard_map/ppermute | solution.py:27
  119.0 13.0 %collective-permute-start.22 = (bf16[64,4736]{1,0:T(8,128)(2,1)}, bf16[64,4736]{1,0:T(8,128)(2,1)S(1)}, u32[]{:S(2)}, u32[]{:S(2)}) collective-permute-start(bf16[64,4736]{1,0:T(8,128)(2,1)} %collective-permute-done.21.refs_8_), channel_id=1, source_target_pairs={{0,1},{1,0},{2,3},{3,2},{4,5},{5,4},{6,7},{7,6},{8,9},{9,8},{10,11... | collective-permute-start | bytes 1818632 | tf_op jit(solution)/shard_map/ppermute | solution.py:27
  120.6 0.8 copy-start.8
  121.7 8.4 %collective-permute-start.27 = (bf16[32,4736]{1,0:T(8,128)(2,1)}, bf16[32,4736]{1,0:T(8,128)(2,1)}, u32[]{:S(2)}, u32[]{:S(2)}) collective-permute-start(bf16[32,4736]{1,0:T(8,128)(2,1)} %slice.19), channel_id=1, source_target_pairs={{0,192},{64,0},{128,64},{192,128},{1,193},{65,1},{129,65},{193,129... | collective-permute-start | bytes 909320 | tf_op jit(solution)/shard_map/ppermute | solution.py:22
  124.3 24.1 %copy-start.1 = (bf16[128,4736]{1,0:T(8,128)(2,1)S(1)}, bf16[128,4736]{1,0:T(8,128)(2,1)}, u32[]{:S(2)}) copy-start(bf16[128,4736]{1,0:T(8,128)(2,1)} %copy-done) | copy-start | bytes 3637252
  130.1 17.6 %collective-permute-start.13 = (f32[8,2304]{1,0:T(8,128)S(1)}, f32[8,2304]{1,0:T(8,128)S(1)}, u32[]{:S(2)}, u32[]{:S(2)}) collective-permute-start(f32[8,2304]{1,0:T(8,128)S(1)} %add.35), channel_id=1, source_target_pairs={{0,1},{1,0},{2,3},{3,2},{4,5},{5,4},{6,7},{7,6},{8,9},{9,8},{10,11... | collective-permute-start | bytes 221192 | tf_op jit(solution)/shard_map/ppermute | solution.py:27
  132.0 1.1 copy-start.7
  133.1 1.1 copy-start.9
  134.1 1.1 copy-start.14
  144.0 29.1 %collective-permute-start.28 = (bf16[4,256,256]{2,1,0:T(8,128)(2,1)S(1)}, bf16[4,256,256]{2,1,0:T(8,128)(2,1)S(1)}, u32[]{:S(2)}, u32[]{:S(2)}) collective-permute-start(bf16[4,256,256]{2,1,0:T(8,128)(2,1)S(1)} %far_products.1.refs_12_), channel_id=1, source_target_pairs={{0,2},{2,0},{1,3},{3,1},{4,6},{6,4},{5,7},{7,5},{8,10},{10,8},{9,1... | collective-permute-start | bytes 1572872 | tf_op jit(solution)/shard_map/ppermute | solution.py:27
  148.4 1.3 copy-start.3

commit v3 on v1

v3 whole, which is shorter than its diff:
```python
import jax
import jax.numpy as jnp
from jax import lax
from jax.experimental import pallas as pl
from jax.experimental.pallas import tpu as pltpu
from jax.sharding import Mesh
from jax.sharding import PartitionSpec as P

F32 = jnp.float32
BF16 = jnp.bfloat16
AXES = ("x", "zl", "y", "zh", "c")
VMEM = pl.BlockSpec(memory_space=pltpu.VMEM)
SMEM = pl.BlockSpec(memory_space=pltpu.SMEM)
ANY = pl.BlockSpec(memory_space=pl.ANY)
HBM = pl.BlockSpec(memory_space=pltpu.HBM)
LARGE = pltpu.CompilerParams(vmem_limit_bytes=48 * 1024 * 1024)


def ring(value, axis):
    size = lax.axis_size(axis)
    pairs = [
        (2 * i + c, 2 * ((i + 1 - 2 * c) % size) + c) for i in range(size) for c in range(2)
    ]
    return lax.ppermute(value, (axis, "c"), pairs)


def fence_kernel(*refs):
    del refs


def fence(values, *ties):
    return pl.pallas_call(
        fence_kernel,
        in_specs=[HBM] * len(values) + [ANY] * len(ties),
        out_specs=[HBM] * len(values),
        out_shape=[shaped(v.shape, v.dtype) for v in values],
        input_output_aliases={i: i for i in range(len(values))},
        name="fence",
    )(*values, *ties)


def back_at(place, core, steps):
    return lax.rem(place - steps * (1 - 2 * core) + 4, 4)


def swap(value, axis, mask):
    size = lax.axis_size(axis)
    return lax.ppermute(value, axis, [(i, i ^ mask) for i in range(size)])


def dot_t(left, right, precision=None):
    return lax.dot_general(
        left, right, (((1,), (1,)), ((), ())), precision=precision, preferred_element_type=F32
    )


def shaped(shape, dtype):
    return jax.ShapeDtypeStruct(shape, dtype)


def cost(flops, moved):
    return pl.CostEstimate(flops=flops, bytes_accessed=moved, transcendentals=0)


def membership(adapters, stacked):
    row = lax.broadcasted_iota(jnp.int32, (adapters, stacked), 0)
    column = lax.broadcasted_iota(jnp.int32, (adapters, stacked), 1)
    low = row * (stacked // adapters)
    return jnp.where((column >= low) & (column < low + stacked // adapters), 1.0, 0.0)


def run(copies):
    for copy in copies:
        copy.start()
    for copy in copies:
        copy.wait()


def split_kernel(at, weight, down, piece, sems):
    width = weight.shape[1]
    quarter = piece.shape[0]
    rows = pl.ds(pl.multiple_of(at[0] * quarter, quarter), quarter)
    run(
        [
            pltpu.make_async_copy(weight.at[rows], piece.at[:, pl.ds(0, width)], sems.at[0]),
            pltpu.make_async_copy(
                down.at[rows], piece.at[:, pl.ds(width, down.shape[1])], sems.at[1]
            ),
        ]
    )


def token_kernel(at, hidden, grad, up, gate, mixed, gates, back, grad_in, up_in, sems):
    stacked = up.shape[0]
    copies = [
        pltpu.make_async_copy(grad, grad_in, sems.at[0]),
        pltpu.make_async_copy(up, up_in, sems.at[1]),
    ]
    for copy in copies:
        copy.start()
    ones = membership(gate.shape[0], stacked)
    gates[...] = jax.nn.sigmoid(dot_t(gate[...], hidden[...]))
    wide = lax.dot_general(
        ones.astype(BF16), gate[...], (((0,), (0,)), ((), ())), preferred_element_type=F32
    ).astype(BF16)
    factor = 2.0 * jax.nn.sigmoid(dot_t(hidden[...], wide))
    for copy in copies:
        copy.wait()
    pulled = dot_t(grad_in[...], up_in[...])
    back[...] = pulled
    mixed[...] = (factor * pulled).astype(BF16)


def act_kernel(at, mixture, down, keep, give, rows_in, down_in, sems):
    c = at[3]
    blocks, _, tokens, depth = mixture.shape
    copies = [
        pltpu.make_async_copy(down, down_in, sems.at[0]),
        pltpu.make_async_copy(mixture.at[:, 1 - c], rows_in.at[0], sems.at[1]),
        pltpu.make_async_copy(mixture.at[:, c], rows_in.at[1], sems.at[2]),
    ]
    for copy in copies:
        copy.start()
    copies[0].wait()
    for out, side in ((give, 0), (keep, 1)):
        copies[1 + side].wait()
        rows = rows_in[side].reshape(blocks * tokens, depth)
        value = jnp.dot(rows, down_in[...], preferred_element_type=F32)
        out[...] = value.reshape(out.shape).astype(out.dtype)


def act_y_kernel(at, keep, got, mixed, first, second, third, rest):
    y = at[1]
    for out, mask in ((first, 1), (second, 2), (third, 3)):
        row = jnp.bitwise_xor(y, mask)
        out[pl.ds(0, 2)] = (keep[row] + got[row].astype(F32)).astype(out.dtype)
        out[2] = mixed[...]
    rest[...] = keep[y] + got[y].astype(F32)


def act_z_kernel(at, rest, first, second, third, mixed, keep, give, all_mixed):
    y, zh = at[1], at[2]
    for out, side in ((give, 1 - zh), (keep, zh)):
        total = (rest[side] + first[side].astype(F32)) + (
            second[side].astype(F32) + third[side].astype(F32)
        )
        out[...] = total.astype(out.dtype)
    all_mixed[y] = mixed[...]
    for ref, mask in ((first, 1), (second, 2), (third, 3)):
        all_mixed[jnp.bitwise_xor(y, mask)] = ref[2]


def gate_kernel(at, keep, got, back, gates, hidden, result, give):
    stacked = keep.shape[1]
    adapters = gates.shape[0]
    half = result.shape[1]
    product = (keep[...] + got[...].astype(F32)) * back[...]
    ones = membership(adapters, stacked)
    delta = 2.0 * dot_t(ones, product, lax.Precision.HIGHEST)
    dlogit = delta * gates[...] * (1.0 - gates[...])
    top = dlogit.astype(BF16).astype(F32)
    middle = (dlogit - top).astype(BF16).astype(F32)
    parts = jnp.concatenate([top, middle, dlogit - top - middle], axis=0).astype(BF16)
    c = at[3]
    for out, side in ((result, c), (give, 1 - c)):
        columns = pl.ds(pl.multiple_of(side * half, 128), half)
        total = jnp.dot(parts, hidden[:, columns], preferred_element_type=F32)
        out[...] = total[:adapters] + (
            total[adapters : 2 * adapters] + total[2 * adapters :]
        )


def add_kernel(left, right, *refs):
    refs[-1][...] = left[...] + right[...]


def add4_kernel(first, second, third, fourth, *refs):
    refs[-1][...] = (first[...] + second[...]) + (third[...] + fourth[...])


def rows_product(at, steps, refs, mixed, weights, downs, out):
    y, c = at[1], at[3]
    both = jnp.concatenate([ref[...] for ref in refs], axis=0)
    ranks = jnp.concatenate(
        [mixed[0][back_at(y, c, steps)], mixed[1][back_at(y, 1 - c, steps)]], axis=0
    )
    value = dot_t(both, weights[...]) + dot_t(ranks, downs[...])
    out[...] = value.astype(out.dtype)


def far_kernel(at, own, own_s, one, one_s, two, two_s, mixed, mixed_s, *refs):
    pieces, (out, weight, down) = refs[:4], refs[4:]
    width = weight.shape[1]
    rows = pieces[0].shape[0]
    for steps, ref in enumerate(pieces):
        place = pl.ds(pl.multiple_of(back_at(at[0], at[3], steps) * rows, rows), rows)
        weight[place, :] = ref[:, :width]
        down[place, :] = ref[:, width:]
    for steps, group in enumerate(((own, own_s), (one, one_s), (two, two_s))):
        rows_product(at, steps, group, (mixed, mixed_s), weight, down, out.at[steps])


def far_last_kernel(at, three, three_s, mixed, mixed_s, weight, down, out):
    rows_product(at, 3, (three, three_s), (mixed, mixed_s), weight, down, out)


def own_kernel(
    at, own, own_s, one, one_s, two, two_s, three, three_s, mixed, mixed_s, weight, down, tie, out
):
    groups = ((own, own_s), (one, one_s), (two, two_s), (three, three_s))
    for steps, group in enumerate(groups):
        rows_product(at, steps, group, (mixed, mixed_s), weight, down, out.at[steps])


def place_kernel(at, own, got, last, out, sems):
    y, zh, c = at[1], at[2], at[3]
    tokens = out.shape[3]
    copies = []
    for steps in range(4):
        other = got.at[steps] if steps < 3 else last
        for ref, side in ((own.at[steps], zh), (other, 1 - zh)):
            for half, core in ((0, c), (1, 1 - c)):
                copies.append(
                    pltpu.make_async_copy(
                        ref.at[pl.ds(half * tokens, tokens)],
                        out.at[back_at(y, core, steps), side, core],
                        sems.at[len(copies)],
                    )
                )
    run(copies)


def on_device(hidden, grad, mixture, weight, down, up, gate_matrix):
    tokens, width = grad.shape
    adapters = gate_matrix.shape[0]
    stacked = up.shape[0]
    features = weight.shape[0]
    depth = width + stacked
    quarter = features // 4
    at = jnp.stack([lax.axis_index(a) for a in ("x", "y", "zh", "c")]).astype(jnp.int32)
    c, zh = at[3], at[2]

    piece = pl.pallas_call(
        split_kernel,
        in_specs=[SMEM, HBM, HBM],
        out_specs=HBM,
        out_shape=shaped((quarter, depth), BF16),
        scratch_shapes=[pltpu.SemaphoreType.DMA((2,))],
        name="split",
    )(at, weight, down)
    with jax.named_scope("weight_z"):
        far_piece = swap(piece, "zh", 1)
    with jax.named_scope("tokens_y"):
        one = ring(grad, "y")

    keep, give = pl.pallas_call(
        act_kernel,
        in_specs=[SMEM, HBM, HBM],
        out_specs=[VMEM, VMEM],
        out_shape=[
            shaped((4, 2, tokens, stacked), F32),
            shaped((4, 2, tokens, stacked), BF16),
        ],
        scratch_shapes=[
            pltpu.VMEM((2, 8, tokens, features), BF16),
            pltpu.VMEM((features, stacked), BF16),
            pltpu.SemaphoreType.DMA((3,)),
        ],
        compiler_params=LARGE,
        cost_estimate=cost(2 * mixture.size * stacked, 4 * mixture.size),
        name="rank_products",
    )(at, mixture.reshape(8, 2, tokens, -1), down)
    with jax.named_scope("act_core"):
        got = swap(give, "c", 1)
    mixed, gates, back = pl.pallas_call(
        token_kernel,
        in_specs=[SMEM, VMEM, HBM, HBM, VMEM],
        out_specs=[VMEM, VMEM, VMEM],
        out_shape=[
            shaped((tokens, stacked), BF16),
            shaped((adapters, tokens), F32),
            shaped((tokens, stacked), F32),
        ],
        scratch_shapes=[
            pltpu.VMEM((tokens, width), BF16),
            pltpu.VMEM((stacked, width), BF16),
            pltpu.SemaphoreType.DMA((2,)),
        ],
        compiler_params=LARGE,
        cost_estimate=cost(6 * tokens * width * stacked, 12 * tokens * width),
        name="token_values",
    )(at, hidden, grad, up, gate_matrix)
    first, second, third, rest = pl.pallas_call(
        act_y_kernel,
        in_specs=[SMEM, VMEM, VMEM, VMEM],
        out_specs=[VMEM] * 4,
        out_shape=[shaped((3, tokens, stacked), BF16)] * 3 + [shaped((2, tokens, stacked), F32)],
        name="rank_sum_core",
    )(at, keep, got, mixed)
    with jax.named_scope("act_y"):
        first, second, third = (
            swap(v, "y", mask) for v, mask in ((first, 1), (second, 2), (third, 3))
        )
    keep, give, all_mixed = pl.pallas_call(
        act_z_kernel,
        in_specs=[SMEM] + [VMEM] * 5,
        out_specs=[VMEM] * 3,
        out_shape=[
            shaped((tokens, stacked), F32),
            shaped((tokens, stacked), BF16),
            shaped((4, tokens, stacked), BF16),
        ],
        name="rank_sum_y",
    )(at, rest, first, second, third, mixed)
    one, far_piece = fence((one, far_piece), give)
    with jax.named_scope("tokens_y"):
        two = ring(one, "y")
    with jax.named_scope("weight_x"):
        w_one = ring(far_piece, "x")
    with jax.named_scope("act_z"):
        got = swap(give, "zh", 1)
    with jax.named_scope("mixed_core"):
        mixed_s = swap(all_mixed, "c", 1)
    with jax.named_scope("tokens_core"):
        own_s, one_s = swap(grad, "c", 1), swap(one, "c", 1)

    total, give = pl.pallas_call(
        gate_kernel,
        in_specs=[SMEM] + [VMEM] * 5,
        out_specs=[VMEM, VMEM],
        out_shape=[shaped((adapters, width // 2), F32)] * 2,
        name="gate_products",
    )(at, keep, got, back, gates, hidden)

    def add(left, right, *ties):
        return pl.pallas_call(
            add_kernel,
            in_specs=[VMEM, VMEM] + [ANY] * len(ties),
            out_specs=VMEM,
            out_shape=shaped(left.shape, F32),
            name="gate_sum",
        )(left, right, *ties)

    def add4(*parts):
        return pl.pallas_call(
            add4_kernel,
            in_specs=[VMEM] * 4 + [ANY] * (len(parts) - 4),
            out_specs=VMEM,
            out_shape=shaped(parts[0].shape, F32),
            name="gate_sum",
        )(*parts)

    def step(total, axis, *ties):
        with jax.named_scope("gate_" + axis):
            got = [swap(total, axis, mask) for mask in (1, 2, 3)]
        return add4(total, *got, *ties)

    with jax.named_scope("gate_core"):
        got = swap(give, "c", 1)
    total = add(total, got)
    (w_one,) = fence((w_one,), total)
    with jax.named_scope("weight_x"):
        w_two = ring(w_one, "x")
    total = step(total, "zl", w_one)
    (two,) = fence((two,), total)
    with jax.named_scope("tokens_y"):
        three = ring(two, "y")
    with jax.named_scope("gate_zh"):
        got = swap(total, "zh", 1)
    total = add(total, got, two)
    (w_two,) = fence((w_two,), total)
    with jax.named_scope("weight_x"):
        w_three = ring(w_two, "x")
    with jax.named_scope("tokens_core"):
        two_s, three_s = swap(two, "c", 1), swap(three, "c", 1)
    near = (grad, own_s, one, one_s, two, two_s)
    total = step(total, "x", w_two)

    far, far_weight, far_down = pl.pallas_call(
        far_kernel,
        in_specs=[SMEM] + [VMEM] * 12,
        out_specs=[VMEM] * 3,
        out_shape=[
            shaped((3, 2 * tokens, features), BF16),
            shaped((features, width), BF16),
            shaped((features, stacked), BF16),
        ],
        cost_estimate=cost(12 * tokens * depth * features, 18 * tokens * depth),
        name="far_products",
    )(at, *near, all_mixed, mixed_s, far_piece, w_one, w_two, w_three)
    with jax.named_scope("out_z"):
        far_got = swap(far, "zh", 1)

    last = pl.pallas_call(
        far_last_kernel,
        in_specs=[SMEM] + [VMEM] * 6,
        out_specs=VMEM,
        out_shape=shaped((2 * tokens, features), BF16),
        cost_estimate=cost(4 * tokens * depth * features, 6 * tokens * depth),
        name="far_products_last",
    )(at, three, three_s, all_mixed, mixed_s, far_weight, far_down)
    with jax.named_scope("out_z_last"):
        last_got = swap(last, "zh", 1)

    total = step(total, "y", far)
    with jax.named_scope("gate_core_back"):
        other = swap(total, "c", 1)
    gate_grad = jnp.where(
        c == 0, jnp.concatenate([total, other], axis=1), jnp.concatenate([other, total], axis=1)
    )

    own_out = pl.pallas_call(
        own_kernel,
        in_specs=[SMEM] + [VMEM] * 12 + [ANY],
        out_specs=VMEM,
        out_shape=shaped((4, 2 * tokens, features), BF16),
        cost_estimate=cost(16 * tokens * depth * features, 24 * tokens * depth),
        name="own_products",
    )(at, *near, three, three_s, all_mixed, mixed_s, weight, down, last)
    out = pl.pallas_call(
        place_kernel,
        in_specs=[SMEM, VMEM, VMEM, VMEM],
        out_specs=HBM,
        out_shape=shaped((4, 2, 2, tokens, features), BF16),
        scratch_shapes=[pltpu.SemaphoreType.DMA((16,))],
        name="place",
    )(at, own_out, far_got, last_got)
    return gate_grad, out.reshape(16 * tokens, features)


def solution(mesh):
    grid = Mesh(mesh.devices.reshape(4, 4, 4, 2, 2), AXES)
    dp, tensor = ("x", "zl"), ("y", "zh", "c")
    return jax.shard_map(
        on_device,
        mesh=grid,
        in_specs=(
            P(AXES, None),
            P(AXES, None),
            P(dp, tensor),
            P(tensor, None),
            P(tensor, None),
            P(),
            P(),
        ),
        out_specs=(P(), P(dp, tensor)),
        check_vma=False,
    )
```

time: 217 us -> 176 us (0.81)
  the two profiles are of different devices: /device:TPU:6 before, /device:TPU:33 now
where the time goes in v3:
time: 176 us; the launch traced here: 175 us
  starting transfers between devices  62.3 us (35%)
  Pallas kernels  60.8 us (35%)
  waiting for transfers between devices  35.9 us (20%)
  local copies, waits for them, and re-layouts  12.9 us (7%)
  other arithmetic  2.26 us (1%)
    ppermute x25, starting transfers between devices, swap(): return lax.ppermute(value, axis, [(i, i ^ mask) for i in range(size)])  51.2 us
    ppermute x25, waiting for transfers between devices, swap(): return lax.ppermute(value, axis, [(i, i ^ mask) for i in range(size)])  35.3 us
    pallas_call x1, Pallas kernels, on_device(): pl.pallas_call(split_kernel, in_specs=[SMEM, HBM, HBM], out_specs=HBM, ou...  20.3 us
    unnamed x78, local copies, waits for them, and re-layouts  12.9 us
    ppermute x6, starting transfers between devices, ring(): return lax.ppermute(value, (axis, 'c'), pairs)  11.1 us
    pallas_call x1, Pallas kernels, on_device(): pl.pallas_call(own_kernel, in_specs=[SMEM] + [VMEM] * 12 + [ANY], out_spe...  8.09 us
    pallas_call x1, Pallas kernels, on_device(): pl.pallas_call(far_kernel, in_specs=[SMEM] + [VMEM] * 12, out_specs=[VMEM...  6.93 us
    pallas_call x3, Pallas kernels, add4(): pl.pallas_call(add4_kernel, in_specs=[VMEM] * 4 + [ANY] * (len(parts) - 4...  4.9 us
  transfers between devices with their start and end apart: 31, of which 15 were waited for; matrix products, arithmetic and copies ran while one was open for 1% of the time, Pallas kernels for 33%

profile of v3, /device:TPU:33, one launch (start us, length us, event | category | flops | bytes accessed | tf_op | source)
XLA Modules:
  0.0 175.1 jit_solution(8473765846123098065)
XLA Ops:
  0.6 2.8 %collective-permute-start.9 = (bf16[128,4608]{1,0:T(8,128)(2,1)}, bf16[128,4608]{1,0:T(8,128)(2,1)}, u32[]{:S(2)}, u32[]{:S(2)}) collective-permute-start(bf16[128,4608]{1,0:T(8,128)(2,1)} %own.3), channel_id=1, source_target_pairs={{0,4},{1,13},{4,8},{5,1},{8,12},{9,5},{12,0},{13,9},{2,6},{3,15},{... | collective-permute-start | bytes 3538952 | tf_op jit(solution)/shard_map/tokens_y/ppermute | solution.py:24
  4.1 20.3 %split.1 = bf16[64,4736]{1,0:T(8,128)(2,1)} custom-call(s32[4]{0:T(128)} %pad_add_fusion.at, bf16[256,4608]{1,0:T(8,128)(2,1)} %weight.3, bf16[256,128]{1,0:T(8,128)(2,1)} %down.5), custom_call_target="tpu_custom_call" | custom-call | tf_op jit(solution)/shard_map/split/pallas_call | solution.py:243
  24.4 6.1 %collective-permute-start.10 = (bf16[64,4736]{1,0:T(8,128)(2,1)}, bf16[64,4736]{1,0:T(8,128)(2,1)}, u32[]{:S(2)}, u32[]{:S(2)}) collective-permute-start(bf16[64,4736]{1,0:T(8,128)(2,1)} %split.1), channel_id=1, source_target_pairs={{0,2},{2,0},{1,3},{3,1},{4,6},{6,4},{5,7},{7,5},{8,10},{10,8},{9,1... | collective-permute-start | bytes 1818632 | tf_op jit(solution)/shard_map/weight_z/ppermute | solution.py:48
  30.5 1.2 copy-done.3
  33.2 1.6 rank_products.1
  35.8 3.2 %token_values.1 = (bf16[128,128]{1,0:T(8,128)(2,1)S(1)}, f32[8,128]{1,0:T(8,128)S(1)}, f32[128,128]{1,0:T(8,128)S(1)}) custom-call(s32[4]{0:T(128)S(1)} %copy-done.9, bf16[128,4608]{1,0:T(8,128)(2,1)S(1)} %copy-done.1, bf16[128,4608]{1,0:T(8,128)(2,1)S(1)} %copy-done, bf16[128,4608]{1,0:T(8,128)(2,1)S(1)} %copy-done.2, bf16[8,4608]{1,0:T(8,128)(2,1)S(1)} %copy-done.7), custom_call_target="tpu_custom_call" | custom-call | flops 452984832 | bytes 7077888 | tf_op jit(solution)/shard_map/token_values/pallas_call | solution.py:275
  41.5 1.9 %rank_sum_core.1 = (bf16[3,128,128]{2,1,0:T(8,128)(2,1)}, bf16[3,128,128]{2,1,0:T(8,128)(2,1)}, bf16[3,128,128]{2,1,0:T(8,128)(2,1)}, f32[2,128,128]{2,1,0:T(8,128)}) custom-call(s32[4]{0:T(128)} %pad_add_fusion.at, f32[4,2,128,128]{3,2,1,0:T(8,128)} %copy-done.5, bf16[4,2,128,128]{3,2,1,0:T(8,128)(2,1)} %copy-done.21, bf16[128,128]{1,0:T(8,128)(2,1)} %copy-done.6), custom_call_target="tpu_custom_call" | custom-call | tf_op jit(solution)/shard_map/rank_sum_core/pallas_call | solution.py:293
  44.5 1.3 collective-permute-start.2
  45.8 1.5 collective-permute-start.3
  47.7 3.4 %collective-permute-done.2.second = bf16[3,128,128]{2,1,0:T(8,128)(2,1)S(1)} collective-permute-done((bf16[3,128,128]{2,1,0:T(8,128)(2,1)}, bf16[3,128,128]{2,1,0:T(8,128)(2,1)S(1)}, u32[]{:S(2)}, u32[]{:S(2)}) %collective-permute-start.2) | collective-permute-done | bytes 98336 | tf_op jit(solution)/shard_map/act_y/ppermute | solution.py:48
  51.2 2.4 %collective-permute-done.3.third = bf16[3,128,128]{2,1,0:T(8,128)(2,1)S(1)} collective-permute-done((bf16[3,128,128]{2,1,0:T(8,128)(2,1)}, bf16[3,128,128]{2,1,0:T(8,128)(2,1)S(1)}, u32[]{:S(2)}, u32[]{:S(2)}) %collective-permute-start.3) | collective-permute-done | bytes 98336 | tf_op jit(solution)/shard_map/act_y/ppermute | solution.py:48
  54.2 1.8 %rank_sum_y.1 = (f32[128,128]{1,0:T(8,128)}, bf16[128,128]{1,0:T(8,128)(2,1)}, bf16[4,128,128]{2,1,0:T(8,128)(2,1)}) custom-call(s32[4]{0:T(128)} %pad_add_fusion.at, f32[2,128,128]{2,1,0:T(8,128)} %get-tuple-element.24.rest, bf16[3,128,128]{2,1,0:T(8,128)(2,1)} %copy-done.23, bf16[3,128,128]{2,1,0:T(8,128)(2,1)} %copy-done.24, ...), custom_call_target="tpu_custom_call" | custom-call | tf_op jit(solution)/shard_map/rank_sum_y/pallas_call | solution.py:304
  56.0 1.5 collective-permute-done.10.refs_1_
  57.9 2.5 %collective-permute-start.11 = (bf16[64,4736]{1,0:T(8,128)(2,1)}, bf16[64,4736]{1,0:T(8,128)(2,1)S(1)}, u32[]{:S(2)}, u32[]{:S(2)}) collective-permute-start(bf16[64,4736]{1,0:T(8,128)(2,1)} %get-tuple-element.34.refs_0_), channel_id=1, source_target_pairs={{0,64},{1,193},{64,128},{65,1},{128,192},{129,65},{192,0},{193,129... | collective-permute-start | bytes 1818632 | tf_op jit(solution)/shard_map/weight_x/ppermute | solution.py:24
  60.4 5.5 %collective-permute-start.4 = (bf16[128,128]{1,0:T(8,128)(2,1)S(1)}, bf16[128,128]{1,0:T(8,128)(2,1)S(1)}, u32[]{:S(2)}, u32[]{:S(2)}) collective-permute-start(bf16[128,128]{1,0:T(8,128)(2,1)S(1)} %copy-done.37), channel_id=1, source_target_pairs={{0,2},{2,0},{1,3},{3,1},{4,6},{6,4},{5,7},{7,5},{8,10},{10,8},{9,1... | collective-permute-start | bytes 98312 | tf_op jit(solution)/shard_map/act_z/ppermute | solution.py:48
  65.9 1.4 collective-permute-done.4.got
  67.9 2.7 %gate_products.1 = (f32[8,2304]{1,0:T(8,128)}, f32[8,2304]{1,0:T(8,128)}) custom-call(s32[4]{0:T(128)} %pad_add_fusion.at, f32[128,128]{1,0:T(8,128)} %get-tuple-element.28.keep, bf16[128,128]{1,0:T(8,128)(2,1)} %copy-done.38, f32[128,128]{1,0:T(8,128)} %copy-done.8, f32[8,128]{1,0:T(8,128)} %copy-done.10, bf16[128,4608]{1,0:T(8,128)(2,1)} %hidden.3), custom_call_target="tpu_custom_call" | custom-call | tf_op jit(solution)/shard_map/gate_products/pallas_call | solution.py:327
  72.8 1.6 gate_sum.5.refs_1_.first
  75.0 2.7 %collective-permute-start.7 = (f32[8,2304]{1,0:T(8,128)}, f32[8,2304]{1,0:T(8,128)S(1)}, u32[]{:S(2)}, u32[]{:S(2)}) collective-permute-start(f32[8,2304]{1,0:T(8,128)} %gate_sum.5.refs_1_.first), channel_id=1, source_target_pairs={{0,32},{16,48},{32,0},{48,16},{1,33},{17,49},{33,1},{49,17},{2,34}... | collective-permute-start | bytes 221192 | tf_op jit(solution)/shard_map/gate_zl/ppermute | solution.py:48
  78.6 4.4 %collective-permute-done.7.third = f32[8,2304]{1,0:T(8,128)S(1)} collective-permute-done((f32[8,2304]{1,0:T(8,128)}, f32[8,2304]{1,0:T(8,128)S(1)}, u32[]{:S(2)}, u32[]{:S(2)}) %collective-permute-start.7) | collective-permute-done | bytes 73760 | tf_op jit(solution)/shard_map/gate_zl/ppermute | solution.py:48
  82.9 1.6 collective-permute-done.8.fourth
  85.2 1.6 gate_sum.6.refs_1_.left
  87.8 2.6 %collective-permute-start.27 = (bf16[128,4608]{1,0:T(8,128)(2,1)}, bf16[128,4608]{1,0:T(8,128)(2,1)}, u32[]{:S(2)}, u32[]{:S(2)}) collective-permute-start(bf16[128,4608]{1,0:T(8,128)(2,1)} %fence.6.refs_0_.two), channel_id=1, source_target_pairs={{0,4},{1,13},{4,8},{5,1},{8,12},{9,5},{12,0},{13,9},{2,6},{3,15},{... | collective-permute-start | bytes 3538952 | tf_op jit(solution)/shard_map/tokens_y/ppermute | solution.py:24
  90.5 1.5 collective-permute-start.17
  92.0 5.6 %collective-permute-start.12 = (f32[8,2304]{1,0:T(8,128)S(1)}, f32[8,2304]{1,0:T(8,128)S(1)}, u32[]{:S(2)}, u32[]{:S(2)}) collective-permute-start(f32[8,2304]{1,0:T(8,128)S(1)} %copy-done.18), channel_id=1, source_target_pairs={{0,2},{2,0},{1,3},{3,1},{4,6},{6,4},{5,7},{7,5},{8,10},{10,8},{9,1... | collective-permute-start | bytes 221192 | tf_op jit(solution)/shard_map/gate_zh/ppermute | solution.py:48
  98.3 1.3 collective-permute-done.12.right
  99.7 2.7 %collective-permute-start.23 = (bf16[128,4608]{1,0:T(8,128)(2,1)}, bf16[128,4608]{1,0:T(8,128)(2,1)}, u32[]{:S(2)}, u32[]{:S(2)}) collective-permute-start(bf16[128,4608]{1,0:T(8,128)(2,1)} %fence.6.refs_0_.two), channel_id=1, source_target_pairs={{0,1},{1,0},{2,3},{3,2},{4,5},{5,4},{6,7},{7,6},{8,9},{9,8},{10,11... | collective-permute-start | bytes 3538952 | tf_op jit(solution)/shard_map/tokens_core/ppermute | solution.py:48
  102.4 1.6 gate_sum.7.refs_1_.first
  104.0 3.3 %collective-permute-done.14.second = f32[8,2304]{1,0:T(8,128)S(1)} collective-permute-done((f32[8,2304]{1,0:T(8,128)}, f32[8,2304]{1,0:T(8,128)S(1)}, u32[]{:S(2)}, u32[]{:S(2)}) %collective-permute-start.14) | collective-permute-done | bytes 73760 | tf_op jit(solution)/shard_map/gate_x/ppermute | solution.py:48
  107.3 1.5 collective-permute-start.15
  108.9 3.4 %collective-permute-done.15.third = f32[8,2304]{1,0:T(8,128)S(1)} collective-permute-done((f32[8,2304]{1,0:T(8,128)}, f32[8,2304]{1,0:T(8,128)S(1)}, u32[]{:S(2)}, u32[]{:S(2)}) %collective-permute-start.15) | collective-permute-done | bytes 73760 | tf_op jit(solution)/shard_map/gate_x/ppermute | solution.py:48
  112.3 1.3 collective-permute-start.16
  113.6 3.3 %collective-permute-done.16.fourth = f32[8,2304]{1,0:T(8,128)S(1)} collective-permute-done((f32[8,2304]{1,0:T(8,128)}, f32[8,2304]{1,0:T(8,128)S(1)}, u32[]{:S(2)}, u32[]{:S(2)}) %collective-permute-start.16) | collective-permute-done | bytes 73760 | tf_op jit(solution)/shard_map/gate_x/ppermute | solution.py:48
  116.9 1.3 collective-permute-start.25
  118.2 2.9 %collective-permute-start.28 = (bf16[128,4608]{1,0:T(8,128)(2,1)}, bf16[128,4608]{1,0:T(8,128)(2,1)S(1)}, u32[]{:S(2)}, u32[]{:S(2)}) collective-permute-start(bf16[128,4608]{1,0:T(8,128)(2,1)} %collective-permute-done.27.three), channel_id=1, source_target_pairs={{0,1},{1,0},{2,3},{3,2},{4,5},{5,4},{6,7},{7,6},{8,9},{9,8},{10,11... | collective-permute-start | bytes 3538952 | tf_op jit(solution)/shard_map/tokens_core/ppermute | solution.py:48
  121.1 1.6 gate_sum.8.first
  123.6 2.1 %collective-permute-start.19 = (f32[8,2304]{1,0:T(8,128)}, f32[8,2304]{1,0:T(8,128)S(1)}, u32[]{:S(2)}, u32[]{:S(2)}) collective-permute-start(f32[8,2304]{1,0:T(8,128)} %gate_sum.8.first), channel_id=1, source_target_pairs={{0,8},{4,12},{8,0},{12,4},{1,9},{5,13},{9,1},{13,5},{2,10},{6,14},... | collective-permute-start | bytes 221192 | tf_op jit(solution)/shard_map/gate_y/ppermute | solution.py:48
  126.3 1.2 collective-permute-start.20
  127.5 6.9 %far_products.1 = (bf16[3,256,256]{2,1,0:T(8,128)(2,1)}, bf16[256,4608]{1,0:T(8,128)(2,1)}, bf16[256,128]{1,0:T(8,128)(2,1)}) custom-call(s32[4]{0:T(128)} %pad_add_fusion.at, bf16[128,4608]{1,0:T(8,128)(2,1)} %own.3, bf16[128,4608]{1,0:T(8,128)(2,1)} %collective-permute-done.21.own_s, bf16[128,4608]{1,0:T(8,128)(2,1)} %get-tuple-element.35.one, ...), custom_call_target="tpu_custom_call" | custom-call | flops 1862270976 | bytes 10911744 | tf_op jit(solution)/shard_map/far_products/pallas_call | solution.py:379
  135.1 1.6 gate_sum.9
  136.7 6.4 %collective-permute-start.26 = (f32[8,2304]{1,0:T(8,128)}, f32[8,2304]{1,0:T(8,128)S(1)}, u32[]{:S(2)}, u32[]{:S(2)}) collective-permute-start(f32[8,2304]{1,0:T(8,128)} %gate_sum.9), channel_id=1, source_target_pairs={{0,1},{1,0},{2,3},{3,2},{4,5},{5,4},{6,7},{7,6},{8,9},{9,8},{10,11... | collective-permute-start | bytes 221192 | tf_op jit(solution)/shard_map/gate_core_back/ppermute | solution.py:48
  143.2 5.3 %collective-permute-start.29 = (bf16[3,256,256]{2,1,0:T(8,128)(2,1)}, bf16[3,256,256]{2,1,0:T(8,128)(2,1)S(1)}, u32[]{:S(2)}, u32[]{:S(2)}) collective-permute-start(bf16[3,256,256]{2,1,0:T(8,128)(2,1)} %get-tuple-element.37.refs_0_), channel_id=1, source_target_pairs={{0,2},{2,0},{1,3},{3,1},{4,6},{6,4},{5,7},{7,5},{8,10},{10,8},{9,1... | collective-permute-start | bytes 1179656 | tf_op jit(solution)/shard_map/out_z/ppermute | solution.py:48
  148.5 1.6 maximum_select_fusion
  151.2 3.9 %far_products_last.1.tie = bf16[256,256]{1,0:T(8,128)(2,1)} custom-call(s32[4]{0:T(128)} %pad_add_fusion.at, bf16[128,4608]{1,0:T(8,128)(2,1)} %collective-permute-done.27.three, bf16[128,4608]{1,0:T(8,128)(2,1)} %copy-done.15, bf16[4,128,128]{2,1,0:T(8,128)(2,1)} %get-tuple-element.36.mixed, bf16[4,128,128]{2,1,0:T(8,128)(2,1)} %copy-done.17, ...), custom_call_target="tpu_custom_call" | custom-call | flops 620756992 | bytes 3637248 | tf_op jit(solution)/shard_map/far_products_last/pallas_call | solution.py:394
  156.2 8.1 %own_products.1.own = bf16[4,256,256]{2,1,0:T(8,128)(2,1)} custom-call(s32[4]{0:T(128)} %pad_add_fusion.at, bf16[128,4608]{1,0:T(8,128)(2,1)} %own.3, bf16[128,4608]{1,0:T(8,128)(2,1)} %collective-permute-done.21.own_s, bf16[128,4608]{1,0:T(8,128)(2,1)} %get-tuple-element.35.one, bf16[128,4608]{1,0:T(8,128)(2,1)} %collective-permute-done.22.one_s, ...), custom_call_target="tpu_custom_call" | custom-call | flops 2483027968 | bytes 14548992 | tf_op jit(solution)/shard_map/own_products/pallas_call | solution.py:412
  164.3 4.9 %collective-permute-done.29.got = bf16[3,256,256]{2,1,0:T(8,128)(2,1)S(1)} collective-permute-done((bf16[3,256,256]{2,1,0:T(8,128)(2,1)}, bf16[3,256,256]{2,1,0:T(8,128)(2,1)S(1)}, u32[]{:S(2)}, u32[]{:S(2)}) %collective-permute-start.29) | collective-permute-done | bytes 393248 | tf_op jit(solution)/shard_map/out_z/ppermute | solution.py:48
  169.2 2.8 %collective-permute-done.30.last = bf16[256,256]{1,0:T(8,128)(2,1)S(1)} collective-permute-done((bf16[256,256]{1,0:T(8,128)(2,1)}, bf16[256,256]{1,0:T(8,128)(2,1)S(1)}, u32[]{:S(2)}, u32[]{:S(2)}) %collective-permute-start.30) | collective-permute-done | bytes 131104 | tf_op jit(solution)/shard_map/out_z_last/ppermute | solution.py:48
  172.7 2.3 %place.1 = bf16[4,2,2,128,256]{4,3,2,1,0:T(8,128)(2,1)} custom-call(s32[4]{0:T(128)} %pad_add_fusion.at, bf16[4,256,256]{2,1,0:T(8,128)(2,1)} %own_products.1.own, bf16[3,256,256]{2,1,0:T(8,128)(2,1)} %copy-done.20, bf16[256,256]{1,0:T(8,128)(2,1)} %copy-done.22), custom_call_target="tpu_custom_call" | custom-call | tf_op jit(solution)/shard_map/place/pallas_call | solution.py:420
  (113 shorter events, 19.9 us)
Async XLA Ops:
  0.6 56.9 %collective-permute-start.9 = (bf16[128,4608]{1,0:T(8,128)(2,1)}, bf16[128,4608]{1,0:T(8,128)(2,1)}, u32[]{:S(2)}, u32[]{:S(2)}) collective-permute-start(bf16[128,4608]{1,0:T(8,128)(2,1)} %own.3), channel_id=1, source_target_pairs={{0,4},{1,13},{4,8},{5,1},{8,12},{9,5},{12,0},{13,9},{2,6},{3,15},{... | collective-permute-start | bytes 3538952 | tf_op jit(solution)/shard_map/tokens_y/ppermute | solution.py:24
  4.1 30.8 %copy-start = (bf16[128,4608]{1,0:T(8,128)(2,1)S(1)}, bf16[128,4608]{1,0:T(8,128)(2,1)}, u32[]{:S(2)}) copy-start(bf16[128,4608]{1,0:T(8,128)(2,1)} %own.3) | copy-start | bytes 3538948
  4.1 30.8 %copy-start.1 = (bf16[128,4608]{1,0:T(8,128)(2,1)S(1)}, bf16[128,4608]{1,0:T(8,128)(2,1)}, u32[]{:S(2)}) copy-start(bf16[128,4608]{1,0:T(8,128)(2,1)} %hidden.3) | copy-start | bytes 3538948
  4.1 30.8 %copy-start.2 = (bf16[128,4608]{1,0:T(8,128)(2,1)S(1)}, bf16[128,4608]{1,0:T(8,128)(2,1)}, u32[]{:S(2)}) copy-start(bf16[128,4608]{1,0:T(8,128)(2,1)} %up.1) | copy-start | bytes 3538948
  24.4 33.2 %collective-permute-start.10 = (bf16[64,4736]{1,0:T(8,128)(2,1)}, bf16[64,4736]{1,0:T(8,128)(2,1)}, u32[]{:S(2)}, u32[]{:S(2)}) collective-permute-start(bf16[64,4736]{1,0:T(8,128)(2,1)} %split.1), channel_id=1, source_target_pairs={{0,2},{2,0},{1,3},{3,1},{4,6},{6,4},{5,7},{7,5},{8,10},{10,8},{9,1... | collective-permute-start | bytes 1818632 | tf_op jit(solution)/shard_map/weight_z/ppermute | solution.py:48
  34.7 4.3 %copy-start.5 = (f32[4,2,128,128]{3,2,1,0:T(8,128)}, f32[4,2,128,128]{3,2,1,0:T(8,128)S(1)}, u32[]{:S(2)}) copy-start(f32[4,2,128,128]{3,2,1,0:T(8,128)S(1)} %get-tuple-element.21.keep) | copy-start | bytes 1572868
  34.7 6.1 %collective-permute-start = (bf16[4,2,128,128]{3,2,1,0:T(8,128)(2,1)S(1)}, bf16[4,2,128,128]{3,2,1,0:T(8,128)(2,1)S(1)}, u32[]{:S(2)}, u32[]{:S(2)}) collective-permute-start(bf16[4,2,128,128]{3,2,1,0:T(8,128)(2,1)S(1)} %get-tuple-element.22), channel_id=1, source_target_pairs={{0,1},{1,0},{2,3},{3,2},{4,5},{5,4},{6,7},{7,6},{8,9},{9,8},{10,11... | collective-permute-start | bytes 786440 | tf_op jit(solution)/shard_map/act_core/ppermute | solution.py:48
  43.5 4.3 %collective-permute-start.1 = (bf16[3,128,128]{2,1,0:T(8,128)(2,1)}, bf16[3,128,128]{2,1,0:T(8,128)(2,1)S(1)}, u32[]{:S(2)}, u32[]{:S(2)}) collective-permute-start(bf16[3,128,128]{2,1,0:T(8,128)(2,1)} %get-tuple-element.25), channel_id=1, source_target_pairs={{0,4},{4,0},{8,12},{12,8},{1,5},{5,1},{9,13},{13,9},{2,6},{6,2},{1... | collective-permute-start | bytes 294920 | tf_op jit(solution)/shard_map/act_y/ppermute | solution.py:48
  44.5 6.7 %collective-permute-start.2 = (bf16[3,128,128]{2,1,0:T(8,128)(2,1)}, bf16[3,128,128]{2,1,0:T(8,128)(2,1)S(1)}, u32[]{:S(2)}, u32[]{:S(2)}) collective-permute-start(bf16[3,128,128]{2,1,0:T(8,128)(2,1)} %get-tuple-element.26), channel_id=1, source_target_pairs={{0,8},{4,12},{8,0},{12,4},{1,9},{5,13},{9,1},{13,5},{2,10},{6,14},... | collective-permute-start | bytes 294920 | tf_op jit(solution)/shard_map/act_y/ppermute | solution.py:48
  45.8 7.7 %collective-permute-start.3 = (bf16[3,128,128]{2,1,0:T(8,128)(2,1)}, bf16[3,128,128]{2,1,0:T(8,128)(2,1)S(1)}, u32[]{:S(2)}, u32[]{:S(2)}) collective-permute-start(bf16[3,128,128]{2,1,0:T(8,128)(2,1)} %get-tuple-element.27), channel_id=1, source_target_pairs={{0,12},{4,8},{8,4},{12,0},{1,13},{5,9},{9,5},{13,1},{2,14},{6,10},... | collective-permute-start | bytes 294920 | tf_op jit(solution)/shard_map/act_y/ppermute | solution.py:48
  47.7 5.8 %copy-start.23 = (bf16[3,128,128]{2,1,0:T(8,128)(2,1)}, bf16[3,128,128]{2,1,0:T(8,128)(2,1)S(1)}, u32[]{:S(2)}) copy-start(bf16[3,128,128]{2,1,0:T(8,128)(2,1)S(1)} %collective-permute-done.1.first) | copy-start | bytes 294916
  56.0 4.4 %copy-start.37 = (bf16[128,128]{1,0:T(8,128)(2,1)S(1)}, bf16[128,128]{1,0:T(8,128)(2,1)}, u32[]{:S(2)}) copy-start(bf16[128,128]{1,0:T(8,128)(2,1)} %get-tuple-element.29.refs_2_) | copy-start | bytes 98308
  57.5 29.3 %collective-permute-start.13 = (bf16[128,4608]{1,0:T(8,128)(2,1)}, bf16[128,4608]{1,0:T(8,128)(2,1)S(1)}, u32[]{:S(2)}, u32[]{:S(2)}) collective-permute-start(bf16[128,4608]{1,0:T(8,128)(2,1)} %get-tuple-element.35.one), channel_id=1, source_target_pairs={{0,4},{1,13},{4,8},{5,1},{8,12},{9,5},{12,0},{13,9},{2,6},{3,15},{... | collective-permute-start | bytes 3538952 | tf_op jit(solution)/shard_map/tokens_y/ppermute | solution.py:24
  57.9 19.8 %collective-permute-start.11 = (bf16[64,4736]{1,0:T(8,128)(2,1)}, bf16[64,4736]{1,0:T(8,128)(2,1)S(1)}, u32[]{:S(2)}, u32[]{:S(2)}) collective-permute-start(bf16[64,4736]{1,0:T(8,128)(2,1)} %get-tuple-element.34.refs_0_), channel_id=1, source_target_pairs={{0,64},{1,193},{64,128},{65,1},{128,192},{129,65},{192,0},{193,129... | collective-permute-start | bytes 1818632 | tf_op jit(solution)/shard_map/weight_x/ppermute | solution.py:24
  60.4 6.9 %collective-permute-start.4 = (bf16[128,128]{1,0:T(8,128)(2,1)S(1)}, bf16[128,128]{1,0:T(8,128)(2,1)S(1)}, u32[]{:S(2)}, u32[]{:S(2)}) collective-permute-start(bf16[128,128]{1,0:T(8,128)(2,1)S(1)} %copy-done.37), channel_id=1, source_target_pairs={{0,2},{2,0},{1,3},{3,1},{4,6},{6,4},{5,7},{7,5},{8,10},{10,8},{9,1... | collective-permute-start | bytes 98312 | tf_op jit(solution)/shard_map/act_z/ppermute | solution.py:48
  70.6 1.5 collective-permute-start.5
  74.3 4.2 %collective-permute-start.6 = (f32[8,2304]{1,0:T(8,128)}, f32[8,2304]{1,0:T(8,128)S(1)}, u32[]{:S(2)}, u32[]{:S(2)}) collective-permute-start(f32[8,2304]{1,0:T(8,128)} %gate_sum.5.refs_1_.first), channel_id=1, source_target_pairs={{0,16},{16,0},{32,48},{48,32},{1,17},{17,1},{33,49},{49,33},{2,18}... | collective-permute-start | bytes 221192 | tf_op jit(solution)/shard_map/gate_zl/ppermute | solution.py:48
  75.0 7.9 %collective-permute-start.7 = (f32[8,2304]{1,0:T(8,128)}, f32[8,2304]{1,0:T(8,128)S(1)}, u32[]{:S(2)}, u32[]{:S(2)}) collective-permute-start(f32[8,2304]{1,0:T(8,128)} %gate_sum.5.refs_1_.first), channel_id=1, source_target_pairs={{0,32},{16,48},{32,0},{48,16},{1,33},{17,49},{33,1},{49,17},{2,34}... | collective-permute-start | bytes 221192 | tf_op jit(solution)/shard_map/gate_zl/ppermute | solution.py:48
  77.7 6.8 %collective-permute-start.8 = (f32[8,2304]{1,0:T(8,128)}, f32[8,2304]{1,0:T(8,128)S(1)}, u32[]{:S(2)}, u32[]{:S(2)}) collective-permute-start(f32[8,2304]{1,0:T(8,128)} %gate_sum.5.refs_1_.first), channel_id=1, source_target_pairs={{0,48},{16,32},{32,16},{48,0},{1,49},{17,33},{33,17},{49,1},{2,50}... | collective-permute-start | bytes 221192 | tf_op jit(solution)/shard_map/gate_zl/ppermute | solution.py:48
  78.6 6.0 %copy-start.33 = (f32[8,2304]{1,0:T(8,128)}, f32[8,2304]{1,0:T(8,128)S(1)}, u32[]{:S(2)}) copy-start(f32[8,2304]{1,0:T(8,128)S(1)} %collective-permute-done.6.second) | copy-start | bytes 221188
  86.8 3.7 %copy-start.14 = (bf16[64,4736]{1,0:T(8,128)(2,1)S(1)}, bf16[64,4736]{1,0:T(8,128)(2,1)}, u32[]{:S(2)}) copy-start(bf16[64,4736]{1,0:T(8,128)(2,1)} %fence.5.refs_0_.refs_1_) | copy-start | bytes 1818628
  86.8 5.2 %copy-start.16 = (bf16[4,128,128]{2,1,0:T(8,128)(2,1)S(1)}, bf16[4,128,128]{2,1,0:T(8,128)(2,1)}, u32[]{:S(2)}) copy-start(bf16[4,128,128]{2,1,0:T(8,128)(2,1)} %get-tuple-element.36.mixed) | copy-start | bytes 393220
  86.8 5.2 %copy-start.18 = (f32[8,2304]{1,0:T(8,128)S(1)}, f32[8,2304]{1,0:T(8,128)}, u32[]{:S(2)}) copy-start(f32[8,2304]{1,0:T(8,128)} %gate_sum.6.refs_1_.left) | copy-start | bytes 221188
  87.8 30.4 %collective-permute-start.27 = (bf16[128,4608]{1,0:T(8,128)(2,1)}, bf16[128,4608]{1,0:T(8,128)(2,1)}, u32[]{:S(2)}, u32[]{:S(2)}) collective-permute-start(bf16[128,4608]{1,0:T(8,128)(2,1)} %fence.6.refs_0_.two), channel_id=1, source_target_pairs={{0,4},{1,13},{4,8},{5,1},{8,12},{9,5},{12,0},{13,9},{2,6},{3,15},{... | collective-permute-start | bytes 3538952 | tf_op jit(solution)/shard_map/tokens_y/ppermute | solution.py:24
  90.5 13.4 %collective-permute-start.17 = (bf16[64,4736]{1,0:T(8,128)(2,1)S(1)}, bf16[64,4736]{1,0:T(8,128)(2,1)S(1)}, u32[]{:S(2)}, u32[]{:S(2)}) collective-permute-start(bf16[64,4736]{1,0:T(8,128)(2,1)S(1)} %copy-done.14), channel_id=1, source_target_pairs={{0,64},{1,193},{64,128},{65,1},{128,192},{129,65},{192,0},{193,129... | collective-permute-start | bytes 1818632 | tf_op jit(solution)/shard_map/weight_x/ppermute | solution.py:24
  91.9 6.3 %collective-permute-start.24 = (bf16[4,128,128]{2,1,0:T(8,128)(2,1)S(1)}, bf16[4,128,128]{2,1,0:T(8,128)(2,1)S(1)}, u32[]{:S(2)}, u32[]{:S(2)}) collective-permute-start(bf16[4,128,128]{2,1,0:T(8,128)(2,1)S(1)} %copy-done.16), channel_id=1, source_target_pairs={{0,1},{1,0},{2,3},{3,2},{4,5},{5,4},{6,7},{7,6},{8,9},{9,8},{10,11... | collective-permute-start | bytes 393224 | tf_op jit(solution)/shard_map/mixed_core/ppermute | solution.py:48
  92.0 7.7 %collective-permute-start.12 = (f32[8,2304]{1,0:T(8,128)S(1)}, f32[8,2304]{1,0:T(8,128)S(1)}, u32[]{:S(2)}, u32[]{:S(2)}) collective-permute-start(f32[8,2304]{1,0:T(8,128)S(1)} %copy-done.18), channel_id=1, source_target_pairs={{0,2},{2,0},{1,3},{3,1},{4,6},{6,4},{5,7},{7,5},{8,10},{10,8},{9,1... | collective-permute-start | bytes 221192 | tf_op jit(solution)/shard_map/gate_zh/ppermute | solution.py:48
  97.5 25.2 %collective-permute-start.21 = (bf16[128,4608]{1,0:T(8,128)(2,1)S(1)}, bf16[128,4608]{1,0:T(8,128)(2,1)}, u32[]{:S(2)}, u32[]{:S(2)}) collective-permute-start(bf16[128,4608]{1,0:T(8,128)(2,1)S(1)} %copy-done), channel_id=1, source_target_pairs={{0,1},{1,0},{2,3},{3,2},{4,5},{5,4},{6,7},{7,6},{8,9},{9,8},{10,11... | collective-permute-start | bytes 3538952 | tf_op jit(solution)/shard_map/tokens_core/ppermute | solution.py:48
  98.3 15.3 %copy-start.17 = (bf16[4,128,128]{2,1,0:T(8,128)(2,1)}, bf16[4,128,128]{2,1,0:T(8,128)(2,1)S(1)}, u32[]{:S(2)}) copy-start(bf16[4,128,128]{2,1,0:T(8,128)(2,1)S(1)} %collective-permute-done.24.mixed_s) | copy-start | bytes 393220
  98.3 25.4 %collective-permute-start.22 = (bf16[128,4608]{1,0:T(8,128)(2,1)}, bf16[128,4608]{1,0:T(8,128)(2,1)}, u32[]{:S(2)}, u32[]{:S(2)}) collective-permute-start(bf16[128,4608]{1,0:T(8,128)(2,1)} %get-tuple-element.35.one), channel_id=1, source_target_pairs={{0,1},{1,0},{2,3},{3,2},{4,5},{5,4},{6,7},{7,6},{8,9},{9,8},{10,11... | collective-permute-start | bytes 3538952 | tf_op jit(solution)/shard_map/tokens_core/ppermute | solution.py:48
  99.7 2.7 %copy-start.29 = (f32[8,2304]{1,0:T(8,128)}, f32[8,2304]{1,0:T(8,128)S(1)}, u32[]{:S(2)}) copy-start(f32[8,2304]{1,0:T(8,128)S(1)} %collective-permute-done.12.right) | copy-start | bytes 221188
  99.7 27.8 %collective-permute-start.23 = (bf16[128,4608]{1,0:T(8,128)(2,1)}, bf16[128,4608]{1,0:T(8,128)(2,1)}, u32[]{:S(2)}, u32[]{:S(2)}) collective-permute-start(bf16[128,4608]{1,0:T(8,128)(2,1)} %fence.6.refs_0_.two), channel_id=1, source_target_pairs={{0,1},{1,0},{2,3},{3,2},{4,5},{5,4},{6,7},{7,6},{8,9},{9,8},{10,11... | collective-permute-start | bytes 3538952 | tf_op jit(solution)/shard_map/tokens_core/ppermute | solution.py:48
  103.9 9.7 %copy-start.12 = (bf16[64,4736]{1,0:T(8,128)(2,1)}, bf16[64,4736]{1,0:T(8,128)(2,1)S(1)}, u32[]{:S(2)}) copy-start(bf16[64,4736]{1,0:T(8,128)(2,1)S(1)} %collective-permute-done.17.refs_0_) | copy-start | bytes 1818628
  103.9 3.4 %collective-permute-start.14 = (f32[8,2304]{1,0:T(8,128)}, f32[8,2304]{1,0:T(8,128)S(1)}, u32[]{:S(2)}, u32[]{:S(2)}) collective-permute-start(f32[8,2304]{1,0:T(8,128)} %gate_sum.7.refs_1_.first), channel_id=1, source_target_pairs={{0,64},{64,0},{128,192},{192,128},{1,65},{65,1},{129,193},{193,129... | collective-permute-start | bytes 221192 | tf_op jit(solution)/shard_map/gate_x/ppermute | solution.py:48
  107.3 13.7 %copy-start.31 = (f32[8,2304]{1,0:T(8,128)}, f32[8,2304]{1,0:T(8,128)S(1)}, u32[]{:S(2)}) copy-start(f32[8,2304]{1,0:T(8,128)S(1)} %collective-permute-done.14.second) | copy-start | bytes 221188
  107.3 4.9 %collective-permute-start.15 = (f32[8,2304]{1,0:T(8,128)}, f32[8,2304]{1,0:T(8,128)S(1)}, u32[]{:S(2)}, u32[]{:S(2)}) collective-permute-start(f32[8,2304]{1,0:T(8,128)} %gate_sum.7.refs_1_.first), channel_id=1, source_target_pairs={{0,128},{64,192},{128,0},{192,64},{1,129},{65,193},{129,1},{193,65... | collective-permute-start | bytes 221192 | tf_op jit(solution)/shard_map/gate_x/ppermute | solution.py:48
  112.3 8.8 %copy-start.32 = (f32[8,2304]{1,0:T(8,128)}, f32[8,2304]{1,0:T(8,128)S(1)}, u32[]{:S(2)}) copy-start(f32[8,2304]{1,0:T(8,128)S(1)} %collective-permute-done.15.third) | copy-start | bytes 221188
  112.3 4.6 %collective-permute-start.16 = (f32[8,2304]{1,0:T(8,128)}, f32[8,2304]{1,0:T(8,128)S(1)}, u32[]{:S(2)}, u32[]{:S(2)}) collective-permute-start(f32[8,2304]{1,0:T(8,128)} %gate_sum.7.refs_1_.first), channel_id=1, source_target_pairs={{0,192},{64,128},{128,64},{192,0},{1,193},{65,129},{129,65},{193,1... | collective-permute-start | bytes 221192 | tf_op jit(solution)/shard_map/gate_x/ppermute | solution.py:48
  116.9 4.2 %copy-start.35 = (f32[8,2304]{1,0:T(8,128)}, f32[8,2304]{1,0:T(8,128)S(1)}, u32[]{:S(2)}) copy-start(f32[8,2304]{1,0:T(8,128)S(1)} %collective-permute-done.16.fourth) | copy-start | bytes 221188
  116.9 9.4 %collective-permute-start.25 = (bf16[64,4736]{1,0:T(8,128)(2,1)}, bf16[64,4736]{1,0:T(8,128)(2,1)S(1)}, u32[]{:S(2)}, u32[]{:S(2)}) collective-permute-start(bf16[64,4736]{1,0:T(8,128)(2,1)} %fence.7.refs_0_.refs_2_), channel_id=1, source_target_pairs={{0,64},{1,193},{64,128},{65,1},{128,192},{129,65},{192,0},{193,129... | collective-permute-start | bytes 1818632 | tf_op jit(solution)/shard_map/weight_x/ppermute | solution.py:24
  118.2 31.9 %collective-permute-start.28 = (bf16[128,4608]{1,0:T(8,128)(2,1)}, bf16[128,4608]{1,0:T(8,128)(2,1)S(1)}, u32[]{:S(2)}, u32[]{:S(2)}) collective-permute-start(bf16[128,4608]{1,0:T(8,128)(2,1)} %collective-permute-done.27.three), channel_id=1, source_target_pairs={{0,1},{1,0},{2,3},{3,2},{4,5},{5,4},{6,7},{7,6},{8,9},{9,8},{10,11... | collective-permute-start | bytes 3538952 | tf_op jit(solution)/shard_map/tokens_core/ppermute | solution.py:48
  122.7 11.7 %collective-permute-start.18 = (f32[8,2304]{1,0:T(8,128)}, f32[8,2304]{1,0:T(8,128)S(1)}, u32[]{:S(2)}, u32[]{:S(2)}) collective-permute-start(f32[8,2304]{1,0:T(8,128)} %gate_sum.8.first), channel_id=1, source_target_pairs={{0,4},{4,0},{8,12},{12,8},{1,5},{5,1},{9,13},{13,9},{2,6},{6,2},{1... | collective-permute-start | bytes 221192 | tf_op jit(solution)/shard_map/gate_y/ppermute | solution.py:48
  123.6 10.8 %collective-permute-start.19 = (f32[8,2304]{1,0:T(8,128)}, f32[8,2304]{1,0:T(8,128)S(1)}, u32[]{:S(2)}, u32[]{:S(2)}) collective-permute-start(f32[8,2304]{1,0:T(8,128)} %gate_sum.8.first), channel_id=1, source_target_pairs={{0,8},{4,12},{8,0},{12,4},{1,9},{5,13},{9,1},{13,5},{2,10},{6,14},... | collective-permute-start | bytes 221192 | tf_op jit(solution)/shard_map/gate_y/ppermute | solution.py:48
  126.3 8.1 %collective-permute-start.20 = (f32[8,2304]{1,0:T(8,128)}, f32[8,2304]{1,0:T(8,128)S(1)}, u32[]{:S(2)}, u32[]{:S(2)}) collective-permute-start(f32[8,2304]{1,0:T(8,128)} %gate_sum.8.first), channel_id=1, source_target_pairs={{0,12},{4,8},{8,4},{12,0},{1,13},{5,9},{9,5},{13,1},{2,14},{6,10},... | collective-permute-start | bytes 221192 | tf_op jit(solution)/shard_map/gate_y/ppermute | solution.py:48
  136.7 11.8 %collective-permute-start.26 = (f32[8,2304]{1,0:T(8,128)}, f32[8,2304]{1,0:T(8,128)S(1)}, u32[]{:S(2)}, u32[]{:S(2)}) collective-permute-start(f32[8,2304]{1,0:T(8,128)} %gate_sum.9), channel_id=1, source_target_pairs={{0,1},{1,0},{2,3},{3,2},{4,5},{5,4},{6,7},{7,6},{8,9},{9,8},{10,11... | collective-permute-start | bytes 221192 | tf_op jit(solution)/shard_map/gate_core_back/ppermute | solution.py:48
  143.2 26.0 %collective-permute-start.29 = (bf16[3,256,256]{2,1,0:T(8,128)(2,1)}, bf16[3,256,256]{2,1,0:T(8,128)(2,1)S(1)}, u32[]{:S(2)}, u32[]{:S(2)}) collective-permute-start(bf16[3,256,256]{2,1,0:T(8,128)(2,1)} %get-tuple-element.37.refs_0_), channel_id=1, source_target_pairs={{0,2},{2,0},{1,3},{3,1},{4,6},{6,4},{5,7},{7,5},{8,10},{10,8},{9,1... | collective-permute-start | bytes 1179656 | tf_op jit(solution)/shard_map/out_z/ppermute | solution.py:48
  155.1 16.9 %collective-permute-start.30 = (bf16[256,256]{1,0:T(8,128)(2,1)}, bf16[256,256]{1,0:T(8,128)(2,1)S(1)}, u32[]{:S(2)}, u32[]{:S(2)}) collective-permute-start(bf16[256,256]{1,0:T(8,128)(2,1)} %far_products_last.1.tie), channel_id=1, source_target_pairs={{0,2},{2,0},{1,3},{3,1},{4,6},{6,4},{5,7},{7,5},{8,10},{10,8},{9,1... | collective-permute-start | bytes 393224 | tf_op jit(solution)/shard_map/out_z_last/ppermute | solution.py:48
  169.2 2.8 %copy-start.20 = (bf16[3,256,256]{2,1,0:T(8,128)(2,1)}, bf16[3,256,256]{2,1,0:T(8,128)(2,1)S(1)}, u32[]{:S(2)}) copy-start(bf16[3,256,256]{2,1,0:T(8,128)(2,1)S(1)} %collective-permute-done.29.got) | copy-start | bytes 1179652
  (22 other events, 19.3 us)

commit v4 on v3

--- a/solution.py
+++ b/solution.py
@@ -13,7 +13,8 @@
 SMEM = pl.BlockSpec(memory_space=pltpu.SMEM)
 ANY = pl.BlockSpec(memory_space=pl.ANY)
 HBM = pl.BlockSpec(memory_space=pltpu.HBM)
-LARGE = pltpu.CompilerParams(vmem_limit_bytes=48 * 1024 * 1024)
+SMALL = pltpu.CompilerParams(vmem_limit_bytes=8 * 1024 * 1024)
+MIDDLE = pltpu.CompilerParams(vmem_limit_bytes=24 * 1024 * 1024)
 
 
 def ring(value, axis):
@@ -24,6 +25,14 @@
     return lax.ppermute(value, (axis, "c"), pairs)
 
 
+def pairs(value, axis, first):
+    size = lax.axis_size(axis)
+    partner = lambda i, c: i ^ 1 if (c == 0) == first else size - 1 - i
+    return lax.ppermute(
+        value, (axis, "c"), [(2 * i + c, 2 * partner(i, c) + c) for i in range(size) for c in range(2)]
+    )
+
+
 def fence_kernel(*refs):
     del refs
 
@@ -31,10 +40,11 @@
 def fence(values, *ties):
     return pl.pallas_call(
         fence_kernel,
-        in_specs=[HBM] * len(values) + [ANY] * len(ties),
-        out_specs=[HBM] * len(values),
+        in_specs=[ANY] * (len(values) + len(ties)),
+        out_specs=[ANY] * len(values),
         out_shape=[shaped(v.shape, v.dtype) for v in values],
         input_output_aliases={i: i for i in range(len(values))},
+        compiler_params=SMALL,
         name="fence",
     )(*values, *ties)
 
@@ -79,7 +89,7 @@
 def split_kernel(at, weight, down, piece, sems):
     width = weight.shape[1]
     quarter = piece.shape[0]
-    rows = pl.ds(pl.multiple_of(at[0] * quarter, quarter), quarter)
+    rows = pl.ds(pl.multiple_of(at[4] * quarter, quarter), quarter)
     run(
         [
             pltpu.make_async_copy(weight.at[rows], piece.at[:, pl.ds(0, width)], sems.at[0]),
@@ -90,21 +100,30 @@
     )
 
 
-def token_kernel(at, hidden, grad, up, gate, mixed, gates, back, grad_in, up_in, sems):
+def join_kernel(at, mine, got, tie, out):
+    quarter = mine.shape[0]
+    side = lax.rem(at[4], 2)
+    for place, ref in ((side, mine), (1 - side, got)):
+        out[pl.ds(pl.multiple_of(place * quarter, quarter), quarter), :] = ref[...]
+
+
+def token_kernel(at, hidden, grad, up, gate, mixed, gates, back, hidden_in, grad_in, up_in, sems):
     stacked = up.shape[0]
     copies = [
-        pltpu.make_async_copy(grad, grad_in, sems.at[0]),
-        pltpu.make_async_copy(up, up_in, sems.at[1]),
+        pltpu.make_async_copy(hidden, hidden_in, sems.at[0]),
+        pltpu.make_async_copy(grad, grad_in, sems.at[1]),
+        pltpu.make_async_copy(up, up_in, sems.at[2]),
     ]
     for copy in copies:
         copy.start()
     ones = membership(gate.shape[0], stacked)
-    gates[...] = jax.nn.sigmoid(dot_t(gate[...], hidden[...]))
     wide = lax.dot_general(
         ones.astype(BF16), gate[...], (((0,), (0,)), ((), ())), preferred_element_type=F32
     ).astype(BF16)
-    factor = 2.0 * jax.nn.sigmoid(dot_t(hidden[...], wide))
-    for copy in copies:
+    copies[0].wait()
+    gates[...] = jax.nn.sigmoid(dot_t(gate[...], hidden_in[...]))
+    factor = 2.0 * jax.nn.sigmoid(dot_t(hidden_in[...], wide))
+    for copy in copies[1:]:
         copy.wait()
     pulled = dot_t(grad_in[...], up_in[...])
     back[...] = pulled
@@ -138,7 +157,7 @@
     rest[...] = keep[y] + got[y].astype(F32)
 
 
-def act_z_kernel(at, rest, first, second, third, mixed, keep, give, all_mixed):
+def act_z_kernel(at, rest, first, second, third, mixed, tie, keep, give, all_mixed):
     y, zh = at[1], at[2]
     for out, side in ((give, 1 - zh), (keep, zh)):
         total = (rest[side] + first[side].astype(F32)) + (
@@ -188,12 +207,12 @@
     out[...] = value.astype(out.dtype)
 
 
-def far_kernel(at, own, own_s, one, one_s, two, two_s, mixed, mixed_s, *refs):
-    pieces, (out, weight, down) = refs[:4], refs[4:]
+def far_kernel(at, own, own_s, one, one_s, two, two_s, mixed, mixed_s, mine, got, tie, out, weight, down):
     width = weight.shape[1]
-    rows = pieces[0].shape[0]
-    for steps, ref in enumerate(pieces):
-        place = pl.ds(pl.multiple_of(back_at(at[0], at[3], steps) * rows, rows), rows)
+    rows = mine.shape[0]
+    block = at[4] // 2
+    for number, ref in ((block, mine), (1 - block, got)):
+        place = pl.ds(pl.multiple_of(number * rows, rows), rows)
         weight[place, :] = ref[:, :width]
         down[place, :] = ref[:, width:]
     for steps, group in enumerate(((own, own_s), (one, one_s), (two, two_s))):
@@ -237,13 +256,14 @@
     features = weight.shape[0]
     depth = width + stacked
     quarter = features // 4
-    at = jnp.stack([lax.axis_index(a) for a in ("x", "y", "zh", "c")]).astype(jnp.int32)
-    c, zh = at[3], at[2]
+    x, y, zh, c = (lax.axis_index(a) for a in ("x", "y", "zh", "c"))
+    turned = jnp.where(x == 0, 0, jnp.where(x == 3, 1, x + 1))
+    at = jnp.stack([x, y, zh, c, jnp.where(c == 0, x, turned)]).astype(jnp.int32)
 
     piece = pl.pallas_call(
         split_kernel,
         in_specs=[SMEM, HBM, HBM],
-        out_specs=HBM,
+        out_specs=VMEM,
         out_shape=shaped((quarter, depth), BF16),
         scratch_shapes=[pltpu.SemaphoreType.DMA((2,))],
         name="split",
@@ -252,6 +272,8 @@
         far_piece = swap(piece, "zh", 1)
     with jax.named_scope("tokens_y"):
         one = ring(grad, "y")
+    with jax.named_scope("tokens_core"):
+        own_s = swap(grad, "c", 1)
 
     keep, give = pl.pallas_call(
         act_kernel,
@@ -266,7 +288,6 @@
             pltpu.VMEM((features, stacked), BF16),
             pltpu.SemaphoreType.DMA((3,)),
         ],
-        compiler_params=LARGE,
         cost_estimate=cost(2 * mixture.size * stacked, 4 * mixture.size),
         name="rank_products",
     )(at, mixture.reshape(8, 2, tokens, -1), down)
@@ -274,7 +295,7 @@
         got = swap(give, "c", 1)
     mixed, gates, back = pl.pallas_call(
         token_kernel,
-        in_specs=[SMEM, VMEM, HBM, HBM, VMEM],
+        in_specs=[SMEM, HBM, HBM, HBM, VMEM],
         out_specs=[VMEM, VMEM, VMEM],
         out_shape=[
             shaped((tokens, stacked), BF16),
@@ -283,10 +304,10 @@
         ],
         scratch_shapes=[
             pltpu.VMEM((tokens, width), BF16),
+            pltpu.VMEM((tokens, width), BF16),
             pltpu.VMEM((stacked, width), BF16),
-            pltpu.SemaphoreType.DMA((2,)),
-        ],
-        compiler_params=LARGE,
+            pltpu.SemaphoreType.DMA((3,)),
+        ],
         cost_estimate=cost(6 * tokens * width * stacked, 12 * tokens * width),
         name="token_values",
     )(at, hidden, grad, up, gate_matrix)
@@ -295,6 +316,7 @@
         in_specs=[SMEM, VMEM, VMEM, VMEM],
         out_specs=[VMEM] * 4,
         out_shape=[shaped((3, tokens, stacked), BF16)] * 3 + [shaped((2, tokens, stacked), F32)],
+        compiler_params=SMALL,
         name="rank_sum_core",
     )(at, keep, got, mixed)
     with jax.named_scope("act_y"):
@@ -303,32 +325,34 @@
         )
     keep, give, all_mixed = pl.pallas_call(
         act_z_kernel,
-        in_specs=[SMEM] + [VMEM] * 5,
+        in_specs=[SMEM] + [VMEM] * 5 + [ANY],
         out_specs=[VMEM] * 3,
         out_shape=[
             shaped((tokens, stacked), F32),
             shaped((tokens, stacked), BF16),
             shaped((4, tokens, stacked), BF16),
         ],
+        compiler_params=SMALL,
         name="rank_sum_y",
-    )(at, rest, first, second, third, mixed)
+    )(at, rest, first, second, third, mixed, own_s)
     one, far_piece = fence((one, far_piece), give)
     with jax.named_scope("tokens_y"):
         two = ring(one, "y")
-    with jax.named_scope("weight_x"):
-        w_one = ring(far_piece, "x")
     with jax.named_scope("act_z"):
         got = swap(give, "zh", 1)
     with jax.named_scope("mixed_core"):
         mixed_s = swap(all_mixed, "c", 1)
     with jax.named_scope("tokens_core"):
-        own_s, one_s = swap(grad, "c", 1), swap(one, "c", 1)
+        one_s = swap(one, "c", 1)
+    with jax.named_scope("weight_x"):
+        w_one = pairs(far_piece, "x", True)
 
     total, give = pl.pallas_call(
         gate_kernel,
         in_specs=[SMEM] + [VMEM] * 5,
         out_specs=[VMEM, VMEM],
         out_shape=[shaped((adapters, width // 2), F32)] * 2,
+        compiler_params=SMALL,
         name="gate_products",
     )(at, keep, got, back, gates, hidden)
 
@@ -338,7 +362,8 @@
             in_specs=[VMEM, VMEM] + [ANY] * len(ties),
             out_specs=VMEM,
             out_shape=shaped(left.shape, F32),
-            name="gate_sum",
+            compiler_params=SMALL,
+        name="gate_sum",
         )(left, right, *ties)
 
     def add4(*parts):
@@ -347,7 +372,8 @@
             in_specs=[VMEM] * 4 + [ANY] * (len(parts) - 4),
             out_specs=VMEM,
             out_shape=shaped(parts[0].shape, F32),
-            name="gate_sum",
+            compiler_params=SMALL,
+        name="gate_sum",
         )(*parts)
 
     def step(total, axis, *ties):
@@ -357,28 +383,35 @@
 
     with jax.named_scope("gate_core"):
         got = swap(give, "c", 1)
-    total = add(total, got)
-    (w_one,) = fence((w_one,), total)
+    total = add(total, got, one_s)
+    w_mine = pl.pallas_call(
+        join_kernel,
+        in_specs=[SMEM, VMEM, VMEM, ANY],
+        out_specs=VMEM,
+        out_shape=shaped((2 * quarter, depth), BF16),
+        compiler_params=SMALL,
+        name="join",
+    )(at, far_piece, w_one, total)
     with jax.named_scope("weight_x"):
-        w_two = ring(w_one, "x")
-    total = step(total, "zl", w_one)
+        w_got = pairs(w_mine, "x", False)
+    total = step(total, "zl", w_mine, mixed_s)
     (two,) = fence((two,), total)
     with jax.named_scope("tokens_y"):
         three = ring(two, "y")
     with jax.named_scope("gate_zh"):
         got = swap(total, "zh", 1)
+    with jax.named_scope("tokens_core"):
+        two_s = swap(two, "c", 1)
     total = add(total, got, two)
-    (w_two,) = fence((w_two,), total)
-    with jax.named_scope("weight_x"):
-        w_three = ring(w_two, "x")
+    near = (grad, own_s, one, one_s, two, two_s)
+    total = step(total, "x", two_s)
+    (three,) = fence((three,), total)
     with jax.named_scope("tokens_core"):
-        two_s, three_s = swap(two, "c", 1), swap(three, "c", 1)
-    near = (grad, own_s, one, one_s, two, two_s)
-    total = step(total, "x", w_two)
+        three_s = swap(three, "c", 1)
 
     far, far_weight, far_down = pl.pallas_call(
         far_kernel,
-        in_specs=[SMEM] + [VMEM] * 12,
+        in_specs=[SMEM] + [VMEM] * 10 + [ANY],
         out_specs=[VMEM] * 3,
         out_shape=[
             shaped((3, 2 * tokens, features), BF16),
@@ -386,8 +419,9 @@
             shaped((features, stacked), BF16),
         ],
         cost_estimate=cost(12 * tokens * depth * features, 18 * tokens * depth),
+        compiler_params=MIDDLE,
         name="far_products",
-    )(at, *near, all_mixed, mixed_s, far_piece, w_one, w_two, w_three)
+    )(at, *near, all_mixed, mixed_s, w_mine, w_got, total)
     with jax.named_scope("out_z"):
         far_got = swap(far, "zh", 1)
 
@@ -397,32 +431,37 @@
         out_specs=VMEM,
         out_shape=shaped((2 * tokens, features), BF16),
         cost_estimate=cost(4 * tokens * depth * features, 6 * tokens * depth),
+        compiler_params=MIDDLE,
         name="far_products_last",
     )(at, three, three_s, all_mixed, mixed_s, far_weight, far_down)
     with jax.named_scope("out_z_last"):
         last_got = swap(last, "zh", 1)
 
-    total = step(total, "y", far)
-    with jax.named_scope("gate_core_back"):
-        other = swap(total, "c", 1)
-    gate_grad = jnp.where(
-        c == 0, jnp.concatenate([total, other], axis=1), jnp.concatenate([other, total], axis=1)
-    )
-
+    (total,) = fence((total,), last)
+    total = step(total, "y")
     own_out = pl.pallas_call(
         own_kernel,
         in_specs=[SMEM] + [VMEM] * 12 + [ANY],
         out_specs=VMEM,
         out_shape=shaped((4, 2 * tokens, features), BF16),
         cost_estimate=cost(16 * tokens * depth * features, 24 * tokens * depth),
+        compiler_params=MIDDLE,
         name="own_products",
     )(at, *near, three, three_s, all_mixed, mixed_s, weight, down, last)
+    (total,) = fence((total,), far_got, own_out)
+    with jax.named_scope("gate_core_back"):
+        other = swap(total, "c", 1)
+    gate_grad = jnp.where(
+        c == 0, jnp.concatenate([total, other], axis=1), jnp.concatenate([other, total], axis=1)
+    )
+
     out = pl.pallas_call(
         place_kernel,
         in_specs=[SMEM, VMEM, VMEM, VMEM],
         out_specs=HBM,
         out_shape=shaped((4, 2, 2, tokens, features), BF16),
         scratch_shapes=[pltpu.SemaphoreType.DMA((16,))],
+        compiler_params=MIDDLE,
         name="place",
     )(at, own_out, far_got, last_got)
     return gate_grad, out.reshape(16 * tokens, features)

time: 176 us -> 124 us (0.70)
  Pallas kernels: 60.8 us -> 23 us
  starting transfers between devices: 62.3 us -> 48.7 us
  waiting for transfers between devices: 35.9 us -> 48 us
  local copies, waits for them, and re-layouts: 12.9 us -> 2.59 us
    pallas_call x8 -> x10, Pallas kernels: 32.2 us -> 11 us  [the longest x1 4.41 us: on_device(): pl.pallas_call(token_kernel, in_specs=[SMEM, HBM, HBM, HBM, VMEM], out_sp...]
    ppermute x25, waiting for transfers between devices: 35.3 us -> 48 us  [swap(): return lax.ppermute(value, axis, [(i, i ^ mask) for i in range(size)])]
    ppermute x25, starting transfers between devices: 51.2 us -> 39.8 us  [swap(): return lax.ppermute(value, axis, [(i, i ^ mask) for i in range(size)])]
    unnamed x78 -> x18, local copies, waits for them, and re-layouts: 12.9 us -> 1.92 us
    ppermute x6 -> x3, starting transfers between devices: 11.1 us -> 6.09 us  [ring(): return lax.ppermute(value, (axis, 'c'), pairs)]
    pallas_call x3, Pallas kernels: 4.9 us -> 0.07 us  [add4(): pl.pallas_call(add4_kernel, in_specs=[VMEM] * 4 + [ANY] * (len(parts) - 4...]
    pallas_call x1, Pallas kernels: 8.09 us -> 3.26 us  [on_device(): pl.pallas_call(own_kernel, in_specs=[SMEM] + [VMEM] * 12 + [ANY], out_spe...]
    pallas_call x2, Pallas kernels: 3.12 us -> 0.02 us  [add(): pl.pallas_call(add_kernel, in_specs=[VMEM, VMEM] + [ANY] * len(ties), out...]
  transfers between devices with their start and end apart: 31 -> 30, of which waited for: 15 -> 15; matrix products, arithmetic and copies ran while one was open for 1% -> 1% of each run, Pallas kernels for 33% -> 19%
where the time goes in v4:
time: 124 us
  starting transfers between devices  48.7 us (39%)
  waiting for transfers between devices  48 us (39%)
  Pallas kernels  23 us (19%)
  local copies, waits for them, and re-layouts  2.59 us (2%)
    ppermute x25, waiting for transfers between devices, swap(): return lax.ppermute(value, axis, [(i, i ^ mask) for i in range(size)])  48 us
    ppermute x25, starting transfers between devices, swap(): return lax.ppermute(value, axis, [(i, i ^ mask) for i in range(size)])  39.8 us
    ppermute x3, starting transfers between devices, ring(): return lax.ppermute(value, (axis, 'c'), pairs)  6.09 us
    pallas_call x1, Pallas kernels, on_device(): pl.pallas_call(token_kernel, in_specs=[SMEM, HBM, HBM, HBM, VMEM], out_sp...  4.41 us
    pallas_call x1, Pallas kernels, on_device(): pl.pallas_call(act_kernel, in_specs=[SMEM, HBM, HBM], out_specs=[VMEM, VM...  3.4 us
    pallas_call x1, Pallas kernels, on_device(): pl.pallas_call(own_kernel, in_specs=[SMEM] + [VMEM] * 12 + [ANY], out_spe...  3.26 us
    pallas_call x1, Pallas kernels, on_device(): pl.pallas_call(far_kernel, in_specs=[SMEM] + [VMEM] * 10 + [ANY], out_spe...  2.81 us
    ppermute x2, starting transfers between devices, pairs(): lax.ppermute(value, (axis, 'c'), [(2 * i + c, 2 * partner(i, c) + c) for...  2.74 us
  transfers between devices with their start and end apart: 30, of which 15 were waited for; matrix products, arithmetic and copies ran while one was open for 1% of the time, Pallas kernels for 19%

profile of v4, /device:TPU:33, one launch (start us, length us, event | category | flops | bytes accessed | tf_op | source)
XLA Modules:
  0.0 123.9 jit_solution(15058927963418965184)
XLA Ops:
  0.6 0.8 collective-permute-start.4
  1.4 2.7 %collective-permute-start.7 = (bf16[128,4608]{1,0:T(8,128)(2,1)}, bf16[128,4608]{1,0:T(8,128)(2,1)S(1)}, u32[]{:S(2)}, u32[]{:S(2)}) collective-permute-start(bf16[128,4608]{1,0:T(8,128)(2,1)} %own.3), channel_id=1, source_target_pairs={{0,4},{1,13},{4,8},{5,1},{8,12},{9,5},{12,0},{13,9},{2,6},{3,15},{... | collective-permute-start | bytes 3538952 | tf_op jit(solution)/shard_map/tokens_y/ppermute | solution.py:25
  4.1 0.7 stack.23.at
  4.8 2.6 %split.1 = bf16[64,4736]{1,0:T(8,128)(2,1)} custom-call(s32[5]{0:T(128)} %stack.23.at, bf16[256,4608]{1,0:T(8,128)(2,1)} %weight.3, bf16[256,128]{1,0:T(8,128)(2,1)} %down.5), custom_call_target="tpu_custom_call" | custom-call | tf_op jit(solution)/shard_map/split/pallas_call | solution.py:263
  7.4 6.1 %collective-permute-start.8 = (bf16[64,4736]{1,0:T(8,128)(2,1)}, bf16[64,4736]{1,0:T(8,128)(2,1)S(1)}, u32[]{:S(2)}, u32[]{:S(2)}) collective-permute-start(bf16[64,4736]{1,0:T(8,128)(2,1)} %split.1), channel_id=1, source_target_pairs={{0,2},{2,0},{1,3},{3,1},{4,6},{6,4},{5,7},{7,5},{8,10},{10,8},{9,1... | collective-permute-start | bytes 1818632 | tf_op jit(solution)/shard_map/weight_z/ppermute | solution.py:58
  13.5 3.4 %rank_products.1 = (f32[4,2,128,128]{3,2,1,0:T(8,128)}, bf16[4,2,128,128]{3,2,1,0:T(8,128)(2,1)}) custom-call(s32[5]{0:T(128)} %stack.23.at, bf16[8,2,128,256]{3,2,1,0:T(8,128)(2,1)} %bitcast.8, bf16[256,128]{1,0:T(8,128)(2,1)} %down.5), custom_call_target="tpu_custom_call" | custom-call | flops 134217728 | bytes 2097152 | tf_op jit(solution)/shard_map/rank_products/pallas_call | solution.py:278
  17.0 4.4 %token_values.1 = (bf16[128,128]{1,0:T(8,128)(2,1)}, f32[8,128]{1,0:T(8,128)}, f32[128,128]{1,0:T(8,128)}) custom-call(s32[5]{0:T(128)} %stack.23.at, bf16[128,4608]{1,0:T(8,128)(2,1)} %hidden.3, bf16[128,4608]{1,0:T(8,128)(2,1)} %own.3, bf16[128,4608]{1,0:T(8,128)(2,1)} %up.1, bf16[8,4608]{1,0:T(8,128)(2,1)} %gate.1), custom_call_target="tpu_custom_call" | custom-call | flops 452984832 | bytes 7077888 | tf_op jit(solution)/shard_map/token_values/pallas_call | solution.py:296
  21.5 0.7 copy-done.5
  22.2 1.0 rank_sum_core.1
  23.2 0.5 collective-permute-start.1
  23.8 1.4 %collective-permute-start.2 = (bf16[3,128,128]{2,1,0:T(8,128)(2,1)S(1)}, bf16[3,128,128]{2,1,0:T(8,128)(2,1)S(1)}, u32[]{:S(2)}, u32[]{:S(2)}) collective-permute-start(bf16[3,128,128]{2,1,0:T(8,128)(2,1)S(1)} %get-tuple-element.26), channel_id=1, source_target_pairs={{0,8},{4,12},{8,0},{12,4},{1,9},{5,13},{9,1},{13,5},{2,10},{6,14},... | collective-permute-start | bytes 294920 | tf_op jit(solution)/shard_map/act_y/ppermute | solution.py:58
  25.2 2.0 %collective-permute-done.1.first = bf16[3,128,128]{2,1,0:T(8,128)(2,1)S(1)} collective-permute-done((bf16[3,128,128]{2,1,0:T(8,128)(2,1)S(1)}, bf16[3,128,128]{2,1,0:T(8,128)(2,1)S(1)}, u32[]{:S(2)}, u32[]{:S(2)}) %collective-permute-start.1) | collective-permute-done | bytes 98336 | tf_op jit(solution)/shard_map/act_y/ppermute | solution.py:58
  27.2 0.8 collective-permute-start.3
  28.0 2.1 %collective-permute-done.2.second = bf16[3,128,128]{2,1,0:T(8,128)(2,1)S(1)} collective-permute-done((bf16[3,128,128]{2,1,0:T(8,128)(2,1)S(1)}, bf16[3,128,128]{2,1,0:T(8,128)(2,1)S(1)}, u32[]{:S(2)}, u32[]{:S(2)}) %collective-permute-start.2) | collective-permute-done | bytes 98336 | tf_op jit(solution)/shard_map/act_y/ppermute | solution.py:58
  30.1 2.1 %collective-permute-done.3.third = bf16[3,128,128]{2,1,0:T(8,128)(2,1)S(1)} collective-permute-done((bf16[3,128,128]{2,1,0:T(8,128)(2,1)S(1)}, bf16[3,128,128]{2,1,0:T(8,128)(2,1)S(1)}, u32[]{:S(2)}, u32[]{:S(2)}) %collective-permute-start.3) | collective-permute-done | bytes 98336 | tf_op jit(solution)/shard_map/act_y/ppermute | solution.py:58
  32.2 0.6 rank_sum_y.1
  32.8 7.0 %collective-permute-done.8.refs_1_ = bf16[64,4736]{1,0:T(8,128)(2,1)S(1)} collective-permute-done((bf16[64,4736]{1,0:T(8,128)(2,1)}, bf16[64,4736]{1,0:T(8,128)(2,1)S(1)}, u32[]{:S(2)}, u32[]{:S(2)}) %collective-permute-start.8) | collective-permute-done | bytes 606240 | tf_op jit(solution)/shard_map/weight_z/ppermute | solution.py:58
  39.9 2.0 %collective-permute-start.16 = (bf16[128,4608]{1,0:T(8,128)(2,1)S(1)}, bf16[128,4608]{1,0:T(8,128)(2,1)S(1)}, u32[]{:S(2)}, u32[]{:S(2)}) collective-permute-start(bf16[128,4608]{1,0:T(8,128)(2,1)S(1)} %get-tuple-element.34.one), channel_id=1, source_target_pairs={{0,4},{1,13},{4,8},{5,1},{8,12},{9,5},{12,0},{13,9},{2,6},{3,15},{... | collective-permute-start | bytes 3538952 | tf_op jit(solution)/shard_map/tokens_y/ppermute | solution.py:25
  41.9 2.5 %collective-permute-start.13 = (bf16[64,4736]{1,0:T(8,128)(2,1)S(1)}, bf16[64,4736]{1,0:T(8,128)(2,1)S(1)}, u32[]{:S(2)}, u32[]{:S(2)}) collective-permute-start(bf16[64,4736]{1,0:T(8,128)(2,1)S(1)} %get-tuple-element.35.mine), channel_id=1, source_target_pairs={{0,64},{1,193},{64,0},{65,129},{128,192},{129,65},{192,128},{193,1... | collective-permute-start | bytes 1818632 | tf_op jit(solution)/shard_map/weight_x/ppermute | solution.py:31
  44.4 5.3 %collective-permute-start.5 = (bf16[128,128]{1,0:T(8,128)(2,1)S(1)}, bf16[128,128]{1,0:T(8,128)(2,1)S(1)}, u32[]{:S(2)}, u32[]{:S(2)}) collective-permute-start(bf16[128,128]{1,0:T(8,128)(2,1)S(1)} %get-tuple-element.29.refs_2_), channel_id=1, source_target_pairs={{0,2},{2,0},{1,3},{3,1},{4,6},{6,4},{5,7},{7,5},{8,10},{10,8},{9,1... | collective-permute-start | bytes 98312 | tf_op jit(solution)/shard_map/act_z/ppermute | solution.py:58
  49.7 1.4 %collective-permute-done.5.got = bf16[128,128]{1,0:T(8,128)(2,1)S(1)} collective-permute-done((bf16[128,128]{1,0:T(8,128)(2,1)S(1)}, bf16[128,128]{1,0:T(8,128)(2,1)S(1)}, u32[]{:S(2)}, u32[]{:S(2)}) %collective-permute-start.5) | collective-permute-done | bytes 32800 | tf_op jit(solution)/shard_map/act_z/ppermute | solution.py:58
  51.1 1.2 gate_products.1
  52.9 0.8 collective-permute-done.6.right
  53.8 2.5 %collective-permute-start.11 = (f32[8,2304]{1,0:T(8,128)S(1)}, f32[8,2304]{1,0:T(8,128)S(1)}, u32[]{:S(2)}, u32[]{:S(2)}) collective-permute-start(f32[8,2304]{1,0:T(8,128)S(1)} %gate_sum.5.tie.first), channel_id=1, source_target_pairs={{0,32},{16,48},{32,0},{48,16},{1,33},{17,49},{33,1},{49,17},{2,34}... | collective-permute-start | bytes 221192 | tf_op jit(solution)/shard_map/gate_zl/ppermute | solution.py:58
  56.4 0.6 join.1.refs_0_.mine
  57.5 3.3 %collective-permute-done.11.third = f32[8,2304]{1,0:T(8,128)S(1)} collective-permute-done((f32[8,2304]{1,0:T(8,128)S(1)}, f32[8,2304]{1,0:T(8,128)S(1)}, u32[]{:S(2)}, u32[]{:S(2)}) %collective-permute-start.11) | collective-permute-done | bytes 73760 | tf_op jit(solution)/shard_map/gate_zl/ppermute | solution.py:58
  60.8 2.7 %collective-permute-done.12.fourth = f32[8,2304]{1,0:T(8,128)S(1)} collective-permute-done((f32[8,2304]{1,0:T(8,128)S(1)}, f32[8,2304]{1,0:T(8,128)S(1)}, u32[]{:S(2)}, u32[]{:S(2)}) %collective-permute-start.12) | collective-permute-done | bytes 73760 | tf_op jit(solution)/shard_map/gate_zl/ppermute | solution.py:58
  63.6 1.2 collective-permute-start.20
  64.8 1.3 %collective-permute-start.21 = (bf16[128,4608]{1,0:T(8,128)(2,1)S(1)}, bf16[128,4608]{1,0:T(8,128)(2,1)S(1)}, u32[]{:S(2)}, u32[]{:S(2)}) collective-permute-start(bf16[128,4608]{1,0:T(8,128)(2,1)S(1)} %fence.6.refs_0_.two), channel_id=1, source_target_pairs={{0,4},{1,13},{4,8},{5,1},{8,12},{9,5},{12,0},{13,9},{2,6},{3,15},{... | collective-permute-start | bytes 3538952 | tf_op jit(solution)/shard_map/tokens_y/ppermute | solution.py:25
  66.4 5.3 %collective-permute-start.15 = (f32[8,2304]{1,0:T(8,128)S(1)}, f32[8,2304]{1,0:T(8,128)S(1)}, u32[]{:S(2)}, u32[]{:S(2)}) collective-permute-start(f32[8,2304]{1,0:T(8,128)S(1)} %gate_sum.6.refs_1_.left), channel_id=1, source_target_pairs={{0,2},{2,0},{1,3},{3,1},{4,6},{6,4},{5,7},{7,5},{8,10},{10,8},{9,1... | collective-permute-start | bytes 221192 | tf_op jit(solution)/shard_map/gate_zh/ppermute | solution.py:58
  71.7 3.8 %collective-permute-done.15.right = f32[8,2304]{1,0:T(8,128)S(1)} collective-permute-done((f32[8,2304]{1,0:T(8,128)S(1)}, f32[8,2304]{1,0:T(8,128)S(1)}, u32[]{:S(2)}, u32[]{:S(2)}) %collective-permute-start.15) | collective-permute-done | bytes 73760 | tf_op jit(solution)/shard_map/gate_zh/ppermute | solution.py:58
  75.5 1.9 %collective-permute-start.17 = (f32[8,2304]{1,0:T(8,128)S(1)}, f32[8,2304]{1,0:T(8,128)S(1)}, u32[]{:S(2)}, u32[]{:S(2)}) collective-permute-start(f32[8,2304]{1,0:T(8,128)S(1)} %gate_sum.7.first), channel_id=1, source_target_pairs={{0,64},{64,0},{128,192},{192,128},{1,65},{65,1},{129,193},{193,129... | collective-permute-start | bytes 221192 | tf_op jit(solution)/shard_map/gate_x/ppermute | solution.py:58
  77.4 2.0 %collective-permute-start.18 = (f32[8,2304]{1,0:T(8,128)S(1)}, f32[8,2304]{1,0:T(8,128)S(1)}, u32[]{:S(2)}, u32[]{:S(2)}) collective-permute-start(f32[8,2304]{1,0:T(8,128)S(1)} %gate_sum.7.first), channel_id=1, source_target_pairs={{0,128},{64,192},{128,0},{192,64},{1,129},{65,193},{129,1},{193,65... | collective-permute-start | bytes 221192 | tf_op jit(solution)/shard_map/gate_x/ppermute | solution.py:58
  79.3 4.8 %collective-permute-done.17.second = f32[8,2304]{1,0:T(8,128)S(1)} collective-permute-done((f32[8,2304]{1,0:T(8,128)S(1)}, f32[8,2304]{1,0:T(8,128)S(1)}, u32[]{:S(2)}, u32[]{:S(2)}) %collective-permute-start.17) | collective-permute-done | bytes 73760 | tf_op jit(solution)/shard_map/gate_x/ppermute | solution.py:58
  84.2 1.5 %collective-permute-start.19 = (f32[8,2304]{1,0:T(8,128)S(1)}, f32[8,2304]{1,0:T(8,128)S(1)}, u32[]{:S(2)}, u32[]{:S(2)}) collective-permute-start(f32[8,2304]{1,0:T(8,128)S(1)} %gate_sum.7.first), channel_id=1, source_target_pairs={{0,192},{64,128},{128,64},{192,0},{1,193},{65,129},{129,65},{193,1... | collective-permute-start | bytes 221192 | tf_op jit(solution)/shard_map/gate_x/ppermute | solution.py:58
  85.7 0.5 collective-permute-done.18.third
  86.2 2.4 %collective-permute-done.19.fourth = f32[8,2304]{1,0:T(8,128)S(1)} collective-permute-done((f32[8,2304]{1,0:T(8,128)S(1)}, f32[8,2304]{1,0:T(8,128)S(1)}, u32[]{:S(2)}, u32[]{:S(2)}) %collective-permute-start.19) | collective-permute-done | bytes 73760 | tf_op jit(solution)/shard_map/gate_x/ppermute | solution.py:58
  88.8 1.1 copy-done
  89.9 2.8 %far_products.1 = (bf16[3,256,256]{2,1,0:T(8,128)(2,1)S(1)}, bf16[256,4608]{1,0:T(8,128)(2,1)S(1)}, bf16[256,128]{1,0:T(8,128)(2,1)S(1)}) custom-call(s32[5]{0:T(128)S(1)} %copy-done.6, bf16[128,4608]{1,0:T(8,128)(2,1)S(1)} %copy-done, bf16[128,4608]{1,0:T(8,128)(2,1)S(1)} %collective-permute-done.4.tie.own_s, bf16[128,4608]{1,0:T(8,128)(2,1)S(1)} %get-tuple-element.34.one, ...), custom_call_target="tpu_custom_call" | custom-call | flops 1862270976 | bytes 10911744 | tf_op jit(solution)/shard_map/far_products/pallas_call | solution.py:412
  92.7 5.4 %collective-permute-start.27 = (bf16[3,256,256]{2,1,0:T(8,128)(2,1)S(1)}, bf16[3,256,256]{2,1,0:T(8,128)(2,1)S(1)}, u32[]{:S(2)}, u32[]{:S(2)}) collective-permute-start(bf16[3,256,256]{2,1,0:T(8,128)(2,1)S(1)} %get-tuple-element.39), channel_id=1, source_target_pairs={{0,2},{2,0},{1,3},{3,1},{4,6},{6,4},{5,7},{7,5},{8,10},{10,8},{9,1... | collective-permute-start | bytes 1179656 | tf_op jit(solution)/shard_map/out_z/ppermute | solution.py:58
  98.1 1.4 %far_products_last.1.refs_1_.tie = bf16[256,256]{1,0:T(8,128)(2,1)S(1)} custom-call(s32[5]{0:T(128)S(1)} %copy-done.6, bf16[128,4608]{1,0:T(8,128)(2,1)S(1)} %fence.7.three, bf16[128,4608]{1,0:T(8,128)(2,1)S(1)} %collective-permute-done.22.three_s, bf16[4,128,128]{2,1,0:T(8,128)(2,1)S(1)} %get-tuple-element.36.mixed, ...), custom_call_target="tpu_custom_call" | custom-call | flops 620756992 | bytes 3637248 | tf_op jit(solution)/shard_map/far_products_last/pallas_call | solution.py:428
  99.8 1.2 collective-permute-start.25
  101.0 2.5 %collective-permute-start.26 = (f32[8,2304]{1,0:T(8,128)S(1)}, f32[8,2304]{1,0:T(8,128)S(1)}, u32[]{:S(2)}, u32[]{:S(2)}) collective-permute-start(f32[8,2304]{1,0:T(8,128)S(1)} %fence.8.first), channel_id=1, source_target_pairs={{0,12},{4,8},{8,4},{12,0},{1,13},{5,9},{9,5},{13,1},{2,14},{6,10},... | collective-permute-start | bytes 221192 | tf_op jit(solution)/shard_map/gate_y/ppermute | solution.py:58
  103.6 3.3 %own_products.1.refs_2_.own = bf16[4,256,256]{2,1,0:T(8,128)(2,1)S(1)} custom-call(s32[5]{0:T(128)S(1)} %copy-done.6, bf16[128,4608]{1,0:T(8,128)(2,1)S(1)} %copy-done, bf16[128,4608]{1,0:T(8,128)(2,1)S(1)} %collective-permute-done.4.tie.own_s, bf16[128,4608]{1,0:T(8,128)(2,1)S(1)} %get-tuple-element.34.one, ...), custom_call_target="tpu_custom_call" | custom-call | flops 2483027968 | bytes 14548992 | tf_op jit(solution)/shard_map/own_products/pallas_call | solution.py:442
  106.9 12.2 %collective-permute-done.27.refs_1_.got = bf16[3,256,256]{2,1,0:T(8,128)(2,1)S(1)} collective-permute-done((bf16[3,256,256]{2,1,0:T(8,128)(2,1)S(1)}, bf16[3,256,256]{2,1,0:T(8,128)(2,1)S(1)}, u32[]{:S(2)}, u32[]{:S(2)}) %collective-permute-start.27) | collective-permute-done | bytes 393248 | tf_op jit(solution)/shard_map/out_z/ppermute | solution.py:58
  119.2 2.4 %collective-permute-done.29.last = bf16[256,256]{1,0:T(8,128)(2,1)S(1)} collective-permute-done((bf16[256,256]{1,0:T(8,128)(2,1)S(1)}, bf16[256,256]{1,0:T(8,128)(2,1)S(1)}, u32[]{:S(2)}, u32[]{:S(2)}) %collective-permute-start.29) | collective-permute-done | bytes 131104 | tf_op jit(solution)/shard_map/out_z_last/ppermute | solution.py:58
  121.5 1.6 %place.1 = bf16[4,2,2,128,256]{4,3,2,1,0:T(8,128)(2,1)} custom-call(s32[5]{0:T(128)S(1)} %copy-done.6, bf16[4,256,256]{2,1,0:T(8,128)(2,1)S(1)} %own_products.1.refs_2_.own, bf16[3,256,256]{2,1,0:T(8,128)(2,1)S(1)} %collective-permute-done.27.refs_1_.got, bf16[256,256]{1,0:T(8,128)(2,1)S(1)} %collective-permute-done.29.last), custom_call_target="tpu_custom_call" | custom-call | tf_op jit(solution)/shard_map/place/pallas_call | solution.py:458
  123.2 0.7 maximum_select_fusion
  (53 shorter events, 2.2 us)
Async XLA Ops:
  0.6 31.6 %collective-permute-start.4 = (bf16[128,4608]{1,0:T(8,128)(2,1)}, bf16[128,4608]{1,0:T(8,128)(2,1)S(1)}, u32[]{:S(2)}, u32[]{:S(2)}) collective-permute-start(bf16[128,4608]{1,0:T(8,128)(2,1)} %own.3), channel_id=1, source_target_pairs={{0,1},{1,0},{2,3},{3,2},{4,5},{5,4},{6,7},{7,6},{8,9},{9,8},{10,11... | collective-permute-start | bytes 3538952 | tf_op jit(solution)/shard_map/tokens_core/ppermute | solution.py:58
  1.4 38.5 %collective-permute-start.7 = (bf16[128,4608]{1,0:T(8,128)(2,1)}, bf16[128,4608]{1,0:T(8,128)(2,1)S(1)}, u32[]{:S(2)}, u32[]{:S(2)}) collective-permute-start(bf16[128,4608]{1,0:T(8,128)(2,1)} %own.3), channel_id=1, source_target_pairs={{0,4},{1,13},{4,8},{5,1},{8,12},{9,5},{12,0},{13,9},{2,6},{3,15},{... | collective-permute-start | bytes 3538952 | tf_op jit(solution)/shard_map/tokens_y/ppermute | solution.py:25
  7.4 32.5 %collective-permute-start.8 = (bf16[64,4736]{1,0:T(8,128)(2,1)}, bf16[64,4736]{1,0:T(8,128)(2,1)S(1)}, u32[]{:S(2)}, u32[]{:S(2)}) collective-permute-start(bf16[64,4736]{1,0:T(8,128)(2,1)} %split.1), channel_id=1, source_target_pairs={{0,2},{2,0},{1,3},{3,1},{4,6},{6,4},{5,7},{7,5},{8,10},{10,8},{9,1... | collective-permute-start | bytes 1818632 | tf_op jit(solution)/shard_map/weight_z/ppermute | solution.py:58
  16.9 4.6 %copy-start.4 = (f32[4,2,128,128]{3,2,1,0:T(8,128)S(1)}, f32[4,2,128,128]{3,2,1,0:T(8,128)}, u32[]{:S(2)}) copy-start(f32[4,2,128,128]{3,2,1,0:T(8,128)} %get-tuple-element.21.keep) | copy-start | bytes 1572868
  16.9 4.6 %copy-start.6 = (s32[5]{0:T(128)S(1)}, s32[5]{0:T(128)}, u32[]{:S(2)}) copy-start(s32[5]{0:T(128)} %stack.23.at) | copy-start | bytes 64
  16.9 4.5 %collective-permute-start = (bf16[4,2,128,128]{3,2,1,0:T(8,128)(2,1)}, bf16[4,2,128,128]{3,2,1,0:T(8,128)(2,1)}, u32[]{:S(2)}, u32[]{:S(2)}) collective-permute-start(bf16[4,2,128,128]{3,2,1,0:T(8,128)(2,1)} %get-tuple-element.22), channel_id=1, source_target_pairs={{0,1},{1,0},{2,3},{3,2},{4,5},{5,4},{6,7},{7,6},{8,9},{9,8},{10,11... | collective-permute-start | bytes 786440 | tf_op jit(solution)/shard_map/act_core/ppermute | solution.py:58
  21.5 0.8 copy-start.5
  23.2 4.0 %collective-permute-start.1 = (bf16[3,128,128]{2,1,0:T(8,128)(2,1)S(1)}, bf16[3,128,128]{2,1,0:T(8,128)(2,1)S(1)}, u32[]{:S(2)}, u32[]{:S(2)}) collective-permute-start(bf16[3,128,128]{2,1,0:T(8,128)(2,1)S(1)} %get-tuple-element.25), channel_id=1, source_target_pairs={{0,4},{4,0},{8,12},{12,8},{1,5},{5,1},{9,13},{13,9},{2,6},{6,2},{1... | collective-permute-start | bytes 294920 | tf_op jit(solution)/shard_map/act_y/ppermute | solution.py:58
  23.8 6.3 %collective-permute-start.2 = (bf16[3,128,128]{2,1,0:T(8,128)(2,1)S(1)}, bf16[3,128,128]{2,1,0:T(8,128)(2,1)S(1)}, u32[]{:S(2)}, u32[]{:S(2)}) collective-permute-start(bf16[3,128,128]{2,1,0:T(8,128)(2,1)S(1)} %get-tuple-element.26), channel_id=1, source_target_pairs={{0,8},{4,12},{8,0},{12,4},{1,9},{5,13},{9,1},{13,5},{2,10},{6,14},... | collective-permute-start | bytes 294920 | tf_op jit(solution)/shard_map/act_y/ppermute | solution.py:58
  27.2 5.0 %collective-permute-start.3 = (bf16[3,128,128]{2,1,0:T(8,128)(2,1)S(1)}, bf16[3,128,128]{2,1,0:T(8,128)(2,1)S(1)}, u32[]{:S(2)}, u32[]{:S(2)}) collective-permute-start(bf16[3,128,128]{2,1,0:T(8,128)(2,1)S(1)} %get-tuple-element.27), channel_id=1, source_target_pairs={{0,12},{4,8},{8,4},{12,0},{1,13},{5,9},{9,5},{13,1},{2,14},{6,10},... | collective-permute-start | bytes 294920 | tf_op jit(solution)/shard_map/act_y/ppermute | solution.py:58
  32.8 18.3 %copy-start.2 = (bf16[128,4608]{1,0:T(8,128)(2,1)S(1)}, bf16[128,4608]{1,0:T(8,128)(2,1)}, u32[]{:S(2)}) copy-start(bf16[128,4608]{1,0:T(8,128)(2,1)} %hidden.3) | copy-start | bytes 3538948
  32.8 18.3 %copy-start.7 = (f32[128,128]{1,0:T(8,128)S(1)}, f32[128,128]{1,0:T(8,128)}, u32[]{:S(2)}) copy-start(f32[128,128]{1,0:T(8,128)} %get-tuple-element.30.back) | copy-start | bytes 196612
  32.8 18.3 %copy-start.8 = (f32[8,128]{1,0:T(8,128)S(1)}, f32[8,128]{1,0:T(8,128)}, u32[]{:S(2)}) copy-start(f32[8,128]{1,0:T(8,128)} %get-tuple-element.31.gates) | copy-start | bytes 12292
  39.9 13.8 %collective-permute-start.9 = (bf16[128,4608]{1,0:T(8,128)(2,1)S(1)}, bf16[128,4608]{1,0:T(8,128)(2,1)S(1)}, u32[]{:S(2)}, u32[]{:S(2)}) collective-permute-start(bf16[128,4608]{1,0:T(8,128)(2,1)S(1)} %get-tuple-element.34.one), channel_id=1, source_target_pairs={{0,1},{1,0},{2,3},{3,2},{4,5},{5,4},{6,7},{7,6},{8,9},{9,8},{10,11... | collective-permute-start | bytes 3538952 | tf_op jit(solution)/shard_map/tokens_core/ppermute | solution.py:58
  39.9 23.7 %collective-permute-start.16 = (bf16[128,4608]{1,0:T(8,128)(2,1)S(1)}, bf16[128,4608]{1,0:T(8,128)(2,1)S(1)}, u32[]{:S(2)}, u32[]{:S(2)}) collective-permute-start(bf16[128,4608]{1,0:T(8,128)(2,1)S(1)} %get-tuple-element.34.one), channel_id=1, source_target_pairs={{0,4},{1,13},{4,8},{5,1},{8,12},{9,5},{12,0},{13,9},{2,6},{3,15},{... | collective-permute-start | bytes 3538952 | tf_op jit(solution)/shard_map/tokens_y/ppermute | solution.py:25
  41.9 14.4 %collective-permute-start.13 = (bf16[64,4736]{1,0:T(8,128)(2,1)S(1)}, bf16[64,4736]{1,0:T(8,128)(2,1)S(1)}, u32[]{:S(2)}, u32[]{:S(2)}) collective-permute-start(bf16[64,4736]{1,0:T(8,128)(2,1)S(1)} %get-tuple-element.35.mine), channel_id=1, source_target_pairs={{0,64},{1,193},{64,0},{65,129},{128,192},{129,65},{192,128},{193,1... | collective-permute-start | bytes 1818632 | tf_op jit(solution)/shard_map/weight_x/ppermute | solution.py:31
  44.4 6.7 %collective-permute-start.5 = (bf16[128,128]{1,0:T(8,128)(2,1)S(1)}, bf16[128,128]{1,0:T(8,128)(2,1)S(1)}, u32[]{:S(2)}, u32[]{:S(2)}) collective-permute-start(bf16[128,128]{1,0:T(8,128)(2,1)S(1)} %get-tuple-element.29.refs_2_), channel_id=1, source_target_pairs={{0,2},{2,0},{1,3},{3,1},{4,6},{6,4},{5,7},{7,5},{8,10},{10,8},{9,1... | collective-permute-start | bytes 98312 | tf_op jit(solution)/shard_map/act_z/ppermute | solution.py:58
  52.3 1.4 %collective-permute-start.6 = (f32[8,2304]{1,0:T(8,128)S(1)}, f32[8,2304]{1,0:T(8,128)S(1)}, u32[]{:S(2)}, u32[]{:S(2)}) collective-permute-start(f32[8,2304]{1,0:T(8,128)S(1)} %get-tuple-element.33), channel_id=1, source_target_pairs={{0,1},{1,0},{2,3},{3,2},{4,5},{5,4},{6,7},{7,6},{8,9},{9,8},{10,11... | collective-permute-start | bytes 221192 | tf_op jit(solution)/shard_map/gate_core/ppermute | solution.py:58
  52.4 4.7 %collective-permute-start.14 = (bf16[4,128,128]{2,1,0:T(8,128)(2,1)S(1)}, bf16[4,128,128]{2,1,0:T(8,128)(2,1)S(1)}, u32[]{:S(2)}, u32[]{:S(2)}) collective-permute-start(bf16[4,128,128]{2,1,0:T(8,128)(2,1)S(1)} %get-tuple-element.36.mixed), channel_id=1, source_target_pairs={{0,1},{1,0},{2,3},{3,2},{4,5},{5,4},{6,7},{7,6},{8,9},{9,8},{10,11... | collective-permute-start | bytes 393224 | tf_op jit(solution)/shard_map/mixed_core/ppermute | solution.py:58
  53.7 3.8 %collective-permute-start.10 = (f32[8,2304]{1,0:T(8,128)S(1)}, f32[8,2304]{1,0:T(8,128)S(1)}, u32[]{:S(2)}, u32[]{:S(2)}) collective-permute-start(f32[8,2304]{1,0:T(8,128)S(1)} %gate_sum.5.tie.first), channel_id=1, source_target_pairs={{0,16},{16,0},{32,48},{48,32},{1,17},{17,1},{33,49},{49,33},{2,18}... | collective-permute-start | bytes 221192 | tf_op jit(solution)/shard_map/gate_zl/ppermute | solution.py:58
  53.8 7.0 %collective-permute-start.11 = (f32[8,2304]{1,0:T(8,128)S(1)}, f32[8,2304]{1,0:T(8,128)S(1)}, u32[]{:S(2)}, u32[]{:S(2)}) collective-permute-start(f32[8,2304]{1,0:T(8,128)S(1)} %gate_sum.5.tie.first), channel_id=1, source_target_pairs={{0,32},{16,48},{32,0},{48,16},{1,33},{17,49},{33,1},{49,17},{2,34}... | collective-permute-start | bytes 221192 | tf_op jit(solution)/shard_map/gate_zl/ppermute | solution.py:58
  56.3 7.2 %collective-permute-start.12 = (f32[8,2304]{1,0:T(8,128)S(1)}, f32[8,2304]{1,0:T(8,128)S(1)}, u32[]{:S(2)}, u32[]{:S(2)}) collective-permute-start(f32[8,2304]{1,0:T(8,128)S(1)} %gate_sum.5.tie.first), channel_id=1, source_target_pairs={{0,48},{16,32},{32,16},{48,0},{1,49},{17,33},{33,17},{49,1},{2,50}... | collective-permute-start | bytes 221192 | tf_op jit(solution)/shard_map/gate_zl/ppermute | solution.py:58
  63.6 25.0 %collective-permute-start.20 = (bf16[128,4608]{1,0:T(8,128)(2,1)S(1)}, bf16[128,4608]{1,0:T(8,128)(2,1)S(1)}, u32[]{:S(2)}, u32[]{:S(2)}) collective-permute-start(bf16[128,4608]{1,0:T(8,128)(2,1)S(1)} %fence.6.refs_0_.two), channel_id=1, source_target_pairs={{0,1},{1,0},{2,3},{3,2},{4,5},{5,4},{6,7},{7,6},{8,9},{9,8},{10,11... | collective-permute-start | bytes 3538952 | tf_op jit(solution)/shard_map/tokens_core/ppermute | solution.py:58
  64.8 23.8 %collective-permute-start.21 = (bf16[128,4608]{1,0:T(8,128)(2,1)S(1)}, bf16[128,4608]{1,0:T(8,128)(2,1)S(1)}, u32[]{:S(2)}, u32[]{:S(2)}) collective-permute-start(bf16[128,4608]{1,0:T(8,128)(2,1)S(1)} %fence.6.refs_0_.two), channel_id=1, source_target_pairs={{0,4},{1,13},{4,8},{5,1},{8,12},{9,5},{12,0},{13,9},{2,6},{3,15},{... | collective-permute-start | bytes 3538952 | tf_op jit(solution)/shard_map/tokens_y/ppermute | solution.py:25
  66.1 22.6 %collective-permute-start.23 = (bf16[128,4736]{1,0:T(8,128)(2,1)S(1)}, bf16[128,4736]{1,0:T(8,128)(2,1)S(1)}, u32[]{:S(2)}, u32[]{:S(2)}) collective-permute-start(bf16[128,4736]{1,0:T(8,128)(2,1)S(1)} %join.1.refs_0_.mine), channel_id=1, source_target_pairs={{0,192},{1,65},{64,128},{65,1},{128,64},{129,193},{192,0},{193,129... | collective-permute-start | bytes 3637256 | tf_op jit(solution)/shard_map/weight_x/ppermute | solution.py:31
  66.4 9.1 %collective-permute-start.15 = (f32[8,2304]{1,0:T(8,128)S(1)}, f32[8,2304]{1,0:T(8,128)S(1)}, u32[]{:S(2)}, u32[]{:S(2)}) collective-permute-start(f32[8,2304]{1,0:T(8,128)S(1)} %gate_sum.6.refs_1_.left), channel_id=1, source_target_pairs={{0,2},{2,0},{1,3},{3,1},{4,6},{6,4},{5,7},{7,5},{8,10},{10,8},{9,1... | collective-permute-start | bytes 221192 | tf_op jit(solution)/shard_map/gate_zh/ppermute | solution.py:58
  75.5 8.7 %collective-permute-start.17 = (f32[8,2304]{1,0:T(8,128)S(1)}, f32[8,2304]{1,0:T(8,128)S(1)}, u32[]{:S(2)}, u32[]{:S(2)}) collective-permute-start(f32[8,2304]{1,0:T(8,128)S(1)} %gate_sum.7.first), channel_id=1, source_target_pairs={{0,64},{64,0},{128,192},{192,128},{1,65},{65,1},{129,193},{193,129... | collective-permute-start | bytes 221192 | tf_op jit(solution)/shard_map/gate_x/ppermute | solution.py:58
  77.4 8.9 %collective-permute-start.18 = (f32[8,2304]{1,0:T(8,128)S(1)}, f32[8,2304]{1,0:T(8,128)S(1)}, u32[]{:S(2)}, u32[]{:S(2)}) collective-permute-start(f32[8,2304]{1,0:T(8,128)S(1)} %gate_sum.7.first), channel_id=1, source_target_pairs={{0,128},{64,192},{128,0},{192,64},{1,129},{65,193},{129,1},{193,65... | collective-permute-start | bytes 221192 | tf_op jit(solution)/shard_map/gate_x/ppermute | solution.py:58
  84.2 4.4 %collective-permute-start.19 = (f32[8,2304]{1,0:T(8,128)S(1)}, f32[8,2304]{1,0:T(8,128)S(1)}, u32[]{:S(2)}, u32[]{:S(2)}) collective-permute-start(f32[8,2304]{1,0:T(8,128)S(1)} %gate_sum.7.first), channel_id=1, source_target_pairs={{0,192},{64,128},{128,64},{192,0},{1,193},{65,129},{129,65},{193,1... | collective-permute-start | bytes 221192 | tf_op jit(solution)/shard_map/gate_x/ppermute | solution.py:58
  88.6 1.3 %copy-start = (bf16[128,4608]{1,0:T(8,128)(2,1)S(1)}, bf16[128,4608]{1,0:T(8,128)(2,1)}, u32[]{:S(2)}) copy-start(bf16[128,4608]{1,0:T(8,128)(2,1)} %own.3) | copy-start | bytes 3538948
  88.7 9.5 %collective-permute-start.22 = (bf16[128,4608]{1,0:T(8,128)(2,1)S(1)}, bf16[128,4608]{1,0:T(8,128)(2,1)S(1)}, u32[]{:S(2)}, u32[]{:S(2)}) collective-permute-start(bf16[128,4608]{1,0:T(8,128)(2,1)S(1)} %fence.7.three), channel_id=1, source_target_pairs={{0,1},{1,0},{2,3},{3,2},{4,5},{5,4},{6,7},{7,6},{8,9},{9,8},{10,11... | collective-permute-start | bytes 3538952 | tf_op jit(solution)/shard_map/tokens_core/ppermute | solution.py:58
  92.7 26.4 %collective-permute-start.27 = (bf16[3,256,256]{2,1,0:T(8,128)(2,1)S(1)}, bf16[3,256,256]{2,1,0:T(8,128)(2,1)S(1)}, u32[]{:S(2)}, u32[]{:S(2)}) collective-permute-start(bf16[3,256,256]{2,1,0:T(8,128)(2,1)S(1)} %get-tuple-element.39), channel_id=1, source_target_pairs={{0,2},{2,0},{1,3},{3,1},{4,6},{6,4},{5,7},{7,5},{8,10},{10,8},{9,1... | collective-permute-start | bytes 1179656 | tf_op jit(solution)/shard_map/out_z/ppermute | solution.py:58
  98.1 5.4 %copy-start.1 = (bf16[256,4608]{1,0:T(8,128)(2,1)S(1)}, bf16[256,4608]{1,0:T(8,128)(2,1)}, u32[]{:S(2)}) copy-start(bf16[256,4608]{1,0:T(8,128)(2,1)} %weight.3) | copy-start | bytes 7077892
  98.1 5.4 %copy-start.3 = (bf16[256,128]{1,0:T(8,128)(2,1)S(1)}, bf16[256,128]{1,0:T(8,128)(2,1)}, u32[]{:S(2)}) copy-start(bf16[256,128]{1,0:T(8,128)(2,1)} %down.5) | copy-start | bytes 196612
  99.5 22.0 %collective-permute-start.29 = (bf16[256,256]{1,0:T(8,128)(2,1)S(1)}, bf16[256,256]{1,0:T(8,128)(2,1)S(1)}, u32[]{:S(2)}, u32[]{:S(2)}) collective-permute-start(bf16[256,256]{1,0:T(8,128)(2,1)S(1)} %far_products_last.1.refs_1_.tie), channel_id=1, source_target_pairs={{0,2},{2,0},{1,3},{3,1},{4,6},{6,4},{5,7},{7,5},{8,10},{10,8},{9,1... | collective-permute-start | bytes 393224 | tf_op jit(solution)/shard_map/out_z_last/ppermute | solution.py:58
  99.6 7.2 %collective-permute-start.24 = (f32[8,2304]{1,0:T(8,128)S(1)}, f32[8,2304]{1,0:T(8,128)S(1)}, u32[]{:S(2)}, u32[]{:S(2)}) collective-permute-start(f32[8,2304]{1,0:T(8,128)S(1)} %fence.8.first), channel_id=1, source_target_pairs={{0,4},{4,0},{8,12},{12,8},{1,5},{5,1},{9,13},{13,9},{2,6},{6,2},{1... | collective-permute-start | bytes 221192 | tf_op jit(solution)/shard_map/gate_y/ppermute | solution.py:58
  99.8 7.1 %collective-permute-start.25 = (f32[8,2304]{1,0:T(8,128)S(1)}, f32[8,2304]{1,0:T(8,128)S(1)}, u32[]{:S(2)}, u32[]{:S(2)}) collective-permute-start(f32[8,2304]{1,0:T(8,128)S(1)} %fence.8.first), channel_id=1, source_target_pairs={{0,8},{4,12},{8,0},{12,4},{1,9},{5,13},{9,1},{13,5},{2,10},{6,14},... | collective-permute-start | bytes 221192 | tf_op jit(solution)/shard_map/gate_y/ppermute | solution.py:58
  101.0 5.8 %collective-permute-start.26 = (f32[8,2304]{1,0:T(8,128)S(1)}, f32[8,2304]{1,0:T(8,128)S(1)}, u32[]{:S(2)}, u32[]{:S(2)}) collective-permute-start(f32[8,2304]{1,0:T(8,128)S(1)} %fence.8.first), channel_id=1, source_target_pairs={{0,12},{4,8},{8,4},{12,0},{1,13},{5,9},{9,5},{13,1},{2,14},{6,10},... | collective-permute-start | bytes 221192 | tf_op jit(solution)/shard_map/gate_y/ppermute | solution.py:58
  119.1 4.1 %collective-permute-start.28 = (f32[8,2304]{1,0:T(8,128)S(1)}, f32[8,2304]{1,0:T(8,128)S(1)}, u32[]{:S(2)}, u32[]{:S(2)}) collective-permute-start(f32[8,2304]{1,0:T(8,128)S(1)} %fence.9), channel_id=1, source_target_pairs={{0,1},{1,0},{2,3},{3,2},{4,5},{5,4},{6,7},{7,6},{8,9},{9,8},{10,11... | collective-permute-start | bytes 221192 | tf_op jit(solution)/shard_map/gate_core_back/ppermute | solution.py:58

commit v5 on v4

--- a/solution.py
+++ b/solution.py
@@ -79,27 +79,6 @@
     return jnp.where((column >= low) & (column < low + stacked // adapters), 1.0, 0.0)
 
 
-def run(copies):
-    for copy in copies:
-        copy.start()
-    for copy in copies:
-        copy.wait()
-
-
-def split_kernel(at, weight, down, piece, sems):
-    width = weight.shape[1]
-    quarter = piece.shape[0]
-    rows = pl.ds(pl.multiple_of(at[4] * quarter, quarter), quarter)
-    run(
-        [
-            pltpu.make_async_copy(weight.at[rows], piece.at[:, pl.ds(0, width)], sems.at[0]),
-            pltpu.make_async_copy(
-                down.at[rows], piece.at[:, pl.ds(width, down.shape[1])], sems.at[1]
-            ),
-        ]
-    )
-
-
 def join_kernel(at, mine, got, tie, out):
     quarter = mine.shape[0]
     side = lax.rem(at[4], 2)
@@ -107,44 +86,25 @@
         out[pl.ds(pl.multiple_of(place * quarter, quarter), quarter), :] = ref[...]
 
 
-def token_kernel(at, hidden, grad, up, gate, mixed, gates, back, hidden_in, grad_in, up_in, sems):
+def token_kernel(at, hidden, grad, up, gate, mixed, gates, back):
     stacked = up.shape[0]
-    copies = [
-        pltpu.make_async_copy(hidden, hidden_in, sems.at[0]),
-        pltpu.make_async_copy(grad, grad_in, sems.at[1]),
-        pltpu.make_async_copy(up, up_in, sems.at[2]),
-    ]
-    for copy in copies:
-        copy.start()
     ones = membership(gate.shape[0], stacked)
     wide = lax.dot_general(
         ones.astype(BF16), gate[...], (((0,), (0,)), ((), ())), preferred_element_type=F32
     ).astype(BF16)
-    copies[0].wait()
-    gates[...] = jax.nn.sigmoid(dot_t(gate[...], hidden_in[...]))
-    factor = 2.0 * jax.nn.sigmoid(dot_t(hidden_in[...], wide))
-    for copy in copies[1:]:
-        copy.wait()
-    pulled = dot_t(grad_in[...], up_in[...])
+    gates[...] = jax.nn.sigmoid(dot_t(gate[...], hidden[...]))
+    factor = 2.0 * jax.nn.sigmoid(dot_t(hidden[...], wide))
+    pulled = dot_t(grad[...], up[...])
     back[...] = pulled
     mixed[...] = (factor * pulled).astype(BF16)
 
 
-def act_kernel(at, mixture, down, keep, give, rows_in, down_in, sems):
+def act_kernel(at, mixture, down, keep, give):
     c = at[3]
     blocks, _, tokens, depth = mixture.shape
-    copies = [
-        pltpu.make_async_copy(down, down_in, sems.at[0]),
-        pltpu.make_async_copy(mixture.at[:, 1 - c], rows_in.at[0], sems.at[1]),
-        pltpu.make_async_copy(mixture.at[:, c], rows_in.at[1], sems.at[2]),
-    ]
-    for copy in copies:
-        copy.start()
-    copies[0].wait()
-    for out, side in ((give, 0), (keep, 1)):
-        copies[1 + side].wait()
-        rows = rows_in[side].reshape(blocks * tokens, depth)
-        value = jnp.dot(rows, down_in[...], preferred_element_type=F32)
+    for out, side in ((give, 1 - c), (keep, c)):
+        rows = mixture[:, side].reshape(blocks * tokens, depth)
+        value = jnp.dot(rows, down[...], preferred_element_type=F32)
         out[...] = value.reshape(out.shape).astype(out.dtype)
 
 
@@ -157,13 +117,15 @@
     rest[...] = keep[y] + got[y].astype(F32)
 
 
-def act_z_kernel(at, rest, first, second, third, mixed, tie, keep, give, all_mixed):
+def act_z_kernel(at, rest, first, second, third, mixed, down, tie, keep, give, all_mixed):
     y, zh = at[1], at[2]
+    tokens = keep.shape[0]
     for out, side in ((give, 1 - zh), (keep, zh)):
         total = (rest[side] + first[side].astype(F32)) + (
             second[side].astype(F32) + third[side].astype(F32)
         )
-        out[...] = total.astype(out.dtype)
+        out[pl.ds(0, tokens), :] = total.astype(out.dtype)
+    give[pl.ds(tokens, down.shape[0]), :] = down[...]
     all_mixed[y] = mixed[...]
     for ref, mask in ((first, 1), (second, 2), (third, 3)):
         all_mixed[jnp.bitwise_xor(y, mask)] = ref[2]
@@ -173,7 +135,7 @@
     stacked = keep.shape[1]
     adapters = gates.shape[0]
     half = result.shape[1]
-    product = (keep[...] + got[...].astype(F32)) * back[...]
+    product = (keep[...] + got[pl.ds(0, keep.shape[0]), :].astype(F32)) * back[...]
     ones = membership(adapters, stacked)
     delta = 2.0 * dot_t(ones, product, lax.Precision.HIGHEST)
     dlogit = delta * gates[...] * (1.0 - gates[...])
@@ -207,19 +169,18 @@
     out[...] = value.astype(out.dtype)
 
 
-def far_kernel(at, own, own_s, one, one_s, two, two_s, mixed, mixed_s, mine, got, tie, out, weight, down):
-    width = weight.shape[1]
+def far_kernel(at, own, own_s, one, one_s, two, two_s, mixed, mixed_s, mine, got, downs, out, weight):
     rows = mine.shape[0]
     block = at[4] // 2
     for number, ref in ((block, mine), (1 - block, got)):
-        place = pl.ds(pl.multiple_of(number * rows, rows), rows)
-        weight[place, :] = ref[:, :width]
-        down[place, :] = ref[:, width:]
+        weight[pl.ds(pl.multiple_of(number * rows, rows), rows), :] = ref[...]
+    down = downs.at[pl.ds(own.shape[0], weight.shape[0])]
     for steps, group in enumerate(((own, own_s), (one, one_s), (two, two_s))):
         rows_product(at, steps, group, (mixed, mixed_s), weight, down, out.at[steps])
 
 
-def far_last_kernel(at, three, three_s, mixed, mixed_s, weight, down, out):
+def far_last_kernel(at, three, three_s, mixed, mixed_s, weight, downs, out):
+    down = downs.at[pl.ds(three.shape[0], weight.shape[0])]
     rows_product(at, 3, (three, three_s), (mixed, mixed_s), weight, down, out)
 
 
@@ -246,7 +207,10 @@
                         sems.at[len(copies)],
                     )
                 )
-    run(copies)
+    for copy in copies:
+        copy.start()
+    for copy in copies:
+        copy.wait()
 
 
 def on_device(hidden, grad, mixture, weight, down, up, gate_matrix):
@@ -258,17 +222,11 @@
     quarter = features // 4
     x, y, zh, c = (lax.axis_index(a) for a in ("x", "y", "zh", "c"))
     turned = jnp.where(x == 0, 0, jnp.where(x == 3, 1, x + 1))
-    at = jnp.stack([x, y, zh, c, jnp.where(c == 0, x, turned)]).astype(jnp.int32)
-
-    piece = pl.pallas_call(
-        split_kernel,
-        in_specs=[SMEM, HBM, HBM],
-        out_specs=VMEM,
-        out_shape=shaped((quarter, depth), BF16),
-        scratch_shapes=[pltpu.SemaphoreType.DMA((2,))],
-        name="split",
-    )(at, weight, down)
+    number = jnp.where(c == 0, x, turned)
+    at = jnp.stack([x, y, zh, c, number]).astype(jnp.int32)
+
     with jax.named_scope("weight_z"):
+        piece = lax.dynamic_slice_in_dim(weight, number * quarter, quarter, 0)
         far_piece = swap(piece, "zh", 1)
     with jax.named_scope("tokens_y"):
         one = ring(grad, "y")
@@ -277,17 +235,13 @@
 
     keep, give = pl.pallas_call(
         act_kernel,
-        in_specs=[SMEM, HBM, HBM],
+        in_specs=[SMEM, VMEM, VMEM],
         out_specs=[VMEM, VMEM],
         out_shape=[
             shaped((4, 2, tokens, stacked), F32),
             shaped((4, 2, tokens, stacked), BF16),
         ],
-        scratch_shapes=[
-            pltpu.VMEM((2, 8, tokens, features), BF16),
-            pltpu.VMEM((features, stacked), BF16),
-            pltpu.SemaphoreType.DMA((3,)),
-        ],
+        compiler_params=SMALL,
         cost_estimate=cost(2 * mixture.size * stacked, 4 * mixture.size),
         name="rank_products",
     )(at, mixture.reshape(8, 2, tokens, -1), down)
@@ -295,19 +249,14 @@
         got = swap(give, "c", 1)
     mixed, gates, back = pl.pallas_call(
         token_kernel,
-        in_specs=[SMEM, HBM, HBM, HBM, VMEM],
+        in_specs=[SMEM] + [VMEM] * 4,
         out_specs=[VMEM, VMEM, VMEM],
         out_shape=[
             shaped((tokens, stacked), BF16),
             shaped((adapters, tokens), F32),
             shaped((tokens, stacked), F32),
         ],
-        scratch_shapes=[
-            pltpu.VMEM((tokens, width), BF16),
-            pltpu.VMEM((tokens, width), BF16),
-            pltpu.VMEM((stacked, width), BF16),
-            pltpu.SemaphoreType.DMA((3,)),
-        ],
+        compiler_params=SMALL,
         cost_estimate=cost(6 * tokens * width * stacked, 12 * tokens * width),
         name="token_values",
     )(at, hidden, grad, up, gate_matrix)
@@ -325,21 +274,21 @@
         )
     keep, give, all_mixed = pl.pallas_call(
         act_z_kernel,
-        in_specs=[SMEM] + [VMEM] * 5 + [ANY],
+        in_specs=[SMEM] + [VMEM] * 6 + [ANY],
         out_specs=[VMEM] * 3,
         out_shape=[
             shaped((tokens, stacked), F32),
-            shaped((tokens, stacked), BF16),
+            shaped((tokens + features, stacked), BF16),
             shaped((4, tokens, stacked), BF16),
         ],
         compiler_params=SMALL,
         name="rank_sum_y",
-    )(at, rest, first, second, third, mixed, own_s)
+    )(at, rest, first, second, third, mixed, down, own_s)
     one, far_piece = fence((one, far_piece), give)
     with jax.named_scope("tokens_y"):
         two = ring(one, "y")
     with jax.named_scope("act_z"):
-        got = swap(give, "zh", 1)
+        message = swap(give, "zh", 1)
     with jax.named_scope("mixed_core"):
         mixed_s = swap(all_mixed, "c", 1)
     with jax.named_scope("tokens_core"):
@@ -354,7 +303,7 @@
         out_shape=[shaped((adapters, width // 2), F32)] * 2,
         compiler_params=SMALL,
         name="gate_products",
-    )(at, keep, got, back, gates, hidden)
+    )(at, keep, message, back, gates, hidden)
 
     def add(left, right, *ties):
         return pl.pallas_call(
@@ -383,12 +332,12 @@
 
     with jax.named_scope("gate_core"):
         got = swap(give, "c", 1)
-    total = add(total, got, one_s)
+    total = add(total, got, one_s, w_one)
     w_mine = pl.pallas_call(
         join_kernel,
         in_specs=[SMEM, VMEM, VMEM, ANY],
         out_specs=VMEM,
-        out_shape=shaped((2 * quarter, depth), BF16),
+        out_shape=shaped((2 * quarter, width), BF16),
         compiler_params=SMALL,
         name="join",
     )(at, far_piece, w_one, total)
@@ -402,26 +351,24 @@
         got = swap(total, "zh", 1)
     with jax.named_scope("tokens_core"):
         two_s = swap(two, "c", 1)
-    total = add(total, got, two)
+    total = add(total, got, two_s, w_got)
     near = (grad, own_s, one, one_s, two, two_s)
-    total = step(total, "x", two_s)
-    (three,) = fence((three,), total)
-    with jax.named_scope("tokens_core"):
-        three_s = swap(three, "c", 1)
-
-    far, far_weight, far_down = pl.pallas_call(
+    far, far_weight = pl.pallas_call(
         far_kernel,
-        in_specs=[SMEM] + [VMEM] * 10 + [ANY],
-        out_specs=[VMEM] * 3,
+        in_specs=[SMEM] + [VMEM] * 11,
+        out_specs=[VMEM] * 2,
         out_shape=[
             shaped((3, 2 * tokens, features), BF16),
             shaped((features, width), BF16),
-            shaped((features, stacked), BF16),
         ],
+        compiler_params=MIDDLE,
         cost_estimate=cost(12 * tokens * depth * features, 18 * tokens * depth),
-        compiler_params=MIDDLE,
         name="far_products",
-    )(at, *near, all_mixed, mixed_s, w_mine, w_got, total)
+    )(at, *near, all_mixed, mixed_s, w_mine, w_got, message)
+    (three,) = fence((three,), far)
+    with jax.named_scope("tokens_core"):
+        three_s = swap(three, "c", 1)
+    total = step(total, "x", far)
     with jax.named_scope("out_z"):
         far_got = swap(far, "zh", 1)
 
@@ -433,7 +380,7 @@
         cost_estimate=cost(4 * tokens * depth * features, 6 * tokens * depth),
         compiler_params=MIDDLE,
         name="far_products_last",
-    )(at, three, three_s, all_mixed, mixed_s, far_weight, far_down)
+    )(at, three, three_s, all_mixed, mixed_s, far_weight, message)
     with jax.named_scope("out_z_last"):
         last_got = swap(last, "zh", 1)
 

time: 124 us -> 122 us (0.984)
  the two profiles are of different devices: /device:TPU:33 before, /device:TPU:1 now
where the time goes in v5:
time: 122 us; the launch traced here: 121 us
  starting transfers between devices  57.9 us (47%)
  waiting for transfers between devices  38 us (31%)
  Pallas kernels  15.7 us (13%)
  local copies, waits for them, and re-layouts  7.5 us (6%)
    ppermute x25, starting transfers between devices, swap(): return lax.ppermute(value, axis, [(i, i ^ mask) for i in range(size)])  49.9 us
    ppermute x25, waiting for transfers between devices, swap(): return lax.ppermute(value, axis, [(i, i ^ mask) for i in range(size)])  27.7 us
    ppermute x2, waiting for transfers between devices, pairs(): lax.ppermute(value, (axis, 'c'), [(2 * i + c, 2 * partner(i, c) + c) for...  6.54 us
    unnamed x18, local copies, waits for them, and re-layouts  5.5 us
    ppermute x3, starting transfers between devices, ring(): return lax.ppermute(value, (axis, 'c'), pairs)  5.14 us
    ppermute x3, waiting for transfers between devices, ring(): return lax.ppermute(value, (axis, 'c'), pairs)  3.8 us
    pallas_call x1, Pallas kernels, on_device(): pl.pallas_call(own_kernel, in_specs=[SMEM] + [VMEM] * 12 + [ANY], out_spe...  3.3 us
    pallas_call x1, Pallas kernels, on_device(): pl.pallas_call(far_kernel, in_specs=[SMEM] + [VMEM] * 11, out_specs=[VMEM...  2.81 us
  transfers between devices with their start and end apart: 30, of which 13 were waited for; matrix products, arithmetic and copies ran while one was open for 2% of the time, Pallas kernels for 13%

profile of v5, /device:TPU:1, one launch (start us, length us, event | category | flops | bytes accessed | tf_op | source)
XLA Modules:
  0.0 120.7 jit_solution(15316053310374003936)
XLA Ops:
  0.6 3.3 %collective-permute-start.4 = (bf16[128,4608]{1,0:T(8,128)(2,1)}, bf16[128,4608]{1,0:T(8,128)(2,1)S(1)}, u32[]{:S(2)}, u32[]{:S(2)}) collective-permute-start(bf16[128,4608]{1,0:T(8,128)(2,1)} %own.3), channel_id=1, source_target_pairs={{0,1},{1,0},{2,3},{3,2},{4,5},{5,4},{6,7},{7,6},{8,9},{9,8},{10,11... | collective-permute-start | bytes 3538952 | tf_op jit(solution)/shard_map/tokens_core/ppermute | solution.py:58
  4.0 1.0 collective-permute-start.7
  5.0 1.9 %constant_dynamic-slice_fusion = bf16[64,4608]{1,0:T(8,128)(2,1)} fusion(bf16[256,4608]{1,0:T(8,128)(2,1)} %weight.1, s32[]{:T(128)S(6)} %select_n.26), kind=kLoop, calls=%fused_computation.1 | loop fusion | bytes 1179652 | tf_op jit(solution)/shard_map/weight_z/dynamic_slice | solution.py:229
  6.9 6.9 %collective-permute-start.8 = (bf16[64,4608]{1,0:T(8,128)(2,1)}, bf16[64,4608]{1,0:T(8,128)(2,1)}, u32[]{:S(2)}, u32[]{:S(2)}) collective-permute-start(bf16[64,4608]{1,0:T(8,128)(2,1)} %constant_dynamic-slice_fusion), channel_id=1, source_target_pairs={{0,2},{2,0},{1,3},{3,1},{4,6},{6,4},{5,7},{7,5},{8,10},{10,8},{9,1... | collective-permute-start | bytes 1769480 | tf_op jit(solution)/shard_map/weight_z/ppermute | solution.py:58
  13.9 1.2 %copy-done.5 = bf16[2048,256]{1,0:T(8,128)(2,1)S(1)} copy-done((bf16[2048,256]{1,0:T(8,128)(2,1)S(1)}, bf16[2048,256]{1,0:T(8,128)(2,1)}, u32[]{:S(2)}) %copy-start.5) | copy-done | bytes 1048600
  15.1 0.8 copy-done.6
  15.9 1.0 rank_products.1
  17.0 1.3 %copy-done.1 = bf16[128,4608]{1,0:T(8,128)(2,1)S(1)} copy-done((bf16[128,4608]{1,0:T(8,128)(2,1)S(1)}, bf16[128,4608]{1,0:T(8,128)(2,1)}, u32[]{:S(2)}) %copy-start.1) | copy-done | bytes 1179672
  18.3 1.3 %copy-done.4 = bf16[128,4608]{1,0:T(8,128)(2,1)S(1)} copy-done((bf16[128,4608]{1,0:T(8,128)(2,1)S(1)}, bf16[128,4608]{1,0:T(8,128)(2,1)}, u32[]{:S(2)}) %copy-start.4) | copy-done | bytes 1179672
  19.6 0.9 copy-done.8
  20.4 2.0 %token_values.1 = (bf16[128,128]{1,0:T(8,128)(2,1)S(1)}, f32[8,128]{1,0:T(8,128)S(1)}, f32[128,128]{1,0:T(8,128)S(1)}) custom-call(s32[5]{0:T(128)S(1)} %stack.23.at, bf16[128,4608]{1,0:T(8,128)(2,1)S(1)} %copy-done.1, bf16[128,4608]{1,0:T(8,128)(2,1)S(1)} %copy-done, bf16[128,4608]{1,0:T(8,128)(2,1)S(1)} %copy-done.4, bf16[8,4608]{1,0:T(8,128)(2,1)S(1)} %copy-done.8), custom_call_target="tpu_custom_call" | custom-call | flops 452984832 | bytes 7077888 | tf_op jit(solution)/shard_map/token_values/pallas_call | solution.py:250
  22.5 0.6 rank_sum_core.1
  23.6 1.4 %collective-permute-start.2 = (bf16[3,128,128]{2,1,0:T(8,128)(2,1)S(1)}, bf16[3,128,128]{2,1,0:T(8,128)(2,1)S(1)}, u32[]{:S(2)}, u32[]{:S(2)}) collective-permute-start(bf16[3,128,128]{2,1,0:T(8,128)(2,1)S(1)} %get-tuple-element.25), channel_id=1, source_target_pairs={{0,8},{4,12},{8,0},{12,4},{1,9},{5,13},{9,1},{13,5},{2,10},{6,14},... | collective-permute-start | bytes 294920 | tf_op jit(solution)/shard_map/act_y/ppermute | solution.py:58
  25.1 2.1 %collective-permute-done.1.first = bf16[3,128,128]{2,1,0:T(8,128)(2,1)S(1)} collective-permute-done((bf16[3,128,128]{2,1,0:T(8,128)(2,1)S(1)}, bf16[3,128,128]{2,1,0:T(8,128)(2,1)S(1)}, u32[]{:S(2)}, u32[]{:S(2)}) %collective-permute-start.1) | collective-permute-done | bytes 98336 | tf_op jit(solution)/shard_map/act_y/ppermute | solution.py:58
  27.1 0.8 collective-permute-start.3
  28.0 2.0 %collective-permute-done.2.second = bf16[3,128,128]{2,1,0:T(8,128)(2,1)S(1)} collective-permute-done((bf16[3,128,128]{2,1,0:T(8,128)(2,1)S(1)}, bf16[3,128,128]{2,1,0:T(8,128)(2,1)S(1)}, u32[]{:S(2)}, u32[]{:S(2)}) %collective-permute-start.2) | collective-permute-done | bytes 98336 | tf_op jit(solution)/shard_map/act_y/ppermute | solution.py:58
  29.9 1.9 %collective-permute-done.3.third = bf16[3,128,128]{2,1,0:T(8,128)(2,1)S(1)} collective-permute-done((bf16[3,128,128]{2,1,0:T(8,128)(2,1)S(1)}, bf16[3,128,128]{2,1,0:T(8,128)(2,1)S(1)}, u32[]{:S(2)}, u32[]{:S(2)}) %collective-permute-start.3) | collective-permute-done | bytes 98336 | tf_op jit(solution)/shard_map/act_y/ppermute | solution.py:58
  31.8 0.6 rank_sum_y.1
  32.4 6.5 %collective-permute-done.8.refs_1_ = bf16[64,4608]{1,0:T(8,128)(2,1)} collective-permute-done((bf16[64,4608]{1,0:T(8,128)(2,1)}, bf16[64,4608]{1,0:T(8,128)(2,1)}, u32[]{:S(2)}, u32[]{:S(2)}) %collective-permute-start.8) | collective-permute-done | bytes 589856 | tf_op jit(solution)/shard_map/weight_z/ppermute | solution.py:58
  39.0 1.2 collective-permute-start.16
  40.1 2.5 %collective-permute-start.10 = (bf16[64,4608]{1,0:T(8,128)(2,1)}, bf16[64,4608]{1,0:T(8,128)(2,1)S(1)}, u32[]{:S(2)}, u32[]{:S(2)}) collective-permute-start(bf16[64,4608]{1,0:T(8,128)(2,1)} %get-tuple-element.34.mine), channel_id=1, source_target_pairs={{0,64},{1,193},{64,0},{65,129},{128,192},{129,65},{192,128},{193,1... | collective-permute-start | bytes 1769480 | tf_op jit(solution)/shard_map/weight_x/ppermute | solution.py:31
  42.6 6.1 %collective-permute-start.5 = (bf16[384,128]{1,0:T(8,128)(2,1)S(1)}, bf16[384,128]{1,0:T(8,128)(2,1)S(1)}, u32[]{:S(2)}, u32[]{:S(2)}) collective-permute-start(bf16[384,128]{1,0:T(8,128)(2,1)S(1)} %get-tuple-element.28.refs_2_), channel_id=1, source_target_pairs={{0,2},{2,0},{1,3},{3,1},{4,6},{6,4},{5,7},{7,5},{8,10},{10,8},{9,1... | collective-permute-start | bytes 294920 | tf_op jit(solution)/shard_map/act_z/ppermute | solution.py:58
  48.8 3.2 %collective-permute-done.5.got.downs = bf16[384,128]{1,0:T(8,128)(2,1)S(1)} collective-permute-done((bf16[384,128]{1,0:T(8,128)(2,1)S(1)}, bf16[384,128]{1,0:T(8,128)(2,1)S(1)}, u32[]{:S(2)}, u32[]{:S(2)}) %collective-permute-start.5) | collective-permute-done | bytes 98336 | tf_op jit(solution)/shard_map/act_z/ppermute | solution.py:58
  51.9 1.2 %gate_products.1 = (f32[8,2304]{1,0:T(8,128)S(1)}, f32[8,2304]{1,0:T(8,128)S(1)}) custom-call(s32[5]{0:T(128)S(1)} %stack.23.at, f32[128,128]{1,0:T(8,128)S(1)} %get-tuple-element.27.keep, bf16[384,128]{1,0:T(8,128)(2,1)S(1)} %collective-permute-done.5.got.downs, f32[128,128]{1,0:T(8,128)S(1)} %get-tuple-element.29.back, ...), custom_call_target="tpu_custom_call" | custom-call | tf_op jit(solution)/shard_map/gate_products/pallas_call | solution.py:299
  53.8 0.8 collective-permute-done.6.right
  54.6 1.2 %collective-permute-start.11 = (f32[8,2304]{1,0:T(8,128)S(1)}, f32[8,2304]{1,0:T(8,128)S(1)}, u32[]{:S(2)}, u32[]{:S(2)}) collective-permute-start(f32[8,2304]{1,0:T(8,128)S(1)} %gate_sum.5.tie.first), channel_id=1, source_target_pairs={{0,16},{16,0},{32,48},{48,32},{1,17},{17,1},{33,49},{49,33},{2,18}... | collective-permute-start | bytes 221192 | tf_op jit(solution)/shard_map/gate_zl/ppermute | solution.py:58
  55.8 1.4 %collective-permute-start.12 = (f32[8,2304]{1,0:T(8,128)S(1)}, f32[8,2304]{1,0:T(8,128)S(1)}, u32[]{:S(2)}, u32[]{:S(2)}) collective-permute-start(f32[8,2304]{1,0:T(8,128)S(1)} %gate_sum.5.tie.first), channel_id=1, source_target_pairs={{0,32},{16,48},{32,0},{48,16},{1,33},{17,49},{33,1},{49,17},{2,34}... | collective-permute-start | bytes 221192 | tf_op jit(solution)/shard_map/gate_zl/ppermute | solution.py:58
  57.2 1.1 collective-permute-start.13
  58.3 1.2 join.1.refs_0_.mine
  59.9 3.8 %collective-permute-done.13.fourth = f32[8,2304]{1,0:T(8,128)S(1)} collective-permute-done((f32[8,2304]{1,0:T(8,128)S(1)}, f32[8,2304]{1,0:T(8,128)S(1)}, u32[]{:S(2)}, u32[]{:S(2)}) %collective-permute-start.13) | collective-permute-done | bytes 73760 | tf_op jit(solution)/shard_map/gate_zl/ppermute | solution.py:58
  63.8 1.6 %collective-permute-start.17 = (bf16[128,4608]{1,0:T(8,128)(2,1)S(1)}, bf16[128,4608]{1,0:T(8,128)(2,1)S(1)}, u32[]{:S(2)}, u32[]{:S(2)}) collective-permute-start(bf16[128,4608]{1,0:T(8,128)(2,1)S(1)} %fence.6.two), channel_id=1, source_target_pairs={{0,1},{1,0},{2,3},{3,2},{4,5},{5,4},{6,7},{7,6},{8,9},{9,8},{10,11... | collective-permute-start | bytes 3538952 | tf_op jit(solution)/shard_map/tokens_core/ppermute | solution.py:58
  65.4 3.0 %collective-permute-start.22 = (bf16[128,4608]{1,0:T(8,128)(2,1)S(1)}, bf16[128,4608]{1,0:T(8,128)(2,1)S(1)}, u32[]{:S(2)}, u32[]{:S(2)}) collective-permute-start(bf16[128,4608]{1,0:T(8,128)(2,1)S(1)} %fence.6.two), channel_id=1, source_target_pairs={{0,4},{1,13},{4,8},{5,1},{8,12},{9,5},{12,0},{13,9},{2,6},{3,15},{... | collective-permute-start | bytes 3538952 | tf_op jit(solution)/shard_map/tokens_y/ppermute | solution.py:25
  68.3 6.5 %collective-permute-done.18.refs_1_.got = bf16[128,4608]{1,0:T(8,128)(2,1)S(1)} collective-permute-done((bf16[128,4608]{1,0:T(8,128)(2,1)S(1)}, bf16[128,4608]{1,0:T(8,128)(2,1)S(1)}, u32[]{:S(2)}, u32[]{:S(2)}) %collective-permute-start.18) | collective-permute-done | bytes 1179680 | tf_op jit(solution)/shard_map/weight_x/ppermute | solution.py:31
  74.9 2.8 %far_products.1 = (bf16[3,256,256]{2,1,0:T(8,128)(2,1)S(1)}, bf16[256,4608]{1,0:T(8,128)(2,1)S(1)}) custom-call(s32[5]{0:T(128)S(1)} %stack.23.at, bf16[128,4608]{1,0:T(8,128)(2,1)S(1)} %copy-done, bf16[128,4608]{1,0:T(8,128)(2,1)S(1)} %collective-permute-done.4.tie.own_s, bf16[128,4608]{1,0:T(8,128)(2,1)S(1)} %get-tuple-element.33.one, ...), custom_call_target="tpu_custom_call" | custom-call | flops 1862270976 | bytes 10911744 | tf_op jit(solution)/shard_map/far_products/pallas_call | solution.py:356
  77.7 3.8 %collective-permute-done.22.refs_0_ = bf16[128,4608]{1,0:T(8,128)(2,1)S(1)} collective-permute-done((bf16[128,4608]{1,0:T(8,128)(2,1)S(1)}, bf16[128,4608]{1,0:T(8,128)(2,1)S(1)}, u32[]{:S(2)}, u32[]{:S(2)}) %collective-permute-start.22) | collective-permute-done | bytes 1179680 | tf_op jit(solution)/shard_map/tokens_y/ppermute | solution.py:25
  81.5 1.4 %collective-permute-start.23 = (bf16[128,4608]{1,0:T(8,128)(2,1)S(1)}, bf16[128,4608]{1,0:T(8,128)(2,1)S(1)}, u32[]{:S(2)}, u32[]{:S(2)}) collective-permute-start(bf16[128,4608]{1,0:T(8,128)(2,1)S(1)} %fence.7.three), channel_id=1, source_target_pairs={{0,1},{1,0},{2,3},{3,2},{4,5},{5,4},{6,7},{7,6},{8,9},{9,8},{10,11... | collective-permute-start | bytes 3538952 | tf_op jit(solution)/shard_map/tokens_core/ppermute | solution.py:58
  82.9 5.4 %collective-permute-start.15 = (f32[8,2304]{1,0:T(8,128)S(1)}, f32[8,2304]{1,0:T(8,128)S(1)}, u32[]{:S(2)}, u32[]{:S(2)}) collective-permute-start(f32[8,2304]{1,0:T(8,128)S(1)} %gate_sum.6.refs_1_.left), channel_id=1, source_target_pairs={{0,2},{2,0},{1,3},{3,1},{4,6},{6,4},{5,7},{7,5},{8,10},{10,8},{9,1... | collective-permute-start | bytes 221192 | tf_op jit(solution)/shard_map/gate_zh/ppermute | solution.py:58
  88.3 2.4 %collective-permute-done.15.right = f32[8,2304]{1,0:T(8,128)S(1)} collective-permute-done((f32[8,2304]{1,0:T(8,128)S(1)}, f32[8,2304]{1,0:T(8,128)S(1)}, u32[]{:S(2)}, u32[]{:S(2)}) %collective-permute-start.15) | collective-permute-done | bytes 73760 | tf_op jit(solution)/shard_map/gate_zh/ppermute | solution.py:58
  91.2 3.1 %collective-permute-start.20 = (f32[8,2304]{1,0:T(8,128)S(1)}, f32[8,2304]{1,0:T(8,128)S(1)}, u32[]{:S(2)}, u32[]{:S(2)}) collective-permute-start(f32[8,2304]{1,0:T(8,128)S(1)} %gate_sum.7.first), channel_id=1, source_target_pairs={{0,128},{64,192},{128,0},{192,64},{1,129},{65,193},{129,1},{193,65... | collective-permute-start | bytes 221192 | tf_op jit(solution)/shard_map/gate_x/ppermute | solution.py:58
  94.7 2.7 %collective-permute-done.20.third = f32[8,2304]{1,0:T(8,128)S(1)} collective-permute-done((f32[8,2304]{1,0:T(8,128)S(1)}, f32[8,2304]{1,0:T(8,128)S(1)}, u32[]{:S(2)}, u32[]{:S(2)}) %collective-permute-start.20) | collective-permute-done | bytes 73760 | tf_op jit(solution)/shard_map/gate_x/ppermute | solution.py:58
  97.4 2.2 %collective-permute-done.21.fourth = f32[8,2304]{1,0:T(8,128)S(1)} collective-permute-done((f32[8,2304]{1,0:T(8,128)S(1)}, f32[8,2304]{1,0:T(8,128)S(1)}, u32[]{:S(2)}, u32[]{:S(2)}) %collective-permute-start.21) | collective-permute-done | bytes 73760 | tf_op jit(solution)/shard_map/gate_x/ppermute | solution.py:58
  99.6 1.4 %far_products_last.1.refs_1_.tie = bf16[256,256]{1,0:T(8,128)(2,1)S(1)} custom-call(s32[5]{0:T(128)S(1)} %stack.23.at, bf16[128,4608]{1,0:T(8,128)(2,1)S(1)} %fence.7.three, bf16[128,4608]{1,0:T(8,128)(2,1)S(1)} %collective-permute-done.23.three_s, bf16[4,128,128]{2,1,0:T(8,128)(2,1)S(1)} %get-tuple-element.35.mixed, ...), custom_call_target="tpu_custom_call" | custom-call | flops 620756992 | bytes 3637248 | tf_op jit(solution)/shard_map/far_products_last/pallas_call | solution.py:375
  101.3 3.7 %collective-permute-start.26 = (f32[8,2304]{1,0:T(8,128)S(1)}, f32[8,2304]{1,0:T(8,128)S(1)}, u32[]{:S(2)}, u32[]{:S(2)}) collective-permute-start(f32[8,2304]{1,0:T(8,128)S(1)} %fence.8.first), channel_id=1, source_target_pairs={{0,12},{4,8},{8,4},{12,0},{1,13},{5,9},{9,5},{13,1},{2,14},{6,10},... | collective-permute-start | bytes 221192 | tf_op jit(solution)/shard_map/gate_y/ppermute | solution.py:58
  105.0 4.7 %collective-permute-start.29 = (bf16[256,256]{1,0:T(8,128)(2,1)S(1)}, bf16[256,256]{1,0:T(8,128)(2,1)S(1)}, u32[]{:S(2)}, u32[]{:S(2)}) collective-permute-start(bf16[256,256]{1,0:T(8,128)(2,1)S(1)} %far_products_last.1.refs_1_.tie), channel_id=1, source_target_pairs={{0,2},{2,0},{1,3},{3,1},{4,6},{6,4},{5,7},{7,5},{8,10},{10,8},{9,1... | collective-permute-start | bytes 393224 | tf_op jit(solution)/shard_map/out_z_last/ppermute | solution.py:58
  109.7 3.3 %own_products.1.refs_2_.own = bf16[4,256,256]{2,1,0:T(8,128)(2,1)S(1)} custom-call(s32[5]{0:T(128)S(1)} %stack.23.at, bf16[128,4608]{1,0:T(8,128)(2,1)S(1)} %copy-done, bf16[128,4608]{1,0:T(8,128)(2,1)S(1)} %collective-permute-done.4.tie.own_s, bf16[128,4608]{1,0:T(8,128)(2,1)S(1)} %get-tuple-element.33.one, ...), custom_call_target="tpu_custom_call" | custom-call | flops 2483027968 | bytes 14548992 | tf_op jit(solution)/shard_map/own_products/pallas_call | solution.py:389
  113.0 5.3 %collective-permute-start.28 = (f32[8,2304]{1,0:T(8,128)S(1)}, f32[8,2304]{1,0:T(8,128)S(1)}, u32[]{:S(2)}, u32[]{:S(2)}) collective-permute-start(f32[8,2304]{1,0:T(8,128)S(1)} %fence.9), channel_id=1, source_target_pairs={{0,1},{1,0},{2,3},{3,2},{4,5},{5,4},{6,7},{7,6},{8,9},{9,8},{10,11... | collective-permute-start | bytes 221192 | tf_op jit(solution)/shard_map/gate_core_back/ppermute | solution.py:58
  118.4 1.6 %place.1 = bf16[4,2,2,128,256]{4,3,2,1,0:T(8,128)(2,1)} custom-call(s32[5]{0:T(128)S(1)} %stack.23.at, bf16[4,256,256]{2,1,0:T(8,128)(2,1)S(1)} %own_products.1.refs_2_.own, bf16[3,256,256]{2,1,0:T(8,128)(2,1)S(1)} %collective-permute-done.27.refs_1_.got, bf16[256,256]{1,0:T(8,128)(2,1)S(1)} %collective-permute-done.29.last), custom_call_target="tpu_custom_call" | custom-call | tf_op jit(solution)/shard_map/place/pallas_call | solution.py:405
  120.0 0.7 maximum_select_fusion
  (53 shorter events, 3.1 us)
Async XLA Ops:
  0.6 16.4 %copy-start = (bf16[128,4608]{1,0:T(8,128)(2,1)S(1)}, bf16[128,4608]{1,0:T(8,128)(2,1)}, u32[]{:S(2)}) copy-start(bf16[128,4608]{1,0:T(8,128)(2,1)} %own.3) | copy-start | bytes 3538948
  0.6 31.2 %collective-permute-start.4 = (bf16[128,4608]{1,0:T(8,128)(2,1)}, bf16[128,4608]{1,0:T(8,128)(2,1)S(1)}, u32[]{:S(2)}, u32[]{:S(2)}) collective-permute-start(bf16[128,4608]{1,0:T(8,128)(2,1)} %own.3), channel_id=1, source_target_pairs={{0,1},{1,0},{2,3},{3,2},{4,5},{5,4},{6,7},{7,6},{8,9},{9,8},{10,11... | collective-permute-start | bytes 3538952 | tf_op jit(solution)/shard_map/tokens_core/ppermute | solution.py:58
  4.0 35.0 %collective-permute-start.7 = (bf16[128,4608]{1,0:T(8,128)(2,1)}, bf16[128,4608]{1,0:T(8,128)(2,1)S(1)}, u32[]{:S(2)}, u32[]{:S(2)}) collective-permute-start(bf16[128,4608]{1,0:T(8,128)(2,1)} %own.3), channel_id=1, source_target_pairs={{0,4},{1,13},{4,8},{5,1},{8,12},{9,5},{12,0},{13,9},{2,6},{3,15},{... | collective-permute-start | bytes 3538952 | tf_op jit(solution)/shard_map/tokens_y/ppermute | solution.py:25
  6.9 32.1 %collective-permute-start.8 = (bf16[64,4608]{1,0:T(8,128)(2,1)}, bf16[64,4608]{1,0:T(8,128)(2,1)}, u32[]{:S(2)}, u32[]{:S(2)}) collective-permute-start(bf16[64,4608]{1,0:T(8,128)(2,1)} %constant_dynamic-slice_fusion), channel_id=1, source_target_pairs={{0,2},{2,0},{1,3},{3,1},{4,6},{6,4},{5,7},{7,5},{8,10},{10,8},{9,1... | collective-permute-start | bytes 1769480 | tf_op jit(solution)/shard_map/weight_z/ppermute | solution.py:58
  13.9 1.2 %copy-start.5 = (bf16[2048,256]{1,0:T(8,128)(2,1)S(1)}, bf16[2048,256]{1,0:T(8,128)(2,1)}, u32[]{:S(2)}) copy-start(bf16[2048,256]{1,0:T(8,128)(2,1)} %param.9) | copy-start | bytes 3145732
  15.1 0.8 copy-start.6
  16.9 5.5 %collective-permute-start = (bf16[4,2,128,128]{3,2,1,0:T(8,128)(2,1)S(1)}, bf16[4,2,128,128]{3,2,1,0:T(8,128)(2,1)S(1)}, u32[]{:S(2)}, u32[]{:S(2)}) collective-permute-start(bf16[4,2,128,128]{3,2,1,0:T(8,128)(2,1)S(1)} %get-tuple-element.21), channel_id=1, source_target_pairs={{0,1},{1,0},{2,3},{3,2},{4,5},{5,4},{6,7},{7,6},{8,9},{9,8},{10,11... | collective-permute-start | bytes 786440 | tf_op jit(solution)/shard_map/act_core/ppermute | solution.py:58
  17.0 1.3 %copy-start.1 = (bf16[128,4608]{1,0:T(8,128)(2,1)S(1)}, bf16[128,4608]{1,0:T(8,128)(2,1)}, u32[]{:S(2)}) copy-start(bf16[128,4608]{1,0:T(8,128)(2,1)} %hidden.3) | copy-start | bytes 3538948
  18.3 1.3 %copy-start.4 = (bf16[128,4608]{1,0:T(8,128)(2,1)S(1)}, bf16[128,4608]{1,0:T(8,128)(2,1)}, u32[]{:S(2)}) copy-start(bf16[128,4608]{1,0:T(8,128)(2,1)} %up.1) | copy-start | bytes 3538948
  19.6 0.9 copy-start.8
  20.4 11.4 %copy-start.7 = (bf16[256,128]{1,0:T(8,128)(2,1)S(1)}, bf16[256,128]{1,0:T(8,128)(2,1)}, u32[]{:S(2)}) copy-start(bf16[256,128]{1,0:T(8,128)(2,1)} %down.5) | copy-start | bytes 196612
  23.1 4.1 %collective-permute-start.1 = (bf16[3,128,128]{2,1,0:T(8,128)(2,1)S(1)}, bf16[3,128,128]{2,1,0:T(8,128)(2,1)S(1)}, u32[]{:S(2)}, u32[]{:S(2)}) collective-permute-start(bf16[3,128,128]{2,1,0:T(8,128)(2,1)S(1)} %get-tuple-element.24), channel_id=1, source_target_pairs={{0,4},{4,0},{8,12},{12,8},{1,5},{5,1},{9,13},{13,9},{2,6},{6,2},{1... | collective-permute-start | bytes 294920 | tf_op jit(solution)/shard_map/act_y/ppermute | solution.py:58
  23.6 6.3 %collective-permute-start.2 = (bf16[3,128,128]{2,1,0:T(8,128)(2,1)S(1)}, bf16[3,128,128]{2,1,0:T(8,128)(2,1)S(1)}, u32[]{:S(2)}, u32[]{:S(2)}) collective-permute-start(bf16[3,128,128]{2,1,0:T(8,128)(2,1)S(1)} %get-tuple-element.25), channel_id=1, source_target_pairs={{0,8},{4,12},{8,0},{12,4},{1,9},{5,13},{9,1},{13,5},{2,10},{6,14},... | collective-permute-start | bytes 294920 | tf_op jit(solution)/shard_map/act_y/ppermute | solution.py:58
  27.1 4.7 %collective-permute-start.3 = (bf16[3,128,128]{2,1,0:T(8,128)(2,1)S(1)}, bf16[3,128,128]{2,1,0:T(8,128)(2,1)S(1)}, u32[]{:S(2)}, u32[]{:S(2)}) collective-permute-start(bf16[3,128,128]{2,1,0:T(8,128)(2,1)S(1)} %get-tuple-element.26), channel_id=1, source_target_pairs={{0,12},{4,8},{8,4},{12,0},{1,13},{5,9},{9,5},{13,1},{2,14},{6,10},... | collective-permute-start | bytes 294920 | tf_op jit(solution)/shard_map/act_y/ppermute | solution.py:58
  32.4 19.5 %copy-start.2 = (bf16[128,4608]{1,0:T(8,128)(2,1)S(1)}, bf16[128,4608]{1,0:T(8,128)(2,1)}, u32[]{:S(2)}) copy-start(bf16[128,4608]{1,0:T(8,128)(2,1)} %hidden.3) | copy-start | bytes 3538948
  39.0 15.6 %collective-permute-start.9 = (bf16[128,4608]{1,0:T(8,128)(2,1)S(1)}, bf16[128,4608]{1,0:T(8,128)(2,1)S(1)}, u32[]{:S(2)}, u32[]{:S(2)}) collective-permute-start(bf16[128,4608]{1,0:T(8,128)(2,1)S(1)} %get-tuple-element.33.one), channel_id=1, source_target_pairs={{0,1},{1,0},{2,3},{3,2},{4,5},{5,4},{6,7},{7,6},{8,9},{9,8},{10,11... | collective-permute-start | bytes 3538952 | tf_op jit(solution)/shard_map/tokens_core/ppermute | solution.py:58
  39.0 24.8 %collective-permute-start.16 = (bf16[128,4608]{1,0:T(8,128)(2,1)S(1)}, bf16[128,4608]{1,0:T(8,128)(2,1)S(1)}, u32[]{:S(2)}, u32[]{:S(2)}) collective-permute-start(bf16[128,4608]{1,0:T(8,128)(2,1)S(1)} %get-tuple-element.33.one), channel_id=1, source_target_pairs={{0,4},{1,13},{4,8},{5,1},{8,12},{9,5},{12,0},{13,9},{2,6},{3,15},{... | collective-permute-start | bytes 3538952 | tf_op jit(solution)/shard_map/tokens_y/ppermute | solution.py:25
  40.1 14.4 %collective-permute-start.10 = (bf16[64,4608]{1,0:T(8,128)(2,1)}, bf16[64,4608]{1,0:T(8,128)(2,1)S(1)}, u32[]{:S(2)}, u32[]{:S(2)}) collective-permute-start(bf16[64,4608]{1,0:T(8,128)(2,1)} %get-tuple-element.34.mine), channel_id=1, source_target_pairs={{0,64},{1,193},{64,0},{65,129},{128,192},{129,65},{192,128},{193,1... | collective-permute-start | bytes 1769480 | tf_op jit(solution)/shard_map/weight_x/ppermute | solution.py:31
  42.6 9.3 %collective-permute-start.5 = (bf16[384,128]{1,0:T(8,128)(2,1)S(1)}, bf16[384,128]{1,0:T(8,128)(2,1)S(1)}, u32[]{:S(2)}, u32[]{:S(2)}) collective-permute-start(bf16[384,128]{1,0:T(8,128)(2,1)S(1)} %get-tuple-element.28.refs_2_), channel_id=1, source_target_pairs={{0,2},{2,0},{1,3},{3,1},{4,6},{6,4},{5,7},{7,5},{8,10},{10,8},{9,1... | collective-permute-start | bytes 294920 | tf_op jit(solution)/shard_map/act_z/ppermute | solution.py:58
  53.2 1.4 %collective-permute-start.6 = (f32[8,2304]{1,0:T(8,128)S(1)}, f32[8,2304]{1,0:T(8,128)S(1)}, u32[]{:S(2)}, u32[]{:S(2)}) collective-permute-start(f32[8,2304]{1,0:T(8,128)S(1)} %get-tuple-element.32), channel_id=1, source_target_pairs={{0,1},{1,0},{2,3},{3,2},{4,5},{5,4},{6,7},{7,6},{8,9},{9,8},{10,11... | collective-permute-start | bytes 221192 | tf_op jit(solution)/shard_map/gate_core/ppermute | solution.py:58
  53.3 6.1 %collective-permute-start.14 = (bf16[4,128,128]{2,1,0:T(8,128)(2,1)S(1)}, bf16[4,128,128]{2,1,0:T(8,128)(2,1)S(1)}, u32[]{:S(2)}, u32[]{:S(2)}) collective-permute-start(bf16[4,128,128]{2,1,0:T(8,128)(2,1)S(1)} %get-tuple-element.35.mixed), channel_id=1, source_target_pairs={{0,1},{1,0},{2,3},{3,2},{4,5},{5,4},{6,7},{7,6},{8,9},{9,8},{10,11... | collective-permute-start | bytes 393224 | tf_op jit(solution)/shard_map/mixed_core/ppermute | solution.py:58
  54.6 5.2 %collective-permute-start.11 = (f32[8,2304]{1,0:T(8,128)S(1)}, f32[8,2304]{1,0:T(8,128)S(1)}, u32[]{:S(2)}, u32[]{:S(2)}) collective-permute-start(f32[8,2304]{1,0:T(8,128)S(1)} %gate_sum.5.tie.first), channel_id=1, source_target_pairs={{0,16},{16,0},{32,48},{48,32},{1,17},{17,1},{33,49},{49,33},{2,18}... | collective-permute-start | bytes 221192 | tf_op jit(solution)/shard_map/gate_zl/ppermute | solution.py:58
  55.8 4.1 %collective-permute-start.12 = (f32[8,2304]{1,0:T(8,128)S(1)}, f32[8,2304]{1,0:T(8,128)S(1)}, u32[]{:S(2)}, u32[]{:S(2)}) collective-permute-start(f32[8,2304]{1,0:T(8,128)S(1)} %gate_sum.5.tie.first), channel_id=1, source_target_pairs={{0,32},{16,48},{32,0},{48,16},{1,33},{17,49},{33,1},{49,17},{2,34}... | collective-permute-start | bytes 221192 | tf_op jit(solution)/shard_map/gate_zl/ppermute | solution.py:58
  57.2 6.5 %collective-permute-start.13 = (f32[8,2304]{1,0:T(8,128)S(1)}, f32[8,2304]{1,0:T(8,128)S(1)}, u32[]{:S(2)}, u32[]{:S(2)}) collective-permute-start(f32[8,2304]{1,0:T(8,128)S(1)} %gate_sum.5.tie.first), channel_id=1, source_target_pairs={{0,48},{16,32},{32,16},{48,0},{1,49},{17,33},{33,17},{49,1},{2,50}... | collective-permute-start | bytes 221192 | tf_op jit(solution)/shard_map/gate_zl/ppermute | solution.py:58
  59.4 15.4 %collective-permute-start.18 = (bf16[128,4608]{1,0:T(8,128)(2,1)S(1)}, bf16[128,4608]{1,0:T(8,128)(2,1)S(1)}, u32[]{:S(2)}, u32[]{:S(2)}) collective-permute-start(bf16[128,4608]{1,0:T(8,128)(2,1)S(1)} %join.1.refs_0_.mine), channel_id=1, source_target_pairs={{0,192},{1,65},{64,128},{65,1},{128,64},{129,193},{192,0},{193,129... | collective-permute-start | bytes 3538952 | tf_op jit(solution)/shard_map/weight_x/ppermute | solution.py:31
  63.8 11.1 %collective-permute-start.17 = (bf16[128,4608]{1,0:T(8,128)(2,1)S(1)}, bf16[128,4608]{1,0:T(8,128)(2,1)S(1)}, u32[]{:S(2)}, u32[]{:S(2)}) collective-permute-start(bf16[128,4608]{1,0:T(8,128)(2,1)S(1)} %fence.6.two), channel_id=1, source_target_pairs={{0,1},{1,0},{2,3},{3,2},{4,5},{5,4},{6,7},{7,6},{8,9},{9,8},{10,11... | collective-permute-start | bytes 3538952 | tf_op jit(solution)/shard_map/tokens_core/ppermute | solution.py:58
  65.4 16.1 %collective-permute-start.22 = (bf16[128,4608]{1,0:T(8,128)(2,1)S(1)}, bf16[128,4608]{1,0:T(8,128)(2,1)S(1)}, u32[]{:S(2)}, u32[]{:S(2)}) collective-permute-start(bf16[128,4608]{1,0:T(8,128)(2,1)S(1)} %fence.6.two), channel_id=1, source_target_pairs={{0,4},{1,13},{4,8},{5,1},{8,12},{9,5},{12,0},{13,9},{2,6},{3,15},{... | collective-permute-start | bytes 3538952 | tf_op jit(solution)/shard_map/tokens_y/ppermute | solution.py:25
  81.5 18.1 %collective-permute-start.23 = (bf16[128,4608]{1,0:T(8,128)(2,1)S(1)}, bf16[128,4608]{1,0:T(8,128)(2,1)S(1)}, u32[]{:S(2)}, u32[]{:S(2)}) collective-permute-start(bf16[128,4608]{1,0:T(8,128)(2,1)S(1)} %fence.7.three), channel_id=1, source_target_pairs={{0,1},{1,0},{2,3},{3,2},{4,5},{5,4},{6,7},{7,6},{8,9},{9,8},{10,11... | collective-permute-start | bytes 3538952 | tf_op jit(solution)/shard_map/tokens_core/ppermute | solution.py:58
  82.9 7.9 %collective-permute-start.15 = (f32[8,2304]{1,0:T(8,128)S(1)}, f32[8,2304]{1,0:T(8,128)S(1)}, u32[]{:S(2)}, u32[]{:S(2)}) collective-permute-start(f32[8,2304]{1,0:T(8,128)S(1)} %gate_sum.6.refs_1_.left), channel_id=1, source_target_pairs={{0,2},{2,0},{1,3},{3,1},{4,6},{6,4},{5,7},{7,5},{8,10},{10,8},{9,1... | collective-permute-start | bytes 221192 | tf_op jit(solution)/shard_map/gate_zh/ppermute | solution.py:58
  88.3 24.7 %collective-permute-start.27 = (bf16[3,256,256]{2,1,0:T(8,128)(2,1)S(1)}, bf16[3,256,256]{2,1,0:T(8,128)(2,1)S(1)}, u32[]{:S(2)}, u32[]{:S(2)}) collective-permute-start(bf16[3,256,256]{2,1,0:T(8,128)(2,1)S(1)} %get-tuple-element.36.refs_0_.refs_1_), channel_id=1, source_target_pairs={{0,2},{2,0},{1,3},{3,1},{4,6},{6,4},{5,7},{7,5},{8,10},{10,8},{9,1... | collective-permute-start | bytes 1179656 | tf_op jit(solution)/shard_map/out_z/ppermute | solution.py:58
  90.8 3.9 %collective-permute-start.19 = (f32[8,2304]{1,0:T(8,128)S(1)}, f32[8,2304]{1,0:T(8,128)S(1)}, u32[]{:S(2)}, u32[]{:S(2)}) collective-permute-start(f32[8,2304]{1,0:T(8,128)S(1)} %gate_sum.7.first), channel_id=1, source_target_pairs={{0,64},{64,0},{128,192},{192,128},{1,65},{65,1},{129,193},{193,129... | collective-permute-start | bytes 221192 | tf_op jit(solution)/shard_map/gate_x/ppermute | solution.py:58
  91.2 6.2 %collective-permute-start.20 = (f32[8,2304]{1,0:T(8,128)S(1)}, f32[8,2304]{1,0:T(8,128)S(1)}, u32[]{:S(2)}, u32[]{:S(2)}) collective-permute-start(f32[8,2304]{1,0:T(8,128)S(1)} %gate_sum.7.first), channel_id=1, source_target_pairs={{0,128},{64,192},{128,0},{192,64},{1,129},{65,193},{129,1},{193,65... | collective-permute-start | bytes 221192 | tf_op jit(solution)/shard_map/gate_x/ppermute | solution.py:58
  94.4 5.2 %collective-permute-start.21 = (f32[8,2304]{1,0:T(8,128)S(1)}, f32[8,2304]{1,0:T(8,128)S(1)}, u32[]{:S(2)}, u32[]{:S(2)}) collective-permute-start(f32[8,2304]{1,0:T(8,128)S(1)} %gate_sum.7.first), channel_id=1, source_target_pairs={{0,192},{64,128},{128,64},{192,0},{1,193},{65,129},{129,65},{193,1... | collective-permute-start | bytes 221192 | tf_op jit(solution)/shard_map/gate_x/ppermute | solution.py:58
  99.6 10.0 %copy-start.3 = (bf16[256,4608]{1,0:T(8,128)(2,1)S(1)}, bf16[256,4608]{1,0:T(8,128)(2,1)}, u32[]{:S(2)}) copy-start(bf16[256,4608]{1,0:T(8,128)(2,1)} %weight.1) | copy-start | bytes 7077892
  101.0 12.0 %collective-permute-start.24 = (f32[8,2304]{1,0:T(8,128)S(1)}, f32[8,2304]{1,0:T(8,128)S(1)}, u32[]{:S(2)}, u32[]{:S(2)}) collective-permute-start(f32[8,2304]{1,0:T(8,128)S(1)} %fence.8.first), channel_id=1, source_target_pairs={{0,4},{4,0},{8,12},{12,8},{1,5},{5,1},{9,13},{13,9},{2,6},{6,2},{1... | collective-permute-start | bytes 221192 | tf_op jit(solution)/shard_map/gate_y/ppermute | solution.py:58
  101.1 11.9 %collective-permute-start.25 = (f32[8,2304]{1,0:T(8,128)S(1)}, f32[8,2304]{1,0:T(8,128)S(1)}, u32[]{:S(2)}, u32[]{:S(2)}) collective-permute-start(f32[8,2304]{1,0:T(8,128)S(1)} %fence.8.first), channel_id=1, source_target_pairs={{0,8},{4,12},{8,0},{12,4},{1,9},{5,13},{9,1},{13,5},{2,10},{6,14},... | collective-permute-start | bytes 221192 | tf_op jit(solution)/shard_map/gate_y/ppermute | solution.py:58
  101.3 11.7 %collective-permute-start.26 = (f32[8,2304]{1,0:T(8,128)S(1)}, f32[8,2304]{1,0:T(8,128)S(1)}, u32[]{:S(2)}, u32[]{:S(2)}) collective-permute-start(f32[8,2304]{1,0:T(8,128)S(1)} %fence.8.first), channel_id=1, source_target_pairs={{0,12},{4,8},{8,4},{12,0},{1,13},{5,9},{9,5},{13,1},{2,14},{6,10},... | collective-permute-start | bytes 221192 | tf_op jit(solution)/shard_map/gate_y/ppermute | solution.py:58
  105.0 13.4 %collective-permute-start.29 = (bf16[256,256]{1,0:T(8,128)(2,1)S(1)}, bf16[256,256]{1,0:T(8,128)(2,1)S(1)}, u32[]{:S(2)}, u32[]{:S(2)}) collective-permute-start(bf16[256,256]{1,0:T(8,128)(2,1)S(1)} %far_products_last.1.refs_1_.tie), channel_id=1, source_target_pairs={{0,2},{2,0},{1,3},{3,1},{4,6},{6,4},{5,7},{7,5},{8,10},{10,8},{9,1... | collective-permute-start | bytes 393224 | tf_op jit(solution)/shard_map/out_z_last/ppermute | solution.py:58
  113.0 7.0 %collective-permute-start.28 = (f32[8,2304]{1,0:T(8,128)S(1)}, f32[8,2304]{1,0:T(8,128)S(1)}, u32[]{:S(2)}, u32[]{:S(2)}) collective-permute-start(f32[8,2304]{1,0:T(8,128)S(1)} %fence.9), channel_id=1, source_target_pairs={{0,1},{1,0},{2,3},{3,2},{4,5},{5,4},{6,7},{7,6},{8,9},{9,8},{10,11... | collective-permute-start | bytes 221192 | tf_op jit(solution)/shard_map/gate_core_back/ppermute | solution.py:58

commit v6 on v5

--- a/solution.py
+++ b/solution.py
@@ -1,3 +1,5 @@
+import functools
+
 import jax
 import jax.numpy as jnp
 from jax import lax
@@ -79,11 +81,21 @@
     return jnp.where((column >= low) & (column < low + stacked // adapters), 1.0, 0.0)
 
 
-def join_kernel(at, mine, got, tie, out):
-    quarter = mine.shape[0]
-    side = lax.rem(at[4], 2)
-    for place, ref in ((side, mine), (1 - side, got)):
-        out[pl.ds(pl.multiple_of(place * quarter, quarter), quarter), :] = ref[...]
+def join_kernel(side, mine, got, tie, out):
+    rows = mine.shape[0]
+    for place, ref in ((side[0], mine), (1 - side[0], got)):
+        out[pl.ds(pl.multiple_of(place * rows, rows), rows), :] = ref[...]
+
+
+def join(side, mine, got, tie):
+    return pl.pallas_call(
+        join_kernel,
+        in_specs=[SMEM, VMEM, VMEM, ANY],
+        out_specs=VMEM,
+        out_shape=shaped((2 * mine.shape[0], mine.shape[1]), mine.dtype),
+        compiler_params=SMALL,
+        name="join",
+    )(side.reshape(1), mine, got, tie)
 
 
 def token_kernel(at, hidden, grad, up, gate, mixed, gates, back):
@@ -117,25 +129,23 @@
     rest[...] = keep[y] + got[y].astype(F32)
 
 
-def act_z_kernel(at, rest, first, second, third, mixed, down, tie, keep, give, all_mixed):
+def act_z_kernel(at, rest, first, second, third, mixed, tie, tie_too, keep, give, all_mixed):
     y, zh = at[1], at[2]
-    tokens = keep.shape[0]
     for out, side in ((give, 1 - zh), (keep, zh)):
         total = (rest[side] + first[side].astype(F32)) + (
             second[side].astype(F32) + third[side].astype(F32)
         )
-        out[pl.ds(0, tokens), :] = total.astype(out.dtype)
-    give[pl.ds(tokens, down.shape[0]), :] = down[...]
+        out[...] = total.astype(out.dtype)
     all_mixed[y] = mixed[...]
     for ref, mask in ((first, 1), (second, 2), (third, 3)):
         all_mixed[jnp.bitwise_xor(y, mask)] = ref[2]
 
 
-def gate_kernel(at, keep, got, back, gates, hidden, result, give):
+def gate_kernel(at, keep, got, back, gates, hidden, tie, result, give):
     stacked = keep.shape[1]
     adapters = gates.shape[0]
     half = result.shape[1]
-    product = (keep[...] + got[pl.ds(0, keep.shape[0]), :].astype(F32)) * back[...]
+    product = (keep[...] + got[...].astype(F32)) * back[...]
     ones = membership(adapters, stacked)
     delta = 2.0 * dot_t(ones, product, lax.Precision.HIGHEST)
     dlogit = delta * gates[...] * (1.0 - gates[...])
@@ -169,36 +179,35 @@
     out[...] = value.astype(out.dtype)
 
 
-def far_kernel(at, own, own_s, one, one_s, two, two_s, mixed, mixed_s, mine, got, downs, out, weight):
+def far_kernel(at, own, own_s, one, one_s, two, two_s, mixed, mixed_s, mine, got, tie, out, weight, down):
+    width = weight.shape[1]
     rows = mine.shape[0]
     block = at[4] // 2
     for number, ref in ((block, mine), (1 - block, got)):
-        weight[pl.ds(pl.multiple_of(number * rows, rows), rows), :] = ref[...]
-    down = downs.at[pl.ds(own.shape[0], weight.shape[0])]
+        place = pl.ds(pl.multiple_of(number * rows, rows), rows)
+        weight[place, :] = ref[:, :width]
+        down[place, :] = ref[:, width:]
     for steps, group in enumerate(((own, own_s), (one, one_s), (two, two_s))):
         rows_product(at, steps, group, (mixed, mixed_s), weight, down, out.at[steps])
 
 
-def far_last_kernel(at, three, three_s, mixed, mixed_s, weight, downs, out):
-    down = downs.at[pl.ds(three.shape[0], weight.shape[0])]
+def far_last_kernel(at, three, three_s, mixed, mixed_s, weight, down, out):
     rows_product(at, 3, (three, three_s), (mixed, mixed_s), weight, down, out)
 
 
-def own_kernel(
-    at, own, own_s, one, one_s, two, two_s, three, three_s, mixed, mixed_s, weight, down, tie, out
-):
-    groups = ((own, own_s), (one, one_s), (two, two_s), (three, three_s))
-    for steps, group in enumerate(groups):
-        rows_product(at, steps, group, (mixed, mixed_s), weight, down, out.at[steps])
-
-
-def place_kernel(at, own, got, last, out, sems):
+def own_kernel(first, at, near, near_s, more, more_s, mixed, mixed_s, weight, down, tie, out):
+    for number, group in enumerate(((near, near_s), (more, more_s))):
+        rows_product(at, first + number, group, (mixed, mixed_s), weight, down, out.at[number])
+
+
+def place_kernel(at, near, rest, got, last, out, sems):
     y, zh, c = at[1], at[2], at[3]
     tokens = out.shape[3]
     copies = []
     for steps in range(4):
+        own = near.at[steps] if steps < 2 else rest.at[steps - 2]
         other = got.at[steps] if steps < 3 else last
-        for ref, side in ((own.at[steps], zh), (other, 1 - zh)):
+        for ref, side in ((own, zh), (other, 1 - zh)):
             for half, core in ((0, c), (1, 1 - c)):
                 copies.append(
                     pltpu.make_async_copy(
@@ -220,13 +229,16 @@
     features = weight.shape[0]
     depth = width + stacked
     quarter = features // 4
-    x, y, zh, c = (lax.axis_index(a) for a in ("x", "y", "zh", "c"))
+    x, y, zl, zh, c = (lax.axis_index(a) for a in ("x", "y", "zl", "zh", "c"))
     turned = jnp.where(x == 0, 0, jnp.where(x == 3, 1, x + 1))
     number = jnp.where(c == 0, x, turned)
     at = jnp.stack([x, y, zh, c, number]).astype(jnp.int32)
 
     with jax.named_scope("weight_z"):
-        piece = lax.dynamic_slice_in_dim(weight, number * quarter, quarter, 0)
+        start = number * quarter + (zl % 2) * (quarter // 2)
+        piece = jnp.concatenate(
+            [lax.dynamic_slice_in_dim(v, start, quarter // 2, 0) for v in (weight, down)], axis=1
+        )
         far_piece = swap(piece, "zh", 1)
     with jax.named_scope("tokens_y"):
         one = ring(grad, "y")
@@ -268,42 +280,59 @@
         compiler_params=SMALL,
         name="rank_sum_core",
     )(at, keep, got, mixed)
+    (far_piece,) = fence((far_piece,), rest)
+    with jax.named_scope("weight_zl"):
+        z_got = swap(far_piece, "zl", 1)
     with jax.named_scope("act_y"):
         first, second, third = (
             swap(v, "y", mask) for v, mask in ((first, 1), (second, 2), (third, 3))
         )
     keep, give, all_mixed = pl.pallas_call(
         act_z_kernel,
-        in_specs=[SMEM] + [VMEM] * 6 + [ANY],
+        in_specs=[SMEM] + [VMEM] * 5 + [ANY] * 2,
         out_specs=[VMEM] * 3,
         out_shape=[
             shaped((tokens, stacked), F32),
-            shaped((tokens + features, stacked), BF16),
+            shaped((tokens, stacked), BF16),
             shaped((4, tokens, stacked), BF16),
         ],
         compiler_params=SMALL,
         name="rank_sum_y",
-    )(at, rest, first, second, third, mixed, down, own_s)
-    one, far_piece = fence((one, far_piece), give)
+    )(at, rest, first, second, third, mixed, own_s, z_got)
+    (one,) = fence((one,), give)
     with jax.named_scope("tokens_y"):
         two = ring(one, "y")
+    far_quarter = join(zl % 2, far_piece, z_got, give)
+    with jax.named_scope("weight_x"):
+        w_one = pairs(far_quarter, "x", True)
     with jax.named_scope("act_z"):
         message = swap(give, "zh", 1)
     with jax.named_scope("mixed_core"):
         mixed_s = swap(all_mixed, "c", 1)
     with jax.named_scope("tokens_core"):
         one_s = swap(one, "c", 1)
-    with jax.named_scope("weight_x"):
-        w_one = pairs(far_piece, "x", True)
+
+    def own_products(first, near, near_s, more, more_s, tie):
+        return pl.pallas_call(
+            functools.partial(own_kernel, first),
+            in_specs=[SMEM] + [VMEM] * 8 + [ANY],
+            out_specs=VMEM,
+            out_shape=shaped((2, 2 * tokens, features), BF16),
+            compiler_params=MIDDLE,
+            cost_estimate=cost(8 * tokens * depth * features, 12 * tokens * depth),
+            name="own_products",
+        )(at, near, near_s, more, more_s, all_mixed, mixed_s, weight, down, tie)
+
+    own_near = own_products(0, grad, own_s, one, one_s, give)
 
     total, give = pl.pallas_call(
         gate_kernel,
-        in_specs=[SMEM] + [VMEM] * 5,
+        in_specs=[SMEM] + [VMEM] * 5 + [ANY],
         out_specs=[VMEM, VMEM],
         out_shape=[shaped((adapters, width // 2), F32)] * 2,
         compiler_params=SMALL,
         name="gate_products",
-    )(at, keep, message, back, gates, hidden)
+    )(at, keep, message, back, gates, hidden, own_near)
 
     def add(left, right, *ties):
         return pl.pallas_call(
@@ -332,15 +361,8 @@
 
     with jax.named_scope("gate_core"):
         got = swap(give, "c", 1)
-    total = add(total, got, one_s, w_one)
-    w_mine = pl.pallas_call(
-        join_kernel,
-        in_specs=[SMEM, VMEM, VMEM, ANY],
-        out_specs=VMEM,
-        out_shape=shaped((2 * quarter, width), BF16),
-        compiler_params=SMALL,
-        name="join",
-    )(at, far_piece, w_one, total)
+    total = add(total, got, w_one)
+    w_mine = join(number % 2, far_quarter, w_one, total)
     with jax.named_scope("weight_x"):
         w_got = pairs(w_mine, "x", False)
     total = step(total, "zl", w_mine, mixed_s)
@@ -353,18 +375,19 @@
         two_s = swap(two, "c", 1)
     total = add(total, got, two_s, w_got)
     near = (grad, own_s, one, one_s, two, two_s)
-    far, far_weight = pl.pallas_call(
+    far, far_weight, far_down = pl.pallas_call(
         far_kernel,
-        in_specs=[SMEM] + [VMEM] * 11,
-        out_specs=[VMEM] * 2,
+        in_specs=[SMEM] + [VMEM] * 10 + [ANY],
+        out_specs=[VMEM] * 3,
         out_shape=[
             shaped((3, 2 * tokens, features), BF16),
             shaped((features, width), BF16),
+            shaped((features, stacked), BF16),
         ],
         compiler_params=MIDDLE,
         cost_estimate=cost(12 * tokens * depth * features, 18 * tokens * depth),
         name="far_products",
-    )(at, *near, all_mixed, mixed_s, w_mine, w_got, message)
+    )(at, *near, all_mixed, mixed_s, w_mine, w_got, total)
     (three,) = fence((three,), far)
     with jax.named_scope("tokens_core"):
         three_s = swap(three, "c", 1)
@@ -380,22 +403,14 @@
         cost_estimate=cost(4 * tokens * depth * features, 6 * tokens * depth),
         compiler_params=MIDDLE,
         name="far_products_last",
-    )(at, three, three_s, all_mixed, mixed_s, far_weight, message)
+    )(at, three, three_s, all_mixed, mixed_s, far_weight, far_down)
     with jax.named_scope("out_z_last"):
         last_got = swap(last, "zh", 1)
 
     (total,) = fence((total,), last)
     total = step(total, "y")
-    own_out = pl.pallas_call(
-        own_kernel,
-        in_specs=[SMEM] + [VMEM] * 12 + [ANY],
-        out_specs=VMEM,
-        out_shape=shaped((4, 2 * tokens, features), BF16),
-        cost_estimate=cost(16 * tokens * depth * features, 24 * tokens * depth),
-        compiler_params=MIDDLE,
-        name="own_products",
-    )(at, *near, three, three_s, all_mixed, mixed_s, weight, down, last)
-    (total,) = fence((total,), far_got, own_out)
+    own_rest = own_products(2, two, two_s, three, three_s, last)
+    (total,) = fence((total,), far_got, own_rest)
     with jax.named_scope("gate_core_back"):
         other = swap(total, "c", 1)
     gate_grad = jnp.where(
@@ -404,13 +419,13 @@
 
     out = pl.pallas_call(
         place_kernel,
-        in_specs=[SMEM, VMEM, VMEM, VMEM],
+        in_specs=[SMEM] + [VMEM] * 4,
         out_specs=HBM,
         out_shape=shaped((4, 2, 2, tokens, features), BF16),
         scratch_shapes=[pltpu.SemaphoreType.DMA((16,))],
         compiler_params=MIDDLE,
         name="place",
-    )(at, own_out, far_got, last_got)
+    )(at, own_near, own_rest, far_got, last_got)
     return gate_grad, out.reshape(16 * tokens, features)
 
 

time: 122 us -> 120 us (0.984)
  the two profiles are of different devices: /device:TPU:1 before, /device:TPU:5 now
where the time goes in v6:
time: 120 us; the launch traced here: 119 us
  starting transfers between devices  55.5 us (46%)
  waiting for transfers between devices  31.6 us (26%)
  Pallas kernels  19.8 us (16%)
  local copies, waits for them, and re-layouts  9.64 us (8%)
  other arithmetic  1.41 us (1%)
    ppermute x26, starting transfers between devices, swap(): return lax.ppermute(value, axis, [(i, i ^ mask) for i in range(size)])  47.1 us
    ppermute x26, waiting for transfers between devices, swap(): return lax.ppermute(value, axis, [(i, i ^ mask) for i in range(size)])  29 us
    unnamed x54, local copies, waits for them, and re-layouts  7.72 us
    ppermute x3, starting transfers between devices, ring(): return lax.ppermute(value, (axis, 'c'), pairs)  7.07 us
    pallas_call x2, Pallas kernels, own_products(): pl.pallas_call(functools.partial(own_kernel, first), in_specs=[SMEM] + [V...  5.13 us
    pallas_call x1, Pallas kernels, on_device(): pl.pallas_call(far_kernel, in_specs=[SMEM] + [VMEM] * 10 + [ANY], out_spe...  3.55 us
  transfers between devices with their start and end apart: 31, of which 14 were waited for; matrix products, arithmetic and copies ran while one was open for 2% of the time, Pallas kernels for 17%

profile of v6, /device:TPU:5, one launch (start us, length us, event | category | flops | bytes accessed | tf_op | source)
XLA Modules:
  0.0 119.1 jit_solution(3623587063998822610)
XLA Ops:
  1.4 2.7 %collective-permute-start.8 = (bf16[128,4608]{1,0:T(8,128)(2,1)}, bf16[128,4608]{1,0:T(8,128)(2,1)}, u32[]{:S(2)}, u32[]{:S(2)}) collective-permute-start(bf16[128,4608]{1,0:T(8,128)(2,1)} %own.1), channel_id=1, source_target_pairs={{0,4},{1,13},{4,8},{5,1},{8,12},{9,5},{12,0},{13,9},{2,6},{3,15},{... | collective-permute-start | bytes 3538952 | tf_op jit(solution)/shard_map/tokens_y/ppermute | solution.py:27
  4.1 1.1 constant_dynamic-slice_fusion.1
  6.7 6.9 %collective-permute-start.5 = (bf16[32,4736]{1,0:T(8,128)(2,1)}, bf16[32,4736]{1,0:T(8,128)(2,1)}, u32[]{:S(2)}, u32[]{:S(2)}) collective-permute-start(bf16[32,4736]{1,0:T(8,128)(2,1)} %pad_maximum_fusion), channel_id=1, source_target_pairs={{0,2},{2,0},{1,3},{3,1},{4,6},{6,4},{5,7},{7,5},{8,10},{10,8},{9,1... | collective-permute-start | bytes 909320 | tf_op jit(solution)/shard_map/weight_z/ppermute | solution.py:60
  13.7 1.2 %copy-done.22 = bf16[2048,256]{1,0:T(8,128)(2,1)S(1)} copy-done((bf16[2048,256]{1,0:T(8,128)(2,1)S(1)}, bf16[2048,256]{1,0:T(8,128)(2,1)}, u32[]{:S(2)}) %copy-start.22) | copy-done | bytes 1048600
  15.8 1.0 rank_products.1
  16.9 1.3 %copy-done.21 = bf16[128,4608]{1,0:T(8,128)(2,1)S(1)} copy-done((bf16[128,4608]{1,0:T(8,128)(2,1)S(1)}, bf16[128,4608]{1,0:T(8,128)(2,1)}, u32[]{:S(2)}) %copy-start.21) | copy-done | bytes 1179672
  18.1 0.9 copy-done.26
  19.0 2.0 %token_values.1 = (bf16[128,128]{1,0:T(8,128)(2,1)S(1)}, f32[8,128]{1,0:T(8,128)S(1)}, f32[128,128]{1,0:T(8,128)S(1)}) custom-call(s32[5]{0:T(128)S(1)} %stack.23.at, bf16[128,4608]{1,0:T(8,128)(2,1)S(1)} %copy-done.7, bf16[128,4608]{1,0:T(8,128)(2,1)S(1)} %copy-done.4, bf16[128,4608]{1,0:T(8,128)(2,1)S(1)} %copy-done.21, bf16[8,4608]{1,0:T(8,128)(2,1)S(1)} %copy-done.26), custom_call_target="tpu_custom_call" | custom-call | flops 452984832 | bytes 7077888 | tf_op jit(solution)/shard_map/token_values/pallas_call | solution.py:262
  21.6 4.8 %collective-permute-done.5.refs_0_ = bf16[32,4736]{1,0:T(8,128)(2,1)} collective-permute-done((bf16[32,4736]{1,0:T(8,128)(2,1)}, bf16[32,4736]{1,0:T(8,128)(2,1)}, u32[]{:S(2)}, u32[]{:S(2)}) %collective-permute-start.5) | collective-permute-done | bytes 303136 | tf_op jit(solution)/shard_map/weight_z/ppermute | solution.py:60
  26.4 1.3 %collective-permute-start.6 = (bf16[32,4736]{1,0:T(8,128)(2,1)}, bf16[32,4736]{1,0:T(8,128)(2,1)S(1)}, u32[]{:S(2)}, u32[]{:S(2)}) collective-permute-start(bf16[32,4736]{1,0:T(8,128)(2,1)} %fence.6.mine), channel_id=1, source_target_pairs={{0,16},{16,0},{32,48},{48,32},{1,17},{17,1},{33,49},{49,33},{2,18}... | collective-permute-start | bytes 909320 | tf_op jit(solution)/shard_map/weight_zl/ppermute | solution.py:60
  27.8 2.7 %collective-permute-start.2 = (bf16[3,128,128]{2,1,0:T(8,128)(2,1)S(1)}, bf16[3,128,128]{2,1,0:T(8,128)(2,1)S(1)}, u32[]{:S(2)}, u32[]{:S(2)}) collective-permute-start(bf16[3,128,128]{2,1,0:T(8,128)(2,1)S(1)} %get-tuple-element.24), channel_id=1, source_target_pairs={{0,8},{4,12},{8,0},{12,4},{1,9},{5,13},{9,1},{13,5},{2,10},{6,14},... | collective-permute-start | bytes 294920 | tf_op jit(solution)/shard_map/act_y/ppermute | solution.py:60
  30.5 1.8 %collective-permute-done.1.first = bf16[3,128,128]{2,1,0:T(8,128)(2,1)S(1)} collective-permute-done((bf16[3,128,128]{2,1,0:T(8,128)(2,1)S(1)}, bf16[3,128,128]{2,1,0:T(8,128)(2,1)S(1)}, u32[]{:S(2)}, u32[]{:S(2)}) %collective-permute-start.1) | collective-permute-done | bytes 98336 | tf_op jit(solution)/shard_map/act_y/ppermute | solution.py:60
  33.1 1.3 %collective-permute-done.2.second = bf16[3,128,128]{2,1,0:T(8,128)(2,1)S(1)} collective-permute-done((bf16[3,128,128]{2,1,0:T(8,128)(2,1)S(1)}, bf16[3,128,128]{2,1,0:T(8,128)(2,1)S(1)}, u32[]{:S(2)}, u32[]{:S(2)}) %collective-permute-start.2) | collective-permute-done | bytes 98336 | tf_op jit(solution)/shard_map/act_y/ppermute | solution.py:60
  34.4 2.5 %collective-permute-done.3.third = bf16[3,128,128]{2,1,0:T(8,128)(2,1)S(1)} collective-permute-done((bf16[3,128,128]{2,1,0:T(8,128)(2,1)S(1)}, bf16[3,128,128]{2,1,0:T(8,128)(2,1)S(1)}, u32[]{:S(2)}, u32[]{:S(2)}) %collective-permute-start.3) | collective-permute-done | bytes 98336 | tf_op jit(solution)/shard_map/act_y/ppermute | solution.py:60
  38.1 2.2 %collective-permute-start.9 = (bf16[128,4608]{1,0:T(8,128)(2,1)}, bf16[128,4608]{1,0:T(8,128)(2,1)S(1)}, u32[]{:S(2)}, u32[]{:S(2)}) collective-permute-start(bf16[128,4608]{1,0:T(8,128)(2,1)} %fence.7.more.one), channel_id=1, source_target_pairs={{0,1},{1,0},{2,3},{3,2},{4,5},{5,4},{6,7},{7,6},{8,9},{9,8},{10,11... | collective-permute-start | bytes 3538952 | tf_op jit(solution)/shard_map/tokens_core/ppermute | solution.py:60
  40.2 2.3 %collective-permute-start.17 = (bf16[128,4608]{1,0:T(8,128)(2,1)}, bf16[128,4608]{1,0:T(8,128)(2,1)S(1)}, u32[]{:S(2)}, u32[]{:S(2)}) collective-permute-start(bf16[128,4608]{1,0:T(8,128)(2,1)} %fence.7.more.one), channel_id=1, source_target_pairs={{0,4},{1,13},{4,8},{5,1},{8,12},{9,5},{12,0},{13,9},{2,6},{3,15},{... | collective-permute-start | bytes 3538952 | tf_op jit(solution)/shard_map/tokens_y/ppermute | solution.py:27
  42.5 1.0 join.2.mine
  43.9 5.1 %collective-permute-start.7 = (bf16[128,128]{1,0:T(8,128)(2,1)S(1)}, bf16[128,128]{1,0:T(8,128)(2,1)S(1)}, u32[]{:S(2)}, u32[]{:S(2)}) collective-permute-start(bf16[128,128]{1,0:T(8,128)(2,1)S(1)} %get-tuple-element.27.refs_1_.tie), channel_id=1, source_target_pairs={{0,2},{2,0},{1,3},{3,1},{4,6},{6,4},{5,7},{7,5},{8,10},{10,8},{9,1... | collective-permute-start | bytes 98312 | tf_op jit(solution)/shard_map/act_z/ppermute | solution.py:60
  49.0 3.2 %own_products.2.tie.near = bf16[2,256,256]{2,1,0:T(8,128)(2,1)S(1)} custom-call(s32[5]{0:T(128)S(1)} %stack.23.at, bf16[128,4608]{1,0:T(8,128)(2,1)S(1)} %copy-done.5, bf16[128,4608]{1,0:T(8,128)(2,1)S(1)} %copy-done.2, bf16[128,4608]{1,0:T(8,128)(2,1)} %fence.7.more.one, bf16[128,4608]{1,0:T(8,128)(2,1)S(1)} %collective-permute-done.9.more_s.one_s, ...), custom_call_target="tpu_custom_call" | custom-call | flops 1241513984 | bytes 7274496 | tf_op jit(solution)/shard_map/own_products/pallas_call | solution.py:316
  52.2 1.2 %gate_products.1 = (f32[8,2304]{1,0:T(8,128)S(1)}, f32[8,2304]{1,0:T(8,128)S(1)}) custom-call(s32[5]{0:T(128)S(1)} %stack.23.at, f32[128,128]{1,0:T(8,128)S(1)} %get-tuple-element.26.keep, bf16[128,128]{1,0:T(8,128)(2,1)S(1)} %collective-permute-done.7.got, f32[128,128]{1,0:T(8,128)S(1)} %get-tuple-element.28.back, f32[8,128]{1,0:T(8,128)S(1)} %get-tuple-element.29.gates, ...), custom_call_target="tpu_custom_call" | custom-call | tf_op jit(solution)/shard_map/gate_products/pallas_call | solution.py:328
  53.5 0.9 collective-permute-start.11
  54.4 0.9 collective-permute-done.11.right
  56.9 1.7 %collective-permute-start.14 = (f32[8,2304]{1,0:T(8,128)}, f32[8,2304]{1,0:T(8,128)}, u32[]{:S(2)}, u32[]{:S(2)}) collective-permute-start(f32[8,2304]{1,0:T(8,128)} %gate_sum.5.tie.first), channel_id=1, source_target_pairs={{0,32},{16,48},{32,0},{48,16},{1,33},{17,49},{33,1},{49,17},{2,34}... | collective-permute-start | bytes 221192 | tf_op jit(solution)/shard_map/gate_zl/ppermute | solution.py:60
  58.6 1.7 %collective-permute-start.15 = (f32[8,2304]{1,0:T(8,128)}, f32[8,2304]{1,0:T(8,128)}, u32[]{:S(2)}, u32[]{:S(2)}) collective-permute-start(f32[8,2304]{1,0:T(8,128)} %gate_sum.5.tie.first), channel_id=1, source_target_pairs={{0,48},{16,32},{32,16},{48,0},{1,49},{17,33},{33,17},{49,1},{2,50}... | collective-permute-start | bytes 221192 | tf_op jit(solution)/shard_map/gate_zl/ppermute | solution.py:60
  60.3 1.1 copy-done.14
  61.4 1.1 copy-done.16
  62.5 1.0 collective-permute-start.19
  64.3 1.0 gate_sum.6.refs_1_.left
  65.3 2.5 %collective-permute-start.18 = (bf16[128,4608]{1,0:T(8,128)(2,1)S(1)}, bf16[128,4608]{1,0:T(8,128)(2,1)S(1)}, u32[]{:S(2)}, u32[]{:S(2)}) collective-permute-start(bf16[128,4608]{1,0:T(8,128)(2,1)S(1)} %fence.8.two.near), channel_id=1, source_target_pairs={{0,1},{1,0},{2,3},{3,2},{4,5},{5,4},{6,7},{7,6},{8,9},{9,8},{10,11... | collective-permute-start | bytes 3538952 | tf_op jit(solution)/shard_map/tokens_core/ppermute | solution.py:60
  67.9 2.0 %collective-permute-start.23 = (bf16[128,4608]{1,0:T(8,128)(2,1)S(1)}, bf16[128,4608]{1,0:T(8,128)(2,1)S(1)}, u32[]{:S(2)}, u32[]{:S(2)}) collective-permute-start(bf16[128,4608]{1,0:T(8,128)(2,1)S(1)} %fence.8.two.near), channel_id=1, source_target_pairs={{0,4},{1,13},{4,8},{5,1},{8,12},{9,5},{12,0},{13,9},{2,6},{3,15},{... | collective-permute-start | bytes 3538952 | tf_op jit(solution)/shard_map/tokens_y/ppermute | solution.py:27
  69.9 4.2 %collective-permute-start.16 = (f32[8,2304]{1,0:T(8,128)S(1)}, f32[8,2304]{1,0:T(8,128)S(1)}, u32[]{:S(2)}, u32[]{:S(2)}) collective-permute-start(f32[8,2304]{1,0:T(8,128)S(1)} %gate_sum.6.refs_1_.left), channel_id=1, source_target_pairs={{0,2},{2,0},{1,3},{3,1},{4,6},{6,4},{5,7},{7,5},{8,10},{10,8},{9,1... | collective-permute-start | bytes 221192 | tf_op jit(solution)/shard_map/gate_zh/ppermute | solution.py:60
  74.1 2.9 %collective-permute-done.16.right = f32[8,2304]{1,0:T(8,128)S(1)} collective-permute-done((f32[8,2304]{1,0:T(8,128)S(1)}, f32[8,2304]{1,0:T(8,128)S(1)}, u32[]{:S(2)}, u32[]{:S(2)}) %collective-permute-start.16) | collective-permute-done | bytes 73760 | tf_op jit(solution)/shard_map/gate_zh/ppermute | solution.py:60
  77.0 1.3 %collective-permute-done.19.refs_1_.got = bf16[128,4736]{1,0:T(8,128)(2,1)S(1)} collective-permute-done((bf16[128,4736]{1,0:T(8,128)(2,1)S(1)}, bf16[128,4736]{1,0:T(8,128)(2,1)S(1)}, u32[]{:S(2)}, u32[]{:S(2)}) %collective-permute-start.19) | collective-permute-done | bytes 1212448 | tf_op jit(solution)/shard_map/weight_x/ppermute | solution.py:33
  78.4 3.6 %far_products.1 = (bf16[3,256,256]{2,1,0:T(8,128)(2,1)S(1)}, bf16[256,4608]{1,0:T(8,128)(2,1)S(1)}, bf16[256,128]{1,0:T(8,128)(2,1)S(1)}) custom-call(s32[5]{0:T(128)S(1)} %stack.23.at, bf16[128,4608]{1,0:T(8,128)(2,1)S(1)} %copy-done.6, bf16[128,4608]{1,0:T(8,128)(2,1)S(1)} %copy-done.3, bf16[128,4608]{1,0:T(8,128)(2,1)} %fence.7.more.one, ...), custom_call_target="tpu_custom_call" | custom-call | flops 1862270976 | bytes 10911744 | tf_op jit(solution)/shard_map/far_products/pallas_call | solution.py:378
  81.9 1.3 %collective-permute-done.23.refs_0_ = bf16[128,4608]{1,0:T(8,128)(2,1)S(1)} collective-permute-done((bf16[128,4608]{1,0:T(8,128)(2,1)S(1)}, bf16[128,4608]{1,0:T(8,128)(2,1)S(1)}, u32[]{:S(2)}, u32[]{:S(2)}) %collective-permute-start.23) | collective-permute-done | bytes 1179680 | tf_op jit(solution)/shard_map/tokens_y/ppermute | solution.py:27
  83.2 2.2 %collective-permute-start.24 = (bf16[128,4608]{1,0:T(8,128)(2,1)S(1)}, bf16[128,4608]{1,0:T(8,128)(2,1)S(1)}, u32[]{:S(2)}, u32[]{:S(2)}) collective-permute-start(bf16[128,4608]{1,0:T(8,128)(2,1)S(1)} %fence.9.three.more), channel_id=1, source_target_pairs={{0,1},{1,0},{2,3},{3,2},{4,5},{5,4},{6,7},{7,6},{8,9},{9,8},{10,11... | collective-permute-start | bytes 3538952 | tf_op jit(solution)/shard_map/tokens_core/ppermute | solution.py:60
  85.4 4.3 %collective-permute-start.28 = (bf16[3,256,256]{2,1,0:T(8,128)(2,1)S(1)}, bf16[3,256,256]{2,1,0:T(8,128)(2,1)S(1)}, u32[]{:S(2)}, u32[]{:S(2)}) collective-permute-start(bf16[3,256,256]{2,1,0:T(8,128)(2,1)S(1)} %get-tuple-element.33.refs_0_.refs_1_), channel_id=1, source_target_pairs={{0,2},{2,0},{1,3},{3,1},{4,6},{6,4},{5,7},{7,5},{8,10},{10,8},{9,1... | collective-permute-start | bytes 1179656 | tf_op jit(solution)/shard_map/out_z/ppermute | solution.py:60
  90.5 1.6 %collective-permute-start.21 = (f32[8,2304]{1,0:T(8,128)S(1)}, f32[8,2304]{1,0:T(8,128)S(1)}, u32[]{:S(2)}, u32[]{:S(2)}) collective-permute-start(f32[8,2304]{1,0:T(8,128)S(1)} %gate_sum.7.tie.first), channel_id=1, source_target_pairs={{0,128},{64,192},{128,0},{192,64},{1,129},{65,193},{129,1},{193,65... | collective-permute-start | bytes 221192 | tf_op jit(solution)/shard_map/gate_x/ppermute | solution.py:60
  93.2 2.5 %collective-permute-done.21.third = f32[8,2304]{1,0:T(8,128)S(1)} collective-permute-done((f32[8,2304]{1,0:T(8,128)S(1)}, f32[8,2304]{1,0:T(8,128)S(1)}, u32[]{:S(2)}, u32[]{:S(2)}) %collective-permute-start.21) | collective-permute-done | bytes 73760 | tf_op jit(solution)/shard_map/gate_x/ppermute | solution.py:60
  95.7 1.9 %collective-permute-done.22.fourth = f32[8,2304]{1,0:T(8,128)S(1)} collective-permute-done((f32[8,2304]{1,0:T(8,128)S(1)}, f32[8,2304]{1,0:T(8,128)S(1)}, u32[]{:S(2)}, u32[]{:S(2)}) %collective-permute-start.22) | collective-permute-done | bytes 73760 | tf_op jit(solution)/shard_map/gate_x/ppermute | solution.py:60
  97.6 1.3 %far_products_last.1.refs_1_.tie = bf16[256,256]{1,0:T(8,128)(2,1)S(1)} custom-call(s32[5]{0:T(128)S(1)} %stack.23.at, bf16[128,4608]{1,0:T(8,128)(2,1)S(1)} %fence.9.three.more, bf16[128,4608]{1,0:T(8,128)(2,1)S(1)} %collective-permute-done.24.three_s.more_s, bf16[4,128,128]{2,1,0:T(8,128)(2,1)S(1)} %copy-done.20, bf16[4,128,128]{2,1,0:T(8,128)(2,1)S(1)} %copy-done.12, ...), custom_call_target="tpu_custom_call" | custom-call | flops 620756992 | bytes 3637248 | tf_op jit(solution)/shard_map/far_products_last/pallas_call | solution.py:398
  99.0 1.2 %collective-permute-start.30 = (bf16[256,256]{1,0:T(8,128)(2,1)S(1)}, bf16[256,256]{1,0:T(8,128)(2,1)S(1)}, u32[]{:S(2)}, u32[]{:S(2)}) collective-permute-start(bf16[256,256]{1,0:T(8,128)(2,1)S(1)} %far_products_last.1.refs_1_.tie), channel_id=1, source_target_pairs={{0,2},{2,0},{1,3},{3,1},{4,6},{6,4},{5,7},{7,5},{8,10},{10,8},{9,1... | collective-permute-start | bytes 393224 | tf_op jit(solution)/shard_map/out_z_last/ppermute | solution.py:60
  101.0 3.1 %collective-permute-start.27 = (f32[8,2304]{1,0:T(8,128)S(1)}, f32[8,2304]{1,0:T(8,128)S(1)}, u32[]{:S(2)}, u32[]{:S(2)}) collective-permute-start(f32[8,2304]{1,0:T(8,128)S(1)} %fence.10.first), channel_id=1, source_target_pairs={{0,12},{4,8},{8,4},{12,0},{1,13},{5,9},{9,5},{13,1},{2,14},{6,10},... | collective-permute-start | bytes 221192 | tf_op jit(solution)/shard_map/gate_y/ppermute | solution.py:60
  104.1 2.0 %own_products.3.refs_2_.rest = bf16[2,256,256]{2,1,0:T(8,128)(2,1)S(1)} custom-call(s32[5]{0:T(128)S(1)} %stack.23.at, bf16[128,4608]{1,0:T(8,128)(2,1)S(1)} %fence.8.two.near, bf16[128,4608]{1,0:T(8,128)(2,1)S(1)} %collective-permute-done.18.refs_0_.two_s.near_s, bf16[128,4608]{1,0:T(8,128)(2,1)S(1)} %fence.9.three.more, ...), custom_call_target="tpu_custom_call" | custom-call | flops 1241513984 | bytes 7274496 | tf_op jit(solution)/shard_map/own_products/pallas_call | solution.py:316
  106.1 1.1 collective-permute-done.27.fourth
  107.2 1.9 %collective-permute-start.29 = (f32[8,2304]{1,0:T(8,128)S(1)}, f32[8,2304]{1,0:T(8,128)S(1)}, u32[]{:S(2)}, u32[]{:S(2)}) collective-permute-start(f32[8,2304]{1,0:T(8,128)S(1)} %fence.11), channel_id=1, source_target_pairs={{0,1},{1,0},{2,3},{3,2},{4,5},{5,4},{6,7},{7,6},{8,9},{9,8},{10,11... | collective-permute-start | bytes 221192 | tf_op jit(solution)/shard_map/gate_core_back/ppermute | solution.py:60
  109.1 7.6 %collective-permute-done.30.last = bf16[256,256]{1,0:T(8,128)(2,1)S(1)} collective-permute-done((bf16[256,256]{1,0:T(8,128)(2,1)S(1)}, bf16[256,256]{1,0:T(8,128)(2,1)S(1)}, u32[]{:S(2)}, u32[]{:S(2)}) %collective-permute-start.30) | collective-permute-done | bytes 131104 | tf_op jit(solution)/shard_map/out_z_last/ppermute | solution.py:60
  116.7 1.6 %place.1 = bf16[4,2,2,128,256]{4,3,2,1,0:T(8,128)(2,1)} custom-call(s32[5]{0:T(128)S(1)} %stack.23.at, bf16[2,256,256]{2,1,0:T(8,128)(2,1)S(1)} %copy-done.18, bf16[2,256,256]{2,1,0:T(8,128)(2,1)S(1)} %own_products.3.refs_2_.rest, bf16[3,256,256]{2,1,0:T(8,128)(2,1)S(1)} %collective-permute-done.28.refs_1_.got, bf16[256,256]{1,0:T(8,128)(2,1)S(1)} %collective-permute-done.30.last), custom_call_target="tpu_custom_call" | custom-call | tf_op jit(solution)/shard_map/place/pallas_call | solution.py:420
  (96 shorter events, 12.1 us)
Async XLA Ops:
  0.6 36.3 %collective-permute-start.4 = (bf16[128,4608]{1,0:T(8,128)(2,1)}, bf16[128,4608]{1,0:T(8,128)(2,1)S(1)}, u32[]{:S(2)}, u32[]{:S(2)}) collective-permute-start(bf16[128,4608]{1,0:T(8,128)(2,1)} %own.1), channel_id=1, source_target_pairs={{0,1},{1,0},{2,3},{3,2},{4,5},{5,4},{6,7},{7,6},{8,9},{9,8},{10,11... | collective-permute-start | bytes 3538952 | tf_op jit(solution)/shard_map/tokens_core/ppermute | solution.py:60
  1.4 36.2 %collective-permute-start.8 = (bf16[128,4608]{1,0:T(8,128)(2,1)}, bf16[128,4608]{1,0:T(8,128)(2,1)}, u32[]{:S(2)}, u32[]{:S(2)}) collective-permute-start(bf16[128,4608]{1,0:T(8,128)(2,1)} %own.1), channel_id=1, source_target_pairs={{0,4},{1,13},{4,8},{5,1},{8,12},{9,5},{12,0},{13,9},{2,6},{3,15},{... | collective-permute-start | bytes 3538952 | tf_op jit(solution)/shard_map/tokens_y/ppermute | solution.py:27
  4.1 12.7 %copy-start.7 = (bf16[128,4608]{1,0:T(8,128)(2,1)S(1)}, bf16[128,4608]{1,0:T(8,128)(2,1)}, u32[]{:S(2)}) copy-start(bf16[128,4608]{1,0:T(8,128)(2,1)} %hidden.3) | copy-start | bytes 3538948
  4.1 12.7 %copy-start.4 = (bf16[128,4608]{1,0:T(8,128)(2,1)S(1)}, bf16[128,4608]{1,0:T(8,128)(2,1)}, u32[]{:S(2)}) copy-start(bf16[128,4608]{1,0:T(8,128)(2,1)} %own.1) | copy-start | bytes 3538948
  6.7 19.7 %collective-permute-start.5 = (bf16[32,4736]{1,0:T(8,128)(2,1)}, bf16[32,4736]{1,0:T(8,128)(2,1)}, u32[]{:S(2)}, u32[]{:S(2)}) collective-permute-start(bf16[32,4736]{1,0:T(8,128)(2,1)} %pad_maximum_fusion), channel_id=1, source_target_pairs={{0,2},{2,0},{1,3},{3,1},{4,6},{6,4},{5,7},{7,5},{8,10},{10,8},{9,1... | collective-permute-start | bytes 909320 | tf_op jit(solution)/shard_map/weight_z/ppermute | solution.py:60
  16.7 4.3 %collective-permute-start = (bf16[4,2,128,128]{3,2,1,0:T(8,128)(2,1)S(1)}, bf16[4,2,128,128]{3,2,1,0:T(8,128)(2,1)S(1)}, u32[]{:S(2)}, u32[]{:S(2)}) collective-permute-start(bf16[4,2,128,128]{3,2,1,0:T(8,128)(2,1)S(1)} %get-tuple-element.20), channel_id=1, source_target_pairs={{0,1},{1,0},{2,3},{3,2},{4,5},{5,4},{6,7},{7,6},{8,9},{9,8},{10,11... | collective-permute-start | bytes 786440 | tf_op jit(solution)/shard_map/act_core/ppermute | solution.py:60
  26.4 10.5 %collective-permute-start.6 = (bf16[32,4736]{1,0:T(8,128)(2,1)}, bf16[32,4736]{1,0:T(8,128)(2,1)S(1)}, u32[]{:S(2)}, u32[]{:S(2)}) collective-permute-start(bf16[32,4736]{1,0:T(8,128)(2,1)} %fence.6.mine), channel_id=1, source_target_pairs={{0,16},{16,0},{32,48},{48,32},{1,17},{17,1},{33,49},{49,33},{2,18}... | collective-permute-start | bytes 909320 | tf_op jit(solution)/shard_map/weight_zl/ppermute | solution.py:60
  27.8 4.5 %collective-permute-start.1 = (bf16[3,128,128]{2,1,0:T(8,128)(2,1)S(1)}, bf16[3,128,128]{2,1,0:T(8,128)(2,1)S(1)}, u32[]{:S(2)}, u32[]{:S(2)}) collective-permute-start(bf16[3,128,128]{2,1,0:T(8,128)(2,1)S(1)} %get-tuple-element.23), channel_id=1, source_target_pairs={{0,4},{4,0},{8,12},{12,8},{1,5},{5,1},{9,13},{13,9},{2,6},{6,2},{1... | collective-permute-start | bytes 294920 | tf_op jit(solution)/shard_map/act_y/ppermute | solution.py:60
  27.8 6.6 %collective-permute-start.2 = (bf16[3,128,128]{2,1,0:T(8,128)(2,1)S(1)}, bf16[3,128,128]{2,1,0:T(8,128)(2,1)S(1)}, u32[]{:S(2)}, u32[]{:S(2)}) collective-permute-start(bf16[3,128,128]{2,1,0:T(8,128)(2,1)S(1)} %get-tuple-element.24), channel_id=1, source_target_pairs={{0,8},{4,12},{8,0},{12,4},{1,9},{5,13},{9,1},{13,5},{2,10},{6,14},... | collective-permute-start | bytes 294920 | tf_op jit(solution)/shard_map/act_y/ppermute | solution.py:60
  32.3 4.7 %collective-permute-start.3 = (bf16[3,128,128]{2,1,0:T(8,128)(2,1)S(1)}, bf16[3,128,128]{2,1,0:T(8,128)(2,1)S(1)}, u32[]{:S(2)}, u32[]{:S(2)}) collective-permute-start(bf16[3,128,128]{2,1,0:T(8,128)(2,1)S(1)} %get-tuple-element.25), channel_id=1, source_target_pairs={{0,12},{4,8},{8,4},{12,0},{1,13},{5,9},{9,5},{13,1},{2,14},{6,10},... | collective-permute-start | bytes 294920 | tf_op jit(solution)/shard_map/act_y/ppermute | solution.py:60
  37.0 12.0 %copy-start.5 = (bf16[128,4608]{1,0:T(8,128)(2,1)S(1)}, bf16[128,4608]{1,0:T(8,128)(2,1)}, u32[]{:S(2)}) copy-start(bf16[128,4608]{1,0:T(8,128)(2,1)} %own.1) | copy-start | bytes 3538948
  37.6 11.4 %copy-start.19 = (bf16[4,128,128]{2,1,0:T(8,128)(2,1)}, bf16[4,128,128]{2,1,0:T(8,128)(2,1)S(1)}, u32[]{:S(2)}) copy-start(bf16[4,128,128]{2,1,0:T(8,128)(2,1)S(1)} %get-tuple-element.30.mixed) | copy-start | bytes 393220
  38.0 10.9 %copy-start = (bf16[256,4608]{1,0:T(8,128)(2,1)S(1)}, bf16[256,4608]{1,0:T(8,128)(2,1)}, u32[]{:S(2)}) copy-start(bf16[256,4608]{1,0:T(8,128)(2,1)} %weight.3) | copy-start | bytes 7077892
  38.1 10.9 %copy-start.2 = (bf16[128,4608]{1,0:T(8,128)(2,1)S(1)}, bf16[128,4608]{1,0:T(8,128)(2,1)}, u32[]{:S(2)}) copy-start(bf16[128,4608]{1,0:T(8,128)(2,1)} %copy-done.1) | copy-start | bytes 3538948
  38.1 11.0 %copy-start.24 = (bf16[256,128]{1,0:T(8,128)(2,1)S(1)}, bf16[256,128]{1,0:T(8,128)(2,1)}, u32[]{:S(2)}) copy-start(bf16[256,128]{1,0:T(8,128)(2,1)} %down.5) | copy-start | bytes 196612
  38.1 10.9 %collective-permute-start.9 = (bf16[128,4608]{1,0:T(8,128)(2,1)}, bf16[128,4608]{1,0:T(8,128)(2,1)S(1)}, u32[]{:S(2)}, u32[]{:S(2)}) collective-permute-start(bf16[128,4608]{1,0:T(8,128)(2,1)} %fence.7.more.one), channel_id=1, source_target_pairs={{0,1},{1,0},{2,3},{3,2},{4,5},{5,4},{6,7},{7,6},{8,9},{9,8},{10,11... | collective-permute-start | bytes 3538952 | tf_op jit(solution)/shard_map/tokens_core/ppermute | solution.py:60
  40.2 25.0 %collective-permute-start.17 = (bf16[128,4608]{1,0:T(8,128)(2,1)}, bf16[128,4608]{1,0:T(8,128)(2,1)S(1)}, u32[]{:S(2)}, u32[]{:S(2)}) collective-permute-start(bf16[128,4608]{1,0:T(8,128)(2,1)} %fence.7.more.one), channel_id=1, source_target_pairs={{0,4},{1,13},{4,8},{5,1},{8,12},{9,5},{12,0},{13,9},{2,6},{3,15},{... | collective-permute-start | bytes 3538952 | tf_op jit(solution)/shard_map/tokens_y/ppermute | solution.py:27
  43.5 8.7 %copy-start.13 = (bf16[64,4736]{1,0:T(8,128)(2,1)}, bf16[64,4736]{1,0:T(8,128)(2,1)S(1)}, u32[]{:S(2)}) copy-start(bf16[64,4736]{1,0:T(8,128)(2,1)S(1)} %join.2.mine) | copy-start | bytes 1818628
  43.5 10.8 %collective-permute-start.12 = (bf16[64,4736]{1,0:T(8,128)(2,1)S(1)}, bf16[64,4736]{1,0:T(8,128)(2,1)S(1)}, u32[]{:S(2)}, u32[]{:S(2)}) collective-permute-start(bf16[64,4736]{1,0:T(8,128)(2,1)S(1)} %join.2.mine), channel_id=1, source_target_pairs={{0,64},{1,193},{64,0},{65,129},{128,192},{129,65},{192,128},{193,1... | collective-permute-start | bytes 1818632 | tf_op jit(solution)/shard_map/weight_x/ppermute | solution.py:33
  43.9 8.4 %copy-start.8 = (bf16[128,4608]{1,0:T(8,128)(2,1)S(1)}, bf16[128,4608]{1,0:T(8,128)(2,1)}, u32[]{:S(2)}) copy-start(bf16[128,4608]{1,0:T(8,128)(2,1)} %hidden.3) | copy-start | bytes 3538948
  43.9 5.1 %collective-permute-start.10 = (bf16[4,128,128]{2,1,0:T(8,128)(2,1)S(1)}, bf16[4,128,128]{2,1,0:T(8,128)(2,1)S(1)}, u32[]{:S(2)}, u32[]{:S(2)}) collective-permute-start(bf16[4,128,128]{2,1,0:T(8,128)(2,1)S(1)} %get-tuple-element.30.mixed), channel_id=1, source_target_pairs={{0,1},{1,0},{2,3},{3,2},{4,5},{5,4},{6,7},{7,6},{8,9},{9,8},{10,11... | collective-permute-start | bytes 393224 | tf_op jit(solution)/shard_map/mixed_core/ppermute | solution.py:60
  43.9 8.3 %collective-permute-start.7 = (bf16[128,128]{1,0:T(8,128)(2,1)S(1)}, bf16[128,128]{1,0:T(8,128)(2,1)S(1)}, u32[]{:S(2)}, u32[]{:S(2)}) collective-permute-start(bf16[128,128]{1,0:T(8,128)(2,1)S(1)} %get-tuple-element.27.refs_1_.tie), channel_id=1, source_target_pairs={{0,2},{2,0},{1,3},{3,1},{4,6},{6,4},{5,7},{7,5},{8,10},{10,8},{9,1... | collective-permute-start | bytes 98312 | tf_op jit(solution)/shard_map/act_z/ppermute | solution.py:60
  49.0 3.2 %copy-start.11 = (bf16[4,128,128]{2,1,0:T(8,128)(2,1)}, bf16[4,128,128]{2,1,0:T(8,128)(2,1)S(1)}, u32[]{:S(2)}) copy-start(bf16[4,128,128]{2,1,0:T(8,128)(2,1)S(1)} %collective-permute-done.10.mixed_s.refs_1_) | copy-start | bytes 393220
  52.2 3.7 %copy-start.17 = (bf16[2,256,256]{2,1,0:T(8,128)(2,1)}, bf16[2,256,256]{2,1,0:T(8,128)(2,1)S(1)}, u32[]{:S(2)}) copy-start(bf16[2,256,256]{2,1,0:T(8,128)(2,1)S(1)} %own_products.2.tie.near) | copy-start | bytes 786436
  53.5 1.8 %collective-permute-start.11 = (f32[8,2304]{1,0:T(8,128)S(1)}, f32[8,2304]{1,0:T(8,128)S(1)}, u32[]{:S(2)}, u32[]{:S(2)}) collective-permute-start(f32[8,2304]{1,0:T(8,128)S(1)} %get-tuple-element.32), channel_id=1, source_target_pairs={{0,1},{1,0},{2,3},{3,2},{4,5},{5,4},{6,7},{7,6},{8,9},{9,8},{10,11... | collective-permute-start | bytes 221192 | tf_op jit(solution)/shard_map/gate_core/ppermute | solution.py:60
  56.8 6.7 %collective-permute-start.13 = (f32[8,2304]{1,0:T(8,128)}, f32[8,2304]{1,0:T(8,128)}, u32[]{:S(2)}, u32[]{:S(2)}) collective-permute-start(f32[8,2304]{1,0:T(8,128)} %gate_sum.5.tie.first), channel_id=1, source_target_pairs={{0,16},{16,0},{32,48},{48,32},{1,17},{17,1},{33,49},{49,33},{2,18}... | collective-permute-start | bytes 221192 | tf_op jit(solution)/shard_map/gate_zl/ppermute | solution.py:60
  56.9 6.7 %collective-permute-start.14 = (f32[8,2304]{1,0:T(8,128)}, f32[8,2304]{1,0:T(8,128)}, u32[]{:S(2)}, u32[]{:S(2)}) collective-permute-start(f32[8,2304]{1,0:T(8,128)} %gate_sum.5.tie.first), channel_id=1, source_target_pairs={{0,32},{16,48},{32,0},{48,16},{1,33},{17,49},{33,1},{49,17},{2,34}... | collective-permute-start | bytes 221192 | tf_op jit(solution)/shard_map/gate_zl/ppermute | solution.py:60
  58.6 5.7 %collective-permute-start.15 = (f32[8,2304]{1,0:T(8,128)}, f32[8,2304]{1,0:T(8,128)}, u32[]{:S(2)}, u32[]{:S(2)}) collective-permute-start(f32[8,2304]{1,0:T(8,128)} %gate_sum.5.tie.first), channel_id=1, source_target_pairs={{0,48},{16,32},{32,16},{48,0},{1,49},{17,33},{33,17},{49,1},{2,50}... | collective-permute-start | bytes 221192 | tf_op jit(solution)/shard_map/gate_zl/ppermute | solution.py:60
  62.5 15.8 %collective-permute-start.19 = (bf16[128,4736]{1,0:T(8,128)(2,1)S(1)}, bf16[128,4736]{1,0:T(8,128)(2,1)S(1)}, u32[]{:S(2)}, u32[]{:S(2)}) collective-permute-start(bf16[128,4736]{1,0:T(8,128)(2,1)S(1)} %join.3.refs_0_.mine), channel_id=1, source_target_pairs={{0,192},{1,65},{64,128},{65,1},{128,64},{129,193},{192,0},{193,129... | collective-permute-start | bytes 3637256 | tf_op jit(solution)/shard_map/weight_x/ppermute | solution.py:33
  65.3 13.1 %copy-start.10 = (bf16[128,4608]{1,0:T(8,128)(2,1)S(1)}, bf16[128,4608]{1,0:T(8,128)(2,1)}, u32[]{:S(2)}) copy-start(bf16[128,4608]{1,0:T(8,128)(2,1)} %copy-done.9) | copy-start | bytes 3538948
  65.3 13.1 %copy-start.3 = (bf16[128,4608]{1,0:T(8,128)(2,1)S(1)}, bf16[128,4608]{1,0:T(8,128)(2,1)}, u32[]{:S(2)}) copy-start(bf16[128,4608]{1,0:T(8,128)(2,1)} %copy-done.1) | copy-start | bytes 3538948
  65.3 13.1 %copy-start.6 = (bf16[128,4608]{1,0:T(8,128)(2,1)S(1)}, bf16[128,4608]{1,0:T(8,128)(2,1)}, u32[]{:S(2)}) copy-start(bf16[128,4608]{1,0:T(8,128)(2,1)} %own.1) | copy-start | bytes 3538948
  65.3 13.1 %copy-start.20 = (bf16[4,128,128]{2,1,0:T(8,128)(2,1)S(1)}, bf16[4,128,128]{2,1,0:T(8,128)(2,1)}, u32[]{:S(2)}) copy-start(bf16[4,128,128]{2,1,0:T(8,128)(2,1)} %copy-done.19) | copy-start | bytes 393220
  65.3 13.0 %collective-permute-start.18 = (bf16[128,4608]{1,0:T(8,128)(2,1)S(1)}, bf16[128,4608]{1,0:T(8,128)(2,1)S(1)}, u32[]{:S(2)}, u32[]{:S(2)}) collective-permute-start(bf16[128,4608]{1,0:T(8,128)(2,1)S(1)} %fence.8.two.near), channel_id=1, source_target_pairs={{0,1},{1,0},{2,3},{3,2},{4,5},{5,4},{6,7},{7,6},{8,9},{9,8},{10,11... | collective-permute-start | bytes 3538952 | tf_op jit(solution)/shard_map/tokens_core/ppermute | solution.py:60
  67.9 15.3 %collective-permute-start.23 = (bf16[128,4608]{1,0:T(8,128)(2,1)S(1)}, bf16[128,4608]{1,0:T(8,128)(2,1)S(1)}, u32[]{:S(2)}, u32[]{:S(2)}) collective-permute-start(bf16[128,4608]{1,0:T(8,128)(2,1)S(1)} %fence.8.two.near), channel_id=1, source_target_pairs={{0,4},{1,13},{4,8},{5,1},{8,12},{9,5},{12,0},{13,9},{2,6},{3,15},{... | collective-permute-start | bytes 3538952 | tf_op jit(solution)/shard_map/tokens_y/ppermute | solution.py:27
  69.9 7.1 %collective-permute-start.16 = (f32[8,2304]{1,0:T(8,128)S(1)}, f32[8,2304]{1,0:T(8,128)S(1)}, u32[]{:S(2)}, u32[]{:S(2)}) collective-permute-start(f32[8,2304]{1,0:T(8,128)S(1)} %gate_sum.6.refs_1_.left), channel_id=1, source_target_pairs={{0,2},{2,0},{1,3},{3,1},{4,6},{6,4},{5,7},{7,5},{8,10},{10,8},{9,1... | collective-permute-start | bytes 221192 | tf_op jit(solution)/shard_map/gate_zh/ppermute | solution.py:60
  83.2 14.4 %collective-permute-start.24 = (bf16[128,4608]{1,0:T(8,128)(2,1)S(1)}, bf16[128,4608]{1,0:T(8,128)(2,1)S(1)}, u32[]{:S(2)}, u32[]{:S(2)}) collective-permute-start(bf16[128,4608]{1,0:T(8,128)(2,1)S(1)} %fence.9.three.more), channel_id=1, source_target_pairs={{0,1},{1,0},{2,3},{3,2},{4,5},{5,4},{6,7},{7,6},{8,9},{9,8},{10,11... | collective-permute-start | bytes 3538952 | tf_op jit(solution)/shard_map/tokens_core/ppermute | solution.py:60
  85.4 21.8 %collective-permute-start.28 = (bf16[3,256,256]{2,1,0:T(8,128)(2,1)S(1)}, bf16[3,256,256]{2,1,0:T(8,128)(2,1)S(1)}, u32[]{:S(2)}, u32[]{:S(2)}) collective-permute-start(bf16[3,256,256]{2,1,0:T(8,128)(2,1)S(1)} %get-tuple-element.33.refs_0_.refs_1_), channel_id=1, source_target_pairs={{0,2},{2,0},{1,3},{3,1},{4,6},{6,4},{5,7},{7,5},{8,10},{10,8},{9,1... | collective-permute-start | bytes 1179656 | tf_op jit(solution)/shard_map/out_z/ppermute | solution.py:60
  89.6 3.6 %collective-permute-start.20 = (f32[8,2304]{1,0:T(8,128)S(1)}, f32[8,2304]{1,0:T(8,128)S(1)}, u32[]{:S(2)}, u32[]{:S(2)}) collective-permute-start(f32[8,2304]{1,0:T(8,128)S(1)} %gate_sum.7.tie.first), channel_id=1, source_target_pairs={{0,64},{64,0},{128,192},{192,128},{1,65},{65,1},{129,193},{193,129... | collective-permute-start | bytes 221192 | tf_op jit(solution)/shard_map/gate_x/ppermute | solution.py:60
  90.5 5.2 %collective-permute-start.21 = (f32[8,2304]{1,0:T(8,128)S(1)}, f32[8,2304]{1,0:T(8,128)S(1)}, u32[]{:S(2)}, u32[]{:S(2)}) collective-permute-start(f32[8,2304]{1,0:T(8,128)S(1)} %gate_sum.7.tie.first), channel_id=1, source_target_pairs={{0,128},{64,192},{128,0},{192,64},{1,129},{65,193},{129,1},{193,65... | collective-permute-start | bytes 221192 | tf_op jit(solution)/shard_map/gate_x/ppermute | solution.py:60
  92.1 5.5 %collective-permute-start.22 = (f32[8,2304]{1,0:T(8,128)S(1)}, f32[8,2304]{1,0:T(8,128)S(1)}, u32[]{:S(2)}, u32[]{:S(2)}) collective-permute-start(f32[8,2304]{1,0:T(8,128)S(1)} %gate_sum.7.tie.first), channel_id=1, source_target_pairs={{0,192},{64,128},{128,64},{192,0},{1,193},{65,129},{129,65},{193,1... | collective-permute-start | bytes 221192 | tf_op jit(solution)/shard_map/gate_x/ppermute | solution.py:60
  97.6 6.4 %copy-start.25 = (bf16[256,128]{1,0:T(8,128)(2,1)S(1)}, bf16[256,128]{1,0:T(8,128)(2,1)}, u32[]{:S(2)}) copy-start(bf16[256,128]{1,0:T(8,128)(2,1)} %down.5) | copy-start | bytes 196612
  99.0 17.7 %collective-permute-start.30 = (bf16[256,256]{1,0:T(8,128)(2,1)S(1)}, bf16[256,256]{1,0:T(8,128)(2,1)S(1)}, u32[]{:S(2)}, u32[]{:S(2)}) collective-permute-start(bf16[256,256]{1,0:T(8,128)(2,1)S(1)} %far_products_last.1.refs_1_.tie), channel_id=1, source_target_pairs={{0,2},{2,0},{1,3},{3,1},{4,6},{6,4},{5,7},{7,5},{8,10},{10,8},{9,1... | collective-permute-start | bytes 393224 | tf_op jit(solution)/shard_map/out_z_last/ppermute | solution.py:60
  100.2 5.9 %collective-permute-start.25 = (f32[8,2304]{1,0:T(8,128)S(1)}, f32[8,2304]{1,0:T(8,128)S(1)}, u32[]{:S(2)}, u32[]{:S(2)}) collective-permute-start(f32[8,2304]{1,0:T(8,128)S(1)} %fence.10.first), channel_id=1, source_target_pairs={{0,4},{4,0},{8,12},{12,8},{1,5},{5,1},{9,13},{13,9},{2,6},{6,2},{1... | collective-permute-start | bytes 221192 | tf_op jit(solution)/shard_map/gate_y/ppermute | solution.py:60
  100.2 5.9 %collective-permute-start.26 = (f32[8,2304]{1,0:T(8,128)S(1)}, f32[8,2304]{1,0:T(8,128)S(1)}, u32[]{:S(2)}, u32[]{:S(2)}) collective-permute-start(f32[8,2304]{1,0:T(8,128)S(1)} %fence.10.first), channel_id=1, source_target_pairs={{0,8},{4,12},{8,0},{12,4},{1,9},{5,13},{9,1},{13,5},{2,10},{6,14},... | collective-permute-start | bytes 221192 | tf_op jit(solution)/shard_map/gate_y/ppermute | solution.py:60
  101.0 6.2 %collective-permute-start.27 = (f32[8,2304]{1,0:T(8,128)S(1)}, f32[8,2304]{1,0:T(8,128)S(1)}, u32[]{:S(2)}, u32[]{:S(2)}) collective-permute-start(f32[8,2304]{1,0:T(8,128)S(1)} %fence.10.first), channel_id=1, source_target_pairs={{0,12},{4,8},{8,4},{12,0},{1,13},{5,9},{9,5},{13,1},{2,14},{6,10},... | collective-permute-start | bytes 221192 | tf_op jit(solution)/shard_map/gate_y/ppermute | solution.py:60
  106.1 10.7 %copy-start.18 = (bf16[2,256,256]{2,1,0:T(8,128)(2,1)S(1)}, bf16[2,256,256]{2,1,0:T(8,128)(2,1)}, u32[]{:S(2)}) copy-start(bf16[2,256,256]{2,1,0:T(8,128)(2,1)} %copy-done.17) | copy-start | bytes 786436
  107.2 11.1 %collective-permute-start.29 = (f32[8,2304]{1,0:T(8,128)S(1)}, f32[8,2304]{1,0:T(8,128)S(1)}, u32[]{:S(2)}, u32[]{:S(2)}) collective-permute-start(f32[8,2304]{1,0:T(8,128)S(1)} %fence.11), channel_id=1, source_target_pairs={{0,1},{1,0},{2,3},{3,2},{4,5},{5,4},{6,7},{7,6},{8,9},{9,8},{10,11... | collective-permute-start | bytes 221192 | tf_op jit(solution)/shard_map/gate_core_back/ppermute | solution.py:60
  (10 other events, 13.3 us)

commit v7 on v6

--- a/solution.py
+++ b/solution.py
@@ -141,7 +141,7 @@
         all_mixed[jnp.bitwise_xor(y, mask)] = ref[2]
 
 
-def gate_kernel(at, keep, got, back, gates, hidden, tie, result, give):
+def gate_kernel(at, keep, got, back, gates, hidden, tie, tie_too, result, give):
     stacked = keep.shape[1]
     adapters = gates.shape[0]
     half = result.shape[1]
@@ -179,7 +179,7 @@
     out[...] = value.astype(out.dtype)
 
 
-def far_kernel(at, own, own_s, one, one_s, two, two_s, mixed, mixed_s, mine, got, tie, out, weight, down):
+def far_kernel(at, own, own_s, one, one_s, mixed, mixed_s, mine, got, tie, out, weight, down):
     width = weight.shape[1]
     rows = mine.shape[0]
     block = at[4] // 2
@@ -187,31 +187,26 @@
         place = pl.ds(pl.multiple_of(number * rows, rows), rows)
         weight[place, :] = ref[:, :width]
         down[place, :] = ref[:, width:]
-    for steps, group in enumerate(((own, own_s), (one, one_s), (two, two_s))):
+    for steps, group in enumerate(((own, own_s), (one, one_s))):
         rows_product(at, steps, group, (mixed, mixed_s), weight, down, out.at[steps])
 
 
-def far_last_kernel(at, three, three_s, mixed, mixed_s, weight, down, out):
-    rows_product(at, 3, (three, three_s), (mixed, mixed_s), weight, down, out)
-
-
-def own_kernel(first, at, near, near_s, more, more_s, mixed, mixed_s, weight, down, tie, out):
+def product_kernel(first, at, near, near_s, more, more_s, mixed, mixed_s, weight, down, tie, out):
     for number, group in enumerate(((near, near_s), (more, more_s))):
         rows_product(at, first + number, group, (mixed, mixed_s), weight, down, out.at[number])
 
 
-def place_kernel(at, near, rest, got, last, out, sems):
+def place_kernel(at, near, rest, far_near, far_rest, out, sems):
     y, zh, c = at[1], at[2], at[3]
     tokens = out.shape[3]
     copies = []
     for steps in range(4):
-        own = near.at[steps] if steps < 2 else rest.at[steps - 2]
-        other = got.at[steps] if steps < 3 else last
+        own, other = (near, far_near) if steps < 2 else (rest, far_rest)
         for ref, side in ((own, zh), (other, 1 - zh)):
             for half, core in ((0, c), (1, 1 - c)):
                 copies.append(
                     pltpu.make_async_copy(
-                        ref.at[pl.ds(half * tokens, tokens)],
+                        ref.at[steps % 2, pl.ds(half * tokens, tokens)],
                         out.at[back_at(y, core, steps), side, core],
                         sems.at[len(copies)],
                     )
@@ -298,13 +293,10 @@
         ],
         compiler_params=SMALL,
         name="rank_sum_y",
-    )(at, rest, first, second, third, mixed, own_s, z_got)
+    )(at, rest, first, second, third, mixed, own_s, far_piece)
     (one,) = fence((one,), give)
     with jax.named_scope("tokens_y"):
         two = ring(one, "y")
-    far_quarter = join(zl % 2, far_piece, z_got, give)
-    with jax.named_scope("weight_x"):
-        w_one = pairs(far_quarter, "x", True)
     with jax.named_scope("act_z"):
         message = swap(give, "zh", 1)
     with jax.named_scope("mixed_core"):
@@ -312,27 +304,30 @@
     with jax.named_scope("tokens_core"):
         one_s = swap(one, "c", 1)
 
-    def own_products(first, near, near_s, more, more_s, tie):
+    def products(name, first, near, near_s, more, more_s, weights, downs, tie):
         return pl.pallas_call(
-            functools.partial(own_kernel, first),
+            functools.partial(product_kernel, first),
             in_specs=[SMEM] + [VMEM] * 8 + [ANY],
             out_specs=VMEM,
             out_shape=shaped((2, 2 * tokens, features), BF16),
             compiler_params=MIDDLE,
             cost_estimate=cost(8 * tokens * depth * features, 12 * tokens * depth),
-            name="own_products",
-        )(at, near, near_s, more, more_s, all_mixed, mixed_s, weight, down, tie)
-
-    own_near = own_products(0, grad, own_s, one, one_s, give)
+            name=name,
+        )(at, near, near_s, more, more_s, all_mixed, mixed_s, weights, downs, tie)
+
+    own_near = products("own_near", 0, grad, own_s, one, one_s, weight, down, give)
+    far_quarter = join(zl % 2, far_piece, z_got, message)
+    with jax.named_scope("weight_x"):
+        w_one = pairs(far_quarter, "x", True)
 
     total, give = pl.pallas_call(
         gate_kernel,
-        in_specs=[SMEM] + [VMEM] * 5 + [ANY],
+        in_specs=[SMEM] + [VMEM] * 5 + [ANY] * 2,
         out_specs=[VMEM, VMEM],
         out_shape=[shaped((adapters, width // 2), F32)] * 2,
         compiler_params=SMALL,
         name="gate_products",
-    )(at, keep, message, back, gates, hidden, own_near)
+    )(at, keep, message, back, gates, hidden, own_near, far_quarter)
 
     def add(left, right, *ties):
         return pl.pallas_call(
@@ -361,56 +356,46 @@
 
     with jax.named_scope("gate_core"):
         got = swap(give, "c", 1)
-    total = add(total, got, w_one)
+    total = add(total, got)
+    total = step(total, "x", w_one)
     w_mine = join(number % 2, far_quarter, w_one, total)
     with jax.named_scope("weight_x"):
         w_got = pairs(w_mine, "x", False)
-    total = step(total, "zl", w_mine, mixed_s)
+    total = step(total, "y", w_mine)
     (two,) = fence((two,), total)
     with jax.named_scope("tokens_y"):
         three = ring(two, "y")
-    with jax.named_scope("gate_zh"):
-        got = swap(total, "zh", 1)
     with jax.named_scope("tokens_core"):
         two_s = swap(two, "c", 1)
-    total = add(total, got, two_s, w_got)
-    near = (grad, own_s, one, one_s, two, two_s)
-    far, far_weight, far_down = pl.pallas_call(
+    total = step(total, "zl", two_s, w_got)
+
+    far_near, far_weight, far_down = pl.pallas_call(
         far_kernel,
-        in_specs=[SMEM] + [VMEM] * 10 + [ANY],
+        in_specs=[SMEM] + [VMEM] * 8 + [ANY],
         out_specs=[VMEM] * 3,
         out_shape=[
-            shaped((3, 2 * tokens, features), BF16),
+            shaped((2, 2 * tokens, features), BF16),
             shaped((features, width), BF16),
             shaped((features, stacked), BF16),
         ],
         compiler_params=MIDDLE,
-        cost_estimate=cost(12 * tokens * depth * features, 18 * tokens * depth),
-        name="far_products",
-    )(at, *near, all_mixed, mixed_s, w_mine, w_got, total)
-    (three,) = fence((three,), far)
+        cost_estimate=cost(8 * tokens * depth * features, 12 * tokens * depth),
+        name="far_near",
+    )(at, grad, own_s, one, one_s, all_mixed, mixed_s, w_mine, w_got, total)
+    with jax.named_scope("out_z"):
+        got_near = swap(far_near, "zh", 1)
+    (total,) = fence((total,), far_near)
+    with jax.named_scope("gate_zh"):
+        got = swap(total, "zh", 1)
+    (three,) = fence((three,), total)
     with jax.named_scope("tokens_core"):
         three_s = swap(three, "c", 1)
-    total = step(total, "x", far)
-    with jax.named_scope("out_z"):
-        far_got = swap(far, "zh", 1)
-
-    last = pl.pallas_call(
-        far_last_kernel,
-        in_specs=[SMEM] + [VMEM] * 6,
-        out_specs=VMEM,
-        out_shape=shaped((2 * tokens, features), BF16),
-        cost_estimate=cost(4 * tokens * depth * features, 6 * tokens * depth),
-        compiler_params=MIDDLE,
-        name="far_products_last",
-    )(at, three, three_s, all_mixed, mixed_s, far_weight, far_down)
-    with jax.named_scope("out_z_last"):
-        last_got = swap(last, "zh", 1)
-
-    (total,) = fence((total,), last)
-    total = step(total, "y")
-    own_rest = own_products(2, two, two_s, three, three_s, last)
-    (total,) = fence((total,), far_got, own_rest)
+    far_rest = products("far_rest", 2, two, two_s, three, three_s, far_weight, far_down, far_near)
+    with jax.named_scope("out_z_rest"):
+        got_rest = swap(far_rest, "zh", 1)
+    own_rest = products("own_rest", 2, two, two_s, three, three_s, weight, down, got_near)
+
+    total = add(total, got, three_s)
     with jax.named_scope("gate_core_back"):
         other = swap(total, "c", 1)
     gate_grad = jnp.where(
@@ -425,7 +410,7 @@
         scratch_shapes=[pltpu.SemaphoreType.DMA((16,))],
         compiler_params=MIDDLE,
         name="place",
-    )(at, own_near, own_rest, far_got, last_got)
+    )(at, own_near, own_rest, got_near, got_rest)
     return gate_grad, out.reshape(16 * tokens, features)
 
 

time: 120 us -> 134 us (1.12)
  the two profiles are of different devices: /device:TPU:5 before, /device:TPU:1 now
where the time goes in v7:
time: 134 us; the launch traced here: 133 us
  starting transfers between devices  53.1 us (40%)
  waiting for transfers between devices  48 us (36%)
  Pallas kernels  19.8 us (15%)
  local copies, waits for them, and re-layouts  9.66 us (7%)
  other arithmetic  1.41 us (1%)
    ppermute x26, waiting for transfers between devices, swap(): return lax.ppermute(value, axis, [(i, i ^ mask) for i in range(size)])  47.7 us
    ppermute x26, starting transfers between devices, swap(): return lax.ppermute(value, axis, [(i, i ^ mask) for i in range(size)])  45.9 us
    unnamed x54, local copies, waits for them, and re-layouts  7.74 us
    pallas_call x3, Pallas kernels, products(): pl.pallas_call(functools.partial(product_kernel, first), in_specs=[SMEM]...  7.11 us
    ppermute x3, starting transfers between devices, ring(): return lax.ppermute(value, (axis, 'c'), pairs)  4.53 us
    pallas_call x1, Pallas kernels, on_device(): pl.pallas_call(far_kernel, in_specs=[SMEM] + [VMEM] * 8 + [ANY], out_spec...  2.88 us
  transfers between devices with their start and end apart: 31, of which 16 were waited for; matrix products, arithmetic and copies ran while one was open for 3% of the time, Pallas kernels for 14%

profile of v7, /device:TPU:1, one launch (start us, length us, event | category | flops | bytes accessed | tf_op | source)
XLA Modules:
  0.0 133.2 jit_solution(15289872849917322448)
XLA Ops:
  0.6 3.3 %collective-permute-start.4 = (bf16[128,4608]{1,0:T(8,128)(2,1)}, bf16[128,4608]{1,0:T(8,128)(2,1)S(1)}, u32[]{:S(2)}, u32[]{:S(2)}) collective-permute-start(bf16[128,4608]{1,0:T(8,128)(2,1)} %own.1), channel_id=1, source_target_pairs={{0,1},{1,0},{2,3},{3,2},{4,5},{5,4},{6,7},{7,6},{8,9},{9,8},{10,11... | collective-permute-start | bytes 3538952 | tf_op jit(solution)/shard_map/tokens_core/ppermute | solution.py:60
  4.0 1.0 collective-permute-start.7
  5.0 1.1 constant_dynamic-slice_fusion.1
  7.5 6.9 %collective-permute-start.5 = (bf16[32,4736]{1,0:T(8,128)(2,1)}, bf16[32,4736]{1,0:T(8,128)(2,1)}, u32[]{:S(2)}, u32[]{:S(2)}) collective-permute-start(bf16[32,4736]{1,0:T(8,128)(2,1)} %pad_maximum_fusion), channel_id=1, source_target_pairs={{0,2},{2,0},{1,3},{3,1},{4,6},{6,4},{5,7},{7,5},{8,10},{10,8},{9,1... | collective-permute-start | bytes 909320 | tf_op jit(solution)/shard_map/weight_z/ppermute | solution.py:60
  14.5 1.2 copy-done.22
  16.6 1.0 rank_products.1
  17.7 1.3 copy-done.21
  19.0 0.9 copy-done.26
  19.8 2.0 %token_values.1 = (bf16[128,128]{1,0:T(8,128)(2,1)S(1)}, f32[8,128]{1,0:T(8,128)S(1)}, f32[128,128]{1,0:T(8,128)S(1)}) custom-call(s32[5]{0:T(128)S(1)} %stack.23.at, bf16[128,4608]{1,0:T(8,128)(2,1)S(1)} %copy-done.9, bf16[128,4608]{1,0:T(8,128)(2,1)S(1)} %copy-done.4, bf16[128,4608]{1,0:T(8,128)(2,1)S(1)} %copy-done.21, bf16[8,4608]{1,0:T(8,128)(2,1)S(1)} %copy-done.26), custom_call_target="tpu_custom_call" | custom-call | flops 452984832 | bytes 7077888 | tf_op jit(solution)/shard_map/token_values/pallas_call | solution.py:257
  23.0 1.4 %collective-permute-start.2 = (bf16[3,128,128]{2,1,0:T(8,128)(2,1)S(1)}, bf16[3,128,128]{2,1,0:T(8,128)(2,1)S(1)}, u32[]{:S(2)}, u32[]{:S(2)}) collective-permute-start(bf16[3,128,128]{2,1,0:T(8,128)(2,1)S(1)} %get-tuple-element.24), channel_id=1, source_target_pairs={{0,8},{4,12},{8,0},{12,4},{1,9},{5,13},{9,1},{13,5},{2,10},{6,14},... | collective-permute-start | bytes 294920 | tf_op jit(solution)/shard_map/act_y/ppermute | solution.py:60
  24.5 2.8 %collective-permute-done.5.refs_0_ = bf16[32,4736]{1,0:T(8,128)(2,1)} collective-permute-done((bf16[32,4736]{1,0:T(8,128)(2,1)}, bf16[32,4736]{1,0:T(8,128)(2,1)}, u32[]{:S(2)}, u32[]{:S(2)}) %collective-permute-start.5) | collective-permute-done | bytes 303136 | tf_op jit(solution)/shard_map/weight_z/ppermute | solution.py:60
  27.3 2.0 %collective-permute-done.2.second = bf16[3,128,128]{2,1,0:T(8,128)(2,1)S(1)} collective-permute-done((bf16[3,128,128]{2,1,0:T(8,128)(2,1)S(1)}, bf16[3,128,128]{2,1,0:T(8,128)(2,1)S(1)}, u32[]{:S(2)}, u32[]{:S(2)}) %collective-permute-start.2) | collective-permute-done | bytes 98336 | tf_op jit(solution)/shard_map/act_y/ppermute | solution.py:60
  29.3 2.6 %collective-permute-done.3.third = bf16[3,128,128]{2,1,0:T(8,128)(2,1)S(1)} collective-permute-done((bf16[3,128,128]{2,1,0:T(8,128)(2,1)S(1)}, bf16[3,128,128]{2,1,0:T(8,128)(2,1)S(1)}, u32[]{:S(2)}, u32[]{:S(2)}) %collective-permute-start.3) | collective-permute-done | bytes 98336 | tf_op jit(solution)/shard_map/act_y/ppermute | solution.py:60
  33.0 2.4 %collective-permute-start.22 = (bf16[128,4608]{1,0:T(8,128)(2,1)}, bf16[128,4608]{1,0:T(8,128)(2,1)S(1)}, u32[]{:S(2)}, u32[]{:S(2)}) collective-permute-start(bf16[128,4608]{1,0:T(8,128)(2,1)} %fence.6.more.one), channel_id=1, source_target_pairs={{0,4},{1,13},{4,8},{5,1},{8,12},{9,5},{12,0},{13,9},{2,6},{3,15},{... | collective-permute-start | bytes 3538952 | tf_op jit(solution)/shard_map/tokens_y/ppermute | solution.py:27
  35.4 2.2 %collective-permute-start.10 = (bf16[32,4736]{1,0:T(8,128)(2,1)}, bf16[32,4736]{1,0:T(8,128)(2,1)S(1)}, u32[]{:S(2)}, u32[]{:S(2)}) collective-permute-start(bf16[32,4736]{1,0:T(8,128)(2,1)} %fence.5.tie_too.mine), channel_id=1, source_target_pairs={{0,16},{16,0},{32,48},{48,32},{1,17},{17,1},{33,49},{49,33},{2,18}... | collective-permute-start | bytes 909320 | tf_op jit(solution)/shard_map/weight_zl/ppermute | solution.py:60
  37.7 5.2 %collective-permute-start.6 = (bf16[128,128]{1,0:T(8,128)(2,1)S(1)}, bf16[128,128]{1,0:T(8,128)(2,1)S(1)}, u32[]{:S(2)}, u32[]{:S(2)}) collective-permute-start(bf16[128,128]{1,0:T(8,128)(2,1)S(1)} %get-tuple-element.27.refs_1_.tie), channel_id=1, source_target_pairs={{0,2},{2,0},{1,3},{3,1},{4,6},{6,4},{5,7},{7,5},{8,10},{10,8},{9,1... | collective-permute-start | bytes 98312 | tf_op jit(solution)/shard_map/act_z/ppermute | solution.py:60
  42.9 1.9 %collective-permute-done.10.got = bf16[32,4736]{1,0:T(8,128)(2,1)S(1)} collective-permute-done((bf16[32,4736]{1,0:T(8,128)(2,1)}, bf16[32,4736]{1,0:T(8,128)(2,1)S(1)}, u32[]{:S(2)}, u32[]{:S(2)}) %collective-permute-start.10) | collective-permute-done | bytes 303136 | tf_op jit(solution)/shard_map/weight_zl/ppermute | solution.py:60
  44.8 6.6 %collective-permute-done.6.tie.got = bf16[128,128]{1,0:T(8,128)(2,1)S(1)} collective-permute-done((bf16[128,128]{1,0:T(8,128)(2,1)S(1)}, bf16[128,128]{1,0:T(8,128)(2,1)S(1)}, u32[]{:S(2)}, u32[]{:S(2)}) %collective-permute-start.6) | collective-permute-done | bytes 32800 | tf_op jit(solution)/shard_map/act_z/ppermute | solution.py:60
  51.4 1.0 join.2.tie_too.mine
  52.4 2.6 %collective-permute-start.15 = (bf16[64,4736]{1,0:T(8,128)(2,1)S(1)}, bf16[64,4736]{1,0:T(8,128)(2,1)S(1)}, u32[]{:S(2)}, u32[]{:S(2)}) collective-permute-start(bf16[64,4736]{1,0:T(8,128)(2,1)S(1)} %join.2.tie_too.mine), channel_id=1, source_target_pairs={{0,64},{1,193},{64,0},{65,129},{128,192},{129,65},{192,128},{193,1... | collective-permute-start | bytes 1818632 | tf_op jit(solution)/shard_map/weight_x/ppermute | solution.py:33
  55.0 1.3 %collective-permute-done.9.mixed_s = bf16[4,128,128]{2,1,0:T(8,128)(2,1)S(1)} collective-permute-done((bf16[4,128,128]{2,1,0:T(8,128)(2,1)S(1)}, bf16[4,128,128]{2,1,0:T(8,128)(2,1)S(1)}, u32[]{:S(2)}, u32[]{:S(2)}) %collective-permute-start.9) | collective-permute-done | bytes 131104 | tf_op jit(solution)/shard_map/mixed_core/ppermute | solution.py:60
  56.4 3.1 %own_near.1.tie.near = bf16[2,256,256]{2,1,0:T(8,128)(2,1)S(1)} custom-call(s32[5]{0:T(128)S(1)} %stack.23.at, bf16[128,4608]{1,0:T(8,128)(2,1)S(1)} %copy-done.5, bf16[128,4608]{1,0:T(8,128)(2,1)S(1)} %copy-done.2, bf16[128,4608]{1,0:T(8,128)(2,1)} %fence.6.more.one, bf16[128,4608]{1,0:T(8,128)(2,1)S(1)} %collective-permute-done.8.more_s.one_s, ...), custom_call_target="tpu_custom_call" | custom-call | flops 1241513984 | bytes 7274496 | tf_op jit(solution)/shard_map/own_near/pallas_call | solution.py:308
  59.6 1.2 gate_products.1
  61.1 1.1 collective-permute-done.11.right
  62.3 1.9 %collective-permute-start.13 = (f32[8,2304]{1,0:T(8,128)S(1)}, f32[8,2304]{1,0:T(8,128)S(1)}, u32[]{:S(2)}, u32[]{:S(2)}) collective-permute-start(f32[8,2304]{1,0:T(8,128)S(1)} %gate_sum.5.first), channel_id=1, source_target_pairs={{0,128},{64,192},{128,0},{192,64},{1,129},{65,193},{129,1},{193,65... | collective-permute-start | bytes 221192 | tf_op jit(solution)/shard_map/gate_x/ppermute | solution.py:60
  64.2 2.0 %collective-permute-start.14 = (f32[8,2304]{1,0:T(8,128)S(1)}, f32[8,2304]{1,0:T(8,128)S(1)}, u32[]{:S(2)}, u32[]{:S(2)}) collective-permute-start(f32[8,2304]{1,0:T(8,128)S(1)} %gate_sum.5.first), channel_id=1, source_target_pairs={{0,192},{64,128},{128,64},{192,0},{1,193},{65,129},{129,65},{193,1... | collective-permute-start | bytes 221192 | tf_op jit(solution)/shard_map/gate_x/ppermute | solution.py:60
  66.2 2.2 %collective-permute-done.13.third = f32[8,2304]{1,0:T(8,128)S(1)} collective-permute-done((f32[8,2304]{1,0:T(8,128)S(1)}, f32[8,2304]{1,0:T(8,128)S(1)}, u32[]{:S(2)}, u32[]{:S(2)}) %collective-permute-start.13) | collective-permute-done | bytes 73760 | tf_op jit(solution)/shard_map/gate_x/ppermute | solution.py:60
  70.7 2.0 %collective-permute-start.17 = (f32[8,2304]{1,0:T(8,128)}, f32[8,2304]{1,0:T(8,128)}, u32[]{:S(2)}, u32[]{:S(2)}) collective-permute-start(f32[8,2304]{1,0:T(8,128)} %gate_sum.6.tie.first), channel_id=1, source_target_pairs={{0,8},{4,12},{8,0},{12,4},{1,9},{5,13},{9,1},{13,5},{2,10},{6,14},... | collective-permute-start | bytes 221192 | tf_op jit(solution)/shard_map/gate_y/ppermute | solution.py:60
  72.8 1.7 %collective-permute-start.18 = (f32[8,2304]{1,0:T(8,128)}, f32[8,2304]{1,0:T(8,128)}, u32[]{:S(2)}, u32[]{:S(2)}) collective-permute-start(f32[8,2304]{1,0:T(8,128)} %gate_sum.6.tie.first), channel_id=1, source_target_pairs={{0,12},{4,8},{8,4},{12,0},{1,13},{5,9},{9,5},{13,1},{2,14},{6,10},... | collective-permute-start | bytes 221192 | tf_op jit(solution)/shard_map/gate_y/ppermute | solution.py:60
  74.5 1.1 copy-done.8
  75.6 1.1 copy-done.14
  76.9 1.4 %collective-permute-done.18.fourth = f32[8,2304]{1,0:T(8,128)} collective-permute-done((f32[8,2304]{1,0:T(8,128)}, f32[8,2304]{1,0:T(8,128)}, u32[]{:S(2)}, u32[]{:S(2)}) %collective-permute-start.18) | collective-permute-done | bytes 73760 | tf_op jit(solution)/shard_map/gate_y/ppermute | solution.py:60
  78.3 1.0 gate_sum.7.refs_1_.first
  79.4 3.2 %collective-permute-start.23 = (bf16[128,4608]{1,0:T(8,128)(2,1)S(1)}, bf16[128,4608]{1,0:T(8,128)(2,1)S(1)}, u32[]{:S(2)}, u32[]{:S(2)}) collective-permute-start(bf16[128,4608]{1,0:T(8,128)(2,1)S(1)} %fence.7.near), channel_id=1, source_target_pairs={{0,1},{1,0},{2,3},{3,2},{4,5},{5,4},{6,7},{7,6},{8,9},{9,8},{10,11... | collective-permute-start | bytes 3538952 | tf_op jit(solution)/shard_map/tokens_core/ppermute | solution.py:60
  82.5 1.1 collective-permute-start.26
  83.7 1.3 collective-permute-start.20
  85.0 4.0 %collective-permute-done.19.second = f32[8,2304]{1,0:T(8,128)S(1)} collective-permute-done((f32[8,2304]{1,0:T(8,128)S(1)}, f32[8,2304]{1,0:T(8,128)S(1)}, u32[]{:S(2)}, u32[]{:S(2)}) %collective-permute-start.19) | collective-permute-done | bytes 73760 | tf_op jit(solution)/shard_map/gate_zl/ppermute | solution.py:60
  88.9 1.2 collective-permute-start.21
  90.2 4.4 %collective-permute-done.21.fourth = f32[8,2304]{1,0:T(8,128)S(1)} collective-permute-done((f32[8,2304]{1,0:T(8,128)S(1)}, f32[8,2304]{1,0:T(8,128)S(1)}, u32[]{:S(2)}, u32[]{:S(2)}) %collective-permute-start.21) | collective-permute-done | bytes 73760 | tf_op jit(solution)/shard_map/gate_zl/ppermute | solution.py:60
  94.7 2.9 %far_near.1 = (bf16[2,256,256]{2,1,0:T(8,128)(2,1)S(1)}, bf16[256,4608]{1,0:T(8,128)(2,1)S(1)}, bf16[256,128]{1,0:T(8,128)(2,1)S(1)}) custom-call(s32[5]{0:T(128)S(1)} %stack.23.at, bf16[128,4608]{1,0:T(8,128)(2,1)S(1)} %copy-done.6, bf16[128,4608]{1,0:T(8,128)(2,1)S(1)} %copy-done.3, bf16[128,4608]{1,0:T(8,128)(2,1)} %fence.6.more.one, ...), custom_call_target="tpu_custom_call" | custom-call | flops 1241513984 | bytes 7274496 | tf_op jit(solution)/shard_map/far_near/pallas_call | solution.py:372
  97.9 2.2 %collective-permute-start.27 = (bf16[128,4608]{1,0:T(8,128)(2,1)S(1)}, bf16[128,4608]{1,0:T(8,128)(2,1)S(1)}, u32[]{:S(2)}, u32[]{:S(2)}) collective-permute-start(bf16[128,4608]{1,0:T(8,128)(2,1)S(1)} %fence.9.more), channel_id=1, source_target_pairs={{0,1},{1,0},{2,3},{3,2},{4,5},{5,4},{6,7},{7,6},{8,9},{9,8},{10,11... | collective-permute-start | bytes 3538952 | tf_op jit(solution)/shard_map/tokens_core/ppermute | solution.py:60
  100.1 5.4 %collective-permute-start.25 = (f32[8,2304]{1,0:T(8,128)S(1)}, f32[8,2304]{1,0:T(8,128)S(1)}, u32[]{:S(2)}, u32[]{:S(2)}) collective-permute-start(f32[8,2304]{1,0:T(8,128)S(1)} %fence.8.refs_1_.left), channel_id=1, source_target_pairs={{0,2},{2,0},{1,3},{3,1},{4,6},{6,4},{5,7},{7,5},{8,10},{10,8},{9,1... | collective-permute-start | bytes 221192 | tf_op jit(solution)/shard_map/gate_zh/ppermute | solution.py:60
  105.5 2.0 %far_rest.1 = bf16[2,256,256]{2,1,0:T(8,128)(2,1)S(1)} custom-call(s32[5]{0:T(128)S(1)} %stack.23.at, bf16[128,4608]{1,0:T(8,128)(2,1)S(1)} %fence.7.near, bf16[128,4608]{1,0:T(8,128)(2,1)S(1)} %collective-permute-done.23.refs_0_.near_s, bf16[128,4608]{1,0:T(8,128)(2,1)S(1)} %fence.9.more, bf16[128,4608]{1,0:T(8,128)(2,1)S(1)} %collective-permute-done.27.refs_0_.more_s, ...), custom_call_target="tpu_custom_call" | custom-call | flops 1241513984 | bytes 7274496 | tf_op jit(solution)/shard_map/far_rest/pallas_call | solution.py:308
  107.6 11.8 %collective-permute-done.25.right = f32[8,2304]{1,0:T(8,128)S(1)} collective-permute-done((f32[8,2304]{1,0:T(8,128)S(1)}, f32[8,2304]{1,0:T(8,128)S(1)}, u32[]{:S(2)}, u32[]{:S(2)}) %collective-permute-start.25) | collective-permute-done | bytes 73760 | tf_op jit(solution)/shard_map/gate_zh/ppermute | solution.py:60
  119.4 4.8 %collective-permute-start.28 = (f32[8,2304]{1,0:T(8,128)S(1)}, f32[8,2304]{1,0:T(8,128)S(1)}, u32[]{:S(2)}, u32[]{:S(2)}) collective-permute-start(f32[8,2304]{1,0:T(8,128)S(1)} %gate_sum.9), channel_id=1, source_target_pairs={{0,1},{1,0},{2,3},{3,2},{4,5},{5,4},{6,7},{7,6},{8,9},{9,8},{10,11... | collective-permute-start | bytes 221192 | tf_op jit(solution)/shard_map/gate_core_back/ppermute | solution.py:60
  124.2 2.0 %own_rest.1.rest = bf16[2,256,256]{2,1,0:T(8,128)(2,1)S(1)} custom-call(s32[5]{0:T(128)S(1)} %stack.23.at, bf16[128,4608]{1,0:T(8,128)(2,1)S(1)} %fence.7.near, bf16[128,4608]{1,0:T(8,128)(2,1)S(1)} %collective-permute-done.23.refs_0_.near_s, bf16[128,4608]{1,0:T(8,128)(2,1)S(1)} %fence.9.more, bf16[128,4608]{1,0:T(8,128)(2,1)S(1)} %collective-permute-done.27.refs_0_.more_s, ...), custom_call_target="tpu_custom_call" | custom-call | flops 1241513984 | bytes 7274496 | tf_op jit(solution)/shard_map/own_rest/pallas_call | solution.py:308
  126.8 4.6 %collective-permute-done.30.far_rest = bf16[2,256,256]{2,1,0:T(8,128)(2,1)S(1)} collective-permute-done((bf16[2,256,256]{2,1,0:T(8,128)(2,1)S(1)}, bf16[2,256,256]{2,1,0:T(8,128)(2,1)S(1)}, u32[]{:S(2)}, u32[]{:S(2)}) %collective-permute-start.30) | collective-permute-done | bytes 262176 | tf_op jit(solution)/shard_map/out_z_rest/ppermute | solution.py:60
  131.4 1.6 %place.1 = bf16[4,2,2,128,256]{4,3,2,1,0:T(8,128)(2,1)} custom-call(s32[5]{0:T(128)S(1)} %stack.23.at, bf16[2,256,256]{2,1,0:T(8,128)(2,1)S(1)} %copy-done.16, bf16[2,256,256]{2,1,0:T(8,128)(2,1)S(1)} %own_rest.1.rest, bf16[2,256,256]{2,1,0:T(8,128)(2,1)S(1)} %collective-permute-done.29.tie.far_near, bf16[2,256,256]{2,1,0:T(8,128)(2,1)S(1)} %collective-permute-done.30.far_rest), custom_call_target="tpu_custom_call" | custom-call | tf_op jit(solution)/shard_map/place/pallas_call | solution.py:405
  (95 shorter events, 8.9 us)
Async XLA Ops:
  0.6 31.3 %collective-permute-start.4 = (bf16[128,4608]{1,0:T(8,128)(2,1)}, bf16[128,4608]{1,0:T(8,128)(2,1)S(1)}, u32[]{:S(2)}, u32[]{:S(2)}) collective-permute-start(bf16[128,4608]{1,0:T(8,128)(2,1)} %own.1), channel_id=1, source_target_pairs={{0,1},{1,0},{2,3},{3,2},{4,5},{5,4},{6,7},{7,6},{8,9},{9,8},{10,11... | collective-permute-start | bytes 3538952 | tf_op jit(solution)/shard_map/tokens_core/ppermute | solution.py:60
  4.0 28.6 %collective-permute-start.7 = (bf16[128,4608]{1,0:T(8,128)(2,1)}, bf16[128,4608]{1,0:T(8,128)(2,1)}, u32[]{:S(2)}, u32[]{:S(2)}) collective-permute-start(bf16[128,4608]{1,0:T(8,128)(2,1)} %own.1), channel_id=1, source_target_pairs={{0,4},{1,13},{4,8},{5,1},{8,12},{9,5},{12,0},{13,9},{2,6},{3,15},{... | collective-permute-start | bytes 3538952 | tf_op jit(solution)/shard_map/tokens_y/ppermute | solution.py:27
  5.0 12.7 %copy-start.9 = (bf16[128,4608]{1,0:T(8,128)(2,1)S(1)}, bf16[128,4608]{1,0:T(8,128)(2,1)}, u32[]{:S(2)}) copy-start(bf16[128,4608]{1,0:T(8,128)(2,1)} %hidden.3) | copy-start | bytes 3538948
  5.0 12.7 %copy-start.4 = (bf16[128,4608]{1,0:T(8,128)(2,1)S(1)}, bf16[128,4608]{1,0:T(8,128)(2,1)}, u32[]{:S(2)}) copy-start(bf16[128,4608]{1,0:T(8,128)(2,1)} %own.1) | copy-start | bytes 3538948
  7.5 19.7 %collective-permute-start.5 = (bf16[32,4736]{1,0:T(8,128)(2,1)}, bf16[32,4736]{1,0:T(8,128)(2,1)}, u32[]{:S(2)}, u32[]{:S(2)}) collective-permute-start(bf16[32,4736]{1,0:T(8,128)(2,1)} %pad_maximum_fusion), channel_id=1, source_target_pairs={{0,2},{2,0},{1,3},{3,1},{4,6},{6,4},{5,7},{7,5},{8,10},{10,8},{9,1... | collective-permute-start | bytes 909320 | tf_op jit(solution)/shard_map/weight_z/ppermute | solution.py:60
  17.6 4.3 %collective-permute-start = (bf16[4,2,128,128]{3,2,1,0:T(8,128)(2,1)S(1)}, bf16[4,2,128,128]{3,2,1,0:T(8,128)(2,1)S(1)}, u32[]{:S(2)}, u32[]{:S(2)}) collective-permute-start(bf16[4,2,128,128]{3,2,1,0:T(8,128)(2,1)S(1)} %get-tuple-element.20), channel_id=1, source_target_pairs={{0,1},{1,0},{2,3},{3,2},{4,5},{5,4},{6,7},{7,6},{8,9},{9,8},{10,11... | collective-permute-start | bytes 786440 | tf_op jit(solution)/shard_map/act_core/ppermute | solution.py:60
  22.5 4.8 %collective-permute-start.1 = (bf16[3,128,128]{2,1,0:T(8,128)(2,1)S(1)}, bf16[3,128,128]{2,1,0:T(8,128)(2,1)S(1)}, u32[]{:S(2)}, u32[]{:S(2)}) collective-permute-start(bf16[3,128,128]{2,1,0:T(8,128)(2,1)S(1)} %get-tuple-element.23), channel_id=1, source_target_pairs={{0,4},{4,0},{8,12},{12,8},{1,5},{5,1},{9,13},{13,9},{2,6},{6,2},{1... | collective-permute-start | bytes 294920 | tf_op jit(solution)/shard_map/act_y/ppermute | solution.py:60
  23.0 6.3 %collective-permute-start.2 = (bf16[3,128,128]{2,1,0:T(8,128)(2,1)S(1)}, bf16[3,128,128]{2,1,0:T(8,128)(2,1)S(1)}, u32[]{:S(2)}, u32[]{:S(2)}) collective-permute-start(bf16[3,128,128]{2,1,0:T(8,128)(2,1)S(1)} %get-tuple-element.24), channel_id=1, source_target_pairs={{0,8},{4,12},{8,0},{12,4},{1,9},{5,13},{9,1},{13,5},{2,10},{6,14},... | collective-permute-start | bytes 294920 | tf_op jit(solution)/shard_map/act_y/ppermute | solution.py:60
  27.3 4.7 %collective-permute-start.3 = (bf16[3,128,128]{2,1,0:T(8,128)(2,1)S(1)}, bf16[3,128,128]{2,1,0:T(8,128)(2,1)S(1)}, u32[]{:S(2)}, u32[]{:S(2)}) collective-permute-start(bf16[3,128,128]{2,1,0:T(8,128)(2,1)S(1)} %get-tuple-element.25), channel_id=1, source_target_pairs={{0,12},{4,8},{8,4},{12,0},{1,13},{5,9},{9,5},{13,1},{2,14},{6,10},... | collective-permute-start | bytes 294920 | tf_op jit(solution)/shard_map/act_y/ppermute | solution.py:60
  32.0 24.4 %copy-start.5 = (bf16[128,4608]{1,0:T(8,128)(2,1)S(1)}, bf16[128,4608]{1,0:T(8,128)(2,1)}, u32[]{:S(2)}) copy-start(bf16[128,4608]{1,0:T(8,128)(2,1)} %own.1) | copy-start | bytes 3538948
  32.5 23.8 %copy-start.17 = (bf16[4,128,128]{2,1,0:T(8,128)(2,1)}, bf16[4,128,128]{2,1,0:T(8,128)(2,1)S(1)}, u32[]{:S(2)}) copy-start(bf16[4,128,128]{2,1,0:T(8,128)(2,1)S(1)} %get-tuple-element.30.mixed) | copy-start | bytes 393220
  33.0 23.3 %copy-start = (bf16[256,4608]{1,0:T(8,128)(2,1)S(1)}, bf16[256,4608]{1,0:T(8,128)(2,1)}, u32[]{:S(2)}) copy-start(bf16[256,4608]{1,0:T(8,128)(2,1)} %weight.3) | copy-start | bytes 7077892
  33.0 23.4 %copy-start.2 = (bf16[128,4608]{1,0:T(8,128)(2,1)S(1)}, bf16[128,4608]{1,0:T(8,128)(2,1)}, u32[]{:S(2)}) copy-start(bf16[128,4608]{1,0:T(8,128)(2,1)} %copy-done.1) | copy-start | bytes 3538948
  33.0 23.4 %copy-start.24 = (bf16[256,128]{1,0:T(8,128)(2,1)S(1)}, bf16[256,128]{1,0:T(8,128)(2,1)}, u32[]{:S(2)}) copy-start(bf16[256,128]{1,0:T(8,128)(2,1)} %down.5) | copy-start | bytes 196612
  33.0 23.3 %collective-permute-start.8 = (bf16[128,4608]{1,0:T(8,128)(2,1)}, bf16[128,4608]{1,0:T(8,128)(2,1)S(1)}, u32[]{:S(2)}, u32[]{:S(2)}) collective-permute-start(bf16[128,4608]{1,0:T(8,128)(2,1)} %fence.6.more.one), channel_id=1, source_target_pairs={{0,1},{1,0},{2,3},{3,2},{4,5},{5,4},{6,7},{7,6},{8,9},{9,8},{10,11... | collective-permute-start | bytes 3538952 | tf_op jit(solution)/shard_map/tokens_core/ppermute | solution.py:60
  33.0 46.3 %collective-permute-start.22 = (bf16[128,4608]{1,0:T(8,128)(2,1)}, bf16[128,4608]{1,0:T(8,128)(2,1)S(1)}, u32[]{:S(2)}, u32[]{:S(2)}) collective-permute-start(bf16[128,4608]{1,0:T(8,128)(2,1)} %fence.6.more.one), channel_id=1, source_target_pairs={{0,4},{1,13},{4,8},{5,1},{8,12},{9,5},{12,0},{13,9},{2,6},{3,15},{... | collective-permute-start | bytes 3538952 | tf_op jit(solution)/shard_map/tokens_y/ppermute | solution.py:27
  35.4 9.3 %collective-permute-start.10 = (bf16[32,4736]{1,0:T(8,128)(2,1)}, bf16[32,4736]{1,0:T(8,128)(2,1)S(1)}, u32[]{:S(2)}, u32[]{:S(2)}) collective-permute-start(bf16[32,4736]{1,0:T(8,128)(2,1)} %fence.5.tie_too.mine), channel_id=1, source_target_pairs={{0,16},{16,0},{32,48},{48,32},{1,17},{17,1},{33,49},{49,33},{2,18}... | collective-permute-start | bytes 909320 | tf_op jit(solution)/shard_map/weight_zl/ppermute | solution.py:60
  37.7 13.7 %collective-permute-start.6 = (bf16[128,128]{1,0:T(8,128)(2,1)S(1)}, bf16[128,128]{1,0:T(8,128)(2,1)S(1)}, u32[]{:S(2)}, u32[]{:S(2)}) collective-permute-start(bf16[128,128]{1,0:T(8,128)(2,1)S(1)} %get-tuple-element.27.refs_1_.tie), channel_id=1, source_target_pairs={{0,2},{2,0},{1,3},{3,1},{4,6},{6,4},{5,7},{7,5},{8,10},{10,8},{9,1... | collective-permute-start | bytes 98312 | tf_op jit(solution)/shard_map/act_z/ppermute | solution.py:60
  52.4 7.2 %copy-start.7 = (bf16[64,4736]{1,0:T(8,128)(2,1)}, bf16[64,4736]{1,0:T(8,128)(2,1)S(1)}, u32[]{:S(2)}) copy-start(bf16[64,4736]{1,0:T(8,128)(2,1)S(1)} %join.2.tie_too.mine) | copy-start | bytes 1818628
  52.4 13.7 %collective-permute-start.15 = (bf16[64,4736]{1,0:T(8,128)(2,1)S(1)}, bf16[64,4736]{1,0:T(8,128)(2,1)S(1)}, u32[]{:S(2)}, u32[]{:S(2)}) collective-permute-start(bf16[64,4736]{1,0:T(8,128)(2,1)S(1)} %join.2.tie_too.mine), channel_id=1, source_target_pairs={{0,64},{1,193},{64,0},{65,129},{128,192},{129,65},{192,128},{193,1... | collective-permute-start | bytes 1818632 | tf_op jit(solution)/shard_map/weight_x/ppermute | solution.py:33
  55.0 4.6 %copy-start.10 = (bf16[128,4608]{1,0:T(8,128)(2,1)S(1)}, bf16[128,4608]{1,0:T(8,128)(2,1)}, u32[]{:S(2)}) copy-start(bf16[128,4608]{1,0:T(8,128)(2,1)} %hidden.3) | copy-start | bytes 3538948
  55.0 1.3 %collective-permute-start.9 = (bf16[4,128,128]{2,1,0:T(8,128)(2,1)S(1)}, bf16[4,128,128]{2,1,0:T(8,128)(2,1)S(1)}, u32[]{:S(2)}, u32[]{:S(2)}) collective-permute-start(bf16[4,128,128]{2,1,0:T(8,128)(2,1)S(1)} %get-tuple-element.30.mixed), channel_id=1, source_target_pairs={{0,1},{1,0},{2,3},{3,2},{4,5},{5,4},{6,7},{7,6},{8,9},{9,8},{10,11... | collective-permute-start | bytes 393224 | tf_op jit(solution)/shard_map/mixed_core/ppermute | solution.py:60
  56.4 3.2 %copy-start.19 = (bf16[4,128,128]{2,1,0:T(8,128)(2,1)}, bf16[4,128,128]{2,1,0:T(8,128)(2,1)S(1)}, u32[]{:S(2)}) copy-start(bf16[4,128,128]{2,1,0:T(8,128)(2,1)S(1)} %collective-permute-done.9.mixed_s) | copy-start | bytes 393220
  60.9 1.4 %collective-permute-start.11 = (f32[8,2304]{1,0:T(8,128)S(1)}, f32[8,2304]{1,0:T(8,128)S(1)}, u32[]{:S(2)}, u32[]{:S(2)}) collective-permute-start(f32[8,2304]{1,0:T(8,128)S(1)} %get-tuple-element.32), channel_id=1, source_target_pairs={{0,1},{1,0},{2,3},{3,2},{4,5},{5,4},{6,7},{7,6},{8,9},{9,8},{10,11... | collective-permute-start | bytes 221192 | tf_op jit(solution)/shard_map/gate_core/ppermute | solution.py:60
  62.2 4.0 %collective-permute-start.12 = (f32[8,2304]{1,0:T(8,128)S(1)}, f32[8,2304]{1,0:T(8,128)S(1)}, u32[]{:S(2)}, u32[]{:S(2)}) collective-permute-start(f32[8,2304]{1,0:T(8,128)S(1)} %gate_sum.5.first), channel_id=1, source_target_pairs={{0,64},{64,0},{128,192},{192,128},{1,65},{65,1},{129,193},{193,129... | collective-permute-start | bytes 221192 | tf_op jit(solution)/shard_map/gate_x/ppermute | solution.py:60
  62.3 6.0 %collective-permute-start.13 = (f32[8,2304]{1,0:T(8,128)S(1)}, f32[8,2304]{1,0:T(8,128)S(1)}, u32[]{:S(2)}, u32[]{:S(2)}) collective-permute-start(f32[8,2304]{1,0:T(8,128)S(1)} %gate_sum.5.first), channel_id=1, source_target_pairs={{0,128},{64,192},{128,0},{192,64},{1,129},{65,193},{129,1},{193,65... | collective-permute-start | bytes 221192 | tf_op jit(solution)/shard_map/gate_x/ppermute | solution.py:60
  64.2 4.9 %collective-permute-start.14 = (f32[8,2304]{1,0:T(8,128)S(1)}, f32[8,2304]{1,0:T(8,128)S(1)}, u32[]{:S(2)}, u32[]{:S(2)}) collective-permute-start(f32[8,2304]{1,0:T(8,128)S(1)} %gate_sum.5.first), channel_id=1, source_target_pairs={{0,192},{64,128},{128,64},{192,0},{1,193},{65,129},{129,65},{193,1... | collective-permute-start | bytes 221192 | tf_op jit(solution)/shard_map/gate_x/ppermute | solution.py:60
  70.7 6.2 %collective-permute-start.16 = (f32[8,2304]{1,0:T(8,128)}, f32[8,2304]{1,0:T(8,128)}, u32[]{:S(2)}, u32[]{:S(2)}) collective-permute-start(f32[8,2304]{1,0:T(8,128)} %gate_sum.6.tie.first), channel_id=1, source_target_pairs={{0,4},{4,0},{8,12},{12,8},{1,5},{5,1},{9,13},{13,9},{2,6},{6,2},{1... | collective-permute-start | bytes 221192 | tf_op jit(solution)/shard_map/gate_y/ppermute | solution.py:60
  70.7 6.1 %collective-permute-start.17 = (f32[8,2304]{1,0:T(8,128)}, f32[8,2304]{1,0:T(8,128)}, u32[]{:S(2)}, u32[]{:S(2)}) collective-permute-start(f32[8,2304]{1,0:T(8,128)} %gate_sum.6.tie.first), channel_id=1, source_target_pairs={{0,8},{4,12},{8,0},{12,4},{1,9},{5,13},{9,1},{13,5},{2,10},{6,14},... | collective-permute-start | bytes 221192 | tf_op jit(solution)/shard_map/gate_y/ppermute | solution.py:60
  72.8 5.5 %collective-permute-start.18 = (f32[8,2304]{1,0:T(8,128)}, f32[8,2304]{1,0:T(8,128)}, u32[]{:S(2)}, u32[]{:S(2)}) collective-permute-start(f32[8,2304]{1,0:T(8,128)} %gate_sum.6.tie.first), channel_id=1, source_target_pairs={{0,12},{4,8},{8,4},{12,0},{1,13},{5,9},{9,5},{13,1},{2,14},{6,10},... | collective-permute-start | bytes 221192 | tf_op jit(solution)/shard_map/gate_y/ppermute | solution.py:60
  76.7 17.9 %collective-permute-start.24 = (bf16[128,4736]{1,0:T(8,128)(2,1)S(1)}, bf16[128,4736]{1,0:T(8,128)(2,1)S(1)}, u32[]{:S(2)}, u32[]{:S(2)}) collective-permute-start(bf16[128,4736]{1,0:T(8,128)(2,1)S(1)} %join.3.refs_0_.mine), channel_id=1, source_target_pairs={{0,192},{1,65},{64,128},{65,1},{128,64},{129,193},{192,0},{193,129... | collective-permute-start | bytes 3637256 | tf_op jit(solution)/shard_map/weight_x/ppermute | solution.py:33
  79.3 15.3 %copy-start.12 = (bf16[128,4608]{1,0:T(8,128)(2,1)S(1)}, bf16[128,4608]{1,0:T(8,128)(2,1)}, u32[]{:S(2)}) copy-start(bf16[128,4608]{1,0:T(8,128)(2,1)} %copy-done.11) | copy-start | bytes 3538948
  79.3 15.3 %copy-start.3 = (bf16[128,4608]{1,0:T(8,128)(2,1)S(1)}, bf16[128,4608]{1,0:T(8,128)(2,1)}, u32[]{:S(2)}) copy-start(bf16[128,4608]{1,0:T(8,128)(2,1)} %copy-done.1) | copy-start | bytes 3538948
  79.3 15.3 %copy-start.6 = (bf16[128,4608]{1,0:T(8,128)(2,1)S(1)}, bf16[128,4608]{1,0:T(8,128)(2,1)}, u32[]{:S(2)}) copy-start(bf16[128,4608]{1,0:T(8,128)(2,1)} %own.1) | copy-start | bytes 3538948
  79.4 15.3 %copy-start.18 = (bf16[4,128,128]{2,1,0:T(8,128)(2,1)S(1)}, bf16[4,128,128]{2,1,0:T(8,128)(2,1)}, u32[]{:S(2)}) copy-start(bf16[4,128,128]{2,1,0:T(8,128)(2,1)} %copy-done.17) | copy-start | bytes 393220
  79.4 15.3 %copy-start.20 = (bf16[4,128,128]{2,1,0:T(8,128)(2,1)S(1)}, bf16[4,128,128]{2,1,0:T(8,128)(2,1)}, u32[]{:S(2)}) copy-start(bf16[4,128,128]{2,1,0:T(8,128)(2,1)} %copy-done.19) | copy-start | bytes 393220
  79.4 15.3 %collective-permute-start.23 = (bf16[128,4608]{1,0:T(8,128)(2,1)S(1)}, bf16[128,4608]{1,0:T(8,128)(2,1)S(1)}, u32[]{:S(2)}, u32[]{:S(2)}) collective-permute-start(bf16[128,4608]{1,0:T(8,128)(2,1)S(1)} %fence.7.near), channel_id=1, source_target_pairs={{0,1},{1,0},{2,3},{3,2},{4,5},{5,4},{6,7},{7,6},{8,9},{9,8},{10,11... | collective-permute-start | bytes 3538952 | tf_op jit(solution)/shard_map/tokens_core/ppermute | solution.py:60
  82.5 15.3 %collective-permute-start.26 = (bf16[128,4608]{1,0:T(8,128)(2,1)S(1)}, bf16[128,4608]{1,0:T(8,128)(2,1)S(1)}, u32[]{:S(2)}, u32[]{:S(2)}) collective-permute-start(bf16[128,4608]{1,0:T(8,128)(2,1)S(1)} %fence.7.near), channel_id=1, source_target_pairs={{0,4},{1,13},{4,8},{5,1},{8,12},{9,5},{12,0},{13,9},{2,6},{3,15},{... | collective-permute-start | bytes 3538952 | tf_op jit(solution)/shard_map/tokens_y/ppermute | solution.py:27
  83.7 5.2 %collective-permute-start.19 = (f32[8,2304]{1,0:T(8,128)S(1)}, f32[8,2304]{1,0:T(8,128)S(1)}, u32[]{:S(2)}, u32[]{:S(2)}) collective-permute-start(f32[8,2304]{1,0:T(8,128)S(1)} %gate_sum.7.refs_1_.first), channel_id=1, source_target_pairs={{0,16},{16,0},{32,48},{48,32},{1,17},{17,1},{33,49},{49,33},{2,18}... | collective-permute-start | bytes 221192 | tf_op jit(solution)/shard_map/gate_zl/ppermute | solution.py:60
  83.7 6.5 %collective-permute-start.20 = (f32[8,2304]{1,0:T(8,128)S(1)}, f32[8,2304]{1,0:T(8,128)S(1)}, u32[]{:S(2)}, u32[]{:S(2)}) collective-permute-start(f32[8,2304]{1,0:T(8,128)S(1)} %gate_sum.7.refs_1_.first), channel_id=1, source_target_pairs={{0,32},{16,48},{32,0},{48,16},{1,33},{17,49},{33,1},{49,17},{2,34}... | collective-permute-start | bytes 221192 | tf_op jit(solution)/shard_map/gate_zl/ppermute | solution.py:60
  88.9 5.7 %collective-permute-start.21 = (f32[8,2304]{1,0:T(8,128)S(1)}, f32[8,2304]{1,0:T(8,128)S(1)}, u32[]{:S(2)}, u32[]{:S(2)}) collective-permute-start(f32[8,2304]{1,0:T(8,128)S(1)} %gate_sum.7.refs_1_.first), channel_id=1, source_target_pairs={{0,48},{16,32},{32,16},{48,0},{1,49},{17,33},{33,17},{49,1},{2,50}... | collective-permute-start | bytes 221192 | tf_op jit(solution)/shard_map/gate_zl/ppermute | solution.py:60
  97.9 7.6 %collective-permute-start.27 = (bf16[128,4608]{1,0:T(8,128)(2,1)S(1)}, bf16[128,4608]{1,0:T(8,128)(2,1)S(1)}, u32[]{:S(2)}, u32[]{:S(2)}) collective-permute-start(bf16[128,4608]{1,0:T(8,128)(2,1)S(1)} %fence.9.more), channel_id=1, source_target_pairs={{0,1},{1,0},{2,3},{3,2},{4,5},{5,4},{6,7},{7,6},{8,9},{9,8},{10,11... | collective-permute-start | bytes 3538952 | tf_op jit(solution)/shard_map/tokens_core/ppermute | solution.py:60
  100.1 24.1 %collective-permute-start.29 = (bf16[2,256,256]{2,1,0:T(8,128)(2,1)S(1)}, bf16[2,256,256]{2,1,0:T(8,128)(2,1)S(1)}, u32[]{:S(2)}, u32[]{:S(2)}) collective-permute-start(bf16[2,256,256]{2,1,0:T(8,128)(2,1)S(1)} %get-tuple-element.33.refs_1_.tie), channel_id=1, source_target_pairs={{0,2},{2,0},{1,3},{3,1},{4,6},{6,4},{5,7},{7,5},{8,10},{10,8},{9,1... | collective-permute-start | bytes 786440 | tf_op jit(solution)/shard_map/out_z/ppermute | solution.py:60
  100.1 19.3 %collective-permute-start.25 = (f32[8,2304]{1,0:T(8,128)S(1)}, f32[8,2304]{1,0:T(8,128)S(1)}, u32[]{:S(2)}, u32[]{:S(2)}) collective-permute-start(f32[8,2304]{1,0:T(8,128)S(1)} %fence.8.refs_1_.left), channel_id=1, source_target_pairs={{0,2},{2,0},{1,3},{3,1},{4,6},{6,4},{5,7},{7,5},{8,10},{10,8},{9,1... | collective-permute-start | bytes 221192 | tf_op jit(solution)/shard_map/gate_zh/ppermute | solution.py:60
  107.5 16.7 %copy-start.25 = (bf16[256,128]{1,0:T(8,128)(2,1)S(1)}, bf16[256,128]{1,0:T(8,128)(2,1)}, u32[]{:S(2)}) copy-start(bf16[256,128]{1,0:T(8,128)(2,1)} %down.5) | copy-start | bytes 196612
  107.5 23.9 %collective-permute-start.30 = (bf16[2,256,256]{2,1,0:T(8,128)(2,1)S(1)}, bf16[2,256,256]{2,1,0:T(8,128)(2,1)S(1)}, u32[]{:S(2)}, u32[]{:S(2)}) collective-permute-start(bf16[2,256,256]{2,1,0:T(8,128)(2,1)S(1)} %far_rest.1), channel_id=1, source_target_pairs={{0,2},{2,0},{1,3},{3,1},{4,6},{6,4},{5,7},{7,5},{8,10},{10,8},{9,1... | collective-permute-start | bytes 786440 | tf_op jit(solution)/shard_map/out_z_rest/ppermute | solution.py:60
  119.4 12.0 %copy-start.16 = (bf16[2,256,256]{2,1,0:T(8,128)(2,1)S(1)}, bf16[2,256,256]{2,1,0:T(8,128)(2,1)}, u32[]{:S(2)}) copy-start(bf16[2,256,256]{2,1,0:T(8,128)(2,1)} %copy-done.15) | copy-start | bytes 786436
  119.4 6.8 %collective-permute-start.28 = (f32[8,2304]{1,0:T(8,128)S(1)}, f32[8,2304]{1,0:T(8,128)S(1)}, u32[]{:S(2)}, u32[]{:S(2)}) collective-permute-start(f32[8,2304]{1,0:T(8,128)S(1)} %gate_sum.9), channel_id=1, source_target_pairs={{0,1},{1,0},{2,3},{3,2},{4,5},{5,4},{6,7},{7,6},{8,9},{9,8},{10,11... | collective-permute-start | bytes 221192 | tf_op jit(solution)/shard_map/gate_core_back/ppermute | solution.py:60
  (10 other events, 14.1 us)

commit v8 on v6

--- a/solution.py
+++ b/solution.py
@@ -79,23 +79,6 @@
     column = lax.broadcasted_iota(jnp.int32, (adapters, stacked), 1)
     low = row * (stacked // adapters)
     return jnp.where((column >= low) & (column < low + stacked // adapters), 1.0, 0.0)
-
-
-def join_kernel(side, mine, got, tie, out):
-    rows = mine.shape[0]
-    for place, ref in ((side[0], mine), (1 - side[0], got)):
-        out[pl.ds(pl.multiple_of(place * rows, rows), rows), :] = ref[...]
-
-
-def join(side, mine, got, tie):
-    return pl.pallas_call(
-        join_kernel,
-        in_specs=[SMEM, VMEM, VMEM, ANY],
-        out_specs=VMEM,
-        out_shape=shaped((2 * mine.shape[0], mine.shape[1]), mine.dtype),
-        compiler_params=SMALL,
-        name="join",
-    )(side.reshape(1), mine, got, tie)
 
 
 def token_kernel(at, hidden, grad, up, gate, mixed, gates, back):
@@ -129,7 +112,7 @@
     rest[...] = keep[y] + got[y].astype(F32)
 
 
-def act_z_kernel(at, rest, first, second, third, mixed, tie, tie_too, keep, give, all_mixed):
+def act_z_kernel(at, rest, first, second, third, mixed, tie, keep, give, all_mixed):
     y, zh = at[1], at[2]
     for out, side in ((give, 1 - zh), (keep, zh)):
         total = (rest[side] + first[side].astype(F32)) + (
@@ -179,12 +162,15 @@
     out[...] = value.astype(out.dtype)
 
 
-def far_kernel(at, own, own_s, one, one_s, two, two_s, mixed, mixed_s, mine, got, tie, out, weight, down):
+def far_kernel(at, own, own_s, one, one_s, two, two_s, mixed, mixed_s, *refs):
+    pieces, (tie, out, weight, down) = refs[:4], refs[4:]
     width = weight.shape[1]
-    rows = mine.shape[0]
-    block = at[4] // 2
-    for number, ref in ((block, mine), (1 - block, got)):
-        place = pl.ds(pl.multiple_of(number * rows, rows), rows)
+    rows = pieces[0].shape[0]
+    x, c = at[0], at[3]
+    up, turned = jnp.bitwise_xor(x, 1), 3 - x
+    first, second = jnp.where(c == 0, up, turned), jnp.where(c == 0, turned, up)
+    for place, ref in zip((x, first, second, jnp.bitwise_xor(x, 2)), pieces):
+        place = pl.ds(pl.multiple_of(place * rows, rows), rows)
         weight[place, :] = ref[:, :width]
         down[place, :] = ref[:, width:]
     for steps, group in enumerate(((own, own_s), (one, one_s), (two, two_s))):
@@ -195,7 +181,7 @@
     rows_product(at, 3, (three, three_s), (mixed, mixed_s), weight, down, out)
 
 
-def own_kernel(first, at, near, near_s, more, more_s, mixed, mixed_s, weight, down, tie, out):
+def product_kernel(first, at, near, near_s, more, more_s, mixed, mixed_s, weight, down, tie, out):
     for number, group in enumerate(((near, near_s), (more, more_s))):
         rows_product(at, first + number, group, (mixed, mixed_s), weight, down, out.at[number])
 
@@ -229,15 +215,12 @@
     features = weight.shape[0]
     depth = width + stacked
     quarter = features // 4
-    x, y, zl, zh, c = (lax.axis_index(a) for a in ("x", "y", "zl", "zh", "c"))
-    turned = jnp.where(x == 0, 0, jnp.where(x == 3, 1, x + 1))
-    number = jnp.where(c == 0, x, turned)
-    at = jnp.stack([x, y, zh, c, number]).astype(jnp.int32)
+    x, y, zh, c = (lax.axis_index(a) for a in ("x", "y", "zh", "c"))
+    at = jnp.stack([x, y, zh, c]).astype(jnp.int32)
 
     with jax.named_scope("weight_z"):
-        start = number * quarter + (zl % 2) * (quarter // 2)
         piece = jnp.concatenate(
-            [lax.dynamic_slice_in_dim(v, start, quarter // 2, 0) for v in (weight, down)], axis=1
+            [lax.dynamic_slice_in_dim(v, x * quarter, quarter, 0) for v in (weight, down)], axis=1
         )
         far_piece = swap(piece, "zh", 1)
     with jax.named_scope("tokens_y"):
@@ -280,16 +263,13 @@
         compiler_params=SMALL,
         name="rank_sum_core",
     )(at, keep, got, mixed)
-    (far_piece,) = fence((far_piece,), rest)
-    with jax.named_scope("weight_zl"):
-        z_got = swap(far_piece, "zl", 1)
     with jax.named_scope("act_y"):
         first, second, third = (
             swap(v, "y", mask) for v, mask in ((first, 1), (second, 2), (third, 3))
         )
     keep, give, all_mixed = pl.pallas_call(
         act_z_kernel,
-        in_specs=[SMEM] + [VMEM] * 5 + [ANY] * 2,
+        in_specs=[SMEM] + [VMEM] * 5 + [ANY],
         out_specs=[VMEM] * 3,
         out_shape=[
             shaped((tokens, stacked), F32),
@@ -298,32 +278,32 @@
         ],
         compiler_params=SMALL,
         name="rank_sum_y",
-    )(at, rest, first, second, third, mixed, own_s, z_got)
-    (one,) = fence((one,), give)
+    )(at, rest, first, second, third, mixed, own_s)
+    one, far_piece = fence((one, far_piece), give)
     with jax.named_scope("tokens_y"):
         two = ring(one, "y")
-    far_quarter = join(zl % 2, far_piece, z_got, give)
+    with jax.named_scope("tokens_core"):
+        one_s = swap(one, "c", 1)
     with jax.named_scope("weight_x"):
-        w_one = pairs(far_quarter, "x", True)
+        w_first = pairs(far_piece, "x", True)
+        w_second = pairs(far_piece, "x", False)
     with jax.named_scope("act_z"):
         message = swap(give, "zh", 1)
     with jax.named_scope("mixed_core"):
         mixed_s = swap(all_mixed, "c", 1)
-    with jax.named_scope("tokens_core"):
-        one_s = swap(one, "c", 1)
-
-    def own_products(first, near, near_s, more, more_s, tie):
+
+    def products(name, first, near, near_s, more, more_s, weights, downs, tie):
         return pl.pallas_call(
-            functools.partial(own_kernel, first),
+            functools.partial(product_kernel, first),
             in_specs=[SMEM] + [VMEM] * 8 + [ANY],
             out_specs=VMEM,
             out_shape=shaped((2, 2 * tokens, features), BF16),
             compiler_params=MIDDLE,
             cost_estimate=cost(8 * tokens * depth * features, 12 * tokens * depth),
-            name="own_products",
-        )(at, near, near_s, more, more_s, all_mixed, mixed_s, weight, down, tie)
-
-    own_near = own_products(0, grad, own_s, one, one_s, give)
+            name=name,
+        )(at, near, near_s, more, more_s, all_mixed, mixed_s, weights, downs, tie)
+
+    own_near = products("own_near", 0, grad, own_s, one, one_s, weight, down, give)
 
     total, give = pl.pallas_call(
         gate_kernel,
@@ -361,23 +341,23 @@
 
     with jax.named_scope("gate_core"):
         got = swap(give, "c", 1)
-    total = add(total, got, w_one)
-    w_mine = join(number % 2, far_quarter, w_one, total)
-    with jax.named_scope("weight_x"):
-        w_got = pairs(w_mine, "x", False)
-    total = step(total, "zl", w_mine, mixed_s)
+    total = add(total, got, w_first, w_second)
+    (w_first,) = fence((w_first,), total)
+    with jax.named_scope("weight_x_far"):
+        w_far = pairs(w_first, "x", False)
+    total = step(total, "zl", mixed_s, w_far)
     (two,) = fence((two,), total)
     with jax.named_scope("tokens_y"):
         three = ring(two, "y")
+    with jax.named_scope("tokens_core"):
+        two_s = swap(two, "c", 1)
     with jax.named_scope("gate_zh"):
         got = swap(total, "zh", 1)
-    with jax.named_scope("tokens_core"):
-        two_s = swap(two, "c", 1)
-    total = add(total, got, two_s, w_got)
-    near = (grad, own_s, one, one_s, two, two_s)
+    total = add(total, got, two_s, w_far)
+
     far, far_weight, far_down = pl.pallas_call(
         far_kernel,
-        in_specs=[SMEM] + [VMEM] * 10 + [ANY],
+        in_specs=[SMEM] + [VMEM] * 12 + [ANY],
         out_specs=[VMEM] * 3,
         out_shape=[
             shaped((3, 2 * tokens, features), BF16),
@@ -387,13 +367,16 @@
         compiler_params=MIDDLE,
         cost_estimate=cost(12 * tokens * depth * features, 18 * tokens * depth),
         name="far_products",
-    )(at, *near, all_mixed, mixed_s, w_mine, w_got, total)
+    )(
+        at, grad, own_s, one, one_s, two, two_s, all_mixed, mixed_s,
+        far_piece, w_first, w_second, w_far, total,
+    )
+    with jax.named_scope("out_z"):
+        far_got = swap(far, "zh", 1)
     (three,) = fence((three,), far)
     with jax.named_scope("tokens_core"):
         three_s = swap(three, "c", 1)
     total = step(total, "x", far)
-    with jax.named_scope("out_z"):
-        far_got = swap(far, "zh", 1)
 
     last = pl.pallas_call(
         far_last_kernel,
@@ -409,7 +392,7 @@
 
     (total,) = fence((total,), last)
     total = step(total, "y")
-    own_rest = own_products(2, two, two_s, three, three_s, last)
+    own_rest = products("own_rest", 2, two, two_s, three, three_s, weight, down, last)
     (total,) = fence((total,), far_got, own_rest)
     with jax.named_scope("gate_core_back"):
         other = swap(total, "c", 1)

time: 120 us -> 123 us (1.025)
  the two profiles are of different devices: /device:TPU:5 before, /device:TPU:1 now
where the time goes in v8:
time: 123 us; the launch traced here: 122 us
  starting transfers between devices  57.6 us (47%)
  waiting for transfers between devices  39 us (32%)
  Pallas kernels  15.8 us (13%)
  local copies, waits for them, and re-layouts  7.34 us (6%)
  other arithmetic  1.62 us (1%)
    ppermute x25, starting transfers between devices, swap(): return lax.ppermute(value, axis, [(i, i ^ mask) for i in range(size)])  50.2 us
    ppermute x25, waiting for transfers between devices, swap(): return lax.ppermute(value, axis, [(i, i ^ mask) for i in range(size)])  33.2 us
    unnamed x22, local copies, waits for them, and re-layouts  5.51 us
    pallas_call x2, Pallas kernels, products(): pl.pallas_call(functools.partial(product_kernel, first), in_specs=[SMEM]...  3.98 us
    ppermute x3, starting transfers between devices, pairs(): lax.ppermute(value, (axis, 'c'), [(2 * i + c, 2 * partner(i, c) + c) for...  3.78 us
    ppermute x3, starting transfers between devices, ring(): return lax.ppermute(value, (axis, 'c'), pairs)  3.64 us
    pallas_call x1, Pallas kernels, on_device(): pl.pallas_call(far_kernel, in_specs=[SMEM] + [VMEM] * 12 + [ANY], out_spe...  3.36 us
    ppermute x3, waiting for transfers between devices, ring(): return lax.ppermute(value, (axis, 'c'), pairs)  3.32 us
  transfers between devices with their start and end apart: 31, of which 15 were waited for; matrix products, arithmetic and copies ran while one was open for 2% of the time, Pallas kernels for 13%

profile of v8, /device:TPU:1, one launch (start us, length us, event | category | flops | bytes accessed | tf_op | source)
XLA Modules:
  0.0 122.3 jit_solution(10725545567208346432)
XLA Ops:
  0.6 3.3 %collective-permute-start.4 = (bf16[128,4608]{1,0:T(8,128)(2,1)}, bf16[128,4608]{1,0:T(8,128)(2,1)S(1)}, u32[]{:S(2)}, u32[]{:S(2)}) collective-permute-start(bf16[128,4608]{1,0:T(8,128)(2,1)} %own.1), channel_id=1, source_target_pairs={{0,1},{1,0},{2,3},{3,2},{4,5},{5,4},{6,7},{7,6},{8,9},{9,8},{10,11... | collective-permute-start | bytes 3538952 | tf_op jit(solution)/shard_map/tokens_core/ppermute | solution.py:60
  4.0 1.0 collective-permute-start.6
  5.0 1.1 constant_dynamic-slice_fusion.1
  6.8 0.9 pad_maximum_fusion
  7.7 6.9 %collective-permute-start.7 = (bf16[64,4736]{1,0:T(8,128)(2,1)}, bf16[64,4736]{1,0:T(8,128)(2,1)}, u32[]{:S(2)}, u32[]{:S(2)}) collective-permute-start(bf16[64,4736]{1,0:T(8,128)(2,1)} %pad_maximum_fusion), channel_id=1, source_target_pairs={{0,2},{2,0},{1,3},{3,1},{4,6},{6,4},{5,7},{7,5},{8,10},{10,8},{9,1... | collective-permute-start | bytes 1818632 | tf_op jit(solution)/shard_map/weight_z/ppermute | solution.py:60
  14.6 1.2 %copy-done.7 = bf16[2048,256]{1,0:T(8,128)(2,1)S(1)} copy-done((bf16[2048,256]{1,0:T(8,128)(2,1)S(1)}, bf16[2048,256]{1,0:T(8,128)(2,1)}, u32[]{:S(2)}) %copy-start.7) | copy-done | bytes 1048600
  15.9 0.8 copy-done.8
  16.7 1.0 rank_products.1
  17.8 1.3 %copy-done.2 = bf16[128,4608]{1,0:T(8,128)(2,1)S(1)} copy-done((bf16[128,4608]{1,0:T(8,128)(2,1)S(1)}, bf16[128,4608]{1,0:T(8,128)(2,1)}, u32[]{:S(2)}) %copy-start.2) | copy-done | bytes 1179672
  19.1 1.3 %copy-done.6 = bf16[128,4608]{1,0:T(8,128)(2,1)S(1)} copy-done((bf16[128,4608]{1,0:T(8,128)(2,1)S(1)}, bf16[128,4608]{1,0:T(8,128)(2,1)}, u32[]{:S(2)}) %copy-start.6) | copy-done | bytes 1179672
  20.3 0.9 copy-done.10
  21.2 2.0 %token_values.1 = (bf16[128,128]{1,0:T(8,128)(2,1)S(1)}, f32[8,128]{1,0:T(8,128)S(1)}, f32[128,128]{1,0:T(8,128)S(1)}) custom-call(s32[4]{0:T(128)S(1)} %pad_add_fusion.at, bf16[128,4608]{1,0:T(8,128)(2,1)S(1)} %copy-done.2, bf16[128,4608]{1,0:T(8,128)(2,1)S(1)} %copy-done.1, bf16[128,4608]{1,0:T(8,128)(2,1)S(1)} %copy-done.6, bf16[8,4608]{1,0:T(8,128)(2,1)S(1)} %copy-done.10), custom_call_target="tpu_custom_call" | custom-call | flops 452984832 | bytes 7077888 | tf_op jit(solution)/shard_map/token_values/pallas_call | solution.py:245
  24.4 1.4 %collective-permute-start.2 = (bf16[3,128,128]{2,1,0:T(8,128)(2,1)S(1)}, bf16[3,128,128]{2,1,0:T(8,128)(2,1)S(1)}, u32[]{:S(2)}, u32[]{:S(2)}) collective-permute-start(bf16[3,128,128]{2,1,0:T(8,128)(2,1)S(1)} %get-tuple-element.26), channel_id=1, source_target_pairs={{0,8},{4,12},{8,0},{12,4},{1,9},{5,13},{9,1},{13,5},{2,10},{6,14},... | collective-permute-start | bytes 294920 | tf_op jit(solution)/shard_map/act_y/ppermute | solution.py:60
  25.8 2.1 %collective-permute-done.1.first = bf16[3,128,128]{2,1,0:T(8,128)(2,1)S(1)} collective-permute-done((bf16[3,128,128]{2,1,0:T(8,128)(2,1)S(1)}, bf16[3,128,128]{2,1,0:T(8,128)(2,1)S(1)}, u32[]{:S(2)}, u32[]{:S(2)}) %collective-permute-start.1) | collective-permute-done | bytes 98336 | tf_op jit(solution)/shard_map/act_y/ppermute | solution.py:60
  28.7 2.0 %collective-permute-done.2.second = bf16[3,128,128]{2,1,0:T(8,128)(2,1)S(1)} collective-permute-done((bf16[3,128,128]{2,1,0:T(8,128)(2,1)S(1)}, bf16[3,128,128]{2,1,0:T(8,128)(2,1)S(1)}, u32[]{:S(2)}, u32[]{:S(2)}) %collective-permute-start.2) | collective-permute-done | bytes 98336 | tf_op jit(solution)/shard_map/act_y/ppermute | solution.py:60
  30.7 1.9 %collective-permute-done.3.third = bf16[3,128,128]{2,1,0:T(8,128)(2,1)S(1)} collective-permute-done((bf16[3,128,128]{2,1,0:T(8,128)(2,1)S(1)}, bf16[3,128,128]{2,1,0:T(8,128)(2,1)S(1)}, u32[]{:S(2)}, u32[]{:S(2)}) %collective-permute-start.3) | collective-permute-done | bytes 98336 | tf_op jit(solution)/shard_map/act_y/ppermute | solution.py:60
  33.2 7.2 %collective-permute-done.7.refs_1_ = bf16[64,4736]{1,0:T(8,128)(2,1)} collective-permute-done((bf16[64,4736]{1,0:T(8,128)(2,1)}, bf16[64,4736]{1,0:T(8,128)(2,1)}, u32[]{:S(2)}, u32[]{:S(2)}) %collective-permute-start.7) | collective-permute-done | bytes 606240 | tf_op jit(solution)/shard_map/weight_z/ppermute | solution.py:60
  40.4 2.5 %collective-permute-start.11 = (bf16[64,4736]{1,0:T(8,128)(2,1)}, bf16[64,4736]{1,0:T(8,128)(2,1)S(1)}, u32[]{:S(2)}, u32[]{:S(2)}) collective-permute-start(bf16[64,4736]{1,0:T(8,128)(2,1)} %get-tuple-element.36.refs_0_), channel_id=1, source_target_pairs={{0,64},{1,193},{64,0},{65,129},{128,192},{129,65},{192,128},{193,1... | collective-permute-start | bytes 1818632 | tf_op jit(solution)/shard_map/weight_x/ppermute | solution.py:33
  42.9 1.2 collective-permute-start.18
  44.5 1.0 collective-permute-done.9.mixed_s.refs_0_
  45.5 6.1 %collective-permute-start.5 = (bf16[128,128]{1,0:T(8,128)(2,1)S(1)}, bf16[128,128]{1,0:T(8,128)(2,1)S(1)}, u32[]{:S(2)}, u32[]{:S(2)}) collective-permute-start(bf16[128,128]{1,0:T(8,128)(2,1)S(1)} %get-tuple-element.29.refs_2_.tie), channel_id=1, source_target_pairs={{0,2},{2,0},{1,3},{3,1},{4,6},{6,4},{5,7},{7,5},{8,10},{10,8},{9,1... | collective-permute-start | bytes 98312 | tf_op jit(solution)/shard_map/act_z/ppermute | solution.py:60
  51.6 2.0 %own_near.1.tie.near = bf16[2,256,256]{2,1,0:T(8,128)(2,1)S(1)} custom-call(s32[4]{0:T(128)S(1)} %pad_add_fusion.at, bf16[128,4608]{1,0:T(8,128)(2,1)S(1)} %copy-done.1, bf16[128,4608]{1,0:T(8,128)(2,1)S(1)} %collective-permute-done.4.tie.near_s.own_s, bf16[128,4608]{1,0:T(8,128)(2,1)S(1)} %get-tuple-element.32.more.one, ...), custom_call_target="tpu_custom_call" | custom-call | flops 1241513984 | bytes 7274496 | tf_op jit(solution)/shard_map/own_near/pallas_call | solution.py:296
  53.6 1.2 %gate_products.1 = (f32[8,2304]{1,0:T(8,128)S(1)}, f32[8,2304]{1,0:T(8,128)S(1)}) custom-call(s32[4]{0:T(128)S(1)} %pad_add_fusion.at, f32[128,128]{1,0:T(8,128)S(1)} %get-tuple-element.28.keep, bf16[128,128]{1,0:T(8,128)(2,1)S(1)} %collective-permute-done.5.got, f32[128,128]{1,0:T(8,128)S(1)} %get-tuple-element.30.back, ...), custom_call_target="tpu_custom_call" | custom-call | tf_op jit(solution)/shard_map/gate_products/pallas_call | solution.py:308
  55.4 1.9 %collective-permute-done.12.refs_1_.refs_2_ = bf16[64,4736]{1,0:T(8,128)(2,1)S(1)} collective-permute-done((bf16[64,4736]{1,0:T(8,128)(2,1)}, bf16[64,4736]{1,0:T(8,128)(2,1)S(1)}, u32[]{:S(2)}, u32[]{:S(2)}) %collective-permute-start.12) | collective-permute-done | bytes 606240 | tf_op jit(solution)/shard_map/weight_x/ppermute | solution.py:33
  57.3 1.3 %collective-permute-start.16 = (bf16[64,4736]{1,0:T(8,128)(2,1)S(1)}, bf16[64,4736]{1,0:T(8,128)(2,1)S(1)}, u32[]{:S(2)}, u32[]{:S(2)}) collective-permute-start(bf16[64,4736]{1,0:T(8,128)(2,1)S(1)} %fence.7.refs_1_), channel_id=1, source_target_pairs={{0,192},{1,65},{64,128},{65,1},{128,64},{129,193},{192,0},{193,129... | collective-permute-start | bytes 1818632 | tf_op jit(solution)/shard_map/weight_x_far/ppermute | solution.py:33
  58.6 1.4 %collective-permute-start.13 = (f32[8,2304]{1,0:T(8,128)S(1)}, f32[8,2304]{1,0:T(8,128)S(1)}, u32[]{:S(2)}, u32[]{:S(2)}) collective-permute-start(f32[8,2304]{1,0:T(8,128)S(1)} %gate_sum.5.refs_1_.first), channel_id=1, source_target_pairs={{0,16},{16,0},{32,48},{48,32},{1,17},{17,1},{33,49},{49,33},{2,18}... | collective-permute-start | bytes 221192 | tf_op jit(solution)/shard_map/gate_zl/ppermute | solution.py:60
  60.0 0.9 collective-permute-start.14
  60.9 1.3 %collective-permute-start.15 = (f32[8,2304]{1,0:T(8,128)S(1)}, f32[8,2304]{1,0:T(8,128)S(1)}, u32[]{:S(2)}, u32[]{:S(2)}) collective-permute-start(f32[8,2304]{1,0:T(8,128)S(1)} %gate_sum.5.refs_1_.first), channel_id=1, source_target_pairs={{0,48},{16,32},{32,16},{48,0},{1,49},{17,33},{33,17},{49,1},{2,50}... | collective-permute-start | bytes 221192 | tf_op jit(solution)/shard_map/gate_zl/ppermute | solution.py:60
  62.2 3.0 %collective-permute-done.14.third = f32[8,2304]{1,0:T(8,128)S(1)} collective-permute-done((f32[8,2304]{1,0:T(8,128)S(1)}, f32[8,2304]{1,0:T(8,128)S(1)}, u32[]{:S(2)}, u32[]{:S(2)}) %collective-permute-start.14) | collective-permute-done | bytes 73760 | tf_op jit(solution)/shard_map/gate_zl/ppermute | solution.py:60
  66.7 3.4 %collective-permute-start.19 = (bf16[128,4608]{1,0:T(8,128)(2,1)S(1)}, bf16[128,4608]{1,0:T(8,128)(2,1)S(1)}, u32[]{:S(2)}, u32[]{:S(2)}) collective-permute-start(bf16[128,4608]{1,0:T(8,128)(2,1)S(1)} %fence.8.two.near), channel_id=1, source_target_pairs={{0,1},{1,0},{2,3},{3,2},{4,5},{5,4},{6,7},{7,6},{8,9},{9,8},{10,11... | collective-permute-start | bytes 3538952 | tf_op jit(solution)/shard_map/tokens_core/ppermute | solution.py:60
  70.1 1.5 %collective-permute-start.23 = (bf16[128,4608]{1,0:T(8,128)(2,1)S(1)}, bf16[128,4608]{1,0:T(8,128)(2,1)S(1)}, u32[]{:S(2)}, u32[]{:S(2)}) collective-permute-start(bf16[128,4608]{1,0:T(8,128)(2,1)S(1)} %fence.8.two.near), channel_id=1, source_target_pairs={{0,4},{1,13},{4,8},{5,1},{8,12},{9,5},{12,0},{13,9},{2,6},{3,15},{... | collective-permute-start | bytes 3538952 | tf_op jit(solution)/shard_map/tokens_y/ppermute | solution.py:27
  71.6 5.2 %collective-permute-start.17 = (f32[8,2304]{1,0:T(8,128)S(1)}, f32[8,2304]{1,0:T(8,128)S(1)}, u32[]{:S(2)}, u32[]{:S(2)}) collective-permute-start(f32[8,2304]{1,0:T(8,128)S(1)} %gate_sum.6.refs_1_.left), channel_id=1, source_target_pairs={{0,2},{2,0},{1,3},{3,1},{4,6},{6,4},{5,7},{7,5},{8,10},{10,8},{9,1... | collective-permute-start | bytes 221192 | tf_op jit(solution)/shard_map/gate_zh/ppermute | solution.py:60
  76.8 2.0 %collective-permute-done.17.right = f32[8,2304]{1,0:T(8,128)S(1)} collective-permute-done((f32[8,2304]{1,0:T(8,128)S(1)}, f32[8,2304]{1,0:T(8,128)S(1)}, u32[]{:S(2)}, u32[]{:S(2)}) %collective-permute-start.17) | collective-permute-done | bytes 73760 | tf_op jit(solution)/shard_map/gate_zh/ppermute | solution.py:60
  78.8 3.4 %far_products.1 = (bf16[3,256,256]{2,1,0:T(8,128)(2,1)S(1)}, bf16[256,4608]{1,0:T(8,128)(2,1)S(1)}, bf16[256,128]{1,0:T(8,128)(2,1)S(1)}) custom-call(s32[4]{0:T(128)S(1)} %pad_add_fusion.at, bf16[128,4608]{1,0:T(8,128)(2,1)S(1)} %copy-done.1, bf16[128,4608]{1,0:T(8,128)(2,1)S(1)} %collective-permute-done.4.tie.near_s.own_s, ...), custom_call_target="tpu_custom_call" | custom-call | flops 1862270976 | bytes 10911744 | tf_op jit(solution)/shard_map/far_products/pallas_call | solution.py:358
  82.1 3.3 %collective-permute-done.23.refs_0_ = bf16[128,4608]{1,0:T(8,128)(2,1)S(1)} collective-permute-done((bf16[128,4608]{1,0:T(8,128)(2,1)S(1)}, bf16[128,4608]{1,0:T(8,128)(2,1)S(1)}, u32[]{:S(2)}, u32[]{:S(2)}) %collective-permute-start.23) | collective-permute-done | bytes 1179680 | tf_op jit(solution)/shard_map/tokens_y/ppermute | solution.py:27
  85.4 2.2 %collective-permute-start.24 = (bf16[128,4608]{1,0:T(8,128)(2,1)S(1)}, bf16[128,4608]{1,0:T(8,128)(2,1)S(1)}, u32[]{:S(2)}, u32[]{:S(2)}) collective-permute-start(bf16[128,4608]{1,0:T(8,128)(2,1)S(1)} %fence.9.three.more), channel_id=1, source_target_pairs={{0,1},{1,0},{2,3},{3,2},{4,5},{5,4},{6,7},{7,6},{8,9},{9,8},{10,11... | collective-permute-start | bytes 3538952 | tf_op jit(solution)/shard_map/tokens_core/ppermute | solution.py:60
  87.6 5.3 %collective-permute-start.28 = (bf16[3,256,256]{2,1,0:T(8,128)(2,1)S(1)}, bf16[3,256,256]{2,1,0:T(8,128)(2,1)S(1)}, u32[]{:S(2)}, u32[]{:S(2)}) collective-permute-start(bf16[3,256,256]{2,1,0:T(8,128)(2,1)S(1)} %get-tuple-element.37.refs_0_.refs_1_), channel_id=1, source_target_pairs={{0,2},{2,0},{1,3},{3,1},{4,6},{6,4},{5,7},{7,5},{8,10},{10,8},{9,1... | collective-permute-start | bytes 1179656 | tf_op jit(solution)/shard_map/out_z/ppermute | solution.py:60
  93.0 3.6 %collective-permute-start.21 = (f32[8,2304]{1,0:T(8,128)S(1)}, f32[8,2304]{1,0:T(8,128)S(1)}, u32[]{:S(2)}, u32[]{:S(2)}) collective-permute-start(f32[8,2304]{1,0:T(8,128)S(1)} %gate_sum.7.refs_4_.first), channel_id=1, source_target_pairs={{0,128},{64,192},{128,0},{192,64},{1,129},{65,193},{129,1},{193,65... | collective-permute-start | bytes 221192 | tf_op jit(solution)/shard_map/gate_x/ppermute | solution.py:60
  96.8 3.5 %collective-permute-done.21.third = f32[8,2304]{1,0:T(8,128)S(1)} collective-permute-done((f32[8,2304]{1,0:T(8,128)S(1)}, f32[8,2304]{1,0:T(8,128)S(1)}, u32[]{:S(2)}, u32[]{:S(2)}) %collective-permute-start.21) | collective-permute-done | bytes 73760 | tf_op jit(solution)/shard_map/gate_x/ppermute | solution.py:60
  100.3 1.5 %collective-permute-done.22.fourth = f32[8,2304]{1,0:T(8,128)S(1)} collective-permute-done((f32[8,2304]{1,0:T(8,128)S(1)}, f32[8,2304]{1,0:T(8,128)S(1)}, u32[]{:S(2)}, u32[]{:S(2)}) %collective-permute-start.22) | collective-permute-done | bytes 73760 | tf_op jit(solution)/shard_map/gate_x/ppermute | solution.py:60
  101.8 1.4 %far_products_last.1.refs_1_.tie = bf16[256,256]{1,0:T(8,128)(2,1)S(1)} custom-call(s32[4]{0:T(128)S(1)} %pad_add_fusion.at, bf16[128,4608]{1,0:T(8,128)(2,1)S(1)} %fence.9.three.more, bf16[128,4608]{1,0:T(8,128)(2,1)S(1)} %collective-permute-done.24.three_s.more_s, bf16[4,128,128]{2,1,0:T(8,128)(2,1)S(1)} %get-tuple-element.33.mixed, ...), custom_call_target="tpu_custom_call" | custom-call | flops 620756992 | bytes 3637248 | tf_op jit(solution)/shard_map/far_products_last/pallas_call | solution.py:381
  103.4 1.3 %collective-permute-start.26 = (f32[8,2304]{1,0:T(8,128)S(1)}, f32[8,2304]{1,0:T(8,128)S(1)}, u32[]{:S(2)}, u32[]{:S(2)}) collective-permute-start(f32[8,2304]{1,0:T(8,128)S(1)} %fence.10.first), channel_id=1, source_target_pairs={{0,8},{4,12},{8,0},{12,4},{1,9},{5,13},{9,1},{13,5},{2,10},{6,14},... | collective-permute-start | bytes 221192 | tf_op jit(solution)/shard_map/gate_y/ppermute | solution.py:60
  104.7 2.6 %collective-permute-start.27 = (f32[8,2304]{1,0:T(8,128)S(1)}, f32[8,2304]{1,0:T(8,128)S(1)}, u32[]{:S(2)}, u32[]{:S(2)}) collective-permute-start(f32[8,2304]{1,0:T(8,128)S(1)} %fence.10.first), channel_id=1, source_target_pairs={{0,12},{4,8},{8,4},{12,0},{1,13},{5,9},{9,5},{13,1},{2,14},{6,10},... | collective-permute-start | bytes 221192 | tf_op jit(solution)/shard_map/gate_y/ppermute | solution.py:60
  107.3 2.0 %own_rest.1.refs_2_.rest = bf16[2,256,256]{2,1,0:T(8,128)(2,1)S(1)} custom-call(s32[4]{0:T(128)S(1)} %pad_add_fusion.at, bf16[128,4608]{1,0:T(8,128)(2,1)S(1)} %fence.8.two.near, bf16[128,4608]{1,0:T(8,128)(2,1)S(1)} %collective-permute-done.19.refs_0_.two_s.near_s, bf16[128,4608]{1,0:T(8,128)(2,1)S(1)} %fence.9.three.more, ...), custom_call_target="tpu_custom_call" | custom-call | flops 1241513984 | bytes 7274496 | tf_op jit(solution)/shard_map/own_rest/pallas_call | solution.py:296
  109.3 0.9 collective-permute-done.27.fourth
  110.2 2.4 %collective-permute-start.29 = (f32[8,2304]{1,0:T(8,128)S(1)}, f32[8,2304]{1,0:T(8,128)S(1)}, u32[]{:S(2)}, u32[]{:S(2)}) collective-permute-start(f32[8,2304]{1,0:T(8,128)S(1)} %fence.11), channel_id=1, source_target_pairs={{0,1},{1,0},{2,3},{3,2},{4,5},{5,4},{6,7},{7,6},{8,9},{9,8},{10,11... | collective-permute-start | bytes 221192 | tf_op jit(solution)/shard_map/gate_core_back/ppermute | solution.py:60
  112.7 7.3 %collective-permute-done.30.last = bf16[256,256]{1,0:T(8,128)(2,1)S(1)} collective-permute-done((bf16[256,256]{1,0:T(8,128)(2,1)S(1)}, bf16[256,256]{1,0:T(8,128)(2,1)S(1)}, u32[]{:S(2)}, u32[]{:S(2)}) %collective-permute-start.30) | collective-permute-done | bytes 131104 | tf_op jit(solution)/shard_map/out_z_last/ppermute | solution.py:60
  120.0 1.6 %place.1 = bf16[4,2,2,128,256]{4,3,2,1,0:T(8,128)(2,1)} custom-call(s32[4]{0:T(128)S(1)} %pad_add_fusion.at, bf16[2,256,256]{2,1,0:T(8,128)(2,1)S(1)} %copy-done.5, bf16[2,256,256]{2,1,0:T(8,128)(2,1)S(1)} %own_rest.1.refs_2_.rest, bf16[3,256,256]{2,1,0:T(8,128)(2,1)S(1)} %collective-permute-done.28.refs_1_.got, ...), custom_call_target="tpu_custom_call" | custom-call | tf_op jit(solution)/shard_map/place/pallas_call | solution.py:403
  (62 shorter events, 7.2 us)
Async XLA Ops:
  0.6 32.0 %collective-permute-start.4 = (bf16[128,4608]{1,0:T(8,128)(2,1)}, bf16[128,4608]{1,0:T(8,128)(2,1)S(1)}, u32[]{:S(2)}, u32[]{:S(2)}) collective-permute-start(bf16[128,4608]{1,0:T(8,128)(2,1)} %own.1), channel_id=1, source_target_pairs={{0,1},{1,0},{2,3},{3,2},{4,5},{5,4},{6,7},{7,6},{8,9},{9,8},{10,11... | collective-permute-start | bytes 3538952 | tf_op jit(solution)/shard_map/tokens_core/ppermute | solution.py:60
  4.0 36.5 %collective-permute-start.6 = (bf16[128,4608]{1,0:T(8,128)(2,1)}, bf16[128,4608]{1,0:T(8,128)(2,1)S(1)}, u32[]{:S(2)}, u32[]{:S(2)}) collective-permute-start(bf16[128,4608]{1,0:T(8,128)(2,1)} %own.1), channel_id=1, source_target_pairs={{0,4},{1,13},{4,8},{5,1},{8,12},{9,5},{12,0},{13,9},{2,6},{3,15},{... | collective-permute-start | bytes 3538952 | tf_op jit(solution)/shard_map/tokens_y/ppermute | solution.py:27
  6.8 11.0 %copy-start.1 = (bf16[128,4608]{1,0:T(8,128)(2,1)S(1)}, bf16[128,4608]{1,0:T(8,128)(2,1)}, u32[]{:S(2)}) copy-start(bf16[128,4608]{1,0:T(8,128)(2,1)} %own.1) | copy-start | bytes 3538948
  7.7 32.8 %collective-permute-start.7 = (bf16[64,4736]{1,0:T(8,128)(2,1)}, bf16[64,4736]{1,0:T(8,128)(2,1)}, u32[]{:S(2)}, u32[]{:S(2)}) collective-permute-start(bf16[64,4736]{1,0:T(8,128)(2,1)} %pad_maximum_fusion), channel_id=1, source_target_pairs={{0,2},{2,0},{1,3},{3,1},{4,6},{6,4},{5,7},{7,5},{8,10},{10,8},{9,1... | collective-permute-start | bytes 1818632 | tf_op jit(solution)/shard_map/weight_z/ppermute | solution.py:60
  14.6 1.2 %copy-start.7 = (bf16[2048,256]{1,0:T(8,128)(2,1)S(1)}, bf16[2048,256]{1,0:T(8,128)(2,1)}, u32[]{:S(2)}) copy-start(bf16[2048,256]{1,0:T(8,128)(2,1)} %param.9) | copy-start | bytes 3145732
  15.9 0.8 copy-start.8
  17.7 5.5 %collective-permute-start = (bf16[4,2,128,128]{3,2,1,0:T(8,128)(2,1)S(1)}, bf16[4,2,128,128]{3,2,1,0:T(8,128)(2,1)S(1)}, u32[]{:S(2)}, u32[]{:S(2)}) collective-permute-start(bf16[4,2,128,128]{3,2,1,0:T(8,128)(2,1)S(1)} %get-tuple-element.22), channel_id=1, source_target_pairs={{0,1},{1,0},{2,3},{3,2},{4,5},{5,4},{6,7},{7,6},{8,9},{9,8},{10,11... | collective-permute-start | bytes 786440 | tf_op jit(solution)/shard_map/act_core/ppermute | solution.py:60
  17.8 1.3 %copy-start.2 = (bf16[128,4608]{1,0:T(8,128)(2,1)S(1)}, bf16[128,4608]{1,0:T(8,128)(2,1)}, u32[]{:S(2)}) copy-start(bf16[128,4608]{1,0:T(8,128)(2,1)} %hidden.3) | copy-start | bytes 3538948
  19.1 1.3 %copy-start.6 = (bf16[128,4608]{1,0:T(8,128)(2,1)S(1)}, bf16[128,4608]{1,0:T(8,128)(2,1)}, u32[]{:S(2)}) copy-start(bf16[128,4608]{1,0:T(8,128)(2,1)} %up.1) | copy-start | bytes 3538948
  20.3 0.9 copy-start.10
  23.8 4.1 %collective-permute-start.1 = (bf16[3,128,128]{2,1,0:T(8,128)(2,1)S(1)}, bf16[3,128,128]{2,1,0:T(8,128)(2,1)S(1)}, u32[]{:S(2)}, u32[]{:S(2)}) collective-permute-start(bf16[3,128,128]{2,1,0:T(8,128)(2,1)S(1)} %get-tuple-element.25), channel_id=1, source_target_pairs={{0,4},{4,0},{8,12},{12,8},{1,5},{5,1},{9,13},{13,9},{2,6},{6,2},{1... | collective-permute-start | bytes 294920 | tf_op jit(solution)/shard_map/act_y/ppermute | solution.py:60
  24.4 6.3 %collective-permute-start.2 = (bf16[3,128,128]{2,1,0:T(8,128)(2,1)S(1)}, bf16[3,128,128]{2,1,0:T(8,128)(2,1)S(1)}, u32[]{:S(2)}, u32[]{:S(2)}) collective-permute-start(bf16[3,128,128]{2,1,0:T(8,128)(2,1)S(1)} %get-tuple-element.26), channel_id=1, source_target_pairs={{0,8},{4,12},{8,0},{12,4},{1,9},{5,13},{9,1},{13,5},{2,10},{6,14},... | collective-permute-start | bytes 294920 | tf_op jit(solution)/shard_map/act_y/ppermute | solution.py:60
  27.9 4.7 %collective-permute-start.3 = (bf16[3,128,128]{2,1,0:T(8,128)(2,1)S(1)}, bf16[3,128,128]{2,1,0:T(8,128)(2,1)S(1)}, u32[]{:S(2)}, u32[]{:S(2)}) collective-permute-start(bf16[3,128,128]{2,1,0:T(8,128)(2,1)S(1)} %get-tuple-element.27), channel_id=1, source_target_pairs={{0,12},{4,8},{8,4},{12,0},{1,13},{5,9},{9,5},{13,1},{2,14},{6,10},... | collective-permute-start | bytes 294920 | tf_op jit(solution)/shard_map/act_y/ppermute | solution.py:60
  32.6 19.0 %copy-start = (bf16[256,4608]{1,0:T(8,128)(2,1)S(1)}, bf16[256,4608]{1,0:T(8,128)(2,1)}, u32[]{:S(2)}) copy-start(bf16[256,4608]{1,0:T(8,128)(2,1)} %weight.3) | copy-start | bytes 7077892
  33.2 18.4 %copy-start.9 = (bf16[256,128]{1,0:T(8,128)(2,1)S(1)}, bf16[256,128]{1,0:T(8,128)(2,1)}, u32[]{:S(2)}) copy-start(bf16[256,128]{1,0:T(8,128)(2,1)} %down.5) | copy-start | bytes 196612
  40.4 11.2 %collective-permute-start.8 = (bf16[128,4608]{1,0:T(8,128)(2,1)S(1)}, bf16[128,4608]{1,0:T(8,128)(2,1)S(1)}, u32[]{:S(2)}, u32[]{:S(2)}) collective-permute-start(bf16[128,4608]{1,0:T(8,128)(2,1)S(1)} %get-tuple-element.32.more.one), channel_id=1, source_target_pairs={{0,1},{1,0},{2,3},{3,2},{4,5},{5,4},{6,7},{7,6},{8,9},{9,8},{10,11... | collective-permute-start | bytes 3538952 | tf_op jit(solution)/shard_map/tokens_core/ppermute | solution.py:60
  40.4 15.0 %collective-permute-start.11 = (bf16[64,4736]{1,0:T(8,128)(2,1)}, bf16[64,4736]{1,0:T(8,128)(2,1)S(1)}, u32[]{:S(2)}, u32[]{:S(2)}) collective-permute-start(bf16[64,4736]{1,0:T(8,128)(2,1)} %get-tuple-element.36.refs_0_), channel_id=1, source_target_pairs={{0,64},{1,193},{64,0},{65,129},{128,192},{129,65},{192,128},{193,1... | collective-permute-start | bytes 1818632 | tf_op jit(solution)/shard_map/weight_x/ppermute | solution.py:33
  42.9 14.4 %collective-permute-start.12 = (bf16[64,4736]{1,0:T(8,128)(2,1)}, bf16[64,4736]{1,0:T(8,128)(2,1)S(1)}, u32[]{:S(2)}, u32[]{:S(2)}) collective-permute-start(bf16[64,4736]{1,0:T(8,128)(2,1)} %get-tuple-element.36.refs_0_), channel_id=1, source_target_pairs={{0,192},{1,65},{64,128},{65,1},{128,64},{129,193},{192,0},{193,129... | collective-permute-start | bytes 1818632 | tf_op jit(solution)/shard_map/weight_x/ppermute | solution.py:33
  42.9 23.7 %collective-permute-start.18 = (bf16[128,4608]{1,0:T(8,128)(2,1)S(1)}, bf16[128,4608]{1,0:T(8,128)(2,1)S(1)}, u32[]{:S(2)}, u32[]{:S(2)}) collective-permute-start(bf16[128,4608]{1,0:T(8,128)(2,1)S(1)} %get-tuple-element.32.more.one), channel_id=1, source_target_pairs={{0,4},{1,13},{4,8},{5,1},{8,12},{9,5},{12,0},{13,9},{2,6},{3,15},{... | collective-permute-start | bytes 3538952 | tf_op jit(solution)/shard_map/tokens_y/ppermute | solution.py:27
  44.1 9.5 %copy-start.3 = (bf16[128,4608]{1,0:T(8,128)(2,1)S(1)}, bf16[128,4608]{1,0:T(8,128)(2,1)}, u32[]{:S(2)}) copy-start(bf16[128,4608]{1,0:T(8,128)(2,1)} %hidden.3) | copy-start | bytes 3538948
  44.1 1.4 %collective-permute-start.9 = (bf16[4,128,128]{2,1,0:T(8,128)(2,1)S(1)}, bf16[4,128,128]{2,1,0:T(8,128)(2,1)S(1)}, u32[]{:S(2)}, u32[]{:S(2)}) collective-permute-start(bf16[4,128,128]{2,1,0:T(8,128)(2,1)S(1)} %get-tuple-element.33.mixed), channel_id=1, source_target_pairs={{0,1},{1,0},{2,3},{3,2},{4,5},{5,4},{6,7},{7,6},{8,9},{9,8},{10,11... | collective-permute-start | bytes 393224 | tf_op jit(solution)/shard_map/mixed_core/ppermute | solution.py:60
  45.5 8.1 %collective-permute-start.5 = (bf16[128,128]{1,0:T(8,128)(2,1)S(1)}, bf16[128,128]{1,0:T(8,128)(2,1)S(1)}, u32[]{:S(2)}, u32[]{:S(2)}) collective-permute-start(bf16[128,128]{1,0:T(8,128)(2,1)S(1)} %get-tuple-element.29.refs_2_.tie), channel_id=1, source_target_pairs={{0,2},{2,0},{1,3},{3,1},{4,6},{6,4},{5,7},{7,5},{8,10},{10,8},{9,1... | collective-permute-start | bytes 98312 | tf_op jit(solution)/shard_map/act_z/ppermute | solution.py:60
  53.6 3.7 %copy-start.4 = (bf16[2,256,256]{2,1,0:T(8,128)(2,1)}, bf16[2,256,256]{2,1,0:T(8,128)(2,1)S(1)}, u32[]{:S(2)}) copy-start(bf16[2,256,256]{2,1,0:T(8,128)(2,1)S(1)} %own_near.1.tie.near) | copy-start | bytes 786436
  54.9 2.5 %collective-permute-start.10 = (f32[8,2304]{1,0:T(8,128)S(1)}, f32[8,2304]{1,0:T(8,128)S(1)}, u32[]{:S(2)}, u32[]{:S(2)}) collective-permute-start(f32[8,2304]{1,0:T(8,128)S(1)} %get-tuple-element.35), channel_id=1, source_target_pairs={{0,1},{1,0},{2,3},{3,2},{4,5},{5,4},{6,7},{7,6},{8,9},{9,8},{10,11... | collective-permute-start | bytes 221192 | tf_op jit(solution)/shard_map/gate_core/ppermute | solution.py:60
  57.3 9.3 %collective-permute-start.16 = (bf16[64,4736]{1,0:T(8,128)(2,1)S(1)}, bf16[64,4736]{1,0:T(8,128)(2,1)S(1)}, u32[]{:S(2)}, u32[]{:S(2)}) collective-permute-start(bf16[64,4736]{1,0:T(8,128)(2,1)S(1)} %fence.7.refs_1_), channel_id=1, source_target_pairs={{0,192},{1,65},{64,128},{65,1},{128,64},{129,193},{192,0},{193,129... | collective-permute-start | bytes 1818632 | tf_op jit(solution)/shard_map/weight_x_far/ppermute | solution.py:33
  58.6 3.6 %collective-permute-start.13 = (f32[8,2304]{1,0:T(8,128)S(1)}, f32[8,2304]{1,0:T(8,128)S(1)}, u32[]{:S(2)}, u32[]{:S(2)}) collective-permute-start(f32[8,2304]{1,0:T(8,128)S(1)} %gate_sum.5.refs_1_.first), channel_id=1, source_target_pairs={{0,16},{16,0},{32,48},{48,32},{1,17},{17,1},{33,49},{49,33},{2,18}... | collective-permute-start | bytes 221192 | tf_op jit(solution)/shard_map/gate_zl/ppermute | solution.py:60
  60.0 5.2 %collective-permute-start.14 = (f32[8,2304]{1,0:T(8,128)S(1)}, f32[8,2304]{1,0:T(8,128)S(1)}, u32[]{:S(2)}, u32[]{:S(2)}) collective-permute-start(f32[8,2304]{1,0:T(8,128)S(1)} %gate_sum.5.refs_1_.first), channel_id=1, source_target_pairs={{0,32},{16,48},{32,0},{48,16},{1,33},{17,49},{33,1},{49,17},{2,34}... | collective-permute-start | bytes 221192 | tf_op jit(solution)/shard_map/gate_zl/ppermute | solution.py:60
  60.9 5.1 %collective-permute-start.15 = (f32[8,2304]{1,0:T(8,128)S(1)}, f32[8,2304]{1,0:T(8,128)S(1)}, u32[]{:S(2)}, u32[]{:S(2)}) collective-permute-start(f32[8,2304]{1,0:T(8,128)S(1)} %gate_sum.5.refs_1_.first), channel_id=1, source_target_pairs={{0,48},{16,32},{32,16},{48,0},{1,49},{17,33},{33,17},{49,1},{2,50}... | collective-permute-start | bytes 221192 | tf_op jit(solution)/shard_map/gate_zl/ppermute | solution.py:60
  66.7 12.1 %collective-permute-start.19 = (bf16[128,4608]{1,0:T(8,128)(2,1)S(1)}, bf16[128,4608]{1,0:T(8,128)(2,1)S(1)}, u32[]{:S(2)}, u32[]{:S(2)}) collective-permute-start(bf16[128,4608]{1,0:T(8,128)(2,1)S(1)} %fence.8.two.near), channel_id=1, source_target_pairs={{0,1},{1,0},{2,3},{3,2},{4,5},{5,4},{6,7},{7,6},{8,9},{9,8},{10,11... | collective-permute-start | bytes 3538952 | tf_op jit(solution)/shard_map/tokens_core/ppermute | solution.py:60
  70.1 15.3 %collective-permute-start.23 = (bf16[128,4608]{1,0:T(8,128)(2,1)S(1)}, bf16[128,4608]{1,0:T(8,128)(2,1)S(1)}, u32[]{:S(2)}, u32[]{:S(2)}) collective-permute-start(bf16[128,4608]{1,0:T(8,128)(2,1)S(1)} %fence.8.two.near), channel_id=1, source_target_pairs={{0,4},{1,13},{4,8},{5,1},{8,12},{9,5},{12,0},{13,9},{2,6},{3,15},{... | collective-permute-start | bytes 3538952 | tf_op jit(solution)/shard_map/tokens_y/ppermute | solution.py:27
  71.6 7.2 %collective-permute-start.17 = (f32[8,2304]{1,0:T(8,128)S(1)}, f32[8,2304]{1,0:T(8,128)S(1)}, u32[]{:S(2)}, u32[]{:S(2)}) collective-permute-start(f32[8,2304]{1,0:T(8,128)S(1)} %gate_sum.6.refs_1_.left), channel_id=1, source_target_pairs={{0,2},{2,0},{1,3},{3,1},{4,6},{6,4},{5,7},{7,5},{8,10},{10,8},{9,1... | collective-permute-start | bytes 221192 | tf_op jit(solution)/shard_map/gate_zh/ppermute | solution.py:60
  85.4 16.3 %collective-permute-start.24 = (bf16[128,4608]{1,0:T(8,128)(2,1)S(1)}, bf16[128,4608]{1,0:T(8,128)(2,1)S(1)}, u32[]{:S(2)}, u32[]{:S(2)}) collective-permute-start(bf16[128,4608]{1,0:T(8,128)(2,1)S(1)} %fence.9.three.more), channel_id=1, source_target_pairs={{0,1},{1,0},{2,3},{3,2},{4,5},{5,4},{6,7},{7,6},{8,9},{9,8},{10,11... | collective-permute-start | bytes 3538952 | tf_op jit(solution)/shard_map/tokens_core/ppermute | solution.py:60
  87.6 22.6 %collective-permute-start.28 = (bf16[3,256,256]{2,1,0:T(8,128)(2,1)S(1)}, bf16[3,256,256]{2,1,0:T(8,128)(2,1)S(1)}, u32[]{:S(2)}, u32[]{:S(2)}) collective-permute-start(bf16[3,256,256]{2,1,0:T(8,128)(2,1)S(1)} %get-tuple-element.37.refs_0_.refs_1_), channel_id=1, source_target_pairs={{0,2},{2,0},{1,3},{3,1},{4,6},{6,4},{5,7},{7,5},{8,10},{10,8},{9,1... | collective-permute-start | bytes 1179656 | tf_op jit(solution)/shard_map/out_z/ppermute | solution.py:60
  92.9 3.9 %collective-permute-start.20 = (f32[8,2304]{1,0:T(8,128)S(1)}, f32[8,2304]{1,0:T(8,128)S(1)}, u32[]{:S(2)}, u32[]{:S(2)}) collective-permute-start(f32[8,2304]{1,0:T(8,128)S(1)} %gate_sum.7.refs_4_.first), channel_id=1, source_target_pairs={{0,64},{64,0},{128,192},{192,128},{1,65},{65,1},{129,193},{193,129... | collective-permute-start | bytes 221192 | tf_op jit(solution)/shard_map/gate_x/ppermute | solution.py:60
  93.0 7.3 %collective-permute-start.21 = (f32[8,2304]{1,0:T(8,128)S(1)}, f32[8,2304]{1,0:T(8,128)S(1)}, u32[]{:S(2)}, u32[]{:S(2)}) collective-permute-start(f32[8,2304]{1,0:T(8,128)S(1)} %gate_sum.7.refs_4_.first), channel_id=1, source_target_pairs={{0,128},{64,192},{128,0},{192,64},{1,129},{65,193},{129,1},{193,65... | collective-permute-start | bytes 221192 | tf_op jit(solution)/shard_map/gate_x/ppermute | solution.py:60
  96.6 5.2 %collective-permute-start.22 = (f32[8,2304]{1,0:T(8,128)S(1)}, f32[8,2304]{1,0:T(8,128)S(1)}, u32[]{:S(2)}, u32[]{:S(2)}) collective-permute-start(f32[8,2304]{1,0:T(8,128)S(1)} %gate_sum.7.refs_4_.first), channel_id=1, source_target_pairs={{0,192},{64,128},{128,64},{192,0},{1,193},{65,129},{129,65},{193,1... | collective-permute-start | bytes 221192 | tf_op jit(solution)/shard_map/gate_x/ppermute | solution.py:60
  103.1 16.9 %collective-permute-start.30 = (bf16[256,256]{1,0:T(8,128)(2,1)S(1)}, bf16[256,256]{1,0:T(8,128)(2,1)S(1)}, u32[]{:S(2)}, u32[]{:S(2)}) collective-permute-start(bf16[256,256]{1,0:T(8,128)(2,1)S(1)} %far_products_last.1.refs_1_.tie), channel_id=1, source_target_pairs={{0,2},{2,0},{1,3},{3,1},{4,6},{6,4},{5,7},{7,5},{8,10},{10,8},{9,1... | collective-permute-start | bytes 393224 | tf_op jit(solution)/shard_map/out_z_last/ppermute | solution.py:60
  103.4 5.9 %collective-permute-start.25 = (f32[8,2304]{1,0:T(8,128)S(1)}, f32[8,2304]{1,0:T(8,128)S(1)}, u32[]{:S(2)}, u32[]{:S(2)}) collective-permute-start(f32[8,2304]{1,0:T(8,128)S(1)} %fence.10.first), channel_id=1, source_target_pairs={{0,4},{4,0},{8,12},{12,8},{1,5},{5,1},{9,13},{13,9},{2,6},{6,2},{1... | collective-permute-start | bytes 221192 | tf_op jit(solution)/shard_map/gate_y/ppermute | solution.py:60
  103.4 5.9 %collective-permute-start.26 = (f32[8,2304]{1,0:T(8,128)S(1)}, f32[8,2304]{1,0:T(8,128)S(1)}, u32[]{:S(2)}, u32[]{:S(2)}) collective-permute-start(f32[8,2304]{1,0:T(8,128)S(1)} %fence.10.first), channel_id=1, source_target_pairs={{0,8},{4,12},{8,0},{12,4},{1,9},{5,13},{9,1},{13,5},{2,10},{6,14},... | collective-permute-start | bytes 221192 | tf_op jit(solution)/shard_map/gate_y/ppermute | solution.py:60
  104.7 5.5 %collective-permute-start.27 = (f32[8,2304]{1,0:T(8,128)S(1)}, f32[8,2304]{1,0:T(8,128)S(1)}, u32[]{:S(2)}, u32[]{:S(2)}) collective-permute-start(f32[8,2304]{1,0:T(8,128)S(1)} %fence.10.first), channel_id=1, source_target_pairs={{0,12},{4,8},{8,4},{12,0},{1,13},{5,9},{9,5},{13,1},{2,14},{6,10},... | collective-permute-start | bytes 221192 | tf_op jit(solution)/shard_map/gate_y/ppermute | solution.py:60
  109.3 10.7 %copy-start.5 = (bf16[2,256,256]{2,1,0:T(8,128)(2,1)S(1)}, bf16[2,256,256]{2,1,0:T(8,128)(2,1)}, u32[]{:S(2)}) copy-start(bf16[2,256,256]{2,1,0:T(8,128)(2,1)} %copy-done.4) | copy-start | bytes 786436
  110.2 11.4 %collective-permute-start.29 = (f32[8,2304]{1,0:T(8,128)S(1)}, f32[8,2304]{1,0:T(8,128)S(1)}, u32[]{:S(2)}, u32[]{:S(2)}) collective-permute-start(f32[8,2304]{1,0:T(8,128)S(1)} %fence.11), channel_id=1, source_target_pairs={{0,1},{1,0},{2,3},{3,2},{4,5},{5,4},{6,7},{7,6},{8,9},{9,8},{10,11... | collective-permute-start | bytes 221192 | tf_op jit(solution)/shard_map/gate_core_back/ppermute | solution.py:60

commit v9 on v8

--- a/solution.py
+++ b/solution.py
@@ -149,7 +149,10 @@
 
 
 def add4_kernel(first, second, third, fourth, *refs):
-    refs[-1][...] = (first[...] + second[...]) + (third[...] + fourth[...])
+    own = first[...].astype(second.dtype).astype(F32)
+    refs[-1][...] = (own + second[...].astype(F32)) + (
+        third[...].astype(F32) + fourth[...].astype(F32)
+    )
 
 
 def rows_product(at, steps, refs, mixed, weights, downs, out):
@@ -177,7 +180,7 @@
         rows_product(at, steps, group, (mixed, mixed_s), weight, down, out.at[steps])
 
 
-def far_last_kernel(at, three, three_s, mixed, mixed_s, weight, down, out):
+def far_last_kernel(at, three, three_s, mixed, mixed_s, weight, down, tie, out):
     rows_product(at, 3, (three, three_s), (mixed, mixed_s), weight, down, out)
 
 
@@ -334,9 +337,9 @@
         name="gate_sum",
         )(*parts)
 
-    def step(total, axis, *ties):
+    def step(total, axis, *ties, dtype=F32):
         with jax.named_scope("gate_" + axis):
-            got = [swap(total, axis, mask) for mask in (1, 2, 3)]
+            got = [swap(total.astype(dtype), axis, mask) for mask in (1, 2, 3)]
         return add4(total, *got, *ties)
 
     with jax.named_scope("gate_core"):
@@ -345,15 +348,12 @@
     (w_first,) = fence((w_first,), total)
     with jax.named_scope("weight_x_far"):
         w_far = pairs(w_first, "x", False)
-    total = step(total, "zl", mixed_s, w_far)
-    (two,) = fence((two,), total)
+    (two,) = fence((two,), w_first)
     with jax.named_scope("tokens_y"):
         three = ring(two, "y")
+    total = step(total, "zl", mixed_s, w_far, two, dtype=BF16)
     with jax.named_scope("tokens_core"):
         two_s = swap(two, "c", 1)
-    with jax.named_scope("gate_zh"):
-        got = swap(total, "zh", 1)
-    total = add(total, got, two_s, w_far)
 
     far, far_weight, far_down = pl.pallas_call(
         far_kernel,
@@ -373,27 +373,28 @@
     )
     with jax.named_scope("out_z"):
         far_got = swap(far, "zh", 1)
-    (three,) = fence((three,), far)
+    total = step(total, "x", far)
+    (three,) = fence((three,), total)
     with jax.named_scope("tokens_core"):
         three_s = swap(three, "c", 1)
-    total = step(total, "x", far)
-
+
+    total = step(total, "y")
     last = pl.pallas_call(
         far_last_kernel,
-        in_specs=[SMEM] + [VMEM] * 6,
+        in_specs=[SMEM] + [VMEM] * 6 + [ANY],
         out_specs=VMEM,
         out_shape=shaped((2 * tokens, features), BF16),
         cost_estimate=cost(4 * tokens * depth * features, 6 * tokens * depth),
         compiler_params=MIDDLE,
         name="far_products_last",
-    )(at, three, three_s, all_mixed, mixed_s, far_weight, far_down)
+    )(at, three, three_s, all_mixed, mixed_s, far_weight, far_down, total)
     with jax.named_scope("out_z_last"):
         last_got = swap(last, "zh", 1)
 
-    (total,) = fence((total,), last)
-    total = step(total, "y")
-    own_rest = products("own_rest", 2, two, two_s, three, three_s, weight, down, last)
-    (total,) = fence((total,), far_got, own_rest)
+    own_rest = products("own_rest", 2, two, two_s, three, three_s, weight, down, far)
+    with jax.named_scope("gate_zh"):
+        got = swap(total, "zh", 1)
+    total = add(total, got, last, far_got)
     with jax.named_scope("gate_core_back"):
         other = swap(total, "c", 1)
     gate_grad = jnp.where(

time: 123 us -> 122 us (level)
  waiting for transfers between devices: 39 us -> 27.8 us
  Pallas kernels: 15.8 us -> 22.5 us
  local copies, waits for them, and re-layouts: 7.34 us -> 13.8 us
  starting transfers between devices: 57.6 us -> 54.9 us
    ppermute x25, waiting for transfers between devices: 33.2 us -> 26.7 us  [swap(): return lax.ppermute(value, axis, [(i, i ^ mask) for i in range(size)])]
    unnamed x22 -> x56, local copies, waits for them, and re-layouts: 5.51 us -> 11.8 us
    ppermute x3, waiting for transfers between devices: 3.32 us -> 0.01 us  [ring(): return lax.ppermute(value, (axis, 'c'), pairs)]
    ppermute x25, starting transfers between devices: 50.2 us -> 47.4 us  [swap(): return lax.ppermute(value, axis, [(i, i ^ mask) for i in range(size)])]
    pallas_call x2, Pallas kernels: 3.98 us -> 5.9 us  [products(): pl.pallas_call(functools.partial(product_kernel, first), in_specs=[SMEM]...]
    pallas_call x1, Pallas kernels: 3.36 us -> 4.89 us  [on_device(): pl.pallas_call(far_kernel, in_specs=[SMEM] + [VMEM] * 12 + [ANY], out_spe...]
    ppermute x3, waiting for transfers between devices: 2.56 us -> 1.08 us  [pairs(): lax.ppermute(value, (axis, 'c'), [(2 * i + c, 2 * partner(i, c) + c) for...]
  transfers between devices with their start and end apart: 31 -> 31, of which waited for: 15 -> 12; matrix products, arithmetic and copies ran while one was open for 2% -> 3% of each run, Pallas kernels for 13% -> 17%
where the time goes in v9:
time: 122 us
  starting transfers between devices  54.9 us (45%)
  waiting for transfers between devices  27.8 us (23%)
  Pallas kernels  22.5 us (18%)
  local copies, waits for them, and re-layouts  13.8 us (11%)
  other arithmetic  1.62 us (1%)
    ppermute x25, starting transfers between devices, swap(): return lax.ppermute(value, axis, [(i, i ^ mask) for i in range(size)])  47.4 us
    ppermute x25, waiting for transfers between devices, swap(): return lax.ppermute(value, axis, [(i, i ^ mask) for i in range(size)])  26.7 us
    unnamed x56, local copies, waits for them, and re-layouts  11.8 us
    pallas_call x2, Pallas kernels, products(): pl.pallas_call(functools.partial(product_kernel, first), in_specs=[SMEM]...  5.9 us
    pallas_call x1, Pallas kernels, on_device(): pl.pallas_call(far_kernel, in_specs=[SMEM] + [VMEM] * 12 + [ANY], out_spe...  4.89 us
    ppermute x3, starting transfers between devices, ring(): return lax.ppermute(value, (axis, 'c'), pairs)  4.74 us
    ppermute x3, starting transfers between devices, pairs(): lax.ppermute(value, (axis, 'c'), [(2 * i + c, 2 * partner(i, c) + c) for...  2.79 us
    pallas_call x1, Pallas kernels, on_device(): pl.pallas_call(far_last_kernel, in_specs=[SMEM] + [VMEM] * 6 + [ANY], out...  2.56 us
  transfers between devices with their start and end apart: 31, of which 12 were waited for; matrix products, arithmetic and copies ran while one was open for 3% of the time, Pallas kernels for 17%

profile of v9, /device:TPU:1, one launch (start us, length us, event | category | flops | bytes accessed | tf_op | source)
XLA Modules:
  0.0 121.7 jit_solution(889604429797962724)
XLA Ops:
  0.6 3.3 %collective-permute-start.4 = (bf16[128,4608]{1,0:T(8,128)(2,1)}, bf16[128,4608]{1,0:T(8,128)(2,1)S(1)}, u32[]{:S(2)}, u32[]{:S(2)}) collective-permute-start(bf16[128,4608]{1,0:T(8,128)(2,1)} %own.1), channel_id=1, source_target_pairs={{0,1},{1,0},{2,3},{3,2},{4,5},{5,4},{6,7},{7,6},{8,9},{9,8},{10,11... | collective-permute-start | bytes 3538952 | tf_op jit(solution)/shard_map/tokens_core/ppermute | solution.py:60
  4.0 1.0 collective-permute-start.6
  5.0 1.1 constant_dynamic-slice_fusion.1
  6.9 0.9 pad_maximum_fusion
  7.8 6.9 %collective-permute-start.7 = (bf16[64,4736]{1,0:T(8,128)(2,1)}, bf16[64,4736]{1,0:T(8,128)(2,1)}, u32[]{:S(2)}, u32[]{:S(2)}) collective-permute-start(bf16[64,4736]{1,0:T(8,128)(2,1)} %pad_maximum_fusion), channel_id=1, source_target_pairs={{0,2},{2,0},{1,3},{3,1},{4,6},{6,4},{5,7},{7,5},{8,10},{10,8},{9,1... | collective-permute-start | bytes 1818632 | tf_op jit(solution)/shard_map/weight_z/ppermute | solution.py:60
  14.7 1.2 %copy-done.21 = bf16[2048,256]{1,0:T(8,128)(2,1)S(1)} copy-done((bf16[2048,256]{1,0:T(8,128)(2,1)S(1)}, bf16[2048,256]{1,0:T(8,128)(2,1)}, u32[]{:S(2)}) %copy-start.21) | copy-done | bytes 1048600
  16.8 1.0 rank_products.1
  17.9 1.3 %copy-done.20 = bf16[128,4608]{1,0:T(8,128)(2,1)S(1)} copy-done((bf16[128,4608]{1,0:T(8,128)(2,1)S(1)}, bf16[128,4608]{1,0:T(8,128)(2,1)}, u32[]{:S(2)}) %copy-start.20) | copy-done | bytes 1179672
  19.2 0.9 copy-done.25
  20.1 2.0 %token_values.1 = (bf16[128,128]{1,0:T(8,128)(2,1)S(1)}, f32[8,128]{1,0:T(8,128)S(1)}, f32[128,128]{1,0:T(8,128)S(1)}) custom-call(s32[4]{0:T(128)S(1)} %pad_add_fusion.at, bf16[128,4608]{1,0:T(8,128)(2,1)S(1)} %copy-done.6, bf16[128,4608]{1,0:T(8,128)(2,1)S(1)} %copy-done.4, bf16[128,4608]{1,0:T(8,128)(2,1)S(1)} %copy-done.20, bf16[8,4608]{1,0:T(8,128)(2,1)S(1)} %copy-done.25), custom_call_target="tpu_custom_call" | custom-call | flops 452984832 | bytes 7077888 | tf_op jit(solution)/shard_map/token_values/pallas_call | solution.py:248
  23.3 1.4 %collective-permute-start.2 = (bf16[3,128,128]{2,1,0:T(8,128)(2,1)S(1)}, bf16[3,128,128]{2,1,0:T(8,128)(2,1)S(1)}, u32[]{:S(2)}, u32[]{:S(2)}) collective-permute-start(bf16[3,128,128]{2,1,0:T(8,128)(2,1)S(1)} %get-tuple-element.26), channel_id=1, source_target_pairs={{0,8},{4,12},{8,0},{12,4},{1,9},{5,13},{9,1},{13,5},{2,10},{6,14},... | collective-permute-start | bytes 294920 | tf_op jit(solution)/shard_map/act_y/ppermute | solution.py:60
  24.7 2.1 %collective-permute-done.1.first = bf16[3,128,128]{2,1,0:T(8,128)(2,1)S(1)} collective-permute-done((bf16[3,128,128]{2,1,0:T(8,128)(2,1)S(1)}, bf16[3,128,128]{2,1,0:T(8,128)(2,1)S(1)}, u32[]{:S(2)}, u32[]{:S(2)}) %collective-permute-start.1) | collective-permute-done | bytes 98336 | tf_op jit(solution)/shard_map/act_y/ppermute | solution.py:60
  27.6 2.0 %collective-permute-done.2.second = bf16[3,128,128]{2,1,0:T(8,128)(2,1)S(1)} collective-permute-done((bf16[3,128,128]{2,1,0:T(8,128)(2,1)S(1)}, bf16[3,128,128]{2,1,0:T(8,128)(2,1)S(1)}, u32[]{:S(2)}, u32[]{:S(2)}) %collective-permute-start.2) | collective-permute-done | bytes 98336 | tf_op jit(solution)/shard_map/act_y/ppermute | solution.py:60
  29.6 1.8 %collective-permute-done.3.third = bf16[3,128,128]{2,1,0:T(8,128)(2,1)S(1)} collective-permute-done((bf16[3,128,128]{2,1,0:T(8,128)(2,1)S(1)}, bf16[3,128,128]{2,1,0:T(8,128)(2,1)S(1)}, u32[]{:S(2)}, u32[]{:S(2)}) %collective-permute-start.3) | collective-permute-done | bytes 98336 | tf_op jit(solution)/shard_map/act_y/ppermute | solution.py:60
  32.1 8.5 %collective-permute-done.7.refs_1_ = bf16[64,4736]{1,0:T(8,128)(2,1)} collective-permute-done((bf16[64,4736]{1,0:T(8,128)(2,1)}, bf16[64,4736]{1,0:T(8,128)(2,1)}, u32[]{:S(2)}, u32[]{:S(2)}) %collective-permute-start.7) | collective-permute-done | bytes 606240 | tf_op jit(solution)/shard_map/weight_z/ppermute | solution.py:60
  40.5 1.2 collective-permute-start.17
  41.7 2.5 %collective-permute-start.11 = (bf16[64,4736]{1,0:T(8,128)(2,1)}, bf16[64,4736]{1,0:T(8,128)(2,1)S(1)}, u32[]{:S(2)}, u32[]{:S(2)}) collective-permute-start(bf16[64,4736]{1,0:T(8,128)(2,1)} %get-tuple-element.36.refs_0_), channel_id=1, source_target_pairs={{0,64},{1,193},{64,0},{65,129},{128,192},{129,65},{192,128},{193,1... | collective-permute-start | bytes 1818632 | tf_op jit(solution)/shard_map/weight_x/ppermute | solution.py:33
  44.6 1.0 collective-permute-done.9.mixed_s.refs_0_
  45.6 6.1 %collective-permute-start.5 = (bf16[128,128]{1,0:T(8,128)(2,1)S(1)}, bf16[128,128]{1,0:T(8,128)(2,1)S(1)}, u32[]{:S(2)}, u32[]{:S(2)}) collective-permute-start(bf16[128,128]{1,0:T(8,128)(2,1)S(1)} %get-tuple-element.29.refs_2_.tie), channel_id=1, source_target_pairs={{0,2},{2,0},{1,3},{3,1},{4,6},{6,4},{5,7},{7,5},{8,10},{10,8},{9,1... | collective-permute-start | bytes 98312 | tf_op jit(solution)/shard_map/act_z/ppermute | solution.py:60
  51.7 1.3 %copy-done.2 = bf16[128,4608]{1,0:T(8,128)(2,1)S(1)} copy-done((bf16[128,4608]{1,0:T(8,128)(2,1)S(1)}, bf16[128,4608]{1,0:T(8,128)(2,1)}, u32[]{:S(2)}) %copy-start.2) | copy-done | bytes 1179672
  53.0 2.8 %own_near.1.tie.near = bf16[2,256,256]{2,1,0:T(8,128)(2,1)S(1)} custom-call(s32[4]{0:T(128)S(1)} %pad_add_fusion.at, bf16[128,4608]{1,0:T(8,128)(2,1)S(1)} %copy-done.5, bf16[128,4608]{1,0:T(8,128)(2,1)S(1)} %copy-done.2, bf16[128,4608]{1,0:T(8,128)(2,1)} %get-tuple-element.32.more.one, bf16[128,4608]{1,0:T(8,128)(2,1)S(1)} %collective-permute-done.8.more_s.one_s, ...), custom_call_target="tpu_custom_call" | custom-call | flops 1241513984 | bytes 7274496 | tf_op jit(solution)/shard_map/own_near/pallas_call | solution.py:299
  55.8 1.2 %gate_products.1 = (f32[8,2304]{1,0:T(8,128)S(1)}, f32[8,2304]{1,0:T(8,128)S(1)}) custom-call(s32[4]{0:T(128)S(1)} %pad_add_fusion.at, f32[128,128]{1,0:T(8,128)S(1)} %get-tuple-element.28.keep, bf16[128,128]{1,0:T(8,128)(2,1)S(1)} %collective-permute-done.5.got, f32[128,128]{1,0:T(8,128)S(1)} %get-tuple-element.30.back, ...), custom_call_target="tpu_custom_call" | custom-call | tf_op jit(solution)/shard_map/gate_products/pallas_call | solution.py:311
  57.6 0.9 collective-permute-done.10.right
  59.4 2.6 %collective-permute-start.26 = (bf16[128,4608]{1,0:T(8,128)(2,1)S(1)}, bf16[128,4608]{1,0:T(8,128)(2,1)}, u32[]{:S(2)}, u32[]{:S(2)}) collective-permute-start(bf16[128,4608]{1,0:T(8,128)(2,1)S(1)} %fence.6.refs_2_.two.near), channel_id=1, source_target_pairs={{0,4},{1,13},{4,8},{5,1},{8,12},{9,5},{12,0},{13,9},{2,6},{3,15},{... | collective-permute-start | bytes 3538952 | tf_op jit(solution)/shard_map/tokens_y/ppermute | solution.py:27
  62.3 1.1 collective-permute-start.13
  63.8 1.6 %collective-permute-done.13.second = bf16[8,2304]{1,0:T(8,128)(2,1)S(1)} collective-permute-done((bf16[8,2304]{1,0:T(8,128)(2,1)S(1)}, bf16[8,2304]{1,0:T(8,128)(2,1)S(1)}, u32[]{:S(2)}, u32[]{:S(2)}) %collective-permute-start.13) | collective-permute-done | bytes 36896 | tf_op jit(solution)/shard_map/gate_zl/ppermute | solution.py:60
  65.5 1.2 collective-permute-start.15
  66.7 1.2 collective-permute-done.14.third
  67.8 2.4 %collective-permute-done.15.fourth = bf16[8,2304]{1,0:T(8,128)(2,1)S(1)} collective-permute-done((bf16[8,2304]{1,0:T(8,128)(2,1)S(1)}, bf16[8,2304]{1,0:T(8,128)(2,1)S(1)}, u32[]{:S(2)}, u32[]{:S(2)}) %collective-permute-start.15) | collective-permute-done | bytes 36896 | tf_op jit(solution)/shard_map/gate_zl/ppermute | solution.py:60
  70.2 1.1 collective-permute-done.16.refs_1_.refs_3_
  71.7 1.7 %collective-permute-start.19 = (f32[8,2304]{1,0:T(8,128)S(1)}, f32[8,2304]{1,0:T(8,128)S(1)}, u32[]{:S(2)}, u32[]{:S(2)}) collective-permute-start(f32[8,2304]{1,0:T(8,128)S(1)} %gate_sum.6.refs_4_.first), channel_id=1, source_target_pairs={{0,128},{64,192},{128,0},{192,64},{1,129},{65,193},{129,1},{193,65... | collective-permute-start | bytes 221192 | tf_op jit(solution)/shard_map/gate_x/ppermute | solution.py:60
  73.4 1.8 %collective-permute-start.20 = (f32[8,2304]{1,0:T(8,128)S(1)}, f32[8,2304]{1,0:T(8,128)S(1)}, u32[]{:S(2)}, u32[]{:S(2)}) collective-permute-start(f32[8,2304]{1,0:T(8,128)S(1)} %gate_sum.6.refs_4_.first), channel_id=1, source_target_pairs={{0,192},{64,128},{128,64},{192,0},{1,193},{65,129},{129,65},{193,1... | collective-permute-start | bytes 221192 | tf_op jit(solution)/shard_map/gate_x/ppermute | solution.py:60
  75.3 4.9 %far_products.1 = (bf16[3,256,256]{2,1,0:T(8,128)(2,1)}, bf16[256,4608]{1,0:T(8,128)(2,1)S(1)}, bf16[256,128]{1,0:T(8,128)(2,1)S(1)}) custom-call(s32[4]{0:T(128)S(1)} %pad_add_fusion.at, bf16[128,4608]{1,0:T(8,128)(2,1)S(1)} %copy-done.5, bf16[128,4608]{1,0:T(8,128)(2,1)S(1)} %copy-done.3, bf16[128,4608]{1,0:T(8,128)(2,1)} %get-tuple-element.32.more.one, ...), custom_call_target="tpu_custom_call" | custom-call | flops 1862270976 | bytes 10911744 | tf_op jit(solution)/shard_map/far_products/pallas_call | solution.py:358
  80.9 1.3 %copy-done.15 = bf16[256,4608]{1,0:T(8,128)(2,1)} copy-done((bf16[256,4608]{1,0:T(8,128)(2,1)}, bf16[256,4608]{1,0:T(8,128)(2,1)S(1)}, u32[]{:S(2)}) %copy-start.15) | copy-done | bytes 2359320
  82.2 2.4 %collective-permute-start.27 = (bf16[128,4608]{1,0:T(8,128)(2,1)}, bf16[128,4608]{1,0:T(8,128)(2,1)}, u32[]{:S(2)}, u32[]{:S(2)}) collective-permute-start(bf16[128,4608]{1,0:T(8,128)(2,1)} %fence.7.three.more), channel_id=1, source_target_pairs={{0,1},{1,0},{2,3},{3,2},{4,5},{5,4},{6,7},{7,6},{8,9},{9,8},{10,11... | collective-permute-start | bytes 3538952 | tf_op jit(solution)/shard_map/tokens_core/ppermute | solution.py:60
  84.6 6.2 %collective-permute-start.28 = (bf16[3,256,256]{2,1,0:T(8,128)(2,1)}, bf16[3,256,256]{2,1,0:T(8,128)(2,1)}, u32[]{:S(2)}, u32[]{:S(2)}) collective-permute-start(bf16[3,256,256]{2,1,0:T(8,128)(2,1)} %get-tuple-element.37.refs_0_.tie), channel_id=1, source_target_pairs={{0,2},{2,0},{1,3},{3,1},{4,6},{6,4},{5,7},{7,5},{8,10},{10,8},{9,1... | collective-permute-start | bytes 1179656 | tf_op jit(solution)/shard_map/out_z/ppermute | solution.py:60
  90.8 3.8 %collective-permute-start.23 = (f32[8,2304]{1,0:T(8,128)S(1)}, f32[8,2304]{1,0:T(8,128)S(1)}, u32[]{:S(2)}, u32[]{:S(2)}) collective-permute-start(f32[8,2304]{1,0:T(8,128)S(1)} %gate_sum.7.first.refs_1_), channel_id=1, source_target_pairs={{0,8},{4,12},{8,0},{12,4},{1,9},{5,13},{9,1},{13,5},{2,10},{6,14},... | collective-permute-start | bytes 221192 | tf_op jit(solution)/shard_map/gate_y/ppermute | solution.py:60
  94.7 3.7 %collective-permute-done.23.third = f32[8,2304]{1,0:T(8,128)S(1)} collective-permute-done((f32[8,2304]{1,0:T(8,128)S(1)}, f32[8,2304]{1,0:T(8,128)S(1)}, u32[]{:S(2)}, u32[]{:S(2)}) %collective-permute-start.23) | collective-permute-done | bytes 73760 | tf_op jit(solution)/shard_map/gate_y/ppermute | solution.py:60
  98.4 1.5 %collective-permute-done.24.fourth = f32[8,2304]{1,0:T(8,128)S(1)} collective-permute-done((f32[8,2304]{1,0:T(8,128)S(1)}, f32[8,2304]{1,0:T(8,128)S(1)}, u32[]{:S(2)}, u32[]{:S(2)}) %collective-permute-start.24) | collective-permute-done | bytes 73760 | tf_op jit(solution)/shard_map/gate_y/ppermute | solution.py:60
  100.8 0.9 copy-done.11
  101.7 1.7 %copy-done.16 = bf16[256,4608]{1,0:T(8,128)(2,1)S(1)} copy-done((bf16[256,4608]{1,0:T(8,128)(2,1)S(1)}, bf16[256,4608]{1,0:T(8,128)(2,1)}, u32[]{:S(2)}) %copy-start.16) | copy-done | bytes 2359320
  103.4 0.9 copy-done.18
  105.1 2.6 %far_products_last.1.refs_0_ = bf16[256,256]{1,0:T(8,128)(2,1)S(1)} custom-call(s32[4]{0:T(128)S(1)} %pad_add_fusion.at, bf16[128,4608]{1,0:T(8,128)(2,1)} %fence.7.three.more, bf16[128,4608]{1,0:T(8,128)(2,1)} %collective-permute-done.27.three_s.more_s, bf16[4,128,128]{2,1,0:T(8,128)(2,1)S(1)} %copy-done.18, bf16[4,128,128]{2,1,0:T(8,128)(2,1)S(1)} %copy-done.11, ...), custom_call_target="tpu_custom_call" | custom-call | flops 620756992 | bytes 3637248 | tf_op jit(solution)/shard_map/far_products_last/pallas_call | solution.py:382
  107.7 5.2 %collective-permute-start.30 = (bf16[256,256]{1,0:T(8,128)(2,1)S(1)}, bf16[256,256]{1,0:T(8,128)(2,1)S(1)}, u32[]{:S(2)}, u32[]{:S(2)}) collective-permute-start(bf16[256,256]{1,0:T(8,128)(2,1)S(1)} %far_products_last.1.refs_0_), channel_id=1, source_target_pairs={{0,2},{2,0},{1,3},{3,1},{4,6},{6,4},{5,7},{7,5},{8,10},{10,8},{9,1... | collective-permute-start | bytes 393224 | tf_op jit(solution)/shard_map/out_z_last/ppermute | solution.py:60
  112.9 0.9 gate_sum.9
  113.8 1.8 %collective-permute-start.29 = (f32[8,2304]{1,0:T(8,128)S(1)}, f32[8,2304]{1,0:T(8,128)S(1)}, u32[]{:S(2)}, u32[]{:S(2)}) collective-permute-start(f32[8,2304]{1,0:T(8,128)S(1)} %gate_sum.9), channel_id=1, source_target_pairs={{0,1},{1,0},{2,3},{3,2},{4,5},{5,4},{6,7},{7,6},{8,9},{9,8},{10,11... | collective-permute-start | bytes 221192 | tf_op jit(solution)/shard_map/gate_core_back/ppermute | solution.py:60
  115.6 3.1 %own_rest.1.rest = bf16[2,256,256]{2,1,0:T(8,128)(2,1)S(1)} custom-call(s32[4]{0:T(128)S(1)} %pad_add_fusion.at, bf16[128,4608]{1,0:T(8,128)(2,1)S(1)} %fence.6.refs_2_.two.near, bf16[128,4608]{1,0:T(8,128)(2,1)S(1)} %copy-done.9, bf16[128,4608]{1,0:T(8,128)(2,1)} %fence.7.three.more, bf16[128,4608]{1,0:T(8,128)(2,1)} %collective-permute-done.27.three_s.more_s, ...), custom_call_target="tpu_custom_call" | custom-call | flops 1241513984 | bytes 7274496 | tf_op jit(solution)/shard_map/own_rest/pallas_call | solution.py:299
  119.4 2.1 %place.1 = bf16[4,2,2,128,256]{4,3,2,1,0:T(8,128)(2,1)} custom-call(s32[4]{0:T(128)S(1)} %pad_add_fusion.at, bf16[2,256,256]{2,1,0:T(8,128)(2,1)S(1)} %copy-done.14, bf16[2,256,256]{2,1,0:T(8,128)(2,1)S(1)} %own_rest.1.rest, bf16[3,256,256]{2,1,0:T(8,128)(2,1)} %collective-permute-done.28.refs_1_.got, bf16[256,256]{1,0:T(8,128)(2,1)S(1)} %collective-permute-done.30.last), custom_call_target="tpu_custom_call" | custom-call | tf_op jit(solution)/shard_map/place/pallas_call | solution.py:404
  (95 shorter events, 10.7 us)
Async XLA Ops:
  0.6 30.8 %collective-permute-start.4 = (bf16[128,4608]{1,0:T(8,128)(2,1)}, bf16[128,4608]{1,0:T(8,128)(2,1)S(1)}, u32[]{:S(2)}, u32[]{:S(2)}) collective-permute-start(bf16[128,4608]{1,0:T(8,128)(2,1)} %own.1), channel_id=1, source_target_pairs={{0,1},{1,0},{2,3},{3,2},{4,5},{5,4},{6,7},{7,6},{8,9},{9,8},{10,11... | collective-permute-start | bytes 3538952 | tf_op jit(solution)/shard_map/tokens_core/ppermute | solution.py:60
  4.0 36.6 %collective-permute-start.6 = (bf16[128,4608]{1,0:T(8,128)(2,1)}, bf16[128,4608]{1,0:T(8,128)(2,1)}, u32[]{:S(2)}, u32[]{:S(2)}) collective-permute-start(bf16[128,4608]{1,0:T(8,128)(2,1)} %own.1), channel_id=1, source_target_pairs={{0,4},{1,13},{4,8},{5,1},{8,12},{9,5},{12,0},{13,9},{2,6},{3,15},{... | collective-permute-start | bytes 3538952 | tf_op jit(solution)/shard_map/tokens_y/ppermute | solution.py:27
  6.1 11.8 %copy-start.6 = (bf16[128,4608]{1,0:T(8,128)(2,1)S(1)}, bf16[128,4608]{1,0:T(8,128)(2,1)}, u32[]{:S(2)}) copy-start(bf16[128,4608]{1,0:T(8,128)(2,1)} %hidden.3) | copy-start | bytes 3538948
  6.9 11.0 %copy-start.4 = (bf16[128,4608]{1,0:T(8,128)(2,1)S(1)}, bf16[128,4608]{1,0:T(8,128)(2,1)}, u32[]{:S(2)}) copy-start(bf16[128,4608]{1,0:T(8,128)(2,1)} %own.1) | copy-start | bytes 3538948
  7.8 32.8 %collective-permute-start.7 = (bf16[64,4736]{1,0:T(8,128)(2,1)}, bf16[64,4736]{1,0:T(8,128)(2,1)}, u32[]{:S(2)}, u32[]{:S(2)}) collective-permute-start(bf16[64,4736]{1,0:T(8,128)(2,1)} %pad_maximum_fusion), channel_id=1, source_target_pairs={{0,2},{2,0},{1,3},{3,1},{4,6},{6,4},{5,7},{7,5},{8,10},{10,8},{9,1... | collective-permute-start | bytes 1818632 | tf_op jit(solution)/shard_map/weight_z/ppermute | solution.py:60
  17.8 4.3 %collective-permute-start = (bf16[4,2,128,128]{3,2,1,0:T(8,128)(2,1)S(1)}, bf16[4,2,128,128]{3,2,1,0:T(8,128)(2,1)S(1)}, u32[]{:S(2)}, u32[]{:S(2)}) collective-permute-start(bf16[4,2,128,128]{3,2,1,0:T(8,128)(2,1)S(1)} %get-tuple-element.22), channel_id=1, source_target_pairs={{0,1},{1,0},{2,3},{3,2},{4,5},{5,4},{6,7},{7,6},{8,9},{9,8},{10,11... | collective-permute-start | bytes 786440 | tf_op jit(solution)/shard_map/act_core/ppermute | solution.py:60
  22.1 29.6 %copy-start.5 = (bf16[128,4608]{1,0:T(8,128)(2,1)S(1)}, bf16[128,4608]{1,0:T(8,128)(2,1)}, u32[]{:S(2)}) copy-start(bf16[128,4608]{1,0:T(8,128)(2,1)} %own.1) | copy-start | bytes 3538948
  22.7 4.1 %collective-permute-start.1 = (bf16[3,128,128]{2,1,0:T(8,128)(2,1)S(1)}, bf16[3,128,128]{2,1,0:T(8,128)(2,1)S(1)}, u32[]{:S(2)}, u32[]{:S(2)}) collective-permute-start(bf16[3,128,128]{2,1,0:T(8,128)(2,1)S(1)} %get-tuple-element.25), channel_id=1, source_target_pairs={{0,4},{4,0},{8,12},{12,8},{1,5},{5,1},{9,13},{13,9},{2,6},{6,2},{1... | collective-permute-start | bytes 294920 | tf_op jit(solution)/shard_map/act_y/ppermute | solution.py:60
  23.3 6.3 %collective-permute-start.2 = (bf16[3,128,128]{2,1,0:T(8,128)(2,1)S(1)}, bf16[3,128,128]{2,1,0:T(8,128)(2,1)S(1)}, u32[]{:S(2)}, u32[]{:S(2)}) collective-permute-start(bf16[3,128,128]{2,1,0:T(8,128)(2,1)S(1)} %get-tuple-element.26), channel_id=1, source_target_pairs={{0,8},{4,12},{8,0},{12,4},{1,9},{5,13},{9,1},{13,5},{2,10},{6,14},... | collective-permute-start | bytes 294920 | tf_op jit(solution)/shard_map/act_y/ppermute | solution.py:60
  26.8 4.7 %collective-permute-start.3 = (bf16[3,128,128]{2,1,0:T(8,128)(2,1)S(1)}, bf16[3,128,128]{2,1,0:T(8,128)(2,1)S(1)}, u32[]{:S(2)}, u32[]{:S(2)}) collective-permute-start(bf16[3,128,128]{2,1,0:T(8,128)(2,1)S(1)} %get-tuple-element.27), channel_id=1, source_target_pairs={{0,12},{4,8},{8,4},{12,0},{1,13},{5,9},{9,5},{13,1},{2,14},{6,10},... | collective-permute-start | bytes 294920 | tf_op jit(solution)/shard_map/act_y/ppermute | solution.py:60
  31.4 9.1 %copy-start.1 = (bf16[128,4608]{1,0:T(8,128)(2,1)}, bf16[128,4608]{1,0:T(8,128)(2,1)S(1)}, u32[]{:S(2)}) copy-start(bf16[128,4608]{1,0:T(8,128)(2,1)S(1)} %collective-permute-done.4.tie.near_s.own_s) | copy-start | bytes 3538948
  31.4 20.3 %copy-start = (bf16[256,4608]{1,0:T(8,128)(2,1)S(1)}, bf16[256,4608]{1,0:T(8,128)(2,1)}, u32[]{:S(2)}) copy-start(bf16[256,4608]{1,0:T(8,128)(2,1)} %weight.3) | copy-start | bytes 7077892
  32.0 43.2 %copy-start.17 = (bf16[4,128,128]{2,1,0:T(8,128)(2,1)}, bf16[4,128,128]{2,1,0:T(8,128)(2,1)S(1)}, u32[]{:S(2)}) copy-start(bf16[4,128,128]{2,1,0:T(8,128)(2,1)S(1)} %get-tuple-element.33.mixed) | copy-start | bytes 393220
  32.0 19.7 %copy-start.23 = (bf16[256,128]{1,0:T(8,128)(2,1)S(1)}, bf16[256,128]{1,0:T(8,128)(2,1)}, u32[]{:S(2)}) copy-start(bf16[256,128]{1,0:T(8,128)(2,1)} %down.5) | copy-start | bytes 196612
  40.5 11.2 %collective-permute-start.8 = (bf16[128,4608]{1,0:T(8,128)(2,1)}, bf16[128,4608]{1,0:T(8,128)(2,1)S(1)}, u32[]{:S(2)}, u32[]{:S(2)}) collective-permute-start(bf16[128,4608]{1,0:T(8,128)(2,1)} %get-tuple-element.32.more.one), channel_id=1, source_target_pairs={{0,1},{1,0},{2,3},{3,2},{4,5},{5,4},{6,7},{7,6},{8,9},{9,8},{10,11... | collective-permute-start | bytes 3538952 | tf_op jit(solution)/shard_map/tokens_core/ppermute | solution.py:60
  40.5 18.0 %collective-permute-start.17 = (bf16[128,4608]{1,0:T(8,128)(2,1)}, bf16[128,4608]{1,0:T(8,128)(2,1)S(1)}, u32[]{:S(2)}, u32[]{:S(2)}) collective-permute-start(bf16[128,4608]{1,0:T(8,128)(2,1)} %get-tuple-element.32.more.one), channel_id=1, source_target_pairs={{0,4},{1,13},{4,8},{5,1},{8,12},{9,5},{12,0},{13,9},{2,6},{3,15},{... | collective-permute-start | bytes 3538952 | tf_op jit(solution)/shard_map/tokens_y/ppermute | solution.py:27
  41.7 15.9 %collective-permute-start.11 = (bf16[64,4736]{1,0:T(8,128)(2,1)}, bf16[64,4736]{1,0:T(8,128)(2,1)S(1)}, u32[]{:S(2)}, u32[]{:S(2)}) collective-permute-start(bf16[64,4736]{1,0:T(8,128)(2,1)} %get-tuple-element.36.refs_0_), channel_id=1, source_target_pairs={{0,64},{1,193},{64,0},{65,129},{128,192},{129,65},{192,128},{193,1... | collective-permute-start | bytes 1818632 | tf_op jit(solution)/shard_map/weight_x/ppermute | solution.py:33
  44.2 13.4 %collective-permute-start.12 = (bf16[64,4736]{1,0:T(8,128)(2,1)}, bf16[64,4736]{1,0:T(8,128)(2,1)S(1)}, u32[]{:S(2)}, u32[]{:S(2)}) collective-permute-start(bf16[64,4736]{1,0:T(8,128)(2,1)} %get-tuple-element.36.refs_0_), channel_id=1, source_target_pairs={{0,192},{1,65},{64,128},{65,1},{128,64},{129,193},{192,0},{193,129... | collective-permute-start | bytes 1818632 | tf_op jit(solution)/shard_map/weight_x/ppermute | solution.py:33
  44.2 1.4 %collective-permute-start.9 = (bf16[4,128,128]{2,1,0:T(8,128)(2,1)S(1)}, bf16[4,128,128]{2,1,0:T(8,128)(2,1)S(1)}, u32[]{:S(2)}, u32[]{:S(2)}) collective-permute-start(bf16[4,128,128]{2,1,0:T(8,128)(2,1)S(1)} %get-tuple-element.33.mixed), channel_id=1, source_target_pairs={{0,1},{1,0},{2,3},{3,2},{4,5},{5,4},{6,7},{7,6},{8,9},{9,8},{10,11... | collective-permute-start | bytes 393224 | tf_op jit(solution)/shard_map/mixed_core/ppermute | solution.py:60
  45.6 29.6 %copy-start.10 = (bf16[4,128,128]{2,1,0:T(8,128)(2,1)}, bf16[4,128,128]{2,1,0:T(8,128)(2,1)S(1)}, u32[]{:S(2)}) copy-start(bf16[4,128,128]{2,1,0:T(8,128)(2,1)S(1)} %collective-permute-done.9.mixed_s.refs_0_) | copy-start | bytes 393220
  45.6 10.2 %collective-permute-start.5 = (bf16[128,128]{1,0:T(8,128)(2,1)S(1)}, bf16[128,128]{1,0:T(8,128)(2,1)S(1)}, u32[]{:S(2)}, u32[]{:S(2)}) collective-permute-start(bf16[128,128]{1,0:T(8,128)(2,1)S(1)} %get-tuple-element.29.refs_2_.tie), channel_id=1, source_target_pairs={{0,2},{2,0},{1,3},{3,1},{4,6},{6,4},{5,7},{7,5},{8,10},{10,8},{9,1... | collective-permute-start | bytes 98312 | tf_op jit(solution)/shard_map/act_z/ppermute | solution.py:60
  53.0 2.9 %copy-start.7 = (bf16[128,4608]{1,0:T(8,128)(2,1)S(1)}, bf16[128,4608]{1,0:T(8,128)(2,1)}, u32[]{:S(2)}) copy-start(bf16[128,4608]{1,0:T(8,128)(2,1)} %hidden.3) | copy-start | bytes 3538948
  55.8 2.7 %copy-start.13 = (bf16[2,256,256]{2,1,0:T(8,128)(2,1)}, bf16[2,256,256]{2,1,0:T(8,128)(2,1)S(1)}, u32[]{:S(2)}) copy-start(bf16[2,256,256]{2,1,0:T(8,128)(2,1)S(1)} %own_near.1.tie.near) | copy-start | bytes 786436
  57.1 1.4 %collective-permute-start.10 = (f32[8,2304]{1,0:T(8,128)S(1)}, f32[8,2304]{1,0:T(8,128)S(1)}, u32[]{:S(2)}, u32[]{:S(2)}) collective-permute-start(f32[8,2304]{1,0:T(8,128)S(1)} %get-tuple-element.35), channel_id=1, source_target_pairs={{0,1},{1,0},{2,3},{3,2},{4,5},{5,4},{6,7},{7,6},{8,9},{9,8},{10,11... | collective-permute-start | bytes 221192 | tf_op jit(solution)/shard_map/gate_core/ppermute | solution.py:60
  58.6 16.7 %copy-start.3 = (bf16[128,4608]{1,0:T(8,128)(2,1)S(1)}, bf16[128,4608]{1,0:T(8,128)(2,1)}, u32[]{:S(2)}) copy-start(bf16[128,4608]{1,0:T(8,128)(2,1)} %copy-done.1) | copy-start | bytes 3538948
  58.6 16.7 %collective-permute-start.21 = (bf16[128,4608]{1,0:T(8,128)(2,1)S(1)}, bf16[128,4608]{1,0:T(8,128)(2,1)S(1)}, u32[]{:S(2)}, u32[]{:S(2)}) collective-permute-start(bf16[128,4608]{1,0:T(8,128)(2,1)S(1)} %fence.6.refs_2_.two.near), channel_id=1, source_target_pairs={{0,1},{1,0},{2,3},{3,2},{4,5},{5,4},{6,7},{7,6},{8,9},{9,8},{10,11... | collective-permute-start | bytes 3538952 | tf_op jit(solution)/shard_map/tokens_core/ppermute | solution.py:60
  59.4 21.4 %collective-permute-start.26 = (bf16[128,4608]{1,0:T(8,128)(2,1)S(1)}, bf16[128,4608]{1,0:T(8,128)(2,1)}, u32[]{:S(2)}, u32[]{:S(2)}) collective-permute-start(bf16[128,4608]{1,0:T(8,128)(2,1)S(1)} %fence.6.refs_2_.two.near), channel_id=1, source_target_pairs={{0,4},{1,13},{4,8},{5,1},{8,12},{9,5},{12,0},{13,9},{2,6},{3,15},{... | collective-permute-start | bytes 3538952 | tf_op jit(solution)/shard_map/tokens_y/ppermute | solution.py:27
  62.0 9.3 %collective-permute-start.16 = (bf16[64,4736]{1,0:T(8,128)(2,1)S(1)}, bf16[64,4736]{1,0:T(8,128)(2,1)S(1)}, u32[]{:S(2)}, u32[]{:S(2)}) collective-permute-start(bf16[64,4736]{1,0:T(8,128)(2,1)S(1)} %fence.5.refs_1_), channel_id=1, source_target_pairs={{0,192},{1,65},{64,128},{65,1},{128,64},{129,193},{192,0},{193,129... | collective-permute-start | bytes 1818632 | tf_op jit(solution)/shard_map/weight_x_far/ppermute | solution.py:33
  62.3 3.2 %collective-permute-start.13 = (bf16[8,2304]{1,0:T(8,128)(2,1)S(1)}, bf16[8,2304]{1,0:T(8,128)(2,1)S(1)}, u32[]{:S(2)}, u32[]{:S(2)}) collective-permute-start(bf16[8,2304]{1,0:T(8,128)(2,1)S(1)} %convert_element_type.2), channel_id=1, source_target_pairs={{0,16},{16,0},{32,48},{48,32},{1,17},{17,1},{33,49},{49,33},{2,18}... | collective-permute-start | bytes 110600 | tf_op jit(solution)/shard_map/gate_zl/ppermute | solution.py:60
  63.3 4.5 %collective-permute-start.14 = (bf16[8,2304]{1,0:T(8,128)(2,1)S(1)}, bf16[8,2304]{1,0:T(8,128)(2,1)S(1)}, u32[]{:S(2)}, u32[]{:S(2)}) collective-permute-start(bf16[8,2304]{1,0:T(8,128)(2,1)S(1)} %convert_element_type.2), channel_id=1, source_target_pairs={{0,32},{16,48},{32,0},{48,16},{1,33},{17,49},{33,1},{49,17},{2,34}... | collective-permute-start | bytes 110600 | tf_op jit(solution)/shard_map/gate_zl/ppermute | solution.py:60
  65.5 4.7 %collective-permute-start.15 = (bf16[8,2304]{1,0:T(8,128)(2,1)S(1)}, bf16[8,2304]{1,0:T(8,128)(2,1)S(1)}, u32[]{:S(2)}, u32[]{:S(2)}) collective-permute-start(bf16[8,2304]{1,0:T(8,128)(2,1)S(1)} %convert_element_type.2), channel_id=1, source_target_pairs={{0,48},{16,32},{32,16},{48,0},{1,49},{17,33},{33,17},{49,1},{2,50}... | collective-permute-start | bytes 110600 | tf_op jit(solution)/shard_map/gate_zl/ppermute | solution.py:60
  71.3 9.5 %collective-permute-start.18 = (f32[8,2304]{1,0:T(8,128)S(1)}, f32[8,2304]{1,0:T(8,128)S(1)}, u32[]{:S(2)}, u32[]{:S(2)}) collective-permute-start(f32[8,2304]{1,0:T(8,128)S(1)} %gate_sum.6.refs_4_.first), channel_id=1, source_target_pairs={{0,64},{64,0},{128,192},{192,128},{1,65},{65,1},{129,193},{193,129... | collective-permute-start | bytes 221192 | tf_op jit(solution)/shard_map/gate_x/ppermute | solution.py:60
  71.7 9.1 %collective-permute-start.19 = (f32[8,2304]{1,0:T(8,128)S(1)}, f32[8,2304]{1,0:T(8,128)S(1)}, u32[]{:S(2)}, u32[]{:S(2)}) collective-permute-start(f32[8,2304]{1,0:T(8,128)S(1)} %gate_sum.6.refs_4_.first), channel_id=1, source_target_pairs={{0,128},{64,192},{128,0},{192,64},{1,129},{65,193},{129,1},{193,65... | collective-permute-start | bytes 221192 | tf_op jit(solution)/shard_map/gate_x/ppermute | solution.py:60
  73.4 7.4 %collective-permute-start.20 = (f32[8,2304]{1,0:T(8,128)S(1)}, f32[8,2304]{1,0:T(8,128)S(1)}, u32[]{:S(2)}, u32[]{:S(2)}) collective-permute-start(f32[8,2304]{1,0:T(8,128)S(1)} %gate_sum.6.refs_4_.first), channel_id=1, source_target_pairs={{0,192},{64,128},{128,64},{192,0},{1,193},{65,129},{129,65},{193,1... | collective-permute-start | bytes 221192 | tf_op jit(solution)/shard_map/gate_x/ppermute | solution.py:60
  75.3 4.9 %copy-start.8 = (bf16[128,4608]{1,0:T(8,128)(2,1)}, bf16[128,4608]{1,0:T(8,128)(2,1)S(1)}, u32[]{:S(2)}) copy-start(bf16[128,4608]{1,0:T(8,128)(2,1)S(1)} %collective-permute-done.21.two_s.near_s) | copy-start | bytes 3538948
  82.2 18.6 %collective-permute-start.27 = (bf16[128,4608]{1,0:T(8,128)(2,1)}, bf16[128,4608]{1,0:T(8,128)(2,1)}, u32[]{:S(2)}, u32[]{:S(2)}) collective-permute-start(bf16[128,4608]{1,0:T(8,128)(2,1)} %fence.7.three.more), channel_id=1, source_target_pairs={{0,1},{1,0},{2,3},{3,2},{4,5},{5,4},{6,7},{7,6},{8,9},{9,8},{10,11... | collective-permute-start | bytes 3538952 | tf_op jit(solution)/shard_map/tokens_core/ppermute | solution.py:60
  84.6 28.3 %collective-permute-start.28 = (bf16[3,256,256]{2,1,0:T(8,128)(2,1)}, bf16[3,256,256]{2,1,0:T(8,128)(2,1)}, u32[]{:S(2)}, u32[]{:S(2)}) collective-permute-start(bf16[3,256,256]{2,1,0:T(8,128)(2,1)} %get-tuple-element.37.refs_0_.tie), channel_id=1, source_target_pairs={{0,2},{2,0},{1,3},{3,1},{4,6},{6,4},{5,7},{7,5},{8,10},{10,8},{9,1... | collective-permute-start | bytes 1179656 | tf_op jit(solution)/shard_map/out_z/ppermute | solution.py:60
  90.8 3.9 %collective-permute-start.22 = (f32[8,2304]{1,0:T(8,128)S(1)}, f32[8,2304]{1,0:T(8,128)S(1)}, u32[]{:S(2)}, u32[]{:S(2)}) collective-permute-start(f32[8,2304]{1,0:T(8,128)S(1)} %gate_sum.7.first.refs_1_), channel_id=1, source_target_pairs={{0,4},{4,0},{8,12},{12,8},{1,5},{5,1},{9,13},{13,9},{2,6},{6,2},{1... | collective-permute-start | bytes 221192 | tf_op jit(solution)/shard_map/gate_y/ppermute | solution.py:60
  90.8 7.6 %collective-permute-start.23 = (f32[8,2304]{1,0:T(8,128)S(1)}, f32[8,2304]{1,0:T(8,128)S(1)}, u32[]{:S(2)}, u32[]{:S(2)}) collective-permute-start(f32[8,2304]{1,0:T(8,128)S(1)} %gate_sum.7.first.refs_1_), channel_id=1, source_target_pairs={{0,8},{4,12},{8,0},{12,4},{1,9},{5,13},{9,1},{13,5},{2,10},{6,14},... | collective-permute-start | bytes 221192 | tf_op jit(solution)/shard_map/gate_y/ppermute | solution.py:60
  94.6 5.3 %collective-permute-start.24 = (f32[8,2304]{1,0:T(8,128)S(1)}, f32[8,2304]{1,0:T(8,128)S(1)}, u32[]{:S(2)}, u32[]{:S(2)}) collective-permute-start(f32[8,2304]{1,0:T(8,128)S(1)} %gate_sum.7.first.refs_1_), channel_id=1, source_target_pairs={{0,12},{4,8},{8,4},{12,0},{1,13},{5,9},{9,5},{13,1},{2,14},{6,10},... | collective-permute-start | bytes 221192 | tf_op jit(solution)/shard_map/gate_y/ppermute | solution.py:60
  100.5 12.4 %collective-permute-start.25 = (f32[8,2304]{1,0:T(8,128)}, f32[8,2304]{1,0:T(8,128)}, u32[]{:S(2)}, u32[]{:S(2)}) collective-permute-start(f32[8,2304]{1,0:T(8,128)} %gate_sum.8.tie.left), channel_id=1, source_target_pairs={{0,2},{2,0},{1,3},{3,1},{4,6},{6,4},{5,7},{7,5},{8,10},{10,8},{9,1... | collective-permute-start | bytes 221192 | tf_op jit(solution)/shard_map/gate_zh/ppermute | solution.py:60
  105.1 10.5 %copy-start.9 = (bf16[128,4608]{1,0:T(8,128)(2,1)S(1)}, bf16[128,4608]{1,0:T(8,128)(2,1)}, u32[]{:S(2)}) copy-start(bf16[128,4608]{1,0:T(8,128)(2,1)} %copy-done.8) | copy-start | bytes 3538948
  105.1 10.5 %copy-start.12 = (bf16[4,128,128]{2,1,0:T(8,128)(2,1)S(1)}, bf16[4,128,128]{2,1,0:T(8,128)(2,1)}, u32[]{:S(2)}) copy-start(bf16[4,128,128]{2,1,0:T(8,128)(2,1)} %copy-done.10) | copy-start | bytes 393220
  105.1 10.5 %copy-start.19 = (bf16[4,128,128]{2,1,0:T(8,128)(2,1)S(1)}, bf16[4,128,128]{2,1,0:T(8,128)(2,1)}, u32[]{:S(2)}) copy-start(bf16[4,128,128]{2,1,0:T(8,128)(2,1)} %copy-done.17) | copy-start | bytes 393220
  105.1 10.5 %copy-start.24 = (bf16[256,128]{1,0:T(8,128)(2,1)S(1)}, bf16[256,128]{1,0:T(8,128)(2,1)}, u32[]{:S(2)}) copy-start(bf16[256,128]{1,0:T(8,128)(2,1)} %down.5) | copy-start | bytes 196612
  107.7 11.7 %collective-permute-start.30 = (bf16[256,256]{1,0:T(8,128)(2,1)S(1)}, bf16[256,256]{1,0:T(8,128)(2,1)S(1)}, u32[]{:S(2)}, u32[]{:S(2)}) collective-permute-start(bf16[256,256]{1,0:T(8,128)(2,1)S(1)} %far_products_last.1.refs_0_), channel_id=1, source_target_pairs={{0,2},{2,0},{1,3},{3,1},{4,6},{6,4},{5,7},{7,5},{8,10},{10,8},{9,1... | collective-permute-start | bytes 393224 | tf_op jit(solution)/shard_map/out_z_last/ppermute | solution.py:60
  113.8 5.6 %copy-start.14 = (bf16[2,256,256]{2,1,0:T(8,128)(2,1)S(1)}, bf16[2,256,256]{2,1,0:T(8,128)(2,1)}, u32[]{:S(2)}) copy-start(bf16[2,256,256]{2,1,0:T(8,128)(2,1)} %copy-done.13) | copy-start | bytes 786436
  113.8 4.9 %collective-permute-start.29 = (f32[8,2304]{1,0:T(8,128)S(1)}, f32[8,2304]{1,0:T(8,128)S(1)}, u32[]{:S(2)}, u32[]{:S(2)}) collective-permute-start(f32[8,2304]{1,0:T(8,128)S(1)} %gate_sum.9), channel_id=1, source_target_pairs={{0,1},{1,0},{2,3},{3,2},{4,5},{5,4},{6,7},{7,6},{8,9},{9,8},{10,11... | collective-permute-start | bytes 221192 | tf_op jit(solution)/shard_map/gate_core_back/ppermute | solution.py:60
  (11 other events, 11.8 us)

commit v10 on v9

--- a/solution.py
+++ b/solution.py
@@ -16,7 +16,7 @@
 ANY = pl.BlockSpec(memory_space=pl.ANY)
 HBM = pl.BlockSpec(memory_space=pltpu.HBM)
 SMALL = pltpu.CompilerParams(vmem_limit_bytes=8 * 1024 * 1024)
-MIDDLE = pltpu.CompilerParams(vmem_limit_bytes=24 * 1024 * 1024)
+MIDDLE = pltpu.CompilerParams(vmem_limit_bytes=16 * 1024 * 1024)
 
 
 def ring(value, axis):
@@ -79,6 +79,23 @@
     column = lax.broadcasted_iota(jnp.int32, (adapters, stacked), 1)
     low = row * (stacked // adapters)
     return jnp.where((column >= low) & (column < low + stacked // adapters), 1.0, 0.0)
+
+
+def join_kernel(side, mine, got, tie, out):
+    rows = mine.shape[0]
+    for place, ref in ((side[0], mine), (1 - side[0], got)):
+        out[pl.ds(pl.multiple_of(place * rows, rows), rows), :] = ref[...]
+
+
+def join(side, mine, got, tie):
+    return pl.pallas_call(
+        join_kernel,
+        in_specs=[SMEM, VMEM, VMEM, ANY],
+        out_specs=VMEM,
+        out_shape=shaped((2 * mine.shape[0], mine.shape[1]), mine.dtype),
+        compiler_params=SMALL,
+        name="join",
+    )(side.reshape(1), mine, got, tie)
 
 
 def token_kernel(at, hidden, grad, up, gate, mixed, gates, back):
@@ -112,7 +129,7 @@
     rest[...] = keep[y] + got[y].astype(F32)
 
 
-def act_z_kernel(at, rest, first, second, third, mixed, tie, keep, give, all_mixed):
+def act_z_kernel(at, rest, first, second, third, mixed, tie, tie_too, keep, give, all_mixed):
     y, zh = at[1], at[2]
     for out, side in ((give, 1 - zh), (keep, zh)):
         total = (rest[side] + first[side].astype(F32)) + (
@@ -218,12 +235,13 @@
     features = weight.shape[0]
     depth = width + stacked
     quarter = features // 4
-    x, y, zh, c = (lax.axis_index(a) for a in ("x", "y", "zh", "c"))
+    x, y, zl, zh, c = (lax.axis_index(a) for a in ("x", "y", "zl", "zh", "c"))
     at = jnp.stack([x, y, zh, c]).astype(jnp.int32)
 
     with jax.named_scope("weight_z"):
+        start = x * quarter + (zl % 2) * (quarter // 2)
         piece = jnp.concatenate(
-            [lax.dynamic_slice_in_dim(v, x * quarter, quarter, 0) for v in (weight, down)], axis=1
+            [lax.dynamic_slice_in_dim(v, start, quarter // 2, 0) for v in (weight, down)], axis=1
         )
         far_piece = swap(piece, "zh", 1)
     with jax.named_scope("tokens_y"):
@@ -266,13 +284,16 @@
         compiler_params=SMALL,
         name="rank_sum_core",
     )(at, keep, got, mixed)
+    (far_piece,) = fence((far_piece,), rest)
+    with jax.named_scope("weight_zl"):
+        z_got = swap(far_piece, "zl", 1)
     with jax.named_scope("act_y"):
         first, second, third = (
             swap(v, "y", mask) for v, mask in ((first, 1), (second, 2), (third, 3))
         )
     keep, give, all_mixed = pl.pallas_call(
         act_z_kernel,
-        in_specs=[SMEM] + [VMEM] * 5 + [ANY],
+        in_specs=[SMEM] + [VMEM] * 5 + [ANY] * 2,
         out_specs=[VMEM] * 3,
         out_shape=[
             shaped((tokens, stacked), F32),
@@ -281,17 +302,19 @@
         ],
         compiler_params=SMALL,
         name="rank_sum_y",
-    )(at, rest, first, second, third, mixed, own_s)
-    one, far_piece = fence((one, far_piece), give)
+    )(at, rest, first, second, third, mixed, own_s, z_got)
+    far_piece = join(zl % 2, far_piece, z_got, give)
+    (give,) = fence((give,), far_piece)
+    with jax.named_scope("act_z"):
+        message = swap(give, "zh", 1)
+    with jax.named_scope("weight_x"):
+        w_first = pairs(far_piece, "x", True)
+        w_second = pairs(far_piece, "x", False)
+    (one,) = fence((one,), message)
     with jax.named_scope("tokens_y"):
         two = ring(one, "y")
     with jax.named_scope("tokens_core"):
         one_s = swap(one, "c", 1)
-    with jax.named_scope("weight_x"):
-        w_first = pairs(far_piece, "x", True)
-        w_second = pairs(far_piece, "x", False)
-    with jax.named_scope("act_z"):
-        message = swap(give, "zh", 1)
     with jax.named_scope("mixed_core"):
         mixed_s = swap(all_mixed, "c", 1)
 
@@ -306,8 +329,6 @@
             name=name,
         )(at, near, near_s, more, more_s, all_mixed, mixed_s, weights, downs, tie)
 
-    own_near = products("own_near", 0, grad, own_s, one, one_s, weight, down, give)
-
     total, give = pl.pallas_call(
         gate_kernel,
         in_specs=[SMEM] + [VMEM] * 5 + [ANY],
@@ -315,7 +336,7 @@
         out_shape=[shaped((adapters, width // 2), F32)] * 2,
         compiler_params=SMALL,
         name="gate_products",
-    )(at, keep, message, back, gates, hidden, own_near)
+    )(at, keep, message, back, gates, hidden, far_piece)
 
     def add(left, right, *ties):
         return pl.pallas_call(
@@ -344,16 +365,19 @@
 
     with jax.named_scope("gate_core"):
         got = swap(give, "c", 1)
-    total = add(total, got, w_first, w_second)
+    total = add(total, got)
+    total = step(total, "zl", mixed_s, w_first, w_second, dtype=BF16)
     (w_first,) = fence((w_first,), total)
     with jax.named_scope("weight_x_far"):
         w_far = pairs(w_first, "x", False)
-    (two,) = fence((two,), w_first)
+    (two,) = fence((two,), total)
     with jax.named_scope("tokens_y"):
         three = ring(two, "y")
-    total = step(total, "zl", mixed_s, w_far, two, dtype=BF16)
+    with jax.named_scope("gate_zh"):
+        got = swap(total, "zh", 1)
     with jax.named_scope("tokens_core"):
         two_s = swap(two, "c", 1)
+    total = add(total, got, two_s, w_far)
 
     far, far_weight, far_down = pl.pallas_call(
         far_kernel,
@@ -391,10 +415,9 @@
     with jax.named_scope("out_z_last"):
         last_got = swap(last, "zh", 1)
 
+    own_near = products("own_near", 0, grad, own_s, one, one_s, weight, down, far)
     own_rest = products("own_rest", 2, two, two_s, three, three_s, weight, down, far)
-    with jax.named_scope("gate_zh"):
-        got = swap(total, "zh", 1)
-    total = add(total, got, last, far_got)
+    (total,) = fence((total,), last)
     with jax.named_scope("gate_core_back"):
         other = swap(total, "c", 1)
     gate_grad = jnp.where(

time: 122 us -> 124 us (1.016)
  the two profiles are of different devices: /device:TPU:1 before, /device:TPU:24 now
where the time goes in v10:
time: 124 us
  starting transfers between devices  56.6 us (46%)
  waiting for transfers between devices  30.4 us (25%)
  Pallas kernels  18.6 us (15%)
  local copies, waits for them, and re-layouts  15.4 us (12%)
  other arithmetic  1.5 us (1%)
  between operations  1.3 us (1%)
    ppermute x26, starting transfers between devices, swap(): return lax.ppermute(value, axis, [(i, i ^ mask) for i in range(size)])  45.7 us
    ppermute x26, waiting for transfers between devices, swap(): return lax.ppermute(value, axis, [(i, i ^ mask) for i in range(size)])  30.1 us
    unnamed x68, local copies, waits for them, and re-layouts  13.6 us
    ppermute x3, starting transfers between devices, pairs(): lax.ppermute(value, (axis, 'c'), [(2 * i + c, 2 * partner(i, c) + c) for...  6.35 us
    pallas_call x2, Pallas kernels, products(): pl.pallas_call(functools.partial(product_kernel, first), in_specs=[SMEM]...  5.07 us
    ppermute x3, starting transfers between devices, ring(): return lax.ppermute(value, (axis, 'c'), pairs)  4.49 us
    pallas_call x1, Pallas kernels, on_device(): pl.pallas_call(far_kernel, in_specs=[SMEM] + [VMEM] * 12 + [ANY], out_spe...  2.81 us
    pallas_call x1, Pallas kernels, on_device(): pl.pallas_call(far_last_kernel, in_specs=[SMEM] + [VMEM] * 6 + [ANY], out...  2.6 us
  transfers between devices with their start and end apart: 32, of which 12 were waited for; matrix products, arithmetic and copies ran while one was open for 3% of the time, Pallas kernels for 14%

profile of v10, /device:TPU:24, one launch (start us, length us, event | category | flops | bytes accessed | tf_op | source)
XLA Modules:
  0.0 123.8 jit_solution(6298222245862917308)
XLA Ops:
  0.7 2.0 %collective-permute-start.16 = (bf16[128,4608]{1,0:T(8,128)(2,1)}, bf16[128,4608]{1,0:T(8,128)(2,1)S(1)}, u32[]{:S(2)}, u32[]{:S(2)}) collective-permute-start(bf16[128,4608]{1,0:T(8,128)(2,1)} %near.1), channel_id=1, source_target_pairs={{0,4},{1,13},{4,8},{5,1},{8,12},{9,5},{12,0},{13,9},{2,6},{3,15},{... | collective-permute-start | bytes 3538952 | tf_op jit(solution)/shard_map/tokens_y/ppermute | solution.py:27
  2.8 1.1 constant_dynamic-slice_fusion.1
  5.3 5.5 %collective-permute-start.5 = (bf16[32,4736]{1,0:T(8,128)(2,1)}, bf16[32,4736]{1,0:T(8,128)(2,1)}, u32[]{:S(2)}, u32[]{:S(2)}) collective-permute-start(bf16[32,4736]{1,0:T(8,128)(2,1)} %pad_maximum_fusion), channel_id=1, source_target_pairs={{0,2},{2,0},{1,3},{3,1},{4,6},{6,4},{5,7},{7,5},{8,10},{10,8},{9,1... | collective-permute-start | bytes 909320 | tf_op jit(solution)/shard_map/weight_z/ppermute | solution.py:60
  10.8 1.2 copy-done.25
  12.9 1.0 rank_products.1
  14.3 1.3 %copy-done.9 = bf16[128,4608]{1,0:T(8,128)(2,1)S(1)} copy-done((bf16[128,4608]{1,0:T(8,128)(2,1)S(1)}, bf16[128,4608]{1,0:T(8,128)(2,1)}, u32[]{:S(2)}) %copy-start.9) | copy-done | bytes 1179672
  15.6 1.3 %copy-done.24 = bf16[128,4608]{1,0:T(8,128)(2,1)S(1)} copy-done((bf16[128,4608]{1,0:T(8,128)(2,1)S(1)}, bf16[128,4608]{1,0:T(8,128)(2,1)}, u32[]{:S(2)}) %copy-start.24) | copy-done | bytes 1179672
  16.9 0.9 copy-done.31
  17.8 2.0 %token_values.1 = (bf16[128,128]{1,0:T(8,128)(2,1)S(1)}, f32[8,128]{1,0:T(8,128)S(1)}, f32[128,128]{1,0:T(8,128)S(1)}) custom-call(s32[4]{0:T(128)S(1)} %pad_add_fusion.at, bf16[128,4608]{1,0:T(8,128)(2,1)S(1)} %copy-done.9, bf16[128,4608]{1,0:T(8,128)(2,1)S(1)} %copy-done.5, bf16[128,4608]{1,0:T(8,128)(2,1)S(1)} %copy-done.24, bf16[8,4608]{1,0:T(8,128)(2,1)S(1)} %copy-done.31), custom_call_target="tpu_custom_call" | custom-call | flops 452984832 | bytes 7077888 | tf_op jit(solution)/shard_map/token_values/pallas_call | solution.py:266
  20.4 6.3 %collective-permute-start.6 = (bf16[32,4736]{1,0:T(8,128)(2,1)}, bf16[32,4736]{1,0:T(8,128)(2,1)S(1)}, u32[]{:S(2)}, u32[]{:S(2)}) collective-permute-start(bf16[32,4736]{1,0:T(8,128)(2,1)} %fence.7.mine), channel_id=1, source_target_pairs={{0,16},{16,0},{32,48},{48,32},{1,17},{17,1},{33,49},{49,33},{2,18}... | collective-permute-start | bytes 909320 | tf_op jit(solution)/shard_map/weight_zl/ppermute | solution.py:60
  27.1 1.6 %collective-permute-start.2 = (bf16[3,128,128]{2,1,0:T(8,128)(2,1)S(1)}, bf16[3,128,128]{2,1,0:T(8,128)(2,1)S(1)}, u32[]{:S(2)}, u32[]{:S(2)}) collective-permute-start(bf16[3,128,128]{2,1,0:T(8,128)(2,1)S(1)} %get-tuple-element.24), channel_id=1, source_target_pairs={{0,8},{4,12},{8,0},{12,4},{1,9},{5,13},{9,1},{13,5},{2,10},{6,14},... | collective-permute-start | bytes 294920 | tf_op jit(solution)/shard_map/act_y/ppermute | solution.py:60
  28.7 3.4 %collective-permute-done.1.first = bf16[3,128,128]{2,1,0:T(8,128)(2,1)S(1)} collective-permute-done((bf16[3,128,128]{2,1,0:T(8,128)(2,1)S(1)}, bf16[3,128,128]{2,1,0:T(8,128)(2,1)S(1)}, u32[]{:S(2)}, u32[]{:S(2)}) %collective-permute-start.1) | collective-permute-done | bytes 98336 | tf_op jit(solution)/shard_map/act_y/ppermute | solution.py:60
  32.8 1.2 collective-permute-done.2.second
  34.0 3.9 %collective-permute-done.3.third = bf16[3,128,128]{2,1,0:T(8,128)(2,1)S(1)} collective-permute-done((bf16[3,128,128]{2,1,0:T(8,128)(2,1)S(1)}, bf16[3,128,128]{2,1,0:T(8,128)(2,1)S(1)}, u32[]{:S(2)}, u32[]{:S(2)}) %collective-permute-start.3) | collective-permute-done | bytes 98336 | tf_op jit(solution)/shard_map/act_y/ppermute | solution.py:60
  38.6 1.1 join.1.refs_1_.tie.refs_0_
  39.7 5.4 %collective-permute-start.7 = (bf16[128,128]{1,0:T(8,128)(2,1)S(1)}, bf16[128,128]{1,0:T(8,128)(2,1)S(1)}, u32[]{:S(2)}, u32[]{:S(2)}) collective-permute-start(bf16[128,128]{1,0:T(8,128)(2,1)S(1)} %fence.8), channel_id=1, source_target_pairs={{0,2},{2,0},{1,3},{3,1},{4,6},{6,4},{5,7},{7,5},{8,10},{10,8},{9,1... | collective-permute-start | bytes 98312 | tf_op jit(solution)/shard_map/act_z/ppermute | solution.py:60
  45.1 2.5 %collective-permute-done.7.got.refs_1_ = bf16[128,128]{1,0:T(8,128)(2,1)S(1)} collective-permute-done((bf16[128,128]{1,0:T(8,128)(2,1)S(1)}, bf16[128,128]{1,0:T(8,128)(2,1)S(1)}, u32[]{:S(2)}, u32[]{:S(2)}) %collective-permute-start.7) | collective-permute-done | bytes 32800 | tf_op jit(solution)/shard_map/act_z/ppermute | solution.py:60
  47.6 1.3 %collective-permute-start.17 = (bf16[128,4608]{1,0:T(8,128)(2,1)S(1)}, bf16[128,4608]{1,0:T(8,128)(2,1)S(1)}, u32[]{:S(2)}, u32[]{:S(2)}) collective-permute-start(bf16[128,4608]{1,0:T(8,128)(2,1)S(1)} %fence.9.one.more), channel_id=1, source_target_pairs={{0,4},{1,13},{4,8},{5,1},{8,12},{9,5},{12,0},{13,9},{2,6},{3,15},{... | collective-permute-start | bytes 3538952 | tf_op jit(solution)/shard_map/tokens_y/ppermute | solution.py:27
  48.9 1.5 %collective-permute-start.13 = (bf16[64,4736]{1,0:T(8,128)(2,1)S(1)}, bf16[64,4736]{1,0:T(8,128)(2,1)S(1)}, u32[]{:S(2)}, u32[]{:S(2)}) collective-permute-start(bf16[64,4736]{1,0:T(8,128)(2,1)S(1)} %join.1.refs_1_.tie.refs_0_), channel_id=1, source_target_pairs={{0,64},{1,193},{64,0},{65,129},{128,192},{129,65},{192,128},{193,1... | collective-permute-start | bytes 1818632 | tf_op jit(solution)/shard_map/weight_x/ppermute | solution.py:33
  50.4 2.1 %collective-permute-start.14 = (bf16[64,4736]{1,0:T(8,128)(2,1)S(1)}, bf16[64,4736]{1,0:T(8,128)(2,1)S(1)}, u32[]{:S(2)}, u32[]{:S(2)}) collective-permute-start(bf16[64,4736]{1,0:T(8,128)(2,1)S(1)} %join.1.refs_1_.tie.refs_0_), channel_id=1, source_target_pairs={{0,192},{1,65},{64,128},{65,1},{128,64},{129,193},{192,0},{193,129... | collective-permute-start | bytes 1818632 | tf_op jit(solution)/shard_map/weight_x/ppermute | solution.py:33
  52.5 1.2 gate_products.1
  54.3 0.9 collective-permute-done.8.right
  55.2 1.3 %collective-permute-start.10 = (bf16[8,2304]{1,0:T(8,128)(2,1)S(1)}, bf16[8,2304]{1,0:T(8,128)(2,1)S(1)}, u32[]{:S(2)}, u32[]{:S(2)}) collective-permute-start(bf16[8,2304]{1,0:T(8,128)(2,1)S(1)} %convert_element_type.2), channel_id=1, source_target_pairs={{0,32},{16,48},{32,0},{48,16},{1,33},{17,49},{33,1},{49,17},{2,34}... | collective-permute-start | bytes 110600 | tf_op jit(solution)/shard_map/gate_zl/ppermute | solution.py:60
  56.5 1.6 %collective-permute-start.11 = (bf16[8,2304]{1,0:T(8,128)(2,1)S(1)}, bf16[8,2304]{1,0:T(8,128)(2,1)S(1)}, u32[]{:S(2)}, u32[]{:S(2)}) collective-permute-start(bf16[8,2304]{1,0:T(8,128)(2,1)S(1)} %convert_element_type.2), channel_id=1, source_target_pairs={{0,48},{16,32},{32,16},{48,0},{1,49},{17,33},{33,17},{49,1},{2,50}... | collective-permute-start | bytes 110600 | tf_op jit(solution)/shard_map/gate_zl/ppermute | solution.py:60
  58.1 2.7 %collective-permute-done.10.third = bf16[8,2304]{1,0:T(8,128)(2,1)S(1)} collective-permute-done((bf16[8,2304]{1,0:T(8,128)(2,1)S(1)}, bf16[8,2304]{1,0:T(8,128)(2,1)S(1)}, u32[]{:S(2)}, u32[]{:S(2)}) %collective-permute-start.10) | collective-permute-done | bytes 36896 | tf_op jit(solution)/shard_map/gate_zl/ppermute | solution.py:60
  60.8 1.4 %collective-permute-done.11.fourth = bf16[8,2304]{1,0:T(8,128)(2,1)S(1)} collective-permute-done((bf16[8,2304]{1,0:T(8,128)(2,1)S(1)}, bf16[8,2304]{1,0:T(8,128)(2,1)S(1)}, u32[]{:S(2)}, u32[]{:S(2)}) %collective-permute-start.11) | collective-permute-done | bytes 36896 | tf_op jit(solution)/shard_map/gate_zl/ppermute | solution.py:60
  62.3 2.5 %collective-permute-done.9.second = bf16[8,2304]{1,0:T(8,128)(2,1)S(1)} collective-permute-done((bf16[8,2304]{1,0:T(8,128)(2,1)S(1)}, bf16[8,2304]{1,0:T(8,128)(2,1)S(1)}, u32[]{:S(2)}, u32[]{:S(2)}) %collective-permute-start.9) | collective-permute-done | bytes 36896 | tf_op jit(solution)/shard_map/gate_zl/ppermute | solution.py:60
  65.6 1.2 collective-permute-start.27
  66.8 2.8 %collective-permute-start.19 = (bf16[64,4736]{1,0:T(8,128)(2,1)S(1)}, bf16[64,4736]{1,0:T(8,128)(2,1)S(1)}, u32[]{:S(2)}, u32[]{:S(2)}) collective-permute-start(bf16[64,4736]{1,0:T(8,128)(2,1)S(1)} %fence.11.refs_1_), channel_id=1, source_target_pairs={{0,192},{1,65},{64,128},{65,1},{128,64},{129,193},{192,0},{193,129... | collective-permute-start | bytes 1818632 | tf_op jit(solution)/shard_map/weight_x_far/ppermute | solution.py:33
  69.6 5.6 %collective-permute-start.15 = (f32[8,2304]{1,0:T(8,128)S(1)}, f32[8,2304]{1,0:T(8,128)S(1)}, u32[]{:S(2)}, u32[]{:S(2)}) collective-permute-start(f32[8,2304]{1,0:T(8,128)S(1)} %gate_sum.6.refs_1_.left), channel_id=1, source_target_pairs={{0,2},{2,0},{1,3},{3,1},{4,6},{6,4},{5,7},{7,5},{8,10},{10,8},{9,1... | collective-permute-start | bytes 221192 | tf_op jit(solution)/shard_map/gate_zh/ppermute | solution.py:60
  75.1 2.7 %collective-permute-done.15.right = f32[8,2304]{1,0:T(8,128)S(1)} collective-permute-done((f32[8,2304]{1,0:T(8,128)S(1)}, f32[8,2304]{1,0:T(8,128)S(1)}, u32[]{:S(2)}, u32[]{:S(2)}) %collective-permute-start.15) | collective-permute-done | bytes 73760 | tf_op jit(solution)/shard_map/gate_zh/ppermute | solution.py:60
  79.0 3.4 %collective-permute-start.21 = (f32[8,2304]{1,0:T(8,128)S(1)}, f32[8,2304]{1,0:T(8,128)S(1)}, u32[]{:S(2)}, u32[]{:S(2)}) collective-permute-start(f32[8,2304]{1,0:T(8,128)S(1)} %gate_sum.7.refs_4_.first), channel_id=1, source_target_pairs={{0,128},{64,192},{128,0},{192,64},{1,129},{65,193},{129,1},{193,65... | collective-permute-start | bytes 221192 | tf_op jit(solution)/shard_map/gate_x/ppermute | solution.py:60
  82.9 2.8 %far_products.1 = (bf16[3,256,256]{2,1,0:T(8,128)(2,1)S(1)}, bf16[256,4608]{1,0:T(8,128)(2,1)S(1)}, bf16[256,128]{1,0:T(8,128)(2,1)S(1)}) custom-call(s32[4]{0:T(128)S(1)} %pad_add_fusion.at, bf16[128,4608]{1,0:T(8,128)(2,1)S(1)} %copy-done.5, bf16[128,4608]{1,0:T(8,128)(2,1)S(1)} %collective-permute-done.4.tie.own_s.near_s, ...), custom_call_target="tpu_custom_call" | custom-call | flops 1862270976 | bytes 10911744 | tf_op jit(solution)/shard_map/far_products/pallas_call | solution.py:382
  85.8 2.2 %collective-permute-done.22.fourth = f32[8,2304]{1,0:T(8,128)S(1)} collective-permute-done((f32[8,2304]{1,0:T(8,128)S(1)}, f32[8,2304]{1,0:T(8,128)S(1)}, u32[]{:S(2)}, u32[]{:S(2)}) %collective-permute-start.22) | collective-permute-done | bytes 73760 | tf_op jit(solution)/shard_map/gate_x/ppermute | solution.py:60
  88.6 5.6 %collective-permute-start.30 = (bf16[3,256,256]{2,1,0:T(8,128)(2,1)}, bf16[3,256,256]{2,1,0:T(8,128)(2,1)S(1)}, u32[]{:S(2)}, u32[]{:S(2)}) collective-permute-start(bf16[3,256,256]{2,1,0:T(8,128)(2,1)} %copy-done.13), channel_id=1, source_target_pairs={{0,2},{2,0},{1,3},{3,1},{4,6},{6,4},{5,7},{7,5},{8,10},{10,8},{9,1... | collective-permute-start | bytes 1179656 | tf_op jit(solution)/shard_map/out_z/ppermute | solution.py:60
  94.2 1.5 %collective-permute-start.25 = (f32[8,2304]{1,0:T(8,128)}, f32[8,2304]{1,0:T(8,128)S(1)}, u32[]{:S(2)}, u32[]{:S(2)}) collective-permute-start(f32[8,2304]{1,0:T(8,128)} %copy-done.26), channel_id=1, source_target_pairs={{0,8},{4,12},{8,0},{12,4},{1,9},{5,13},{9,1},{13,5},{2,10},{6,14},... | collective-permute-start | bytes 221192 | tf_op jit(solution)/shard_map/gate_y/ppermute | solution.py:60
  95.7 3.2 %collective-permute-start.26 = (f32[8,2304]{1,0:T(8,128)}, f32[8,2304]{1,0:T(8,128)S(1)}, u32[]{:S(2)}, u32[]{:S(2)}) collective-permute-start(f32[8,2304]{1,0:T(8,128)} %copy-done.26), channel_id=1, source_target_pairs={{0,12},{4,8},{8,4},{12,0},{1,13},{5,9},{9,5},{13,1},{2,14},{6,10},... | collective-permute-start | bytes 221192 | tf_op jit(solution)/shard_map/gate_y/ppermute | solution.py:60
  98.9 1.3 %copy-done.2 = bf16[128,4608]{1,0:T(8,128)(2,1)S(1)} copy-done((bf16[128,4608]{1,0:T(8,128)(2,1)S(1)}, bf16[128,4608]{1,0:T(8,128)(2,1)}, u32[]{:S(2)}) %copy-start.2) | copy-done | bytes 1179672
  100.2 1.3 %copy-done.6 = bf16[128,4608]{1,0:T(8,128)(2,1)S(1)} copy-done((bf16[128,4608]{1,0:T(8,128)(2,1)S(1)}, bf16[128,4608]{1,0:T(8,128)(2,1)}, u32[]{:S(2)}) %copy-start.6) | copy-done | bytes 1179672
  101.4 1.3 %copy-done.12 = bf16[128,4608]{1,0:T(8,128)(2,1)S(1)} copy-done((bf16[128,4608]{1,0:T(8,128)(2,1)S(1)}, bf16[128,4608]{1,0:T(8,128)(2,1)}, u32[]{:S(2)}) %copy-start.12) | copy-done | bytes 1179672
  102.7 1.0 copy-done.14
  103.7 0.9 copy-done.17
  104.6 0.9 copy-done.22
  106.4 2.0 %own_near.1.near = bf16[2,256,256]{2,1,0:T(8,128)(2,1)S(1)} custom-call(s32[4]{0:T(128)S(1)} %pad_add_fusion.at, bf16[128,4608]{1,0:T(8,128)(2,1)S(1)} %copy-done.6, bf16[128,4608]{1,0:T(8,128)(2,1)S(1)} %collective-permute-done.4.tie.own_s.near_s, bf16[128,4608]{1,0:T(8,128)(2,1)S(1)} %copy-done.2, bf16[128,4608]{1,0:T(8,128)(2,1)S(1)} %copy-done.12, ...), custom_call_target="tpu_custom_call" | custom-call | flops 1241513984 | bytes 7274496 | tf_op jit(solution)/shard_map/own_near/pallas_call | solution.py:322
  108.5 2.6 %far_products_last.1.refs_1_ = bf16[256,256]{1,0:T(8,128)(2,1)S(1)} custom-call(s32[4]{0:T(128)S(1)} %pad_add_fusion.at, bf16[128,4608]{1,0:T(8,128)(2,1)} %fence.12.three.more, bf16[128,4608]{1,0:T(8,128)(2,1)} %collective-permute-done.28.three_s.more_s, bf16[4,128,128]{2,1,0:T(8,128)(2,1)S(1)} %copy-done.23, bf16[4,128,128]{2,1,0:T(8,128)(2,1)S(1)} %copy-done.18, ...), custom_call_target="tpu_custom_call" | custom-call | flops 620756992 | bytes 3637248 | tf_op jit(solution)/shard_map/far_products_last/pallas_call | solution.py:406
  111.6 3.1 %own_rest.1.rest = bf16[2,256,256]{2,1,0:T(8,128)(2,1)S(1)} custom-call(s32[4]{0:T(128)S(1)} %pad_add_fusion.at, bf16[128,4608]{1,0:T(8,128)(2,1)S(1)} %copy-done.4, bf16[128,4608]{1,0:T(8,128)(2,1)S(1)} %copy-done.8, bf16[128,4608]{1,0:T(8,128)(2,1)} %fence.12.three.more, bf16[128,4608]{1,0:T(8,128)(2,1)} %collective-permute-done.28.three_s.more_s, ...), custom_call_target="tpu_custom_call" | custom-call | flops 1241513984 | bytes 7274496 | tf_op jit(solution)/shard_map/own_rest/pallas_call | solution.py:322
  115.4 6.6 %collective-permute-done.31.last = bf16[256,256]{1,0:T(8,128)(2,1)S(1)} collective-permute-done((bf16[256,256]{1,0:T(8,128)(2,1)S(1)}, bf16[256,256]{1,0:T(8,128)(2,1)S(1)}, u32[]{:S(2)}, u32[]{:S(2)}) %collective-permute-start.31) | collective-permute-done | bytes 131104 | tf_op jit(solution)/shard_map/out_z_last/ppermute | solution.py:60
  122.0 1.6 %place.1 = bf16[4,2,2,128,256]{4,3,2,1,0:T(8,128)(2,1)} custom-call(s32[4]{0:T(128)S(1)} %pad_add_fusion.at, bf16[2,256,256]{2,1,0:T(8,128)(2,1)S(1)} %own_near.1.near, bf16[2,256,256]{2,1,0:T(8,128)(2,1)S(1)} %own_rest.1.rest, bf16[3,256,256]{2,1,0:T(8,128)(2,1)S(1)} %collective-permute-done.30.got, bf16[256,256]{1,0:T(8,128)(2,1)S(1)} %collective-permute-done.31.last), custom_call_target="tpu_custom_call" | custom-call | tf_op jit(solution)/shard_map/place/pallas_call | solution.py:427
  (113 shorter events, 11.0 us)
Async XLA Ops:
  0.6 37.3 %collective-permute-start.4 = (bf16[128,4608]{1,0:T(8,128)(2,1)}, bf16[128,4608]{1,0:T(8,128)(2,1)S(1)}, u32[]{:S(2)}, u32[]{:S(2)}) collective-permute-start(bf16[128,4608]{1,0:T(8,128)(2,1)} %near.1), channel_id=1, source_target_pairs={{0,1},{1,0},{2,3},{3,2},{4,5},{5,4},{6,7},{7,6},{8,9},{9,8},{10,11... | collective-permute-start | bytes 3538952 | tf_op jit(solution)/shard_map/tokens_core/ppermute | solution.py:60
  0.7 44.4 %collective-permute-start.16 = (bf16[128,4608]{1,0:T(8,128)(2,1)}, bf16[128,4608]{1,0:T(8,128)(2,1)S(1)}, u32[]{:S(2)}, u32[]{:S(2)}) collective-permute-start(bf16[128,4608]{1,0:T(8,128)(2,1)} %near.1), channel_id=1, source_target_pairs={{0,4},{1,13},{4,8},{5,1},{8,12},{9,5},{12,0},{13,9},{2,6},{3,15},{... | collective-permute-start | bytes 3538952 | tf_op jit(solution)/shard_map/tokens_y/ppermute | solution.py:27
  2.8 11.6 %copy-start.5 = (bf16[128,4608]{1,0:T(8,128)(2,1)S(1)}, bf16[128,4608]{1,0:T(8,128)(2,1)}, u32[]{:S(2)}) copy-start(bf16[128,4608]{1,0:T(8,128)(2,1)} %near.1) | copy-start | bytes 3538948
  5.3 15.1 %collective-permute-start.5 = (bf16[32,4736]{1,0:T(8,128)(2,1)}, bf16[32,4736]{1,0:T(8,128)(2,1)}, u32[]{:S(2)}, u32[]{:S(2)}) collective-permute-start(bf16[32,4736]{1,0:T(8,128)(2,1)} %pad_maximum_fusion), channel_id=1, source_target_pairs={{0,2},{2,0},{1,3},{3,1},{4,6},{6,4},{5,7},{7,5},{8,10},{10,8},{9,1... | collective-permute-start | bytes 909320 | tf_op jit(solution)/shard_map/weight_z/ppermute | solution.py:60
  13.9 5.9 %collective-permute-start = (bf16[4,2,128,128]{3,2,1,0:T(8,128)(2,1)S(1)}, bf16[4,2,128,128]{3,2,1,0:T(8,128)(2,1)S(1)}, u32[]{:S(2)}, u32[]{:S(2)}) collective-permute-start(bf16[4,2,128,128]{3,2,1,0:T(8,128)(2,1)S(1)} %get-tuple-element.20), channel_id=1, source_target_pairs={{0,1},{1,0},{2,3},{3,2},{4,5},{5,4},{6,7},{7,6},{8,9},{9,8},{10,11... | collective-permute-start | bytes 786440 | tf_op jit(solution)/shard_map/act_core/ppermute | solution.py:60
  20.4 17.6 %collective-permute-start.6 = (bf16[32,4736]{1,0:T(8,128)(2,1)}, bf16[32,4736]{1,0:T(8,128)(2,1)S(1)}, u32[]{:S(2)}, u32[]{:S(2)}) collective-permute-start(bf16[32,4736]{1,0:T(8,128)(2,1)} %fence.7.mine), channel_id=1, source_target_pairs={{0,16},{16,0},{32,48},{48,32},{1,17},{17,1},{33,49},{49,33},{2,18}... | collective-permute-start | bytes 909320 | tf_op jit(solution)/shard_map/weight_zl/ppermute | solution.py:60
  26.6 5.5 %collective-permute-start.1 = (bf16[3,128,128]{2,1,0:T(8,128)(2,1)S(1)}, bf16[3,128,128]{2,1,0:T(8,128)(2,1)S(1)}, u32[]{:S(2)}, u32[]{:S(2)}) collective-permute-start(bf16[3,128,128]{2,1,0:T(8,128)(2,1)S(1)} %get-tuple-element.23), channel_id=1, source_target_pairs={{0,4},{4,0},{8,12},{12,8},{1,5},{5,1},{9,13},{13,9},{2,6},{6,2},{1... | collective-permute-start | bytes 294920 | tf_op jit(solution)/shard_map/act_y/ppermute | solution.py:60
  27.1 6.9 %collective-permute-start.2 = (bf16[3,128,128]{2,1,0:T(8,128)(2,1)S(1)}, bf16[3,128,128]{2,1,0:T(8,128)(2,1)S(1)}, u32[]{:S(2)}, u32[]{:S(2)}) collective-permute-start(bf16[3,128,128]{2,1,0:T(8,128)(2,1)S(1)} %get-tuple-element.24), channel_id=1, source_target_pairs={{0,8},{4,12},{8,0},{12,4},{1,9},{5,13},{9,1},{13,5},{2,10},{6,14},... | collective-permute-start | bytes 294920 | tf_op jit(solution)/shard_map/act_y/ppermute | solution.py:60
  32.1 5.8 %collective-permute-start.3 = (bf16[3,128,128]{2,1,0:T(8,128)(2,1)S(1)}, bf16[3,128,128]{2,1,0:T(8,128)(2,1)S(1)}, u32[]{:S(2)}, u32[]{:S(2)}) collective-permute-start(bf16[3,128,128]{2,1,0:T(8,128)(2,1)S(1)} %get-tuple-element.25), channel_id=1, source_target_pairs={{0,12},{4,8},{8,4},{12,0},{1,13},{5,9},{9,5},{13,1},{2,14},{6,10},... | collective-permute-start | bytes 294920 | tf_op jit(solution)/shard_map/act_y/ppermute | solution.py:60
  38.6 44.3 %copy-start.21 = (bf16[4,128,128]{2,1,0:T(8,128)(2,1)}, bf16[4,128,128]{2,1,0:T(8,128)(2,1)S(1)}, u32[]{:S(2)}) copy-start(bf16[4,128,128]{2,1,0:T(8,128)(2,1)S(1)} %get-tuple-element.32.mixed) | copy-start | bytes 393220
  39.6 12.8 %copy-start.10 = (bf16[128,4608]{1,0:T(8,128)(2,1)S(1)}, bf16[128,4608]{1,0:T(8,128)(2,1)}, u32[]{:S(2)}) copy-start(bf16[128,4608]{1,0:T(8,128)(2,1)} %hidden.3) | copy-start | bytes 3538948
  39.7 7.9 %collective-permute-start.7 = (bf16[128,128]{1,0:T(8,128)(2,1)S(1)}, bf16[128,128]{1,0:T(8,128)(2,1)S(1)}, u32[]{:S(2)}, u32[]{:S(2)}) collective-permute-start(bf16[128,128]{1,0:T(8,128)(2,1)S(1)} %fence.8), channel_id=1, source_target_pairs={{0,2},{2,0},{1,3},{3,1},{4,6},{6,4},{5,7},{7,5},{8,10},{10,8},{9,1... | collective-permute-start | bytes 98312 | tf_op jit(solution)/shard_map/act_z/ppermute | solution.py:60
  47.6 35.3 %copy-start.1 = (bf16[128,4608]{1,0:T(8,128)(2,1)}, bf16[128,4608]{1,0:T(8,128)(2,1)S(1)}, u32[]{:S(2)}) copy-start(bf16[128,4608]{1,0:T(8,128)(2,1)S(1)} %fence.9.one.more) | copy-start | bytes 3538948
  47.6 17.3 %collective-permute-start.17 = (bf16[128,4608]{1,0:T(8,128)(2,1)S(1)}, bf16[128,4608]{1,0:T(8,128)(2,1)S(1)}, u32[]{:S(2)}, u32[]{:S(2)}) collective-permute-start(bf16[128,4608]{1,0:T(8,128)(2,1)S(1)} %fence.9.one.more), channel_id=1, source_target_pairs={{0,4},{1,13},{4,8},{5,1},{8,12},{9,5},{12,0},{13,9},{2,6},{3,15},{... | collective-permute-start | bytes 3538952 | tf_op jit(solution)/shard_map/tokens_y/ppermute | solution.py:27
  48.9 15.9 %collective-permute-start.13 = (bf16[64,4736]{1,0:T(8,128)(2,1)S(1)}, bf16[64,4736]{1,0:T(8,128)(2,1)S(1)}, u32[]{:S(2)}, u32[]{:S(2)}) collective-permute-start(bf16[64,4736]{1,0:T(8,128)(2,1)S(1)} %join.1.refs_1_.tie.refs_0_), channel_id=1, source_target_pairs={{0,64},{1,193},{64,0},{65,129},{128,192},{129,65},{192,128},{193,1... | collective-permute-start | bytes 1818632 | tf_op jit(solution)/shard_map/weight_x/ppermute | solution.py:33
  50.4 14.4 %collective-permute-start.14 = (bf16[64,4736]{1,0:T(8,128)(2,1)S(1)}, bf16[64,4736]{1,0:T(8,128)(2,1)S(1)}, u32[]{:S(2)}, u32[]{:S(2)}) collective-permute-start(bf16[64,4736]{1,0:T(8,128)(2,1)S(1)} %join.1.refs_1_.tie.refs_0_), channel_id=1, source_target_pairs={{0,192},{1,65},{64,128},{65,1},{128,64},{129,193},{192,0},{193,129... | collective-permute-start | bytes 1818632 | tf_op jit(solution)/shard_map/weight_x/ppermute | solution.py:33
  52.5 4.0 %collective-permute-start.12 = (bf16[4,128,128]{2,1,0:T(8,128)(2,1)S(1)}, bf16[4,128,128]{2,1,0:T(8,128)(2,1)S(1)}, u32[]{:S(2)}, u32[]{:S(2)}) collective-permute-start(bf16[4,128,128]{2,1,0:T(8,128)(2,1)S(1)} %get-tuple-element.32.mixed), channel_id=1, source_target_pairs={{0,1},{1,0},{2,3},{3,2},{4,5},{5,4},{6,7},{7,6},{8,9},{9,8},{10,11... | collective-permute-start | bytes 393224 | tf_op jit(solution)/shard_map/mixed_core/ppermute | solution.py:60
  53.7 1.5 %collective-permute-start.8 = (f32[8,2304]{1,0:T(8,128)S(1)}, f32[8,2304]{1,0:T(8,128)S(1)}, u32[]{:S(2)}, u32[]{:S(2)}) collective-permute-start(f32[8,2304]{1,0:T(8,128)S(1)} %get-tuple-element.31), channel_id=1, source_target_pairs={{0,1},{1,0},{2,3},{3,2},{4,5},{5,4},{6,7},{7,6},{8,9},{9,8},{10,11... | collective-permute-start | bytes 221192 | tf_op jit(solution)/shard_map/gate_core/ppermute | solution.py:60
  55.2 5.6 %collective-permute-start.10 = (bf16[8,2304]{1,0:T(8,128)(2,1)S(1)}, bf16[8,2304]{1,0:T(8,128)(2,1)S(1)}, u32[]{:S(2)}, u32[]{:S(2)}) collective-permute-start(bf16[8,2304]{1,0:T(8,128)(2,1)S(1)} %convert_element_type.2), channel_id=1, source_target_pairs={{0,32},{16,48},{32,0},{48,16},{1,33},{17,49},{33,1},{49,17},{2,34}... | collective-permute-start | bytes 110600 | tf_op jit(solution)/shard_map/gate_zl/ppermute | solution.py:60
  56.5 26.4 %copy-start.16 = (bf16[4,128,128]{2,1,0:T(8,128)(2,1)}, bf16[4,128,128]{2,1,0:T(8,128)(2,1)S(1)}, u32[]{:S(2)}) copy-start(bf16[4,128,128]{2,1,0:T(8,128)(2,1)S(1)} %collective-permute-done.12.refs_0_.mixed_s) | copy-start | bytes 393220
  56.5 5.8 %collective-permute-start.11 = (bf16[8,2304]{1,0:T(8,128)(2,1)S(1)}, bf16[8,2304]{1,0:T(8,128)(2,1)S(1)}, u32[]{:S(2)}, u32[]{:S(2)}) collective-permute-start(bf16[8,2304]{1,0:T(8,128)(2,1)S(1)} %convert_element_type.2), channel_id=1, source_target_pairs={{0,48},{16,32},{32,16},{48,0},{1,49},{17,33},{33,17},{49,1},{2,50}... | collective-permute-start | bytes 110600 | tf_op jit(solution)/shard_map/gate_zl/ppermute | solution.py:60
  60.8 4.0 %collective-permute-start.9 = (bf16[8,2304]{1,0:T(8,128)(2,1)S(1)}, bf16[8,2304]{1,0:T(8,128)(2,1)S(1)}, u32[]{:S(2)}, u32[]{:S(2)}) collective-permute-start(bf16[8,2304]{1,0:T(8,128)(2,1)S(1)} %convert_element_type.2), channel_id=1, source_target_pairs={{0,16},{16,0},{32,48},{48,32},{1,17},{17,1},{33,49},{49,33},{2,18}... | collective-permute-start | bytes 110600 | tf_op jit(solution)/shard_map/gate_zl/ppermute | solution.py:60
  64.9 18.0 %copy-start.3 = (bf16[128,4608]{1,0:T(8,128)(2,1)}, bf16[128,4608]{1,0:T(8,128)(2,1)S(1)}, u32[]{:S(2)}) copy-start(bf16[128,4608]{1,0:T(8,128)(2,1)S(1)} %fence.10.two.near) | copy-start | bytes 3538948
  64.9 13.2 %collective-permute-start.18 = (bf16[128,4608]{1,0:T(8,128)(2,1)S(1)}, bf16[128,4608]{1,0:T(8,128)(2,1)S(1)}, u32[]{:S(2)}, u32[]{:S(2)}) collective-permute-start(bf16[128,4608]{1,0:T(8,128)(2,1)S(1)} %fence.10.two.near), channel_id=1, source_target_pairs={{0,1},{1,0},{2,3},{3,2},{4,5},{5,4},{6,7},{7,6},{8,9},{9,8},{10,11... | collective-permute-start | bytes 3538952 | tf_op jit(solution)/shard_map/tokens_core/ppermute | solution.py:60
  65.1 17.7 %collective-permute-start.23 = (bf16[128,4608]{1,0:T(8,128)(2,1)S(1)}, bf16[128,4608]{1,0:T(8,128)(2,1)S(1)}, u32[]{:S(2)}, u32[]{:S(2)}) collective-permute-start(bf16[128,4608]{1,0:T(8,128)(2,1)S(1)} %fence.9.one.more), channel_id=1, source_target_pairs={{0,1},{1,0},{2,3},{3,2},{4,5},{5,4},{6,7},{7,6},{8,9},{9,8},{10,11... | collective-permute-start | bytes 3538952 | tf_op jit(solution)/shard_map/tokens_core/ppermute | solution.py:60
  65.6 22.4 %collective-permute-start.27 = (bf16[128,4608]{1,0:T(8,128)(2,1)S(1)}, bf16[128,4608]{1,0:T(8,128)(2,1)}, u32[]{:S(2)}, u32[]{:S(2)}) collective-permute-start(bf16[128,4608]{1,0:T(8,128)(2,1)S(1)} %fence.10.two.near), channel_id=1, source_target_pairs={{0,4},{1,13},{4,8},{5,1},{8,12},{9,5},{12,0},{13,9},{2,6},{3,15},{... | collective-permute-start | bytes 3538952 | tf_op jit(solution)/shard_map/tokens_y/ppermute | solution.py:27
  66.8 11.3 %collective-permute-start.19 = (bf16[64,4736]{1,0:T(8,128)(2,1)S(1)}, bf16[64,4736]{1,0:T(8,128)(2,1)S(1)}, u32[]{:S(2)}, u32[]{:S(2)}) collective-permute-start(bf16[64,4736]{1,0:T(8,128)(2,1)S(1)} %fence.11.refs_1_), channel_id=1, source_target_pairs={{0,192},{1,65},{64,128},{65,1},{128,64},{129,193},{192,0},{193,129... | collective-permute-start | bytes 1818632 | tf_op jit(solution)/shard_map/weight_x_far/ppermute | solution.py:33
  69.6 8.3 %collective-permute-start.15 = (f32[8,2304]{1,0:T(8,128)S(1)}, f32[8,2304]{1,0:T(8,128)S(1)}, u32[]{:S(2)}, u32[]{:S(2)}) collective-permute-start(f32[8,2304]{1,0:T(8,128)S(1)} %gate_sum.6.refs_1_.left), channel_id=1, source_target_pairs={{0,2},{2,0},{1,3},{3,1},{4,6},{6,4},{5,7},{7,5},{8,10},{10,8},{9,1... | collective-permute-start | bytes 221192 | tf_op jit(solution)/shard_map/gate_zh/ppermute | solution.py:60
  78.1 7.7 %copy-start.7 = (bf16[128,4608]{1,0:T(8,128)(2,1)}, bf16[128,4608]{1,0:T(8,128)(2,1)S(1)}, u32[]{:S(2)}) copy-start(bf16[128,4608]{1,0:T(8,128)(2,1)S(1)} %collective-permute-done.18.refs_0_.two_s.near_s) | copy-start | bytes 3538948
  78.1 7.7 %collective-permute-start.20 = (f32[8,2304]{1,0:T(8,128)S(1)}, f32[8,2304]{1,0:T(8,128)S(1)}, u32[]{:S(2)}, u32[]{:S(2)}) collective-permute-start(f32[8,2304]{1,0:T(8,128)S(1)} %gate_sum.7.refs_4_.first), channel_id=1, source_target_pairs={{0,64},{64,0},{128,192},{192,128},{1,65},{65,1},{129,193},{193,129... | collective-permute-start | bytes 221192 | tf_op jit(solution)/shard_map/gate_x/ppermute | solution.py:60
  79.0 6.8 %collective-permute-start.21 = (f32[8,2304]{1,0:T(8,128)S(1)}, f32[8,2304]{1,0:T(8,128)S(1)}, u32[]{:S(2)}, u32[]{:S(2)}) collective-permute-start(f32[8,2304]{1,0:T(8,128)S(1)} %gate_sum.7.refs_4_.first), channel_id=1, source_target_pairs={{0,128},{64,192},{128,0},{192,64},{1,129},{65,193},{129,1},{193,65... | collective-permute-start | bytes 221192 | tf_op jit(solution)/shard_map/gate_x/ppermute | solution.py:60
  82.4 5.6 %collective-permute-start.22 = (f32[8,2304]{1,0:T(8,128)S(1)}, f32[8,2304]{1,0:T(8,128)S(1)}, u32[]{:S(2)}, u32[]{:S(2)}) collective-permute-start(f32[8,2304]{1,0:T(8,128)S(1)} %gate_sum.7.refs_4_.first), channel_id=1, source_target_pairs={{0,192},{64,128},{128,64},{192,0},{1,193},{65,129},{129,65},{193,1... | collective-permute-start | bytes 221192 | tf_op jit(solution)/shard_map/gate_x/ppermute | solution.py:60
  82.9 2.8 %copy-start.11 = (bf16[128,4608]{1,0:T(8,128)(2,1)}, bf16[128,4608]{1,0:T(8,128)(2,1)S(1)}, u32[]{:S(2)}) copy-start(bf16[128,4608]{1,0:T(8,128)(2,1)S(1)} %collective-permute-done.23.one_s.more_s) | copy-start | bytes 3538948
  85.8 2.3 %copy-start.13 = (bf16[3,256,256]{2,1,0:T(8,128)(2,1)}, bf16[3,256,256]{2,1,0:T(8,128)(2,1)S(1)}, u32[]{:S(2)}) copy-start(bf16[3,256,256]{2,1,0:T(8,128)(2,1)S(1)} %get-tuple-element.33.refs_0_.tie) | copy-start | bytes 1179652
  85.8 2.3 %copy-start.19 = (bf16[256,4608]{1,0:T(8,128)(2,1)}, bf16[256,4608]{1,0:T(8,128)(2,1)S(1)}, u32[]{:S(2)}) copy-start(bf16[256,4608]{1,0:T(8,128)(2,1)S(1)} %get-tuple-element.34.weight) | copy-start | bytes 7077892
  85.8 2.3 %copy-start.32 = (bf16[256,128]{1,0:T(8,128)(2,1)}, bf16[256,128]{1,0:T(8,128)(2,1)S(1)}, u32[]{:S(2)}) copy-start(bf16[256,128]{1,0:T(8,128)(2,1)S(1)} %get-tuple-element.35.down) | copy-start | bytes 196612
  88.0 10.9 %copy-start = (bf16[256,4608]{1,0:T(8,128)(2,1)S(1)}, bf16[256,4608]{1,0:T(8,128)(2,1)}, u32[]{:S(2)}) copy-start(bf16[256,4608]{1,0:T(8,128)(2,1)} %weight.3) | copy-start | bytes 7077892
  88.6 19.8 %collective-permute-start.28 = (bf16[128,4608]{1,0:T(8,128)(2,1)}, bf16[128,4608]{1,0:T(8,128)(2,1)}, u32[]{:S(2)}, u32[]{:S(2)}) collective-permute-start(bf16[128,4608]{1,0:T(8,128)(2,1)} %fence.12.three.more), channel_id=1, source_target_pairs={{0,1},{1,0},{2,3},{3,2},{4,5},{5,4},{6,7},{7,6},{8,9},{9,8},{10,11... | collective-permute-start | bytes 3538952 | tf_op jit(solution)/shard_map/tokens_core/ppermute | solution.py:60
  88.6 26.8 %collective-permute-start.30 = (bf16[3,256,256]{2,1,0:T(8,128)(2,1)}, bf16[3,256,256]{2,1,0:T(8,128)(2,1)S(1)}, u32[]{:S(2)}, u32[]{:S(2)}) collective-permute-start(bf16[3,256,256]{2,1,0:T(8,128)(2,1)} %copy-done.13), channel_id=1, source_target_pairs={{0,2},{2,0},{1,3},{3,1},{4,6},{6,4},{5,7},{7,5},{8,10},{10,8},{9,1... | collective-permute-start | bytes 1179656 | tf_op jit(solution)/shard_map/out_z/ppermute | solution.py:60
  94.2 14.2 %collective-permute-start.24 = (f32[8,2304]{1,0:T(8,128)}, f32[8,2304]{1,0:T(8,128)S(1)}, u32[]{:S(2)}, u32[]{:S(2)}) collective-permute-start(f32[8,2304]{1,0:T(8,128)} %copy-done.26), channel_id=1, source_target_pairs={{0,4},{4,0},{8,12},{12,8},{1,5},{5,1},{9,13},{13,9},{2,6},{6,2},{1... | collective-permute-start | bytes 221192 | tf_op jit(solution)/shard_map/gate_y/ppermute | solution.py:60
  94.2 14.2 %collective-permute-start.25 = (f32[8,2304]{1,0:T(8,128)}, f32[8,2304]{1,0:T(8,128)S(1)}, u32[]{:S(2)}, u32[]{:S(2)}) collective-permute-start(f32[8,2304]{1,0:T(8,128)} %copy-done.26), channel_id=1, source_target_pairs={{0,8},{4,12},{8,0},{12,4},{1,9},{5,13},{9,1},{13,5},{2,10},{6,14},... | collective-permute-start | bytes 221192 | tf_op jit(solution)/shard_map/gate_y/ppermute | solution.py:60
  95.7 12.7 %collective-permute-start.26 = (f32[8,2304]{1,0:T(8,128)}, f32[8,2304]{1,0:T(8,128)S(1)}, u32[]{:S(2)}, u32[]{:S(2)}) collective-permute-start(f32[8,2304]{1,0:T(8,128)} %copy-done.26), channel_id=1, source_target_pairs={{0,12},{4,8},{8,4},{12,0},{1,13},{5,9},{9,5},{13,1},{2,14},{6,10},... | collective-permute-start | bytes 221192 | tf_op jit(solution)/shard_map/gate_y/ppermute | solution.py:60
  108.5 3.1 %copy-start.4 = (bf16[128,4608]{1,0:T(8,128)(2,1)S(1)}, bf16[128,4608]{1,0:T(8,128)(2,1)}, u32[]{:S(2)}) copy-start(bf16[128,4608]{1,0:T(8,128)(2,1)} %copy-done.3) | copy-start | bytes 3538948
  108.5 3.1 %copy-start.8 = (bf16[128,4608]{1,0:T(8,128)(2,1)S(1)}, bf16[128,4608]{1,0:T(8,128)(2,1)}, u32[]{:S(2)}) copy-start(bf16[128,4608]{1,0:T(8,128)(2,1)} %copy-done.7) | copy-start | bytes 3538948
  108.5 3.1 %copy-start.15 = (bf16[3,256,256]{2,1,0:T(8,128)(2,1)S(1)}, bf16[3,256,256]{2,1,0:T(8,128)(2,1)}, u32[]{:S(2)}) copy-start(bf16[3,256,256]{2,1,0:T(8,128)(2,1)} %copy-done.13) | copy-start | bytes 1179652
  108.5 3.1 %copy-start.30 = (bf16[256,128]{1,0:T(8,128)(2,1)S(1)}, bf16[256,128]{1,0:T(8,128)(2,1)}, u32[]{:S(2)}) copy-start(bf16[256,128]{1,0:T(8,128)(2,1)} %down.5) | copy-start | bytes 196612
  111.1 10.8 %collective-permute-start.31 = (bf16[256,256]{1,0:T(8,128)(2,1)S(1)}, bf16[256,256]{1,0:T(8,128)(2,1)S(1)}, u32[]{:S(2)}, u32[]{:S(2)}) collective-permute-start(bf16[256,256]{1,0:T(8,128)(2,1)S(1)} %far_products_last.1.refs_1_), channel_id=1, source_target_pairs={{0,2},{2,0},{1,3},{3,1},{4,6},{6,4},{5,7},{7,5},{8,10},{10,8},{9,1... | collective-permute-start | bytes 393224 | tf_op jit(solution)/shard_map/out_z_last/ppermute | solution.py:60
  111.6 3.1 %collective-permute-start.29 = (f32[8,2304]{1,0:T(8,128)S(1)}, f32[8,2304]{1,0:T(8,128)S(1)}, u32[]{:S(2)}, u32[]{:S(2)}) collective-permute-start(f32[8,2304]{1,0:T(8,128)S(1)} %fence.13), channel_id=1, source_target_pairs={{0,1},{1,0},{2,3},{3,2},{4,5},{5,4},{6,7},{7,6},{8,9},{9,8},{10,11... | collective-permute-start | bytes 221192 | tf_op jit(solution)/shard_map/gate_core_back/ppermute | solution.py:60
  (18 other events, 24.0 us)

commit v11 on v9

--- a/solution.py
+++ b/solution.py
@@ -16,7 +16,7 @@
 ANY = pl.BlockSpec(memory_space=pl.ANY)
 HBM = pl.BlockSpec(memory_space=pltpu.HBM)
 SMALL = pltpu.CompilerParams(vmem_limit_bytes=8 * 1024 * 1024)
-MIDDLE = pltpu.CompilerParams(vmem_limit_bytes=24 * 1024 * 1024)
+MIDDLE = pltpu.CompilerParams(vmem_limit_bytes=16 * 1024 * 1024)
 
 
 def ring(value, axis):
@@ -145,7 +145,16 @@
 
 
 def add_kernel(left, right, *refs):
-    refs[-1][...] = left[...] + right[...]
+    total = left[...] + right[...]
+    refs[-2][...] = total
+    refs[-1][...] = total.astype(refs[-1].dtype)
+
+
+def halves_kernel(at, mine, other, out):
+    half = mine.shape[1]
+    c = at[3]
+    for side, ref in ((c, mine), (1 - c, other)):
+        out[:, pl.ds(pl.multiple_of(side * half, 128), half)] = ref[...]
 
 
 def add4_kernel(first, second, third, fourth, *refs):
@@ -321,10 +330,10 @@
         return pl.pallas_call(
             add_kernel,
             in_specs=[VMEM, VMEM] + [ANY] * len(ties),
-            out_specs=VMEM,
-            out_shape=shaped(left.shape, F32),
+            out_specs=[VMEM, VMEM],
+            out_shape=[shaped(left.shape, F32), shaped(left.shape, BF16)],
             compiler_params=SMALL,
-        name="gate_sum",
+            name="gate_sum",
         )(left, right, *ties)
 
     def add4(*parts):
@@ -337,21 +346,22 @@
         name="gate_sum",
         )(*parts)
 
-    def step(total, axis, *ties, dtype=F32):
+    def step(total, axis, *ties, message=None):
+        message = total if message is None else message
         with jax.named_scope("gate_" + axis):
-            got = [swap(total.astype(dtype), axis, mask) for mask in (1, 2, 3)]
+            got = [swap(message, axis, mask) for mask in (1, 2, 3)]
         return add4(total, *got, *ties)
 
     with jax.named_scope("gate_core"):
         got = swap(give, "c", 1)
-    total = add(total, got, w_first, w_second)
+    total, message = add(total, got, w_first, w_second)
     (w_first,) = fence((w_first,), total)
     with jax.named_scope("weight_x_far"):
         w_far = pairs(w_first, "x", False)
     (two,) = fence((two,), w_first)
     with jax.named_scope("tokens_y"):
         three = ring(two, "y")
-    total = step(total, "zl", mixed_s, w_far, two, dtype=BF16)
+    total = step(total, "zl", mixed_s, w_far, two, message=message)
     with jax.named_scope("tokens_core"):
         two_s = swap(two, "c", 1)
 
@@ -394,12 +404,17 @@
     own_rest = products("own_rest", 2, two, two_s, three, three_s, weight, down, far)
     with jax.named_scope("gate_zh"):
         got = swap(total, "zh", 1)
-    total = add(total, got, last, far_got)
+    total, _ = add(total, got, last, far_got)
     with jax.named_scope("gate_core_back"):
         other = swap(total, "c", 1)
-    gate_grad = jnp.where(
-        c == 0, jnp.concatenate([total, other], axis=1), jnp.concatenate([other, total], axis=1)
-    )
+    gate_grad = pl.pallas_call(
+        halves_kernel,
+        in_specs=[SMEM, VMEM, VMEM],
+        out_specs=VMEM,
+        out_shape=shaped((adapters, width), F32),
+        compiler_params=SMALL,
+        name="gate_halves",
+    )(at, total, other)
 
     out = pl.pallas_call(
         place_kernel,

time: 122 us -> 122 us (level)
  waiting for transfers between devices: 27.8 us -> 37 us
  local copies, waits for them, and re-layouts: 13.8 us -> 7.33 us
  Pallas kernels: 22.5 us -> 17.6 us
  starting transfers between devices: 54.9 us -> 57.4 us
    ppermute x25, waiting for transfers between devices: 26.7 us -> 34.4 us  [swap(): return lax.ppermute(value, axis, [(i, i ^ mask) for i in range(size)])]
    unnamed x56 -> x18, local copies, waits for them, and re-layouts: 11.8 us -> 5.5 us
    ppermute x25, starting transfers between devices: 47.4 us -> 51.3 us  [swap(): return lax.ppermute(value, axis, [(i, i ^ mask) for i in range(size)])]
    pallas_call x2, Pallas kernels: 5.9 us -> 3.97 us  [products(): pl.pallas_call(functools.partial(product_kernel, first), in_specs=[SMEM]...]
    ppermute x3, waiting for transfers between devices: 1.08 us -> 2.66 us  [pairs(): lax.ppermute(value, (axis, 'c'), [(2 * i + c, 2 * partner(i, c) + c) for...]
    pallas_call x1, Pallas kernels: 4.89 us -> 3.35 us  [on_device(): pl.pallas_call(far_kernel, in_specs=[SMEM] + [VMEM] * 12 + [ANY], out_spe...]
  transfers between devices with their start and end apart: 31 -> 31, of which waited for: 12 -> 13; matrix products, arithmetic and copies ran while one was open for 3% -> 2% of each run, Pallas kernels for 17% -> 13%
where the time goes in v11:
time: 122 us; the launch traced here: 121 us
  starting transfers between devices  57.4 us (47%)
  waiting for transfers between devices  37 us (30%)
  Pallas kernels  17.6 us (14%)
  local copies, waits for them, and re-layouts  7.33 us (6%)
    ppermute x25, starting transfers between devices, swap(): return lax.ppermute(value, axis, [(i, i ^ mask) for i in range(size)])  51.3 us
    ppermute x25, waiting for transfers between devices, swap(): return lax.ppermute(value, axis, [(i, i ^ mask) for i in range(size)])  34.4 us
    unnamed x18, local copies, waits for them, and re-layouts  5.5 us
    pallas_call x2, Pallas kernels, products(): pl.pallas_call(functools.partial(product_kernel, first), in_specs=[SMEM]...  3.97 us
    ppermute x3, starting transfers between devices, ring(): return lax.ppermute(value, (axis, 'c'), pairs)  3.62 us
    pallas_call x1, Pallas kernels, on_device(): pl.pallas_call(far_kernel, in_specs=[SMEM] + [VMEM] * 12 + [ANY], out_spe...  3.35 us
    ppermute x3, waiting for transfers between devices, pairs(): lax.ppermute(value, (axis, 'c'), [(2 * i + c, 2 * partner(i, c) + c) for...  2.66 us
    ppermute x3, starting transfers between devices, pairs(): lax.ppermute(value, (axis, 'c'), [(2 * i + c, 2 * partner(i, c) + c) for...  2.52 us
  transfers between devices with their start and end apart: 31, of which 13 were waited for; matrix products, arithmetic and copies ran while one was open for 2% of the time, Pallas kernels for 13%

profile of v11, /device:TPU:1, one launch (start us, length us, event | category | flops | bytes accessed | tf_op | source)
XLA Modules:
  0.0 121.4 jit_solution(7657241353959122209)
XLA Ops:
  0.6 3.3 %collective-permute-start.4 = (bf16[128,4608]{1,0:T(8,128)(2,1)}, bf16[128,4608]{1,0:T(8,128)(2,1)S(1)}, u32[]{:S(2)}, u32[]{:S(2)}) collective-permute-start(bf16[128,4608]{1,0:T(8,128)(2,1)} %own.1), channel_id=1, source_target_pairs={{0,1},{1,0},{2,3},{3,2},{4,5},{5,4},{6,7},{7,6},{8,9},{9,8},{10,11... | collective-permute-start | bytes 3538952 | tf_op jit(solution)/shard_map/tokens_core/ppermute | solution.py:60
  4.0 1.0 collective-permute-start.6
  5.0 1.1 constant_dynamic-slice_fusion.1
  6.1 0.7 constant_dynamic-slice_fusion
  6.8 0.9 pad_maximum_fusion
  7.7 6.9 %collective-permute-start.7 = (bf16[64,4736]{1,0:T(8,128)(2,1)}, bf16[64,4736]{1,0:T(8,128)(2,1)}, u32[]{:S(2)}, u32[]{:S(2)}) collective-permute-start(bf16[64,4736]{1,0:T(8,128)(2,1)} %pad_maximum_fusion), channel_id=1, source_target_pairs={{0,2},{2,0},{1,3},{3,1},{4,6},{6,4},{5,7},{7,5},{8,10},{10,8},{9,1... | collective-permute-start | bytes 1818632 | tf_op jit(solution)/shard_map/weight_z/ppermute | solution.py:60
  14.6 1.2 %copy-done.5 = bf16[2048,256]{1,0:T(8,128)(2,1)S(1)} copy-done((bf16[2048,256]{1,0:T(8,128)(2,1)S(1)}, bf16[2048,256]{1,0:T(8,128)(2,1)}, u32[]{:S(2)}) %copy-start.5) | copy-done | bytes 1048600
  15.9 0.8 copy-done.6
  16.7 1.0 rank_products.1
  17.8 1.3 %copy-done.2 = bf16[128,4608]{1,0:T(8,128)(2,1)S(1)} copy-done((bf16[128,4608]{1,0:T(8,128)(2,1)S(1)}, bf16[128,4608]{1,0:T(8,128)(2,1)}, u32[]{:S(2)}) %copy-start.2) | copy-done | bytes 1179672
  19.1 1.3 %copy-done.4 = bf16[128,4608]{1,0:T(8,128)(2,1)S(1)} copy-done((bf16[128,4608]{1,0:T(8,128)(2,1)S(1)}, bf16[128,4608]{1,0:T(8,128)(2,1)}, u32[]{:S(2)}) %copy-start.4) | copy-done | bytes 1179672
  20.3 0.9 copy-done.8
  21.2 2.0 %token_values.1 = (bf16[128,128]{1,0:T(8,128)(2,1)S(1)}, f32[8,128]{1,0:T(8,128)S(1)}, f32[128,128]{1,0:T(8,128)S(1)}) custom-call(s32[4]{0:T(128)S(1)} %pad_add_fusion.at, bf16[128,4608]{1,0:T(8,128)(2,1)S(1)} %copy-done.2, bf16[128,4608]{1,0:T(8,128)(2,1)S(1)} %copy-done.1, bf16[128,4608]{1,0:T(8,128)(2,1)S(1)} %copy-done.4, bf16[8,4608]{1,0:T(8,128)(2,1)S(1)} %copy-done.8), custom_call_target="tpu_custom_call" | custom-call | flops 452984832 | bytes 7077888 | tf_op jit(solution)/shard_map/token_values/pallas_call | solution.py:257
  24.4 1.4 %collective-permute-start.2 = (bf16[3,128,128]{2,1,0:T(8,128)(2,1)S(1)}, bf16[3,128,128]{2,1,0:T(8,128)(2,1)S(1)}, u32[]{:S(2)}, u32[]{:S(2)}) collective-permute-start(bf16[3,128,128]{2,1,0:T(8,128)(2,1)S(1)} %get-tuple-element.29), channel_id=1, source_target_pairs={{0,8},{4,12},{8,0},{12,4},{1,9},{5,13},{9,1},{13,5},{2,10},{6,14},... | collective-permute-start | bytes 294920 | tf_op jit(solution)/shard_map/act_y/ppermute | solution.py:60
  25.8 2.1 %collective-permute-done.1.first = bf16[3,128,128]{2,1,0:T(8,128)(2,1)S(1)} collective-permute-done((bf16[3,128,128]{2,1,0:T(8,128)(2,1)S(1)}, bf16[3,128,128]{2,1,0:T(8,128)(2,1)S(1)}, u32[]{:S(2)}, u32[]{:S(2)}) %collective-permute-start.1) | collective-permute-done | bytes 98336 | tf_op jit(solution)/shard_map/act_y/ppermute | solution.py:60
  27.9 0.8 collective-permute-start.3
  28.7 2.0 %collective-permute-done.2.second = bf16[3,128,128]{2,1,0:T(8,128)(2,1)S(1)} collective-permute-done((bf16[3,128,128]{2,1,0:T(8,128)(2,1)S(1)}, bf16[3,128,128]{2,1,0:T(8,128)(2,1)S(1)}, u32[]{:S(2)}, u32[]{:S(2)}) %collective-permute-start.2) | collective-permute-done | bytes 98336 | tf_op jit(solution)/shard_map/act_y/ppermute | solution.py:60
  30.7 1.9 %collective-permute-done.3.third = bf16[3,128,128]{2,1,0:T(8,128)(2,1)S(1)} collective-permute-done((bf16[3,128,128]{2,1,0:T(8,128)(2,1)S(1)}, bf16[3,128,128]{2,1,0:T(8,128)(2,1)S(1)}, u32[]{:S(2)}, u32[]{:S(2)}) %collective-permute-start.3) | collective-permute-done | bytes 98336 | tf_op jit(solution)/shard_map/act_y/ppermute | solution.py:60
  33.2 7.2 %collective-permute-done.7.refs_1_ = bf16[64,4736]{1,0:T(8,128)(2,1)} collective-permute-done((bf16[64,4736]{1,0:T(8,128)(2,1)}, bf16[64,4736]{1,0:T(8,128)(2,1)}, u32[]{:S(2)}, u32[]{:S(2)}) %collective-permute-start.7) | collective-permute-done | bytes 606240 | tf_op jit(solution)/shard_map/weight_z/ppermute | solution.py:60
  40.4 1.2 collective-permute-start.17
  41.6 2.5 %collective-permute-start.11 = (bf16[64,4736]{1,0:T(8,128)(2,1)}, bf16[64,4736]{1,0:T(8,128)(2,1)S(1)}, u32[]{:S(2)}, u32[]{:S(2)}) collective-permute-start(bf16[64,4736]{1,0:T(8,128)(2,1)} %get-tuple-element.39.refs_0_), channel_id=1, source_target_pairs={{0,64},{1,193},{64,0},{65,129},{128,192},{129,65},{192,128},{193,1... | collective-permute-start | bytes 1818632 | tf_op jit(solution)/shard_map/weight_x/ppermute | solution.py:33
  44.5 1.0 collective-permute-done.9.mixed_s.refs_0_
  45.5 6.1 %collective-permute-start.5 = (bf16[128,128]{1,0:T(8,128)(2,1)S(1)}, bf16[128,128]{1,0:T(8,128)(2,1)S(1)}, u32[]{:S(2)}, u32[]{:S(2)}) collective-permute-start(bf16[128,128]{1,0:T(8,128)(2,1)S(1)} %get-tuple-element.32.refs_2_.tie), channel_id=1, source_target_pairs={{0,2},{2,0},{1,3},{3,1},{4,6},{6,4},{5,7},{7,5},{8,10},{10,8},{9,1... | collective-permute-start | bytes 98312 | tf_op jit(solution)/shard_map/act_z/ppermute | solution.py:60
  51.6 2.0 %own_near.1.tie.near = bf16[2,256,256]{2,1,0:T(8,128)(2,1)S(1)} custom-call(s32[4]{0:T(128)S(1)} %pad_add_fusion.at, bf16[128,4608]{1,0:T(8,128)(2,1)S(1)} %copy-done.1, bf16[128,4608]{1,0:T(8,128)(2,1)S(1)} %collective-permute-done.4.tie.near_s.own_s, bf16[128,4608]{1,0:T(8,128)(2,1)S(1)} %get-tuple-element.35.more.one, ...), custom_call_target="tpu_custom_call" | custom-call | flops 1241513984 | bytes 7274496 | tf_op jit(solution)/shard_map/own_near/pallas_call | solution.py:308
  53.6 1.2 %gate_products.1 = (f32[8,2304]{1,0:T(8,128)S(1)}, f32[8,2304]{1,0:T(8,128)S(1)}) custom-call(s32[4]{0:T(128)S(1)} %pad_add_fusion.at, f32[128,128]{1,0:T(8,128)S(1)} %get-tuple-element.31.keep, bf16[128,128]{1,0:T(8,128)(2,1)S(1)} %collective-permute-done.5.got, f32[128,128]{1,0:T(8,128)S(1)} %get-tuple-element.33.back, ...), custom_call_target="tpu_custom_call" | custom-call | tf_op jit(solution)/shard_map/gate_products/pallas_call | solution.py:320
  55.4 2.0 %collective-permute-done.11.refs_0_ = bf16[64,4736]{1,0:T(8,128)(2,1)S(1)} collective-permute-done((bf16[64,4736]{1,0:T(8,128)(2,1)}, bf16[64,4736]{1,0:T(8,128)(2,1)S(1)}, u32[]{:S(2)}, u32[]{:S(2)}) %collective-permute-start.11) | collective-permute-done | bytes 606240 | tf_op jit(solution)/shard_map/weight_x/ppermute | solution.py:33
  57.5 1.8 %collective-permute-start.21 = (bf16[128,4608]{1,0:T(8,128)(2,1)S(1)}, bf16[128,4608]{1,0:T(8,128)(2,1)S(1)}, u32[]{:S(2)}, u32[]{:S(2)}) collective-permute-start(bf16[128,4608]{1,0:T(8,128)(2,1)S(1)} %fence.6.refs_2_.two.near), channel_id=1, source_target_pairs={{0,1},{1,0},{2,3},{3,2},{4,5},{5,4},{6,7},{7,6},{8,9},{9,8},{10,11... | collective-permute-start | bytes 3538952 | tf_op jit(solution)/shard_map/tokens_core/ppermute | solution.py:60
  59.3 1.4 %collective-permute-start.26 = (bf16[128,4608]{1,0:T(8,128)(2,1)S(1)}, bf16[128,4608]{1,0:T(8,128)(2,1)S(1)}, u32[]{:S(2)}, u32[]{:S(2)}) collective-permute-start(bf16[128,4608]{1,0:T(8,128)(2,1)S(1)} %fence.6.refs_2_.two.near), channel_id=1, source_target_pairs={{0,4},{1,13},{4,8},{5,1},{8,12},{9,5},{12,0},{13,9},{2,6},{3,15},{... | collective-permute-start | bytes 3538952 | tf_op jit(solution)/shard_map/tokens_y/ppermute | solution.py:27
  60.7 2.2 %collective-permute-start.13 = (bf16[8,2304]{1,0:T(8,128)(2,1)S(1)}, bf16[8,2304]{1,0:T(8,128)(2,1)S(1)}, u32[]{:S(2)}, u32[]{:S(2)}) collective-permute-start(bf16[8,2304]{1,0:T(8,128)(2,1)S(1)} %get-tuple-element.41), channel_id=1, source_target_pairs={{0,16},{16,0},{32,48},{48,32},{1,17},{17,1},{33,49},{49,33},{2,18}... | collective-permute-start | bytes 110600 | tf_op jit(solution)/shard_map/gate_zl/ppermute | solution.py:60
  63.0 0.6 collective-permute-start.14
  63.6 1.0 collective-permute-done.13.second
  64.6 1.8 %collective-permute-start.15 = (bf16[8,2304]{1,0:T(8,128)(2,1)S(1)}, bf16[8,2304]{1,0:T(8,128)(2,1)S(1)}, u32[]{:S(2)}, u32[]{:S(2)}) collective-permute-start(bf16[8,2304]{1,0:T(8,128)(2,1)S(1)} %get-tuple-element.41), channel_id=1, source_target_pairs={{0,48},{16,32},{32,16},{48,0},{1,49},{17,33},{33,17},{49,1},{2,50}... | collective-permute-start | bytes 110600 | tf_op jit(solution)/shard_map/gate_zl/ppermute | solution.py:60
  66.4 0.8 collective-permute-done.14.third
  67.2 2.1 %collective-permute-done.15.fourth = bf16[8,2304]{1,0:T(8,128)(2,1)S(1)} collective-permute-done((bf16[8,2304]{1,0:T(8,128)(2,1)S(1)}, bf16[8,2304]{1,0:T(8,128)(2,1)S(1)}, u32[]{:S(2)}, u32[]{:S(2)}) %collective-permute-start.15) | collective-permute-done | bytes 36896 | tf_op jit(solution)/shard_map/gate_zl/ppermute | solution.py:60
  70.3 2.1 %collective-permute-start.19 = (f32[8,2304]{1,0:T(8,128)S(1)}, f32[8,2304]{1,0:T(8,128)S(1)}, u32[]{:S(2)}, u32[]{:S(2)}) collective-permute-start(f32[8,2304]{1,0:T(8,128)S(1)} %gate_sum.6.refs_4_.first), channel_id=1, source_target_pairs={{0,128},{64,192},{128,0},{192,64},{1,129},{65,193},{129,1},{193,65... | collective-permute-start | bytes 221192 | tf_op jit(solution)/shard_map/gate_x/ppermute | solution.py:60
  72.4 1.5 %collective-permute-start.20 = (f32[8,2304]{1,0:T(8,128)S(1)}, f32[8,2304]{1,0:T(8,128)S(1)}, u32[]{:S(2)}, u32[]{:S(2)}) collective-permute-start(f32[8,2304]{1,0:T(8,128)S(1)} %gate_sum.6.refs_4_.first), channel_id=1, source_target_pairs={{0,192},{64,128},{128,64},{192,0},{1,193},{65,129},{129,65},{193,1... | collective-permute-start | bytes 221192 | tf_op jit(solution)/shard_map/gate_x/ppermute | solution.py:60
  73.9 3.3 %far_products.1 = (bf16[3,256,256]{2,1,0:T(8,128)(2,1)S(1)}, bf16[256,4608]{1,0:T(8,128)(2,1)S(1)}, bf16[256,128]{1,0:T(8,128)(2,1)S(1)}) custom-call(s32[4]{0:T(128)S(1)} %pad_add_fusion.at, bf16[128,4608]{1,0:T(8,128)(2,1)S(1)} %copy-done.1, bf16[128,4608]{1,0:T(8,128)(2,1)S(1)} %collective-permute-done.4.tie.near_s.own_s, ...), custom_call_target="tpu_custom_call" | custom-call | flops 1862270976 | bytes 10911744 | tf_op jit(solution)/shard_map/far_products/pallas_call | solution.py:368
  77.3 4.1 %collective-permute-start.27 = (bf16[128,4608]{1,0:T(8,128)(2,1)S(1)}, bf16[128,4608]{1,0:T(8,128)(2,1)S(1)}, u32[]{:S(2)}, u32[]{:S(2)}) collective-permute-start(bf16[128,4608]{1,0:T(8,128)(2,1)S(1)} %fence.7.three.more), channel_id=1, source_target_pairs={{0,1},{1,0},{2,3},{3,2},{4,5},{5,4},{6,7},{7,6},{8,9},{9,8},{10,11... | collective-permute-start | bytes 3538952 | tf_op jit(solution)/shard_map/tokens_core/ppermute | solution.py:60
  81.4 5.9 %collective-permute-start.28 = (bf16[3,256,256]{2,1,0:T(8,128)(2,1)S(1)}, bf16[3,256,256]{2,1,0:T(8,128)(2,1)S(1)}, u32[]{:S(2)}, u32[]{:S(2)}) collective-permute-start(bf16[3,256,256]{2,1,0:T(8,128)(2,1)S(1)} %get-tuple-element.42.refs_0_.tie), channel_id=1, source_target_pairs={{0,2},{2,0},{1,3},{3,1},{4,6},{6,4},{5,7},{7,5},{8,10},{10,8},{9,1... | collective-permute-start | bytes 1179656 | tf_op jit(solution)/shard_map/out_z/ppermute | solution.py:60
  87.3 4.6 %collective-permute-start.23 = (f32[8,2304]{1,0:T(8,128)S(1)}, f32[8,2304]{1,0:T(8,128)S(1)}, u32[]{:S(2)}, u32[]{:S(2)}) collective-permute-start(f32[8,2304]{1,0:T(8,128)S(1)} %gate_sum.7.first.refs_1_), channel_id=1, source_target_pairs={{0,8},{4,12},{8,0},{12,4},{1,9},{5,13},{9,1},{13,5},{2,10},{6,14},... | collective-permute-start | bytes 221192 | tf_op jit(solution)/shard_map/gate_y/ppermute | solution.py:60
  91.9 3.6 %collective-permute-done.23.third = f32[8,2304]{1,0:T(8,128)S(1)} collective-permute-done((f32[8,2304]{1,0:T(8,128)S(1)}, f32[8,2304]{1,0:T(8,128)S(1)}, u32[]{:S(2)}, u32[]{:S(2)}) %collective-permute-start.23) | collective-permute-done | bytes 73760 | tf_op jit(solution)/shard_map/gate_y/ppermute | solution.py:60
  95.5 1.6 %collective-permute-done.24.fourth = f32[8,2304]{1,0:T(8,128)S(1)} collective-permute-done((f32[8,2304]{1,0:T(8,128)S(1)}, f32[8,2304]{1,0:T(8,128)S(1)}, u32[]{:S(2)}, u32[]{:S(2)}) %collective-permute-start.24) | collective-permute-done | bytes 73760 | tf_op jit(solution)/shard_map/gate_y/ppermute | solution.py:60
  97.2 1.4 %far_products_last.1.refs_0_ = bf16[256,256]{1,0:T(8,128)(2,1)S(1)} custom-call(s32[4]{0:T(128)S(1)} %pad_add_fusion.at, bf16[128,4608]{1,0:T(8,128)(2,1)S(1)} %fence.7.three.more, bf16[128,4608]{1,0:T(8,128)(2,1)S(1)} %collective-permute-done.27.three_s.more_s, bf16[4,128,128]{2,1,0:T(8,128)(2,1)S(1)} %get-tuple-element.36.mixed, ...), custom_call_target="tpu_custom_call" | custom-call | flops 620756992 | bytes 3637248 | tf_op jit(solution)/shard_map/far_products_last/pallas_call | solution.py:392
  98.6 5.4 %collective-permute-start.30 = (bf16[256,256]{1,0:T(8,128)(2,1)S(1)}, bf16[256,256]{1,0:T(8,128)(2,1)S(1)}, u32[]{:S(2)}, u32[]{:S(2)}) collective-permute-start(bf16[256,256]{1,0:T(8,128)(2,1)S(1)} %far_products_last.1.refs_0_), channel_id=1, source_target_pairs={{0,2},{2,0},{1,3},{3,1},{4,6},{6,4},{5,7},{7,5},{8,10},{10,8},{9,1... | collective-permute-start | bytes 393224 | tf_op jit(solution)/shard_map/out_z_last/ppermute | solution.py:60
  104.0 11.1 %collective-permute-done.25.right = f32[8,2304]{1,0:T(8,128)S(1)} collective-permute-done((f32[8,2304]{1,0:T(8,128)S(1)}, f32[8,2304]{1,0:T(8,128)S(1)}, u32[]{:S(2)}, u32[]{:S(2)}) %collective-permute-start.25) | collective-permute-done | bytes 73760 | tf_op jit(solution)/shard_map/gate_zh/ppermute | solution.py:60
  116.4 2.0 %own_rest.1.rest = bf16[2,256,256]{2,1,0:T(8,128)(2,1)S(1)} custom-call(s32[4]{0:T(128)S(1)} %pad_add_fusion.at, bf16[128,4608]{1,0:T(8,128)(2,1)S(1)} %fence.6.refs_2_.two.near, bf16[128,4608]{1,0:T(8,128)(2,1)S(1)} %collective-permute-done.21.two_s.near_s, bf16[128,4608]{1,0:T(8,128)(2,1)S(1)} %fence.7.three.more, ...), custom_call_target="tpu_custom_call" | custom-call | flops 1241513984 | bytes 7274496 | tf_op jit(solution)/shard_map/own_rest/pallas_call | solution.py:308
  118.4 1.2 %gate_halves.1 = f32[8,4608]{1,0:T(8,128)} custom-call(s32[4]{0:T(128)S(1)} %pad_add_fusion.at, f32[8,2304]{1,0:T(8,128)S(1)} %get-tuple-element.45.mine, f32[8,2304]{1,0:T(8,128)S(1)} %collective-permute-done.29.other), custom_call_target="tpu_custom_call" | custom-call | tf_op jit(solution)/shard_map/gate_halves/pallas_call | solution.py:410
  119.6 1.6 %place.1 = bf16[4,2,2,128,256]{4,3,2,1,0:T(8,128)(2,1)} custom-call(s32[4]{0:T(128)S(1)} %pad_add_fusion.at, bf16[2,256,256]{2,1,0:T(8,128)(2,1)S(1)} %own_near.1.tie.near, bf16[2,256,256]{2,1,0:T(8,128)(2,1)S(1)} %own_rest.1.rest, bf16[3,256,256]{2,1,0:T(8,128)(2,1)S(1)} %collective-permute-done.28.refs_1_.got, ...), custom_call_target="tpu_custom_call" | custom-call | tf_op jit(solution)/shard_map/place/pallas_call | solution.py:419
  (56 shorter events, 5.4 us)
Async XLA Ops:
  0.6 32.0 %collective-permute-start.4 = (bf16[128,4608]{1,0:T(8,128)(2,1)}, bf16[128,4608]{1,0:T(8,128)(2,1)S(1)}, u32[]{:S(2)}, u32[]{:S(2)}) collective-permute-start(bf16[128,4608]{1,0:T(8,128)(2,1)} %own.1), channel_id=1, source_target_pairs={{0,1},{1,0},{2,3},{3,2},{4,5},{5,4},{6,7},{7,6},{8,9},{9,8},{10,11... | collective-permute-start | bytes 3538952 | tf_op jit(solution)/shard_map/tokens_core/ppermute | solution.py:60
  4.0 36.5 %collective-permute-start.6 = (bf16[128,4608]{1,0:T(8,128)(2,1)}, bf16[128,4608]{1,0:T(8,128)(2,1)S(1)}, u32[]{:S(2)}, u32[]{:S(2)}) collective-permute-start(bf16[128,4608]{1,0:T(8,128)(2,1)} %own.1), channel_id=1, source_target_pairs={{0,4},{1,13},{4,8},{5,1},{8,12},{9,5},{12,0},{13,9},{2,6},{3,15},{... | collective-permute-start | bytes 3538952 | tf_op jit(solution)/shard_map/tokens_y/ppermute | solution.py:27
  6.8 11.0 %copy-start.1 = (bf16[128,4608]{1,0:T(8,128)(2,1)S(1)}, bf16[128,4608]{1,0:T(8,128)(2,1)}, u32[]{:S(2)}) copy-start(bf16[128,4608]{1,0:T(8,128)(2,1)} %own.1) | copy-start | bytes 3538948
  7.7 32.8 %collective-permute-start.7 = (bf16[64,4736]{1,0:T(8,128)(2,1)}, bf16[64,4736]{1,0:T(8,128)(2,1)}, u32[]{:S(2)}, u32[]{:S(2)}) collective-permute-start(bf16[64,4736]{1,0:T(8,128)(2,1)} %pad_maximum_fusion), channel_id=1, source_target_pairs={{0,2},{2,0},{1,3},{3,1},{4,6},{6,4},{5,7},{7,5},{8,10},{10,8},{9,1... | collective-permute-start | bytes 1818632 | tf_op jit(solution)/shard_map/weight_z/ppermute | solution.py:60
  14.6 1.2 %copy-start.5 = (bf16[2048,256]{1,0:T(8,128)(2,1)S(1)}, bf16[2048,256]{1,0:T(8,128)(2,1)}, u32[]{:S(2)}) copy-start(bf16[2048,256]{1,0:T(8,128)(2,1)} %param.9) | copy-start | bytes 3145732
  15.9 0.8 copy-start.6
  17.7 5.5 %collective-permute-start = (bf16[4,2,128,128]{3,2,1,0:T(8,128)(2,1)S(1)}, bf16[4,2,128,128]{3,2,1,0:T(8,128)(2,1)S(1)}, u32[]{:S(2)}, u32[]{:S(2)}) collective-permute-start(bf16[4,2,128,128]{3,2,1,0:T(8,128)(2,1)S(1)} %get-tuple-element.25), channel_id=1, source_target_pairs={{0,1},{1,0},{2,3},{3,2},{4,5},{5,4},{6,7},{7,6},{8,9},{9,8},{10,11... | collective-permute-start | bytes 786440 | tf_op jit(solution)/shard_map/act_core/ppermute | solution.py:60
  17.8 1.3 %copy-start.2 = (bf16[128,4608]{1,0:T(8,128)(2,1)S(1)}, bf16[128,4608]{1,0:T(8,128)(2,1)}, u32[]{:S(2)}) copy-start(bf16[128,4608]{1,0:T(8,128)(2,1)} %hidden.3) | copy-start | bytes 3538948
  19.1 1.3 %copy-start.4 = (bf16[128,4608]{1,0:T(8,128)(2,1)S(1)}, bf16[128,4608]{1,0:T(8,128)(2,1)}, u32[]{:S(2)}) copy-start(bf16[128,4608]{1,0:T(8,128)(2,1)} %up.1) | copy-start | bytes 3538948
  20.3 0.9 copy-start.8
  23.8 4.1 %collective-permute-start.1 = (bf16[3,128,128]{2,1,0:T(8,128)(2,1)S(1)}, bf16[3,128,128]{2,1,0:T(8,128)(2,1)S(1)}, u32[]{:S(2)}, u32[]{:S(2)}) collective-permute-start(bf16[3,128,128]{2,1,0:T(8,128)(2,1)S(1)} %get-tuple-element.28), channel_id=1, source_target_pairs={{0,4},{4,0},{8,12},{12,8},{1,5},{5,1},{9,13},{13,9},{2,6},{6,2},{1... | collective-permute-start | bytes 294920 | tf_op jit(solution)/shard_map/act_y/ppermute | solution.py:60
  24.4 6.3 %collective-permute-start.2 = (bf16[3,128,128]{2,1,0:T(8,128)(2,1)S(1)}, bf16[3,128,128]{2,1,0:T(8,128)(2,1)S(1)}, u32[]{:S(2)}, u32[]{:S(2)}) collective-permute-start(bf16[3,128,128]{2,1,0:T(8,128)(2,1)S(1)} %get-tuple-element.29), channel_id=1, source_target_pairs={{0,8},{4,12},{8,0},{12,4},{1,9},{5,13},{9,1},{13,5},{2,10},{6,14},... | collective-permute-start | bytes 294920 | tf_op jit(solution)/shard_map/act_y/ppermute | solution.py:60
  27.9 4.7 %collective-permute-start.3 = (bf16[3,128,128]{2,1,0:T(8,128)(2,1)S(1)}, bf16[3,128,128]{2,1,0:T(8,128)(2,1)S(1)}, u32[]{:S(2)}, u32[]{:S(2)}) collective-permute-start(bf16[3,128,128]{2,1,0:T(8,128)(2,1)S(1)} %get-tuple-element.30), channel_id=1, source_target_pairs={{0,12},{4,8},{8,4},{12,0},{1,13},{5,9},{9,5},{13,1},{2,14},{6,10},... | collective-permute-start | bytes 294920 | tf_op jit(solution)/shard_map/act_y/ppermute | solution.py:60
  32.6 19.0 %copy-start = (bf16[256,4608]{1,0:T(8,128)(2,1)S(1)}, bf16[256,4608]{1,0:T(8,128)(2,1)}, u32[]{:S(2)}) copy-start(bf16[256,4608]{1,0:T(8,128)(2,1)} %weight.3) | copy-start | bytes 7077892
  33.2 18.4 %copy-start.7 = (bf16[256,128]{1,0:T(8,128)(2,1)S(1)}, bf16[256,128]{1,0:T(8,128)(2,1)}, u32[]{:S(2)}) copy-start(bf16[256,128]{1,0:T(8,128)(2,1)} %down.5) | copy-start | bytes 196612
  40.4 11.2 %collective-permute-start.8 = (bf16[128,4608]{1,0:T(8,128)(2,1)S(1)}, bf16[128,4608]{1,0:T(8,128)(2,1)S(1)}, u32[]{:S(2)}, u32[]{:S(2)}) collective-permute-start(bf16[128,4608]{1,0:T(8,128)(2,1)S(1)} %get-tuple-element.35.more.one), channel_id=1, source_target_pairs={{0,1},{1,0},{2,3},{3,2},{4,5},{5,4},{6,7},{7,6},{8,9},{9,8},{10,11... | collective-permute-start | bytes 3538952 | tf_op jit(solution)/shard_map/tokens_core/ppermute | solution.py:60
  40.4 17.0 %collective-permute-start.17 = (bf16[128,4608]{1,0:T(8,128)(2,1)S(1)}, bf16[128,4608]{1,0:T(8,128)(2,1)S(1)}, u32[]{:S(2)}, u32[]{:S(2)}) collective-permute-start(bf16[128,4608]{1,0:T(8,128)(2,1)S(1)} %get-tuple-element.35.more.one), channel_id=1, source_target_pairs={{0,4},{1,13},{4,8},{5,1},{8,12},{9,5},{12,0},{13,9},{2,6},{3,15},{... | collective-permute-start | bytes 3538952 | tf_op jit(solution)/shard_map/tokens_y/ppermute | solution.py:27
  41.6 15.8 %collective-permute-start.11 = (bf16[64,4736]{1,0:T(8,128)(2,1)}, bf16[64,4736]{1,0:T(8,128)(2,1)S(1)}, u32[]{:S(2)}, u32[]{:S(2)}) collective-permute-start(bf16[64,4736]{1,0:T(8,128)(2,1)} %get-tuple-element.39.refs_0_), channel_id=1, source_target_pairs={{0,64},{1,193},{64,0},{65,129},{128,192},{129,65},{192,128},{193,1... | collective-permute-start | bytes 1818632 | tf_op jit(solution)/shard_map/weight_x/ppermute | solution.py:33
  44.1 13.3 %collective-permute-start.12 = (bf16[64,4736]{1,0:T(8,128)(2,1)}, bf16[64,4736]{1,0:T(8,128)(2,1)S(1)}, u32[]{:S(2)}, u32[]{:S(2)}) collective-permute-start(bf16[64,4736]{1,0:T(8,128)(2,1)} %get-tuple-element.39.refs_0_), channel_id=1, source_target_pairs={{0,192},{1,65},{64,128},{65,1},{128,64},{129,193},{192,0},{193,129... | collective-permute-start | bytes 1818632 | tf_op jit(solution)/shard_map/weight_x/ppermute | solution.py:33
  44.1 9.5 %copy-start.3 = (bf16[128,4608]{1,0:T(8,128)(2,1)S(1)}, bf16[128,4608]{1,0:T(8,128)(2,1)}, u32[]{:S(2)}) copy-start(bf16[128,4608]{1,0:T(8,128)(2,1)} %hidden.3) | copy-start | bytes 3538948
  44.1 1.4 %collective-permute-start.9 = (bf16[4,128,128]{2,1,0:T(8,128)(2,1)S(1)}, bf16[4,128,128]{2,1,0:T(8,128)(2,1)S(1)}, u32[]{:S(2)}, u32[]{:S(2)}) collective-permute-start(bf16[4,128,128]{2,1,0:T(8,128)(2,1)S(1)} %get-tuple-element.36.mixed), channel_id=1, source_target_pairs={{0,1},{1,0},{2,3},{3,2},{4,5},{5,4},{6,7},{7,6},{8,9},{9,8},{10,11... | collective-permute-start | bytes 393224 | tf_op jit(solution)/shard_map/mixed_core/ppermute | solution.py:60
  45.5 8.1 %collective-permute-start.5 = (bf16[128,128]{1,0:T(8,128)(2,1)S(1)}, bf16[128,128]{1,0:T(8,128)(2,1)S(1)}, u32[]{:S(2)}, u32[]{:S(2)}) collective-permute-start(bf16[128,128]{1,0:T(8,128)(2,1)S(1)} %get-tuple-element.32.refs_2_.tie), channel_id=1, source_target_pairs={{0,2},{2,0},{1,3},{3,1},{4,6},{6,4},{5,7},{7,5},{8,10},{10,8},{9,1... | collective-permute-start | bytes 98312 | tf_op jit(solution)/shard_map/act_z/ppermute | solution.py:60
  54.8 2.6 %collective-permute-start.10 = (f32[8,2304]{1,0:T(8,128)S(1)}, f32[8,2304]{1,0:T(8,128)S(1)}, u32[]{:S(2)}, u32[]{:S(2)}) collective-permute-start(f32[8,2304]{1,0:T(8,128)S(1)} %get-tuple-element.38), channel_id=1, source_target_pairs={{0,1},{1,0},{2,3},{3,2},{4,5},{5,4},{6,7},{7,6},{8,9},{9,8},{10,11... | collective-permute-start | bytes 221192 | tf_op jit(solution)/shard_map/gate_core/ppermute | solution.py:60
  57.5 16.4 %collective-permute-start.21 = (bf16[128,4608]{1,0:T(8,128)(2,1)S(1)}, bf16[128,4608]{1,0:T(8,128)(2,1)S(1)}, u32[]{:S(2)}, u32[]{:S(2)}) collective-permute-start(bf16[128,4608]{1,0:T(8,128)(2,1)S(1)} %fence.6.refs_2_.two.near), channel_id=1, source_target_pairs={{0,1},{1,0},{2,3},{3,2},{4,5},{5,4},{6,7},{7,6},{8,9},{9,8},{10,11... | collective-permute-start | bytes 3538952 | tf_op jit(solution)/shard_map/tokens_core/ppermute | solution.py:60
  59.3 18.0 %collective-permute-start.26 = (bf16[128,4608]{1,0:T(8,128)(2,1)S(1)}, bf16[128,4608]{1,0:T(8,128)(2,1)S(1)}, u32[]{:S(2)}, u32[]{:S(2)}) collective-permute-start(bf16[128,4608]{1,0:T(8,128)(2,1)S(1)} %fence.6.refs_2_.two.near), channel_id=1, source_target_pairs={{0,4},{1,13},{4,8},{5,1},{8,12},{9,5},{12,0},{13,9},{2,6},{3,15},{... | collective-permute-start | bytes 3538952 | tf_op jit(solution)/shard_map/tokens_y/ppermute | solution.py:27
  60.7 9.2 %collective-permute-start.16 = (bf16[64,4736]{1,0:T(8,128)(2,1)S(1)}, bf16[64,4736]{1,0:T(8,128)(2,1)S(1)}, u32[]{:S(2)}, u32[]{:S(2)}) collective-permute-start(bf16[64,4736]{1,0:T(8,128)(2,1)S(1)} %fence.5.refs_1_), channel_id=1, source_target_pairs={{0,192},{1,65},{64,128},{65,1},{128,64},{129,193},{192,0},{193,129... | collective-permute-start | bytes 1818632 | tf_op jit(solution)/shard_map/weight_x_far/ppermute | solution.py:33
  60.7 3.9 %collective-permute-start.13 = (bf16[8,2304]{1,0:T(8,128)(2,1)S(1)}, bf16[8,2304]{1,0:T(8,128)(2,1)S(1)}, u32[]{:S(2)}, u32[]{:S(2)}) collective-permute-start(bf16[8,2304]{1,0:T(8,128)(2,1)S(1)} %get-tuple-element.41), channel_id=1, source_target_pairs={{0,16},{16,0},{32,48},{48,32},{1,17},{17,1},{33,49},{49,33},{2,18}... | collective-permute-start | bytes 110600 | tf_op jit(solution)/shard_map/gate_zl/ppermute | solution.py:60
  63.0 4.3 %collective-permute-start.14 = (bf16[8,2304]{1,0:T(8,128)(2,1)S(1)}, bf16[8,2304]{1,0:T(8,128)(2,1)S(1)}, u32[]{:S(2)}, u32[]{:S(2)}) collective-permute-start(bf16[8,2304]{1,0:T(8,128)(2,1)S(1)} %get-tuple-element.41), channel_id=1, source_target_pairs={{0,32},{16,48},{32,0},{48,16},{1,33},{17,49},{33,1},{49,17},{2,34}... | collective-permute-start | bytes 110600 | tf_op jit(solution)/shard_map/gate_zl/ppermute | solution.py:60
  64.6 4.7 %collective-permute-start.15 = (bf16[8,2304]{1,0:T(8,128)(2,1)S(1)}, bf16[8,2304]{1,0:T(8,128)(2,1)S(1)}, u32[]{:S(2)}, u32[]{:S(2)}) collective-permute-start(bf16[8,2304]{1,0:T(8,128)(2,1)S(1)} %get-tuple-element.41), channel_id=1, source_target_pairs={{0,48},{16,32},{32,16},{48,0},{1,49},{17,33},{33,17},{49,1},{2,50}... | collective-permute-start | bytes 110600 | tf_op jit(solution)/shard_map/gate_zl/ppermute | solution.py:60
  69.9 7.3 %collective-permute-start.18 = (f32[8,2304]{1,0:T(8,128)S(1)}, f32[8,2304]{1,0:T(8,128)S(1)}, u32[]{:S(2)}, u32[]{:S(2)}) collective-permute-start(f32[8,2304]{1,0:T(8,128)S(1)} %gate_sum.6.refs_4_.first), channel_id=1, source_target_pairs={{0,64},{64,0},{128,192},{192,128},{1,65},{65,1},{129,193},{193,129... | collective-permute-start | bytes 221192 | tf_op jit(solution)/shard_map/gate_x/ppermute | solution.py:60
  70.3 6.9 %collective-permute-start.19 = (f32[8,2304]{1,0:T(8,128)S(1)}, f32[8,2304]{1,0:T(8,128)S(1)}, u32[]{:S(2)}, u32[]{:S(2)}) collective-permute-start(f32[8,2304]{1,0:T(8,128)S(1)} %gate_sum.6.refs_4_.first), channel_id=1, source_target_pairs={{0,128},{64,192},{128,0},{192,64},{1,129},{65,193},{129,1},{193,65... | collective-permute-start | bytes 221192 | tf_op jit(solution)/shard_map/gate_x/ppermute | solution.py:60
  72.4 4.9 %collective-permute-start.20 = (f32[8,2304]{1,0:T(8,128)S(1)}, f32[8,2304]{1,0:T(8,128)S(1)}, u32[]{:S(2)}, u32[]{:S(2)}) collective-permute-start(f32[8,2304]{1,0:T(8,128)S(1)} %gate_sum.6.refs_4_.first), channel_id=1, source_target_pairs={{0,192},{64,128},{128,64},{192,0},{1,193},{65,129},{129,65},{193,1... | collective-permute-start | bytes 221192 | tf_op jit(solution)/shard_map/gate_x/ppermute | solution.py:60
  77.3 19.9 %collective-permute-start.27 = (bf16[128,4608]{1,0:T(8,128)(2,1)S(1)}, bf16[128,4608]{1,0:T(8,128)(2,1)S(1)}, u32[]{:S(2)}, u32[]{:S(2)}) collective-permute-start(bf16[128,4608]{1,0:T(8,128)(2,1)S(1)} %fence.7.three.more), channel_id=1, source_target_pairs={{0,1},{1,0},{2,3},{3,2},{4,5},{5,4},{6,7},{7,6},{8,9},{9,8},{10,11... | collective-permute-start | bytes 3538952 | tf_op jit(solution)/shard_map/tokens_core/ppermute | solution.py:60
  81.4 33.8 %collective-permute-start.28 = (bf16[3,256,256]{2,1,0:T(8,128)(2,1)S(1)}, bf16[3,256,256]{2,1,0:T(8,128)(2,1)S(1)}, u32[]{:S(2)}, u32[]{:S(2)}) collective-permute-start(bf16[3,256,256]{2,1,0:T(8,128)(2,1)S(1)} %get-tuple-element.42.refs_0_.tie), channel_id=1, source_target_pairs={{0,2},{2,0},{1,3},{3,1},{4,6},{6,4},{5,7},{7,5},{8,10},{10,8},{9,1... | collective-permute-start | bytes 1179656 | tf_op jit(solution)/shard_map/out_z/ppermute | solution.py:60
  87.3 4.6 %collective-permute-start.22 = (f32[8,2304]{1,0:T(8,128)S(1)}, f32[8,2304]{1,0:T(8,128)S(1)}, u32[]{:S(2)}, u32[]{:S(2)}) collective-permute-start(f32[8,2304]{1,0:T(8,128)S(1)} %gate_sum.7.first.refs_1_), channel_id=1, source_target_pairs={{0,4},{4,0},{8,12},{12,8},{1,5},{5,1},{9,13},{13,9},{2,6},{6,2},{1... | collective-permute-start | bytes 221192 | tf_op jit(solution)/shard_map/gate_y/ppermute | solution.py:60
  87.3 8.2 %collective-permute-start.23 = (f32[8,2304]{1,0:T(8,128)S(1)}, f32[8,2304]{1,0:T(8,128)S(1)}, u32[]{:S(2)}, u32[]{:S(2)}) collective-permute-start(f32[8,2304]{1,0:T(8,128)S(1)} %gate_sum.7.first.refs_1_), channel_id=1, source_target_pairs={{0,8},{4,12},{8,0},{12,4},{1,9},{5,13},{9,1},{13,5},{2,10},{6,14},... | collective-permute-start | bytes 221192 | tf_op jit(solution)/shard_map/gate_y/ppermute | solution.py:60
  91.9 5.2 %collective-permute-start.24 = (f32[8,2304]{1,0:T(8,128)S(1)}, f32[8,2304]{1,0:T(8,128)S(1)}, u32[]{:S(2)}, u32[]{:S(2)}) collective-permute-start(f32[8,2304]{1,0:T(8,128)S(1)} %gate_sum.7.first.refs_1_), channel_id=1, source_target_pairs={{0,12},{4,8},{8,4},{12,0},{1,13},{5,9},{9,5},{13,1},{2,14},{6,10},... | collective-permute-start | bytes 221192 | tf_op jit(solution)/shard_map/gate_y/ppermute | solution.py:60
  97.1 18.0 %collective-permute-start.25 = (f32[8,2304]{1,0:T(8,128)S(1)}, f32[8,2304]{1,0:T(8,128)S(1)}, u32[]{:S(2)}, u32[]{:S(2)}) collective-permute-start(f32[8,2304]{1,0:T(8,128)S(1)} %gate_sum.8.tie.left), channel_id=1, source_target_pairs={{0,2},{2,0},{1,3},{3,1},{4,6},{6,4},{5,7},{7,5},{8,10},{10,8},{9,1... | collective-permute-start | bytes 221192 | tf_op jit(solution)/shard_map/gate_zh/ppermute | solution.py:60
  98.6 21.0 %collective-permute-start.30 = (bf16[256,256]{1,0:T(8,128)(2,1)S(1)}, bf16[256,256]{1,0:T(8,128)(2,1)S(1)}, u32[]{:S(2)}, u32[]{:S(2)}) collective-permute-start(bf16[256,256]{1,0:T(8,128)(2,1)S(1)} %far_products_last.1.refs_0_), channel_id=1, source_target_pairs={{0,2},{2,0},{1,3},{3,1},{4,6},{6,4},{5,7},{7,5},{8,10},{10,8},{9,1... | collective-permute-start | bytes 393224 | tf_op jit(solution)/shard_map/out_z_last/ppermute | solution.py:60
  115.8 2.6 %collective-permute-start.29 = (f32[8,2304]{1,0:T(8,128)S(1)}, f32[8,2304]{1,0:T(8,128)S(1)}, u32[]{:S(2)}, u32[]{:S(2)}) collective-permute-start(f32[8,2304]{1,0:T(8,128)S(1)} %get-tuple-element.45.mine), channel_id=1, source_target_pairs={{0,1},{1,0},{2,3},{3,2},{4,5},{5,4},{6,7},{7,6},{8,9},{9,8},{10,11... | collective-permute-start | bytes 221192 | tf_op jit(solution)/shard_map/gate_core_back/ppermute | solution.py:60

commit v12 on v11

--- a/solution.py
+++ b/solution.py
@@ -79,6 +79,22 @@
     column = lax.broadcasted_iota(jnp.int32, (adapters, stacked), 1)
     low = row * (stacked // adapters)
     return jnp.where((column >= low) & (column < low + stacked // adapters), 1.0, 0.0)
+
+
+def piece_kernel(at, weight, down, piece, sems):
+    width = weight.shape[1]
+    quarter = piece.shape[0]
+    rows = pl.ds(pl.multiple_of(at[0] * quarter, quarter), quarter)
+    copies = [
+        pltpu.make_async_copy(weight.at[rows], piece.at[:, pl.ds(0, width)], sems.at[0]),
+        pltpu.make_async_copy(
+            down.at[rows], piece.at[:, pl.ds(width, down.shape[1])], sems.at[1]
+        ),
+    ]
+    for copy in copies:
+        copy.start()
+    for copy in copies:
+        copy.wait()
 
 
 def token_kernel(at, hidden, grad, up, gate, mixed, gates, back):
@@ -231,9 +247,15 @@
     at = jnp.stack([x, y, zh, c]).astype(jnp.int32)
 
     with jax.named_scope("weight_z"):
-        piece = jnp.concatenate(
-            [lax.dynamic_slice_in_dim(v, x * quarter, quarter, 0) for v in (weight, down)], axis=1
-        )
+        piece = pl.pallas_call(
+            piece_kernel,
+            in_specs=[SMEM, ANY, ANY],
+            out_specs=VMEM,
+            out_shape=shaped((quarter, depth), BF16),
+            scratch_shapes=[pltpu.SemaphoreType.DMA((2,))],
+            compiler_params=pltpu.CompilerParams(vmem_limit_bytes=56 * 1024 * 1024),
+            name="weight_piece",
+        )(at, weight, down)
         far_piece = swap(piece, "zh", 1)
     with jax.named_scope("tokens_y"):
         one = ring(grad, "y")
@@ -404,7 +426,7 @@
     own_rest = products("own_rest", 2, two, two_s, three, three_s, weight, down, far)
     with jax.named_scope("gate_zh"):
         got = swap(total, "zh", 1)
-    total, _ = add(total, got, last, far_got)
+    total, _ = add(total, got, last, far_got, own_rest)
     with jax.named_scope("gate_core_back"):
         other = swap(total, "c", 1)
     gate_grad = pl.pallas_call(

time: 122 us -> 121 us (level)
  local copies, waits for them, and re-layouts: 7.33 us -> 2.79 us
  Pallas kernels: 17.6 us -> 20 us
  waiting for transfers between devices: 37 us -> 38.9 us
    pallas_call x0 -> x1, Pallas kernels: none -> 2.96 us  [on_device(): pl.pallas_call(piece_kernel, in_specs=[SMEM, ANY, ANY], out_specs=VMEM, o...]
    unnamed x18, local copies, waits for them, and re-layouts: 5.5 us -> 2.79 us
    ppermute x25, waiting for transfers between devices: 34.4 us -> 36.2 us  [swap(): return lax.ppermute(value, axis, [(i, i ^ mask) for i in range(size)])]
    dynamic_slice x2 -> x0, local copies, waits for them, and re-layouts: 1.83 us -> none  [on_device(): lax.dynamic_slice_in_dim(v, x * quarter, quarter, 0)]
  transfers between devices with their start and end apart: 31 -> 31, of which waited for: 13 -> 15; matrix products, arithmetic and copies ran while one was open for 2% -> 1% of each run, Pallas kernels for 13% -> 15%
where the time goes in v12:
time: 121 us
  starting transfers between devices  57.7 us (48%)
  waiting for transfers between devices  38.9 us (32%)
  Pallas kernels  20 us (17%)
  local copies, waits for them, and re-layouts  2.79 us (2%)
    ppermute x25, starting transfers between devices, swap(): return lax.ppermute(value, axis, [(i, i ^ mask) for i in range(size)])  51.6 us
    ppermute x25, waiting for transfers between devices, swap(): return lax.ppermute(value, axis, [(i, i ^ mask) for i in range(size)])  36.2 us
    pallas_call x2, Pallas kernels, products(): pl.pallas_call(functools.partial(product_kernel, first), in_specs=[SMEM]...  3.96 us
    ppermute x3, starting transfers between devices, ring(): return lax.ppermute(value, (axis, 'c'), pairs)  3.62 us
    pallas_call x1, Pallas kernels, on_device(): pl.pallas_call(piece_kernel, in_specs=[SMEM, ANY, ANY], out_specs=VMEM, o...  2.96 us
    pallas_call x1, Pallas kernels, on_device(): pl.pallas_call(far_kernel, in_specs=[SMEM] + [VMEM] * 12 + [ANY], out_spe...  2.81 us
    unnamed x18, local copies, waits for them, and re-layouts  2.79 us
    ppermute x3, waiting for transfers between devices, pairs(): lax.ppermute(value, (axis, 'c'), [(2 * i + c, 2 * partner(i, c) + c) for...  2.66 us
  transfers between devices with their start and end apart: 31, of which 15 were waited for; matrix products, arithmetic and copies ran while one was open for 1% of the time, Pallas kernels for 15%

profile of v12, /device:TPU:1, one launch (start us, length us, event | category | flops | bytes accessed | tf_op | source)
XLA Modules:
  0.0 121.1 jit_solution(17459511456956239817)
XLA Ops:
  0.6 3.3 %collective-permute-start.4 = (bf16[128,4608]{1,0:T(8,128)(2,1)}, bf16[128,4608]{1,0:T(8,128)(2,1)S(1)}, u32[]{:S(2)}, u32[]{:S(2)}) collective-permute-start(bf16[128,4608]{1,0:T(8,128)(2,1)} %own.1), channel_id=1, source_target_pairs={{0,1},{1,0},{2,3},{3,2},{4,5},{5,4},{6,7},{7,6},{8,9},{9,8},{10,11... | collective-permute-start | bytes 3538952 | tf_op jit(solution)/shard_map/tokens_core/ppermute | solution.py:60
  4.0 1.0 collective-permute-start.6
  5.0 0.7 pad_add_fusion.at
  5.6 3.0 %weight_piece.1 = bf16[64,4736]{1,0:T(8,128)(2,1)} custom-call(s32[4]{0:T(128)} %pad_add_fusion.at, bf16[256,4608]{1,0:T(8,128)(2,1)} %weight.5, bf16[256,128]{1,0:T(8,128)(2,1)} %down.7), custom_call_target="tpu_custom_call" | custom-call | tf_op jit(solution)/shard_map/weight_z/weight_piece/pallas_call | solution.py:250
  8.6 7.0 %collective-permute-start.7 = (bf16[64,4736]{1,0:T(8,128)(2,1)}, bf16[64,4736]{1,0:T(8,128)(2,1)S(1)}, u32[]{:S(2)}, u32[]{:S(2)}) collective-permute-start(bf16[64,4736]{1,0:T(8,128)(2,1)} %weight_piece.1), channel_id=1, source_target_pairs={{0,2},{2,0},{1,3},{3,1},{4,6},{6,4},{5,7},{7,5},{8,10},{10,8},{9,1... | collective-permute-start | bytes 1818632 | tf_op jit(solution)/shard_map/weight_z/ppermute | solution.py:60
  15.6 1.2 %copy-done.5 = bf16[2048,256]{1,0:T(8,128)(2,1)S(1)} copy-done((bf16[2048,256]{1,0:T(8,128)(2,1)S(1)}, bf16[2048,256]{1,0:T(8,128)(2,1)}, u32[]{:S(2)}) %copy-start.5) | copy-done | bytes 1048600
  16.8 0.7 copy-done.6
  17.5 1.0 rank_products.1
  18.6 0.9 copy-done.8
  19.5 2.0 %token_values.1 = (bf16[128,128]{1,0:T(8,128)(2,1)S(1)}, f32[8,128]{1,0:T(8,128)S(1)}, f32[128,128]{1,0:T(8,128)S(1)}) custom-call(s32[4]{0:T(128)S(1)} %copy-done.6, bf16[128,4608]{1,0:T(8,128)(2,1)S(1)} %copy-done.2, bf16[128,4608]{1,0:T(8,128)(2,1)S(1)} %copy-done.1, bf16[128,4608]{1,0:T(8,128)(2,1)S(1)} %copy-done.3, bf16[8,4608]{1,0:T(8,128)(2,1)S(1)} %copy-done.8), custom_call_target="tpu_custom_call" | custom-call | flops 452984832 | bytes 7077888 | tf_op jit(solution)/shard_map/token_values/pallas_call | solution.py:279
  22.7 1.4 %collective-permute-start.2 = (bf16[3,128,128]{2,1,0:T(8,128)(2,1)S(1)}, bf16[3,128,128]{2,1,0:T(8,128)(2,1)S(1)}, u32[]{:S(2)}, u32[]{:S(2)}) collective-permute-start(bf16[3,128,128]{2,1,0:T(8,128)(2,1)S(1)} %get-tuple-element.29), channel_id=1, source_target_pairs={{0,8},{4,12},{8,0},{12,4},{1,9},{5,13},{9,1},{13,5},{2,10},{6,14},... | collective-permute-start | bytes 294920 | tf_op jit(solution)/shard_map/act_y/ppermute | solution.py:60
  24.1 2.0 %collective-permute-done.1.first = bf16[3,128,128]{2,1,0:T(8,128)(2,1)S(1)} collective-permute-done((bf16[3,128,128]{2,1,0:T(8,128)(2,1)S(1)}, bf16[3,128,128]{2,1,0:T(8,128)(2,1)S(1)}, u32[]{:S(2)}, u32[]{:S(2)}) %collective-permute-start.1) | collective-permute-done | bytes 98336 | tf_op jit(solution)/shard_map/act_y/ppermute | solution.py:60
  26.1 0.8 collective-permute-start.3
  26.9 2.1 %collective-permute-done.2.second = bf16[3,128,128]{2,1,0:T(8,128)(2,1)S(1)} collective-permute-done((bf16[3,128,128]{2,1,0:T(8,128)(2,1)S(1)}, bf16[3,128,128]{2,1,0:T(8,128)(2,1)S(1)}, u32[]{:S(2)}, u32[]{:S(2)}) %collective-permute-start.2) | collective-permute-done | bytes 98336 | tf_op jit(solution)/shard_map/act_y/ppermute | solution.py:60
  29.0 1.8 %collective-permute-done.3.third = bf16[3,128,128]{2,1,0:T(8,128)(2,1)S(1)} collective-permute-done((bf16[3,128,128]{2,1,0:T(8,128)(2,1)S(1)}, bf16[3,128,128]{2,1,0:T(8,128)(2,1)S(1)}, u32[]{:S(2)}, u32[]{:S(2)}) %collective-permute-start.3) | collective-permute-done | bytes 98336 | tf_op jit(solution)/shard_map/act_y/ppermute | solution.py:60
  31.3 10.1 %collective-permute-done.7.refs_1_ = bf16[64,4736]{1,0:T(8,128)(2,1)S(1)} collective-permute-done((bf16[64,4736]{1,0:T(8,128)(2,1)}, bf16[64,4736]{1,0:T(8,128)(2,1)S(1)}, u32[]{:S(2)}, u32[]{:S(2)}) %collective-permute-start.7) | collective-permute-done | bytes 606240 | tf_op jit(solution)/shard_map/weight_z/ppermute | solution.py:60
  41.4 1.2 collective-permute-start.17
  42.6 2.5 %collective-permute-start.11 = (bf16[64,4736]{1,0:T(8,128)(2,1)S(1)}, bf16[64,4736]{1,0:T(8,128)(2,1)S(1)}, u32[]{:S(2)}, u32[]{:S(2)}) collective-permute-start(bf16[64,4736]{1,0:T(8,128)(2,1)S(1)} %get-tuple-element.39.refs_0_), channel_id=1, source_target_pairs={{0,64},{1,193},{64,0},{65,129},{128,192},{129,65},{192,128},{193,1... | collective-permute-start | bytes 1818632 | tf_op jit(solution)/shard_map/weight_x/ppermute | solution.py:33
  45.5 1.0 collective-permute-done.9.mixed_s.refs_0_
  46.5 6.0 %collective-permute-start.5 = (bf16[128,128]{1,0:T(8,128)(2,1)S(1)}, bf16[128,128]{1,0:T(8,128)(2,1)S(1)}, u32[]{:S(2)}, u32[]{:S(2)}) collective-permute-start(bf16[128,128]{1,0:T(8,128)(2,1)S(1)} %get-tuple-element.32.refs_2_.tie), channel_id=1, source_target_pairs={{0,2},{2,0},{1,3},{3,1},{4,6},{6,4},{5,7},{7,5},{8,10},{10,8},{9,1... | collective-permute-start | bytes 98312 | tf_op jit(solution)/shard_map/act_z/ppermute | solution.py:60
  52.5 2.0 %own_near.1.tie.near = bf16[2,256,256]{2,1,0:T(8,128)(2,1)S(1)} custom-call(s32[4]{0:T(128)S(1)} %copy-done.7, bf16[128,4608]{1,0:T(8,128)(2,1)S(1)} %copy-done.1, bf16[128,4608]{1,0:T(8,128)(2,1)S(1)} %collective-permute-done.4.tie.near_s.own_s, bf16[128,4608]{1,0:T(8,128)(2,1)S(1)} %get-tuple-element.35.more.one, ...), custom_call_target="tpu_custom_call" | custom-call | flops 1241513984 | bytes 7274496 | tf_op jit(solution)/shard_map/own_near/pallas_call | solution.py:330
  54.5 1.2 %gate_products.1 = (f32[8,2304]{1,0:T(8,128)S(1)}, f32[8,2304]{1,0:T(8,128)S(1)}) custom-call(s32[4]{0:T(128)S(1)} %copy-done.7, f32[128,128]{1,0:T(8,128)S(1)} %get-tuple-element.31.keep, bf16[128,128]{1,0:T(8,128)(2,1)S(1)} %collective-permute-done.5.got, f32[128,128]{1,0:T(8,128)S(1)} %get-tuple-element.33.back, f32[8,128]{1,0:T(8,128)S(1)} %get-tuple-element.34.gates, ...), custom_call_target="tpu_custom_call" | custom-call | tf_op jit(solution)/shard_map/gate_products/pallas_call | solution.py:342
  56.3 1.9 %collective-permute-done.11.refs_0_ = bf16[64,4736]{1,0:T(8,128)(2,1)S(1)} collective-permute-done((bf16[64,4736]{1,0:T(8,128)(2,1)S(1)}, bf16[64,4736]{1,0:T(8,128)(2,1)S(1)}, u32[]{:S(2)}, u32[]{:S(2)}) %collective-permute-start.11) | collective-permute-done | bytes 606240 | tf_op jit(solution)/shard_map/weight_x/ppermute | solution.py:33
  58.3 1.8 %collective-permute-start.21 = (bf16[128,4608]{1,0:T(8,128)(2,1)S(1)}, bf16[128,4608]{1,0:T(8,128)(2,1)S(1)}, u32[]{:S(2)}, u32[]{:S(2)}) collective-permute-start(bf16[128,4608]{1,0:T(8,128)(2,1)S(1)} %fence.6.refs_2_.two.near), channel_id=1, source_target_pairs={{0,1},{1,0},{2,3},{3,2},{4,5},{5,4},{6,7},{7,6},{8,9},{9,8},{10,11... | collective-permute-start | bytes 3538952 | tf_op jit(solution)/shard_map/tokens_core/ppermute | solution.py:60
  60.1 1.4 %collective-permute-start.26 = (bf16[128,4608]{1,0:T(8,128)(2,1)S(1)}, bf16[128,4608]{1,0:T(8,128)(2,1)S(1)}, u32[]{:S(2)}, u32[]{:S(2)}) collective-permute-start(bf16[128,4608]{1,0:T(8,128)(2,1)S(1)} %fence.6.refs_2_.two.near), channel_id=1, source_target_pairs={{0,4},{1,13},{4,8},{5,1},{8,12},{9,5},{12,0},{13,9},{2,6},{3,15},{... | collective-permute-start | bytes 3538952 | tf_op jit(solution)/shard_map/tokens_y/ppermute | solution.py:27
  61.5 2.1 %collective-permute-start.13 = (bf16[8,2304]{1,0:T(8,128)(2,1)S(1)}, bf16[8,2304]{1,0:T(8,128)(2,1)S(1)}, u32[]{:S(2)}, u32[]{:S(2)}) collective-permute-start(bf16[8,2304]{1,0:T(8,128)(2,1)S(1)} %get-tuple-element.41), channel_id=1, source_target_pairs={{0,16},{16,0},{32,48},{48,32},{1,17},{17,1},{33,49},{49,33},{2,18}... | collective-permute-start | bytes 110600 | tf_op jit(solution)/shard_map/gate_zl/ppermute | solution.py:60
  63.6 0.6 collective-permute-start.14
  64.3 1.0 collective-permute-done.13.second
  65.3 1.8 %collective-permute-start.15 = (bf16[8,2304]{1,0:T(8,128)(2,1)S(1)}, bf16[8,2304]{1,0:T(8,128)(2,1)S(1)}, u32[]{:S(2)}, u32[]{:S(2)}) collective-permute-start(bf16[8,2304]{1,0:T(8,128)(2,1)S(1)} %get-tuple-element.41), channel_id=1, source_target_pairs={{0,48},{16,32},{32,16},{48,0},{1,49},{17,33},{33,17},{49,1},{2,50}... | collective-permute-start | bytes 110600 | tf_op jit(solution)/shard_map/gate_zl/ppermute | solution.py:60
  67.1 0.8 collective-permute-done.14.third
  67.9 2.1 %collective-permute-done.15.fourth = bf16[8,2304]{1,0:T(8,128)(2,1)S(1)} collective-permute-done((bf16[8,2304]{1,0:T(8,128)(2,1)S(1)}, bf16[8,2304]{1,0:T(8,128)(2,1)S(1)}, u32[]{:S(2)}, u32[]{:S(2)}) %collective-permute-start.15) | collective-permute-done | bytes 36896 | tf_op jit(solution)/shard_map/gate_zl/ppermute | solution.py:60
  70.0 0.7 collective-permute-done.16.refs_1_.refs_3_
  71.1 2.1 %collective-permute-start.19 = (f32[8,2304]{1,0:T(8,128)S(1)}, f32[8,2304]{1,0:T(8,128)S(1)}, u32[]{:S(2)}, u32[]{:S(2)}) collective-permute-start(f32[8,2304]{1,0:T(8,128)S(1)} %gate_sum.6.refs_4_.first), channel_id=1, source_target_pairs={{0,128},{64,192},{128,0},{192,64},{1,129},{65,193},{129,1},{193,65... | collective-permute-start | bytes 221192 | tf_op jit(solution)/shard_map/gate_x/ppermute | solution.py:60
  73.2 1.5 %collective-permute-start.20 = (f32[8,2304]{1,0:T(8,128)S(1)}, f32[8,2304]{1,0:T(8,128)S(1)}, u32[]{:S(2)}, u32[]{:S(2)}) collective-permute-start(f32[8,2304]{1,0:T(8,128)S(1)} %gate_sum.6.refs_4_.first), channel_id=1, source_target_pairs={{0,192},{64,128},{128,64},{192,0},{1,193},{65,129},{129,65},{193,1... | collective-permute-start | bytes 221192 | tf_op jit(solution)/shard_map/gate_x/ppermute | solution.py:60
  74.7 2.8 %far_products.1 = (bf16[3,256,256]{2,1,0:T(8,128)(2,1)S(1)}, bf16[256,4608]{1,0:T(8,128)(2,1)S(1)}, bf16[256,128]{1,0:T(8,128)(2,1)S(1)}) custom-call(s32[4]{0:T(128)S(1)} %copy-done.7, bf16[128,4608]{1,0:T(8,128)(2,1)S(1)} %copy-done.1, bf16[128,4608]{1,0:T(8,128)(2,1)S(1)} %collective-permute-done.4.tie.near_s.own_s, ...), custom_call_target="tpu_custom_call" | custom-call | flops 1862270976 | bytes 10911744 | tf_op jit(solution)/shard_map/far_products/pallas_call | solution.py:390
  77.7 4.5 %collective-permute-start.27 = (bf16[128,4608]{1,0:T(8,128)(2,1)S(1)}, bf16[128,4608]{1,0:T(8,128)(2,1)S(1)}, u32[]{:S(2)}, u32[]{:S(2)}) collective-permute-start(bf16[128,4608]{1,0:T(8,128)(2,1)S(1)} %fence.7.three.more), channel_id=1, source_target_pairs={{0,1},{1,0},{2,3},{3,2},{4,5},{5,4},{6,7},{7,6},{8,9},{9,8},{10,11... | collective-permute-start | bytes 3538952 | tf_op jit(solution)/shard_map/tokens_core/ppermute | solution.py:60
  82.2 5.8 %collective-permute-start.28 = (bf16[3,256,256]{2,1,0:T(8,128)(2,1)S(1)}, bf16[3,256,256]{2,1,0:T(8,128)(2,1)S(1)}, u32[]{:S(2)}, u32[]{:S(2)}) collective-permute-start(bf16[3,256,256]{2,1,0:T(8,128)(2,1)S(1)} %get-tuple-element.42.refs_0_.tie), channel_id=1, source_target_pairs={{0,2},{2,0},{1,3},{3,1},{4,6},{6,4},{5,7},{7,5},{8,10},{10,8},{9,1... | collective-permute-start | bytes 1179656 | tf_op jit(solution)/shard_map/out_z/ppermute | solution.py:60
  88.0 4.6 %collective-permute-start.23 = (f32[8,2304]{1,0:T(8,128)S(1)}, f32[8,2304]{1,0:T(8,128)S(1)}, u32[]{:S(2)}, u32[]{:S(2)}) collective-permute-start(f32[8,2304]{1,0:T(8,128)S(1)} %gate_sum.7.first.refs_1_), channel_id=1, source_target_pairs={{0,8},{4,12},{8,0},{12,4},{1,9},{5,13},{9,1},{13,5},{2,10},{6,14},... | collective-permute-start | bytes 221192 | tf_op jit(solution)/shard_map/gate_y/ppermute | solution.py:60
  92.6 3.6 %collective-permute-done.23.third = f32[8,2304]{1,0:T(8,128)S(1)} collective-permute-done((f32[8,2304]{1,0:T(8,128)S(1)}, f32[8,2304]{1,0:T(8,128)S(1)}, u32[]{:S(2)}, u32[]{:S(2)}) %collective-permute-start.23) | collective-permute-done | bytes 73760 | tf_op jit(solution)/shard_map/gate_y/ppermute | solution.py:60
  96.2 1.6 %collective-permute-done.24.fourth = f32[8,2304]{1,0:T(8,128)S(1)} collective-permute-done((f32[8,2304]{1,0:T(8,128)S(1)}, f32[8,2304]{1,0:T(8,128)S(1)}, u32[]{:S(2)}, u32[]{:S(2)}) %collective-permute-start.24) | collective-permute-done | bytes 73760 | tf_op jit(solution)/shard_map/gate_y/ppermute | solution.py:60
  97.9 1.4 %far_products_last.1.refs_0_ = bf16[256,256]{1,0:T(8,128)(2,1)S(1)} custom-call(s32[4]{0:T(128)S(1)} %copy-done.7, bf16[128,4608]{1,0:T(8,128)(2,1)S(1)} %fence.7.three.more, bf16[128,4608]{1,0:T(8,128)(2,1)S(1)} %collective-permute-done.27.three_s.more_s, bf16[4,128,128]{2,1,0:T(8,128)(2,1)S(1)} %get-tuple-element.36.mixed, ...), custom_call_target="tpu_custom_call" | custom-call | flops 620756992 | bytes 3637248 | tf_op jit(solution)/shard_map/far_products_last/pallas_call | solution.py:414
  99.3 5.4 %collective-permute-start.30 = (bf16[256,256]{1,0:T(8,128)(2,1)S(1)}, bf16[256,256]{1,0:T(8,128)(2,1)S(1)}, u32[]{:S(2)}, u32[]{:S(2)}) collective-permute-start(bf16[256,256]{1,0:T(8,128)(2,1)S(1)} %far_products_last.1.refs_0_), channel_id=1, source_target_pairs={{0,2},{2,0},{1,3},{3,1},{4,6},{6,4},{5,7},{7,5},{8,10},{10,8},{9,1... | collective-permute-start | bytes 393224 | tf_op jit(solution)/shard_map/out_z_last/ppermute | solution.py:60
  104.7 2.0 %own_rest.1.refs_2_.rest = bf16[2,256,256]{2,1,0:T(8,128)(2,1)S(1)} custom-call(s32[4]{0:T(128)S(1)} %copy-done.7, bf16[128,4608]{1,0:T(8,128)(2,1)S(1)} %fence.6.refs_2_.two.near, bf16[128,4608]{1,0:T(8,128)(2,1)S(1)} %collective-permute-done.21.two_s.near_s, bf16[128,4608]{1,0:T(8,128)(2,1)S(1)} %fence.7.three.more, ...), custom_call_target="tpu_custom_call" | custom-call | flops 1241513984 | bytes 7274496 | tf_op jit(solution)/shard_map/own_rest/pallas_call | solution.py:330
  106.7 9.2 %collective-permute-done.25.right = f32[8,2304]{1,0:T(8,128)S(1)} collective-permute-done((f32[8,2304]{1,0:T(8,128)S(1)}, f32[8,2304]{1,0:T(8,128)S(1)}, u32[]{:S(2)}, u32[]{:S(2)}) %collective-permute-start.25) | collective-permute-done | bytes 73760 | tf_op jit(solution)/shard_map/gate_zh/ppermute | solution.py:60
  115.9 0.6 gate_sum.9
  117.1 0.9 collective-permute-done.29.other
  118.0 1.2 %gate_halves.1 = f32[8,4608]{1,0:T(8,128)} custom-call(s32[4]{0:T(128)S(1)} %copy-done.7, f32[8,2304]{1,0:T(8,128)S(1)} %get-tuple-element.45.mine, f32[8,2304]{1,0:T(8,128)S(1)} %collective-permute-done.29.other), custom_call_target="tpu_custom_call" | custom-call | tf_op jit(solution)/shard_map/gate_halves/pallas_call | solution.py:432
  119.3 1.6 %place.1 = bf16[4,2,2,128,256]{4,3,2,1,0:T(8,128)(2,1)} custom-call(s32[4]{0:T(128)S(1)} %copy-done.7, bf16[2,256,256]{2,1,0:T(8,128)(2,1)S(1)} %own_near.1.tie.near, bf16[2,256,256]{2,1,0:T(8,128)(2,1)S(1)} %own_rest.1.refs_2_.rest, bf16[3,256,256]{2,1,0:T(8,128)(2,1)S(1)} %collective-permute-done.28.refs_1_.got, ...), custom_call_target="tpu_custom_call" | custom-call | tf_op jit(solution)/shard_map/place/pallas_call | solution.py:441
  (54 shorter events, 4.2 us)
Async XLA Ops:
  0.6 30.1 %collective-permute-start.4 = (bf16[128,4608]{1,0:T(8,128)(2,1)}, bf16[128,4608]{1,0:T(8,128)(2,1)S(1)}, u32[]{:S(2)}, u32[]{:S(2)}) collective-permute-start(bf16[128,4608]{1,0:T(8,128)(2,1)} %own.1), channel_id=1, source_target_pairs={{0,1},{1,0},{2,3},{3,2},{4,5},{5,4},{6,7},{7,6},{8,9},{9,8},{10,11... | collective-permute-start | bytes 3538952 | tf_op jit(solution)/shard_map/tokens_core/ppermute | solution.py:60
  4.0 37.5 %collective-permute-start.6 = (bf16[128,4608]{1,0:T(8,128)(2,1)}, bf16[128,4608]{1,0:T(8,128)(2,1)S(1)}, u32[]{:S(2)}, u32[]{:S(2)}) collective-permute-start(bf16[128,4608]{1,0:T(8,128)(2,1)} %own.1), channel_id=1, source_target_pairs={{0,4},{1,13},{4,8},{5,1},{8,12},{9,5},{12,0},{13,9},{2,6},{3,15},{... | collective-permute-start | bytes 3538952 | tf_op jit(solution)/shard_map/tokens_y/ppermute | solution.py:27
  5.0 10.6 %copy-start.4 = (bf16[256,128]{1,0:T(8,128)(2,1)S(1)}, bf16[256,128]{1,0:T(8,128)(2,1)}, u32[]{:S(2)}) copy-start(bf16[256,128]{1,0:T(8,128)(2,1)} %down.7) | copy-start | bytes 196612
  5.6 12.9 %copy-start.1 = (bf16[128,4608]{1,0:T(8,128)(2,1)S(1)}, bf16[128,4608]{1,0:T(8,128)(2,1)}, u32[]{:S(2)}) copy-start(bf16[128,4608]{1,0:T(8,128)(2,1)} %own.1) | copy-start | bytes 3538948
  5.6 12.9 %copy-start.2 = (bf16[128,4608]{1,0:T(8,128)(2,1)S(1)}, bf16[128,4608]{1,0:T(8,128)(2,1)}, u32[]{:S(2)}) copy-start(bf16[128,4608]{1,0:T(8,128)(2,1)} %hidden.3) | copy-start | bytes 3538948
  5.6 12.9 %copy-start.3 = (bf16[128,4608]{1,0:T(8,128)(2,1)S(1)}, bf16[128,4608]{1,0:T(8,128)(2,1)}, u32[]{:S(2)}) copy-start(bf16[128,4608]{1,0:T(8,128)(2,1)} %up.1) | copy-start | bytes 3538948
  8.6 32.9 %collective-permute-start.7 = (bf16[64,4736]{1,0:T(8,128)(2,1)}, bf16[64,4736]{1,0:T(8,128)(2,1)S(1)}, u32[]{:S(2)}, u32[]{:S(2)}) collective-permute-start(bf16[64,4736]{1,0:T(8,128)(2,1)} %weight_piece.1), channel_id=1, source_target_pairs={{0,2},{2,0},{1,3},{3,1},{4,6},{6,4},{5,7},{7,5},{8,10},{10,8},{9,1... | collective-permute-start | bytes 1818632 | tf_op jit(solution)/shard_map/weight_z/ppermute | solution.py:60
  15.6 1.2 %copy-start.5 = (bf16[2048,256]{1,0:T(8,128)(2,1)S(1)}, bf16[2048,256]{1,0:T(8,128)(2,1)}, u32[]{:S(2)}) copy-start(bf16[2048,256]{1,0:T(8,128)(2,1)} %param.9) | copy-start | bytes 3145732
  16.8 0.7 copy-start.6
  18.4 3.0 %collective-permute-start = (bf16[4,2,128,128]{3,2,1,0:T(8,128)(2,1)S(1)}, bf16[4,2,128,128]{3,2,1,0:T(8,128)(2,1)S(1)}, u32[]{:S(2)}, u32[]{:S(2)}) collective-permute-start(bf16[4,2,128,128]{3,2,1,0:T(8,128)(2,1)S(1)} %get-tuple-element.25), channel_id=1, source_target_pairs={{0,1},{1,0},{2,3},{3,2},{4,5},{5,4},{6,7},{7,6},{8,9},{9,8},{10,11... | collective-permute-start | bytes 786440 | tf_op jit(solution)/shard_map/act_core/ppermute | solution.py:60
  18.6 0.9 copy-start.8
  22.1 4.0 %collective-permute-start.1 = (bf16[3,128,128]{2,1,0:T(8,128)(2,1)S(1)}, bf16[3,128,128]{2,1,0:T(8,128)(2,1)S(1)}, u32[]{:S(2)}, u32[]{:S(2)}) collective-permute-start(bf16[3,128,128]{2,1,0:T(8,128)(2,1)S(1)} %get-tuple-element.28), channel_id=1, source_target_pairs={{0,4},{4,0},{8,12},{12,8},{1,5},{5,1},{9,13},{13,9},{2,6},{6,2},{1... | collective-permute-start | bytes 294920 | tf_op jit(solution)/shard_map/act_y/ppermute | solution.py:60
  22.7 6.3 %collective-permute-start.2 = (bf16[3,128,128]{2,1,0:T(8,128)(2,1)S(1)}, bf16[3,128,128]{2,1,0:T(8,128)(2,1)S(1)}, u32[]{:S(2)}, u32[]{:S(2)}) collective-permute-start(bf16[3,128,128]{2,1,0:T(8,128)(2,1)S(1)} %get-tuple-element.29), channel_id=1, source_target_pairs={{0,8},{4,12},{8,0},{12,4},{1,9},{5,13},{9,1},{13,5},{2,10},{6,14},... | collective-permute-start | bytes 294920 | tf_op jit(solution)/shard_map/act_y/ppermute | solution.py:60
  26.1 4.7 %collective-permute-start.3 = (bf16[3,128,128]{2,1,0:T(8,128)(2,1)S(1)}, bf16[3,128,128]{2,1,0:T(8,128)(2,1)S(1)}, u32[]{:S(2)}, u32[]{:S(2)}) collective-permute-start(bf16[3,128,128]{2,1,0:T(8,128)(2,1)S(1)} %get-tuple-element.30), channel_id=1, source_target_pairs={{0,12},{4,8},{8,4},{12,0},{1,13},{5,9},{9,5},{13,1},{2,14},{6,10},... | collective-permute-start | bytes 294920 | tf_op jit(solution)/shard_map/act_y/ppermute | solution.py:60
  30.7 21.7 %copy-start = (bf16[256,4608]{1,0:T(8,128)(2,1)S(1)}, bf16[256,4608]{1,0:T(8,128)(2,1)}, u32[]{:S(2)}) copy-start(bf16[256,4608]{1,0:T(8,128)(2,1)} %weight.5) | copy-start | bytes 7077892
  31.3 21.2 %copy-start.7 = (s32[4]{0:T(128)S(1)}, s32[4]{0:T(128)}, u32[]{:S(2)}) copy-start(s32[4]{0:T(128)} %pad_add_fusion.at) | copy-start | bytes 52
  41.4 11.0 %collective-permute-start.8 = (bf16[128,4608]{1,0:T(8,128)(2,1)S(1)}, bf16[128,4608]{1,0:T(8,128)(2,1)S(1)}, u32[]{:S(2)}, u32[]{:S(2)}) collective-permute-start(bf16[128,4608]{1,0:T(8,128)(2,1)S(1)} %get-tuple-element.35.more.one), channel_id=1, source_target_pairs={{0,1},{1,0},{2,3},{3,2},{4,5},{5,4},{6,7},{7,6},{8,9},{9,8},{10,11... | collective-permute-start | bytes 3538952 | tf_op jit(solution)/shard_map/tokens_core/ppermute | solution.py:60
  41.4 16.8 %collective-permute-start.17 = (bf16[128,4608]{1,0:T(8,128)(2,1)S(1)}, bf16[128,4608]{1,0:T(8,128)(2,1)S(1)}, u32[]{:S(2)}, u32[]{:S(2)}) collective-permute-start(bf16[128,4608]{1,0:T(8,128)(2,1)S(1)} %get-tuple-element.35.more.one), channel_id=1, source_target_pairs={{0,4},{1,13},{4,8},{5,1},{8,12},{9,5},{12,0},{13,9},{2,6},{3,15},{... | collective-permute-start | bytes 3538952 | tf_op jit(solution)/shard_map/tokens_y/ppermute | solution.py:27
  42.6 15.6 %collective-permute-start.11 = (bf16[64,4736]{1,0:T(8,128)(2,1)S(1)}, bf16[64,4736]{1,0:T(8,128)(2,1)S(1)}, u32[]{:S(2)}, u32[]{:S(2)}) collective-permute-start(bf16[64,4736]{1,0:T(8,128)(2,1)S(1)} %get-tuple-element.39.refs_0_), channel_id=1, source_target_pairs={{0,64},{1,193},{64,0},{65,129},{128,192},{129,65},{192,128},{193,1... | collective-permute-start | bytes 1818632 | tf_op jit(solution)/shard_map/weight_x/ppermute | solution.py:33
  45.1 13.1 %collective-permute-start.12 = (bf16[64,4736]{1,0:T(8,128)(2,1)S(1)}, bf16[64,4736]{1,0:T(8,128)(2,1)S(1)}, u32[]{:S(2)}, u32[]{:S(2)}) collective-permute-start(bf16[64,4736]{1,0:T(8,128)(2,1)S(1)} %get-tuple-element.39.refs_0_), channel_id=1, source_target_pairs={{0,192},{1,65},{64,128},{65,1},{128,64},{129,193},{192,0},{193,129... | collective-permute-start | bytes 1818632 | tf_op jit(solution)/shard_map/weight_x/ppermute | solution.py:33
  45.1 1.4 %collective-permute-start.9 = (bf16[4,128,128]{2,1,0:T(8,128)(2,1)S(1)}, bf16[4,128,128]{2,1,0:T(8,128)(2,1)S(1)}, u32[]{:S(2)}, u32[]{:S(2)}) collective-permute-start(bf16[4,128,128]{2,1,0:T(8,128)(2,1)S(1)} %get-tuple-element.36.mixed), channel_id=1, source_target_pairs={{0,1},{1,0},{2,3},{3,2},{4,5},{5,4},{6,7},{7,6},{8,9},{9,8},{10,11... | collective-permute-start | bytes 393224 | tf_op jit(solution)/shard_map/mixed_core/ppermute | solution.py:60
  46.5 8.0 %collective-permute-start.5 = (bf16[128,128]{1,0:T(8,128)(2,1)S(1)}, bf16[128,128]{1,0:T(8,128)(2,1)S(1)}, u32[]{:S(2)}, u32[]{:S(2)}) collective-permute-start(bf16[128,128]{1,0:T(8,128)(2,1)S(1)} %get-tuple-element.32.refs_2_.tie), channel_id=1, source_target_pairs={{0,2},{2,0},{1,3},{3,1},{4,6},{6,4},{5,7},{7,5},{8,10},{10,8},{9,1... | collective-permute-start | bytes 98312 | tf_op jit(solution)/shard_map/act_z/ppermute | solution.py:60
  55.7 2.5 %collective-permute-start.10 = (f32[8,2304]{1,0:T(8,128)S(1)}, f32[8,2304]{1,0:T(8,128)S(1)}, u32[]{:S(2)}, u32[]{:S(2)}) collective-permute-start(f32[8,2304]{1,0:T(8,128)S(1)} %get-tuple-element.38), channel_id=1, source_target_pairs={{0,1},{1,0},{2,3},{3,2},{4,5},{5,4},{6,7},{7,6},{8,9},{9,8},{10,11... | collective-permute-start | bytes 221192 | tf_op jit(solution)/shard_map/gate_core/ppermute | solution.py:60
  58.3 16.4 %collective-permute-start.21 = (bf16[128,4608]{1,0:T(8,128)(2,1)S(1)}, bf16[128,4608]{1,0:T(8,128)(2,1)S(1)}, u32[]{:S(2)}, u32[]{:S(2)}) collective-permute-start(bf16[128,4608]{1,0:T(8,128)(2,1)S(1)} %fence.6.refs_2_.two.near), channel_id=1, source_target_pairs={{0,1},{1,0},{2,3},{3,2},{4,5},{5,4},{6,7},{7,6},{8,9},{9,8},{10,11... | collective-permute-start | bytes 3538952 | tf_op jit(solution)/shard_map/tokens_core/ppermute | solution.py:60
  60.1 17.6 %collective-permute-start.26 = (bf16[128,4608]{1,0:T(8,128)(2,1)S(1)}, bf16[128,4608]{1,0:T(8,128)(2,1)S(1)}, u32[]{:S(2)}, u32[]{:S(2)}) collective-permute-start(bf16[128,4608]{1,0:T(8,128)(2,1)S(1)} %fence.6.refs_2_.two.near), channel_id=1, source_target_pairs={{0,4},{1,13},{4,8},{5,1},{8,12},{9,5},{12,0},{13,9},{2,6},{3,15},{... | collective-permute-start | bytes 3538952 | tf_op jit(solution)/shard_map/tokens_y/ppermute | solution.py:27
  61.5 9.2 %collective-permute-start.16 = (bf16[64,4736]{1,0:T(8,128)(2,1)S(1)}, bf16[64,4736]{1,0:T(8,128)(2,1)S(1)}, u32[]{:S(2)}, u32[]{:S(2)}) collective-permute-start(bf16[64,4736]{1,0:T(8,128)(2,1)S(1)} %fence.5.refs_1_), channel_id=1, source_target_pairs={{0,192},{1,65},{64,128},{65,1},{128,64},{129,193},{192,0},{193,129... | collective-permute-start | bytes 1818632 | tf_op jit(solution)/shard_map/weight_x_far/ppermute | solution.py:33
  61.5 3.8 %collective-permute-start.13 = (bf16[8,2304]{1,0:T(8,128)(2,1)S(1)}, bf16[8,2304]{1,0:T(8,128)(2,1)S(1)}, u32[]{:S(2)}, u32[]{:S(2)}) collective-permute-start(bf16[8,2304]{1,0:T(8,128)(2,1)S(1)} %get-tuple-element.41), channel_id=1, source_target_pairs={{0,16},{16,0},{32,48},{48,32},{1,17},{17,1},{33,49},{49,33},{2,18}... | collective-permute-start | bytes 110600 | tf_op jit(solution)/shard_map/gate_zl/ppermute | solution.py:60
  63.6 4.2 %collective-permute-start.14 = (bf16[8,2304]{1,0:T(8,128)(2,1)S(1)}, bf16[8,2304]{1,0:T(8,128)(2,1)S(1)}, u32[]{:S(2)}, u32[]{:S(2)}) collective-permute-start(bf16[8,2304]{1,0:T(8,128)(2,1)S(1)} %get-tuple-element.41), channel_id=1, source_target_pairs={{0,32},{16,48},{32,0},{48,16},{1,33},{17,49},{33,1},{49,17},{2,34}... | collective-permute-start | bytes 110600 | tf_op jit(solution)/shard_map/gate_zl/ppermute | solution.py:60
  65.3 4.7 %collective-permute-start.15 = (bf16[8,2304]{1,0:T(8,128)(2,1)S(1)}, bf16[8,2304]{1,0:T(8,128)(2,1)S(1)}, u32[]{:S(2)}, u32[]{:S(2)}) collective-permute-start(bf16[8,2304]{1,0:T(8,128)(2,1)S(1)} %get-tuple-element.41), channel_id=1, source_target_pairs={{0,48},{16,32},{32,16},{48,0},{1,49},{17,33},{33,17},{49,1},{2,50}... | collective-permute-start | bytes 110600 | tf_op jit(solution)/shard_map/gate_zl/ppermute | solution.py:60
  70.7 6.8 %collective-permute-start.18 = (f32[8,2304]{1,0:T(8,128)S(1)}, f32[8,2304]{1,0:T(8,128)S(1)}, u32[]{:S(2)}, u32[]{:S(2)}) collective-permute-start(f32[8,2304]{1,0:T(8,128)S(1)} %gate_sum.6.refs_4_.first), channel_id=1, source_target_pairs={{0,64},{64,0},{128,192},{192,128},{1,65},{65,1},{129,193},{193,129... | collective-permute-start | bytes 221192 | tf_op jit(solution)/shard_map/gate_x/ppermute | solution.py:60
  71.1 6.4 %collective-permute-start.19 = (f32[8,2304]{1,0:T(8,128)S(1)}, f32[8,2304]{1,0:T(8,128)S(1)}, u32[]{:S(2)}, u32[]{:S(2)}) collective-permute-start(f32[8,2304]{1,0:T(8,128)S(1)} %gate_sum.6.refs_4_.first), channel_id=1, source_target_pairs={{0,128},{64,192},{128,0},{192,64},{1,129},{65,193},{129,1},{193,65... | collective-permute-start | bytes 221192 | tf_op jit(solution)/shard_map/gate_x/ppermute | solution.py:60
  73.2 4.4 %collective-permute-start.20 = (f32[8,2304]{1,0:T(8,128)S(1)}, f32[8,2304]{1,0:T(8,128)S(1)}, u32[]{:S(2)}, u32[]{:S(2)}) collective-permute-start(f32[8,2304]{1,0:T(8,128)S(1)} %gate_sum.6.refs_4_.first), channel_id=1, source_target_pairs={{0,192},{64,128},{128,64},{192,0},{1,193},{65,129},{129,65},{193,1... | collective-permute-start | bytes 221192 | tf_op jit(solution)/shard_map/gate_x/ppermute | solution.py:60
  77.7 20.3 %collective-permute-start.27 = (bf16[128,4608]{1,0:T(8,128)(2,1)S(1)}, bf16[128,4608]{1,0:T(8,128)(2,1)S(1)}, u32[]{:S(2)}, u32[]{:S(2)}) collective-permute-start(bf16[128,4608]{1,0:T(8,128)(2,1)S(1)} %fence.7.three.more), channel_id=1, source_target_pairs={{0,1},{1,0},{2,3},{3,2},{4,5},{5,4},{6,7},{7,6},{8,9},{9,8},{10,11... | collective-permute-start | bytes 3538952 | tf_op jit(solution)/shard_map/tokens_core/ppermute | solution.py:60
  82.2 33.7 %collective-permute-start.28 = (bf16[3,256,256]{2,1,0:T(8,128)(2,1)S(1)}, bf16[3,256,256]{2,1,0:T(8,128)(2,1)S(1)}, u32[]{:S(2)}, u32[]{:S(2)}) collective-permute-start(bf16[3,256,256]{2,1,0:T(8,128)(2,1)S(1)} %get-tuple-element.42.refs_0_.tie), channel_id=1, source_target_pairs={{0,2},{2,0},{1,3},{3,1},{4,6},{6,4},{5,7},{7,5},{8,10},{10,8},{9,1... | collective-permute-start | bytes 1179656 | tf_op jit(solution)/shard_map/out_z/ppermute | solution.py:60
  88.0 4.6 %collective-permute-start.22 = (f32[8,2304]{1,0:T(8,128)S(1)}, f32[8,2304]{1,0:T(8,128)S(1)}, u32[]{:S(2)}, u32[]{:S(2)}) collective-permute-start(f32[8,2304]{1,0:T(8,128)S(1)} %gate_sum.7.first.refs_1_), channel_id=1, source_target_pairs={{0,4},{4,0},{8,12},{12,8},{1,5},{5,1},{9,13},{13,9},{2,6},{6,2},{1... | collective-permute-start | bytes 221192 | tf_op jit(solution)/shard_map/gate_y/ppermute | solution.py:60
  88.0 8.2 %collective-permute-start.23 = (f32[8,2304]{1,0:T(8,128)S(1)}, f32[8,2304]{1,0:T(8,128)S(1)}, u32[]{:S(2)}, u32[]{:S(2)}) collective-permute-start(f32[8,2304]{1,0:T(8,128)S(1)} %gate_sum.7.first.refs_1_), channel_id=1, source_target_pairs={{0,8},{4,12},{8,0},{12,4},{1,9},{5,13},{9,1},{13,5},{2,10},{6,14},... | collective-permute-start | bytes 221192 | tf_op jit(solution)/shard_map/gate_y/ppermute | solution.py:60
  92.6 5.2 %collective-permute-start.24 = (f32[8,2304]{1,0:T(8,128)S(1)}, f32[8,2304]{1,0:T(8,128)S(1)}, u32[]{:S(2)}, u32[]{:S(2)}) collective-permute-start(f32[8,2304]{1,0:T(8,128)S(1)} %gate_sum.7.first.refs_1_), channel_id=1, source_target_pairs={{0,12},{4,8},{8,4},{12,0},{1,13},{5,9},{9,5},{13,1},{2,14},{6,10},... | collective-permute-start | bytes 221192 | tf_op jit(solution)/shard_map/gate_y/ppermute | solution.py:60
  97.8 18.1 %collective-permute-start.25 = (f32[8,2304]{1,0:T(8,128)S(1)}, f32[8,2304]{1,0:T(8,128)S(1)}, u32[]{:S(2)}, u32[]{:S(2)}) collective-permute-start(f32[8,2304]{1,0:T(8,128)S(1)} %gate_sum.8.tie.left), channel_id=1, source_target_pairs={{0,2},{2,0},{1,3},{3,1},{4,6},{6,4},{5,7},{7,5},{8,10},{10,8},{9,1... | collective-permute-start | bytes 221192 | tf_op jit(solution)/shard_map/gate_zh/ppermute | solution.py:60
  99.3 20.0 %collective-permute-start.30 = (bf16[256,256]{1,0:T(8,128)(2,1)S(1)}, bf16[256,256]{1,0:T(8,128)(2,1)S(1)}, u32[]{:S(2)}, u32[]{:S(2)}) collective-permute-start(bf16[256,256]{1,0:T(8,128)(2,1)S(1)} %far_products_last.1.refs_0_), channel_id=1, source_target_pairs={{0,2},{2,0},{1,3},{3,1},{4,6},{6,4},{5,7},{7,5},{8,10},{10,8},{9,1... | collective-permute-start | bytes 393224 | tf_op jit(solution)/shard_map/out_z_last/ppermute | solution.py:60
  116.5 1.5 %collective-permute-start.29 = (f32[8,2304]{1,0:T(8,128)S(1)}, f32[8,2304]{1,0:T(8,128)S(1)}, u32[]{:S(2)}, u32[]{:S(2)}) collective-permute-start(f32[8,2304]{1,0:T(8,128)S(1)} %get-tuple-element.45.mine), channel_id=1, source_target_pairs={{0,1},{1,0},{2,3},{3,2},{4,5},{5,4},{6,7},{7,6},{8,9},{9,8},{10,11... | collective-permute-start | bytes 221192 | tf_op jit(solution)/shard_map/gate_core_back/ppermute | solution.py:60

commit v13 on v11

--- a/solution.py
+++ b/solution.py
@@ -383,10 +383,10 @@
     )
     with jax.named_scope("out_z"):
         far_got = swap(far, "zh", 1)
-    total = step(total, "x", far)
-    (three,) = fence((three,), total)
+    (three,) = fence((three,), far)
     with jax.named_scope("tokens_core"):
         three_s = swap(three, "c", 1)
+    total = step(total, "x", far)
 
     total = step(total, "y")
     last = pl.pallas_call(
@@ -404,7 +404,7 @@
     own_rest = products("own_rest", 2, two, two_s, three, three_s, weight, down, far)
     with jax.named_scope("gate_zh"):
         got = swap(total, "zh", 1)
-    total, _ = add(total, got, last, far_got)
+    total, _ = add(total, got, last, far_got, own_rest)
     with jax.named_scope("gate_core_back"):
         other = swap(total, "c", 1)
     gate_grad = pl.pallas_call(

time: 122 us -> 116 us (0.951)
  waiting for transfers between devices: 37 us -> 30.9 us
    ppermute x25, waiting for transfers between devices: 34.4 us -> 27 us  [swap(): return lax.ppermute(value, axis, [(i, i ^ mask) for i in range(size)])]
    ppermute x3, waiting for transfers between devices: 0.01 us -> 1.3 us  [ring(): return lax.ppermute(value, (axis, 'c'), pairs)]
  transfers between devices with their start and end apart: 31 -> 31, of which waited for: 13 -> 16; matrix products, arithmetic and copies ran while one was open for 2% -> 2% of each run, Pallas kernels for 13% -> 14%
where the time goes in v13:
time: 116 us
  starting transfers between devices  57.7 us (50%)
  waiting for transfers between devices  30.9 us (27%)
  Pallas kernels  17.6 us (15%)
  local copies, waits for them, and re-layouts  7.33 us (6%)
    ppermute x25, starting transfers between devices, swap(): return lax.ppermute(value, axis, [(i, i ^ mask) for i in range(size)])  51.6 us
    ppermute x25, waiting for transfers between devices, swap(): return lax.ppermute(value, axis, [(i, i ^ mask) for i in range(size)])  27 us
    unnamed x18, local copies, waits for them, and re-layouts  5.5 us
    pallas_call x2, Pallas kernels, products(): pl.pallas_call(functools.partial(product_kernel, first), in_specs=[SMEM]...  3.97 us
    ppermute x3, starting transfers between devices, ring(): return lax.ppermute(value, (axis, 'c'), pairs)  3.62 us
    pallas_call x1, Pallas kernels, on_device(): pl.pallas_call(far_kernel, in_specs=[SMEM] + [VMEM] * 12 + [ANY], out_spe...  3.36 us
    ppermute x3, waiting for transfers between devices, pairs(): lax.ppermute(value, (axis, 'c'), [(2 * i + c, 2 * partner(i, c) + c) for...  2.66 us
    ppermute x3, starting transfers between devices, pairs(): lax.ppermute(value, (axis, 'c'), [(2 * i + c, 2 * partner(i, c) + c) for...  2.52 us
  transfers between devices with their start and end apart: 31, of which 16 were waited for; matrix products, arithmetic and copies ran while one was open for 2% of the time, Pallas kernels for 14%

profile of v13, /device:TPU:1, one launch (start us, length us, event | category | flops | bytes accessed | tf_op | source)
XLA Modules:
  0.0 115.5 jit_solution(12978560409707389881)
XLA Ops:
  0.6 3.3 %collective-permute-start.4 = (bf16[128,4608]{1,0:T(8,128)(2,1)}, bf16[128,4608]{1,0:T(8,128)(2,1)S(1)}, u32[]{:S(2)}, u32[]{:S(2)}) collective-permute-start(bf16[128,4608]{1,0:T(8,128)(2,1)} %own.1), channel_id=1, source_target_pairs={{0,1},{1,0},{2,3},{3,2},{4,5},{5,4},{6,7},{7,6},{8,9},{9,8},{10,11... | collective-permute-start | bytes 3538952 | tf_op jit(solution)/shard_map/tokens_core/ppermute | solution.py:60
  4.0 1.0 collective-permute-start.6
  5.0 1.1 constant_dynamic-slice_fusion.1
  6.8 0.9 pad_maximum_fusion
  7.7 6.9 %collective-permute-start.7 = (bf16[64,4736]{1,0:T(8,128)(2,1)}, bf16[64,4736]{1,0:T(8,128)(2,1)}, u32[]{:S(2)}, u32[]{:S(2)}) collective-permute-start(bf16[64,4736]{1,0:T(8,128)(2,1)} %pad_maximum_fusion), channel_id=1, source_target_pairs={{0,2},{2,0},{1,3},{3,1},{4,6},{6,4},{5,7},{7,5},{8,10},{10,8},{9,1... | collective-permute-start | bytes 1818632 | tf_op jit(solution)/shard_map/weight_z/ppermute | solution.py:60
  14.6 1.2 %copy-done.5 = bf16[2048,256]{1,0:T(8,128)(2,1)S(1)} copy-done((bf16[2048,256]{1,0:T(8,128)(2,1)S(1)}, bf16[2048,256]{1,0:T(8,128)(2,1)}, u32[]{:S(2)}) %copy-start.5) | copy-done | bytes 1048600
  15.9 0.8 copy-done.6
  16.7 1.0 rank_products.1
  17.8 1.3 %copy-done.2 = bf16[128,4608]{1,0:T(8,128)(2,1)S(1)} copy-done((bf16[128,4608]{1,0:T(8,128)(2,1)S(1)}, bf16[128,4608]{1,0:T(8,128)(2,1)}, u32[]{:S(2)}) %copy-start.2) | copy-done | bytes 1179672
  19.1 1.3 %copy-done.4 = bf16[128,4608]{1,0:T(8,128)(2,1)S(1)} copy-done((bf16[128,4608]{1,0:T(8,128)(2,1)S(1)}, bf16[128,4608]{1,0:T(8,128)(2,1)}, u32[]{:S(2)}) %copy-start.4) | copy-done | bytes 1179672
  20.3 0.9 copy-done.8
  21.2 2.0 %token_values.1 = (bf16[128,128]{1,0:T(8,128)(2,1)S(1)}, f32[8,128]{1,0:T(8,128)S(1)}, f32[128,128]{1,0:T(8,128)S(1)}) custom-call(s32[4]{0:T(128)S(1)} %pad_add_fusion.at, bf16[128,4608]{1,0:T(8,128)(2,1)S(1)} %copy-done.2, bf16[128,4608]{1,0:T(8,128)(2,1)S(1)} %copy-done.1, bf16[128,4608]{1,0:T(8,128)(2,1)S(1)} %copy-done.4, bf16[8,4608]{1,0:T(8,128)(2,1)S(1)} %copy-done.8), custom_call_target="tpu_custom_call" | custom-call | flops 452984832 | bytes 7077888 | tf_op jit(solution)/shard_map/token_values/pallas_call | solution.py:257
  24.4 1.4 %collective-permute-start.2 = (bf16[3,128,128]{2,1,0:T(8,128)(2,1)S(1)}, bf16[3,128,128]{2,1,0:T(8,128)(2,1)S(1)}, u32[]{:S(2)}, u32[]{:S(2)}) collective-permute-start(bf16[3,128,128]{2,1,0:T(8,128)(2,1)S(1)} %get-tuple-element.29), channel_id=1, source_target_pairs={{0,8},{4,12},{8,0},{12,4},{1,9},{5,13},{9,1},{13,5},{2,10},{6,14},... | collective-permute-start | bytes 294920 | tf_op jit(solution)/shard_map/act_y/ppermute | solution.py:60
  25.8 2.1 %collective-permute-done.1.first = bf16[3,128,128]{2,1,0:T(8,128)(2,1)S(1)} collective-permute-done((bf16[3,128,128]{2,1,0:T(8,128)(2,1)S(1)}, bf16[3,128,128]{2,1,0:T(8,128)(2,1)S(1)}, u32[]{:S(2)}, u32[]{:S(2)}) %collective-permute-start.1) | collective-permute-done | bytes 98336 | tf_op jit(solution)/shard_map/act_y/ppermute | solution.py:60
  28.7 2.0 %collective-permute-done.2.second = bf16[3,128,128]{2,1,0:T(8,128)(2,1)S(1)} collective-permute-done((bf16[3,128,128]{2,1,0:T(8,128)(2,1)S(1)}, bf16[3,128,128]{2,1,0:T(8,128)(2,1)S(1)}, u32[]{:S(2)}, u32[]{:S(2)}) %collective-permute-start.2) | collective-permute-done | bytes 98336 | tf_op jit(solution)/shard_map/act_y/ppermute | solution.py:60
  30.7 1.9 %collective-permute-done.3.third = bf16[3,128,128]{2,1,0:T(8,128)(2,1)S(1)} collective-permute-done((bf16[3,128,128]{2,1,0:T(8,128)(2,1)S(1)}, bf16[3,128,128]{2,1,0:T(8,128)(2,1)S(1)}, u32[]{:S(2)}, u32[]{:S(2)}) %collective-permute-start.3) | collective-permute-done | bytes 98336 | tf_op jit(solution)/shard_map/act_y/ppermute | solution.py:60
  33.2 7.2 %collective-permute-done.7.refs_1_ = bf16[64,4736]{1,0:T(8,128)(2,1)} collective-permute-done((bf16[64,4736]{1,0:T(8,128)(2,1)}, bf16[64,4736]{1,0:T(8,128)(2,1)}, u32[]{:S(2)}, u32[]{:S(2)}) %collective-permute-start.7) | collective-permute-done | bytes 606240 | tf_op jit(solution)/shard_map/weight_z/ppermute | solution.py:60
  40.4 1.2 %collective-permute-start.17 = (bf16[128,4608]{1,0:T(8,128)(2,1)S(1)}, bf16[128,4608]{1,0:T(8,128)(2,1)S(1)}, u32[]{:S(2)}, u32[]{:S(2)}) collective-permute-start(bf16[128,4608]{1,0:T(8,128)(2,1)S(1)} %get-tuple-element.35.more.one), channel_id=1, source_target_pairs={{0,4},{1,13},{4,8},{5,1},{8,12},{9,5},{12,0},{13,9},{2,6},{3,15},{... | collective-permute-start | bytes 3538952 | tf_op jit(solution)/shard_map/tokens_y/ppermute | solution.py:27
  41.6 2.5 %collective-permute-start.11 = (bf16[64,4736]{1,0:T(8,128)(2,1)}, bf16[64,4736]{1,0:T(8,128)(2,1)S(1)}, u32[]{:S(2)}, u32[]{:S(2)}) collective-permute-start(bf16[64,4736]{1,0:T(8,128)(2,1)} %get-tuple-element.39.refs_0_), channel_id=1, source_target_pairs={{0,64},{1,193},{64,0},{65,129},{128,192},{129,65},{192,128},{193,1... | collective-permute-start | bytes 1818632 | tf_op jit(solution)/shard_map/weight_x/ppermute | solution.py:33
  44.5 1.0 collective-permute-done.9.mixed_s.refs_0_
  45.5 6.1 %collective-permute-start.5 = (bf16[128,128]{1,0:T(8,128)(2,1)S(1)}, bf16[128,128]{1,0:T(8,128)(2,1)S(1)}, u32[]{:S(2)}, u32[]{:S(2)}) collective-permute-start(bf16[128,128]{1,0:T(8,128)(2,1)S(1)} %get-tuple-element.32.refs_2_.tie), channel_id=1, source_target_pairs={{0,2},{2,0},{1,3},{3,1},{4,6},{6,4},{5,7},{7,5},{8,10},{10,8},{9,1... | collective-permute-start | bytes 98312 | tf_op jit(solution)/shard_map/act_z/ppermute | solution.py:60
  51.6 2.0 %own_near.1.tie.near = bf16[2,256,256]{2,1,0:T(8,128)(2,1)S(1)} custom-call(s32[4]{0:T(128)S(1)} %pad_add_fusion.at, bf16[128,4608]{1,0:T(8,128)(2,1)S(1)} %copy-done.1, bf16[128,4608]{1,0:T(8,128)(2,1)S(1)} %collective-permute-done.4.tie.near_s.own_s, bf16[128,4608]{1,0:T(8,128)(2,1)S(1)} %get-tuple-element.35.more.one, ...), custom_call_target="tpu_custom_call" | custom-call | flops 1241513984 | bytes 7274496 | tf_op jit(solution)/shard_map/own_near/pallas_call | solution.py:308
  53.6 1.2 %gate_products.1 = (f32[8,2304]{1,0:T(8,128)S(1)}, f32[8,2304]{1,0:T(8,128)S(1)}) custom-call(s32[4]{0:T(128)S(1)} %pad_add_fusion.at, f32[128,128]{1,0:T(8,128)S(1)} %get-tuple-element.31.keep, bf16[128,128]{1,0:T(8,128)(2,1)S(1)} %collective-permute-done.5.got, f32[128,128]{1,0:T(8,128)S(1)} %get-tuple-element.33.back, ...), custom_call_target="tpu_custom_call" | custom-call | tf_op jit(solution)/shard_map/gate_products/pallas_call | solution.py:320
  55.4 2.0 %collective-permute-done.11.refs_0_ = bf16[64,4736]{1,0:T(8,128)(2,1)S(1)} collective-permute-done((bf16[64,4736]{1,0:T(8,128)(2,1)}, bf16[64,4736]{1,0:T(8,128)(2,1)S(1)}, u32[]{:S(2)}, u32[]{:S(2)}) %collective-permute-start.11) | collective-permute-done | bytes 606240 | tf_op jit(solution)/shard_map/weight_x/ppermute | solution.py:33
  57.5 1.8 %collective-permute-start.21 = (bf16[128,4608]{1,0:T(8,128)(2,1)S(1)}, bf16[128,4608]{1,0:T(8,128)(2,1)S(1)}, u32[]{:S(2)}, u32[]{:S(2)}) collective-permute-start(bf16[128,4608]{1,0:T(8,128)(2,1)S(1)} %fence.6.refs_2_.two.near), channel_id=1, source_target_pairs={{0,1},{1,0},{2,3},{3,2},{4,5},{5,4},{6,7},{7,6},{8,9},{9,8},{10,11... | collective-permute-start | bytes 3538952 | tf_op jit(solution)/shard_map/tokens_core/ppermute | solution.py:60
  59.3 1.4 %collective-permute-start.26 = (bf16[128,4608]{1,0:T(8,128)(2,1)S(1)}, bf16[128,4608]{1,0:T(8,128)(2,1)S(1)}, u32[]{:S(2)}, u32[]{:S(2)}) collective-permute-start(bf16[128,4608]{1,0:T(8,128)(2,1)S(1)} %fence.6.refs_2_.two.near), channel_id=1, source_target_pairs={{0,4},{1,13},{4,8},{5,1},{8,12},{9,5},{12,0},{13,9},{2,6},{3,15},{... | collective-permute-start | bytes 3538952 | tf_op jit(solution)/shard_map/tokens_y/ppermute | solution.py:27
  60.7 2.2 %collective-permute-start.13 = (bf16[8,2304]{1,0:T(8,128)(2,1)S(1)}, bf16[8,2304]{1,0:T(8,128)(2,1)S(1)}, u32[]{:S(2)}, u32[]{:S(2)}) collective-permute-start(bf16[8,2304]{1,0:T(8,128)(2,1)S(1)} %get-tuple-element.41), channel_id=1, source_target_pairs={{0,16},{16,0},{32,48},{48,32},{1,17},{17,1},{33,49},{49,33},{2,18}... | collective-permute-start | bytes 110600 | tf_op jit(solution)/shard_map/gate_zl/ppermute | solution.py:60
  63.6 1.0 collective-permute-done.13.second
  64.6 1.8 %collective-permute-start.15 = (bf16[8,2304]{1,0:T(8,128)(2,1)S(1)}, bf16[8,2304]{1,0:T(8,128)(2,1)S(1)}, u32[]{:S(2)}, u32[]{:S(2)}) collective-permute-start(bf16[8,2304]{1,0:T(8,128)(2,1)S(1)} %get-tuple-element.41), channel_id=1, source_target_pairs={{0,48},{16,32},{32,16},{48,0},{1,49},{17,33},{33,17},{49,1},{2,50}... | collective-permute-start | bytes 110600 | tf_op jit(solution)/shard_map/gate_zl/ppermute | solution.py:60
  67.2 2.1 %collective-permute-done.15.fourth = bf16[8,2304]{1,0:T(8,128)(2,1)S(1)} collective-permute-done((bf16[8,2304]{1,0:T(8,128)(2,1)S(1)}, bf16[8,2304]{1,0:T(8,128)(2,1)S(1)}, u32[]{:S(2)}, u32[]{:S(2)}) %collective-permute-start.15) | collective-permute-done | bytes 36896 | tf_op jit(solution)/shard_map/gate_zl/ppermute | solution.py:60
  70.0 3.4 %far_products.1 = (bf16[3,256,256]{2,1,0:T(8,128)(2,1)S(1)}, bf16[256,4608]{1,0:T(8,128)(2,1)S(1)}, bf16[256,128]{1,0:T(8,128)(2,1)S(1)}) custom-call(s32[4]{0:T(128)S(1)} %pad_add_fusion.at, bf16[128,4608]{1,0:T(8,128)(2,1)S(1)} %copy-done.1, bf16[128,4608]{1,0:T(8,128)(2,1)S(1)} %collective-permute-done.4.tie.near_s.own_s, ...), custom_call_target="tpu_custom_call" | custom-call | flops 1862270976 | bytes 10911744 | tf_op jit(solution)/shard_map/far_products/pallas_call | solution.py:368
  73.3 1.3 %collective-permute-done.26.refs_0_ = bf16[128,4608]{1,0:T(8,128)(2,1)S(1)} collective-permute-done((bf16[128,4608]{1,0:T(8,128)(2,1)S(1)}, bf16[128,4608]{1,0:T(8,128)(2,1)S(1)}, u32[]{:S(2)}, u32[]{:S(2)}) %collective-permute-start.26) | collective-permute-done | bytes 1179680 | tf_op jit(solution)/shard_map/tokens_y/ppermute | solution.py:27
  74.6 2.3 %collective-permute-start.27 = (bf16[128,4608]{1,0:T(8,128)(2,1)S(1)}, bf16[128,4608]{1,0:T(8,128)(2,1)S(1)}, u32[]{:S(2)}, u32[]{:S(2)}) collective-permute-start(bf16[128,4608]{1,0:T(8,128)(2,1)S(1)} %fence.7.three.more), channel_id=1, source_target_pairs={{0,1},{1,0},{2,3},{3,2},{4,5},{5,4},{6,7},{7,6},{8,9},{9,8},{10,11... | collective-permute-start | bytes 3538952 | tf_op jit(solution)/shard_map/tokens_core/ppermute | solution.py:60
  77.0 6.1 %collective-permute-start.28 = (bf16[3,256,256]{2,1,0:T(8,128)(2,1)S(1)}, bf16[3,256,256]{2,1,0:T(8,128)(2,1)S(1)}, u32[]{:S(2)}, u32[]{:S(2)}) collective-permute-start(bf16[3,256,256]{2,1,0:T(8,128)(2,1)S(1)} %get-tuple-element.42.refs_0_.refs_1_.tie), channel_id=1, source_target_pairs={{0,2},{2,0},{1,3},{3,1},{4,6},{6,4},{5,7},{7,5},{8,10},{10,8},{9,1... | collective-permute-start | bytes 1179656 | tf_op jit(solution)/shard_map/out_z/ppermute | solution.py:60
  83.1 3.7 %collective-permute-start.19 = (f32[8,2304]{1,0:T(8,128)S(1)}, f32[8,2304]{1,0:T(8,128)S(1)}, u32[]{:S(2)}, u32[]{:S(2)}) collective-permute-start(f32[8,2304]{1,0:T(8,128)S(1)} %gate_sum.6.refs_4_.first), channel_id=1, source_target_pairs={{0,128},{64,192},{128,0},{192,64},{1,129},{65,193},{129,1},{193,65... | collective-permute-start | bytes 221192 | tf_op jit(solution)/shard_map/gate_x/ppermute | solution.py:60
  86.9 3.5 %collective-permute-done.19.third = f32[8,2304]{1,0:T(8,128)S(1)} collective-permute-done((f32[8,2304]{1,0:T(8,128)S(1)}, f32[8,2304]{1,0:T(8,128)S(1)}, u32[]{:S(2)}, u32[]{:S(2)}) %collective-permute-start.19) | collective-permute-done | bytes 73760 | tf_op jit(solution)/shard_map/gate_x/ppermute | solution.py:60
  90.4 1.5 %collective-permute-done.20.fourth = f32[8,2304]{1,0:T(8,128)S(1)} collective-permute-done((f32[8,2304]{1,0:T(8,128)S(1)}, f32[8,2304]{1,0:T(8,128)S(1)}, u32[]{:S(2)}, u32[]{:S(2)}) %collective-permute-start.20) | collective-permute-done | bytes 73760 | tf_op jit(solution)/shard_map/gate_x/ppermute | solution.py:60
  92.1 1.5 %collective-permute-start.23 = (f32[8,2304]{1,0:T(8,128)S(1)}, f32[8,2304]{1,0:T(8,128)S(1)}, u32[]{:S(2)}, u32[]{:S(2)}) collective-permute-start(f32[8,2304]{1,0:T(8,128)S(1)} %gate_sum.7.first), channel_id=1, source_target_pairs={{0,8},{4,12},{8,0},{12,4},{1,9},{5,13},{9,1},{13,5},{2,10},{6,14},... | collective-permute-start | bytes 221192 | tf_op jit(solution)/shard_map/gate_y/ppermute | solution.py:60
  93.6 2.3 %collective-permute-start.24 = (f32[8,2304]{1,0:T(8,128)S(1)}, f32[8,2304]{1,0:T(8,128)S(1)}, u32[]{:S(2)}, u32[]{:S(2)}) collective-permute-start(f32[8,2304]{1,0:T(8,128)S(1)} %gate_sum.7.first), channel_id=1, source_target_pairs={{0,12},{4,8},{8,4},{12,0},{1,13},{5,9},{9,5},{13,1},{2,14},{6,10},... | collective-permute-start | bytes 221192 | tf_op jit(solution)/shard_map/gate_y/ppermute | solution.py:60
  95.9 1.5 %collective-permute-done.23.third = f32[8,2304]{1,0:T(8,128)S(1)} collective-permute-done((f32[8,2304]{1,0:T(8,128)S(1)}, f32[8,2304]{1,0:T(8,128)S(1)}, u32[]{:S(2)}, u32[]{:S(2)}) %collective-permute-start.23) | collective-permute-done | bytes 73760 | tf_op jit(solution)/shard_map/gate_y/ppermute | solution.py:60
  97.4 1.5 %collective-permute-done.24.fourth = f32[8,2304]{1,0:T(8,128)S(1)} collective-permute-done((f32[8,2304]{1,0:T(8,128)S(1)}, f32[8,2304]{1,0:T(8,128)S(1)}, u32[]{:S(2)}, u32[]{:S(2)}) %collective-permute-start.24) | collective-permute-done | bytes 73760 | tf_op jit(solution)/shard_map/gate_y/ppermute | solution.py:60
  99.5 1.3 %far_products_last.1.refs_0_ = bf16[256,256]{1,0:T(8,128)(2,1)S(1)} custom-call(s32[4]{0:T(128)S(1)} %pad_add_fusion.at, bf16[128,4608]{1,0:T(8,128)(2,1)S(1)} %fence.7.three.more, bf16[128,4608]{1,0:T(8,128)(2,1)S(1)} %collective-permute-done.27.three_s.more_s, bf16[4,128,128]{2,1,0:T(8,128)(2,1)S(1)} %get-tuple-element.36.mixed, ...), custom_call_target="tpu_custom_call" | custom-call | flops 620756992 | bytes 3637248 | tf_op jit(solution)/shard_map/far_products_last/pallas_call | solution.py:392
  100.9 5.0 %collective-permute-start.30 = (bf16[256,256]{1,0:T(8,128)(2,1)S(1)}, bf16[256,256]{1,0:T(8,128)(2,1)S(1)}, u32[]{:S(2)}, u32[]{:S(2)}) collective-permute-start(bf16[256,256]{1,0:T(8,128)(2,1)S(1)} %far_products_last.1.refs_0_), channel_id=1, source_target_pairs={{0,2},{2,0},{1,3},{3,1},{4,6},{6,4},{5,7},{7,5},{8,10},{10,8},{9,1... | collective-permute-start | bytes 393224 | tf_op jit(solution)/shard_map/out_z_last/ppermute | solution.py:60
  105.8 2.0 %own_rest.1.refs_2_.rest = bf16[2,256,256]{2,1,0:T(8,128)(2,1)S(1)} custom-call(s32[4]{0:T(128)S(1)} %pad_add_fusion.at, bf16[128,4608]{1,0:T(8,128)(2,1)S(1)} %fence.6.refs_2_.two.near, bf16[128,4608]{1,0:T(8,128)(2,1)S(1)} %collective-permute-done.21.two_s.near_s, bf16[128,4608]{1,0:T(8,128)(2,1)S(1)} %fence.7.three.more, ...), custom_call_target="tpu_custom_call" | custom-call | flops 1241513984 | bytes 7274496 | tf_op jit(solution)/shard_map/own_rest/pallas_call | solution.py:308
  108.5 3.1 %collective-permute-start.29 = (f32[8,2304]{1,0:T(8,128)S(1)}, f32[8,2304]{1,0:T(8,128)S(1)}, u32[]{:S(2)}, u32[]{:S(2)}) collective-permute-start(f32[8,2304]{1,0:T(8,128)S(1)} %get-tuple-element.45.mine), channel_id=1, source_target_pairs={{0,1},{1,0},{2,3},{3,2},{4,5},{5,4},{6,7},{7,6},{8,9},{9,8},{10,11... | collective-permute-start | bytes 221192 | tf_op jit(solution)/shard_map/gate_core_back/ppermute | solution.py:60
  111.6 0.9 collective-permute-done.29.other
  112.5 1.2 %gate_halves.1 = f32[8,4608]{1,0:T(8,128)} custom-call(s32[4]{0:T(128)S(1)} %pad_add_fusion.at, f32[8,2304]{1,0:T(8,128)S(1)} %get-tuple-element.45.mine, f32[8,2304]{1,0:T(8,128)S(1)} %collective-permute-done.29.other), custom_call_target="tpu_custom_call" | custom-call | tf_op jit(solution)/shard_map/gate_halves/pallas_call | solution.py:410
  113.7 1.6 %place.1 = bf16[4,2,2,128,256]{4,3,2,1,0:T(8,128)(2,1)} custom-call(s32[4]{0:T(128)S(1)} %pad_add_fusion.at, bf16[2,256,256]{2,1,0:T(8,128)(2,1)S(1)} %own_near.1.tie.near, bf16[2,256,256]{2,1,0:T(8,128)(2,1)S(1)} %own_rest.1.refs_2_.rest, bf16[3,256,256]{2,1,0:T(8,128)(2,1)S(1)} %collective-permute-done.28.refs_1_.got, ...), custom_call_target="tpu_custom_call" | custom-call | tf_op jit(solution)/shard_map/place/pallas_call | solution.py:419
  (56 shorter events, 8.1 us)
Async XLA Ops:
  0.6 32.0 %collective-permute-start.4 = (bf16[128,4608]{1,0:T(8,128)(2,1)}, bf16[128,4608]{1,0:T(8,128)(2,1)S(1)}, u32[]{:S(2)}, u32[]{:S(2)}) collective-permute-start(bf16[128,4608]{1,0:T(8,128)(2,1)} %own.1), channel_id=1, source_target_pairs={{0,1},{1,0},{2,3},{3,2},{4,5},{5,4},{6,7},{7,6},{8,9},{9,8},{10,11... | collective-permute-start | bytes 3538952 | tf_op jit(solution)/shard_map/tokens_core/ppermute | solution.py:60
  4.0 36.5 %collective-permute-start.6 = (bf16[128,4608]{1,0:T(8,128)(2,1)}, bf16[128,4608]{1,0:T(8,128)(2,1)S(1)}, u32[]{:S(2)}, u32[]{:S(2)}) collective-permute-start(bf16[128,4608]{1,0:T(8,128)(2,1)} %own.1), channel_id=1, source_target_pairs={{0,4},{1,13},{4,8},{5,1},{8,12},{9,5},{12,0},{13,9},{2,6},{3,15},{... | collective-permute-start | bytes 3538952 | tf_op jit(solution)/shard_map/tokens_y/ppermute | solution.py:27
  6.8 11.0 %copy-start.1 = (bf16[128,4608]{1,0:T(8,128)(2,1)S(1)}, bf16[128,4608]{1,0:T(8,128)(2,1)}, u32[]{:S(2)}) copy-start(bf16[128,4608]{1,0:T(8,128)(2,1)} %own.1) | copy-start | bytes 3538948
  7.7 32.8 %collective-permute-start.7 = (bf16[64,4736]{1,0:T(8,128)(2,1)}, bf16[64,4736]{1,0:T(8,128)(2,1)}, u32[]{:S(2)}, u32[]{:S(2)}) collective-permute-start(bf16[64,4736]{1,0:T(8,128)(2,1)} %pad_maximum_fusion), channel_id=1, source_target_pairs={{0,2},{2,0},{1,3},{3,1},{4,6},{6,4},{5,7},{7,5},{8,10},{10,8},{9,1... | collective-permute-start | bytes 1818632 | tf_op jit(solution)/shard_map/weight_z/ppermute | solution.py:60
  14.6 1.2 %copy-start.5 = (bf16[2048,256]{1,0:T(8,128)(2,1)S(1)}, bf16[2048,256]{1,0:T(8,128)(2,1)}, u32[]{:S(2)}) copy-start(bf16[2048,256]{1,0:T(8,128)(2,1)} %param.9) | copy-start | bytes 3145732
  15.9 0.8 copy-start.6
  17.7 5.5 %collective-permute-start = (bf16[4,2,128,128]{3,2,1,0:T(8,128)(2,1)S(1)}, bf16[4,2,128,128]{3,2,1,0:T(8,128)(2,1)S(1)}, u32[]{:S(2)}, u32[]{:S(2)}) collective-permute-start(bf16[4,2,128,128]{3,2,1,0:T(8,128)(2,1)S(1)} %get-tuple-element.25), channel_id=1, source_target_pairs={{0,1},{1,0},{2,3},{3,2},{4,5},{5,4},{6,7},{7,6},{8,9},{9,8},{10,11... | collective-permute-start | bytes 786440 | tf_op jit(solution)/shard_map/act_core/ppermute | solution.py:60
  17.8 1.3 %copy-start.2 = (bf16[128,4608]{1,0:T(8,128)(2,1)S(1)}, bf16[128,4608]{1,0:T(8,128)(2,1)}, u32[]{:S(2)}) copy-start(bf16[128,4608]{1,0:T(8,128)(2,1)} %hidden.3) | copy-start | bytes 3538948
  19.1 1.3 %copy-start.4 = (bf16[128,4608]{1,0:T(8,128)(2,1)S(1)}, bf16[128,4608]{1,0:T(8,128)(2,1)}, u32[]{:S(2)}) copy-start(bf16[128,4608]{1,0:T(8,128)(2,1)} %up.1) | copy-start | bytes 3538948
  20.3 0.9 copy-start.8
  23.8 4.1 %collective-permute-start.1 = (bf16[3,128,128]{2,1,0:T(8,128)(2,1)S(1)}, bf16[3,128,128]{2,1,0:T(8,128)(2,1)S(1)}, u32[]{:S(2)}, u32[]{:S(2)}) collective-permute-start(bf16[3,128,128]{2,1,0:T(8,128)(2,1)S(1)} %get-tuple-element.28), channel_id=1, source_target_pairs={{0,4},{4,0},{8,12},{12,8},{1,5},{5,1},{9,13},{13,9},{2,6},{6,2},{1... | collective-permute-start | bytes 294920 | tf_op jit(solution)/shard_map/act_y/ppermute | solution.py:60
  24.4 6.3 %collective-permute-start.2 = (bf16[3,128,128]{2,1,0:T(8,128)(2,1)S(1)}, bf16[3,128,128]{2,1,0:T(8,128)(2,1)S(1)}, u32[]{:S(2)}, u32[]{:S(2)}) collective-permute-start(bf16[3,128,128]{2,1,0:T(8,128)(2,1)S(1)} %get-tuple-element.29), channel_id=1, source_target_pairs={{0,8},{4,12},{8,0},{12,4},{1,9},{5,13},{9,1},{13,5},{2,10},{6,14},... | collective-permute-start | bytes 294920 | tf_op jit(solution)/shard_map/act_y/ppermute | solution.py:60
  27.9 4.7 %collective-permute-start.3 = (bf16[3,128,128]{2,1,0:T(8,128)(2,1)S(1)}, bf16[3,128,128]{2,1,0:T(8,128)(2,1)S(1)}, u32[]{:S(2)}, u32[]{:S(2)}) collective-permute-start(bf16[3,128,128]{2,1,0:T(8,128)(2,1)S(1)} %get-tuple-element.30), channel_id=1, source_target_pairs={{0,12},{4,8},{8,4},{12,0},{1,13},{5,9},{9,5},{13,1},{2,14},{6,10},... | collective-permute-start | bytes 294920 | tf_op jit(solution)/shard_map/act_y/ppermute | solution.py:60
  32.6 19.0 %copy-start = (bf16[256,4608]{1,0:T(8,128)(2,1)S(1)}, bf16[256,4608]{1,0:T(8,128)(2,1)}, u32[]{:S(2)}) copy-start(bf16[256,4608]{1,0:T(8,128)(2,1)} %weight.3) | copy-start | bytes 7077892
  33.2 18.4 %copy-start.7 = (bf16[256,128]{1,0:T(8,128)(2,1)S(1)}, bf16[256,128]{1,0:T(8,128)(2,1)}, u32[]{:S(2)}) copy-start(bf16[256,128]{1,0:T(8,128)(2,1)} %down.5) | copy-start | bytes 196612
  40.4 11.2 %collective-permute-start.8 = (bf16[128,4608]{1,0:T(8,128)(2,1)S(1)}, bf16[128,4608]{1,0:T(8,128)(2,1)S(1)}, u32[]{:S(2)}, u32[]{:S(2)}) collective-permute-start(bf16[128,4608]{1,0:T(8,128)(2,1)S(1)} %get-tuple-element.35.more.one), channel_id=1, source_target_pairs={{0,1},{1,0},{2,3},{3,2},{4,5},{5,4},{6,7},{7,6},{8,9},{9,8},{10,11... | collective-permute-start | bytes 3538952 | tf_op jit(solution)/shard_map/tokens_core/ppermute | solution.py:60
  40.4 17.0 %collective-permute-start.17 = (bf16[128,4608]{1,0:T(8,128)(2,1)S(1)}, bf16[128,4608]{1,0:T(8,128)(2,1)S(1)}, u32[]{:S(2)}, u32[]{:S(2)}) collective-permute-start(bf16[128,4608]{1,0:T(8,128)(2,1)S(1)} %get-tuple-element.35.more.one), channel_id=1, source_target_pairs={{0,4},{1,13},{4,8},{5,1},{8,12},{9,5},{12,0},{13,9},{2,6},{3,15},{... | collective-permute-start | bytes 3538952 | tf_op jit(solution)/shard_map/tokens_y/ppermute | solution.py:27
  41.6 15.8 %collective-permute-start.11 = (bf16[64,4736]{1,0:T(8,128)(2,1)}, bf16[64,4736]{1,0:T(8,128)(2,1)S(1)}, u32[]{:S(2)}, u32[]{:S(2)}) collective-permute-start(bf16[64,4736]{1,0:T(8,128)(2,1)} %get-tuple-element.39.refs_0_), channel_id=1, source_target_pairs={{0,64},{1,193},{64,0},{65,129},{128,192},{129,65},{192,128},{193,1... | collective-permute-start | bytes 1818632 | tf_op jit(solution)/shard_map/weight_x/ppermute | solution.py:33
  44.1 13.3 %collective-permute-start.12 = (bf16[64,4736]{1,0:T(8,128)(2,1)}, bf16[64,4736]{1,0:T(8,128)(2,1)S(1)}, u32[]{:S(2)}, u32[]{:S(2)}) collective-permute-start(bf16[64,4736]{1,0:T(8,128)(2,1)} %get-tuple-element.39.refs_0_), channel_id=1, source_target_pairs={{0,192},{1,65},{64,128},{65,1},{128,64},{129,193},{192,0},{193,129... | collective-permute-start | bytes 1818632 | tf_op jit(solution)/shard_map/weight_x/ppermute | solution.py:33
  44.1 9.5 %copy-start.3 = (bf16[128,4608]{1,0:T(8,128)(2,1)S(1)}, bf16[128,4608]{1,0:T(8,128)(2,1)}, u32[]{:S(2)}) copy-start(bf16[128,4608]{1,0:T(8,128)(2,1)} %hidden.3) | copy-start | bytes 3538948
  44.1 1.4 %collective-permute-start.9 = (bf16[4,128,128]{2,1,0:T(8,128)(2,1)S(1)}, bf16[4,128,128]{2,1,0:T(8,128)(2,1)S(1)}, u32[]{:S(2)}, u32[]{:S(2)}) collective-permute-start(bf16[4,128,128]{2,1,0:T(8,128)(2,1)S(1)} %get-tuple-element.36.mixed), channel_id=1, source_target_pairs={{0,1},{1,0},{2,3},{3,2},{4,5},{5,4},{6,7},{7,6},{8,9},{9,8},{10,11... | collective-permute-start | bytes 393224 | tf_op jit(solution)/shard_map/mixed_core/ppermute | solution.py:60
  45.5 8.1 %collective-permute-start.5 = (bf16[128,128]{1,0:T(8,128)(2,1)S(1)}, bf16[128,128]{1,0:T(8,128)(2,1)S(1)}, u32[]{:S(2)}, u32[]{:S(2)}) collective-permute-start(bf16[128,128]{1,0:T(8,128)(2,1)S(1)} %get-tuple-element.32.refs_2_.tie), channel_id=1, source_target_pairs={{0,2},{2,0},{1,3},{3,1},{4,6},{6,4},{5,7},{7,5},{8,10},{10,8},{9,1... | collective-permute-start | bytes 98312 | tf_op jit(solution)/shard_map/act_z/ppermute | solution.py:60
  54.8 2.6 %collective-permute-start.10 = (f32[8,2304]{1,0:T(8,128)S(1)}, f32[8,2304]{1,0:T(8,128)S(1)}, u32[]{:S(2)}, u32[]{:S(2)}) collective-permute-start(f32[8,2304]{1,0:T(8,128)S(1)} %get-tuple-element.38), channel_id=1, source_target_pairs={{0,1},{1,0},{2,3},{3,2},{4,5},{5,4},{6,7},{7,6},{8,9},{9,8},{10,11... | collective-permute-start | bytes 221192 | tf_op jit(solution)/shard_map/gate_core/ppermute | solution.py:60
  57.5 12.5 %collective-permute-start.21 = (bf16[128,4608]{1,0:T(8,128)(2,1)S(1)}, bf16[128,4608]{1,0:T(8,128)(2,1)S(1)}, u32[]{:S(2)}, u32[]{:S(2)}) collective-permute-start(bf16[128,4608]{1,0:T(8,128)(2,1)S(1)} %fence.6.refs_2_.two.near), channel_id=1, source_target_pairs={{0,1},{1,0},{2,3},{3,2},{4,5},{5,4},{6,7},{7,6},{8,9},{9,8},{10,11... | collective-permute-start | bytes 3538952 | tf_op jit(solution)/shard_map/tokens_core/ppermute | solution.py:60
  59.3 15.3 %collective-permute-start.26 = (bf16[128,4608]{1,0:T(8,128)(2,1)S(1)}, bf16[128,4608]{1,0:T(8,128)(2,1)S(1)}, u32[]{:S(2)}, u32[]{:S(2)}) collective-permute-start(bf16[128,4608]{1,0:T(8,128)(2,1)S(1)} %fence.6.refs_2_.two.near), channel_id=1, source_target_pairs={{0,4},{1,13},{4,8},{5,1},{8,12},{9,5},{12,0},{13,9},{2,6},{3,15},{... | collective-permute-start | bytes 3538952 | tf_op jit(solution)/shard_map/tokens_y/ppermute | solution.py:27
  60.7 9.2 %collective-permute-start.16 = (bf16[64,4736]{1,0:T(8,128)(2,1)S(1)}, bf16[64,4736]{1,0:T(8,128)(2,1)S(1)}, u32[]{:S(2)}, u32[]{:S(2)}) collective-permute-start(bf16[64,4736]{1,0:T(8,128)(2,1)S(1)} %fence.5.refs_1_), channel_id=1, source_target_pairs={{0,192},{1,65},{64,128},{65,1},{128,64},{129,193},{192,0},{193,129... | collective-permute-start | bytes 1818632 | tf_op jit(solution)/shard_map/weight_x_far/ppermute | solution.py:33
  60.7 3.9 %collective-permute-start.13 = (bf16[8,2304]{1,0:T(8,128)(2,1)S(1)}, bf16[8,2304]{1,0:T(8,128)(2,1)S(1)}, u32[]{:S(2)}, u32[]{:S(2)}) collective-permute-start(bf16[8,2304]{1,0:T(8,128)(2,1)S(1)} %get-tuple-element.41), channel_id=1, source_target_pairs={{0,16},{16,0},{32,48},{48,32},{1,17},{17,1},{33,49},{49,33},{2,18}... | collective-permute-start | bytes 110600 | tf_op jit(solution)/shard_map/gate_zl/ppermute | solution.py:60
  63.0 4.3 %collective-permute-start.14 = (bf16[8,2304]{1,0:T(8,128)(2,1)S(1)}, bf16[8,2304]{1,0:T(8,128)(2,1)S(1)}, u32[]{:S(2)}, u32[]{:S(2)}) collective-permute-start(bf16[8,2304]{1,0:T(8,128)(2,1)S(1)} %get-tuple-element.41), channel_id=1, source_target_pairs={{0,32},{16,48},{32,0},{48,16},{1,33},{17,49},{33,1},{49,17},{2,34}... | collective-permute-start | bytes 110600 | tf_op jit(solution)/shard_map/gate_zl/ppermute | solution.py:60
  64.6 4.7 %collective-permute-start.15 = (bf16[8,2304]{1,0:T(8,128)(2,1)S(1)}, bf16[8,2304]{1,0:T(8,128)(2,1)S(1)}, u32[]{:S(2)}, u32[]{:S(2)}) collective-permute-start(bf16[8,2304]{1,0:T(8,128)(2,1)S(1)} %get-tuple-element.41), channel_id=1, source_target_pairs={{0,48},{16,32},{32,16},{48,0},{1,49},{17,33},{33,17},{49,1},{2,50}... | collective-permute-start | bytes 110600 | tf_op jit(solution)/shard_map/gate_zl/ppermute | solution.py:60
  74.6 24.9 %collective-permute-start.27 = (bf16[128,4608]{1,0:T(8,128)(2,1)S(1)}, bf16[128,4608]{1,0:T(8,128)(2,1)S(1)}, u32[]{:S(2)}, u32[]{:S(2)}) collective-permute-start(bf16[128,4608]{1,0:T(8,128)(2,1)S(1)} %fence.7.three.more), channel_id=1, source_target_pairs={{0,1},{1,0},{2,3},{3,2},{4,5},{5,4},{6,7},{7,6},{8,9},{9,8},{10,11... | collective-permute-start | bytes 3538952 | tf_op jit(solution)/shard_map/tokens_core/ppermute | solution.py:60
  77.0 30.9 %collective-permute-start.28 = (bf16[3,256,256]{2,1,0:T(8,128)(2,1)S(1)}, bf16[3,256,256]{2,1,0:T(8,128)(2,1)S(1)}, u32[]{:S(2)}, u32[]{:S(2)}) collective-permute-start(bf16[3,256,256]{2,1,0:T(8,128)(2,1)S(1)} %get-tuple-element.42.refs_0_.refs_1_.tie), channel_id=1, source_target_pairs={{0,2},{2,0},{1,3},{3,1},{4,6},{6,4},{5,7},{7,5},{8,10},{10,8},{9,1... | collective-permute-start | bytes 1179656 | tf_op jit(solution)/shard_map/out_z/ppermute | solution.py:60
  83.1 3.9 %collective-permute-start.18 = (f32[8,2304]{1,0:T(8,128)S(1)}, f32[8,2304]{1,0:T(8,128)S(1)}, u32[]{:S(2)}, u32[]{:S(2)}) collective-permute-start(f32[8,2304]{1,0:T(8,128)S(1)} %gate_sum.6.refs_4_.first), channel_id=1, source_target_pairs={{0,64},{64,0},{128,192},{192,128},{1,65},{65,1},{129,193},{193,129... | collective-permute-start | bytes 221192 | tf_op jit(solution)/shard_map/gate_x/ppermute | solution.py:60
  83.1 7.4 %collective-permute-start.19 = (f32[8,2304]{1,0:T(8,128)S(1)}, f32[8,2304]{1,0:T(8,128)S(1)}, u32[]{:S(2)}, u32[]{:S(2)}) collective-permute-start(f32[8,2304]{1,0:T(8,128)S(1)} %gate_sum.6.refs_4_.first), channel_id=1, source_target_pairs={{0,128},{64,192},{128,0},{192,64},{1,129},{65,193},{129,1},{193,65... | collective-permute-start | bytes 221192 | tf_op jit(solution)/shard_map/gate_x/ppermute | solution.py:60
  86.7 5.2 %collective-permute-start.20 = (f32[8,2304]{1,0:T(8,128)S(1)}, f32[8,2304]{1,0:T(8,128)S(1)}, u32[]{:S(2)}, u32[]{:S(2)}) collective-permute-start(f32[8,2304]{1,0:T(8,128)S(1)} %gate_sum.6.refs_4_.first), channel_id=1, source_target_pairs={{0,192},{64,128},{128,64},{192,0},{1,193},{65,129},{129,65},{193,1... | collective-permute-start | bytes 221192 | tf_op jit(solution)/shard_map/gate_x/ppermute | solution.py:60
  92.0 3.9 %collective-permute-start.22 = (f32[8,2304]{1,0:T(8,128)S(1)}, f32[8,2304]{1,0:T(8,128)S(1)}, u32[]{:S(2)}, u32[]{:S(2)}) collective-permute-start(f32[8,2304]{1,0:T(8,128)S(1)} %gate_sum.7.first), channel_id=1, source_target_pairs={{0,4},{4,0},{8,12},{12,8},{1,5},{5,1},{9,13},{13,9},{2,6},{6,2},{1... | collective-permute-start | bytes 221192 | tf_op jit(solution)/shard_map/gate_y/ppermute | solution.py:60
  92.1 5.4 %collective-permute-start.23 = (f32[8,2304]{1,0:T(8,128)S(1)}, f32[8,2304]{1,0:T(8,128)S(1)}, u32[]{:S(2)}, u32[]{:S(2)}) collective-permute-start(f32[8,2304]{1,0:T(8,128)S(1)} %gate_sum.7.first), channel_id=1, source_target_pairs={{0,8},{4,12},{8,0},{12,4},{1,9},{5,13},{9,1},{13,5},{2,10},{6,14},... | collective-permute-start | bytes 221192 | tf_op jit(solution)/shard_map/gate_y/ppermute | solution.py:60
  93.6 5.3 %collective-permute-start.24 = (f32[8,2304]{1,0:T(8,128)S(1)}, f32[8,2304]{1,0:T(8,128)S(1)}, u32[]{:S(2)}, u32[]{:S(2)}) collective-permute-start(f32[8,2304]{1,0:T(8,128)S(1)} %gate_sum.7.first), channel_id=1, source_target_pairs={{0,12},{4,8},{8,4},{12,0},{1,13},{5,9},{9,5},{13,1},{2,14},{6,10},... | collective-permute-start | bytes 221192 | tf_op jit(solution)/shard_map/gate_y/ppermute | solution.py:60
  98.9 8.9 %collective-permute-start.25 = (f32[8,2304]{1,0:T(8,128)S(1)}, f32[8,2304]{1,0:T(8,128)S(1)}, u32[]{:S(2)}, u32[]{:S(2)}) collective-permute-start(f32[8,2304]{1,0:T(8,128)S(1)} %gate_sum.8.tie.left), channel_id=1, source_target_pairs={{0,2},{2,0},{1,3},{3,1},{4,6},{6,4},{5,7},{7,5},{8,10},{10,8},{9,1... | collective-permute-start | bytes 221192 | tf_op jit(solution)/shard_map/gate_zh/ppermute | solution.py:60
  100.9 12.9 %collective-permute-start.30 = (bf16[256,256]{1,0:T(8,128)(2,1)S(1)}, bf16[256,256]{1,0:T(8,128)(2,1)S(1)}, u32[]{:S(2)}, u32[]{:S(2)}) collective-permute-start(bf16[256,256]{1,0:T(8,128)(2,1)S(1)} %far_products_last.1.refs_0_), channel_id=1, source_target_pairs={{0,2},{2,0},{1,3},{3,1},{4,6},{6,4},{5,7},{7,5},{8,10},{10,8},{9,1... | collective-permute-start | bytes 393224 | tf_op jit(solution)/shard_map/out_z_last/ppermute | solution.py:60
  108.5 4.0 %collective-permute-start.29 = (f32[8,2304]{1,0:T(8,128)S(1)}, f32[8,2304]{1,0:T(8,128)S(1)}, u32[]{:S(2)}, u32[]{:S(2)}) collective-permute-start(f32[8,2304]{1,0:T(8,128)S(1)} %get-tuple-element.45.mine), channel_id=1, source_target_pairs={{0,1},{1,0},{2,3},{3,2},{4,5},{5,4},{6,7},{7,6},{8,9},{9,8},{10,11... | collective-permute-start | bytes 221192 | tf_op jit(solution)/shard_map/gate_core_back/ppermute | solution.py:60

commit v14 on v13

--- a/solution.py
+++ b/solution.py
@@ -198,7 +198,7 @@
         rows_product(at, first + number, group, (mixed, mixed_s), weight, down, out.at[number])
 
 
-def place_kernel(at, near, rest, got, last, out, sems):
+def place_kernel(at, near, rest, got, last, tie, out, sems):
     y, zh, c = at[1], at[2], at[3]
     tokens = out.shape[3]
     copies = []
@@ -388,7 +388,8 @@
         three_s = swap(three, "c", 1)
     total = step(total, "x", far)
 
-    total = step(total, "y")
+    own_rest = products("own_rest", 2, two, two_s, three, three_s, weight, down, far)
+    total = step(total, "y", own_rest)
     last = pl.pallas_call(
         far_last_kernel,
         in_specs=[SMEM] + [VMEM] * 6 + [ANY],
@@ -401,10 +402,9 @@
     with jax.named_scope("out_z_last"):
         last_got = swap(last, "zh", 1)
 
-    own_rest = products("own_rest", 2, two, two_s, three, three_s, weight, down, far)
     with jax.named_scope("gate_zh"):
         got = swap(total, "zh", 1)
-    total, _ = add(total, got, last, far_got, own_rest)
+    total, _ = add(total, got, last, far_got)
     with jax.named_scope("gate_core_back"):
         other = swap(total, "c", 1)
     gate_grad = pl.pallas_call(
@@ -418,13 +418,13 @@
 
     out = pl.pallas_call(
         place_kernel,
-        in_specs=[SMEM] + [VMEM] * 4,
+        in_specs=[SMEM] + [VMEM] * 4 + [ANY],
         out_specs=HBM,
         out_shape=shaped((4, 2, 2, tokens, features), BF16),
         scratch_shapes=[pltpu.SemaphoreType.DMA((16,))],
         compiler_params=MIDDLE,
         name="place",
-    )(at, own_near, own_rest, far_got, last_got)
+    )(at, own_near, own_rest, far_got, last_got, gate_grad)
     return gate_grad, out.reshape(16 * tokens, features)
 
 

time: 116 us -> 117 us (level)
  starting transfers between devices: 57.7 us -> 58.9 us
    unnamed x18 -> x20, local copies, waits for them, and re-layouts: 5.5 us -> 6.41 us
where the time goes in v14:
time: 117 us; the launch traced here: 116 us
  starting transfers between devices  58.9 us (50%)
  waiting for transfers between devices  29.8 us (25%)
  Pallas kernels  17.6 us (15%)
  local copies, waits for them, and re-layouts  8.24 us (7%)
    ppermute x25, starting transfers between devices, swap(): return lax.ppermute(value, axis, [(i, i ^ mask) for i in range(size)])  52.7 us
    ppermute x25, waiting for transfers between devices, swap(): return lax.ppermute(value, axis, [(i, i ^ mask) for i in range(size)])  25.8 us
    unnamed x20, local copies, waits for them, and re-layouts  6.41 us
    pallas_call x2, Pallas kernels, products(): pl.pallas_call(functools.partial(product_kernel, first), in_specs=[SMEM]...  3.97 us
    ppermute x3, starting transfers between devices, ring(): return lax.ppermute(value, (axis, 'c'), pairs)  3.62 us
    pallas_call x1, Pallas kernels, on_device(): pl.pallas_call(far_kernel, in_specs=[SMEM] + [VMEM] * 12 + [ANY], out_spe...  3.36 us
    ppermute x3, waiting for transfers between devices, pairs(): lax.ppermute(value, (axis, 'c'), [(2 * i + c, 2 * partner(i, c) + c) for...  2.66 us
    ppermute x3, starting transfers between devices, pairs(): lax.ppermute(value, (axis, 'c'), [(2 * i + c, 2 * partner(i, c) + c) for...  2.52 us
  transfers between devices with their start and end apart: 31, of which 16 were waited for; matrix products, arithmetic and copies ran while one was open for 2% of the time, Pallas kernels for 14%

profile of v14, /device:TPU:1, one launch (start us, length us, event | category | flops | bytes accessed | tf_op | source)
XLA Modules:
  0.0 116.4 jit_solution(9959142548057711554)
XLA Ops:
  0.6 3.3 %collective-permute-start.4 = (bf16[128,4608]{1,0:T(8,128)(2,1)}, bf16[128,4608]{1,0:T(8,128)(2,1)S(1)}, u32[]{:S(2)}, u32[]{:S(2)}) collective-permute-start(bf16[128,4608]{1,0:T(8,128)(2,1)} %own.1), channel_id=1, source_target_pairs={{0,1},{1,0},{2,3},{3,2},{4,5},{5,4},{6,7},{7,6},{8,9},{9,8},{10,11... | collective-permute-start | bytes 3538952 | tf_op jit(solution)/shard_map/tokens_core/ppermute | solution.py:60
  4.0 1.0 collective-permute-start.6
  5.0 1.1 constant_dynamic-slice_fusion.1
  6.8 0.9 pad_maximum_fusion
  7.7 6.9 %collective-permute-start.7 = (bf16[64,4736]{1,0:T(8,128)(2,1)}, bf16[64,4736]{1,0:T(8,128)(2,1)}, u32[]{:S(2)}, u32[]{:S(2)}) collective-permute-start(bf16[64,4736]{1,0:T(8,128)(2,1)} %pad_maximum_fusion), channel_id=1, source_target_pairs={{0,2},{2,0},{1,3},{3,1},{4,6},{6,4},{5,7},{7,5},{8,10},{10,8},{9,1... | collective-permute-start | bytes 1818632 | tf_op jit(solution)/shard_map/weight_z/ppermute | solution.py:60
  14.6 1.2 %copy-done.5 = bf16[2048,256]{1,0:T(8,128)(2,1)S(1)} copy-done((bf16[2048,256]{1,0:T(8,128)(2,1)S(1)}, bf16[2048,256]{1,0:T(8,128)(2,1)}, u32[]{:S(2)}) %copy-start.5) | copy-done | bytes 1048600
  16.7 1.0 rank_products.1
  17.8 1.3 %copy-done.2 = bf16[128,4608]{1,0:T(8,128)(2,1)S(1)} copy-done((bf16[128,4608]{1,0:T(8,128)(2,1)S(1)}, bf16[128,4608]{1,0:T(8,128)(2,1)}, u32[]{:S(2)}) %copy-start.2) | copy-done | bytes 1179672
  19.1 1.3 %copy-done.4 = bf16[128,4608]{1,0:T(8,128)(2,1)S(1)} copy-done((bf16[128,4608]{1,0:T(8,128)(2,1)S(1)}, bf16[128,4608]{1,0:T(8,128)(2,1)}, u32[]{:S(2)}) %copy-start.4) | copy-done | bytes 1179672
  20.3 0.9 copy-done.9
  21.2 2.0 %token_values.1 = (bf16[128,128]{1,0:T(8,128)(2,1)S(1)}, f32[8,128]{1,0:T(8,128)S(1)}, f32[128,128]{1,0:T(8,128)S(1)}) custom-call(s32[4]{0:T(128)S(1)} %pad_add_fusion.at, bf16[128,4608]{1,0:T(8,128)(2,1)S(1)} %copy-done.2, bf16[128,4608]{1,0:T(8,128)(2,1)S(1)} %copy-done.1, bf16[128,4608]{1,0:T(8,128)(2,1)S(1)} %copy-done.4, bf16[8,4608]{1,0:T(8,128)(2,1)S(1)} %copy-done.9), custom_call_target="tpu_custom_call" | custom-call | flops 452984832 | bytes 7077888 | tf_op jit(solution)/shard_map/token_values/pallas_call | solution.py:257
  24.4 1.4 %collective-permute-start.2 = (bf16[3,128,128]{2,1,0:T(8,128)(2,1)S(1)}, bf16[3,128,128]{2,1,0:T(8,128)(2,1)S(1)}, u32[]{:S(2)}, u32[]{:S(2)}) collective-permute-start(bf16[3,128,128]{2,1,0:T(8,128)(2,1)S(1)} %get-tuple-element.29), channel_id=1, source_target_pairs={{0,8},{4,12},{8,0},{12,4},{1,9},{5,13},{9,1},{13,5},{2,10},{6,14},... | collective-permute-start | bytes 294920 | tf_op jit(solution)/shard_map/act_y/ppermute | solution.py:60
  25.8 2.1 %collective-permute-done.1.first = bf16[3,128,128]{2,1,0:T(8,128)(2,1)S(1)} collective-permute-done((bf16[3,128,128]{2,1,0:T(8,128)(2,1)S(1)}, bf16[3,128,128]{2,1,0:T(8,128)(2,1)S(1)}, u32[]{:S(2)}, u32[]{:S(2)}) %collective-permute-start.1) | collective-permute-done | bytes 98336 | tf_op jit(solution)/shard_map/act_y/ppermute | solution.py:60
  28.7 2.0 %collective-permute-done.2.second = bf16[3,128,128]{2,1,0:T(8,128)(2,1)S(1)} collective-permute-done((bf16[3,128,128]{2,1,0:T(8,128)(2,1)S(1)}, bf16[3,128,128]{2,1,0:T(8,128)(2,1)S(1)}, u32[]{:S(2)}, u32[]{:S(2)}) %collective-permute-start.2) | collective-permute-done | bytes 98336 | tf_op jit(solution)/shard_map/act_y/ppermute | solution.py:60
  30.7 1.9 %collective-permute-done.3.third = bf16[3,128,128]{2,1,0:T(8,128)(2,1)S(1)} collective-permute-done((bf16[3,128,128]{2,1,0:T(8,128)(2,1)S(1)}, bf16[3,128,128]{2,1,0:T(8,128)(2,1)S(1)}, u32[]{:S(2)}, u32[]{:S(2)}) %collective-permute-start.3) | collective-permute-done | bytes 98336 | tf_op jit(solution)/shard_map/act_y/ppermute | solution.py:60
  33.2 7.2 %collective-permute-done.7.refs_1_ = bf16[64,4736]{1,0:T(8,128)(2,1)} collective-permute-done((bf16[64,4736]{1,0:T(8,128)(2,1)}, bf16[64,4736]{1,0:T(8,128)(2,1)}, u32[]{:S(2)}, u32[]{:S(2)}) %collective-permute-start.7) | collective-permute-done | bytes 606240 | tf_op jit(solution)/shard_map/weight_z/ppermute | solution.py:60
  40.4 1.2 %collective-permute-start.17 = (bf16[128,4608]{1,0:T(8,128)(2,1)S(1)}, bf16[128,4608]{1,0:T(8,128)(2,1)S(1)}, u32[]{:S(2)}, u32[]{:S(2)}) collective-permute-start(bf16[128,4608]{1,0:T(8,128)(2,1)S(1)} %get-tuple-element.35.more.one), channel_id=1, source_target_pairs={{0,4},{1,13},{4,8},{5,1},{8,12},{9,5},{12,0},{13,9},{2,6},{3,15},{... | collective-permute-start | bytes 3538952 | tf_op jit(solution)/shard_map/tokens_y/ppermute | solution.py:27
  41.6 2.5 %collective-permute-start.11 = (bf16[64,4736]{1,0:T(8,128)(2,1)}, bf16[64,4736]{1,0:T(8,128)(2,1)S(1)}, u32[]{:S(2)}, u32[]{:S(2)}) collective-permute-start(bf16[64,4736]{1,0:T(8,128)(2,1)} %get-tuple-element.39.refs_0_), channel_id=1, source_target_pairs={{0,64},{1,193},{64,0},{65,129},{128,192},{129,65},{192,128},{193,1... | collective-permute-start | bytes 1818632 | tf_op jit(solution)/shard_map/weight_x/ppermute | solution.py:33
  44.5 1.0 collective-permute-done.9.mixed_s.refs_0_
  45.5 6.1 %collective-permute-start.5 = (bf16[128,128]{1,0:T(8,128)(2,1)S(1)}, bf16[128,128]{1,0:T(8,128)(2,1)S(1)}, u32[]{:S(2)}, u32[]{:S(2)}) collective-permute-start(bf16[128,128]{1,0:T(8,128)(2,1)S(1)} %get-tuple-element.32.refs_2_.tie), channel_id=1, source_target_pairs={{0,2},{2,0},{1,3},{3,1},{4,6},{6,4},{5,7},{7,5},{8,10},{10,8},{9,1... | collective-permute-start | bytes 98312 | tf_op jit(solution)/shard_map/act_z/ppermute | solution.py:60
  51.6 2.0 %own_near.1.tie.near = bf16[2,256,256]{2,1,0:T(8,128)(2,1)S(1)} custom-call(s32[4]{0:T(128)S(1)} %pad_add_fusion.at, bf16[128,4608]{1,0:T(8,128)(2,1)S(1)} %copy-done.1, bf16[128,4608]{1,0:T(8,128)(2,1)S(1)} %collective-permute-done.4.tie.near_s.own_s, bf16[128,4608]{1,0:T(8,128)(2,1)S(1)} %get-tuple-element.35.more.one, ...), custom_call_target="tpu_custom_call" | custom-call | flops 1241513984 | bytes 7274496 | tf_op jit(solution)/shard_map/own_near/pallas_call | solution.py:308
  53.6 1.2 %gate_products.1 = (f32[8,2304]{1,0:T(8,128)S(1)}, f32[8,2304]{1,0:T(8,128)S(1)}) custom-call(s32[4]{0:T(128)S(1)} %pad_add_fusion.at, f32[128,128]{1,0:T(8,128)S(1)} %get-tuple-element.31.keep, bf16[128,128]{1,0:T(8,128)(2,1)S(1)} %collective-permute-done.5.got, f32[128,128]{1,0:T(8,128)S(1)} %get-tuple-element.33.back, ...), custom_call_target="tpu_custom_call" | custom-call | tf_op jit(solution)/shard_map/gate_products/pallas_call | solution.py:320
  55.4 2.0 %collective-permute-done.11.refs_0_ = bf16[64,4736]{1,0:T(8,128)(2,1)S(1)} collective-permute-done((bf16[64,4736]{1,0:T(8,128)(2,1)}, bf16[64,4736]{1,0:T(8,128)(2,1)S(1)}, u32[]{:S(2)}, u32[]{:S(2)}) %collective-permute-start.11) | collective-permute-done | bytes 606240 | tf_op jit(solution)/shard_map/weight_x/ppermute | solution.py:33
  57.5 1.8 %collective-permute-start.21 = (bf16[128,4608]{1,0:T(8,128)(2,1)S(1)}, bf16[128,4608]{1,0:T(8,128)(2,1)S(1)}, u32[]{:S(2)}, u32[]{:S(2)}) collective-permute-start(bf16[128,4608]{1,0:T(8,128)(2,1)S(1)} %fence.6.refs_2_.two.near), channel_id=1, source_target_pairs={{0,1},{1,0},{2,3},{3,2},{4,5},{5,4},{6,7},{7,6},{8,9},{9,8},{10,11... | collective-permute-start | bytes 3538952 | tf_op jit(solution)/shard_map/tokens_core/ppermute | solution.py:60
  59.3 1.4 %collective-permute-start.25 = (bf16[128,4608]{1,0:T(8,128)(2,1)S(1)}, bf16[128,4608]{1,0:T(8,128)(2,1)S(1)}, u32[]{:S(2)}, u32[]{:S(2)}) collective-permute-start(bf16[128,4608]{1,0:T(8,128)(2,1)S(1)} %fence.6.refs_2_.two.near), channel_id=1, source_target_pairs={{0,4},{1,13},{4,8},{5,1},{8,12},{9,5},{12,0},{13,9},{2,6},{3,15},{... | collective-permute-start | bytes 3538952 | tf_op jit(solution)/shard_map/tokens_y/ppermute | solution.py:27
  60.7 2.2 %collective-permute-start.13 = (bf16[8,2304]{1,0:T(8,128)(2,1)S(1)}, bf16[8,2304]{1,0:T(8,128)(2,1)S(1)}, u32[]{:S(2)}, u32[]{:S(2)}) collective-permute-start(bf16[8,2304]{1,0:T(8,128)(2,1)S(1)} %get-tuple-element.41), channel_id=1, source_target_pairs={{0,16},{16,0},{32,48},{48,32},{1,17},{17,1},{33,49},{49,33},{2,18}... | collective-permute-start | bytes 110600 | tf_op jit(solution)/shard_map/gate_zl/ppermute | solution.py:60
  63.6 1.0 collective-permute-done.13.second
  64.6 1.8 %collective-permute-start.15 = (bf16[8,2304]{1,0:T(8,128)(2,1)S(1)}, bf16[8,2304]{1,0:T(8,128)(2,1)S(1)}, u32[]{:S(2)}, u32[]{:S(2)}) collective-permute-start(bf16[8,2304]{1,0:T(8,128)(2,1)S(1)} %get-tuple-element.41), channel_id=1, source_target_pairs={{0,48},{16,32},{32,16},{48,0},{1,49},{17,33},{33,17},{49,1},{2,50}... | collective-permute-start | bytes 110600 | tf_op jit(solution)/shard_map/gate_zl/ppermute | solution.py:60
  67.2 2.1 %collective-permute-done.15.fourth = bf16[8,2304]{1,0:T(8,128)(2,1)S(1)} collective-permute-done((bf16[8,2304]{1,0:T(8,128)(2,1)S(1)}, bf16[8,2304]{1,0:T(8,128)(2,1)S(1)}, u32[]{:S(2)}, u32[]{:S(2)}) %collective-permute-start.15) | collective-permute-done | bytes 36896 | tf_op jit(solution)/shard_map/gate_zl/ppermute | solution.py:60
  70.0 3.4 %far_products.1 = (bf16[3,256,256]{2,1,0:T(8,128)(2,1)S(1)}, bf16[256,4608]{1,0:T(8,128)(2,1)S(1)}, bf16[256,128]{1,0:T(8,128)(2,1)S(1)}) custom-call(s32[4]{0:T(128)S(1)} %pad_add_fusion.at, bf16[128,4608]{1,0:T(8,128)(2,1)S(1)} %copy-done.1, bf16[128,4608]{1,0:T(8,128)(2,1)S(1)} %collective-permute-done.4.tie.near_s.own_s, ...), custom_call_target="tpu_custom_call" | custom-call | flops 1862270976 | bytes 10911744 | tf_op jit(solution)/shard_map/far_products/pallas_call | solution.py:368
  73.3 1.3 %collective-permute-done.25.refs_0_ = bf16[128,4608]{1,0:T(8,128)(2,1)S(1)} collective-permute-done((bf16[128,4608]{1,0:T(8,128)(2,1)S(1)}, bf16[128,4608]{1,0:T(8,128)(2,1)S(1)}, u32[]{:S(2)}, u32[]{:S(2)}) %collective-permute-start.25) | collective-permute-done | bytes 1179680 | tf_op jit(solution)/shard_map/tokens_y/ppermute | solution.py:27
  74.6 2.3 %collective-permute-start.26 = (bf16[128,4608]{1,0:T(8,128)(2,1)S(1)}, bf16[128,4608]{1,0:T(8,128)(2,1)S(1)}, u32[]{:S(2)}, u32[]{:S(2)}) collective-permute-start(bf16[128,4608]{1,0:T(8,128)(2,1)S(1)} %fence.7.more.three), channel_id=1, source_target_pairs={{0,1},{1,0},{2,3},{3,2},{4,5},{5,4},{6,7},{7,6},{8,9},{9,8},{10,11... | collective-permute-start | bytes 3538952 | tf_op jit(solution)/shard_map/tokens_core/ppermute | solution.py:60
  77.0 6.1 %collective-permute-start.28 = (bf16[3,256,256]{2,1,0:T(8,128)(2,1)S(1)}, bf16[3,256,256]{2,1,0:T(8,128)(2,1)S(1)}, u32[]{:S(2)}, u32[]{:S(2)}) collective-permute-start(bf16[3,256,256]{2,1,0:T(8,128)(2,1)S(1)} %get-tuple-element.42.refs_0_.refs_1_.tie), channel_id=1, source_target_pairs={{0,2},{2,0},{1,3},{3,1},{4,6},{6,4},{5,7},{7,5},{8,10},{10,8},{9,1... | collective-permute-start | bytes 1179656 | tf_op jit(solution)/shard_map/out_z/ppermute | solution.py:60
  83.1 3.7 %collective-permute-start.19 = (f32[8,2304]{1,0:T(8,128)S(1)}, f32[8,2304]{1,0:T(8,128)S(1)}, u32[]{:S(2)}, u32[]{:S(2)}) collective-permute-start(f32[8,2304]{1,0:T(8,128)S(1)} %gate_sum.6.refs_4_.first), channel_id=1, source_target_pairs={{0,128},{64,192},{128,0},{192,64},{1,129},{65,193},{129,1},{193,65... | collective-permute-start | bytes 221192 | tf_op jit(solution)/shard_map/gate_x/ppermute | solution.py:60
  86.9 3.5 %collective-permute-done.19.third = f32[8,2304]{1,0:T(8,128)S(1)} collective-permute-done((f32[8,2304]{1,0:T(8,128)S(1)}, f32[8,2304]{1,0:T(8,128)S(1)}, u32[]{:S(2)}, u32[]{:S(2)}) %collective-permute-start.19) | collective-permute-done | bytes 73760 | tf_op jit(solution)/shard_map/gate_x/ppermute | solution.py:60
  90.4 1.5 %collective-permute-done.20.fourth = f32[8,2304]{1,0:T(8,128)S(1)} collective-permute-done((f32[8,2304]{1,0:T(8,128)S(1)}, f32[8,2304]{1,0:T(8,128)S(1)}, u32[]{:S(2)}, u32[]{:S(2)}) %collective-permute-start.20) | collective-permute-done | bytes 73760 | tf_op jit(solution)/shard_map/gate_x/ppermute | solution.py:60
  92.1 1.5 %collective-permute-start.23 = (f32[8,2304]{1,0:T(8,128)S(1)}, f32[8,2304]{1,0:T(8,128)S(1)}, u32[]{:S(2)}, u32[]{:S(2)}) collective-permute-start(f32[8,2304]{1,0:T(8,128)S(1)} %gate_sum.7.first), channel_id=1, source_target_pairs={{0,8},{4,12},{8,0},{12,4},{1,9},{5,13},{9,1},{13,5},{2,10},{6,14},... | collective-permute-start | bytes 221192 | tf_op jit(solution)/shard_map/gate_y/ppermute | solution.py:60
  93.6 2.3 %collective-permute-start.24 = (f32[8,2304]{1,0:T(8,128)S(1)}, f32[8,2304]{1,0:T(8,128)S(1)}, u32[]{:S(2)}, u32[]{:S(2)}) collective-permute-start(f32[8,2304]{1,0:T(8,128)S(1)} %gate_sum.7.first), channel_id=1, source_target_pairs={{0,12},{4,8},{8,4},{12,0},{1,13},{5,9},{9,5},{13,1},{2,14},{6,10},... | collective-permute-start | bytes 221192 | tf_op jit(solution)/shard_map/gate_y/ppermute | solution.py:60
  95.9 2.0 %own_rest.1.refs_0_.rest = bf16[2,256,256]{2,1,0:T(8,128)(2,1)S(1)} custom-call(s32[4]{0:T(128)S(1)} %pad_add_fusion.at, bf16[128,4608]{1,0:T(8,128)(2,1)S(1)} %fence.6.refs_2_.two.near, bf16[128,4608]{1,0:T(8,128)(2,1)S(1)} %collective-permute-done.21.two_s.near_s, bf16[128,4608]{1,0:T(8,128)(2,1)S(1)} %fence.7.more.three, ...), custom_call_target="tpu_custom_call" | custom-call | flops 1241513984 | bytes 7274496 | tf_op jit(solution)/shard_map/own_rest/pallas_call | solution.py:308
  97.9 1.0 collective-permute-done.24.fourth
  99.5 1.3 %far_products_last.1.refs_0_ = bf16[256,256]{1,0:T(8,128)(2,1)S(1)} custom-call(s32[4]{0:T(128)S(1)} %pad_add_fusion.at, bf16[128,4608]{1,0:T(8,128)(2,1)S(1)} %fence.7.more.three, bf16[128,4608]{1,0:T(8,128)(2,1)S(1)} %collective-permute-done.26.more_s.three_s, bf16[4,128,128]{2,1,0:T(8,128)(2,1)S(1)} %get-tuple-element.36.mixed, ...), custom_call_target="tpu_custom_call" | custom-call | flops 620756992 | bytes 3637248 | tf_op jit(solution)/shard_map/far_products_last/pallas_call | solution.py:393
  100.9 5.0 %collective-permute-start.30 = (bf16[256,256]{1,0:T(8,128)(2,1)S(1)}, bf16[256,256]{1,0:T(8,128)(2,1)S(1)}, u32[]{:S(2)}, u32[]{:S(2)}) collective-permute-start(bf16[256,256]{1,0:T(8,128)(2,1)S(1)} %far_products_last.1.refs_0_), channel_id=1, source_target_pairs={{0,2},{2,0},{1,3},{3,1},{4,6},{6,4},{5,7},{7,5},{8,10},{10,8},{9,1... | collective-permute-start | bytes 393224 | tf_op jit(solution)/shard_map/out_z_last/ppermute | solution.py:60
  105.8 0.9 collective-permute-done.27.right
  107.3 4.3 %collective-permute-start.29 = (f32[8,2304]{1,0:T(8,128)S(1)}, f32[8,2304]{1,0:T(8,128)S(1)}, u32[]{:S(2)}, u32[]{:S(2)}) collective-permute-start(f32[8,2304]{1,0:T(8,128)S(1)} %get-tuple-element.45.mine), channel_id=1, source_target_pairs={{0,1},{1,0},{2,3},{3,2},{4,5},{5,4},{6,7},{7,6},{8,9},{9,8},{10,11... | collective-permute-start | bytes 221192 | tf_op jit(solution)/shard_map/gate_core_back/ppermute | solution.py:60
  111.6 0.9 collective-permute-done.29.other
  112.5 1.2 %gate_halves.1.tie = f32[8,4608]{1,0:T(8,128)} custom-call(s32[4]{0:T(128)S(1)} %pad_add_fusion.at, f32[8,2304]{1,0:T(8,128)S(1)} %get-tuple-element.45.mine, f32[8,2304]{1,0:T(8,128)S(1)} %collective-permute-done.29.other), custom_call_target="tpu_custom_call" | custom-call | tf_op jit(solution)/shard_map/gate_halves/pallas_call | solution.py:410
  113.7 0.9 copy-done.8
  114.7 1.6 %place.1 = bf16[4,2,2,128,256]{4,3,2,1,0:T(8,128)(2,1)} custom-call(s32[4]{0:T(128)S(1)} %pad_add_fusion.at, bf16[2,256,256]{2,1,0:T(8,128)(2,1)S(1)} %own_near.1.tie.near, bf16[2,256,256]{2,1,0:T(8,128)(2,1)S(1)} %own_rest.1.refs_0_.rest, bf16[3,256,256]{2,1,0:T(8,128)(2,1)S(1)} %collective-permute-done.28.refs_1_.got, ...), custom_call_target="tpu_custom_call" | custom-call | tf_op jit(solution)/shard_map/place/pallas_call | solution.py:419
  (58 shorter events, 9.0 us)
Async XLA Ops:
  0.6 32.0 %collective-permute-start.4 = (bf16[128,4608]{1,0:T(8,128)(2,1)}, bf16[128,4608]{1,0:T(8,128)(2,1)S(1)}, u32[]{:S(2)}, u32[]{:S(2)}) collective-permute-start(bf16[128,4608]{1,0:T(8,128)(2,1)} %own.1), channel_id=1, source_target_pairs={{0,1},{1,0},{2,3},{3,2},{4,5},{5,4},{6,7},{7,6},{8,9},{9,8},{10,11... | collective-permute-start | bytes 3538952 | tf_op jit(solution)/shard_map/tokens_core/ppermute | solution.py:60
  4.0 36.5 %collective-permute-start.6 = (bf16[128,4608]{1,0:T(8,128)(2,1)}, bf16[128,4608]{1,0:T(8,128)(2,1)S(1)}, u32[]{:S(2)}, u32[]{:S(2)}) collective-permute-start(bf16[128,4608]{1,0:T(8,128)(2,1)} %own.1), channel_id=1, source_target_pairs={{0,4},{1,13},{4,8},{5,1},{8,12},{9,5},{12,0},{13,9},{2,6},{3,15},{... | collective-permute-start | bytes 3538952 | tf_op jit(solution)/shard_map/tokens_y/ppermute | solution.py:27
  6.8 11.0 %copy-start.1 = (bf16[128,4608]{1,0:T(8,128)(2,1)S(1)}, bf16[128,4608]{1,0:T(8,128)(2,1)}, u32[]{:S(2)}) copy-start(bf16[128,4608]{1,0:T(8,128)(2,1)} %own.1) | copy-start | bytes 3538948
  7.7 32.8 %collective-permute-start.7 = (bf16[64,4736]{1,0:T(8,128)(2,1)}, bf16[64,4736]{1,0:T(8,128)(2,1)}, u32[]{:S(2)}, u32[]{:S(2)}) collective-permute-start(bf16[64,4736]{1,0:T(8,128)(2,1)} %pad_maximum_fusion), channel_id=1, source_target_pairs={{0,2},{2,0},{1,3},{3,1},{4,6},{6,4},{5,7},{7,5},{8,10},{10,8},{9,1... | collective-permute-start | bytes 1818632 | tf_op jit(solution)/shard_map/weight_z/ppermute | solution.py:60
  14.6 1.2 %copy-start.5 = (bf16[2048,256]{1,0:T(8,128)(2,1)S(1)}, bf16[2048,256]{1,0:T(8,128)(2,1)}, u32[]{:S(2)}) copy-start(bf16[2048,256]{1,0:T(8,128)(2,1)} %param.9) | copy-start | bytes 3145732
  15.9 0.8 copy-start.6
  17.7 5.5 %collective-permute-start = (bf16[4,2,128,128]{3,2,1,0:T(8,128)(2,1)S(1)}, bf16[4,2,128,128]{3,2,1,0:T(8,128)(2,1)S(1)}, u32[]{:S(2)}, u32[]{:S(2)}) collective-permute-start(bf16[4,2,128,128]{3,2,1,0:T(8,128)(2,1)S(1)} %get-tuple-element.25), channel_id=1, source_target_pairs={{0,1},{1,0},{2,3},{3,2},{4,5},{5,4},{6,7},{7,6},{8,9},{9,8},{10,11... | collective-permute-start | bytes 786440 | tf_op jit(solution)/shard_map/act_core/ppermute | solution.py:60
  17.8 1.3 %copy-start.2 = (bf16[128,4608]{1,0:T(8,128)(2,1)S(1)}, bf16[128,4608]{1,0:T(8,128)(2,1)}, u32[]{:S(2)}) copy-start(bf16[128,4608]{1,0:T(8,128)(2,1)} %hidden.3) | copy-start | bytes 3538948
  19.1 1.3 %copy-start.4 = (bf16[128,4608]{1,0:T(8,128)(2,1)S(1)}, bf16[128,4608]{1,0:T(8,128)(2,1)}, u32[]{:S(2)}) copy-start(bf16[128,4608]{1,0:T(8,128)(2,1)} %up.1) | copy-start | bytes 3538948
  20.3 0.9 copy-start.9
  23.8 4.1 %collective-permute-start.1 = (bf16[3,128,128]{2,1,0:T(8,128)(2,1)S(1)}, bf16[3,128,128]{2,1,0:T(8,128)(2,1)S(1)}, u32[]{:S(2)}, u32[]{:S(2)}) collective-permute-start(bf16[3,128,128]{2,1,0:T(8,128)(2,1)S(1)} %get-tuple-element.28), channel_id=1, source_target_pairs={{0,4},{4,0},{8,12},{12,8},{1,5},{5,1},{9,13},{13,9},{2,6},{6,2},{1... | collective-permute-start | bytes 294920 | tf_op jit(solution)/shard_map/act_y/ppermute | solution.py:60
  24.4 6.3 %collective-permute-start.2 = (bf16[3,128,128]{2,1,0:T(8,128)(2,1)S(1)}, bf16[3,128,128]{2,1,0:T(8,128)(2,1)S(1)}, u32[]{:S(2)}, u32[]{:S(2)}) collective-permute-start(bf16[3,128,128]{2,1,0:T(8,128)(2,1)S(1)} %get-tuple-element.29), channel_id=1, source_target_pairs={{0,8},{4,12},{8,0},{12,4},{1,9},{5,13},{9,1},{13,5},{2,10},{6,14},... | collective-permute-start | bytes 294920 | tf_op jit(solution)/shard_map/act_y/ppermute | solution.py:60
  27.9 4.7 %collective-permute-start.3 = (bf16[3,128,128]{2,1,0:T(8,128)(2,1)S(1)}, bf16[3,128,128]{2,1,0:T(8,128)(2,1)S(1)}, u32[]{:S(2)}, u32[]{:S(2)}) collective-permute-start(bf16[3,128,128]{2,1,0:T(8,128)(2,1)S(1)} %get-tuple-element.30), channel_id=1, source_target_pairs={{0,12},{4,8},{8,4},{12,0},{1,13},{5,9},{9,5},{13,1},{2,14},{6,10},... | collective-permute-start | bytes 294920 | tf_op jit(solution)/shard_map/act_y/ppermute | solution.py:60
  32.6 19.0 %copy-start = (bf16[256,4608]{1,0:T(8,128)(2,1)S(1)}, bf16[256,4608]{1,0:T(8,128)(2,1)}, u32[]{:S(2)}) copy-start(bf16[256,4608]{1,0:T(8,128)(2,1)} %weight.3) | copy-start | bytes 7077892
  33.2 18.4 %copy-start.7 = (bf16[256,128]{1,0:T(8,128)(2,1)S(1)}, bf16[256,128]{1,0:T(8,128)(2,1)}, u32[]{:S(2)}) copy-start(bf16[256,128]{1,0:T(8,128)(2,1)} %down.5) | copy-start | bytes 196612
  40.4 11.2 %collective-permute-start.8 = (bf16[128,4608]{1,0:T(8,128)(2,1)S(1)}, bf16[128,4608]{1,0:T(8,128)(2,1)S(1)}, u32[]{:S(2)}, u32[]{:S(2)}) collective-permute-start(bf16[128,4608]{1,0:T(8,128)(2,1)S(1)} %get-tuple-element.35.more.one), channel_id=1, source_target_pairs={{0,1},{1,0},{2,3},{3,2},{4,5},{5,4},{6,7},{7,6},{8,9},{9,8},{10,11... | collective-permute-start | bytes 3538952 | tf_op jit(solution)/shard_map/tokens_core/ppermute | solution.py:60
  40.4 17.0 %collective-permute-start.17 = (bf16[128,4608]{1,0:T(8,128)(2,1)S(1)}, bf16[128,4608]{1,0:T(8,128)(2,1)S(1)}, u32[]{:S(2)}, u32[]{:S(2)}) collective-permute-start(bf16[128,4608]{1,0:T(8,128)(2,1)S(1)} %get-tuple-element.35.more.one), channel_id=1, source_target_pairs={{0,4},{1,13},{4,8},{5,1},{8,12},{9,5},{12,0},{13,9},{2,6},{3,15},{... | collective-permute-start | bytes 3538952 | tf_op jit(solution)/shard_map/tokens_y/ppermute | solution.py:27
  41.6 15.8 %collective-permute-start.11 = (bf16[64,4736]{1,0:T(8,128)(2,1)}, bf16[64,4736]{1,0:T(8,128)(2,1)S(1)}, u32[]{:S(2)}, u32[]{:S(2)}) collective-permute-start(bf16[64,4736]{1,0:T(8,128)(2,1)} %get-tuple-element.39.refs_0_), channel_id=1, source_target_pairs={{0,64},{1,193},{64,0},{65,129},{128,192},{129,65},{192,128},{193,1... | collective-permute-start | bytes 1818632 | tf_op jit(solution)/shard_map/weight_x/ppermute | solution.py:33
  44.1 13.3 %collective-permute-start.12 = (bf16[64,4736]{1,0:T(8,128)(2,1)}, bf16[64,4736]{1,0:T(8,128)(2,1)S(1)}, u32[]{:S(2)}, u32[]{:S(2)}) collective-permute-start(bf16[64,4736]{1,0:T(8,128)(2,1)} %get-tuple-element.39.refs_0_), channel_id=1, source_target_pairs={{0,192},{1,65},{64,128},{65,1},{128,64},{129,193},{192,0},{193,129... | collective-permute-start | bytes 1818632 | tf_op jit(solution)/shard_map/weight_x/ppermute | solution.py:33
  44.1 9.5 %copy-start.3 = (bf16[128,4608]{1,0:T(8,128)(2,1)S(1)}, bf16[128,4608]{1,0:T(8,128)(2,1)}, u32[]{:S(2)}) copy-start(bf16[128,4608]{1,0:T(8,128)(2,1)} %hidden.3) | copy-start | bytes 3538948
  44.1 1.4 %collective-permute-start.9 = (bf16[4,128,128]{2,1,0:T(8,128)(2,1)S(1)}, bf16[4,128,128]{2,1,0:T(8,128)(2,1)S(1)}, u32[]{:S(2)}, u32[]{:S(2)}) collective-permute-start(bf16[4,128,128]{2,1,0:T(8,128)(2,1)S(1)} %get-tuple-element.36.mixed), channel_id=1, source_target_pairs={{0,1},{1,0},{2,3},{3,2},{4,5},{5,4},{6,7},{7,6},{8,9},{9,8},{10,11... | collective-permute-start | bytes 393224 | tf_op jit(solution)/shard_map/mixed_core/ppermute | solution.py:60
  45.5 8.1 %collective-permute-start.5 = (bf16[128,128]{1,0:T(8,128)(2,1)S(1)}, bf16[128,128]{1,0:T(8,128)(2,1)S(1)}, u32[]{:S(2)}, u32[]{:S(2)}) collective-permute-start(bf16[128,128]{1,0:T(8,128)(2,1)S(1)} %get-tuple-element.32.refs_2_.tie), channel_id=1, source_target_pairs={{0,2},{2,0},{1,3},{3,1},{4,6},{6,4},{5,7},{7,5},{8,10},{10,8},{9,1... | collective-permute-start | bytes 98312 | tf_op jit(solution)/shard_map/act_z/ppermute | solution.py:60
  54.8 2.6 %collective-permute-start.10 = (f32[8,2304]{1,0:T(8,128)S(1)}, f32[8,2304]{1,0:T(8,128)S(1)}, u32[]{:S(2)}, u32[]{:S(2)}) collective-permute-start(f32[8,2304]{1,0:T(8,128)S(1)} %get-tuple-element.38), channel_id=1, source_target_pairs={{0,1},{1,0},{2,3},{3,2},{4,5},{5,4},{6,7},{7,6},{8,9},{9,8},{10,11... | collective-permute-start | bytes 221192 | tf_op jit(solution)/shard_map/gate_core/ppermute | solution.py:60
  57.5 12.5 %collective-permute-start.21 = (bf16[128,4608]{1,0:T(8,128)(2,1)S(1)}, bf16[128,4608]{1,0:T(8,128)(2,1)S(1)}, u32[]{:S(2)}, u32[]{:S(2)}) collective-permute-start(bf16[128,4608]{1,0:T(8,128)(2,1)S(1)} %fence.6.refs_2_.two.near), channel_id=1, source_target_pairs={{0,1},{1,0},{2,3},{3,2},{4,5},{5,4},{6,7},{7,6},{8,9},{9,8},{10,11... | collective-permute-start | bytes 3538952 | tf_op jit(solution)/shard_map/tokens_core/ppermute | solution.py:60
  59.3 15.3 %collective-permute-start.25 = (bf16[128,4608]{1,0:T(8,128)(2,1)S(1)}, bf16[128,4608]{1,0:T(8,128)(2,1)S(1)}, u32[]{:S(2)}, u32[]{:S(2)}) collective-permute-start(bf16[128,4608]{1,0:T(8,128)(2,1)S(1)} %fence.6.refs_2_.two.near), channel_id=1, source_target_pairs={{0,4},{1,13},{4,8},{5,1},{8,12},{9,5},{12,0},{13,9},{2,6},{3,15},{... | collective-permute-start | bytes 3538952 | tf_op jit(solution)/shard_map/tokens_y/ppermute | solution.py:27
  60.7 9.2 %collective-permute-start.16 = (bf16[64,4736]{1,0:T(8,128)(2,1)S(1)}, bf16[64,4736]{1,0:T(8,128)(2,1)S(1)}, u32[]{:S(2)}, u32[]{:S(2)}) collective-permute-start(bf16[64,4736]{1,0:T(8,128)(2,1)S(1)} %fence.5.refs_1_), channel_id=1, source_target_pairs={{0,192},{1,65},{64,128},{65,1},{128,64},{129,193},{192,0},{193,129... | collective-permute-start | bytes 1818632 | tf_op jit(solution)/shard_map/weight_x_far/ppermute | solution.py:33
  60.7 3.9 %collective-permute-start.13 = (bf16[8,2304]{1,0:T(8,128)(2,1)S(1)}, bf16[8,2304]{1,0:T(8,128)(2,1)S(1)}, u32[]{:S(2)}, u32[]{:S(2)}) collective-permute-start(bf16[8,2304]{1,0:T(8,128)(2,1)S(1)} %get-tuple-element.41), channel_id=1, source_target_pairs={{0,16},{16,0},{32,48},{48,32},{1,17},{17,1},{33,49},{49,33},{2,18}... | collective-permute-start | bytes 110600 | tf_op jit(solution)/shard_map/gate_zl/ppermute | solution.py:60
  63.0 4.3 %collective-permute-start.14 = (bf16[8,2304]{1,0:T(8,128)(2,1)S(1)}, bf16[8,2304]{1,0:T(8,128)(2,1)S(1)}, u32[]{:S(2)}, u32[]{:S(2)}) collective-permute-start(bf16[8,2304]{1,0:T(8,128)(2,1)S(1)} %get-tuple-element.41), channel_id=1, source_target_pairs={{0,32},{16,48},{32,0},{48,16},{1,33},{17,49},{33,1},{49,17},{2,34}... | collective-permute-start | bytes 110600 | tf_op jit(solution)/shard_map/gate_zl/ppermute | solution.py:60
  64.6 4.7 %collective-permute-start.15 = (bf16[8,2304]{1,0:T(8,128)(2,1)S(1)}, bf16[8,2304]{1,0:T(8,128)(2,1)S(1)}, u32[]{:S(2)}, u32[]{:S(2)}) collective-permute-start(bf16[8,2304]{1,0:T(8,128)(2,1)S(1)} %get-tuple-element.41), channel_id=1, source_target_pairs={{0,48},{16,32},{32,16},{48,0},{1,49},{17,33},{33,17},{49,1},{2,50}... | collective-permute-start | bytes 110600 | tf_op jit(solution)/shard_map/gate_zl/ppermute | solution.py:60
  74.6 21.3 %collective-permute-start.26 = (bf16[128,4608]{1,0:T(8,128)(2,1)S(1)}, bf16[128,4608]{1,0:T(8,128)(2,1)S(1)}, u32[]{:S(2)}, u32[]{:S(2)}) collective-permute-start(bf16[128,4608]{1,0:T(8,128)(2,1)S(1)} %fence.7.more.three), channel_id=1, source_target_pairs={{0,1},{1,0},{2,3},{3,2},{4,5},{5,4},{6,7},{7,6},{8,9},{9,8},{10,11... | collective-permute-start | bytes 3538952 | tf_op jit(solution)/shard_map/tokens_core/ppermute | solution.py:60
  77.0 28.9 %collective-permute-start.28 = (bf16[3,256,256]{2,1,0:T(8,128)(2,1)S(1)}, bf16[3,256,256]{2,1,0:T(8,128)(2,1)S(1)}, u32[]{:S(2)}, u32[]{:S(2)}) collective-permute-start(bf16[3,256,256]{2,1,0:T(8,128)(2,1)S(1)} %get-tuple-element.42.refs_0_.refs_1_.tie), channel_id=1, source_target_pairs={{0,2},{2,0},{1,3},{3,1},{4,6},{6,4},{5,7},{7,5},{8,10},{10,8},{9,1... | collective-permute-start | bytes 1179656 | tf_op jit(solution)/shard_map/out_z/ppermute | solution.py:60
  83.1 3.9 %collective-permute-start.18 = (f32[8,2304]{1,0:T(8,128)S(1)}, f32[8,2304]{1,0:T(8,128)S(1)}, u32[]{:S(2)}, u32[]{:S(2)}) collective-permute-start(f32[8,2304]{1,0:T(8,128)S(1)} %gate_sum.6.refs_4_.first), channel_id=1, source_target_pairs={{0,64},{64,0},{128,192},{192,128},{1,65},{65,1},{129,193},{193,129... | collective-permute-start | bytes 221192 | tf_op jit(solution)/shard_map/gate_x/ppermute | solution.py:60
  83.1 7.4 %collective-permute-start.19 = (f32[8,2304]{1,0:T(8,128)S(1)}, f32[8,2304]{1,0:T(8,128)S(1)}, u32[]{:S(2)}, u32[]{:S(2)}) collective-permute-start(f32[8,2304]{1,0:T(8,128)S(1)} %gate_sum.6.refs_4_.first), channel_id=1, source_target_pairs={{0,128},{64,192},{128,0},{192,64},{1,129},{65,193},{129,1},{193,65... | collective-permute-start | bytes 221192 | tf_op jit(solution)/shard_map/gate_x/ppermute | solution.py:60
  86.7 5.2 %collective-permute-start.20 = (f32[8,2304]{1,0:T(8,128)S(1)}, f32[8,2304]{1,0:T(8,128)S(1)}, u32[]{:S(2)}, u32[]{:S(2)}) collective-permute-start(f32[8,2304]{1,0:T(8,128)S(1)} %gate_sum.6.refs_4_.first), channel_id=1, source_target_pairs={{0,192},{64,128},{128,64},{192,0},{1,193},{65,129},{129,65},{193,1... | collective-permute-start | bytes 221192 | tf_op jit(solution)/shard_map/gate_x/ppermute | solution.py:60
  92.0 5.9 %collective-permute-start.22 = (f32[8,2304]{1,0:T(8,128)S(1)}, f32[8,2304]{1,0:T(8,128)S(1)}, u32[]{:S(2)}, u32[]{:S(2)}) collective-permute-start(f32[8,2304]{1,0:T(8,128)S(1)} %gate_sum.7.first), channel_id=1, source_target_pairs={{0,4},{4,0},{8,12},{12,8},{1,5},{5,1},{9,13},{13,9},{2,6},{6,2},{1... | collective-permute-start | bytes 221192 | tf_op jit(solution)/shard_map/gate_y/ppermute | solution.py:60
  92.1 5.9 %collective-permute-start.23 = (f32[8,2304]{1,0:T(8,128)S(1)}, f32[8,2304]{1,0:T(8,128)S(1)}, u32[]{:S(2)}, u32[]{:S(2)}) collective-permute-start(f32[8,2304]{1,0:T(8,128)S(1)} %gate_sum.7.first), channel_id=1, source_target_pairs={{0,8},{4,12},{8,0},{12,4},{1,9},{5,13},{9,1},{13,5},{2,10},{6,14},... | collective-permute-start | bytes 221192 | tf_op jit(solution)/shard_map/gate_y/ppermute | solution.py:60
  93.6 5.3 %collective-permute-start.24 = (f32[8,2304]{1,0:T(8,128)S(1)}, f32[8,2304]{1,0:T(8,128)S(1)}, u32[]{:S(2)}, u32[]{:S(2)}) collective-permute-start(f32[8,2304]{1,0:T(8,128)S(1)} %gate_sum.7.first), channel_id=1, source_target_pairs={{0,12},{4,8},{8,4},{12,0},{1,13},{5,9},{9,5},{13,1},{2,14},{6,10},... | collective-permute-start | bytes 221192 | tf_op jit(solution)/shard_map/gate_y/ppermute | solution.py:60
  98.9 7.8 %collective-permute-start.27 = (f32[8,2304]{1,0:T(8,128)S(1)}, f32[8,2304]{1,0:T(8,128)S(1)}, u32[]{:S(2)}, u32[]{:S(2)}) collective-permute-start(f32[8,2304]{1,0:T(8,128)S(1)} %gate_sum.8.tie.left), channel_id=1, source_target_pairs={{0,2},{2,0},{1,3},{3,1},{4,6},{6,4},{5,7},{7,5},{8,10},{10,8},{9,1... | collective-permute-start | bytes 221192 | tf_op jit(solution)/shard_map/gate_zh/ppermute | solution.py:60
  100.9 12.9 %collective-permute-start.30 = (bf16[256,256]{1,0:T(8,128)(2,1)S(1)}, bf16[256,256]{1,0:T(8,128)(2,1)S(1)}, u32[]{:S(2)}, u32[]{:S(2)}) collective-permute-start(bf16[256,256]{1,0:T(8,128)(2,1)S(1)} %far_products_last.1.refs_0_), channel_id=1, source_target_pairs={{0,2},{2,0},{1,3},{3,1},{4,6},{6,4},{5,7},{7,5},{8,10},{10,8},{9,1... | collective-permute-start | bytes 393224 | tf_op jit(solution)/shard_map/out_z_last/ppermute | solution.py:60
  107.3 5.2 %collective-permute-start.29 = (f32[8,2304]{1,0:T(8,128)S(1)}, f32[8,2304]{1,0:T(8,128)S(1)}, u32[]{:S(2)}, u32[]{:S(2)}) collective-permute-start(f32[8,2304]{1,0:T(8,128)S(1)} %get-tuple-element.45.mine), channel_id=1, source_target_pairs={{0,1},{1,0},{2,3},{3,2},{4,5},{5,4},{6,7},{7,6},{8,9},{9,8},{10,11... | collective-permute-start | bytes 221192 | tf_op jit(solution)/shard_map/gate_core_back/ppermute | solution.py:60
  113.7 0.9 copy-start.8

commit v15 on v14

--- a/solution.py
+++ b/solution.py
@@ -145,7 +145,7 @@
 
 
 def add_kernel(left, right, *refs):
-    total = left[...] + right[...]
+    total = left[...].astype(right.dtype).astype(F32) + right[...].astype(F32)
     refs[-2][...] = total
     refs[-1][...] = total.astype(refs[-1].dtype)
 
@@ -159,9 +159,9 @@
 
 def add4_kernel(first, second, third, fourth, *refs):
     own = first[...].astype(second.dtype).astype(F32)
-    refs[-1][...] = (own + second[...].astype(F32)) + (
-        third[...].astype(F32) + fourth[...].astype(F32)
-    )
+    total = (own + second[...].astype(F32)) + (third[...].astype(F32) + fourth[...].astype(F32))
+    refs[-2][...] = total
+    refs[-1][...] = total.astype(refs[-1].dtype)
 
 
 def rows_product(at, steps, refs, mixed, weights, downs, out):
@@ -340,8 +340,8 @@
         return pl.pallas_call(
             add4_kernel,
             in_specs=[VMEM] * 4 + [ANY] * (len(parts) - 4),
-            out_specs=VMEM,
-            out_shape=shaped(parts[0].shape, F32),
+            out_specs=[VMEM, VMEM],
+            out_shape=[shaped(parts[0].shape, F32), shaped(parts[0].shape, BF16)],
             compiler_params=SMALL,
         name="gate_sum",
         )(*parts)
@@ -361,7 +361,7 @@
     (two,) = fence((two,), w_first)
     with jax.named_scope("tokens_y"):
         three = ring(two, "y")
-    total = step(total, "zl", mixed_s, w_far, two, message=message)
+    total, _ = step(total, "zl", mixed_s, w_far, two, message=message)
     with jax.named_scope("tokens_core"):
         two_s = swap(two, "c", 1)
 
@@ -386,10 +386,10 @@
     (three,) = fence((three,), far)
     with jax.named_scope("tokens_core"):
         three_s = swap(three, "c", 1)
-    total = step(total, "x", far)
+    total, _ = step(total, "x", far)
 
     own_rest = products("own_rest", 2, two, two_s, three, three_s, weight, down, far)
-    total = step(total, "y", own_rest)
+    total, message = step(total, "y", own_rest)
     last = pl.pallas_call(
         far_last_kernel,
         in_specs=[SMEM] + [VMEM] * 6 + [ANY],
@@ -403,7 +403,7 @@
         last_got = swap(last, "zh", 1)
 
     with jax.named_scope("gate_zh"):
-        got = swap(total, "zh", 1)
+        got = swap(message, "zh", 1)
     total, _ = add(total, got, last, far_got)
     with jax.named_scope("gate_core_back"):
         other = swap(total, "c", 1)

time: 117 us -> 121 us (1.034)
  waiting for transfers between devices: 29.8 us -> 32.5 us
    ppermute x25, waiting for transfers between devices: 25.8 us -> 29.2 us  [swap(): return lax.ppermute(value, axis, [(i, i ^ mask) for i in range(size)])]
    pallas_call x3, Pallas kernels: 0.07 us -> 1.3 us  [add4(): pl.pallas_call(add4_kernel, in_specs=[VMEM] * 4 + [ANY] * (len(parts) - 4...]
where the time goes in v15:
time: 121 us
  starting transfers between devices  59 us (49%)
  waiting for transfers between devices  32.5 us (27%)
  Pallas kernels  18.8 us (16%)
  local copies, waits for them, and re-layouts  8.24 us (7%)
    ppermute x25, starting transfers between devices, swap(): return lax.ppermute(value, axis, [(i, i ^ mask) for i in range(size)])  52.9 us
    ppermute x25, waiting for transfers between devices, swap(): return lax.ppermute(value, axis, [(i, i ^ mask) for i in range(size)])  29.2 us
    unnamed x20, local copies, waits for them, and re-layouts  6.41 us
    pallas_call x2, Pallas kernels, products(): pl.pallas_call(functools.partial(product_kernel, first), in_specs=[SMEM]...  3.97 us
    ppermute x3, starting transfers between devices, ring(): return lax.ppermute(value, (axis, 'c'), pairs)  3.62 us
    pallas_call x1, Pallas kernels, on_device(): pl.pallas_call(far_kernel, in_specs=[SMEM] + [VMEM] * 12 + [ANY], out_spe...  3.35 us
    ppermute x3, waiting for transfers between devices, pairs(): lax.ppermute(value, (axis, 'c'), [(2 * i + c, 2 * partner(i, c) + c) for...  2.66 us
    ppermute x3, starting transfers between devices, pairs(): lax.ppermute(value, (axis, 'c'), [(2 * i + c, 2 * partner(i, c) + c) for...  2.52 us
  transfers between devices with their start and end apart: 31, of which 16 were waited for; matrix products, arithmetic and copies ran while one was open for 2% of the time, Pallas kernels for 14%

profile of v15, /device:TPU:1, one launch (start us, length us, event | category | flops | bytes accessed | tf_op | source)
XLA Modules:
  0.0 120.6 jit_solution(16424047295429015674)
XLA Ops:
  0.6 3.3 %collective-permute-start.4 = (bf16[128,4608]{1,0:T(8,128)(2,1)}, bf16[128,4608]{1,0:T(8,128)(2,1)S(1)}, u32[]{:S(2)}, u32[]{:S(2)}) collective-permute-start(bf16[128,4608]{1,0:T(8,128)(2,1)} %own.1), channel_id=1, source_target_pairs={{0,1},{1,0},{2,3},{3,2},{4,5},{5,4},{6,7},{7,6},{8,9},{9,8},{10,11... | collective-permute-start | bytes 3538952 | tf_op jit(solution)/shard_map/tokens_core/ppermute | solution.py:60
  4.0 1.0 collective-permute-start.6
  5.0 1.1 constant_dynamic-slice_fusion.1
  6.8 0.9 pad_maximum_fusion
  7.7 6.9 %collective-permute-start.7 = (bf16[64,4736]{1,0:T(8,128)(2,1)}, bf16[64,4736]{1,0:T(8,128)(2,1)}, u32[]{:S(2)}, u32[]{:S(2)}) collective-permute-start(bf16[64,4736]{1,0:T(8,128)(2,1)} %pad_maximum_fusion), channel_id=1, source_target_pairs={{0,2},{2,0},{1,3},{3,1},{4,6},{6,4},{5,7},{7,5},{8,10},{10,8},{9,1... | collective-permute-start | bytes 1818632 | tf_op jit(solution)/shard_map/weight_z/ppermute | solution.py:60
  14.6 1.2 %copy-done.5 = bf16[2048,256]{1,0:T(8,128)(2,1)S(1)} copy-done((bf16[2048,256]{1,0:T(8,128)(2,1)S(1)}, bf16[2048,256]{1,0:T(8,128)(2,1)}, u32[]{:S(2)}) %copy-start.5) | copy-done | bytes 1048600
  15.9 0.8 copy-done.6
  16.7 1.0 rank_products.1
  17.8 1.3 %copy-done.2 = bf16[128,4608]{1,0:T(8,128)(2,1)S(1)} copy-done((bf16[128,4608]{1,0:T(8,128)(2,1)S(1)}, bf16[128,4608]{1,0:T(8,128)(2,1)}, u32[]{:S(2)}) %copy-start.2) | copy-done | bytes 1179672
  19.1 1.3 %copy-done.4 = bf16[128,4608]{1,0:T(8,128)(2,1)S(1)} copy-done((bf16[128,4608]{1,0:T(8,128)(2,1)S(1)}, bf16[128,4608]{1,0:T(8,128)(2,1)}, u32[]{:S(2)}) %copy-start.4) | copy-done | bytes 1179672
  20.3 0.9 copy-done.9
  21.2 2.0 %token_values.1 = (bf16[128,128]{1,0:T(8,128)(2,1)S(1)}, f32[8,128]{1,0:T(8,128)S(1)}, f32[128,128]{1,0:T(8,128)S(1)}) custom-call(s32[4]{0:T(128)S(1)} %pad_add_fusion.at, bf16[128,4608]{1,0:T(8,128)(2,1)S(1)} %copy-done.2, bf16[128,4608]{1,0:T(8,128)(2,1)S(1)} %copy-done.1, bf16[128,4608]{1,0:T(8,128)(2,1)S(1)} %copy-done.4, bf16[8,4608]{1,0:T(8,128)(2,1)S(1)} %copy-done.9), custom_call_target="tpu_custom_call" | custom-call | flops 452984832 | bytes 7077888 | tf_op jit(solution)/shard_map/token_values/pallas_call | solution.py:257
  24.4 1.4 %collective-permute-start.2 = (bf16[3,128,128]{2,1,0:T(8,128)(2,1)S(1)}, bf16[3,128,128]{2,1,0:T(8,128)(2,1)S(1)}, u32[]{:S(2)}, u32[]{:S(2)}) collective-permute-start(bf16[3,128,128]{2,1,0:T(8,128)(2,1)S(1)} %get-tuple-element.33), channel_id=1, source_target_pairs={{0,8},{4,12},{8,0},{12,4},{1,9},{5,13},{9,1},{13,5},{2,10},{6,14},... | collective-permute-start | bytes 294920 | tf_op jit(solution)/shard_map/act_y/ppermute | solution.py:60
  25.8 2.1 %collective-permute-done.1.first = bf16[3,128,128]{2,1,0:T(8,128)(2,1)S(1)} collective-permute-done((bf16[3,128,128]{2,1,0:T(8,128)(2,1)S(1)}, bf16[3,128,128]{2,1,0:T(8,128)(2,1)S(1)}, u32[]{:S(2)}, u32[]{:S(2)}) %collective-permute-start.1) | collective-permute-done | bytes 98336 | tf_op jit(solution)/shard_map/act_y/ppermute | solution.py:60
  28.7 2.0 %collective-permute-done.2.second = bf16[3,128,128]{2,1,0:T(8,128)(2,1)S(1)} collective-permute-done((bf16[3,128,128]{2,1,0:T(8,128)(2,1)S(1)}, bf16[3,128,128]{2,1,0:T(8,128)(2,1)S(1)}, u32[]{:S(2)}, u32[]{:S(2)}) %collective-permute-start.2) | collective-permute-done | bytes 98336 | tf_op jit(solution)/shard_map/act_y/ppermute | solution.py:60
  30.7 1.9 %collective-permute-done.3.third = bf16[3,128,128]{2,1,0:T(8,128)(2,1)S(1)} collective-permute-done((bf16[3,128,128]{2,1,0:T(8,128)(2,1)S(1)}, bf16[3,128,128]{2,1,0:T(8,128)(2,1)S(1)}, u32[]{:S(2)}, u32[]{:S(2)}) %collective-permute-start.3) | collective-permute-done | bytes 98336 | tf_op jit(solution)/shard_map/act_y/ppermute | solution.py:60
  33.2 7.2 %collective-permute-done.7.refs_1_ = bf16[64,4736]{1,0:T(8,128)(2,1)} collective-permute-done((bf16[64,4736]{1,0:T(8,128)(2,1)}, bf16[64,4736]{1,0:T(8,128)(2,1)}, u32[]{:S(2)}, u32[]{:S(2)}) %collective-permute-start.7) | collective-permute-done | bytes 606240 | tf_op jit(solution)/shard_map/weight_z/ppermute | solution.py:60
  40.4 1.2 collective-permute-start.17
  41.6 2.5 %collective-permute-start.11 = (bf16[64,4736]{1,0:T(8,128)(2,1)}, bf16[64,4736]{1,0:T(8,128)(2,1)S(1)}, u32[]{:S(2)}, u32[]{:S(2)}) collective-permute-start(bf16[64,4736]{1,0:T(8,128)(2,1)} %get-tuple-element.43.refs_0_), channel_id=1, source_target_pairs={{0,64},{1,193},{64,0},{65,129},{128,192},{129,65},{192,128},{193,1... | collective-permute-start | bytes 1818632 | tf_op jit(solution)/shard_map/weight_x/ppermute | solution.py:33
  44.5 1.0 collective-permute-done.9.mixed_s.refs_0_
  45.5 6.1 %collective-permute-start.5 = (bf16[128,128]{1,0:T(8,128)(2,1)S(1)}, bf16[128,128]{1,0:T(8,128)(2,1)S(1)}, u32[]{:S(2)}, u32[]{:S(2)}) collective-permute-start(bf16[128,128]{1,0:T(8,128)(2,1)S(1)} %get-tuple-element.36.refs_2_.tie), channel_id=1, source_target_pairs={{0,2},{2,0},{1,3},{3,1},{4,6},{6,4},{5,7},{7,5},{8,10},{10,8},{9,1... | collective-permute-start | bytes 98312 | tf_op jit(solution)/shard_map/act_z/ppermute | solution.py:60
  51.6 2.0 %own_near.1.tie.near = bf16[2,256,256]{2,1,0:T(8,128)(2,1)S(1)} custom-call(s32[4]{0:T(128)S(1)} %pad_add_fusion.at, bf16[128,4608]{1,0:T(8,128)(2,1)S(1)} %copy-done.1, bf16[128,4608]{1,0:T(8,128)(2,1)S(1)} %collective-permute-done.4.tie.near_s.own_s, bf16[128,4608]{1,0:T(8,128)(2,1)S(1)} %get-tuple-element.39.more.one, ...), custom_call_target="tpu_custom_call" | custom-call | flops 1241513984 | bytes 7274496 | tf_op jit(solution)/shard_map/own_near/pallas_call | solution.py:308
  53.6 1.2 %gate_products.1 = (f32[8,2304]{1,0:T(8,128)S(1)}, f32[8,2304]{1,0:T(8,128)S(1)}) custom-call(s32[4]{0:T(128)S(1)} %pad_add_fusion.at, f32[128,128]{1,0:T(8,128)S(1)} %get-tuple-element.35.keep, bf16[128,128]{1,0:T(8,128)(2,1)S(1)} %collective-permute-done.5.got, f32[128,128]{1,0:T(8,128)S(1)} %get-tuple-element.37.back, ...), custom_call_target="tpu_custom_call" | custom-call | tf_op jit(solution)/shard_map/gate_products/pallas_call | solution.py:320
  55.4 2.0 %collective-permute-done.11.refs_0_ = bf16[64,4736]{1,0:T(8,128)(2,1)S(1)} collective-permute-done((bf16[64,4736]{1,0:T(8,128)(2,1)}, bf16[64,4736]{1,0:T(8,128)(2,1)S(1)}, u32[]{:S(2)}, u32[]{:S(2)}) %collective-permute-start.11) | collective-permute-done | bytes 606240 | tf_op jit(solution)/shard_map/weight_x/ppermute | solution.py:33
  57.5 1.8 %collective-permute-start.21 = (bf16[128,4608]{1,0:T(8,128)(2,1)S(1)}, bf16[128,4608]{1,0:T(8,128)(2,1)S(1)}, u32[]{:S(2)}, u32[]{:S(2)}) collective-permute-start(bf16[128,4608]{1,0:T(8,128)(2,1)S(1)} %fence.6.refs_2_.two.near), channel_id=1, source_target_pairs={{0,1},{1,0},{2,3},{3,2},{4,5},{5,4},{6,7},{7,6},{8,9},{9,8},{10,11... | collective-permute-start | bytes 3538952 | tf_op jit(solution)/shard_map/tokens_core/ppermute | solution.py:60
  59.3 1.4 %collective-permute-start.25 = (bf16[128,4608]{1,0:T(8,128)(2,1)S(1)}, bf16[128,4608]{1,0:T(8,128)(2,1)S(1)}, u32[]{:S(2)}, u32[]{:S(2)}) collective-permute-start(bf16[128,4608]{1,0:T(8,128)(2,1)S(1)} %fence.6.refs_2_.two.near), channel_id=1, source_target_pairs={{0,4},{1,13},{4,8},{5,1},{8,12},{9,5},{12,0},{13,9},{2,6},{3,15},{... | collective-permute-start | bytes 3538952 | tf_op jit(solution)/shard_map/tokens_y/ppermute | solution.py:27
  60.7 2.2 %collective-permute-start.13 = (bf16[8,2304]{1,0:T(8,128)(2,1)S(1)}, bf16[8,2304]{1,0:T(8,128)(2,1)S(1)}, u32[]{:S(2)}, u32[]{:S(2)}) collective-permute-start(bf16[8,2304]{1,0:T(8,128)(2,1)S(1)} %get-tuple-element.45), channel_id=1, source_target_pairs={{0,16},{16,0},{32,48},{48,32},{1,17},{17,1},{33,49},{49,33},{2,18}... | collective-permute-start | bytes 110600 | tf_op jit(solution)/shard_map/gate_zl/ppermute | solution.py:60
  63.6 1.0 collective-permute-done.13.second
  64.6 1.8 %collective-permute-start.15 = (bf16[8,2304]{1,0:T(8,128)(2,1)S(1)}, bf16[8,2304]{1,0:T(8,128)(2,1)S(1)}, u32[]{:S(2)}, u32[]{:S(2)}) collective-permute-start(bf16[8,2304]{1,0:T(8,128)(2,1)S(1)} %get-tuple-element.45), channel_id=1, source_target_pairs={{0,48},{16,32},{32,16},{48,0},{1,49},{17,33},{33,17},{49,1},{2,50}... | collective-permute-start | bytes 110600 | tf_op jit(solution)/shard_map/gate_zl/ppermute | solution.py:60
  67.2 2.1 %collective-permute-done.15.fourth = bf16[8,2304]{1,0:T(8,128)(2,1)S(1)} collective-permute-done((bf16[8,2304]{1,0:T(8,128)(2,1)S(1)}, bf16[8,2304]{1,0:T(8,128)(2,1)S(1)}, u32[]{:S(2)}, u32[]{:S(2)}) %collective-permute-start.15) | collective-permute-done | bytes 36896 | tf_op jit(solution)/shard_map/gate_zl/ppermute | solution.py:60
  70.6 3.3 %far_products.1 = (bf16[3,256,256]{2,1,0:T(8,128)(2,1)S(1)}, bf16[256,4608]{1,0:T(8,128)(2,1)S(1)}, bf16[256,128]{1,0:T(8,128)(2,1)S(1)}) custom-call(s32[4]{0:T(128)S(1)} %pad_add_fusion.at, bf16[128,4608]{1,0:T(8,128)(2,1)S(1)} %copy-done.1, bf16[128,4608]{1,0:T(8,128)(2,1)S(1)} %collective-permute-done.4.tie.near_s.own_s, ...), custom_call_target="tpu_custom_call" | custom-call | flops 1862270976 | bytes 10911744 | tf_op jit(solution)/shard_map/far_products/pallas_call | solution.py:368
  74.6 2.3 %collective-permute-start.26 = (bf16[128,4608]{1,0:T(8,128)(2,1)S(1)}, bf16[128,4608]{1,0:T(8,128)(2,1)S(1)}, u32[]{:S(2)}, u32[]{:S(2)}) collective-permute-start(bf16[128,4608]{1,0:T(8,128)(2,1)S(1)} %fence.7.more.three), channel_id=1, source_target_pairs={{0,1},{1,0},{2,3},{3,2},{4,5},{5,4},{6,7},{7,6},{8,9},{9,8},{10,11... | collective-permute-start | bytes 3538952 | tf_op jit(solution)/shard_map/tokens_core/ppermute | solution.py:60
  77.0 6.1 %collective-permute-start.28 = (bf16[3,256,256]{2,1,0:T(8,128)(2,1)S(1)}, bf16[3,256,256]{2,1,0:T(8,128)(2,1)S(1)}, u32[]{:S(2)}, u32[]{:S(2)}) collective-permute-start(bf16[3,256,256]{2,1,0:T(8,128)(2,1)S(1)} %get-tuple-element.47.refs_0_.refs_1_.tie), channel_id=1, source_target_pairs={{0,2},{2,0},{1,3},{3,1},{4,6},{6,4},{5,7},{7,5},{8,10},{10,8},{9,1... | collective-permute-start | bytes 1179656 | tf_op jit(solution)/shard_map/out_z/ppermute | solution.py:60
  83.1 3.7 %collective-permute-start.19 = (f32[8,2304]{1,0:T(8,128)S(1)}, f32[8,2304]{1,0:T(8,128)S(1)}, u32[]{:S(2)}, u32[]{:S(2)}) collective-permute-start(f32[8,2304]{1,0:T(8,128)S(1)} %get-tuple-element.46.refs_4_.first), channel_id=1, source_target_pairs={{0,128},{64,192},{128,0},{192,64},{1,129},{65,193},{129,1},{193,65... | collective-permute-start | bytes 221192 | tf_op jit(solution)/shard_map/gate_x/ppermute | solution.py:60
  86.9 3.5 %collective-permute-done.19.third = f32[8,2304]{1,0:T(8,128)S(1)} collective-permute-done((f32[8,2304]{1,0:T(8,128)S(1)}, f32[8,2304]{1,0:T(8,128)S(1)}, u32[]{:S(2)}, u32[]{:S(2)}) %collective-permute-start.19) | collective-permute-done | bytes 73760 | tf_op jit(solution)/shard_map/gate_x/ppermute | solution.py:60
  90.4 1.5 %collective-permute-done.20.fourth = f32[8,2304]{1,0:T(8,128)S(1)} collective-permute-done((f32[8,2304]{1,0:T(8,128)S(1)}, f32[8,2304]{1,0:T(8,128)S(1)}, u32[]{:S(2)}, u32[]{:S(2)}) %collective-permute-start.20) | collective-permute-done | bytes 73760 | tf_op jit(solution)/shard_map/gate_x/ppermute | solution.py:60
  92.6 2.1 %collective-permute-start.23 = (f32[8,2304]{1,0:T(8,128)S(1)}, f32[8,2304]{1,0:T(8,128)S(1)}, u32[]{:S(2)}, u32[]{:S(2)}) collective-permute-start(f32[8,2304]{1,0:T(8,128)S(1)} %get-tuple-element.48.first), channel_id=1, source_target_pairs={{0,8},{4,12},{8,0},{12,4},{1,9},{5,13},{9,1},{13,5},{2,10},{6,14},... | collective-permute-start | bytes 221192 | tf_op jit(solution)/shard_map/gate_y/ppermute | solution.py:60
  94.7 1.7 %collective-permute-start.24 = (f32[8,2304]{1,0:T(8,128)S(1)}, f32[8,2304]{1,0:T(8,128)S(1)}, u32[]{:S(2)}, u32[]{:S(2)}) collective-permute-start(f32[8,2304]{1,0:T(8,128)S(1)} %get-tuple-element.48.first), channel_id=1, source_target_pairs={{0,12},{4,8},{8,4},{12,0},{1,13},{5,9},{9,5},{13,1},{2,14},{6,10},... | collective-permute-start | bytes 221192 | tf_op jit(solution)/shard_map/gate_y/ppermute | solution.py:60
  96.4 2.0 %own_rest.1.refs_0_.rest = bf16[2,256,256]{2,1,0:T(8,128)(2,1)S(1)} custom-call(s32[4]{0:T(128)S(1)} %pad_add_fusion.at, bf16[128,4608]{1,0:T(8,128)(2,1)S(1)} %fence.6.refs_2_.two.near, bf16[128,4608]{1,0:T(8,128)(2,1)S(1)} %collective-permute-done.21.two_s.near_s, bf16[128,4608]{1,0:T(8,128)(2,1)S(1)} %fence.7.more.three, ...), custom_call_target="tpu_custom_call" | custom-call | flops 1241513984 | bytes 7274496 | tf_op jit(solution)/shard_map/own_rest/pallas_call | solution.py:308
  98.4 1.3 %collective-permute-done.24.fourth = f32[8,2304]{1,0:T(8,128)S(1)} collective-permute-done((f32[8,2304]{1,0:T(8,128)S(1)}, f32[8,2304]{1,0:T(8,128)S(1)}, u32[]{:S(2)}, u32[]{:S(2)}) %collective-permute-start.24) | collective-permute-done | bytes 73760 | tf_op jit(solution)/shard_map/gate_y/ppermute | solution.py:60
  99.8 1.3 %far_products_last.1.refs_0_ = bf16[256,256]{1,0:T(8,128)(2,1)S(1)} custom-call(s32[4]{0:T(128)S(1)} %pad_add_fusion.at, bf16[128,4608]{1,0:T(8,128)(2,1)S(1)} %fence.7.more.three, bf16[128,4608]{1,0:T(8,128)(2,1)S(1)} %collective-permute-done.26.more_s.three_s, bf16[4,128,128]{2,1,0:T(8,128)(2,1)S(1)} %get-tuple-element.40.mixed, ...), custom_call_target="tpu_custom_call" | custom-call | flops 620756992 | bytes 3637248 | tf_op jit(solution)/shard_map/far_products_last/pallas_call | solution.py:393
  101.6 5.0 %collective-permute-start.27 = (bf16[8,2304]{1,0:T(8,128)(2,1)S(1)}, bf16[8,2304]{1,0:T(8,128)(2,1)S(1)}, u32[]{:S(2)}, u32[]{:S(2)}) collective-permute-start(bf16[8,2304]{1,0:T(8,128)(2,1)S(1)} %get-tuple-element.50), channel_id=1, source_target_pairs={{0,2},{2,0},{1,3},{3,1},{4,6},{6,4},{5,7},{7,5},{8,10},{10,8},{9,1... | collective-permute-start | bytes 110600 | tf_op jit(solution)/shard_map/gate_zh/ppermute | solution.py:60
  106.6 3.9 %collective-permute-done.27.right = bf16[8,2304]{1,0:T(8,128)(2,1)S(1)} collective-permute-done((bf16[8,2304]{1,0:T(8,128)(2,1)S(1)}, bf16[8,2304]{1,0:T(8,128)(2,1)S(1)}, u32[]{:S(2)}, u32[]{:S(2)}) %collective-permute-start.27) | collective-permute-done | bytes 36896 | tf_op jit(solution)/shard_map/gate_zh/ppermute | solution.py:60
  111.1 4.6 %collective-permute-start.29 = (f32[8,2304]{1,0:T(8,128)S(1)}, f32[8,2304]{1,0:T(8,128)S(1)}, u32[]{:S(2)}, u32[]{:S(2)}) collective-permute-start(f32[8,2304]{1,0:T(8,128)S(1)} %get-tuple-element.53.mine), channel_id=1, source_target_pairs={{0,1},{1,0},{2,3},{3,2},{4,5},{5,4},{6,7},{7,6},{8,9},{9,8},{10,11... | collective-permute-start | bytes 221192 | tf_op jit(solution)/shard_map/gate_core_back/ppermute | solution.py:60
  115.7 0.9 collective-permute-done.29.other
  116.6 1.2 %gate_halves.1.tie = f32[8,4608]{1,0:T(8,128)} custom-call(s32[4]{0:T(128)S(1)} %pad_add_fusion.at, f32[8,2304]{1,0:T(8,128)S(1)} %get-tuple-element.53.mine, f32[8,2304]{1,0:T(8,128)S(1)} %collective-permute-done.29.other), custom_call_target="tpu_custom_call" | custom-call | tf_op jit(solution)/shard_map/gate_halves/pallas_call | solution.py:410
  117.9 0.9 copy-done.8
  118.8 1.6 %place.1 = bf16[4,2,2,128,256]{4,3,2,1,0:T(8,128)(2,1)} custom-call(s32[4]{0:T(128)S(1)} %pad_add_fusion.at, bf16[2,256,256]{2,1,0:T(8,128)(2,1)S(1)} %own_near.1.tie.near, bf16[2,256,256]{2,1,0:T(8,128)(2,1)S(1)} %own_rest.1.refs_0_.rest, bf16[3,256,256]{2,1,0:T(8,128)(2,1)S(1)} %collective-permute-done.28.refs_1_.got, ...), custom_call_target="tpu_custom_call" | custom-call | tf_op jit(solution)/shard_map/place/pallas_call | solution.py:419
  (58 shorter events, 9.9 us)
Async XLA Ops:
  0.6 32.0 %collective-permute-start.4 = (bf16[128,4608]{1,0:T(8,128)(2,1)}, bf16[128,4608]{1,0:T(8,128)(2,1)S(1)}, u32[]{:S(2)}, u32[]{:S(2)}) collective-permute-start(bf16[128,4608]{1,0:T(8,128)(2,1)} %own.1), channel_id=1, source_target_pairs={{0,1},{1,0},{2,3},{3,2},{4,5},{5,4},{6,7},{7,6},{8,9},{9,8},{10,11... | collective-permute-start | bytes 3538952 | tf_op jit(solution)/shard_map/tokens_core/ppermute | solution.py:60
  4.0 36.5 %collective-permute-start.6 = (bf16[128,4608]{1,0:T(8,128)(2,1)}, bf16[128,4608]{1,0:T(8,128)(2,1)S(1)}, u32[]{:S(2)}, u32[]{:S(2)}) collective-permute-start(bf16[128,4608]{1,0:T(8,128)(2,1)} %own.1), channel_id=1, source_target_pairs={{0,4},{1,13},{4,8},{5,1},{8,12},{9,5},{12,0},{13,9},{2,6},{3,15},{... | collective-permute-start | bytes 3538952 | tf_op jit(solution)/shard_map/tokens_y/ppermute | solution.py:27
  6.8 11.0 %copy-start.1 = (bf16[128,4608]{1,0:T(8,128)(2,1)S(1)}, bf16[128,4608]{1,0:T(8,128)(2,1)}, u32[]{:S(2)}) copy-start(bf16[128,4608]{1,0:T(8,128)(2,1)} %own.1) | copy-start | bytes 3538948
  7.7 32.8 %collective-permute-start.7 = (bf16[64,4736]{1,0:T(8,128)(2,1)}, bf16[64,4736]{1,0:T(8,128)(2,1)}, u32[]{:S(2)}, u32[]{:S(2)}) collective-permute-start(bf16[64,4736]{1,0:T(8,128)(2,1)} %pad_maximum_fusion), channel_id=1, source_target_pairs={{0,2},{2,0},{1,3},{3,1},{4,6},{6,4},{5,7},{7,5},{8,10},{10,8},{9,1... | collective-permute-start | bytes 1818632 | tf_op jit(solution)/shard_map/weight_z/ppermute | solution.py:60
  14.6 1.2 %copy-start.5 = (bf16[2048,256]{1,0:T(8,128)(2,1)S(1)}, bf16[2048,256]{1,0:T(8,128)(2,1)}, u32[]{:S(2)}) copy-start(bf16[2048,256]{1,0:T(8,128)(2,1)} %param.9) | copy-start | bytes 3145732
  15.9 0.8 copy-start.6
  17.7 5.5 %collective-permute-start = (bf16[4,2,128,128]{3,2,1,0:T(8,128)(2,1)S(1)}, bf16[4,2,128,128]{3,2,1,0:T(8,128)(2,1)S(1)}, u32[]{:S(2)}, u32[]{:S(2)}) collective-permute-start(bf16[4,2,128,128]{3,2,1,0:T(8,128)(2,1)S(1)} %get-tuple-element.29), channel_id=1, source_target_pairs={{0,1},{1,0},{2,3},{3,2},{4,5},{5,4},{6,7},{7,6},{8,9},{9,8},{10,11... | collective-permute-start | bytes 786440 | tf_op jit(solution)/shard_map/act_core/ppermute | solution.py:60
  17.8 1.3 %copy-start.2 = (bf16[128,4608]{1,0:T(8,128)(2,1)S(1)}, bf16[128,4608]{1,0:T(8,128)(2,1)}, u32[]{:S(2)}) copy-start(bf16[128,4608]{1,0:T(8,128)(2,1)} %hidden.3) | copy-start | bytes 3538948
  19.1 1.3 %copy-start.4 = (bf16[128,4608]{1,0:T(8,128)(2,1)S(1)}, bf16[128,4608]{1,0:T(8,128)(2,1)}, u32[]{:S(2)}) copy-start(bf16[128,4608]{1,0:T(8,128)(2,1)} %up.1) | copy-start | bytes 3538948
  20.3 0.9 copy-start.9
  23.8 4.1 %collective-permute-start.1 = (bf16[3,128,128]{2,1,0:T(8,128)(2,1)S(1)}, bf16[3,128,128]{2,1,0:T(8,128)(2,1)S(1)}, u32[]{:S(2)}, u32[]{:S(2)}) collective-permute-start(bf16[3,128,128]{2,1,0:T(8,128)(2,1)S(1)} %get-tuple-element.32), channel_id=1, source_target_pairs={{0,4},{4,0},{8,12},{12,8},{1,5},{5,1},{9,13},{13,9},{2,6},{6,2},{1... | collective-permute-start | bytes 294920 | tf_op jit(solution)/shard_map/act_y/ppermute | solution.py:60
  24.4 6.3 %collective-permute-start.2 = (bf16[3,128,128]{2,1,0:T(8,128)(2,1)S(1)}, bf16[3,128,128]{2,1,0:T(8,128)(2,1)S(1)}, u32[]{:S(2)}, u32[]{:S(2)}) collective-permute-start(bf16[3,128,128]{2,1,0:T(8,128)(2,1)S(1)} %get-tuple-element.33), channel_id=1, source_target_pairs={{0,8},{4,12},{8,0},{12,4},{1,9},{5,13},{9,1},{13,5},{2,10},{6,14},... | collective-permute-start | bytes 294920 | tf_op jit(solution)/shard_map/act_y/ppermute | solution.py:60
  27.9 4.7 %collective-permute-start.3 = (bf16[3,128,128]{2,1,0:T(8,128)(2,1)S(1)}, bf16[3,128,128]{2,1,0:T(8,128)(2,1)S(1)}, u32[]{:S(2)}, u32[]{:S(2)}) collective-permute-start(bf16[3,128,128]{2,1,0:T(8,128)(2,1)S(1)} %get-tuple-element.34), channel_id=1, source_target_pairs={{0,12},{4,8},{8,4},{12,0},{1,13},{5,9},{9,5},{13,1},{2,14},{6,10},... | collective-permute-start | bytes 294920 | tf_op jit(solution)/shard_map/act_y/ppermute | solution.py:60
  32.6 19.0 %copy-start = (bf16[256,4608]{1,0:T(8,128)(2,1)S(1)}, bf16[256,4608]{1,0:T(8,128)(2,1)}, u32[]{:S(2)}) copy-start(bf16[256,4608]{1,0:T(8,128)(2,1)} %weight.3) | copy-start | bytes 7077892
  33.2 18.4 %copy-start.7 = (bf16[256,128]{1,0:T(8,128)(2,1)S(1)}, bf16[256,128]{1,0:T(8,128)(2,1)}, u32[]{:S(2)}) copy-start(bf16[256,128]{1,0:T(8,128)(2,1)} %down.5) | copy-start | bytes 196612
  40.4 11.2 %collective-permute-start.8 = (bf16[128,4608]{1,0:T(8,128)(2,1)S(1)}, bf16[128,4608]{1,0:T(8,128)(2,1)S(1)}, u32[]{:S(2)}, u32[]{:S(2)}) collective-permute-start(bf16[128,4608]{1,0:T(8,128)(2,1)S(1)} %get-tuple-element.39.more.one), channel_id=1, source_target_pairs={{0,1},{1,0},{2,3},{3,2},{4,5},{5,4},{6,7},{7,6},{8,9},{9,8},{10,11... | collective-permute-start | bytes 3538952 | tf_op jit(solution)/shard_map/tokens_core/ppermute | solution.py:60
  40.4 17.0 %collective-permute-start.17 = (bf16[128,4608]{1,0:T(8,128)(2,1)S(1)}, bf16[128,4608]{1,0:T(8,128)(2,1)S(1)}, u32[]{:S(2)}, u32[]{:S(2)}) collective-permute-start(bf16[128,4608]{1,0:T(8,128)(2,1)S(1)} %get-tuple-element.39.more.one), channel_id=1, source_target_pairs={{0,4},{1,13},{4,8},{5,1},{8,12},{9,5},{12,0},{13,9},{2,6},{3,15},{... | collective-permute-start | bytes 3538952 | tf_op jit(solution)/shard_map/tokens_y/ppermute | solution.py:27
  41.6 15.8 %collective-permute-start.11 = (bf16[64,4736]{1,0:T(8,128)(2,1)}, bf16[64,4736]{1,0:T(8,128)(2,1)S(1)}, u32[]{:S(2)}, u32[]{:S(2)}) collective-permute-start(bf16[64,4736]{1,0:T(8,128)(2,1)} %get-tuple-element.43.refs_0_), channel_id=1, source_target_pairs={{0,64},{1,193},{64,0},{65,129},{128,192},{129,65},{192,128},{193,1... | collective-permute-start | bytes 1818632 | tf_op jit(solution)/shard_map/weight_x/ppermute | solution.py:33
  44.1 13.3 %collective-permute-start.12 = (bf16[64,4736]{1,0:T(8,128)(2,1)}, bf16[64,4736]{1,0:T(8,128)(2,1)S(1)}, u32[]{:S(2)}, u32[]{:S(2)}) collective-permute-start(bf16[64,4736]{1,0:T(8,128)(2,1)} %get-tuple-element.43.refs_0_), channel_id=1, source_target_pairs={{0,192},{1,65},{64,128},{65,1},{128,64},{129,193},{192,0},{193,129... | collective-permute-start | bytes 1818632 | tf_op jit(solution)/shard_map/weight_x/ppermute | solution.py:33
  44.1 9.5 %copy-start.3 = (bf16[128,4608]{1,0:T(8,128)(2,1)S(1)}, bf16[128,4608]{1,0:T(8,128)(2,1)}, u32[]{:S(2)}) copy-start(bf16[128,4608]{1,0:T(8,128)(2,1)} %hidden.3) | copy-start | bytes 3538948
  44.1 1.4 %collective-permute-start.9 = (bf16[4,128,128]{2,1,0:T(8,128)(2,1)S(1)}, bf16[4,128,128]{2,1,0:T(8,128)(2,1)S(1)}, u32[]{:S(2)}, u32[]{:S(2)}) collective-permute-start(bf16[4,128,128]{2,1,0:T(8,128)(2,1)S(1)} %get-tuple-element.40.mixed), channel_id=1, source_target_pairs={{0,1},{1,0},{2,3},{3,2},{4,5},{5,4},{6,7},{7,6},{8,9},{9,8},{10,11... | collective-permute-start | bytes 393224 | tf_op jit(solution)/shard_map/mixed_core/ppermute | solution.py:60
  45.5 8.1 %collective-permute-start.5 = (bf16[128,128]{1,0:T(8,128)(2,1)S(1)}, bf16[128,128]{1,0:T(8,128)(2,1)S(1)}, u32[]{:S(2)}, u32[]{:S(2)}) collective-permute-start(bf16[128,128]{1,0:T(8,128)(2,1)S(1)} %get-tuple-element.36.refs_2_.tie), channel_id=1, source_target_pairs={{0,2},{2,0},{1,3},{3,1},{4,6},{6,4},{5,7},{7,5},{8,10},{10,8},{9,1... | collective-permute-start | bytes 98312 | tf_op jit(solution)/shard_map/act_z/ppermute | solution.py:60
  54.8 2.6 %collective-permute-start.10 = (f32[8,2304]{1,0:T(8,128)S(1)}, f32[8,2304]{1,0:T(8,128)S(1)}, u32[]{:S(2)}, u32[]{:S(2)}) collective-permute-start(f32[8,2304]{1,0:T(8,128)S(1)} %get-tuple-element.42), channel_id=1, source_target_pairs={{0,1},{1,0},{2,3},{3,2},{4,5},{5,4},{6,7},{7,6},{8,9},{9,8},{10,11... | collective-permute-start | bytes 221192 | tf_op jit(solution)/shard_map/gate_core/ppermute | solution.py:60
  57.5 13.1 %collective-permute-start.21 = (bf16[128,4608]{1,0:T(8,128)(2,1)S(1)}, bf16[128,4608]{1,0:T(8,128)(2,1)S(1)}, u32[]{:S(2)}, u32[]{:S(2)}) collective-permute-start(bf16[128,4608]{1,0:T(8,128)(2,1)S(1)} %fence.6.refs_2_.two.near), channel_id=1, source_target_pairs={{0,1},{1,0},{2,3},{3,2},{4,5},{5,4},{6,7},{7,6},{8,9},{9,8},{10,11... | collective-permute-start | bytes 3538952 | tf_op jit(solution)/shard_map/tokens_core/ppermute | solution.py:60
  59.3 15.3 %collective-permute-start.25 = (bf16[128,4608]{1,0:T(8,128)(2,1)S(1)}, bf16[128,4608]{1,0:T(8,128)(2,1)S(1)}, u32[]{:S(2)}, u32[]{:S(2)}) collective-permute-start(bf16[128,4608]{1,0:T(8,128)(2,1)S(1)} %fence.6.refs_2_.two.near), channel_id=1, source_target_pairs={{0,4},{1,13},{4,8},{5,1},{8,12},{9,5},{12,0},{13,9},{2,6},{3,15},{... | collective-permute-start | bytes 3538952 | tf_op jit(solution)/shard_map/tokens_y/ppermute | solution.py:27
  60.7 9.2 %collective-permute-start.16 = (bf16[64,4736]{1,0:T(8,128)(2,1)S(1)}, bf16[64,4736]{1,0:T(8,128)(2,1)S(1)}, u32[]{:S(2)}, u32[]{:S(2)}) collective-permute-start(bf16[64,4736]{1,0:T(8,128)(2,1)S(1)} %fence.5.refs_1_), channel_id=1, source_target_pairs={{0,192},{1,65},{64,128},{65,1},{128,64},{129,193},{192,0},{193,129... | collective-permute-start | bytes 1818632 | tf_op jit(solution)/shard_map/weight_x_far/ppermute | solution.py:33
  60.7 3.9 %collective-permute-start.13 = (bf16[8,2304]{1,0:T(8,128)(2,1)S(1)}, bf16[8,2304]{1,0:T(8,128)(2,1)S(1)}, u32[]{:S(2)}, u32[]{:S(2)}) collective-permute-start(bf16[8,2304]{1,0:T(8,128)(2,1)S(1)} %get-tuple-element.45), channel_id=1, source_target_pairs={{0,16},{16,0},{32,48},{48,32},{1,17},{17,1},{33,49},{49,33},{2,18}... | collective-permute-start | bytes 110600 | tf_op jit(solution)/shard_map/gate_zl/ppermute | solution.py:60
  63.0 4.3 %collective-permute-start.14 = (bf16[8,2304]{1,0:T(8,128)(2,1)S(1)}, bf16[8,2304]{1,0:T(8,128)(2,1)S(1)}, u32[]{:S(2)}, u32[]{:S(2)}) collective-permute-start(bf16[8,2304]{1,0:T(8,128)(2,1)S(1)} %get-tuple-element.45), channel_id=1, source_target_pairs={{0,32},{16,48},{32,0},{48,16},{1,33},{17,49},{33,1},{49,17},{2,34}... | collective-permute-start | bytes 110600 | tf_op jit(solution)/shard_map/gate_zl/ppermute | solution.py:60
  64.6 4.7 %collective-permute-start.15 = (bf16[8,2304]{1,0:T(8,128)(2,1)S(1)}, bf16[8,2304]{1,0:T(8,128)(2,1)S(1)}, u32[]{:S(2)}, u32[]{:S(2)}) collective-permute-start(bf16[8,2304]{1,0:T(8,128)(2,1)S(1)} %get-tuple-element.45), channel_id=1, source_target_pairs={{0,48},{16,32},{32,16},{48,0},{1,49},{17,33},{33,17},{49,1},{2,50}... | collective-permute-start | bytes 110600 | tf_op jit(solution)/shard_map/gate_zl/ppermute | solution.py:60
  74.6 21.8 %collective-permute-start.26 = (bf16[128,4608]{1,0:T(8,128)(2,1)S(1)}, bf16[128,4608]{1,0:T(8,128)(2,1)S(1)}, u32[]{:S(2)}, u32[]{:S(2)}) collective-permute-start(bf16[128,4608]{1,0:T(8,128)(2,1)S(1)} %fence.7.more.three), channel_id=1, source_target_pairs={{0,1},{1,0},{2,3},{3,2},{4,5},{5,4},{6,7},{7,6},{8,9},{9,8},{10,11... | collective-permute-start | bytes 3538952 | tf_op jit(solution)/shard_map/tokens_core/ppermute | solution.py:60
  77.0 29.7 %collective-permute-start.28 = (bf16[3,256,256]{2,1,0:T(8,128)(2,1)S(1)}, bf16[3,256,256]{2,1,0:T(8,128)(2,1)S(1)}, u32[]{:S(2)}, u32[]{:S(2)}) collective-permute-start(bf16[3,256,256]{2,1,0:T(8,128)(2,1)S(1)} %get-tuple-element.47.refs_0_.refs_1_.tie), channel_id=1, source_target_pairs={{0,2},{2,0},{1,3},{3,1},{4,6},{6,4},{5,7},{7,5},{8,10},{10,8},{9,1... | collective-permute-start | bytes 1179656 | tf_op jit(solution)/shard_map/out_z/ppermute | solution.py:60
  83.1 3.9 %collective-permute-start.18 = (f32[8,2304]{1,0:T(8,128)S(1)}, f32[8,2304]{1,0:T(8,128)S(1)}, u32[]{:S(2)}, u32[]{:S(2)}) collective-permute-start(f32[8,2304]{1,0:T(8,128)S(1)} %get-tuple-element.46.refs_4_.first), channel_id=1, source_target_pairs={{0,64},{64,0},{128,192},{192,128},{1,65},{65,1},{129,193},{193,129... | collective-permute-start | bytes 221192 | tf_op jit(solution)/shard_map/gate_x/ppermute | solution.py:60
  83.1 7.4 %collective-permute-start.19 = (f32[8,2304]{1,0:T(8,128)S(1)}, f32[8,2304]{1,0:T(8,128)S(1)}, u32[]{:S(2)}, u32[]{:S(2)}) collective-permute-start(f32[8,2304]{1,0:T(8,128)S(1)} %get-tuple-element.46.refs_4_.first), channel_id=1, source_target_pairs={{0,128},{64,192},{128,0},{192,64},{1,129},{65,193},{129,1},{193,65... | collective-permute-start | bytes 221192 | tf_op jit(solution)/shard_map/gate_x/ppermute | solution.py:60
  86.7 5.2 %collective-permute-start.20 = (f32[8,2304]{1,0:T(8,128)S(1)}, f32[8,2304]{1,0:T(8,128)S(1)}, u32[]{:S(2)}, u32[]{:S(2)}) collective-permute-start(f32[8,2304]{1,0:T(8,128)S(1)} %get-tuple-element.46.refs_4_.first), channel_id=1, source_target_pairs={{0,192},{64,128},{128,64},{192,0},{1,193},{65,129},{129,65},{193,1... | collective-permute-start | bytes 221192 | tf_op jit(solution)/shard_map/gate_x/ppermute | solution.py:60
  92.6 5.8 %collective-permute-start.22 = (f32[8,2304]{1,0:T(8,128)S(1)}, f32[8,2304]{1,0:T(8,128)S(1)}, u32[]{:S(2)}, u32[]{:S(2)}) collective-permute-start(f32[8,2304]{1,0:T(8,128)S(1)} %get-tuple-element.48.first), channel_id=1, source_target_pairs={{0,4},{4,0},{8,12},{12,8},{1,5},{5,1},{9,13},{13,9},{2,6},{6,2},{1... | collective-permute-start | bytes 221192 | tf_op jit(solution)/shard_map/gate_y/ppermute | solution.py:60
  92.6 5.9 %collective-permute-start.23 = (f32[8,2304]{1,0:T(8,128)S(1)}, f32[8,2304]{1,0:T(8,128)S(1)}, u32[]{:S(2)}, u32[]{:S(2)}) collective-permute-start(f32[8,2304]{1,0:T(8,128)S(1)} %get-tuple-element.48.first), channel_id=1, source_target_pairs={{0,8},{4,12},{8,0},{12,4},{1,9},{5,13},{9,1},{13,5},{2,10},{6,14},... | collective-permute-start | bytes 221192 | tf_op jit(solution)/shard_map/gate_y/ppermute | solution.py:60
  94.7 5.0 %collective-permute-start.24 = (f32[8,2304]{1,0:T(8,128)S(1)}, f32[8,2304]{1,0:T(8,128)S(1)}, u32[]{:S(2)}, u32[]{:S(2)}) collective-permute-start(f32[8,2304]{1,0:T(8,128)S(1)} %get-tuple-element.48.first), channel_id=1, source_target_pairs={{0,12},{4,8},{8,4},{12,0},{1,13},{5,9},{9,5},{13,1},{2,14},{6,10},... | collective-permute-start | bytes 221192 | tf_op jit(solution)/shard_map/gate_y/ppermute | solution.py:60
  101.2 16.7 %collective-permute-start.30 = (bf16[256,256]{1,0:T(8,128)(2,1)S(1)}, bf16[256,256]{1,0:T(8,128)(2,1)S(1)}, u32[]{:S(2)}, u32[]{:S(2)}) collective-permute-start(bf16[256,256]{1,0:T(8,128)(2,1)S(1)} %far_products_last.1.refs_0_), channel_id=1, source_target_pairs={{0,2},{2,0},{1,3},{3,1},{4,6},{6,4},{5,7},{7,5},{8,10},{10,8},{9,1... | collective-permute-start | bytes 393224 | tf_op jit(solution)/shard_map/out_z_last/ppermute | solution.py:60
  101.6 8.9 %collective-permute-start.27 = (bf16[8,2304]{1,0:T(8,128)(2,1)S(1)}, bf16[8,2304]{1,0:T(8,128)(2,1)S(1)}, u32[]{:S(2)}, u32[]{:S(2)}) collective-permute-start(bf16[8,2304]{1,0:T(8,128)(2,1)S(1)} %get-tuple-element.50), channel_id=1, source_target_pairs={{0,2},{2,0},{1,3},{3,1},{4,6},{6,4},{5,7},{7,5},{8,10},{10,8},{9,1... | collective-permute-start | bytes 110600 | tf_op jit(solution)/shard_map/gate_zh/ppermute | solution.py:60
  111.1 5.5 %collective-permute-start.29 = (f32[8,2304]{1,0:T(8,128)S(1)}, f32[8,2304]{1,0:T(8,128)S(1)}, u32[]{:S(2)}, u32[]{:S(2)}) collective-permute-start(f32[8,2304]{1,0:T(8,128)S(1)} %get-tuple-element.53.mine), channel_id=1, source_target_pairs={{0,1},{1,0},{2,3},{3,2},{4,5},{5,4},{6,7},{7,6},{8,9},{9,8},{10,11... | collective-permute-start | bytes 221192 | tf_op jit(solution)/shard_map/gate_core_back/ppermute | solution.py:60
  117.9 0.9 copy-start.8
